TPU v7x, 32 devices: a whole 2x2x4 slice. The times are simulated.
32 devices in a mesh: seq: 8 (over z, y), mp: 4 (over x, core).
Axes of the slice: x: 2, y: 2, z: 4, core: 2. Of those that a mesh axis runs over, the one named last changes fastest.
Arguments:
- queries: bfloat16 [2048, 2048], P('seq', 'mp'), may hold values from -120 to 120
- keys: bfloat16 [2048, 2048], P('seq', 'mp'), may hold values from -8 to 8
- values: bfloat16 [2048, 2048], P('seq', 'mp'), may hold values from -7 to 7
- out_weight: bfloat16 [2048, 2048], P('mp'), may hold values from -0.125 to 0.125
- out_grad: bfloat16 [2048, 2048], P(('seq', 'mp')), may hold values from -6 to 6
Outputs:
- mixed: bfloat16 [2048, 2048], P(('seq', 'mp'))
- query_grad: bfloat16 [2048, 2048], P('seq', 'mp')
- key_grad: bfloat16 [2048, 2048], P('seq', 'mp')
- value_grad: bfloat16 [2048, 2048], P('seq', 'mp')
All inputs are finite; a program needn't handle non-finite values.
Results may differ from a plain program's by a relative error of at most 0.012.
The roundings to bfloat16 on the way count: a program that leaves them out, or rounds other values in their place, can miss the bound.
Values may be sent and summed in bfloat16 or wider, within the bound.
No kernel may reach another device: no remote copies, remote signals or barrier semaphores. Data moves between devices by JAX's collectives and lax.ppermute only.
A program may use at most 64 MiB of HBM per device.

v0:
```python
import jax
import jax.numpy as jnp
from jax import lax
from jax.sharding import PartitionSpec as P

HEAD_DIM = 128
BLOCK = 256
LEVELS = 2


def swapped(x, axis, bit):
    return lax.ppermute(x, axis, [(i, i ^ 1 << bit) for i in range(lax.axis_size(axis))])


def with_halo(block, sides, width):
    for axis, dim in sides:
        count = lax.axis_size(axis)
        forward = [(i, i + 1) for i in range(count - 1)]
        backward = [(target, source) for source, target in forward]
        low = lax.ppermute(
            lax.slice_in_dim(block, block.shape[dim] - width, None, axis=dim), axis, forward
        )
        high = lax.ppermute(lax.slice_in_dim(block, 0, width, axis=dim), axis, backward)
        block = jnp.concatenate([low, block, high], axis=dim)
    return block


def pool_rows(rows):
    pairs = rows.astype(jnp.float32).reshape(rows.shape[0] // 2, 2, rows.shape[1])
    return ((pairs[:, 0] + pairs[:, 1]) * 0.5).astype(jnp.bfloat16)


def to_half(numbers):
    return lax.optimization_barrier(numbers.astype(jnp.bfloat16))


def flat_rows(stat):
    count, heads, length = stat.shape
    return stat.transpose(1, 0, 2).reshape(heads, count * length)


def split_rows(stat, count):
    heads, whole = stat.shape
    return stat.reshape(heads, count, whole // count).transpose(1, 0, 2)


def partner_rows(block_rows, bit):
    return swapped(block_rows, "seq", bit)


def partner_grads(block_rows, bit):
    return swapped(block_rows.astype(jnp.bfloat16), "seq", bit).astype(block_rows.dtype)


def ordered(mine, other, upper):
    return jnp.where(upper, jnp.concatenate([other, mine], 0), jnp.concatenate([mine, other], 0))


def regather(owned, bit, here):
    for step in range(bit):
        owned = ordered(owned, partner_rows(owned, step), here >> step & 1 == 1)
    return owned


def per_device(queries, keys, values, out_weight, out_grad):
    rows, width = queries.shape
    heads = width // HEAD_DIM
    scale = HEAD_DIM ** (-0.5)
    block = BLOCK
    blocks_here = rows // block
    here = lax.axis_index("seq")
    devices_seq = lax.axis_size("seq")
    query_heads = queries.reshape(blocks_here, block, heads, HEAD_DIM)
    stacked = jnp.concatenate([keys, values], axis=1)
    widened = with_halo(stacked, (("seq", 0),), block)
    windows = jnp.concatenate(
        [
            widened[shift_index * block : shift_index * block + rows].reshape(
                blocks_here, block, 2 * width
            )
            for shift_index in range(3)
        ],
        axis=1,
    )
    near_keys = windows[..., :width].reshape(blocks_here, 3 * block, heads, HEAD_DIM)
    near_values = windows[..., width:].reshape(blocks_here, 3 * block, heads, HEAD_DIM)
    near_scores = scale * jnp.einsum(
        "nthd,nshd->nhts", query_heads, near_keys, preferred_element_type=jnp.float32
    )
    beside = (
        here * blocks_here
        + jnp.arange(blocks_here, dtype=jnp.int32)[:, None]
        + (jnp.arange(3 * block, dtype=jnp.int32) // block)[None, :]
        - 1
    )
    present = (beside >= 0) & (beside < blocks_here * devices_seq)
    near_scores = jnp.where(present[:, None, None, :], near_scores, -jnp.inf)
    top = flat_rows(near_scores.max(-1))
    stored = []
    current_queries, current_pairs = (queries, stacked)
    for level in range(1, LEVELS + 1):
        current_queries = pool_rows(current_queries)
        current_pairs = pool_rows(current_pairs)
        count = rows >> level
        span = max(block // count, 1)
        bit = span.bit_length() - 1
        owned = regather(current_pairs, bit, here)
        other = partner_rows(owned, bit)
        sibling = other[None]
        groups = sibling.shape[0]
        coarse_heads = current_queries.reshape(groups, count // groups, heads, HEAD_DIM)
        other_keys = sibling[..., :width].reshape(groups, block, heads, HEAD_DIM)
        other_values = sibling[..., width:].reshape(groups, block, heads, HEAD_DIM)
        scores = scale * jnp.einsum(
            "nihd,njhd->nhij", coarse_heads, other_keys, preferred_element_type=jnp.float32
        )
        top = jnp.maximum(top, flat_rows(jnp.repeat(scores.max(-1), 2**level, axis=2)))
        stored.append((level, count, coarse_heads, other_keys, other_values, scores))
    near_weights = jnp.exp(near_scores - split_rows(top, blocks_here)[..., None])
    total = flat_rows(near_weights.sum(-1))
    level_weights = []
    for level, count, coarse_heads, other_keys, other_values, scores in stored:
        groups, _, per_group, keys_count = scores.shape
        repeat = 2**level
        fine_top = split_rows(top, groups).reshape(groups, heads, per_group, repeat)
        weight = 2.0**level * jnp.exp(scores[:, :, :, None, :] - fine_top[..., None])
        weight = weight.reshape(groups, heads, per_group * repeat, keys_count)
        total = total + flat_rows(weight.sum(-1))
        level_weights.append(weight)
    near_prob = to_half(near_weights / split_rows(total, blocks_here)[..., None])
    context = jnp.einsum(
        "nhts,nshd->nthd", near_prob, near_values, preferred_element_type=jnp.float32
    ).reshape(rows, width)
    level_probs = []
    for entry, weight in zip(stored, level_weights):
        groups = weight.shape[0]
        prob = to_half(weight / split_rows(total, groups)[..., None])
        level_probs.append(prob)
        context = context + jnp.einsum(
            "nhts,nshd->nthd", prob, entry[4], preferred_element_type=jnp.float32
        ).reshape(rows, width)
    attended = context.astype(jnp.bfloat16)
    mixed = lax.psum_scatter(
        jnp.dot(attended, out_weight, preferred_element_type=jnp.float32).astype(jnp.bfloat16),
        "mp",
        scatter_dimension=0,
        tiled=True,
    )
    grad_attended = lax.dot_general(
        lax.all_gather(out_grad, "mp", axis=0, tiled=True),
        out_weight,
        (((1,), (1,)), ((), ())),
        preferred_element_type=jnp.float32,
    ).astype(jnp.bfloat16)
    grad_heads = grad_attended.reshape(rows, heads, HEAD_DIM)
    delta = (grad_heads.astype(jnp.float32) * context.reshape(rows, heads, HEAD_DIM)).sum(-1).T
    grad_blocks = grad_heads.reshape(blocks_here, block, heads, HEAD_DIM)
    near_slope = jnp.einsum(
        "nthd,nshd->nhts", grad_blocks, near_values, preferred_element_type=jnp.float32
    )
    near_shift = to_half(
        near_prob.astype(jnp.float32) * (near_slope - split_rows(delta, blocks_here)[..., None])
    )
    grad_queries = scale * jnp.einsum(
        "nhts,nshd->nthd", near_shift, near_keys, preferred_element_type=jnp.float32
    ).reshape(rows, width)
    key_window = scale * jnp.einsum(
        "nhts,nthd->nshd", near_shift, query_heads, preferred_element_type=jnp.float32
    )
    value_window = jnp.einsum(
        "nhts,nthd->nshd", near_prob, grad_blocks, preferred_element_type=jnp.float32
    )
    pair_window = jnp.concatenate(
        [
            key_window.reshape(blocks_here, 3 * block, width),
            value_window.reshape(blocks_here, 3 * block, width),
        ],
        -1,
    )
    spread = jnp.zeros((rows + 2 * block, 2 * width), jnp.float32)
    for shift_index in range(3):
        piece = pair_window[:, shift_index * block : (shift_index + 1) * block].reshape(
            rows, 2 * width
        )
        spread = spread + jnp.pad(piece, ((shift_index * block, (2 - shift_index) * block), (0, 0)))
    grad_pairs = spread[block : block + rows]
    rims = jnp.concatenate([spread[:block], spread[rows + block :]], axis=0)
    returned = with_halo(rims.astype(jnp.bfloat16), (("seq", 0),), block).astype(rims.dtype)
    grad_pairs = grad_pairs.at[:block].add(returned[:block])
    grad_pairs = grad_pairs.at[rows - block :].add(returned[3 * block :])
    for entry, prob in zip(stored, level_probs):
        level, count, coarse_heads, other_keys, other_values, scores = entry
        groups = prob.shape[0]
        repeat = 2**level
        per_group = count // groups
        grad_groups = grad_heads.reshape(groups, rows // groups, heads, HEAD_DIM)
        slope = jnp.einsum(
            "nthd,nshd->nhts", grad_groups, other_values, preferred_element_type=jnp.float32
        )
        shift = to_half(prob.astype(jnp.float32) * (slope - split_rows(delta, groups)[..., None]))
        fine_query = scale * jnp.einsum(
            "nhts,nshd->nthd", shift, other_keys, preferred_element_type=jnp.float32
        )
        coarse_query = fine_query.reshape(groups, per_group, repeat, width).sum(2)
        repeated_heads = jnp.repeat(coarse_heads, repeat, axis=1)
        coarse_key = scale * jnp.einsum(
            "nhts,nthd->nshd", shift, repeated_heads, preferred_element_type=jnp.float32
        )
        coarse_value = jnp.einsum(
            "nhts,nthd->nshd", prob, grad_groups, preferred_element_type=jnp.float32
        )
        sent = jnp.concatenate(
            [coarse_key.reshape(groups, block, width), coarse_value.reshape(groups, block, width)],
            -1,
        )
        span = max(block // count, 1)
        bit = span.bit_length() - 1
        mine = partner_grads(sent[0], bit)
        for step in range(bit - 1, -1, -1):
            half = mine.shape[0] // 2
            upper = here >> step & 1 == 1
            kept = jnp.where(upper, mine[half:], mine[:half])
            given = jnp.where(upper, mine[:half], mine[half:])
            mine = kept + partner_grads(given, step)
        grad_queries = (
            grad_queries + jnp.repeat(coarse_query.reshape(count, width), repeat, axis=0) / repeat
        )
        grad_pairs = grad_pairs + jnp.repeat(mine, repeat, axis=0) / repeat
    return (
        mixed,
        grad_queries.astype(jnp.bfloat16),
        grad_pairs[:, :width].astype(jnp.bfloat16),
        grad_pairs[:, width:].astype(jnp.bfloat16),
    )


def solution(mesh):
    return jax.shard_map(
        per_device,
        mesh=mesh,
        in_specs=(
            P("seq", "mp"),
            P("seq", "mp"),
            P("seq", "mp"),
            P("mp", None),
            P(("seq", "mp"), None),
        ),
        out_specs=(P(("seq", "mp"), None), P("seq", "mp"), P("seq", "mp"), P("seq", "mp")),
        check_vma=False,
    )
```

profile of v0, /device:TPU:0, one launch (start us, length us, event | category | flops | bytes accessed | tf_op | source)
XLA Modules:
  0.0 205.1 jit_solution(6980223724844784070)
XLA Ops:
  11.7 6.3 %collective-permute-start = (bf16[256,1024]{0,1:T(8,128)(2,1)}, bf16[256,1024]{0,1:T(8,128)(2,1)}, u32[]{:S(2)}, u32[]{:S(2)}) collective-permute-start(bf16[256,1024]{0,1:T(8,128)(2,1)} %get-tuple-element.60), channel_id=1, source_target_pairs={{0,4},{4,8},{8,12},{12,16},{16,20},{20,24},{24,28},{1,5},{5,9},{9,... | collective-permute-start | bytes 1572872 | tf_op jit(solution)/shard_map/ppermute | solution.py:20
  19.7 2.7 %convert_reduce_fusion = (f32[128,1024]{1,0:T(8,128)}, bf16[128,1,1024]{2,1,0:T(2,128)(2,1)}) fusion(f32[128,2,1024]{2,1,0:T(2,128)S(1)} %maximum_convert_fusion), kind=kLoop, calls=%fused_computation.87 | loop fusion | flops 524288 | bytes 1835008 | tf_op jit(solution)/shard_map/convert_element_type | solution.py:29
  24.8 2.1 %collective-permute-start.4 = (bf16[64,1024]{1,0:T(8,128)(2,1)}, bf16[64,1024]{1,0:T(8,128)(2,1)}, u32[]{:S(2)}, u32[]{:S(2)}) collective-permute-start(bf16[64,1024]{1,0:T(8,128)(2,1)} %bitcast.207), channel_id=1, source_target_pairs={{0,4},{4,0},{8,12},{12,8},{16,20},{20,16},{24,28},{28,24},{1,5},{5... | collective-permute-start | bytes 393224 | tf_op jit(solution)/shard_map/ppermute | solution.py:12
  30.5 11.3 %collective-permute-done.4 = bf16[64,1024]{1,0:T(8,128)(2,1)} collective-permute-done((bf16[64,1024]{1,0:T(8,128)(2,1)}, bf16[64,1024]{1,0:T(8,128)(2,1)}, u32[]{:S(2)}, u32[]{:S(2)}) %collective-permute-start.4) | collective-permute-done | bytes 131104 | tf_op jit(solution)/shard_map/ppermute | solution.py:12
  43.0 2.7 %collective-permute-start.5 = (bf16[128,1024]{1,0:T(8,128)(2,1)S(1)}, bf16[128,1024]{1,0:T(8,128)(2,1)}, u32[]{:S(2)}, u32[]{:S(2)}) collective-permute-start(bf16[128,1024]{1,0:T(8,128)(2,1)S(1)} %maximum_select_fusion.2), channel_id=1, source_target_pairs={{0,8},{4,12},{8,0},{12,4},{16,24},{20,28},{24,16},{28,20},{1,9},{5... | collective-permute-start | bytes 786440 | tf_op jit(solution)/shard_map/ppermute | solution.py:12
  48.4 2.3 %maximum_select_fusion = bf16[256,1024]{1,0:T(8,128)(2,1)} fusion(bf16[128,1024]{1,0:T(8,128)(2,1)} %bitcast.206, bf16[128,1024]{1,0:T(8,128)(2,1)} %collective-permute-done.2, pred[]{:T(512)S(6)} %eq.4), kind=kLoop, calls=%fused_computation.71 | loop fusion | flops 2359296 | bytes 1048577 | tf_op jit(solution)/shard_map/jit(_where)/select_n | solution.py:56
  53.4 2.6 %collective-permute-start.6 = (bf16[256,1024]{1,0:T(8,128)(2,1)}, bf16[256,1024]{1,0:T(8,128)(2,1)}, u32[]{:S(2)}, u32[]{:S(2)}) collective-permute-start(bf16[256,1024]{1,0:T(8,128)(2,1)} %maximum_select_fusion.1), channel_id=1, source_target_pairs={{0,16},{4,20},{8,24},{12,28},{16,0},{20,4},{24,8},{28,12},{1,17},{... | collective-permute-start | bytes 1572872 | tf_op jit(solution)/shard_map/ppermute | solution.py:12
  59.2 2.4 %bitcast_reduce_fusion = (f32[4,256]{1,0:T(4,128)S(1)}, f32[4,768,256]{2,1,0:T(8,128)}) fusion(pred[768]{0:T(1024)(128)(4,1)S(1)} %fusion.67, bf16[768,4,128]{0,2,1:T(8,128)(2,1)S(1)} %bitcast.216, bf16[256,4,128]{0,2,1:T(8,128)(2,1)S(1)} %bitcast.228), kind=kOutput, calls=%fused_computation.7 | convolution fusion | flops 203684864 | bytes 4199168 | tf_op jit(solution)/shard_map/nthd,nshd->nhts/dot_general | solution.py:87
  63.1 9.8 %collective-permute-done.3 = bf16[256,1024]{1,0:T(8,128)(2,1)} collective-permute-done((bf16[256,1024]{1,0:T(8,128)(2,1)}, bf16[256,1024]{1,0:T(8,128)(2,1)}, u32[]{:S(2)}, u32[]{:S(2)}) %collective-permute-start.3) | collective-permute-done | bytes 524320 | tf_op jit(solution)/shard_map/ppermute | solution.py:12
  76.5 3.0 %sub.124 = f32[1,4,256,256]{3,2,1,0:T(8,128)} reshape(f32[4,128,2,256]{3,2,1,0:T(2,128)} %sub.118) | data formatting | bytes 2097152 | tf_op jit(solution)/shard_map/sub | solution.py:126
  95.4 2.6 %copy.247 = f32[4,128,2]{2,1,0:T(8,128)} copy(f32[4,128,2]{0,2,1:T(2,128)} %maximum_maximum_fusion.1) | data formatting | bytes 8192 | tf_op jit(solution)/shard_map/max | solution.py:117
  98.0 3.2 %multiply_reduce_fusion.1 = f32[4,128,2]{2,1,0:T(8,128)} fusion(f32[4,128,2]{2,1,0:T(8,128)} %copy.247, f32[4,128,256]{2,1,0:T(8,128)S(1)} %get-tuple-element.72), kind=kLoop, calls=%fused_computation.63 | loop fusion | flops 785408 | bytes 532480 | tf_op jit(solution)/shard_map/reduce_sum | solution.py:128
  105.7 2.7 %fusion.2 = f32[4,256]{1,0:T(4,128)S(1)} fusion(f32[4,768,256]{2,1,0:T(8,128)} %get-tuple-element.70, f32[4,256]{1,0:T(4,128)S(1)} %get-tuple-element.66, pred[768]{0:T(1024)(128)(4,1)S(1)} %copy-done.32), kind=kLoop, calls=%fused_computation.13 | loop fusion | flops 3144704 | bytes 3154688 | tf_op jit(solution)/shard_map/reduce_sum | solution.py:120
  113.6 2.7 %convolution_convert_fusion.3 = bf16[256,512]{1,0:T(8,128)(2,1)} fusion(bf16[256,2048]{1,0:T(8,128)(2,1)} %all-gather.2.cloned.1.call-done, bf16[512,2048]{1,0:T(8,128)(2,1)S(1)} %copy-done), kind=kOutput, calls=%fused_computation.47 | convolution fusion | flops 537001984 | bytes 3407872 | tf_op jit(solution)/shard_map/dot_general | solution.py:149
  119.9 3.2 %fusion = bf16[1,4,256,768]{2,3,1,0:T(8,128)(2,1)} fusion(bf16[1,4,256,768]{2,3,1,0:T(8,128)(2,1)S(1)} %copy-done.4, bf16[256,4,128]{0,2,1:T(8,128)(2,1)S(1)} %bitcast.209, bf16[768,4,128]{0,2,1:T(8,128)(2,1)} %bitcast.214, f32[4,256]{1,0:T(4,128)S(1)} %bitcast.248), kind=kOutput, calls=%fused_computation.5 | convolution fusion | flops 204472320 | bytes 4198400 | tf_op jit(solution)/shard_map/nthd,nshd->nhts/dot_general | solution.py:158
  141.8 3.0 %copy.270 = f32[1,768,512]{2,1,0:T(8,128)} copy(f32[1,768,512]{1,2,0:T(8,128)} %bitcast.219) | data formatting | bytes 3145728 | tf_op jit(solution)/shard_map/reshape | solution.py:175
  144.9 3.0 %copy.271 = f32[1,768,512]{2,1,0:T(8,128)} copy(f32[1,768,512]{1,2,0:T(8,128)} %bitcast.218) | data formatting | bytes 3145728 | tf_op jit(solution)/shard_map/reshape | solution.py:176
  147.9 2.4 %fusion.37 = (f32[256,1024]{1,0:T(8,128)S(1)}, f32[256,1024]{1,0:T(8,128)S(1)}, f32[256,1024]{1,0:T(8,128)S(1)}) fusion(f32[1,768,512]{2,1,0:T(8,128)} %copy.270, f32[1,768,512]{2,1,0:T(8,128)} %copy.271), kind=kLoop, calls=%fused_computation.52 | loop fusion | flops 786432 | bytes 6291456 | tf_op jit(solution)/shard_map/reshape | solution.py:182
  150.3 2.2 %fusion.70 = (bf16[768,1024]{1,0:T(8,128)(2,1)S(1)}, f32[768,1024]{1,0:T(8,128)}) fusion(f32[256,1024]{1,0:T(8,128)S(1)} %get-tuple-element.49, f32[256,1024]{1,0:T(8,128)S(1)} %get-tuple-element.50, f32[256,1024]{1,0:T(8,128)S(1)} %get-tuple-element.48), kind=kLoop, calls=%fused_computation.129 | loop fusion | flops 2359296 | bytes 7864320 | tf_op jit(solution)/shard_map/convert.23
  156.4 5.4 %collective-permute-start.7 = (bf16[256,1024]{1,0:T(8,128)(2,1)}, bf16[256,1024]{1,0:T(8,128)(2,1)}, u32[]{:S(2)}, u32[]{:S(2)}) collective-permute-start(bf16[256,1024]{1,0:T(8,128)(2,1)} %get-tuple-element.51), channel_id=1, source_target_pairs={{0,4},{4,8},{8,12},{12,16},{16,20},{20,24},{24,28},{1,5},{5,9},{9,... | collective-permute-start | bytes 1572872 | tf_op jit(solution)/shard_map/ppermute | solution.py:20
  167.6 10.5 %collective-permute-done.12 = bf16[128,1024]{0,1:T(8,128)(2,1)S(1)} collective-permute-done((bf16[128,1024]{0,1:T(8,128)(2,1)S(1)}, bf16[128,1024]{0,1:T(8,128)(2,1)S(1)}, u32[]{:S(2)}, u32[]{:S(2)}) %collective-permute-start.12) | collective-permute-done | bytes 262176 | tf_op jit(solution)/shard_map/ppermute | solution.py:12
  179.6 8.9 %collective-permute-done.10 = bf16[128,1024]{1,0:T(8,128)(2,1)S(1)} collective-permute-done((bf16[128,1024]{1,0:T(8,128)(2,1)S(1)}, bf16[128,1024]{1,0:T(8,128)(2,1)S(1)}, u32[]{:S(2)}, u32[]{:S(2)}) %collective-permute-start.10) | collective-permute-done | bytes 262176 | tf_op jit(solution)/shard_map/ppermute | solution.py:12
  190.6 2.3 %collective-permute-done.13 = bf16[64,1024]{0,1:T(8,128)(2,1)S(1)} collective-permute-done((bf16[64,1024]{0,1:T(8,128)(2,1)S(1)}, bf16[64,1024]{0,1:T(8,128)(2,1)S(1)}, u32[]{:S(2)}, u32[]{:S(2)}) %collective-permute-start.13) | collective-permute-done | bytes 131104 | tf_op jit(solution)/shard_map/ppermute | solution.py:12
  195.0 2.4 %fusion.41 = bf16[256,1024]{1,0:T(8,128)(2,1)S(1)} fusion(f32[256,1024]{1,0:T(8,128)} %div.97, f32[256,1024]{1,0:T(8,128)S(1)} %copy-done.14, f32[768,1024]{1,0:T(8,128)} %get-tuple-element.47, bf16[256,1024]{1,0:T(8,128)(2,1)} %collective-permute-done.8, bf16[256,1024]{1,0:T(8,128)(2,1)} %get-tuple-element.51, bf16[256,1024]{1,0:T(8,128)(2,1)} %get-tuple-element.52, ...), kind=kLoop, calls=%fused_computation.57 | loop fusion | flops 5505024 | bytes 5767168 | tf_op jit(solution)/shard_map/convert.4
  (199 shorter events, 90.5 us)
Async XLA Ops:
  7.2 104.6 %copy-start = (bf16[512,2048]{1,0:T(8,128)(2,1)S(1)}, bf16[512,2048]{1,0:T(8,128)(2,1)}, u32[]{:S(2)}) copy-start(bf16[512,2048]{1,0:T(8,128)(2,1)} %param.16) | copy-start | bytes 6291460
  7.2 11.9 %copy-start.24 = (bf16[256,512]{1,0:T(8,128)(2,1)S(1)}, bf16[256,512]{1,0:T(8,128)(2,1)}, u32[]{:S(2)}) copy-start(bf16[256,512]{1,0:T(8,128)(2,1)} %param.14) | copy-start | bytes 786436
  7.2 106.4 %all-gather.2.cloned.1.call-start = ((), (), s32[]{:S(2)}) async-start(), calls=%async_computation.2 | async-start | bytes 1310720 | tf_op jit(solution)/shard_map/all_gather | solution.py:150
  10.4 45.5 %collective-permute-start.1 = (bf16[256,1024]{0,1:T(8,128)(2,1)}, bf16[256,1024]{0,1:T(8,128)(2,1)}, u32[]{:S(2)}, u32[]{:S(2)}) collective-permute-start(bf16[256,1024]{0,1:T(8,128)(2,1)} %get-tuple-element.60), channel_id=1, source_target_pairs={{4,0},{8,4},{12,8},{16,12},{20,16},{24,20},{28,24},{5,1},{9,5},{13... | collective-permute-start | bytes 1572872 | tf_op jit(solution)/shard_map/ppermute | solution.py:23
  11.7 44.2 %collective-permute-start = (bf16[256,1024]{0,1:T(8,128)(2,1)}, bf16[256,1024]{0,1:T(8,128)(2,1)}, u32[]{:S(2)}, u32[]{:S(2)}) collective-permute-start(bf16[256,1024]{0,1:T(8,128)(2,1)} %get-tuple-element.60), channel_id=1, source_target_pairs={{0,4},{4,8},{8,12},{12,16},{16,20},{20,24},{24,28},{1,5},{5,9},{9,... | collective-permute-start | bytes 1572872 | tf_op jit(solution)/shard_map/ppermute | solution.py:20
  24.8 17.0 %collective-permute-start.4 = (bf16[64,1024]{1,0:T(8,128)(2,1)}, bf16[64,1024]{1,0:T(8,128)(2,1)}, u32[]{:S(2)}, u32[]{:S(2)}) collective-permute-start(bf16[64,1024]{1,0:T(8,128)(2,1)} %bitcast.207), channel_id=1, source_target_pairs={{0,4},{4,0},{8,12},{12,8},{16,20},{20,16},{24,28},{28,24},{1,5},{5... | collective-permute-start | bytes 393224 | tf_op jit(solution)/shard_map/ppermute | solution.py:12
  28.8 19.6 %collective-permute-start.2 = (bf16[128,1024]{1,0:T(8,128)(2,1)}, bf16[128,1024]{1,0:T(8,128)(2,1)}, u32[]{:S(2)}, u32[]{:S(2)}) collective-permute-start(bf16[128,1024]{1,0:T(8,128)(2,1)} %bitcast.206), channel_id=1, source_target_pairs={{0,4},{4,0},{8,12},{12,8},{16,20},{20,16},{24,28},{28,24},{1,5},{5... | collective-permute-start | bytes 786440 | tf_op jit(solution)/shard_map/ppermute | solution.py:12
  28.8 169.5 %reduce-scatter.2.cloned.1.call-start = ((), (), s32[]{:S(2)}) async-start(), calls=%async_computation.1 | async-start | bytes 1310720 | tf_op jit(solution)/shard_map/reduce_scatter | solution.py:143
  43.0 8.3 %collective-permute-start.5 = (bf16[128,1024]{1,0:T(8,128)(2,1)S(1)}, bf16[128,1024]{1,0:T(8,128)(2,1)}, u32[]{:S(2)}, u32[]{:S(2)}) collective-permute-start(bf16[128,1024]{1,0:T(8,128)(2,1)S(1)} %maximum_select_fusion.2), channel_id=1, source_target_pairs={{0,8},{4,12},{8,0},{12,4},{16,24},{20,28},{24,16},{28,20},{1,9},{5... | collective-permute-start | bytes 786440 | tf_op jit(solution)/shard_map/ppermute | solution.py:12
  47.6 10.7 %copy-start.21 = (bf16[256,512]{0,1:T(8,128)(2,1)}, bf16[256,512]{0,1:T(8,128)(2,1)S(1)}, u32[]{:S(2)}) copy-start(bf16[256,512]{0,1:T(8,128)(2,1)S(1)} %copy.301) | copy-start | bytes 786436
  50.7 22.2 %collective-permute-start.3 = (bf16[256,1024]{1,0:T(8,128)(2,1)}, bf16[256,1024]{1,0:T(8,128)(2,1)}, u32[]{:S(2)}, u32[]{:S(2)}) collective-permute-start(bf16[256,1024]{1,0:T(8,128)(2,1)} %maximum_select_fusion), channel_id=1, source_target_pairs={{0,8},{4,12},{8,0},{12,4},{16,24},{20,28},{24,16},{28,20},{1,9},{5... | collective-permute-start | bytes 1572872 | tf_op jit(solution)/shard_map/ppermute | solution.py:12
  53.4 28.4 %collective-permute-start.6 = (bf16[256,1024]{1,0:T(8,128)(2,1)}, bf16[256,1024]{1,0:T(8,128)(2,1)}, u32[]{:S(2)}, u32[]{:S(2)}) collective-permute-start(bf16[256,1024]{1,0:T(8,128)(2,1)} %maximum_select_fusion.1), channel_id=1, source_target_pairs={{0,16},{4,20},{8,24},{12,28},{16,0},{20,4},{24,8},{28,12},{1,17},{... | collective-permute-start | bytes 1572872 | tf_op jit(solution)/shard_map/ppermute | solution.py:12
  83.8 19.2 %copy-start.15 = (bf16[1,256,512]{1,2,0:T(8,128)(2,1)}, bf16[1,256,512]{1,2,0:T(8,128)(2,1)S(1)}, u32[]{:S(2)}) copy-start(bf16[1,256,512]{1,2,0:T(8,128)(2,1)S(1)} %copy.242) | copy-start | bytes 786436
  84.1 19.0 %copy-start.17 = (f32[4,64,256]{2,1,0:T(8,128)}, f32[4,64,256]{2,1,0:T(8,128)S(1)}, u32[]{:S(2)}) copy-start(f32[4,64,256]{2,1,0:T(8,128)S(1)} %get-tuple-element.74) | copy-start | bytes 786436
  92.1 13.5 %copy-start.29 = (f32[4,256]{1,0:T(4,128)S(1)}, f32[4,256]{1,0:T(4,128)}, u32[]{:S(2)}) copy-start(f32[4,256]{1,0:T(4,128)} %copy.253) | copy-start | bytes 12292
  95.4 10.2 %copy-start.30 = (f32[4,256]{1,0:T(4,128)S(1)}, f32[4,256]{1,0:T(4,128)}, u32[]{:S(2)}) copy-start(f32[4,256]{1,0:T(4,128)} %broadcast_in_dim.71) | copy-start | bytes 12292
  95.4 10.3 %copy-start.32 = (pred[768]{0:T(1024)(128)(4,1)S(1)}, pred[768]{0:T(1024)(128)(4,1)}, u32[]{:S(2)}) copy-start(pred[768]{0:T(1024)(128)(4,1)} %copy-done.31) | copy-start | bytes 2308
  136.3 25.5 %collective-permute-start.11 = (bf16[256,1024]{0,1:T(8,128)(2,1)}, bf16[256,1024]{0,1:T(8,128)(2,1)}, u32[]{:S(2)}, u32[]{:S(2)}) collective-permute-start(bf16[256,1024]{0,1:T(8,128)(2,1)} %maximum_bitcast_fusion.1), channel_id=1, source_target_pairs={{0,16},{4,20},{8,24},{12,28},{16,0},{20,4},{24,8},{28,12},{1,17},{... | collective-permute-start | bytes 1572872 | tf_op jit(solution)/shard_map/ppermute | solution.py:12
  137.9 26.6 %collective-permute-start.9 = (bf16[256,1024]{1,0:T(8,128)(2,1)}, bf16[256,1024]{1,0:T(8,128)(2,1)}, u32[]{:S(2)}, u32[]{:S(2)}) collective-permute-start(bf16[256,1024]{1,0:T(8,128)(2,1)} %maximum_bitcast_fusion), channel_id=1, source_target_pairs={{0,8},{4,12},{8,0},{12,4},{16,24},{20,28},{24,16},{28,20},{1,9},{5... | collective-permute-start | bytes 1572872 | tf_op jit(solution)/shard_map/ppermute | solution.py:12
  155.1 39.9 %collective-permute-start.8 = (bf16[256,1024]{1,0:T(8,128)(2,1)}, bf16[256,1024]{1,0:T(8,128)(2,1)}, u32[]{:S(2)}, u32[]{:S(2)}) collective-permute-start(bf16[256,1024]{1,0:T(8,128)(2,1)} %get-tuple-element.52), channel_id=1, source_target_pairs={{4,0},{8,4},{12,8},{16,12},{20,16},{24,20},{28,24},{5,1},{9,5},{13... | collective-permute-start | bytes 1572872 | tf_op jit(solution)/shard_map/ppermute | solution.py:23
  156.4 38.6 %collective-permute-start.7 = (bf16[256,1024]{1,0:T(8,128)(2,1)}, bf16[256,1024]{1,0:T(8,128)(2,1)}, u32[]{:S(2)}, u32[]{:S(2)}) collective-permute-start(bf16[256,1024]{1,0:T(8,128)(2,1)} %get-tuple-element.51), channel_id=1, source_target_pairs={{0,4},{4,8},{8,12},{12,16},{16,20},{20,24},{24,28},{1,5},{5,9},{9,... | collective-permute-start | bytes 1572872 | tf_op jit(solution)/shard_map/ppermute | solution.py:20
  162.9 15.2 %collective-permute-start.12 = (bf16[128,1024]{0,1:T(8,128)(2,1)S(1)}, bf16[128,1024]{0,1:T(8,128)(2,1)S(1)}, u32[]{:S(2)}, u32[]{:S(2)}) collective-permute-start(bf16[128,1024]{0,1:T(8,128)(2,1)S(1)} %select_convert_fusion.1), channel_id=1, source_target_pairs={{0,8},{4,12},{8,0},{12,4},{16,24},{20,28},{24,16},{28,20},{1,9},{5... | collective-permute-start | bytes 786440 | tf_op jit(solution)/shard_map/ppermute | solution.py:12
  165.7 22.7 %collective-permute-start.10 = (bf16[128,1024]{1,0:T(8,128)(2,1)S(1)}, bf16[128,1024]{1,0:T(8,128)(2,1)S(1)}, u32[]{:S(2)}, u32[]{:S(2)}) collective-permute-start(bf16[128,1024]{1,0:T(8,128)(2,1)S(1)} %select_convert_fusion.2), channel_id=1, source_target_pairs={{0,4},{4,0},{8,12},{12,8},{16,20},{20,16},{24,28},{28,24},{1,5},{5... | collective-permute-start | bytes 786440 | tf_op jit(solution)/shard_map/ppermute | solution.py:12
  178.3 14.6 %collective-permute-start.13 = (bf16[64,1024]{0,1:T(8,128)(2,1)S(1)}, bf16[64,1024]{0,1:T(8,128)(2,1)S(1)}, u32[]{:S(2)}, u32[]{:S(2)}) collective-permute-start(bf16[64,1024]{0,1:T(8,128)(2,1)S(1)} %select_convert_fusion), channel_id=1, source_target_pairs={{0,4},{4,0},{8,12},{12,8},{16,20},{20,16},{24,28},{28,24},{1,5},{5... | collective-permute-start | bytes 393224 | tf_op jit(solution)/shard_map/ppermute | solution.py:12
  (25 other events, 110.2 us)
Sparse Core Ops, SparseCore 0:
  28.9 17.4 all-gather.1
  113.7 24.6 reduce-scatter.1
where the time goes:
time: 206 us; the launch traced here: 205 us
  local copies, waits for them, and re-layouts  56 us (27%)
  waiting for transfers between devices  42.9 us (21%)
  other arithmetic  41 us (20%)
  starting transfers between devices  28.5 us (14%)
  matrix products  21.9 us (11%)
  between operations  14.8 us (7%)
    ppermute x10, waiting for transfers between devices, swapped(): lax.ppermute(x, axis, [(i, i ^ 1 << bit) for i in range(lax.axis_size(axi...  42.9 us
    ppermute x10, starting transfers between devices, swapped(): lax.ppermute(x, axis, [(i, i ^ 1 << bit) for i in range(lax.axis_size(axi...  14 us
    ppermute x2, starting transfers between devices, with_halo(): lax.ppermute(lax.slice_in_dim(block, block.shape[dim] - width, None, axis...  11.7 us
    sub x4, local copies, waits for them, and re-layouts, per_device(): scores[:, :, :, None, :] - fine_top[..., None]  6.83 us
    broadcast_in_dim x8, local copies, waits for them, and re-layouts, per_device(): jnp.repeat(scores.max(-1), 2 ** level, axis=2)  6.75 us
    unnamed x70, local copies, waits for them, and re-layouts  6.09 us
    select_n x3, other arithmetic, ordered(): jnp.where(upper, jnp.concatenate([other, mine], 0), jnp.concatenate([mine...  5.54 us
    another operation x2, other arithmetic  4.6 us
  transfers between devices with their start and end apart: 16, of which 5 were waited for; matrix products, arithmetic and copies ran while one was open for 56% of the time, Pallas kernels for 0%

commit v1 on v0

v1 whole, which is shorter than its diff:
```python
import functools

import jax
import jax.numpy as jnp
from jax import lax
from jax.experimental import pallas as pl
from jax.experimental.pallas import tpu as pltpu
from jax.sharding import PartitionSpec as P

HEAD_DIM = 128
BLOCK = 256
LEVELS = 2
GROUP = 4
SCALE = HEAD_DIM**-0.5
LOG2E = 1.4426950408889634
BF16 = jnp.bfloat16
F32 = jnp.float32


def dot(a, b):
    return lax.dot_general(a, b, (((1,), (0,)), ((), ())), preferred_element_type=F32)


def dot_nt(a, b):
    return lax.dot_general(a, b, (((1,), (1,)), ((), ())), preferred_element_type=F32)


def shape(*dims, dtype=BF16):
    return jax.ShapeDtypeStruct(dims, dtype)


def call(kernel, out_shape, args, scratch=(), flops=0, limit=32):
    whole = pl.BlockSpec(memory_space=pltpu.VMEM)
    moved = sum(x.size * x.dtype.itemsize for x in (*args, *out_shape))
    return pl.pallas_call(
        kernel,
        out_shape=out_shape,
        in_specs=[whole] * len(args),
        out_specs=[whole] * len(out_shape),
        scratch_shapes=scratch,
        compiler_params=pltpu.CompilerParams(vmem_limit_bytes=limit << 20),
        cost_estimate=pl.CostEstimate(flops=flops, bytes_accessed=moved, transcendentals=0),
    )(*args)


def member():
    return lax.rem(lax.axis_index("seq"), GROUP)


def columns(index):
    return pl.ds(pl.multiple_of(index * HEAD_DIM, HEAD_DIM), HEAD_DIM)


def span(index, size):
    return pl.ds(pl.multiple_of(index * size, size), size)


def iota(dims, axis):
    return lax.broadcasted_iota(jnp.int32, dims, axis)


def averaging(level):
    dims = (BLOCK, BLOCK)
    same = (iota(dims, 0) >> level) == (iota(dims, 1) >> level)
    return jnp.where(same, 2.0**-level, 0.0).astype(BF16)


def pooling():
    dims = (BLOCK // 2, BLOCK)
    return jnp.where(iota(dims, 0) == (iota(dims, 1) >> 1), 0.5, 0.0).astype(BF16)


def spreading(level):
    dims = (BLOCK, BLOCK >> level)
    return jnp.where((iota(dims, 0) >> level) == iota(dims, 1), 2.0**-level, 0.0).astype(BF16)


def halves(x):
    high = x.astype(BF16)
    return high, (x - high.astype(F32)).astype(BF16)


def pack_kernel(q, k, v, *outs):
    me = member()
    for step, out in enumerate(outs):
        for part, source in enumerate((q, k, v)):
            out[part] = source[:, columns(me ^ step)]


def gather_kernel(nb, groups, *refs):
    chunks, (full, spread_q, level_1, level_2, sent) = refs[:GROUP], refs[GROUP:]
    me = member()
    rows = chunks[0].shape[1]
    for step, chunk in enumerate(chunks):
        full[:, span(me ^ step, rows), :] = chunk[...]
    pool, even_1, even_2 = pooling(), averaging(1), averaging(2)
    for b in range(nb):
        at = slice(b * BLOCK, (b + 1) * BLOCK)
        once = dot(even_1, full[0, at]).astype(BF16)
        spread_q[0, at] = once
        spread_q[1, at] = dot(even_2, once).astype(BF16)
        for part in range(2):
            half = BLOCK // 2
            level_1[part, b * half : (b + 1) * half] = dot(pool, full[part + 1, at]).astype(BF16)
    for b in range(nb // 2):
        half = BLOCK // 2
        for part in range(2):
            block = level_1[part, b * BLOCK : (b + 1) * BLOCK]
            level_2[part, b * half : (b + 1) * half] = dot(pool, block).astype(BF16)
    upper = lax.axis_index("seq") >= GROUP
    for part in range(2):
        sent[part] = level_2[part]
        low, high = full[part + 1, :BLOCK], full[part + 1, (nb - 1) * BLOCK :]
        if groups == 2:
            sent[2 + part] = jnp.where(upper, low, high)
        else:
            sent[2 + part] = high
            sent[4 + part] = low


def sibling(b):
    return (b >> 1) ^ 1


def rim_present(groups):
    group = lax.axis_index("seq") // GROUP
    return group > 0, group < groups - 1


def forward_kernel(nb, groups, *refs):
    full, spread_q, level_1, level_2, rim_low, rim_high, prob, *outs, keys, v_t, v1_t, v2_t = refs
    rows = outs[0].shape[0]
    tokens = nb * BLOCK
    me = member()
    present = rim_present(groups)
    keys[:BLOCK] = rim_low[0]
    keys[BLOCK : BLOCK + tokens] = full[1]
    keys[BLOCK + tokens :] = rim_high[0]
    v_t[:, :BLOCK] = rim_low[1].T
    v_t[:, BLOCK + tokens :] = rim_high[1].T
    for b in range(nb):
        v_t[:, (b + 1) * BLOCK : (b + 2) * BLOCK] = full[2, b * BLOCK : (b + 1) * BLOCK].T
    for b in range(level_1.shape[1] // BLOCK):
        v1_t[:, b * BLOCK : (b + 1) * BLOCK] = level_1[1, b * BLOCK : (b + 1) * BLOCK].T
    for b in range(level_2.shape[1] // BLOCK):
        v2_t[:, b * BLOCK : (b + 1) * BLOCK] = level_2[1, b * BLOCK : (b + 1) * BLOCK].T
    for b in range(nb):
        at = slice(b * BLOCK, (b + 1) * BLOCK)
        at_1 = slice(sibling(b) * BLOCK, (sibling(b) + 1) * BLOCK)
        at_2 = slice(0, BLOCK)
        query = full[0, at]
        scores = []
        for near in range(3):
            score = dot_nt(keys[(b + near) * BLOCK : (b + near + 1) * BLOCK], query)
            score = score * (SCALE * LOG2E)
            if b + near == 0:
                score = jnp.where(present[0], score, -jnp.inf)
            if b + near == nb + 1:
                score = jnp.where(present[1], score, -jnp.inf)
            scores.append(score)
        scores.append(dot_nt(level_1[0, at_1], spread_q[0, at]) * (SCALE * LOG2E))
        scores.append(dot_nt(level_2[0, at_2], spread_q[1, at]) * (SCALE * LOG2E))
        top = scores[0].max(0, keepdims=True)
        for score in scores[1:]:
            top = jnp.maximum(top, score.max(0, keepdims=True))
        weights = [jnp.exp2(score - top) for score in scores[:3]]
        weights.append(2.0 * jnp.exp2(scores[3] - top))
        weights.append(4.0 * jnp.exp2(scores[4] - top))
        total = weights[0].sum(0, keepdims=True)
        for weight in weights[1:]:
            total = total + weight.sum(0, keepdims=True)
        inverse = 1.0 / total
        for part, weight in enumerate(weights):
            prob[b, part * BLOCK : (part + 1) * BLOCK] = (weight * inverse).astype(BF16)
        context = dot(v_t[:, b * BLOCK : (b + 3) * BLOCK], prob[b, : 3 * BLOCK])
        context = context + dot(v1_t[:, at_1], prob[b, 3 * BLOCK : 4 * BLOCK])
        context = context + dot(v2_t[:, at_2], prob[b, 4 * BLOCK :])
        attended = context.T.astype(BF16)
        per = rows // BLOCK
        for step, out in enumerate(outs):

            @pl.when(me ^ step == b // per)
            def _():
                out[(b % per) * BLOCK : (b % per + 1) * BLOCK] = attended


def backward_kernel(nb, groups, *refs):
    full, spread_q, level_1, level_2, rim_low, rim_high, prob = refs[:7]
    chunks = refs[7 : 7 + GROUP]
    grad_q, grad_kv, sent, grads, values, k_t, k1_t, k2_t, sums, sums_1, sums_2 = refs[7 + GROUP :]
    rows = chunks[0].shape[0]
    tokens = nb * BLOCK
    me = member()
    for step, chunk in enumerate(chunks):
        grads[span(me ^ step, rows), :] = chunk[...]
    values[:BLOCK] = rim_low[1]
    values[BLOCK : BLOCK + tokens] = full[2]
    values[BLOCK + tokens :] = rim_high[1]
    k_t[:, :BLOCK] = rim_low[0].T
    k_t[:, BLOCK + tokens :] = rim_high[0].T
    for b in range(nb):
        k_t[:, (b + 1) * BLOCK : (b + 2) * BLOCK] = full[1, b * BLOCK : (b + 1) * BLOCK].T
    for b in range(level_1.shape[1] // BLOCK):
        k1_t[:, b * BLOCK : (b + 1) * BLOCK] = level_1[0, b * BLOCK : (b + 1) * BLOCK].T
    for b in range(level_2.shape[1] // BLOCK):
        k2_t[:, b * BLOCK : (b + 1) * BLOCK] = level_2[0, b * BLOCK : (b + 1) * BLOCK].T
    even_1, even_2 = averaging(1), averaging(2)
    sums[...] = jnp.zeros_like(sums)
    sums_1[...] = jnp.zeros_like(sums_1)
    sums_2[...] = jnp.zeros_like(sums_2)
    for b in range(nb):
        at = slice(b * BLOCK, (b + 1) * BLOCK)
        window = slice(b * BLOCK, (b + 3) * BLOCK)
        at_1 = slice(sibling(b) * BLOCK, (sibling(b) + 1) * BLOCK)
        at_2 = slice(0, BLOCK)
        grad = grads[at]
        slope = [
            dot_nt(values[window], grad),
            dot_nt(level_1[1, at_1], grad),
            dot_nt(level_2[1, at_2], grad),
        ]
        parts = (slice(0, 3 * BLOCK), slice(3 * BLOCK, 4 * BLOCK), slice(4 * BLOCK, 5 * BLOCK))
        delta = 0.0
        for part, s in zip(parts, slope):
            delta = delta + (prob[b, part].astype(F32) * s).sum(0, keepdims=True)
        shift = [
            (prob[b, part].astype(F32) * (s - delta)).astype(BF16) for part, s in zip(parts, slope)
        ]
        grad_t = dot(k_t[:, window], shift[0])
        for spread, key_t, s in ((even_1, k1_t[:, at_1], shift[1]), (even_2, k2_t[:, at_2], shift[2])):
            high, low = halves(dot(key_t, s))
            grad_t = grad_t + (dot(high, spread) + dot(low, spread))
        grad_q[at] = (SCALE * grad_t).T.astype(BF16)
        sums[0, window] += dot(shift[0], full[0, at])
        sums[1, window] += dot(prob[b, parts[0]], grad)
        sums_1[0, at_1] += dot(shift[1], spread_q[0, at])
        sums_1[1, at_1] += dot(prob[b, parts[1]], grad)
        sums_2[0, at_2] += dot(shift[2], spread_q[1, at])
        sums_2[1, at_2] += dot(prob[b, parts[2]], grad)
    upper = lax.axis_index("seq") >= GROUP
    for part, factor in enumerate((SCALE, 1.0)):
        spread = spreading(1)
        half = BLOCK // 2
        for b in range(nb):
            total = sums[part, (b + 1) * BLOCK : (b + 2) * BLOCK]
            high, low = halves(sums_1[part, b * half : (b + 1) * half])
            total = total + (dot(spread, high) + dot(spread, low))
            grad_kv[part, b * BLOCK : (b + 1) * BLOCK] = factor * total
        low, high = sums[part, :BLOCK], sums[part, BLOCK + tokens :]
        sent[part] = (factor * sums_2[part]).astype(BF16)
        if groups == 2:
            sent[2 + part] = (factor * jnp.where(upper, low, high)).astype(BF16)
        else:
            sent[2 + part] = (factor * high).astype(BF16)
            sent[4 + part] = (factor * low).astype(BF16)


def combine_kernel(nb, groups, *refs):
    grad_q, grad_kv, got_2, got_low, got_high = refs[:5]
    outs, (final,) = refs[5 : 5 + GROUP], refs[5 + GROUP :]
    rows = outs[0].shape[1]
    me = member()
    present = rim_present(groups)
    spread = spreading(2)
    for part in range(2):
        for b in range(nb):
            total = grad_kv[part, b * BLOCK : (b + 1) * BLOCK]
            quarter = BLOCK // 4
            total = total + dot(spread, got_2[part, b * quarter : (b + 1) * quarter])
            if b == 0:
                total = total + jnp.where(present[0], got_low[part].astype(F32), 0.0)
            if b == nb - 1:
                total = total + jnp.where(present[1], got_high[part].astype(F32), 0.0)
            final[part, b * BLOCK : (b + 1) * BLOCK] = total.astype(BF16)
    for step, out in enumerate(outs):
        at = span(me ^ step, rows)
        out[0] = grad_q[at, :]
        out[1] = final[0, at, :]
        out[2] = final[1, at, :]


def unpack_kernel(*refs):
    chunks, outs = refs[:GROUP], refs[GROUP:]
    me = member()
    for step, chunk in enumerate(chunks):
        for part, out in enumerate(outs):
            out[:, columns(me ^ step)] = chunk[part]


def grad_kernel(out_grad, out_weight, *outs):
    me = member()
    for step, out in enumerate(outs):
        weight = out_weight[span(me ^ step, HEAD_DIM), :]
        out[...] = dot_nt(out_grad[...], weight).astype(BF16)


def project_kernel(*refs):
    chunks, (out_weight, out, attended) = refs[:GROUP], refs[GROUP:]
    me = member()
    for step, chunk in enumerate(chunks):
        attended[:, columns(me ^ step)] = chunk[...]
    out[...] = dot(attended[...], out_weight[...]).astype(BF16)


def moved(x, pairs):
    return lax.ppermute(x, "seq", pairs)


def exchanged(chunks, count):
    got = [chunks[0]]
    for step in range(1, GROUP):
        got.append(moved(chunks[step], [(i, i ^ step) for i in range(count)]))
    return got


def crossed(sent, count):
    across = [(i, i ^ GROUP) for i in range(count)]
    if count == 2 * GROUP:
        got = moved(sent, across)
        return got[:2], got[2:], got[2:]
    up = [(i, i + GROUP) for i in range(count - GROUP)]
    down = [(j, i) for i, j in up]
    return moved(sent[:2], across), moved(sent[2:4], up), moved(sent[4:], down)


def per_device(queries, keys, values, out_weight, out_grad):
    rows, width = queries.shape
    assert width == GROUP * HEAD_DIM and rows == BLOCK
    count = lax.axis_size("seq")
    groups = count // GROUP
    nb = GROUP
    tokens = GROUP * rows
    assert count % (2 * GROUP) == 0

    whole_grad = lax.all_gather(out_grad, "mp", axis=0, tiled=True)
    packed = call(pack_kernel, [shape(3, rows, HEAD_DIM)] * GROUP, (queries, keys, values))
    chunks = exchanged(packed, count)
    full, spread_q, level_1, level_2, sent = call(
        functools.partial(gather_kernel, nb, groups),
        [
            shape(3, tokens, HEAD_DIM),
            shape(2, tokens, HEAD_DIM),
            shape(2, tokens // 2, HEAD_DIM),
            shape(2, tokens // 4, HEAD_DIM),
            shape(4 if groups == 2 else 6, BLOCK, HEAD_DIM),
        ],
        chunks,
    )
    other_2, rim_low, rim_high = crossed(sent, count)
    score_flops = 2 * tokens * 5 * BLOCK * HEAD_DIM
    prob, *attended = call(
        functools.partial(forward_kernel, nb, groups),
        [shape(nb, 5 * BLOCK, BLOCK)] + [shape(rows, HEAD_DIM)] * GROUP,
        (full, spread_q, level_1, other_2, rim_low, rim_high),
        scratch=[
            pltpu.VMEM((tokens + 2 * BLOCK, HEAD_DIM), BF16),
            pltpu.VMEM((HEAD_DIM, tokens + 2 * BLOCK), BF16),
            pltpu.VMEM((HEAD_DIM, tokens // 2), BF16),
            pltpu.VMEM((HEAD_DIM, tokens // 4), BF16),
        ],
        flops=2 * score_flops,
    )
    grad_chunks = call(
        grad_kernel,
        [shape(rows, HEAD_DIM)] * GROUP,
        (whole_grad, out_weight),
        flops=2 * rows * out_weight.size,
    )
    grad_chunks = exchanged(grad_chunks, count)
    attended = exchanged(attended, count)
    (partial_mixed,) = call(
        project_kernel,
        [shape(rows, out_weight.shape[1])],
        (*attended, out_weight),
        scratch=[pltpu.VMEM((rows, width), BF16)],
        flops=2 * rows * out_weight.size,
    )
    mixed = lax.psum_scatter(partial_mixed, "mp", scatter_dimension=0, tiled=True)
    grad_q, grad_kv, sent = call(
        functools.partial(backward_kernel, nb, groups),
        [
            shape(tokens, HEAD_DIM),
            shape(2, tokens, HEAD_DIM, dtype=F32),
            shape(4 if groups == 2 else 6, BLOCK, HEAD_DIM),
        ],
        (full, spread_q, level_1, other_2, rim_low, rim_high, prob, *grad_chunks),
        scratch=[
            pltpu.VMEM((tokens, HEAD_DIM), BF16),
            pltpu.VMEM((tokens + 2 * BLOCK, HEAD_DIM), BF16),
            pltpu.VMEM((HEAD_DIM, tokens + 2 * BLOCK), BF16),
            pltpu.VMEM((HEAD_DIM, tokens // 2), BF16),
            pltpu.VMEM((HEAD_DIM, tokens // 4), BF16),
            pltpu.VMEM((2, tokens + 2 * BLOCK, HEAD_DIM), F32),
            pltpu.VMEM((2, tokens // 2, HEAD_DIM), F32),
            pltpu.VMEM((2, tokens // 4, HEAD_DIM), F32),
        ],
        flops=4 * score_flops,
    )
    got_2, got_low, got_high = crossed(sent, count)
    final = call(
        functools.partial(combine_kernel, nb, groups),
        [shape(3, rows, HEAD_DIM)] * GROUP,
        (grad_q, grad_kv, got_2, got_low, got_high),
        scratch=[pltpu.VMEM((2, tokens, HEAD_DIM), BF16)],
    )
    grads = call(unpack_kernel, [shape(rows, width)] * 3, exchanged(final, count))
    return (mixed, *grads)


def solution(mesh):
    return jax.shard_map(
        per_device,
        mesh=mesh,
        in_specs=(
            P("seq", "mp"),
            P("seq", "mp"),
            P("seq", "mp"),
            P("mp", None),
            P(("seq", "mp"), None),
        ),
        out_specs=(P(("seq", "mp"), None), P("seq", "mp"), P("seq", "mp"), P("seq", "mp")),
        check_vma=False,
    )
```

time: 206 us -> 101 us (0.49)
  local copies, waits for them, and re-layouts: 56 us -> 5.59 us
  other arithmetic: 41 us -> 0 us
  matrix products: 21.9 us -> 0 us
  Pallas kernels: 0 us -> 15.5 us
  starting transfers between devices: 28.5 us -> 20.9 us
    dot_general x20 -> x0, matrix products: 21.9 us -> none  [the longest x1 3.19 us: per_device(): jnp.einsum('nthd,nshd->nhts', grad_blocks, near_values, preferred_element...]
    pallas_call x0 -> x8, Pallas kernels: none -> 15.5 us  [call(): pl.pallas_call(kernel, out_shape=out_shape, in_specs=[whole] * len(args),...]
    convert_element_type x15 -> x0, other arithmetic: 11.3 us -> none  [the longest x2 3.17 us: pool_rows(): rows.astype(jnp.float32).reshape(rows.shape[0] // 2, 2, rows.shape[1])]
    reduce_sum x6 -> x0, other arithmetic: 10.8 us -> none  [the longest x2 4.58 us: per_device(): total = total + flat_rows(weight.sum(-1))]
    broadcast_in_dim x14 -> x0, local copies, waits for them, and re-layouts: 8.72 us -> none  [the longest x8 6.75 us: per_device(): jnp.repeat(scores.max(-1), 2 ** level, axis=2)]
    slice x10 -> x2, local copies, waits for them, and re-layouts: 8.11 us -> 0.04 us  [crossed(): return (got[:2], got[2:], got[2:])]
    ppermute x14, starting transfers between devices: 28.3 us -> 20.8 us  [moved(): return lax.ppermute(x, 'seq', pairs)]
    reshape x7 -> x0, local copies, waits for them, and re-layouts: 7.38 us -> none  [the longest x1 3.04 us: per_device(): value_window.reshape(blocks_here, 3 * block, width)]
  transfers between devices with their start and end apart: 16 -> 16, of which waited for: 5 -> 13; matrix products, arithmetic and copies ran while one was open for 56% -> 0% of each run, Pallas kernels for 0% -> 15%
where the time goes in v1:
time: 101 us
  waiting for transfers between devices  44.4 us (44%)
  starting transfers between devices  20.9 us (21%)
  Pallas kernels  15.5 us (15%)
  between operations  14.1 us (14%)
  local copies, waits for them, and re-layouts  5.59 us (6%)
    ppermute x14, waiting for transfers between devices, moved(): return lax.ppermute(x, 'seq', pairs)  43.7 us
    ppermute x14, starting transfers between devices, moved(): return lax.ppermute(x, 'seq', pairs)  20.8 us
    pallas_call x8, Pallas kernels, call(): pl.pallas_call(kernel, out_shape=out_shape, in_specs=[whole] * len(args),...  15.5 us
    unnamed x18, local copies, waits for them, and re-layouts  5.56 us
  transfers between devices with their start and end apart: 16, of which 13 were waited for; matrix products, arithmetic and copies ran while one was open for 0% of the time, Pallas kernels for 15%

profile of v1, /device:TPU:0, one launch (start us, length us, event | category | flops | bytes accessed | tf_op | source)
XLA Modules:
  0.0 100.5 jit_solution(16734703792856744793)
XLA Ops:
  10.9 3.0 %collective-permute-start = (bf16[3,256,128]{2,1,0:T(8,128)(2,1)S(1)}, bf16[3,256,128]{2,1,0:T(8,128)(2,1)S(1)}, u32[]{:S(2)}, u32[]{:S(2)}) collective-permute-start(bf16[3,256,128]{2,1,0:T(8,128)(2,1)S(1)} %get-tuple-element.32), channel_id=1, source_target_pairs={{0,4},{4,0},{8,12},{12,8},{16,20},{20,16},{24,28},{28,24},{1,5},{5... | collective-permute-start | bytes 589832 | tf_op jit(solution)/shard_map/ppermute | solution.py:306
  14.0 1.6 %collective-permute-start.1 = (bf16[3,256,128]{2,1,0:T(8,128)(2,1)S(1)}, bf16[3,256,128]{2,1,0:T(8,128)(2,1)S(1)}, u32[]{:S(2)}, u32[]{:S(2)}) collective-permute-start(bf16[3,256,128]{2,1,0:T(8,128)(2,1)S(1)} %get-tuple-element.33), channel_id=1, source_target_pairs={{0,8},{4,12},{8,0},{12,4},{16,24},{20,28},{24,16},{28,20},{1,9},{5... | collective-permute-start | bytes 589832 | tf_op jit(solution)/shard_map/ppermute | solution.py:306
  15.6 3.3 %collective-permute-done.refs_1_ = bf16[3,256,128]{2,1,0:T(8,128)(2,1)S(1)} collective-permute-done((bf16[3,256,128]{2,1,0:T(8,128)(2,1)S(1)}, bf16[3,256,128]{2,1,0:T(8,128)(2,1)S(1)}, u32[]{:S(2)}, u32[]{:S(2)}) %collective-permute-start) | collective-permute-done | bytes 196640 | tf_op jit(solution)/shard_map/ppermute | solution.py:306
  18.9 2.9 %collective-permute-done.1.refs_2_ = bf16[3,256,128]{2,1,0:T(8,128)(2,1)S(1)} collective-permute-done((bf16[3,256,128]{2,1,0:T(8,128)(2,1)S(1)}, bf16[3,256,128]{2,1,0:T(8,128)(2,1)S(1)}, u32[]{:S(2)}, u32[]{:S(2)}) %collective-permute-start.1) | collective-permute-done | bytes 196640 | tf_op jit(solution)/shard_map/ppermute | solution.py:306
  21.8 2.5 %collective-permute-done.2.refs_3_ = bf16[3,256,128]{2,1,0:T(8,128)(2,1)S(1)} collective-permute-done((bf16[3,256,128]{2,1,0:T(8,128)(2,1)S(1)}, bf16[3,256,128]{2,1,0:T(8,128)(2,1)S(1)}, u32[]{:S(2)}, u32[]{:S(2)}) %collective-permute-start.2) | collective-permute-done | bytes 196640 | tf_op jit(solution)/shard_map/ppermute | solution.py:306
  24.4 1.7 %shard_map.85 = (bf16[3,1024,128]{2,1,0:T(8,128)(2,1)S(1)}, bf16[2,1024,128]{2,1,0:T(8,128)(2,1)S(1)}, bf16[2,512,128]{2,1,0:T(8,128)(2,1)S(1)}, bf16[2,256,128]{2,1,0:T(8,128)(2,1)}, bf16[4,256,128]{2,1,0:T(8,128)(2,1)S(1)}) custom-call(bf16[3,256,128]{2,1,0:T(8,128)(2,1)S(1)} %get-tuple-element.31.refs_0_, ...), custom_call_target="tpu_custom_call" | custom-call | bytes 2752512 | tf_op jit(solution)/shard_map/pallas_call | solution.py:35
  26.0 2.7 %collective-permute-start.3 = (bf16[4,256,128]{2,1,0:T(8,128)(2,1)S(1)}, bf16[4,256,128]{2,1,0:T(8,128)(2,1)S(1)}, u32[]{:S(2)}, u32[]{:S(2)}) collective-permute-start(bf16[4,256,128]{2,1,0:T(8,128)(2,1)S(1)} %get-tuple-element.38), channel_id=1, source_target_pairs={{0,16},{4,20},{8,24},{12,28},{16,0},{20,4},{24,8},{28,12},{1,17},{... | collective-permute-start | bytes 786440 | tf_op jit(solution)/shard_map/ppermute | solution.py:306
  28.8 11.0 %collective-permute-done.3 = bf16[4,256,128]{2,1,0:T(8,128)(2,1)S(1)} collective-permute-done((bf16[4,256,128]{2,1,0:T(8,128)(2,1)S(1)}, bf16[4,256,128]{2,1,0:T(8,128)(2,1)S(1)}, u32[]{:S(2)}, u32[]{:S(2)}) %collective-permute-start.3) | collective-permute-done | bytes 262176 | tf_op jit(solution)/shard_map/ppermute | solution.py:306
  39.7 4.8 %shard_map.86 = (bf16[4,1280,256]{2,1,0:T(8,128)(2,1)S(1)}, bf16[256,128]{1,0:T(8,128)(2,1)S(1)}, bf16[256,128]{1,0:T(8,128)(2,1)S(1)}, bf16[256,128]{1,0:T(8,128)(2,1)S(1)}, bf16[256,128]{1,0:T(8,128)(2,1)S(1)}) custom-call(bf16[3,1024,128]{2,1,0:T(8,128)(2,1)S(1)} %get-tuple-element.35.refs_0_, bf16[2,1024,128]{2,1,0:T(8,128)(2,1)S(1)} %get-tuple-element.36.refs_1_, ...), custom_call_target="tpu_custom_call" | custom-call | flops 671088640 | bytes 4849664 | tf_op jit(solution)/shard_map/pallas_call | solution.py:35
  44.5 1.5 %copy-done.7 = bf16[4,1280,256]{2,1,0:T(8,128)(2,1)} copy-done((bf16[4,1280,256]{2,1,0:T(8,128)(2,1)}, bf16[4,1280,256]{2,1,0:T(8,128)(2,1)S(1)}, u32[]{:S(2)}) %copy-start.7) | copy-done | bytes 2621464
  48.0 1.5 %collective-permute-start.6 = (bf16[256,128]{1,0:T(8,128)(2,1)S(1)}, bf16[256,128]{1,0:T(8,128)(2,1)S(1)}, u32[]{:S(2)}, u32[]{:S(2)}) collective-permute-start(bf16[256,128]{1,0:T(8,128)(2,1)S(1)} %get-tuple-element.42), channel_id=1, source_target_pairs={{0,12},{4,8},{8,4},{12,0},{16,28},{20,24},{24,20},{28,16},{1,13},{... | collective-permute-start | bytes 196616 | tf_op jit(solution)/shard_map/ppermute | solution.py:306
  50.3 1.4 %collective-permute-done.5.refs_2_ = bf16[256,128]{1,0:T(8,128)(2,1)S(1)} collective-permute-done((bf16[256,128]{1,0:T(8,128)(2,1)S(1)}, bf16[256,128]{1,0:T(8,128)(2,1)S(1)}, u32[]{:S(2)}, u32[]{:S(2)}) %collective-permute-start.5) | collective-permute-done | bytes 65568 | tf_op jit(solution)/shard_map/ppermute | solution.py:306
  51.6 1.6 %collective-permute-done.6.refs_3_ = bf16[256,128]{1,0:T(8,128)(2,1)S(1)} collective-permute-done((bf16[256,128]{1,0:T(8,128)(2,1)S(1)}, bf16[256,128]{1,0:T(8,128)(2,1)S(1)}, u32[]{:S(2)}, u32[]{:S(2)}) %collective-permute-start.6) | collective-permute-done | bytes 65568 | tf_op jit(solution)/shard_map/ppermute | solution.py:306
  53.2 1.7 %shard_map.87 = bf16[256,2048]{1,0:T(8,128)(2,1)} custom-call(bf16[256,128]{1,0:T(8,128)(2,1)S(1)} %get-tuple-element.39.refs_0_, bf16[256,128]{1,0:T(8,128)(2,1)S(1)} %collective-permute-done.4.refs_1_, bf16[256,128]{1,0:T(8,128)(2,1)S(1)} %collective-permute-done.5.refs_2_, bf16[256,128]{1,0:T(8,128)(2,1)S(1)} %collective-permute-done.6.refs_3_, ...), custom_call_target="tpu_custom_call" | custom-call | flops 536870912 | bytes 3407872 | tf_op jit(solution)/shard_map/pallas_call | solution.py:35
  58.1 1.4 %collective-permute-start.8 = (bf16[256,128]{1,0:T(8,128)(2,1)S(1)}, bf16[256,128]{1,0:T(8,128)(2,1)S(1)}, u32[]{:S(2)}, u32[]{:S(2)}) collective-permute-start(bf16[256,128]{1,0:T(8,128)(2,1)S(1)} %get-tuple-element.46), channel_id=1, source_target_pairs={{0,8},{4,12},{8,0},{12,4},{16,24},{20,28},{24,16},{28,20},{1,9},{5... | collective-permute-start | bytes 196616 | tf_op jit(solution)/shard_map/ppermute | solution.py:306
  59.6 1.5 %collective-permute-start.9 = (bf16[256,128]{1,0:T(8,128)(2,1)S(1)}, bf16[256,128]{1,0:T(8,128)(2,1)S(1)}, u32[]{:S(2)}, u32[]{:S(2)}) collective-permute-start(bf16[256,128]{1,0:T(8,128)(2,1)S(1)} %get-tuple-element.47), channel_id=1, source_target_pairs={{0,12},{4,8},{8,4},{12,0},{16,28},{20,24},{24,20},{28,16},{1,13},{... | collective-permute-start | bytes 196616 | tf_op jit(solution)/shard_map/ppermute | solution.py:306
  62.4 2.3 %collective-permute-done.9.refs_10_ = bf16[256,128]{1,0:T(8,128)(2,1)S(1)} collective-permute-done((bf16[256,128]{1,0:T(8,128)(2,1)S(1)}, bf16[256,128]{1,0:T(8,128)(2,1)S(1)}, u32[]{:S(2)}, u32[]{:S(2)}) %collective-permute-start.9) | collective-permute-done | bytes 65568 | tf_op jit(solution)/shard_map/ppermute | solution.py:306
  64.7 4.6 %shard_map.89 = (bf16[1024,128]{1,0:T(8,128)(2,1)S(1)}, f32[2,1024,128]{2,1,0:T(8,128)S(1)}, bf16[4,256,128]{2,1,0:T(8,128)(2,1)S(1)}) custom-call(bf16[3,1024,128]{2,1,0:T(8,128)(2,1)S(1)} %get-tuple-element.35.refs_0_, bf16[2,1024,128]{2,1,0:T(8,128)(2,1)S(1)} %copy-done.6, bf16[2,512,128]{2,1,0:T(8,128)(2,1)S(1)} %get-tuple-element.37.refs_2_, ...), custom_call_target="tpu_custom_call" | custom-call | flops 1342177280 | bytes 6422528 | tf_op jit(solution)/shard_map/pallas_call | solution.py:35
  69.4 2.9 %collective-permute-start.10 = (bf16[4,256,128]{2,1,0:T(8,128)(2,1)S(1)}, bf16[4,256,128]{2,1,0:T(8,128)(2,1)S(1)}, u32[]{:S(2)}, u32[]{:S(2)}) collective-permute-start(bf16[4,256,128]{2,1,0:T(8,128)(2,1)S(1)} %get-tuple-element.50), channel_id=1, source_target_pairs={{0,16},{4,20},{8,24},{12,28},{16,0},{20,4},{24,8},{28,12},{1,17},{... | collective-permute-start | bytes 786440 | tf_op jit(solution)/shard_map/ppermute | solution.py:306
  72.2 8.9 %collective-permute-done.10 = bf16[4,256,128]{2,1,0:T(8,128)(2,1)S(1)} collective-permute-done((bf16[4,256,128]{2,1,0:T(8,128)(2,1)S(1)}, bf16[4,256,128]{2,1,0:T(8,128)(2,1)S(1)}, u32[]{:S(2)}, u32[]{:S(2)}) %collective-permute-start.10) | collective-permute-done | bytes 262176 | tf_op jit(solution)/shard_map/ppermute | solution.py:306
  83.3 1.7 %collective-permute-start.13 = (bf16[3,256,128]{2,1,0:T(8,128)(2,1)S(1)}, bf16[3,256,128]{2,1,0:T(8,128)(2,1)S(1)}, u32[]{:S(2)}, u32[]{:S(2)}) collective-permute-start(bf16[3,256,128]{2,1,0:T(8,128)(2,1)S(1)} %get-tuple-element.54), channel_id=1, source_target_pairs={{0,12},{4,8},{8,4},{12,0},{16,28},{20,24},{24,20},{28,16},{1,13},{... | collective-permute-start | bytes 589832 | tf_op jit(solution)/shard_map/ppermute | solution.py:306
  85.1 3.4 %collective-permute-done.11.refs_1_ = bf16[3,256,128]{2,1,0:T(8,128)(2,1)S(1)} collective-permute-done((bf16[3,256,128]{2,1,0:T(8,128)(2,1)S(1)}, bf16[3,256,128]{2,1,0:T(8,128)(2,1)S(1)}, u32[]{:S(2)}, u32[]{:S(2)}) %collective-permute-start.11) | collective-permute-done | bytes 196640 | tf_op jit(solution)/shard_map/ppermute | solution.py:306
  88.5 1.5 %collective-permute-done.12.refs_2_ = bf16[3,256,128]{2,1,0:T(8,128)(2,1)S(1)} collective-permute-done((bf16[3,256,128]{2,1,0:T(8,128)(2,1)S(1)}, bf16[3,256,128]{2,1,0:T(8,128)(2,1)S(1)}, u32[]{:S(2)}, u32[]{:S(2)}) %collective-permute-start.12) | collective-permute-done | bytes 196640 | tf_op jit(solution)/shard_map/ppermute | solution.py:306
  90.0 2.7 %collective-permute-done.13.refs_3_ = bf16[3,256,128]{2,1,0:T(8,128)(2,1)S(1)} collective-permute-done((bf16[3,256,128]{2,1,0:T(8,128)(2,1)S(1)}, bf16[3,256,128]{2,1,0:T(8,128)(2,1)S(1)}, u32[]{:S(2)}, u32[]{:S(2)}) %collective-permute-start.13) | collective-permute-done | bytes 196640 | tf_op jit(solution)/shard_map/ppermute | solution.py:306
  (38 shorter events, 14.3 us)
Async XLA Ops:
  7.2 46.1 %copy-start = (bf16[512,2048]{1,0:T(8,128)(2,1)S(1)}, bf16[512,2048]{1,0:T(8,128)(2,1)}, u32[]{:S(2)}) copy-start(bf16[512,2048]{1,0:T(8,128)(2,1)} %out_weight.1) | copy-start | bytes 6291460
  7.2 47.8 %all-gather.2.cloned.1.call-start = ((), (), s32[]{:S(2)}) async-start(), calls=%async_computation.2 | async-start | bytes 1310720 | tf_op jit(solution)/shard_map/all_gather | solution.py:335
  7.9 85.8 %reduce-scatter.2.cloned.1.call-start = ((), (), s32[]{:S(2)}) async-start(), calls=%async_computation.1 | async-start | bytes 1310720 | tf_op jit(solution)/shard_map/reduce_scatter | solution.py:378
  8.0 1.0 copy-start.2
  8.9 0.9 copy-start.3
  10.9 7.9 %collective-permute-start = (bf16[3,256,128]{2,1,0:T(8,128)(2,1)S(1)}, bf16[3,256,128]{2,1,0:T(8,128)(2,1)S(1)}, u32[]{:S(2)}, u32[]{:S(2)}) collective-permute-start(bf16[3,256,128]{2,1,0:T(8,128)(2,1)S(1)} %get-tuple-element.32), channel_id=1, source_target_pairs={{0,4},{4,0},{8,12},{12,8},{16,20},{20,16},{24,28},{28,24},{1,5},{5... | collective-permute-start | bytes 589832 | tf_op jit(solution)/shard_map/ppermute | solution.py:306
  14.0 7.8 %collective-permute-start.1 = (bf16[3,256,128]{2,1,0:T(8,128)(2,1)S(1)}, bf16[3,256,128]{2,1,0:T(8,128)(2,1)S(1)}, u32[]{:S(2)}, u32[]{:S(2)}) collective-permute-start(bf16[3,256,128]{2,1,0:T(8,128)(2,1)S(1)} %get-tuple-element.33), channel_id=1, source_target_pairs={{0,8},{4,12},{8,0},{12,4},{16,24},{20,28},{24,16},{28,20},{1,9},{5... | collective-permute-start | bytes 589832 | tf_op jit(solution)/shard_map/ppermute | solution.py:306
  15.6 8.8 %collective-permute-start.2 = (bf16[3,256,128]{2,1,0:T(8,128)(2,1)S(1)}, bf16[3,256,128]{2,1,0:T(8,128)(2,1)S(1)}, u32[]{:S(2)}, u32[]{:S(2)}) collective-permute-start(bf16[3,256,128]{2,1,0:T(8,128)(2,1)S(1)} %get-tuple-element.34), channel_id=1, source_target_pairs={{0,12},{4,8},{8,4},{12,0},{16,28},{20,24},{24,20},{28,16},{1,13},{... | collective-permute-start | bytes 589832 | tf_op jit(solution)/shard_map/ppermute | solution.py:306
  26.0 27.2 %copy-start.5 = (bf16[2,1024,128]{2,1,0:T(8,128)(2,1)}, bf16[2,1024,128]{2,1,0:T(8,128)(2,1)S(1)}, u32[]{:S(2)}) copy-start(bf16[2,1024,128]{2,1,0:T(8,128)(2,1)S(1)} %get-tuple-element.36.refs_1_) | copy-start | bytes 1572868
  26.0 13.7 %collective-permute-start.3 = (bf16[4,256,128]{2,1,0:T(8,128)(2,1)S(1)}, bf16[4,256,128]{2,1,0:T(8,128)(2,1)S(1)}, u32[]{:S(2)}, u32[]{:S(2)}) collective-permute-start(bf16[4,256,128]{2,1,0:T(8,128)(2,1)S(1)} %get-tuple-element.38), channel_id=1, source_target_pairs={{0,16},{4,20},{8,24},{12,28},{16,0},{20,4},{24,8},{28,12},{1,17},{... | collective-permute-start | bytes 786440 | tf_op jit(solution)/shard_map/ppermute | solution.py:306
  44.5 1.5 %copy-start.7 = (bf16[4,1280,256]{2,1,0:T(8,128)(2,1)}, bf16[4,1280,256]{2,1,0:T(8,128)(2,1)S(1)}, u32[]{:S(2)}) copy-start(bf16[4,1280,256]{2,1,0:T(8,128)(2,1)S(1)} %get-tuple-element.43.refs_6_) | copy-start | bytes 7864324
  46.0 4.3 %collective-permute-start.4 = (bf16[256,128]{1,0:T(8,128)(2,1)S(1)}, bf16[256,128]{1,0:T(8,128)(2,1)S(1)}, u32[]{:S(2)}, u32[]{:S(2)}) collective-permute-start(bf16[256,128]{1,0:T(8,128)(2,1)S(1)} %get-tuple-element.40), channel_id=1, source_target_pairs={{0,4},{4,0},{8,12},{12,8},{16,20},{20,16},{24,28},{28,24},{1,5},{5... | collective-permute-start | bytes 196616 | tf_op jit(solution)/shard_map/ppermute | solution.py:306
  47.4 4.3 %collective-permute-start.5 = (bf16[256,128]{1,0:T(8,128)(2,1)S(1)}, bf16[256,128]{1,0:T(8,128)(2,1)S(1)}, u32[]{:S(2)}, u32[]{:S(2)}) collective-permute-start(bf16[256,128]{1,0:T(8,128)(2,1)S(1)} %get-tuple-element.41), channel_id=1, source_target_pairs={{0,8},{4,12},{8,0},{12,4},{16,24},{20,28},{24,16},{28,20},{1,9},{5... | collective-permute-start | bytes 196616 | tf_op jit(solution)/shard_map/ppermute | solution.py:306
  48.0 5.2 %collective-permute-start.6 = (bf16[256,128]{1,0:T(8,128)(2,1)S(1)}, bf16[256,128]{1,0:T(8,128)(2,1)S(1)}, u32[]{:S(2)}, u32[]{:S(2)}) collective-permute-start(bf16[256,128]{1,0:T(8,128)(2,1)S(1)} %get-tuple-element.42), channel_id=1, source_target_pairs={{0,12},{4,8},{8,4},{12,0},{16,28},{20,24},{24,20},{28,16},{1,13},{... | collective-permute-start | bytes 196616 | tf_op jit(solution)/shard_map/ppermute | solution.py:306
  55.0 1.2 %copy-start.1 = (bf16[256,2048]{1,0:T(8,128)(2,1)S(1)}, bf16[256,2048]{1,0:T(8,128)(2,1)}, u32[]{:S(2)}) copy-start(bf16[256,2048]{1,0:T(8,128)(2,1)} %all-gather.2.cloned.1.call-done.out_grad) | copy-start | bytes 3145732
  56.2 8.5 %copy-start.6 = (bf16[2,1024,128]{2,1,0:T(8,128)(2,1)S(1)}, bf16[2,1024,128]{2,1,0:T(8,128)(2,1)}, u32[]{:S(2)}) copy-start(bf16[2,1024,128]{2,1,0:T(8,128)(2,1)} %copy-done.5) | copy-start | bytes 1572868
  56.2 8.5 %copy-start.8 = (bf16[4,1280,256]{2,1,0:T(8,128)(2,1)S(1)}, bf16[4,1280,256]{2,1,0:T(8,128)(2,1)}, u32[]{:S(2)}) copy-start(bf16[4,1280,256]{2,1,0:T(8,128)(2,1)} %copy-done.7) | copy-start | bytes 7864324
  57.5 4.9 %collective-permute-start.7 = (bf16[256,128]{1,0:T(8,128)(2,1)S(1)}, bf16[256,128]{1,0:T(8,128)(2,1)S(1)}, u32[]{:S(2)}, u32[]{:S(2)}) collective-permute-start(bf16[256,128]{1,0:T(8,128)(2,1)S(1)} %get-tuple-element.45), channel_id=1, source_target_pairs={{0,4},{4,0},{8,12},{12,8},{16,20},{20,16},{24,28},{28,24},{1,5},{5... | collective-permute-start | bytes 196616 | tf_op jit(solution)/shard_map/ppermute | solution.py:306
  58.1 4.3 %collective-permute-start.8 = (bf16[256,128]{1,0:T(8,128)(2,1)S(1)}, bf16[256,128]{1,0:T(8,128)(2,1)S(1)}, u32[]{:S(2)}, u32[]{:S(2)}) collective-permute-start(bf16[256,128]{1,0:T(8,128)(2,1)S(1)} %get-tuple-element.46), channel_id=1, source_target_pairs={{0,8},{4,12},{8,0},{12,4},{16,24},{20,28},{24,16},{28,20},{1,9},{5... | collective-permute-start | bytes 196616 | tf_op jit(solution)/shard_map/ppermute | solution.py:306
  59.6 5.2 %collective-permute-start.9 = (bf16[256,128]{1,0:T(8,128)(2,1)S(1)}, bf16[256,128]{1,0:T(8,128)(2,1)S(1)}, u32[]{:S(2)}, u32[]{:S(2)}) collective-permute-start(bf16[256,128]{1,0:T(8,128)(2,1)S(1)} %get-tuple-element.47), channel_id=1, source_target_pairs={{0,12},{4,8},{8,4},{12,0},{16,28},{20,24},{24,20},{28,16},{1,13},{... | collective-permute-start | bytes 196616 | tf_op jit(solution)/shard_map/ppermute | solution.py:306
  69.4 11.8 %collective-permute-start.10 = (bf16[4,256,128]{2,1,0:T(8,128)(2,1)S(1)}, bf16[4,256,128]{2,1,0:T(8,128)(2,1)S(1)}, u32[]{:S(2)}, u32[]{:S(2)}) collective-permute-start(bf16[4,256,128]{2,1,0:T(8,128)(2,1)S(1)} %get-tuple-element.50), channel_id=1, source_target_pairs={{0,16},{4,20},{8,24},{12,28},{16,0},{20,4},{24,8},{28,12},{1,17},{... | collective-permute-start | bytes 786440 | tf_op jit(solution)/shard_map/ppermute | solution.py:306
  81.5 7.0 %collective-permute-start.11 = (bf16[3,256,128]{2,1,0:T(8,128)(2,1)S(1)}, bf16[3,256,128]{2,1,0:T(8,128)(2,1)S(1)}, u32[]{:S(2)}, u32[]{:S(2)}) collective-permute-start(bf16[3,256,128]{2,1,0:T(8,128)(2,1)S(1)} %get-tuple-element.52), channel_id=1, source_target_pairs={{0,4},{4,0},{8,12},{12,8},{16,20},{20,16},{24,28},{28,24},{1,5},{5... | collective-permute-start | bytes 589832 | tf_op jit(solution)/shard_map/ppermute | solution.py:306
  82.7 7.3 %collective-permute-start.12 = (bf16[3,256,128]{2,1,0:T(8,128)(2,1)S(1)}, bf16[3,256,128]{2,1,0:T(8,128)(2,1)S(1)}, u32[]{:S(2)}, u32[]{:S(2)}) collective-permute-start(bf16[3,256,128]{2,1,0:T(8,128)(2,1)S(1)} %get-tuple-element.53), channel_id=1, source_target_pairs={{0,8},{4,12},{8,0},{12,4},{16,24},{20,28},{24,16},{28,20},{1,9},{5... | collective-permute-start | bytes 589832 | tf_op jit(solution)/shard_map/ppermute | solution.py:306
  83.3 9.3 %collective-permute-start.13 = (bf16[3,256,128]{2,1,0:T(8,128)(2,1)S(1)}, bf16[3,256,128]{2,1,0:T(8,128)(2,1)S(1)}, u32[]{:S(2)}, u32[]{:S(2)}) collective-permute-start(bf16[3,256,128]{2,1,0:T(8,128)(2,1)S(1)} %get-tuple-element.54), channel_id=1, source_target_pairs={{0,12},{4,8},{8,4},{12,0},{16,28},{20,24},{24,20},{28,16},{1,13},{... | collective-permute-start | bytes 589832 | tf_op jit(solution)/shard_map/ppermute | solution.py:306
  (1 other events, 0.9 us)
Sparse Core Ops, SparseCore 0:
  9.6 19.4 all-gather.1
  55.1 25.2 reduce-scatter.1

commit v2 on v1

v2 whole, which is shorter than its diff:
```python
import functools

import jax
import jax.numpy as jnp
from jax import lax
from jax.experimental import pallas as pl
from jax.experimental.pallas import tpu as pltpu
from jax.sharding import PartitionSpec as P

HEAD_DIM = 128
BLOCK = 256
LEVELS = 2
GROUP = 4
N_MP = 4
SCALE = HEAD_DIM**-0.5
LOG2E = 1.4426950408889634
BF16 = jnp.bfloat16
F32 = jnp.float32


def dot(a, b):
    return lax.dot_general(a, b, (((1,), (0,)), ((), ())), preferred_element_type=F32)


def dot_nt(a, b):
    return lax.dot_general(a, b, (((1,), (1,)), ((), ())), preferred_element_type=F32)


def shape(*dims, dtype=BF16):
    return jax.ShapeDtypeStruct(dims, dtype)


def call(kernel, out_shape, args, scratch=(), flops=0, limit=32, space=pltpu.VMEM):
    whole = pl.BlockSpec(memory_space=pltpu.VMEM)
    moved = sum(x.size * x.dtype.itemsize for x in (*args, *out_shape))
    return pl.pallas_call(
        kernel,
        out_shape=out_shape,
        in_specs=[pl.BlockSpec(memory_space=space)] * len(args),
        out_specs=[whole] * len(out_shape),
        scratch_shapes=scratch,
        compiler_params=pltpu.CompilerParams(vmem_limit_bytes=limit << 20),
        cost_estimate=pl.CostEstimate(flops=flops, bytes_accessed=moved, transcendentals=0),
    )(*args)


def member():
    return lax.rem(lax.axis_index("seq"), GROUP)


def columns(index):
    return pl.ds(pl.multiple_of(index * HEAD_DIM, HEAD_DIM), HEAD_DIM)


def span(index, size):
    return pl.ds(pl.multiple_of(index * size, size), size)


def iota(dims, axis):
    return lax.broadcasted_iota(jnp.int32, dims, axis)


def averaging(level):
    dims = (BLOCK, BLOCK)
    same = (iota(dims, 0) >> level) == (iota(dims, 1) >> level)
    return jnp.where(same, 2.0**-level, 0.0).astype(BF16)


def pooling():
    dims = (BLOCK // 2, BLOCK)
    return jnp.where(iota(dims, 0) == (iota(dims, 1) >> 1), 0.5, 0.0).astype(BF16)


def spreading(level):
    dims = (BLOCK, BLOCK >> level)
    return jnp.where((iota(dims, 0) >> level) == iota(dims, 1), 2.0**-level, 0.0).astype(BF16)


def halves(x):
    high = x.astype(BF16)
    return high, (x - high.astype(F32)).astype(BF16)


def pack_kernel(q, k, v, *refs):
    chunks, rims, tops = refs[:GROUP], refs[GROUP : 2 * GROUP], refs[2 * GROUP : 3 * GROUP]
    held, sems = refs[3 * GROUP :]
    me = member()
    copies = [
        pltpu.make_async_copy(source, held.at[part], sems.at[part])
        for part, source in enumerate((q, k, v))
    ]
    for copy in copies:
        copy.start()
    pool = pooling()
    half = BLOCK // 2
    for part, copy in enumerate(copies):
        copy.wait()
        for step in range(GROUP):
            chunks[step][part] = held[part, :, columns(me ^ step)]
            if part:
                rims[step][part - 1] = held[part, :, columns(me ^ step)]
        if part:
            once = dot(pool, held[part]).astype(BF16)
            held[part, :half] = once
            held[part, half : half + half // 2] = dot(pool[: half // 2, :half], once).astype(BF16)
            for step in range(GROUP):
                tops[step][part - 1] = held[part, half : half + half // 2, columns(me ^ step)]


def sibling(b):
    return (b >> 1) ^ 1


def rim_present(groups):
    group = lax.axis_index("seq") // GROUP
    return group > 0, group < groups - 1


def picked(out, index, refs):
    for step, ref in enumerate(refs):

        @pl.when(index == step)
        def _():
            out[...] = ref[...]


def forward_kernel(nb, groups, *refs):
    chunks, tops, refs = refs[:GROUP], refs[GROUP : 2 * GROUP], refs[2 * GROUP :]
    lows, refs = refs[:GROUP], refs[GROUP:]
    highs = lows
    if groups > 2:
        highs, refs = refs[:GROUP], refs[GROUP:]
    query, near, level_1, level_2, prob, *outs, rim_low, rim_high, v_t, v1_t, v2_t = refs
    tokens = nb * BLOCK
    me = member()
    present = rim_present(groups)
    for step, chunk in enumerate(chunks):
        query[0, span(me ^ step, BLOCK), :] = chunk[0]
        near[:, pl.ds(pl.multiple_of((me ^ step) * BLOCK + BLOCK, BLOCK), BLOCK), :] = chunk[1:]
    quarter = BLOCK // 4
    for step, chunk in enumerate(tops):
        level_2[:, span(me ^ step, quarter), :] = chunk[...]
    if groups > 2:
        picked(rim_low, me ^ 3, lows)
        picked(rim_high, me, highs)
    else:
        picked(rim_low, jnp.where(present[0], me ^ 3, me), lows)
        rim_high = rim_low
    near[:, :BLOCK] = rim_low[...]
    near[:, BLOCK + tokens :] = rim_high[...]
    pool, even_1, even_2 = pooling(), averaging(1), averaging(2)
    half = BLOCK // 2
    for b in range(nb):
        at = slice(b * BLOCK, (b + 1) * BLOCK)
        once = dot(even_1, query[0, at]).astype(BF16)
        query[1, at] = once
        query[2, at] = dot(even_2, once).astype(BF16)
        for part in range(2):
            block = near[part, (b + 1) * BLOCK : (b + 2) * BLOCK]
            level_1[part, b * half : (b + 1) * half] = dot(pool, block).astype(BF16)
    for b in range(nb + 2):
        v_t[:, b * BLOCK : (b + 1) * BLOCK] = near[1, b * BLOCK : (b + 1) * BLOCK].T
    for b in range(nb // 2):
        v1_t[:, b * BLOCK : (b + 1) * BLOCK] = level_1[1, b * BLOCK : (b + 1) * BLOCK].T
    v2_t[...] = level_2[1].T
    for b in range(nb):
        at = slice(b * BLOCK, (b + 1) * BLOCK)
        at_1 = slice(sibling(b) * BLOCK, (sibling(b) + 1) * BLOCK)
        scores = []
        for side in range(3):
            score = dot_nt(near[0, (b + side) * BLOCK : (b + side + 1) * BLOCK], query[0, at])
            score = score * (SCALE * LOG2E)
            if b + side == 0:
                score = jnp.where(present[0], score, -jnp.inf)
            if b + side == nb + 1:
                score = jnp.where(present[1], score, -jnp.inf)
            scores.append(score)
        scores.append(dot_nt(level_1[0, at_1], query[1, at]) * (SCALE * LOG2E))
        scores.append(dot_nt(level_2[0], query[2, at]) * (SCALE * LOG2E))
        top = scores[0].max(0, keepdims=True)
        for score in scores[1:]:
            top = jnp.maximum(top, score.max(0, keepdims=True))
        weights = [jnp.exp2(score - top) for score in scores[:3]]
        weights.append(2.0 * jnp.exp2(scores[3] - top))
        weights.append(4.0 * jnp.exp2(scores[4] - top))
        total = weights[0].sum(0, keepdims=True)
        for weight in weights[1:]:
            total = total + weight.sum(0, keepdims=True)
        inverse = 1.0 / total
        for part, weight in enumerate(weights):
            prob[b, part * BLOCK : (part + 1) * BLOCK] = (weight * inverse).astype(BF16)
        context = dot(v_t[:, b * BLOCK : (b + 3) * BLOCK], prob[b, : 3 * BLOCK])
        context = context + dot(v1_t[:, at_1], prob[b, 3 * BLOCK : 4 * BLOCK])
        context = context + dot(v2_t[...], prob[b, 4 * BLOCK :])
        attended = context.T.astype(BF16)
        for step, out in enumerate(outs):

            @pl.when(me ^ step == b)
            def _():
                out[...] = attended


def backward_kernel(nb, groups, *refs):
    (query, near, level_1, level_2, prob), refs = refs[:5], refs[5:]
    chunks, refs = refs[:GROUP], refs[GROUP:]
    outs, tops, refs = refs[:GROUP], refs[GROUP : 2 * GROUP], refs[2 * GROUP :]
    rims, refs = refs[: 1 if groups == 2 else 2], refs[1 if groups == 2 else 2 :]
    grads, k_t, k1_t, k2_t, sums, sums_1, sums_2 = refs
    tokens = nb * BLOCK
    me = member()
    for step, chunk in enumerate(chunks):
        grads[span(me ^ step, BLOCK), :] = chunk[...]
    for b in range(nb + 2):
        k_t[:, b * BLOCK : (b + 1) * BLOCK] = near[0, b * BLOCK : (b + 1) * BLOCK].T
    for b in range(nb // 2):
        k1_t[:, b * BLOCK : (b + 1) * BLOCK] = level_1[0, b * BLOCK : (b + 1) * BLOCK].T
    k2_t[...] = level_2[0].T
    even_1, even_2 = averaging(1), averaging(2)
    sums[...] = jnp.zeros_like(sums)
    sums_1[...] = jnp.zeros_like(sums_1)
    sums_2[...] = jnp.zeros_like(sums_2)
    for b in range(nb):
        at = slice(b * BLOCK, (b + 1) * BLOCK)
        window = slice(b * BLOCK, (b + 3) * BLOCK)
        at_1 = slice(sibling(b) * BLOCK, (sibling(b) + 1) * BLOCK)
        grad = grads[at]
        slope = [
            dot_nt(near[1, window], grad),
            dot_nt(level_1[1, at_1], grad),
            dot_nt(level_2[1], grad),
        ]
        parts = (slice(0, 3 * BLOCK), slice(3 * BLOCK, 4 * BLOCK), slice(4 * BLOCK, 5 * BLOCK))
        delta = 0.0
        for part, s in zip(parts, slope):
            delta = delta + (prob[b, part].astype(F32) * s).sum(0, keepdims=True)
        shift = [
            (prob[b, part].astype(F32) * (s - delta)).astype(BF16) for part, s in zip(parts, slope)
        ]
        grad_t = dot(k_t[:, window], shift[0])
        for spread, key_t, s in ((even_1, k1_t[:, at_1], shift[1]), (even_2, k2_t[...], shift[2])):
            high, low = halves(dot(key_t, s))
            grad_t = grad_t + (dot(high, spread) + dot(low, spread))
        grad_q = (SCALE * grad_t).T.astype(BF16)
        for step, out in enumerate(outs):

            @pl.when(me ^ step == b)
            def _():
                out[0] = grad_q

        sums[0, window] += dot(shift[0], query[0, at])
        sums[1, window] += dot(prob[b, parts[0]], grad)
        sums_1[0, at_1] += dot(shift[1], query[1, at])
        sums_1[1, at_1] += dot(prob[b, parts[1]], grad)
        sums_2[0] += dot(shift[2], query[2, at])
        sums_2[1] += dot(prob[b, parts[2]], grad)
    upper = lax.axis_index("seq") >= GROUP
    spread = spreading(1)
    half, quarter = BLOCK // 2, BLOCK // 4
    for part, factor in enumerate((SCALE, 1.0)):
        for b in range(nb):
            total = sums[part, (b + 1) * BLOCK : (b + 2) * BLOCK]
            high, low = halves(sums_1[part, b * half : (b + 1) * half])
            total = total + (dot(spread, high) + dot(spread, low))
            total = (factor * total).astype(BF16)
            for step, out in enumerate(outs):

                @pl.when(me ^ step == b)
                def _():
                    out[1 + part] = total

        for step, out in enumerate(tops):
            out[part] = (factor * sums_2[part, span(me ^ step, quarter), :]).astype(BF16)
        low, high = sums[part, :BLOCK], sums[part, BLOCK + tokens :]
        if groups == 2:
            rims[0][part] = (factor * jnp.where(upper, low, high)).astype(BF16)
        else:
            rims[0][part] = (factor * low).astype(BF16)
            rims[1][part] = (factor * high).astype(BF16)


def unpack_kernel(groups, *refs):
    chunks, tops, refs = refs[:GROUP], refs[GROUP : 2 * GROUP], refs[2 * GROUP :]
    rims, outs = refs[:-3], refs[-3:]
    me = member()
    spread = spreading(2)
    for step, chunk in enumerate(chunks):
        at = columns(me ^ step)
        outs[0][:, at] = chunk[0]
        for part in range(2):
            total = chunk[1 + part].astype(F32) + dot(spread, tops[step][part])
            for rim in rims[step::GROUP]:
                total = total + rim[part].astype(F32)
            outs[1 + part][:, at] = total.astype(BF16)


def share():
    return lax.axis_index("mp")


def grad_kernel(*refs):
    pieces, out_weight, outs, whole = refs[:N_MP], refs[N_MP], refs[N_MP + 1 : -1], refs[-1]
    me = member()
    for step, piece in enumerate(pieces):
        whole[span(share() ^ step, piece.shape[0]), :] = piece[...]
    for step, out in enumerate(outs):
        weight = out_weight[span(me ^ step, HEAD_DIM), :]
        out[...] = dot_nt(whole[...], weight).astype(BF16)


def project_kernel(*refs):
    chunks, out_weight, outs, (attended, whole) = refs[:GROUP], refs[GROUP], refs[GROUP + 1 : -2], refs[-2:]
    me = member()
    for step, chunk in enumerate(chunks):
        attended[:, columns(me ^ step)] = chunk[...]
    whole[...] = dot(attended[...], out_weight[...]).astype(BF16)
    for step, out in enumerate(outs):
        out[...] = whole[span(share() ^ step, out.shape[0]), :]


def swapped(x, axis, step):
    return lax.ppermute(x, axis, [(i, i ^ step) for i in range(lax.axis_size(axis))])


def exchanged(chunks):
    return [chunks[0]] + [swapped(chunks[step], "seq", step) for step in range(1, GROUP)]


def rim_pairs(step, count):
    last = GROUP - 1
    up = [(i + last, i + GROUP + (last ^ step)) for i in range(0, count - GROUP, GROUP)]
    down = [(i, i - GROUP + step) for i in range(GROUP, count, GROUP)]
    return [up + down] if count == 2 * GROUP else [up, down]


def per_device(queries, keys, values, out_weight, out_grad):
    rows, width = queries.shape
    assert width == GROUP * HEAD_DIM and rows == BLOCK and lax.axis_size("mp") == N_MP
    count = lax.axis_size("seq")
    groups = count // GROUP
    nb = GROUP
    tokens = GROUP * rows
    assert count % (2 * GROUP) == 0
    quarter = rows // 4
    model = out_weight.shape[1]
    local = rows // N_MP

    chunk_shapes = [shape(3, rows, HEAD_DIM)] * GROUP
    rim_shapes = [shape(2, rows, HEAD_DIM)] * GROUP
    top_shapes = [shape(2, quarter, HEAD_DIM)] * GROUP
    packed = call(
        pack_kernel,
        chunk_shapes + rim_shapes + top_shapes,
        (queries, keys, values),
        scratch=[pltpu.VMEM((3, rows, width), BF16), pltpu.SemaphoreType.DMA((3,))],
        space=pltpu.HBM,
    )
    chunks, rims, tops = packed[:GROUP], packed[GROUP : 2 * GROUP], packed[2 * GROUP :]
    far = swapped(out_grad, "mp", 2)
    rims = [
        lax.ppermute(rims[step], "seq", pairs)
        for side in range(1 if groups == 2 else 2)
        for step in range(GROUP)
        for pairs in [rim_pairs(step, count)[side]]
    ]
    tops = [swapped(tops[step], "seq", GROUP + step) for step in range(GROUP)]
    chunks = exchanged(chunks)
    pieces = [out_grad, swapped(out_grad, "mp", 1), far, swapped(far, "mp", 1)]
    grad_chunks = call(
        grad_kernel,
        [shape(rows, HEAD_DIM)] * GROUP,
        (*pieces, out_weight),
        scratch=[pltpu.VMEM((rows, model), BF16)],
        flops=2 * rows * out_weight.size,
    )
    grad_chunks = exchanged(grad_chunks)
    score_flops = 2 * tokens * 5 * BLOCK * HEAD_DIM
    *kept, attended_0, attended_1, attended_2, attended_3 = call(
        functools.partial(forward_kernel, nb, groups),
        [
            shape(3, tokens, HEAD_DIM),
            shape(2, tokens + 2 * BLOCK, HEAD_DIM),
            shape(2, tokens // 2, HEAD_DIM),
            shape(2, tokens // 4, HEAD_DIM),
            shape(nb, 5 * BLOCK, BLOCK),
        ]
        + [shape(rows, HEAD_DIM)] * GROUP,
        (*chunks, *tops, *rims),
        scratch=[
            pltpu.VMEM((2, BLOCK, HEAD_DIM), BF16),
            pltpu.VMEM((2, BLOCK, HEAD_DIM), BF16),
            pltpu.VMEM((HEAD_DIM, tokens + 2 * BLOCK), BF16),
            pltpu.VMEM((HEAD_DIM, tokens // 2), BF16),
            pltpu.VMEM((HEAD_DIM, tokens // 4), BF16),
        ],
        flops=2 * score_flops,
    )
    attended = exchanged([attended_0, attended_1, attended_2, attended_3])
    mixed = call(
        project_kernel,
        [shape(local, model)] * N_MP,
        (*attended, out_weight),
        scratch=[pltpu.VMEM((rows, width), BF16), pltpu.VMEM((rows, model), BF16)],
        flops=2 * rows * out_weight.size,
    )
    across = (mixed[2].astype(F32) + swapped(mixed[3], "mp", 1).astype(F32)).astype(BF16)
    here = mixed[0].astype(F32) + swapped(mixed[1], "mp", 1).astype(F32)
    mixed = (here + swapped(across, "mp", 2).astype(F32)).astype(BF16)
    grads = call(
        functools.partial(backward_kernel, nb, groups),
        chunk_shapes + top_shapes + rim_shapes[: 1 if groups == 2 else 2],
        (*kept, *grad_chunks),
        scratch=[
            pltpu.VMEM((tokens, HEAD_DIM), BF16),
            pltpu.VMEM((HEAD_DIM, tokens + 2 * BLOCK), BF16),
            pltpu.VMEM((HEAD_DIM, tokens // 2), BF16),
            pltpu.VMEM((HEAD_DIM, tokens // 4), BF16),
            pltpu.VMEM((2, tokens + 2 * BLOCK, HEAD_DIM), F32),
            pltpu.VMEM((2, tokens // 2, HEAD_DIM), F32),
            pltpu.VMEM((2, tokens // 4, HEAD_DIM), F32),
        ],
        flops=4 * score_flops,
    )
    chunks, tops, rims = grads[:GROUP], grads[GROUP : 2 * GROUP], grads[2 * GROUP :]
    rims = [
        lax.ppermute(rims[side], "seq", [(j, i) for i, j in rim_pairs(step, count)[side]])
        for side in range(len(rims))
        for step in range(GROUP)
    ]
    tops = [swapped(tops[step], "seq", GROUP + step) for step in range(GROUP)]
    chunks = exchanged(chunks)
    grads = call(
        functools.partial(unpack_kernel, groups), [shape(rows, width)] * 3, (*chunks, *tops, *rims)
    )
    return (mixed, *grads)


def solution(mesh):
    return jax.shard_map(
        per_device,
        mesh=mesh,
        in_specs=(
            P("seq", "mp"),
            P("seq", "mp"),
            P("seq", "mp"),
            P("mp", None),
            P(("seq", "mp"), None),
        ),
        out_specs=(P(("seq", "mp"), None), P("seq", "mp"), P("seq", "mp"), P("seq", "mp")),
        check_vma=False,
    )
```

time: 101 us -> 101 us (level)
  starting transfers between devices: 20.9 us -> 43.6 us
  between operations: 14.1 us -> 0.84 us
  waiting for transfers between devices: 44.4 us -> 35 us
  local copies, waits for them, and re-layouts: 5.59 us -> 2.85 us
  Pallas kernels: 15.5 us -> 17.8 us
    ppermute x14 -> x34, starting transfers between devices: 20.8 us -> 43.6 us  [the longest x26 35.3 us: swapped(): lax.ppermute(x, axis, [(i, i ^ step) for i in range(lax.axis_size(axis))])]
    ppermute x14 -> x34, waiting for transfers between devices: 43.7 us -> 35 us  [the longest x26 35 us: swapped(): lax.ppermute(x, axis, [(i, i ^ step) for i in range(lax.axis_size(axis))])]
    unnamed x18 -> x10, local copies, waits for them, and re-layouts: 5.56 us -> 2.85 us
    pallas_call x8 -> x6, Pallas kernels: 15.5 us -> 17.8 us  [call(): pl.pallas_call(kernel, out_shape=out_shape, in_specs=[pl.BlockSpec(memory...]
  transfers between devices with their start and end apart: 16 -> 34, of which waited for: 13 -> 15; matrix products, arithmetic and copies ran while one was open for 0% -> 1% of each run, Pallas kernels for 15% -> 16%
where the time goes in v2:
time: 101 us
  starting transfers between devices  43.6 us (43%)
  waiting for transfers between devices  35 us (35%)
  Pallas kernels  17.8 us (18%)
  local copies, waits for them, and re-layouts  2.85 us (3%)
    ppermute x26, starting transfers between devices, swapped(): lax.ppermute(x, axis, [(i, i ^ step) for i in range(lax.axis_size(axis))])  35.3 us
    ppermute x26, waiting for transfers between devices, swapped(): lax.ppermute(x, axis, [(i, i ^ step) for i in range(lax.axis_size(axis))])  35 us
    pallas_call x6, Pallas kernels, call(): pl.pallas_call(kernel, out_shape=out_shape, in_specs=[pl.BlockSpec(memory...  17.8 us
    ppermute x4, starting transfers between devices, per_device(): lax.ppermute(rims[side], 'seq', [(j, i) for i, j in rim_pairs(step, count...  4.95 us
    ppermute x4, starting transfers between devices, per_device(): lax.ppermute(rims[step], 'seq', pairs)  3.28 us
    unnamed x10, local copies, waits for them, and re-layouts  2.85 us
  transfers between devices with their start and end apart: 34, of which 15 were waited for; matrix products, arithmetic and copies ran while one was open for 1% of the time, Pallas kernels for 16%

profile of v2, /device:TPU:0, one launch (start us, length us, event | category | flops | bytes accessed | tf_op | source)
XLA Modules:
  0.0 100.9 jit_solution(13712726830715702038)
XLA Ops:
  6.5 6.8 %collective-permute-start.3 = (bf16[2,64,128]{2,1,0:T(8,128)(2,1)S(1)}, bf16[2,64,128]{2,1,0:T(8,128)(2,1)S(1)}, u32[]{:S(2)}, u32[]{:S(2)}) collective-permute-start(bf16[2,64,128]{2,1,0:T(8,128)(2,1)S(1)} %get-tuple-element.49), channel_id=1, source_target_pairs={{0,16},{4,20},{8,24},{12,28},{16,0},{20,4},{24,8},{28,12},{1,17},{... | collective-permute-start | bytes 98312 | tf_op jit(solution)/shard_map/ppermute | solution.py:321
  13.9 6.5 %collective-permute-done.3.refs_4_ = bf16[2,64,128]{2,1,0:T(8,128)(2,1)S(1)} collective-permute-done((bf16[2,64,128]{2,1,0:T(8,128)(2,1)S(1)}, bf16[2,64,128]{2,1,0:T(8,128)(2,1)S(1)}, u32[]{:S(2)}, u32[]{:S(2)}) %collective-permute-start.3) | collective-permute-done | bytes 32800 | tf_op jit(solution)/shard_map/ppermute | solution.py:321
  20.4 2.8 %collective-permute-start.6 = (bf16[2,64,128]{2,1,0:T(8,128)(2,1)S(1)}, bf16[2,64,128]{2,1,0:T(8,128)(2,1)S(1)}, u32[]{:S(2)}, u32[]{:S(2)}) collective-permute-start(bf16[2,64,128]{2,1,0:T(8,128)(2,1)S(1)} %get-tuple-element.52), channel_id=1, source_target_pairs={{0,28},{4,24},{8,20},{12,16},{16,12},{20,8},{24,4},{28,0},{1,29},{... | collective-permute-start | bytes 98312 | tf_op jit(solution)/shard_map/ppermute | solution.py:321
  23.2 3.2 %collective-permute-done.5.refs_6_ = bf16[2,64,128]{2,1,0:T(8,128)(2,1)S(1)} collective-permute-done((bf16[2,64,128]{2,1,0:T(8,128)(2,1)S(1)}, bf16[2,64,128]{2,1,0:T(8,128)(2,1)S(1)}, u32[]{:S(2)}, u32[]{:S(2)}) %collective-permute-start.5) | collective-permute-done | bytes 32800 | tf_op jit(solution)/shard_map/ppermute | solution.py:321
  27.1 4.8 %collective-permute-start.2 = (bf16[3,256,128]{2,1,0:T(8,128)(2,1)S(1)}, bf16[3,256,128]{2,1,0:T(8,128)(2,1)S(1)}, u32[]{:S(2)}, u32[]{:S(2)}) collective-permute-start(bf16[3,256,128]{2,1,0:T(8,128)(2,1)S(1)} %get-tuple-element.48), channel_id=1, source_target_pairs={{0,12},{4,8},{8,4},{12,0},{16,28},{20,24},{24,20},{28,16},{1,13},{... | collective-permute-start | bytes 589832 | tf_op jit(solution)/shard_map/ppermute | solution.py:321
  31.9 1.6 %collective-permute-start.18 = (bf16[64,2048]{1,0:T(8,128)(2,1)}, bf16[64,2048]{1,0:T(8,128)(2,1)S(1)}, u32[]{:S(2)}, u32[]{:S(2)}) collective-permute-start(bf16[64,2048]{1,0:T(8,128)(2,1)} %refs_0_.1), channel_id=1, source_target_pairs={{0,2},{1,3},{2,0},{3,1},{4,6},{5,7},{6,4},{7,5},{8,10},{9,11},{10,... | collective-permute-start | bytes 786440 | tf_op jit(solution)/shard_map/ppermute | solution.py:321
  34.2 4.1 %collective-permute-done.2.refs_3_ = bf16[3,256,128]{2,1,0:T(8,128)(2,1)S(1)} collective-permute-done((bf16[3,256,128]{2,1,0:T(8,128)(2,1)S(1)}, bf16[3,256,128]{2,1,0:T(8,128)(2,1)S(1)}, u32[]{:S(2)}, u32[]{:S(2)}) %collective-permute-start.2) | collective-permute-done | bytes 196640 | tf_op jit(solution)/shard_map/ppermute | solution.py:321
  38.3 5.3 %shard_map.85 = (bf16[3,1024,128]{2,1,0:T(8,128)(2,1)S(1)}, bf16[2,1536,128]{2,1,0:T(8,128)(2,1)S(1)}, bf16[2,512,128]{2,1,0:T(8,128)(2,1)S(1)}, bf16[2,256,128]...) custom-call(bf16[3,256,128]{2,1,0:T(8,128)(2,1)S(1)} %get-tuple-elem, ...), custom_call_target="tpu_custom_call" | custom-call | flops 671088640 | bytes 6291456 | tf_op jit(solution)/shard_map/pallas_call | solution.py:36
  43.7 2.1 %collective-permute-start.12 = (bf16[256,128]{1,0:T(8,128)(2,1)S(1)}, bf16[256,128]{1,0:T(8,128)(2,1)S(1)}, u32[]{:S(2)}, u32[]{:S(2)}) collective-permute-start(bf16[256,128]{1,0:T(8,128)(2,1)S(1)} %get-tuple-element.59), channel_id=1, source_target_pairs={{0,8},{4,12},{8,0},{12,4},{16,24},{20,28},{24,16},{28,20},{1,9},{5... | collective-permute-start | bytes 196616 | tf_op jit(solution)/shard_map/ppermute | solution.py:321
  48.0 2.9 %collective-permute-done.13.refs_3_ = bf16[256,128]{1,0:T(8,128)(2,1)S(1)} collective-permute-done((bf16[256,128]{1,0:T(8,128)(2,1)S(1)}, bf16[256,128]{1,0:T(8,128)(2,1)S(1)}, u32[]{:S(2)}, u32[]{:S(2)}) %collective-permute-start.13) | collective-permute-done | bytes 65568 | tf_op jit(solution)/shard_map/ppermute | solution.py:321
  53.6 2.0 %collective-permute-start.20 = (bf16[256,128]{1,0:T(8,128)(2,1)S(1)}, bf16[256,128]{1,0:T(8,128)(2,1)S(1)}, u32[]{:S(2)}, u32[]{:S(2)}) collective-permute-start(bf16[256,128]{1,0:T(8,128)(2,1)S(1)} %get-tuple-element.71), channel_id=1, source_target_pairs={{0,4},{4,0},{8,12},{12,8},{16,20},{20,16},{24,28},{28,24},{1,5},{5... | collective-permute-start | bytes 196616 | tf_op jit(solution)/shard_map/ppermute | solution.py:321
  55.7 1.5 %collective-permute-start.22 = (bf16[256,128]{1,0:T(8,128)(2,1)S(1)}, bf16[256,128]{1,0:T(8,128)(2,1)S(1)}, u32[]{:S(2)}, u32[]{:S(2)}) collective-permute-start(bf16[256,128]{1,0:T(8,128)(2,1)S(1)} %get-tuple-element.73), channel_id=1, source_target_pairs={{0,12},{4,8},{8,4},{12,0},{16,28},{20,24},{24,20},{28,16},{1,13},{... | collective-permute-start | bytes 196616 | tf_op jit(solution)/shard_map/ppermute | solution.py:321
  58.0 2.2 %collective-permute-done.21.refs_7_ = bf16[256,128]{1,0:T(8,128)(2,1)S(1)} collective-permute-done((bf16[256,128]{1,0:T(8,128)(2,1)S(1)}, bf16[256,128]{1,0:T(8,128)(2,1)S(1)}, u32[]{:S(2)}, u32[]{:S(2)}) %collective-permute-start.21) | collective-permute-done | bytes 65568 | tf_op jit(solution)/shard_map/ppermute | solution.py:321
  60.8 8.3 %shard_map.88 = (bf16[3,256,128]{2,1,0:T(8,128)(2,1)S(1)}, bf16[3,256,128]{2,1,0:T(8,128)(2,1)S(1)}, bf16[3,256,128]{2,1,0:T(8,128)(2,1)S(1)}, bf16[3,256,128]{2...) custom-call(bf16[3,1024,128]{2,1,0:T(8,128)(2,1)S(1)} %get-tuple-ele, ...), custom_call_target="tpu_custom_call" | custom-call | flops 1342177280 | bytes 5898240 | tf_op jit(solution)/shard_map/pallas_call | solution.py:36
  69.2 3.0 %collective-permute-start.30 = (bf16[2,256,128]{2,1,0:T(8,128)(2,1)S(1)}, bf16[2,256,128]{2,1,0:T(8,128)(2,1)S(1)}, u32[]{:S(2)}, u32[]{:S(2)}) collective-permute-start(bf16[2,256,128]{2,1,0:T(8,128)(2,1)S(1)} %get-tuple-element.82), channel_id=1, source_target_pairs={{28,12},{0,16},{29,13},{1,17},{30,14},{2,18},{31,15},{3,19}} | collective-permute-start | bytes 393224 | tf_op jit(solution)/shard_map/ppermute | solution.py:425
  72.9 4.4 %collective-permute-start.27 = (bf16[2,64,128]{2,1,0:T(8,128)(2,1)S(1)}, bf16[2,64,128]{2,1,0:T(8,128)(2,1)S(1)}, u32[]{:S(2)}, u32[]{:S(2)}) collective-permute-start(bf16[2,64,128]{2,1,0:T(8,128)(2,1)S(1)} %get-tuple-element.79), channel_id=1, source_target_pairs={{0,20},{4,16},{8,28},{12,24},{16,4},{20,0},{24,12},{28,8},{1,21},{... | collective-permute-start | bytes 98312 | tf_op jit(solution)/shard_map/ppermute | solution.py:321
  77.3 3.8 %collective-permute-done.26.refs_4_ = bf16[2,64,128]{2,1,0:T(8,128)(2,1)S(1)} collective-permute-done((bf16[2,64,128]{2,1,0:T(8,128)(2,1)S(1)}, bf16[2,64,128]{2,1,0:T(8,128)(2,1)S(1)}, u32[]{:S(2)}, u32[]{:S(2)}) %collective-permute-start.26) | collective-permute-done | bytes 32800 | tf_op jit(solution)/shard_map/ppermute | solution.py:321
  81.2 2.3 %collective-permute-start.29 = (bf16[2,64,128]{2,1,0:T(8,128)(2,1)S(1)}, bf16[2,64,128]{2,1,0:T(8,128)(2,1)S(1)}, u32[]{:S(2)}, u32[]{:S(2)}) collective-permute-start(bf16[2,64,128]{2,1,0:T(8,128)(2,1)S(1)} %get-tuple-element.81), channel_id=1, source_target_pairs={{0,28},{4,24},{8,20},{12,16},{16,12},{20,8},{24,4},{28,0},{1,29},{... | collective-permute-start | bytes 98312 | tf_op jit(solution)/shard_map/ppermute | solution.py:321
  83.5 3.5 %collective-permute-done.28.refs_6_ = bf16[2,64,128]{2,1,0:T(8,128)(2,1)S(1)} collective-permute-done((bf16[2,64,128]{2,1,0:T(8,128)(2,1)S(1)}, bf16[2,64,128]{2,1,0:T(8,128)(2,1)S(1)}, u32[]{:S(2)}, u32[]{:S(2)}) %collective-permute-start.28) | collective-permute-done | bytes 32800 | tf_op jit(solution)/shard_map/ppermute | solution.py:321
  88.6 2.1 %collective-permute-start.23 = (bf16[3,256,128]{2,1,0:T(8,128)(2,1)S(1)}, bf16[3,256,128]{2,1,0:T(8,128)(2,1)S(1)}, u32[]{:S(2)}, u32[]{:S(2)}) collective-permute-start(bf16[3,256,128]{2,1,0:T(8,128)(2,1)S(1)} %get-tuple-element.75), channel_id=1, source_target_pairs={{0,4},{4,0},{8,12},{12,8},{16,20},{20,16},{24,28},{28,24},{1,5},{5... | collective-permute-start | bytes 589832 | tf_op jit(solution)/shard_map/ppermute | solution.py:321
  90.8 1.4 %collective-permute-start.25 = (bf16[3,256,128]{2,1,0:T(8,128)(2,1)S(1)}, bf16[3,256,128]{2,1,0:T(8,128)(2,1)S(1)}, u32[]{:S(2)}, u32[]{:S(2)}) collective-permute-start(bf16[3,256,128]{2,1,0:T(8,128)(2,1)S(1)} %get-tuple-element.77), channel_id=1, source_target_pairs={{0,12},{4,8},{8,4},{12,0},{16,28},{20,24},{24,20},{28,16},{1,13},{... | collective-permute-start | bytes 589832 | tf_op jit(solution)/shard_map/ppermute | solution.py:321
  93.1 2.6 %collective-permute-done.23.refs_1_ = bf16[3,256,128]{2,1,0:T(8,128)(2,1)S(1)} collective-permute-done((bf16[3,256,128]{2,1,0:T(8,128)(2,1)S(1)}, bf16[3,256,128]{2,1,0:T(8,128)(2,1)S(1)}, u32[]{:S(2)}, u32[]{:S(2)}) %collective-permute-start.23) | collective-permute-done | bytes 196640 | tf_op jit(solution)/shard_map/ppermute | solution.py:321
  95.7 2.2 %collective-permute-done.24.refs_2_ = bf16[3,256,128]{2,1,0:T(8,128)(2,1)S(1)} collective-permute-done((bf16[3,256,128]{2,1,0:T(8,128)(2,1)S(1)}, bf16[3,256,128]{2,1,0:T(8,128)(2,1)S(1)}, u32[]{:S(2)}, u32[]{:S(2)}) %collective-permute-start.24) | collective-permute-done | bytes 196640 | tf_op jit(solution)/shard_map/ppermute | solution.py:321
  97.9 1.9 %collective-permute-done.25.refs_3_ = bf16[3,256,128]{2,1,0:T(8,128)(2,1)S(1)} collective-permute-done((bf16[3,256,128]{2,1,0:T(8,128)(2,1)S(1)}, bf16[3,256,128]{2,1,0:T(8,128)(2,1)S(1)}, u32[]{:S(2)}, u32[]{:S(2)}) %collective-permute-start.25) | collective-permute-done | bytes 196640 | tf_op jit(solution)/shard_map/ppermute | solution.py:321
  (62 shorter events, 18.7 us)
Async XLA Ops:
  4.5 22.6 %collective-permute-start.10 = (bf16[2,256,128]{2,1,0:T(8,128)(2,1)S(1)}, bf16[2,256,128]{2,1,0:T(8,128)(2,1)S(1)}, u32[]{:S(2)}, u32[]{:S(2)}) collective-permute-start(bf16[2,256,128]{2,1,0:T(8,128)(2,1)S(1)} %get-tuple-element.56), channel_id=1, source_target_pairs={{12,16},{16,12},{13,17},{17,13},{14,18},{18,14},{15,19},{19,15}} | collective-permute-start | bytes 393224 | tf_op jit(solution)/shard_map/ppermute | solution.py:360
  5.2 26.8 %collective-permute-start.7 = (bf16[2,256,128]{2,1,0:T(8,128)(2,1)S(1)}, bf16[2,256,128]{2,1,0:T(8,128)(2,1)S(1)}, u32[]{:S(2)}, u32[]{:S(2)}) collective-permute-start(bf16[2,256,128]{2,1,0:T(8,128)(2,1)S(1)} %get-tuple-element.53), channel_id=1, source_target_pairs={{12,28},{16,0},{13,29},{17,1},{14,30},{18,2},{15,31},{19,3}} | collective-permute-start | bytes 393224 | tf_op jit(solution)/shard_map/ppermute | solution.py:360
  6.5 13.9 %collective-permute-start.3 = (bf16[2,64,128]{2,1,0:T(8,128)(2,1)S(1)}, bf16[2,64,128]{2,1,0:T(8,128)(2,1)S(1)}, u32[]{:S(2)}, u32[]{:S(2)}) collective-permute-start(bf16[2,64,128]{2,1,0:T(8,128)(2,1)S(1)} %get-tuple-element.49), channel_id=1, source_target_pairs={{0,16},{4,20},{8,24},{12,28},{16,0},{20,4},{24,8},{28,12},{1,17},{... | collective-permute-start | bytes 98312 | tf_op jit(solution)/shard_map/ppermute | solution.py:321
  13.2 7.2 %collective-permute-start.4 = (bf16[2,64,128]{2,1,0:T(8,128)(2,1)S(1)}, bf16[2,64,128]{2,1,0:T(8,128)(2,1)S(1)}, u32[]{:S(2)}, u32[]{:S(2)}) collective-permute-start(bf16[2,64,128]{2,1,0:T(8,128)(2,1)S(1)} %get-tuple-element.50), channel_id=1, source_target_pairs={{0,20},{4,16},{8,28},{12,24},{16,4},{20,0},{24,12},{28,8},{1,21},{... | collective-permute-start | bytes 98312 | tf_op jit(solution)/shard_map/ppermute | solution.py:321
  13.2 20.3 %collective-permute-start.8 = (bf16[2,256,128]{2,1,0:T(8,128)(2,1)S(1)}, bf16[2,256,128]{2,1,0:T(8,128)(2,1)S(1)}, u32[]{:S(2)}, u32[]{:S(2)}) collective-permute-start(bf16[2,256,128]{2,1,0:T(8,128)(2,1)S(1)} %get-tuple-element.54), channel_id=1, source_target_pairs={{12,24},{16,4},{13,25},{17,5},{14,26},{18,6},{15,27},{19,7}} | collective-permute-start | bytes 393224 | tf_op jit(solution)/shard_map/ppermute | solution.py:360
  20.4 6.0 %collective-permute-start.5 = (bf16[2,64,128]{2,1,0:T(8,128)(2,1)S(1)}, bf16[2,64,128]{2,1,0:T(8,128)(2,1)S(1)}, u32[]{:S(2)}, u32[]{:S(2)}) collective-permute-start(bf16[2,64,128]{2,1,0:T(8,128)(2,1)S(1)} %get-tuple-element.51), channel_id=1, source_target_pairs={{0,24},{4,28},{8,16},{12,20},{16,8},{20,12},{24,0},{28,4},{1,25},{... | collective-permute-start | bytes 98312 | tf_op jit(solution)/shard_map/ppermute | solution.py:321
  20.4 6.7 %collective-permute-start.6 = (bf16[2,64,128]{2,1,0:T(8,128)(2,1)S(1)}, bf16[2,64,128]{2,1,0:T(8,128)(2,1)S(1)}, u32[]{:S(2)}, u32[]{:S(2)}) collective-permute-start(bf16[2,64,128]{2,1,0:T(8,128)(2,1)S(1)} %get-tuple-element.52), channel_id=1, source_target_pairs={{0,28},{4,24},{8,20},{12,16},{16,12},{20,8},{24,4},{28,0},{1,29},{... | collective-permute-start | bytes 98312 | tf_op jit(solution)/shard_map/ppermute | solution.py:321
  26.4 7.8 %collective-permute-start = (bf16[3,256,128]{2,1,0:T(8,128)(2,1)S(1)}, bf16[3,256,128]{2,1,0:T(8,128)(2,1)S(1)}, u32[]{:S(2)}, u32[]{:S(2)}) collective-permute-start(bf16[3,256,128]{2,1,0:T(8,128)(2,1)S(1)} %get-tuple-element.46), channel_id=1, source_target_pairs={{0,4},{4,0},{8,12},{12,8},{16,20},{20,16},{24,28},{28,24},{1,5},{5... | collective-permute-start | bytes 589832 | tf_op jit(solution)/shard_map/ppermute | solution.py:321
  27.1 7.1 %collective-permute-start.1 = (bf16[3,256,128]{2,1,0:T(8,128)(2,1)S(1)}, bf16[3,256,128]{2,1,0:T(8,128)(2,1)S(1)}, u32[]{:S(2)}, u32[]{:S(2)}) collective-permute-start(bf16[3,256,128]{2,1,0:T(8,128)(2,1)S(1)} %get-tuple-element.47), channel_id=1, source_target_pairs={{0,8},{4,12},{8,0},{12,4},{16,24},{20,28},{24,16},{28,20},{1,9},{5... | collective-permute-start | bytes 589832 | tf_op jit(solution)/shard_map/ppermute | solution.py:321
  27.1 11.2 %collective-permute-start.2 = (bf16[3,256,128]{2,1,0:T(8,128)(2,1)S(1)}, bf16[3,256,128]{2,1,0:T(8,128)(2,1)S(1)}, u32[]{:S(2)}, u32[]{:S(2)}) collective-permute-start(bf16[3,256,128]{2,1,0:T(8,128)(2,1)S(1)} %get-tuple-element.48), channel_id=1, source_target_pairs={{0,12},{4,8},{8,4},{12,0},{16,28},{20,24},{24,20},{28,16},{1,13},{... | collective-permute-start | bytes 589832 | tf_op jit(solution)/shard_map/ppermute | solution.py:321
  31.9 15.2 %collective-permute-start.18 = (bf16[64,2048]{1,0:T(8,128)(2,1)}, bf16[64,2048]{1,0:T(8,128)(2,1)S(1)}, u32[]{:S(2)}, u32[]{:S(2)}) collective-permute-start(bf16[64,2048]{1,0:T(8,128)(2,1)} %refs_0_.1), channel_id=1, source_target_pairs={{0,2},{1,3},{2,0},{3,1},{4,6},{5,7},{6,4},{7,5},{8,10},{9,11},{10,... | collective-permute-start | bytes 786440 | tf_op jit(solution)/shard_map/ppermute | solution.py:321
  51.8 5.4 %collective-permute-start.15 = (bf16[64,2048]{1,0:T(8,128)(2,1)S(1)}, bf16[64,2048]{1,0:T(8,128)(2,1)S(1)}, u32[]{:S(2)}, u32[]{:S(2)}) collective-permute-start(bf16[64,2048]{1,0:T(8,128)(2,1)S(1)} %get-tuple-element.64), channel_id=1, source_target_pairs={{0,1},{1,0},{2,3},{3,2},{4,5},{5,4},{6,7},{7,6},{8,9},{9,8},{10,11... | collective-permute-start | bytes 786440 | tf_op jit(solution)/shard_map/ppermute | solution.py:321
  51.8 21.1 %collective-permute-start.14 = (bf16[64,2048]{1,0:T(8,128)(2,1)S(1)}, bf16[64,2048]{1,0:T(8,128)(2,1)S(1)}, u32[]{:S(2)}, u32[]{:S(2)}) collective-permute-start(bf16[64,2048]{1,0:T(8,128)(2,1)S(1)} %get-tuple-element.62), channel_id=1, source_target_pairs={{0,1},{1,0},{2,3},{3,2},{4,5},{5,4},{6,7},{7,6},{8,9},{9,8},{10,11... | collective-permute-start | bytes 786440 | tf_op jit(solution)/shard_map/ppermute | solution.py:321
  57.3 33.5 %collective-permute-start.16 = (bf16[64,2048]{1,0:T(8,128)(2,1)S(1)}, bf16[64,2048]{1,0:T(8,128)(2,1)S(1)}, u32[]{:S(2)}, u32[]{:S(2)}) collective-permute-start(bf16[64,2048]{1,0:T(8,128)(2,1)S(1)} %add_convert_fusion.1), channel_id=1, source_target_pairs={{0,2},{1,3},{2,0},{3,1},{4,6},{5,7},{6,4},{7,5},{8,10},{9,11},{10,... | collective-permute-start | bytes 786440 | tf_op jit(solution)/shard_map/ppermute | solution.py:321
  69.2 19.4 %collective-permute-start.30 = (bf16[2,256,128]{2,1,0:T(8,128)(2,1)S(1)}, bf16[2,256,128]{2,1,0:T(8,128)(2,1)S(1)}, u32[]{:S(2)}, u32[]{:S(2)}) collective-permute-start(bf16[2,256,128]{2,1,0:T(8,128)(2,1)S(1)} %get-tuple-element.82), channel_id=1, source_target_pairs={{28,12},{0,16},{29,13},{1,17},{30,14},{2,18},{31,15},{3,19}} | collective-permute-start | bytes 393224 | tf_op jit(solution)/shard_map/ppermute | solution.py:425
  72.1 18.6 %collective-permute-start.31 = (bf16[2,256,128]{2,1,0:T(8,128)(2,1)S(1)}, bf16[2,256,128]{2,1,0:T(8,128)(2,1)S(1)}, u32[]{:S(2)}, u32[]{:S(2)}) collective-permute-start(bf16[2,256,128]{2,1,0:T(8,128)(2,1)S(1)} %get-tuple-element.82), channel_id=1, source_target_pairs={{24,12},{4,16},{25,13},{5,17},{26,14},{6,18},{27,15},{7,19}} | collective-permute-start | bytes 393224 | tf_op jit(solution)/shard_map/ppermute | solution.py:425
  72.8 8.3 %collective-permute-start.26 = (bf16[2,64,128]{2,1,0:T(8,128)(2,1)S(1)}, bf16[2,64,128]{2,1,0:T(8,128)(2,1)S(1)}, u32[]{:S(2)}, u32[]{:S(2)}) collective-permute-start(bf16[2,64,128]{2,1,0:T(8,128)(2,1)S(1)} %get-tuple-element.78), channel_id=1, source_target_pairs={{0,16},{4,20},{8,24},{12,28},{16,0},{20,4},{24,8},{28,12},{1,17},{... | collective-permute-start | bytes 98312 | tf_op jit(solution)/shard_map/ppermute | solution.py:321
  72.9 8.3 %collective-permute-start.27 = (bf16[2,64,128]{2,1,0:T(8,128)(2,1)S(1)}, bf16[2,64,128]{2,1,0:T(8,128)(2,1)S(1)}, u32[]{:S(2)}, u32[]{:S(2)}) collective-permute-start(bf16[2,64,128]{2,1,0:T(8,128)(2,1)S(1)} %get-tuple-element.79), channel_id=1, source_target_pairs={{0,20},{4,16},{8,28},{12,24},{16,4},{20,0},{24,12},{28,8},{1,21},{... | collective-permute-start | bytes 98312 | tf_op jit(solution)/shard_map/ppermute | solution.py:321
  81.1 5.8 %collective-permute-start.28 = (bf16[2,64,128]{2,1,0:T(8,128)(2,1)S(1)}, bf16[2,64,128]{2,1,0:T(8,128)(2,1)S(1)}, u32[]{:S(2)}, u32[]{:S(2)}) collective-permute-start(bf16[2,64,128]{2,1,0:T(8,128)(2,1)S(1)} %get-tuple-element.80), channel_id=1, source_target_pairs={{0,24},{4,28},{8,16},{12,20},{16,8},{20,12},{24,0},{28,4},{1,25},{... | collective-permute-start | bytes 98312 | tf_op jit(solution)/shard_map/ppermute | solution.py:321
  81.2 6.7 %collective-permute-start.29 = (bf16[2,64,128]{2,1,0:T(8,128)(2,1)S(1)}, bf16[2,64,128]{2,1,0:T(8,128)(2,1)S(1)}, u32[]{:S(2)}, u32[]{:S(2)}) collective-permute-start(bf16[2,64,128]{2,1,0:T(8,128)(2,1)S(1)} %get-tuple-element.81), channel_id=1, source_target_pairs={{0,28},{4,24},{8,20},{12,16},{16,12},{20,8},{24,4},{28,0},{1,29},{... | collective-permute-start | bytes 98312 | tf_op jit(solution)/shard_map/ppermute | solution.py:321
  87.0 6.1 %collective-permute-start.32 = (bf16[2,256,128]{2,1,0:T(8,128)(2,1)S(1)}, bf16[2,256,128]{2,1,0:T(8,128)(2,1)S(1)}, u32[]{:S(2)}, u32[]{:S(2)}) collective-permute-start(bf16[2,256,128]{2,1,0:T(8,128)(2,1)S(1)} %get-tuple-element.82), channel_id=1, source_target_pairs={{20,12},{8,16},{21,13},{9,17},{22,14},{10,18},{23,15},{11,19}} | collective-permute-start | bytes 393224 | tf_op jit(solution)/shard_map/ppermute | solution.py:425
  88.6 7.1 %collective-permute-start.23 = (bf16[3,256,128]{2,1,0:T(8,128)(2,1)S(1)}, bf16[3,256,128]{2,1,0:T(8,128)(2,1)S(1)}, u32[]{:S(2)}, u32[]{:S(2)}) collective-permute-start(bf16[3,256,128]{2,1,0:T(8,128)(2,1)S(1)} %get-tuple-element.75), channel_id=1, source_target_pairs={{0,4},{4,0},{8,12},{12,8},{16,20},{20,16},{24,28},{28,24},{1,5},{5... | collective-permute-start | bytes 589832 | tf_op jit(solution)/shard_map/ppermute | solution.py:321
  90.7 7.2 %collective-permute-start.24 = (bf16[3,256,128]{2,1,0:T(8,128)(2,1)S(1)}, bf16[3,256,128]{2,1,0:T(8,128)(2,1)S(1)}, u32[]{:S(2)}, u32[]{:S(2)}) collective-permute-start(bf16[3,256,128]{2,1,0:T(8,128)(2,1)S(1)} %get-tuple-element.76), channel_id=1, source_target_pairs={{0,8},{4,12},{8,0},{12,4},{16,24},{20,28},{24,16},{28,20},{1,9},{5... | collective-permute-start | bytes 589832 | tf_op jit(solution)/shard_map/ppermute | solution.py:321
  90.8 9.0 %collective-permute-start.25 = (bf16[3,256,128]{2,1,0:T(8,128)(2,1)S(1)}, bf16[3,256,128]{2,1,0:T(8,128)(2,1)S(1)}, u32[]{:S(2)}, u32[]{:S(2)}) collective-permute-start(bf16[3,256,128]{2,1,0:T(8,128)(2,1)S(1)} %get-tuple-element.77), channel_id=1, source_target_pairs={{0,12},{4,8},{8,4},{12,0},{16,28},{20,24},{24,20},{28,16},{1,13},{... | collective-permute-start | bytes 589832 | tf_op jit(solution)/shard_map/ppermute | solution.py:321
  (15 other events, 138.0 us)

commit v3 on v2

v3 whole, which is shorter than its diff:
```python
import functools

import jax
import jax.numpy as jnp
from jax import lax
from jax.experimental import pallas as pl
from jax.experimental.pallas import tpu as pltpu
from jax.sharding import PartitionSpec as P

HEAD_DIM = 128
BLOCK = 256
LEVELS = 2
GROUP = 4
N_MP = 4
SCALE = HEAD_DIM**-0.5
LOG2E = 1.4426950408889634
BF16 = jnp.bfloat16
F32 = jnp.float32


def dot(a, b):
    return lax.dot_general(a, b, (((1,), (0,)), ((), ())), preferred_element_type=F32)


def dot_nt(a, b):
    return lax.dot_general(a, b, (((1,), (1,)), ((), ())), preferred_element_type=F32)


def shape(*dims, dtype=BF16):
    return jax.ShapeDtypeStruct(dims, dtype)


def call(kernel, out_shape, args, scratch=(), flops=0, limit=32, space=pltpu.VMEM):
    whole = pl.BlockSpec(memory_space=pltpu.VMEM)
    moved = sum(x.size * x.dtype.itemsize for x in (*args, *out_shape))
    return pl.pallas_call(
        kernel,
        out_shape=out_shape,
        in_specs=[pl.BlockSpec(memory_space=space)] * len(args),
        out_specs=[whole] * len(out_shape),
        scratch_shapes=scratch,
        compiler_params=pltpu.CompilerParams(vmem_limit_bytes=limit << 20),
        cost_estimate=pl.CostEstimate(flops=flops, bytes_accessed=moved, transcendentals=0),
    )(*args)


def columns(index):
    return pl.ds(pl.multiple_of(index * HEAD_DIM, HEAD_DIM), HEAD_DIM)


def span(index, size):
    return pl.ds(pl.multiple_of(index * size, size), size)


def iota(dims, axis):
    return lax.broadcasted_iota(jnp.int32, dims, axis)


def averaging(level):
    dims = (BLOCK, BLOCK)
    same = (iota(dims, 0) >> level) == (iota(dims, 1) >> level)
    return jnp.where(same, 2.0**-level, 0.0).astype(BF16)


def pooling():
    dims = (BLOCK // 2, BLOCK)
    return jnp.where(iota(dims, 0) == (iota(dims, 1) >> 1), 0.5, 0.0).astype(BF16)


def spreading(level):
    dims = (BLOCK, BLOCK >> level)
    return jnp.where((iota(dims, 0) >> level) == iota(dims, 1), 2.0**-level, 0.0).astype(BF16)


def halves(x):
    high = x.astype(BF16)
    return high, (x - high.astype(F32)).astype(BF16)


def at_block(b):
    return slice(b * BLOCK, (b + 1) * BLOCK)


def sibling(b):
    return (b >> 1) ^ 1


def rim_present(groups):
    group = lax.axis_index("seq") // GROUP
    return group > 0, group < groups - 1


def pack_kernel(q, k, v, chunks, tops, held, sems):
    copies = [
        pltpu.make_async_copy(source, held.at[part], sems.at[part])
        for part, source in enumerate((k, v, q))
    ]
    for copy in copies:
        copy.start()
    pool = pooling()
    half = BLOCK // 2
    for part, copy in enumerate(copies):
        copy.wait()
        for head in range(GROUP):
            at = slice(head * HEAD_DIM, (head + 1) * HEAD_DIM)
            chunks[head, part] = held[part, :, at]
        if part < 2:
            once = dot(pool, held[part]).astype(BF16)
            twice = dot(pool[: half // 2, :half], once).astype(BF16)
            for head in range(GROUP):
                tops[head, part] = twice[:, head * HEAD_DIM : (head + 1) * HEAD_DIM]


def rim_kernel(groups, full, *outs):
    last = full.shape[0] - 1
    if groups == 2:
        upper = lax.axis_index("seq") >= GROUP
        outs[0][...] = jnp.where(upper, full[0, :2], full[last, :2])
    else:
        outs[0][...] = full[last, :2]
        outs[1][...] = full[0, :2]


def near_sides(b, nb):
    return [side for side in range(3) if 0 <= b + side - 1 < nb]


def local_kernel(nb, full, spread_q, level_1, k_t, v_t, k1_t, v1_t, weights, stats):
    pool, even_1, even_2 = pooling(), averaging(1), averaging(2)
    half = BLOCK // 2
    for b in range(nb):
        once = dot(even_1, full[b, 2]).astype(BF16)
        spread_q[0, b] = once
        spread_q[1, b] = dot(even_2, once).astype(BF16)
        for part, transposed in enumerate((k_t, v_t)):
            level_1[part, b * half : (b + 1) * half] = dot(pool, full[b, part]).astype(BF16)
            transposed[:, at_block(b)] = full[b, part].T
    for c in range(nb // 2):
        for part, transposed in enumerate((k1_t, v1_t)):
            transposed[:, at_block(c)] = level_1[part, at_block(c)].T
    for b in range(nb):
        sides = near_sides(b, nb)
        scores = [dot_nt(full[b + side - 1, 0], full[b, 2]) * (SCALE * LOG2E) for side in sides]
        coarse = dot_nt(level_1[0, at_block(sibling(b))], spread_q[0, b]) * (SCALE * LOG2E)
        top = coarse.max(0, keepdims=True)
        for score in scores:
            top = jnp.maximum(top, score.max(0, keepdims=True))
        weight = 2.0 * jnp.exp2(coarse - top)
        weights[b, 3] = weight
        total = weight.sum(0, keepdims=True)
        for side, score in zip(sides, scores):
            weight = jnp.exp2(score - top)
            weights[b, side] = weight
            total = total + weight.sum(0, keepdims=True)
        stats[b, :1] = top
        stats[b, 1:2] = total


def rim_sides(b, nb):
    return [side for side in range(3) if not 0 <= b + side - 1 < nb]


def forward_kernel(nb, groups, *refs):
    full, spread_q, v_t, v1_t, weights, stats, tops, rim_low, rim_high, prob, attended, level_2 = refs
    present = rim_present(groups)
    quarter = BLOCK // 4
    for step in range(GROUP):
        level_2[:, step * quarter : (step + 1) * quarter] = tops[step]
    v2_t = level_2[1].T
    for b in range(nb):
        sides = rim_sides(b, nb)
        scores = []
        for side in sides:
            score = dot_nt((rim_high if side else rim_low)[0], full[b, 2]) * (SCALE * LOG2E)
            scores.append(jnp.where(present[side // 2], score, -jnp.inf))
        coarse = dot_nt(level_2[0], spread_q[1, b]) * (SCALE * LOG2E)
        old = stats[b, :1]
        top = jnp.maximum(old, coarse.max(0, keepdims=True))
        for score in scores:
            top = jnp.maximum(top, score.max(0, keepdims=True))
        shrink = jnp.exp2(old - top)
        far = 4.0 * jnp.exp2(coarse - top)
        total = shrink * stats[b, 1:2] + far.sum(0, keepdims=True)
        fresh = []
        for score in scores:
            fresh.append(jnp.exp2(score - top))
            total = total + fresh[-1].sum(0, keepdims=True)
        inverse = 1.0 / total
        shrink = shrink * inverse
        prob[b, 4] = (far * inverse).astype(BF16)
        prob[b, 3] = (weights[b, 3] * shrink).astype(BF16)
        context = dot(v2_t, prob[b, 4]) + dot(v1_t[:, at_block(sibling(b))], prob[b, 3])
        for side in near_sides(b, nb):
            prob[b, side] = (weights[b, side] * shrink).astype(BF16)
            context = context + dot(v_t[:, at_block(b + side - 1)], prob[b, side])
        for side, weight in zip(sides, fresh):
            prob[b, side] = (weight * inverse).astype(BF16)
            context = context + dot((rim_high if side else rim_low)[1].T, prob[b, side])
        attended[b] = context.T.astype(BF16)


def slope_kernel(nb, groups, *refs):
    full, spread_q, level_1, tops, rim_low, rim_high, prob, grads, shift, top_out = refs[:10]
    rim_outs, level_2, sums, rim_sums = refs[10:-3], refs[-3], refs[-2], refs[-1]
    quarter = BLOCK // 4
    for step in range(GROUP):
        level_2[:, step * quarter : (step + 1) * quarter] = tops[step]
    for b in range(nb):
        grad = grads[b]
        slopes = []
        for side in range(3):
            if side in near_sides(b, nb):
                value = full[b + side - 1, 1]
            else:
                value = (rim_high if side else rim_low)[1]
            slopes.append(dot_nt(value, grad))
        slopes.append(dot_nt(level_1[1, at_block(sibling(b))], grad))
        slopes.append(dot_nt(level_2[1], grad))
        delta = 0.0
        for part, slope in enumerate(slopes):
            delta = delta + (prob[b, part].astype(F32) * slope).sum(0, keepdims=True)
        for part, slope in enumerate(slopes):
            shift[b, part] = (prob[b, part].astype(F32) * (slope - delta)).astype(BF16)
        for side in rim_sides(b, nb):
            rim_sums[side // 2, 0] = SCALE * dot(shift[b, side], full[b, 2])
            rim_sums[side // 2, 1] = dot(prob[b, side], grad)
        key, value = SCALE * dot(shift[b, 4], spread_q[1, b]), dot(prob[b, 4], grad)
        if b:
            key, value = key + sums[0], value + sums[1]
        if b < nb - 1:
            sums[0], sums[1] = key, value
        else:
            top_out[0], top_out[1] = key.astype(BF16), value.astype(BF16)
    low, high = rim_sums[0], rim_sums[1]
    if groups == 2:
        upper = lax.axis_index("seq") >= GROUP
        rim_outs[0][...] = jnp.where(upper, low, high).astype(BF16)
    else:
        rim_outs[0][...] = high.astype(BF16)
        rim_outs[1][...] = low.astype(BF16)


def backward_kernel(nb, full, spread_q, k_t, k1_t, tops, rim_low, rim_high, prob, shift, grads, *refs):
    grad_q, grad_kv, k2_t, sums_1 = refs
    quarter = BLOCK // 4
    for step in range(GROUP):
        k2_t[:, step * quarter : (step + 1) * quarter] = tops[step, 0].T
    even_1, even_2 = averaging(1), averaging(2)
    for b in range(nb):
        grad_t = 0.0
        for side in range(3):
            if side in near_sides(b, nb):
                key_t = k_t[:, at_block(b + side - 1)]
            else:
                key_t = (rim_high if side else rim_low)[0].T
            grad_t = grad_t + dot(key_t, shift[b, side])
        for spread, key_t, part in ((even_1, k1_t[:, at_block(sibling(b))], 3), (even_2, k2_t[...], 4)):
            high, low = halves(dot(key_t, shift[b, part]))
            grad_t = grad_t + (dot(high, spread) + dot(low, spread))
        grad_q[b] = (SCALE * grad_t).T.astype(BF16)
    for c in range(nb // 2):
        users = [b for b in range(nb) if sibling(b) == c]
        sums_1[0, at_block(c)] = SCALE * sum(dot(shift[b, 3], spread_q[0, b]) for b in users)
        sums_1[1, at_block(c)] = sum(dot(prob[b, 3], grads[b]) for b in users)
    spread = spreading(1)
    half = BLOCK // 2
    for s in range(nb):
        users = [(s + 1 - side, side) for side in range(3) if 0 <= s + 1 - side < nb]
        key = SCALE * sum(dot(shift[b, side], full[b, 2]) for b, side in users)
        value = sum(dot(prob[b, side], grads[b]) for b, side in users)
        for part, total in enumerate((key, value)):
            high, low = halves(sums_1[part, s * half : (s + 1) * half])
            grad_kv[part, s] = total + (dot(spread, high) + dot(spread, low))


def combine_kernel(nb, groups, grad_kv, got_top, got_low, got_high, out):
    present = rim_present(groups)
    spread = spreading(2)
    quarter = BLOCK // 4
    for b in range(nb):
        for part in range(2):
            total = grad_kv[part, b] + dot(spread, got_top[part, b * quarter : (b + 1) * quarter])
            if b == 0:
                total = total + jnp.where(present[0], got_low[part].astype(F32), 0.0)
            if b == nb - 1:
                total = total + jnp.where(present[1], got_high[part].astype(F32), 0.0)
            out[b, part] = total.astype(BF16)


def unpack_kernel(grad_q, grad_kv, *outs):
    for head in range(GROUP):
        at = slice(head * HEAD_DIM, (head + 1) * HEAD_DIM)
        outs[0][:, at] = grad_q[head]
        outs[1][:, at] = grad_kv[head, 0]
        outs[2][:, at] = grad_kv[head, 1]


def share():
    return lax.axis_index("mp")


def grad_kernel(*refs):
    pieces, (out_weight, out, whole) = refs[:N_MP], refs[N_MP:]
    for step, piece in enumerate(pieces):
        whole[span(share() ^ step, piece.shape[0]), :] = piece[...]
    rows = dot_nt(whole[...], out_weight[...]).astype(BF16)
    for head in range(GROUP):
        out[head] = rows[:, head * HEAD_DIM : (head + 1) * HEAD_DIM]


def project_kernel(chunks, out_weight, *refs):
    outs, (attended, whole) = refs[:-2], refs[-2:]
    for head in range(GROUP):
        attended[:, head * HEAD_DIM : (head + 1) * HEAD_DIM] = chunks[head]
    whole[...] = dot(attended[...], out_weight[...]).astype(BF16)
    for step, out in enumerate(outs):
        out[...] = whole[span(share() ^ step, out.shape[0]), :]


def swapped(x, axis, step):
    return lax.ppermute(x, axis, [(i, i ^ step) for i in range(lax.axis_size(axis))])


def regrouped(x):
    count = lax.axis_size("seq")
    members = [list(range(i, i + GROUP)) for i in range(0, count, GROUP)]
    return lax.all_to_all(x, "seq", 0, 0, axis_index_groups=members)


def beside(arrays):
    count = lax.axis_size("seq")
    if len(arrays) == 1:
        got = swapped(arrays[0], "seq", GROUP)
        return got, got
    up = [(i, i + GROUP) for i in range(count - GROUP)]
    return (
        lax.ppermute(arrays[0], "seq", up),
        lax.ppermute(arrays[1], "seq", [(j, i) for i, j in up]),
    )


def per_device(queries, keys, values, out_weight, out_grad):
    rows, width = queries.shape
    assert width == GROUP * HEAD_DIM and rows == BLOCK and lax.axis_size("mp") == N_MP
    count = lax.axis_size("seq")
    assert count % (2 * GROUP) == 0
    groups = count // GROUP
    nb = GROUP
    tokens = nb * rows
    half, quarter = rows // 2, rows // 4
    model = out_weight.shape[1]
    block = shape(2, rows, HEAD_DIM)
    rims = [block] * (1 if groups == 2 else 2)
    score_flops = 2 * tokens * 5 * BLOCK * HEAD_DIM
    weight_flops = 2 * rows * out_weight.size

    chunks, tops = call(
        pack_kernel,
        [shape(GROUP, 3, rows, HEAD_DIM), shape(GROUP, 2, quarter, HEAD_DIM)],
        (queries, keys, values),
        scratch=[pltpu.VMEM((3, rows, width), BF16), pltpu.SemaphoreType.DMA((3,))],
        space=pltpu.HBM,
    )
    tops = swapped(tops, "seq", GROUP)
    far = swapped(out_grad, "mp", 2)
    pieces = [out_grad, swapped(out_grad, "mp", 1), far, swapped(far, "mp", 1)]
    full = regrouped(chunks)
    rim_low, rim_high = beside(call(functools.partial(rim_kernel, groups), rims, (full,)))
    tops = regrouped(tops)
    (grads,) = call(
        grad_kernel,
        [shape(GROUP, rows, HEAD_DIM)],
        (*pieces, out_weight),
        scratch=[pltpu.VMEM((rows, model), BF16)],
        flops=weight_flops,
    )
    grads = regrouped(grads)
    spread_q, level_1, k_t, v_t, k1_t, v1_t, weights, stats = call(
        functools.partial(local_kernel, nb),
        [
            shape(2, nb, rows, HEAD_DIM),
            shape(2, tokens // 2, HEAD_DIM),
            shape(HEAD_DIM, tokens),
            shape(HEAD_DIM, tokens),
            shape(HEAD_DIM, tokens // 2),
            shape(HEAD_DIM, tokens // 2),
            shape(nb, 4, BLOCK, BLOCK, dtype=F32),
            shape(nb, 8, BLOCK, dtype=F32),
        ],
        (full,),
        flops=score_flops,
    )
    prob, attended = call(
        functools.partial(forward_kernel, nb, groups),
        [shape(nb, 5, BLOCK, BLOCK), shape(nb, rows, HEAD_DIM)],
        (full, spread_q, v_t, v1_t, weights, stats, tops, rim_low, rim_high),
        scratch=[pltpu.VMEM((2, BLOCK, HEAD_DIM), BF16)],
        flops=score_flops,
    )
    attended = regrouped(attended)
    mixed = call(
        project_kernel,
        [shape(rows // N_MP, model)] * N_MP,
        (attended, out_weight),
        scratch=[pltpu.VMEM((rows, width), BF16), pltpu.VMEM((rows, model), BF16)],
        flops=weight_flops,
    )
    across = (mixed[2].astype(F32) + swapped(mixed[3], "mp", 1).astype(F32)).astype(BF16)
    here = mixed[0].astype(F32) + swapped(mixed[1], "mp", 1).astype(F32)
    mixed = (here + swapped(across, "mp", 2).astype(F32)).astype(BF16)
    shift, top_grads, *rim_grads = call(
        functools.partial(slope_kernel, nb, groups),
        [shape(nb, 5, BLOCK, BLOCK), block] + rims,
        (full, spread_q, level_1, tops, rim_low, rim_high, prob, grads),
        scratch=[
            pltpu.VMEM((2, BLOCK, HEAD_DIM), BF16),
            pltpu.VMEM((2, BLOCK, HEAD_DIM), F32),
            pltpu.VMEM((2, 2, BLOCK, HEAD_DIM), F32),
        ],
        flops=score_flops,
    )
    top_grads = swapped(top_grads, "seq", GROUP)
    got_low, got_high = beside(rim_grads)
    grad_q, grad_kv = call(
        functools.partial(backward_kernel, nb),
        [shape(nb, rows, HEAD_DIM), shape(2, nb, rows, HEAD_DIM, dtype=F32)],
        (full, spread_q, k_t, k1_t, tops, rim_low, rim_high, prob, shift, grads),
        scratch=[pltpu.VMEM((HEAD_DIM, BLOCK), BF16), pltpu.VMEM((2, tokens // 2, HEAD_DIM), F32)],
        flops=3 * score_flops,
    )
    grad_q = regrouped(grad_q)
    (grad_kv,) = call(
        functools.partial(combine_kernel, nb, groups),
        [shape(nb, 2, rows, HEAD_DIM)],
        (grad_kv, top_grads, got_low, got_high),
    )
    grads = call(unpack_kernel, [shape(rows, width)] * 3, (grad_q, regrouped(grad_kv)))
    return (mixed, *grads)


def solution(mesh):
    return jax.shard_map(
        per_device,
        mesh=mesh,
        in_specs=(
            P("seq", "mp"),
            P("seq", "mp"),
            P("seq", "mp"),
            P("mp", None),
            P(("seq", "mp"), None),
        ),
        out_specs=(P(("seq", "mp"), None), P("seq", "mp"), P("seq", "mp"), P("seq", "mp")),
        check_vma=False,
    )
```

time: 101 us -> 111 us (1.099)
  local copies, waits for them, and re-layouts: 2.85 us -> 15.7 us
  blocking collectives: 0 us -> 8.06 us
  starting transfers between devices: 43.6 us -> 35.7 us
  waiting for transfers between devices: 35 us -> 32.4 us
    all_to_all x0 -> x5, starting transfers between devices: none -> 22 us  [regrouped(): return lax.all_to_all(x, 'seq', 0, 0, axis_index_groups=members)]
    ppermute x26 -> x10, starting transfers between devices: 35.3 us -> 13.7 us  [swapped(): lax.ppermute(x, axis, [(i, i ^ step) for i in range(lax.axis_size(axis))])]
    unnamed x10 -> x52, local copies, waits for them, and re-layouts: 2.85 us -> 15.7 us
    ppermute x8 -> x0, starting transfers between devices: 8.22 us -> none  [the longest x4 4.95 us: per_device(): lax.ppermute(rims[side], 'seq', [(j, i) for i, j in rim_pairs(step, count...]
    all_to_all x0 -> x1, blocking collectives: none -> 8.06 us  [regrouped(): return lax.all_to_all(x, 'seq', 0, 0, axis_index_groups=members)]
    ppermute x26 -> x10, waiting for transfers between devices: 35 us -> 32.4 us  [swapped(): lax.ppermute(x, axis, [(i, i ^ step) for i in range(lax.axis_size(axis))])]
    pallas_call x6 -> x10, Pallas kernels: 17.8 us -> 16.9 us  [call(): pl.pallas_call(kernel, out_shape=out_shape, in_specs=[pl.BlockSpec(memory...]
  transfers between devices with their start and end apart: 34 -> 15, of which waited for: 15 -> 7; matrix products, arithmetic and copies ran while one was open for 1% -> 1% of each run, Pallas kernels for 16% -> 14%
where the time goes in v3:
time: 111 us; the launch traced here: 110 us
  starting transfers between devices  35.7 us (32%)
  waiting for transfers between devices  32.4 us (29%)
  Pallas kernels  16.9 us (15%)
  local copies, waits for them, and re-layouts  15.7 us (14%)
  blocking collectives  8.06 us (7%)
    ppermute x10, waiting for transfers between devices, swapped(): lax.ppermute(x, axis, [(i, i ^ step) for i in range(lax.axis_size(axis))])  32.4 us
    all_to_all x5, starting transfers between devices, regrouped(): return lax.all_to_all(x, 'seq', 0, 0, axis_index_groups=members)  22 us
    pallas_call x10, Pallas kernels, call(): pl.pallas_call(kernel, out_shape=out_shape, in_specs=[pl.BlockSpec(memory...  16.9 us
    unnamed x52, local copies, waits for them, and re-layouts  15.7 us
    ppermute x10, starting transfers between devices, swapped(): lax.ppermute(x, axis, [(i, i ^ step) for i in range(lax.axis_size(axis))])  13.7 us
    all_to_all x1, blocking collectives, regrouped(): return lax.all_to_all(x, 'seq', 0, 0, axis_index_groups=members)  8.06 us
  transfers between devices with their start and end apart: 15, of which 7 were waited for; matrix products, arithmetic and copies ran while one was open for 1% of the time, Pallas kernels for 14%

profile of v3, /device:TPU:0, one launch (start us, length us, event | category | flops | bytes accessed | tf_op | source)
XLA Modules:
  0.0 110.5 jit_solution(10264939225159743884)
XLA Ops:
  5.3 4.0 %collective-permute-start = (bf16[4,2,64,128]{3,2,1,0:T(8,128)(2,1)S(1)}, bf16[4,2,64,128]{3,2,1,0:T(8,128)(2,1)S(1)}, u32[]{:S(2)}, u32[]{:S(2)}) collective-permute-start(bf16[4,2,64,128]{3,2,1,0:T(8,128)(2,1)S(1)} %get-tuple-element.34), channel_id=1, source_target_pairs={{0,16},{4,20},{8,24},{12,28},{16,0},{20,4},{24,8},{28,12},{1,17},{... | collective-permute-start | bytes 393224 | tf_op jit(solution)/shard_map/ppermute | solution.py:321
  9.3 6.3 %collective-permute-done = bf16[4,2,64,128]{3,2,1,0:T(8,128)(2,1)S(1)} collective-permute-done((bf16[4,2,64,128]{3,2,1,0:T(8,128)(2,1)S(1)}, bf16[4,2,64,128]{3,2,1,0:T(8,128)(2,1)S(1)}, u32[]{:S(2)}, u32[]{:S(2)}) %collective-permute-start) | collective-permute-done | bytes 131104 | tf_op jit(solution)/shard_map/ppermute | solution.py:321
  15.6 8.1 %all_to_all.30.refs_6_.refs_3_.tops = bf16[4,2,64,128]{3,2,1,0:T(8,128)(2,1)} all-to-all(bf16[4,2,64,128]{3,2,1,0:T(8,128)(2,1)S(1)} %collective-permute-done), channel_id=1, replica_groups={{0,4,8,12},{16,20,24,28},{1,5,9,13},{17,21,25,29},{2,6,10,14},{18,22,26..., dimensions={0} | all-to-all | bytes 262144 | tf_op jit(solution)/shard_map/all_to_all | solution.py:327
  23.7 3.5 %all-to-all-start = ((bf16[4,3,256,128]{3,2,1,0:T(8,128)(2,1)}), bf16[4,3,256,128]{3,2,1,0:T(8,128)(2,1)S(1)}, u32[]{:S(2)}, u32[]{:S(2)}) async-start(bf16[4,3,256,128]{3,2,1,0:T(8,128)(2,1)} %copy-done.9), calls=%async_computation | async-start | bytes 1572864 | tf_op jit(solution)/shard_map/all_to_all | solution.py:327
  27.2 1.6 %collective-permute-start.6 = (bf16[64,2048]{1,0:T(8,128)(2,1)S(1)}, bf16[64,2048]{1,0:T(8,128)(2,1)S(1)}, u32[]{:S(2)}, u32[]{:S(2)}) collective-permute-start(bf16[64,2048]{1,0:T(8,128)(2,1)S(1)} %copy-done.17), channel_id=1, source_target_pairs={{0,2},{1,3},{2,0},{3,1},{4,6},{5,7},{6,4},{7,5},{8,10},{9,11},{10,... | collective-permute-start | bytes 786440 | tf_op jit(solution)/shard_map/ppermute | solution.py:321
  28.8 5.0 %collective-permute-done.6.refs_2_ = bf16[64,2048]{1,0:T(8,128)(2,1)S(1)} collective-permute-done((bf16[64,2048]{1,0:T(8,128)(2,1)S(1)}, bf16[64,2048]{1,0:T(8,128)(2,1)S(1)}, u32[]{:S(2)}, u32[]{:S(2)}) %collective-permute-start.6) | collective-permute-done | bytes 262176 | tf_op jit(solution)/shard_map/ppermute | solution.py:321
  33.9 1.5 %collective-permute-done.7.refs_3_ = bf16[64,2048]{1,0:T(8,128)(2,1)S(1)} collective-permute-done((bf16[64,2048]{1,0:T(8,128)(2,1)S(1)}, bf16[64,2048]{1,0:T(8,128)(2,1)S(1)}, u32[]{:S(2)}, u32[]{:S(2)}) %collective-permute-start.7) | collective-permute-done | bytes 262176 | tf_op jit(solution)/shard_map/ppermute | solution.py:321
  35.4 1.5 %shard_map.89 = bf16[4,256,128]{2,1,0:T(8,128)(2,1)} custom-call(bf16[64,2048]{1,0:T(8,128)(2,1)S(1)} %copy-done.17, bf16[64,2048]{1,0:T(8,128)(2,1)S(1)} %collective-permute-done.5.refs_1_, bf16[64,2048]{1,0:T(8,128)(2,1)S(1)} %collective-permute-done.6.refs_2_, bf16[64,2048]{1,0:T(8,128)(2,1)S(1)} %collective-permute-done.7.refs_3_, ...), custom_call_target="tpu_custom_call" | custom-call | flops 536870912 | bytes 3407872 | tf_op jit(solution)/shard_map/pallas_call | solution.py:36
  36.9 4.0 %all-to-all-start.3 = ((bf16[4,256,128]{2,1,0:T(8,128)(2,1)}), bf16[4,256,128]{2,1,0:T(8,128)(2,1)}, u32[]{:S(2)}, u32[]{:S(2)}) async-start(bf16[4,256,128]{2,1,0:T(8,128)(2,1)} %shard_map.89), calls=%async_computation.3 | async-start | bytes 524288 | tf_op jit(solution)/shard_map/all_to_all | solution.py:327
  41.0 3.4 %collective-permute-start.1 = (bf16[2,256,128]{2,1,0:T(8,128)(2,1)S(1)}, bf16[2,256,128]{2,1,0:T(8,128)(2,1)S(1)}, u32[]{:S(2)}, u32[]{:S(2)}) collective-permute-start(bf16[2,256,128]{2,1,0:T(8,128)(2,1)S(1)} %shard_map.86), channel_id=1, source_target_pairs={{0,16},{4,20},{8,24},{12,28},{16,0},{20,4},{24,8},{28,12},{1,17},{... | collective-permute-start | bytes 393224 | tf_op jit(solution)/shard_map/ppermute | solution.py:321
  44.4 1.8 %shard_map.85 = (bf16[2,4,256,128]{3,2,1,0:T(8,128)(2,1)S(1)}, bf16[2,512,128]{2,1,0:T(8,128)(2,1)S(1)}, bf16[128,1024]{1,0:T(8,128)(2,1)S(1)}, bf16[128,1024]{1...) custom-call(bf16[4,3,256,128]{3,2,1,0:T(8,128)(2,1)S(1)} %all-to-all, ...), custom_call_target="tpu_custom_call" | custom-call | flops 335544320 | bytes 6586368 | tf_op jit(solution)/shard_map/pallas_call | solution.py:36
  49.2 1.6 %shard_map.87 = (bf16[4,5,256,256]{3,2,1,0:T(8,128)(2,1)S(1)}, bf16[4,256,128]{2,1,0:T(8,128)(2,1)S(1)}) custom-call(bf16[4,3,256,128]{3,2,1,0:T(8,128)(2,1)S(1)} %all-to-all-done.full.refs_0_, bf16[2,4,256,128]{3,2,1,0:T(8,128)(2,1)S(1)} %get-tuple-element.29.refs_1_.spread_q, bf16[128,1024]{1,0:T(8,128)(2,1)S(1)} %get-tuple-element.30.refs_2_, ...), custom_call_target="tpu_custom_call" | custom-call | flops 335544320 | bytes 9207808 | tf_op jit(solution)/shard_map/pallas_call | solution.py:36
  52.3 6.7 %all-to-all-start.2 = ((bf16[4,256,128]{2,1,0:T(8,128)(2,1)}), bf16[4,256,128]{2,1,0:T(8,128)(2,1)}, u32[]{:S(2)}, u32[]{:S(2)}) async-start(bf16[4,256,128]{2,1,0:T(8,128)(2,1)} %copy-done.16), calls=%async_computation.2 | async-start | bytes 524288 | tf_op jit(solution)/shard_map/all_to_all | solution.py:327
  61.9 3.8 %shard_map.90 = (bf16[4,5,256,256]{3,2,1,0:T(8,128)(2,1)S(1)}, bf16[2,256,128]{2,1,0:T(8,128)(2,1)S(1)}, bf16[2,256,128]{2,1,0:T(8,128)(2,1)S(1)}) custom-call(bf16[4,3,256,128]{3,2,1,0:T(8,128)(2,1)S(1)} %all-to-all-done.full.refs_0_, bf16[2,4,256,128]{3,2,1,0:T(8,128)(2,1)S(1)} %copy-done.3, bf16[2,512,128]{2,1,0:T(8,128)(2,1)S(1)} %copy-done.14, ...), custom_call_target="tpu_custom_call" | custom-call | flops 335544320 | bytes 7733248 | tf_op jit(solution)/shard_map/pallas_call | solution.py:36
  67.1 3.4 %shard_map.91 = (bf16[4,256,128]{2,1,0:T(8,128)(2,1)S(1)}, f32[2,4,256,128]{3,2,1,0:T(8,128)S(1)}) custom-call(bf16[4,3,256,128]{3,2,1,0:T(8,128)(2,1)S(1)} %all-to-all-done.full.refs_0_, bf16[2,4,256,128]{3,2,1,0:T(8,128)(2,1)S(1)} %copy-done.3, bf16[128,1024]{1,0:T(8,128)(2,1)S(1)} %copy-done.19, bf16[128,512]{1,0:T(8,128)(2,1)S(1)} %copy-done.21, ...), custom_call_target="tpu_custom_call" | custom-call | flops 1006632960 | bytes 8912896 | tf_op jit(solution)/shard_map/pallas_call | solution.py:36
  72.1 4.3 %all-to-all-start.4 = ((bf16[4,256,128]{2,1,0:T(8,128)(2,1)}), bf16[4,256,128]{2,1,0:T(8,128)(2,1)S(1)}, u32[]{:S(2)}, u32[]{:S(2)}) async-start(bf16[4,256,128]{2,1,0:T(8,128)(2,1)} %copy-done.15), calls=%async_computation.4 | async-start | bytes 524288 | tf_op jit(solution)/shard_map/all_to_all | solution.py:327
  76.5 1.6 %copy-done.1 = bf16[512,2048]{1,0:T(8,128)(2,1)S(1)} copy-done((bf16[512,2048]{1,0:T(8,128)(2,1)S(1)}, bf16[512,2048]{1,0:T(8,128)(2,1)}, u32[]{:S(2)}) %copy-start.1) | copy-done | bytes 2097176
  78.1 1.8 %shard_map.88 = (bf16[64,2048]{1,0:T(8,128)(2,1)S(1)}, bf16[64,2048]{1,0:T(8,128)(2,1)S(1)}, bf16[64,2048]{1,0:T(8,128)(2,1)S(1)}, bf16[64,2048]{1,0:T(8,128)(2,1)S(1)}) custom-call(bf16[4,256,128]{2,1,0:T(8,128)(2,1)} %all-to-all-done.2.chunks, bf16[512,2048]{1,0:T(8,128)(2,1)S(1)} %copy-done.1), custom_call_target="tpu_custom_call" | custom-call | flops 536870912 | bytes 3407872 | tf_op jit(solution)/shard_map/pallas_call | solution.py:36
  80.0 2.6 %collective-permute-start.8 = (bf16[2,256,128]{2,1,0:T(8,128)(2,1)S(1)}, bf16[2,256,128]{2,1,0:T(8,128)(2,1)S(1)}, u32[]{:S(2)}, u32[]{:S(2)}) collective-permute-start(bf16[2,256,128]{2,1,0:T(8,128)(2,1)S(1)} %copy-done.25), channel_id=1, source_target_pairs={{0,16},{4,20},{8,24},{12,28},{16,0},{20,4},{24,8},{28,12},{1,17},{... | collective-permute-start | bytes 393224 | tf_op jit(solution)/shard_map/ppermute | solution.py:321
  83.0 9.9 %collective-permute-done.8.got_top = bf16[2,256,128]{2,1,0:T(8,128)(2,1)S(1)} collective-permute-done((bf16[2,256,128]{2,1,0:T(8,128)(2,1)S(1)}, bf16[2,256,128]{2,1,0:T(8,128)(2,1)S(1)}, u32[]{:S(2)}, u32[]{:S(2)}) %collective-permute-start.8) | collective-permute-done | bytes 131104 | tf_op jit(solution)/shard_map/ppermute | solution.py:321
  92.9 2.3 %collective-permute-done.9.got_low.got_high = bf16[2,256,128]{2,1,0:T(8,128)(2,1)S(1)} collective-permute-done((bf16[2,256,128]{2,1,0:T(8,128)(2,1)S(1)}, bf16[2,256,128]{2,1,0:T(8,128)(2,1)S(1)}, u32[]{:S(2)}, u32[]{:S(2)}) %collective-permute-start.9) | collective-permute-done | bytes 131104 | tf_op jit(solution)/shard_map/ppermute | solution.py:321
  96.3 3.5 %all-to-all-start.5 = ((bf16[4,2,256,128]{3,2,1,0:T(8,128)(2,1)}), bf16[4,2,256,128]{3,2,1,0:T(8,128)(2,1)S(1)}, u32[]{:S(2)}, u32[]{:S(2)}) async-start(bf16[4,2,256,128]{3,2,1,0:T(8,128)(2,1)} %shard_map.92), calls=%async_computation.5 | async-start | bytes 1048576 | tf_op jit(solution)/shard_map/all_to_all | solution.py:327
  99.9 1.6 %collective-permute-start.4 = (bf16[64,2048]{1,0:T(8,128)(2,1)S(1)}, bf16[64,2048]{1,0:T(8,128)(2,1)S(1)}, u32[]{:S(2)}, u32[]{:S(2)}) collective-permute-start(bf16[64,2048]{1,0:T(8,128)(2,1)S(1)} %add_convert_fusion.1), channel_id=1, source_target_pairs={{0,2},{1,3},{2,0},{3,1},{4,6},{5,7},{6,4},{7,5},{8,10},{9,11},{10,... | collective-permute-start | bytes 786440 | tf_op jit(solution)/shard_map/ppermute | solution.py:321
  101.4 7.2 %collective-permute-done.4 = bf16[64,2048]{1,0:T(8,128)(2,1)S(1)} collective-permute-done((bf16[64,2048]{1,0:T(8,128)(2,1)S(1)}, bf16[64,2048]{1,0:T(8,128)(2,1)S(1)}, u32[]{:S(2)}, u32[]{:S(2)}) %collective-permute-start.4) | collective-permute-done | bytes 262176 | tf_op jit(solution)/shard_map/ppermute | solution.py:321
  (71 shorter events, 18.5 us)
Async XLA Ops:
  3.5 23.7 %copy-start.17 = (bf16[64,2048]{1,0:T(8,128)(2,1)S(1)}, bf16[64,2048]{1,0:T(8,128)(2,1)}, u32[]{:S(2)}) copy-start(bf16[64,2048]{1,0:T(8,128)(2,1)} %refs_0_.1) | copy-start | bytes 786436
  3.5 31.9 %copy-start = (bf16[512,2048]{1,0:T(8,128)(2,1)S(1)}, bf16[512,2048]{1,0:T(8,128)(2,1)}, u32[]{:S(2)}) copy-start(bf16[512,2048]{1,0:T(8,128)(2,1)} %refs_4_.1) | copy-start | bytes 6291460
  5.3 10.3 %collective-permute-start = (bf16[4,2,64,128]{3,2,1,0:T(8,128)(2,1)S(1)}, bf16[4,2,64,128]{3,2,1,0:T(8,128)(2,1)S(1)}, u32[]{:S(2)}, u32[]{:S(2)}) collective-permute-start(bf16[4,2,64,128]{3,2,1,0:T(8,128)(2,1)S(1)} %get-tuple-element.34), channel_id=1, source_target_pairs={{0,16},{4,20},{8,24},{12,28},{16,0},{20,4},{24,8},{28,12},{1,17},{... | collective-permute-start | bytes 393224 | tf_op jit(solution)/shard_map/ppermute | solution.py:321
  23.7 13.2 %all-to-all-start = ((bf16[4,3,256,128]{3,2,1,0:T(8,128)(2,1)}), bf16[4,3,256,128]{3,2,1,0:T(8,128)(2,1)S(1)}, u32[]{:S(2)}, u32[]{:S(2)}) async-start(bf16[4,3,256,128]{3,2,1,0:T(8,128)(2,1)} %copy-done.9), calls=%async_computation | async-start | bytes 1572864 | tf_op jit(solution)/shard_map/all_to_all | solution.py:327
  27.2 6.7 %collective-permute-start.6 = (bf16[64,2048]{1,0:T(8,128)(2,1)S(1)}, bf16[64,2048]{1,0:T(8,128)(2,1)S(1)}, u32[]{:S(2)}, u32[]{:S(2)}) collective-permute-start(bf16[64,2048]{1,0:T(8,128)(2,1)S(1)} %copy-done.17), channel_id=1, source_target_pairs={{0,2},{1,3},{2,0},{3,1},{4,6},{5,7},{6,4},{7,5},{8,10},{9,11},{10,... | collective-permute-start | bytes 786440 | tf_op jit(solution)/shard_map/ppermute | solution.py:321
  28.8 5.1 %collective-permute-start.5 = (bf16[64,2048]{1,0:T(8,128)(2,1)S(1)}, bf16[64,2048]{1,0:T(8,128)(2,1)S(1)}, u32[]{:S(2)}, u32[]{:S(2)}) collective-permute-start(bf16[64,2048]{1,0:T(8,128)(2,1)S(1)} %copy-done.17), channel_id=1, source_target_pairs={{0,1},{1,0},{2,3},{3,2},{4,5},{5,4},{6,7},{7,6},{8,9},{9,8},{10,11... | collective-permute-start | bytes 786440 | tf_op jit(solution)/shard_map/ppermute | solution.py:321
  33.9 1.5 %collective-permute-start.7 = (bf16[64,2048]{1,0:T(8,128)(2,1)S(1)}, bf16[64,2048]{1,0:T(8,128)(2,1)S(1)}, u32[]{:S(2)}, u32[]{:S(2)}) collective-permute-start(bf16[64,2048]{1,0:T(8,128)(2,1)S(1)} %collective-permute-done.6.refs_2_), channel_id=1, source_target_pairs={{0,1},{1,0},{2,3},{3,2},{4,5},{5,4},{6,7},{7,6},{8,9},{9,8},{10,11... | collective-permute-start | bytes 786440 | tf_op jit(solution)/shard_map/ppermute | solution.py:321
  36.9 15.5 %all-to-all-start.3 = ((bf16[4,256,128]{2,1,0:T(8,128)(2,1)}), bf16[4,256,128]{2,1,0:T(8,128)(2,1)}, u32[]{:S(2)}, u32[]{:S(2)}) async-start(bf16[4,256,128]{2,1,0:T(8,128)(2,1)} %shard_map.89), calls=%async_computation.3 | async-start | bytes 524288 | tf_op jit(solution)/shard_map/all_to_all | solution.py:327
  41.0 7.3 %collective-permute-start.1 = (bf16[2,256,128]{2,1,0:T(8,128)(2,1)S(1)}, bf16[2,256,128]{2,1,0:T(8,128)(2,1)S(1)}, u32[]{:S(2)}, u32[]{:S(2)}) collective-permute-start(bf16[2,256,128]{2,1,0:T(8,128)(2,1)S(1)} %shard_map.86), channel_id=1, source_target_pairs={{0,16},{4,20},{8,24},{12,28},{16,0},{20,4},{24,8},{28,12},{1,17},{... | collective-permute-start | bytes 393224 | tf_op jit(solution)/shard_map/ppermute | solution.py:321
  52.3 19.8 %all-to-all-start.2 = ((bf16[4,256,128]{2,1,0:T(8,128)(2,1)}), bf16[4,256,128]{2,1,0:T(8,128)(2,1)}, u32[]{:S(2)}, u32[]{:S(2)}) async-start(bf16[4,256,128]{2,1,0:T(8,128)(2,1)} %copy-done.16), calls=%async_computation.2 | async-start | bytes 524288 | tf_op jit(solution)/shard_map/all_to_all | solution.py:327
  61.9 5.2 %copy-start.6 = (bf16[4,2,64,128]{3,2,1,0:T(8,128)(2,1)S(1)}, bf16[4,2,64,128]{3,2,1,0:T(8,128)(2,1)}, u32[]{:S(2)}) copy-start(bf16[4,2,64,128]{3,2,1,0:T(8,128)(2,1)} %all_to_all.30.refs_6_.refs_3_.tops) | copy-start | bytes 393220
  61.9 5.2 %copy-start.19 = (bf16[128,1024]{1,0:T(8,128)(2,1)S(1)}, bf16[128,1024]{1,0:T(8,128)(2,1)}, u32[]{:S(2)}) copy-start(bf16[128,1024]{1,0:T(8,128)(2,1)} %copy-done.18) | copy-start | bytes 786436
  61.9 5.2 %copy-start.21 = (bf16[128,512]{1,0:T(8,128)(2,1)S(1)}, bf16[128,512]{1,0:T(8,128)(2,1)}, u32[]{:S(2)}) copy-start(bf16[128,512]{1,0:T(8,128)(2,1)} %copy-done.20) | copy-start | bytes 393220
  72.1 7.8 %copy-start.25 = (bf16[2,256,128]{2,1,0:T(8,128)(2,1)S(1)}, bf16[2,256,128]{2,1,0:T(8,128)(2,1)}, u32[]{:S(2)}) copy-start(bf16[2,256,128]{2,1,0:T(8,128)(2,1)} %copy-done.24) | copy-start | bytes 393220
  72.1 10.4 %copy-start.23 = (bf16[2,256,128]{2,1,0:T(8,128)(2,1)S(1)}, bf16[2,256,128]{2,1,0:T(8,128)(2,1)}, u32[]{:S(2)}) copy-start(bf16[2,256,128]{2,1,0:T(8,128)(2,1)} %copy-done.22) | copy-start | bytes 393220
  72.1 24.2 %all-to-all-start.4 = ((bf16[4,256,128]{2,1,0:T(8,128)(2,1)}), bf16[4,256,128]{2,1,0:T(8,128)(2,1)S(1)}, u32[]{:S(2)}, u32[]{:S(2)}) async-start(bf16[4,256,128]{2,1,0:T(8,128)(2,1)} %copy-done.15), calls=%async_computation.4 | async-start | bytes 524288 | tf_op jit(solution)/shard_map/all_to_all | solution.py:327
  76.5 1.6 %copy-start.1 = (bf16[512,2048]{1,0:T(8,128)(2,1)S(1)}, bf16[512,2048]{1,0:T(8,128)(2,1)}, u32[]{:S(2)}) copy-start(bf16[512,2048]{1,0:T(8,128)(2,1)} %refs_4_.1) | copy-start | bytes 6291460
  78.1 17.1 %copy-start.8 = (f32[2,4,256,128]{3,2,1,0:T(8,128)S(1)}, f32[2,4,256,128]{3,2,1,0:T(8,128)}, u32[]{:S(2)}) copy-start(f32[2,4,256,128]{3,2,1,0:T(8,128)} %copy-done.7) | copy-start | bytes 3145732
  79.9 19.9 %collective-permute-start.3 = (bf16[64,2048]{1,0:T(8,128)(2,1)S(1)}, bf16[64,2048]{1,0:T(8,128)(2,1)S(1)}, u32[]{:S(2)}, u32[]{:S(2)}) collective-permute-start(bf16[64,2048]{1,0:T(8,128)(2,1)S(1)} %get-tuple-element.39), channel_id=1, source_target_pairs={{0,1},{1,0},{2,3},{3,2},{4,5},{5,4},{6,7},{7,6},{8,9},{9,8},{10,11... | collective-permute-start | bytes 786440 | tf_op jit(solution)/shard_map/ppermute | solution.py:321
  80.0 12.9 %collective-permute-start.8 = (bf16[2,256,128]{2,1,0:T(8,128)(2,1)S(1)}, bf16[2,256,128]{2,1,0:T(8,128)(2,1)S(1)}, u32[]{:S(2)}, u32[]{:S(2)}) collective-permute-start(bf16[2,256,128]{2,1,0:T(8,128)(2,1)S(1)} %copy-done.25), channel_id=1, source_target_pairs={{0,16},{4,20},{8,24},{12,28},{16,0},{20,4},{24,8},{28,12},{1,17},{... | collective-permute-start | bytes 393224 | tf_op jit(solution)/shard_map/ppermute | solution.py:321
  82.6 12.6 %collective-permute-start.9 = (bf16[2,256,128]{2,1,0:T(8,128)(2,1)S(1)}, bf16[2,256,128]{2,1,0:T(8,128)(2,1)S(1)}, u32[]{:S(2)}, u32[]{:S(2)}) collective-permute-start(bf16[2,256,128]{2,1,0:T(8,128)(2,1)S(1)} %copy-done.23), channel_id=1, source_target_pairs={{0,16},{4,20},{8,24},{12,28},{16,0},{20,4},{24,8},{28,12},{1,17},{... | collective-permute-start | bytes 393224 | tf_op jit(solution)/shard_map/ppermute | solution.py:321
  96.3 5.1 %collective-permute-start.2 = (bf16[64,2048]{1,0:T(8,128)(2,1)S(1)}, bf16[64,2048]{1,0:T(8,128)(2,1)S(1)}, u32[]{:S(2)}, u32[]{:S(2)}) collective-permute-start(bf16[64,2048]{1,0:T(8,128)(2,1)S(1)} %get-tuple-element.37), channel_id=1, source_target_pairs={{0,1},{1,0},{2,3},{3,2},{4,5},{5,4},{6,7},{7,6},{8,9},{9,8},{10,11... | collective-permute-start | bytes 786440 | tf_op jit(solution)/shard_map/ppermute | solution.py:321
  96.3 13.1 %all-to-all-start.5 = ((bf16[4,2,256,128]{3,2,1,0:T(8,128)(2,1)}), bf16[4,2,256,128]{3,2,1,0:T(8,128)(2,1)S(1)}, u32[]{:S(2)}, u32[]{:S(2)}) async-start(bf16[4,2,256,128]{3,2,1,0:T(8,128)(2,1)} %shard_map.92), calls=%async_computation.5 | async-start | bytes 1048576 | tf_op jit(solution)/shard_map/all_to_all | solution.py:327
  99.9 8.8 %collective-permute-start.4 = (bf16[64,2048]{1,0:T(8,128)(2,1)S(1)}, bf16[64,2048]{1,0:T(8,128)(2,1)S(1)}, u32[]{:S(2)}, u32[]{:S(2)}) collective-permute-start(bf16[64,2048]{1,0:T(8,128)(2,1)S(1)} %add_convert_fusion.1), channel_id=1, source_target_pairs={{0,2},{1,3},{2,0},{3,1},{4,6},{5,7},{6,4},{7,5},{8,10},{9,11},{10,... | collective-permute-start | bytes 786440 | tf_op jit(solution)/shard_map/ppermute | solution.py:321
  (17 other events, 14.1 us)

commit v4 on v3

v4 whole, which is shorter than its diff:
```python
import functools

import jax
import jax.numpy as jnp
from jax import lax
from jax.experimental import pallas as pl
from jax.experimental.pallas import tpu as pltpu
from jax.sharding import PartitionSpec as P

HEAD_DIM = 128
BLOCK = 256
LEVELS = 2
GROUP = 4
N_MP = 4
SCALE = HEAD_DIM**-0.5
LOG2E = 1.4426950408889634
BF16 = jnp.bfloat16
F32 = jnp.float32


def dot(a, b):
    return lax.dot_general(a, b, (((1,), (0,)), ((), ())), preferred_element_type=F32)


def dot_nt(a, b):
    return lax.dot_general(a, b, (((1,), (1,)), ((), ())), preferred_element_type=F32)


def shape(*dims, dtype=BF16):
    return jax.ShapeDtypeStruct(dims, dtype)


def call(kernel, out_shape, args, scratch=(), flops=0, limit=32, space=pltpu.VMEM):
    whole = pl.BlockSpec(memory_space=pltpu.VMEM)
    moved = sum(x.size * x.dtype.itemsize for x in (*args, *out_shape))
    return pl.pallas_call(
        kernel,
        out_shape=out_shape,
        in_specs=[pl.BlockSpec(memory_space=space)] * len(args),
        out_specs=[whole] * len(out_shape),
        scratch_shapes=scratch,
        compiler_params=pltpu.CompilerParams(vmem_limit_bytes=limit << 20),
        cost_estimate=pl.CostEstimate(flops=flops, bytes_accessed=moved if flops else 0, transcendentals=0),
    )(*args)


def columns(index):
    return pl.ds(pl.multiple_of(index * HEAD_DIM, HEAD_DIM), HEAD_DIM)


def span(index, size):
    return pl.ds(pl.multiple_of(index * size, size), size)


def iota(dims, axis):
    return lax.broadcasted_iota(jnp.int32, dims, axis)


def averaging(level):
    dims = (BLOCK, BLOCK)
    same = (iota(dims, 0) >> level) == (iota(dims, 1) >> level)
    return jnp.where(same, 2.0**-level, 0.0).astype(BF16)


def pooling():
    dims = (BLOCK // 2, BLOCK)
    return jnp.where(iota(dims, 0) == (iota(dims, 1) >> 1), 0.5, 0.0).astype(BF16)


def spreading(level):
    dims = (BLOCK, BLOCK >> level)
    return jnp.where((iota(dims, 0) >> level) == iota(dims, 1), 2.0**-level, 0.0).astype(BF16)


def halves(x):
    high = x.astype(BF16)
    return high, (x - high.astype(F32)).astype(BF16)


def at_block(b):
    return slice(b * BLOCK, (b + 1) * BLOCK)


def sibling(b):
    return (b >> 1) ^ 1


def rim_present(groups):
    group = lax.axis_index("seq") // GROUP
    return group > 0, group < groups - 1


def member():
    return lax.rem(lax.axis_index("seq"), GROUP)


def columns(index):
    return pl.ds(pl.multiple_of(index * HEAD_DIM, HEAD_DIM), HEAD_DIM)


def pack_kernel(k, v, *outs):
    me = member()
    for step, out in enumerate(outs):
        for part, source in enumerate((k, v)):
            out[part] = source[:, columns(me ^ step)]


def gather_kernel(nb, groups, q, far, *refs):
    chunks, (near, level_1, far_out, *refs) = refs[:GROUP], refs[GROUP:]
    far_out[...] = far[...]
    rims, queries = refs[:-GROUP], refs[-GROUP:]
    me = member()
    for step, chunk in enumerate(chunks):
        near[me ^ step] = chunk[...]
        queries[step][...] = q[:, columns(me ^ step)]
    pool = pooling()
    half = BLOCK // 2
    for part in range(2):
        for b in range(nb):
            level_1[part, b * half : (b + 1) * half] = dot(pool, near[b, part]).astype(BF16)
        for c in range(nb // 2):
            block = dot(pool, level_1[part, at_block(c)]).astype(BF16)
            rims[0][part, c * half : (c + 1) * half] = block
    if groups == 2:
        upper = lax.axis_index("seq") >= GROUP
        rims[0][2:] = jnp.where(upper, near[0], near[nb - 1])
    else:
        rims[1][...] = near[nb - 1]
        rims[2][...] = near[0]


def from_others(groups, refs):
    if groups == 2:
        return (refs[0].at[:2], refs[0].at[2:], refs[0].at[2:]), refs[1:]
    return refs[:3], refs[3:]


def near_sides(b, nb):
    return [side for side in range(3) if 0 <= b + side - 1 < nb]


def local_kernel(nb, near, level_1, *refs):
    chunks, _, (query, k_t, v_t, k1_t, v1_t, weights, stats) = refs[:GROUP], refs[GROUP], refs[GROUP + 1 :]
    me = member()
    for step, chunk in enumerate(chunks):
        query[0, me ^ step] = chunk[...]
    even_1, even_2 = averaging(1), averaging(2)
    for b in range(nb):
        once = dot(even_1, query[0, b]).astype(BF16)
        query[1, b] = once
        query[2, b] = dot(even_2, once).astype(BF16)
        for part, transposed in enumerate((k_t, v_t)):
            transposed[:, at_block(b)] = near[b, part].T
    for c in range(nb // 2):
        for part, transposed in enumerate((k1_t, v1_t)):
            transposed[:, at_block(c)] = level_1[part, at_block(c)].T
    for b in range(nb):
        sides = near_sides(b, nb)
        scores = [dot_nt(near[b + side - 1, 0], query[0, b]) * (SCALE * LOG2E) for side in sides]
        coarse = dot_nt(level_1[0, at_block(sibling(b))], query[1, b]) * (SCALE * LOG2E)
        top = coarse.max(0, keepdims=True)
        for score in scores:
            top = jnp.maximum(top, score.max(0, keepdims=True))
        weight = 2.0 * jnp.exp2(coarse - top)
        weights[b, 3] = weight
        total = weight.sum(0, keepdims=True)
        for side, score in zip(sides, scores):
            weight = jnp.exp2(score - top)
            weights[b, side] = weight
            total = total + weight.sum(0, keepdims=True)
        stats[b, :1] = top
        stats[b, 1:2] = total


def rim_sides(b, nb):
    return [side for side in range(3) if not 0 <= b + side - 1 < nb]


def forward_kernel(nb, groups, *refs):
    (query, v_t, v1_t, weights, stats), refs = refs[:5], refs[5:]
    (top_2, rim_low, rim_high), refs = from_others(groups, refs)
    prob, *outs, attended = refs[GROUP:]
    present = rim_present(groups)
    v2_t = top_2[1].T
    for b in range(nb):
        sides = rim_sides(b, nb)
        scores = []
        for side in sides:
            score = dot_nt((rim_high if side else rim_low)[0], query[0, b]) * (SCALE * LOG2E)
            scores.append(jnp.where(present[side // 2], score, -jnp.inf))
        coarse = dot_nt(top_2[0], query[2, b]) * (SCALE * LOG2E)
        old = stats[b, :1]
        top = jnp.maximum(old, coarse.max(0, keepdims=True))
        for score in scores:
            top = jnp.maximum(top, score.max(0, keepdims=True))
        shrink = jnp.exp2(old - top)
        far = 4.0 * jnp.exp2(coarse - top)
        total = shrink * stats[b, 1:2] + far.sum(0, keepdims=True)
        fresh = []
        for score in scores:
            fresh.append(jnp.exp2(score - top))
            total = total + fresh[-1].sum(0, keepdims=True)
        inverse = 1.0 / total
        shrink = shrink * inverse
        prob[b, 4] = (far * inverse).astype(BF16)
        prob[b, 3] = (weights[b, 3] * shrink).astype(BF16)
        context = dot(v2_t, prob[b, 4]) + dot(v1_t[:, at_block(sibling(b))], prob[b, 3])
        for side in near_sides(b, nb):
            prob[b, side] = (weights[b, side] * shrink).astype(BF16)
            context = context + dot(v_t[:, at_block(b + side - 1)], prob[b, side])
        for side, weight in zip(sides, fresh):
            prob[b, side] = (weight * inverse).astype(BF16)
            context = context + dot((rim_high if side else rim_low)[1].T, prob[b, side])
        attended[b] = context.T.astype(BF16)
    me = member()
    for step, out in enumerate(outs):
        out[...] = attended[me ^ step]


def slope_kernel(nb, groups, *refs):
    (query, near, level_1, prob), refs = refs[:4], refs[4:]
    (top_2, rim_low, rim_high), refs = from_others(groups, refs)
    chunks, (grads, shift, *rim_outs, sums, rim_sums) = refs[:GROUP], refs[GROUP:]
    me = member()
    for step, chunk in enumerate(chunks):
        grads[me ^ step] = chunk[...]
    for b in range(nb):
        grad = grads[b]
        slopes = []
        for side in range(3):
            if side in near_sides(b, nb):
                value = near[b + side - 1, 1]
            else:
                value = (rim_high if side else rim_low)[1]
            slopes.append(dot_nt(value, grad))
        slopes.append(dot_nt(level_1[1, at_block(sibling(b))], grad))
        slopes.append(dot_nt(top_2[1], grad))
        delta = 0.0
        for part, slope in enumerate(slopes):
            delta = delta + (prob[b, part].astype(F32) * slope).sum(0, keepdims=True)
        for part, slope in enumerate(slopes):
            shift[b, part] = (prob[b, part].astype(F32) * (slope - delta)).astype(BF16)
        for side in rim_sides(b, nb):
            rim_sums[side // 2, 0] = SCALE * dot(shift[b, side], query[0, b])
            rim_sums[side // 2, 1] = dot(prob[b, side], grad)
        key, value = SCALE * dot(shift[b, 4], query[2, b]), dot(prob[b, 4], grad)
        if b:
            key, value = key + sums[0], value + sums[1]
        if b < nb - 1:
            sums[0], sums[1] = key, value
        else:
            rim_outs[0][0], rim_outs[0][1] = key.astype(BF16), value.astype(BF16)
    low, high = rim_sums[0], rim_sums[1]
    if groups == 2:
        upper = lax.axis_index("seq") >= GROUP
        rim_outs[0][2:] = jnp.where(upper, low, high).astype(BF16)
    else:
        rim_outs[1][...] = high.astype(BF16)
        rim_outs[2][...] = low.astype(BF16)


def backward_kernel(nb, groups, *refs):
    (query, k_t, k1_t, prob, shift, grads), refs = refs[:6], refs[6:]
    (top_2, rim_low, rim_high), refs = from_others(groups, refs)
    *outs, grad_kv, grad_q, sums_1 = refs
    k2_t = top_2[0].T
    even_1, even_2 = averaging(1), averaging(2)
    for b in range(nb):
        grad_t = 0.0
        for side in range(3):
            if side in near_sides(b, nb):
                key_t = k_t[:, at_block(b + side - 1)]
            else:
                key_t = (rim_high if side else rim_low)[0].T
            grad_t = grad_t + dot(key_t, shift[b, side])
        for spread, key_t, part in ((even_1, k1_t[:, at_block(sibling(b))], 3), (even_2, k2_t, 4)):
            high, low = halves(dot(key_t, shift[b, part]))
            grad_t = grad_t + (dot(high, spread) + dot(low, spread))
        grad_q[b] = (SCALE * grad_t).T.astype(BF16)
    me = member()
    for step, out in enumerate(outs):
        out[...] = grad_q[me ^ step]
    for c in range(nb // 2):
        users = [b for b in range(nb) if sibling(b) == c]
        sums_1[0, at_block(c)] = SCALE * sum(dot(shift[b, 3], query[1, b]) for b in users)
        sums_1[1, at_block(c)] = sum(dot(prob[b, 3], grads[b]) for b in users)
    spread = spreading(1)
    half = BLOCK // 2
    for s in range(nb):
        users = [(s + 1 - side, side) for side in range(3) if 0 <= s + 1 - side < nb]
        key = SCALE * sum(dot(shift[b, side], query[0, b]) for b, side in users)
        value = sum(dot(prob[b, side], grads[b]) for b, side in users)
        for part, total in enumerate((key, value)):
            high, low = halves(sums_1[part, s * half : (s + 1) * half])
            grad_kv[part, s] = total + (dot(spread, high) + dot(spread, low))


def share_kernel(kept, got, _, across, here):
    across[...] = (kept[1].astype(F32) + got[1].astype(F32)).astype(BF16)
    here[...] = kept[0].astype(F32) + got[0].astype(F32)


def combine_kernel(nb, groups, grad_kv, *refs):
    (got_top, got_low, got_high), refs = from_others(groups, refs)
    chunks, (grad_q, *outs, out) = refs[:GROUP], refs[GROUP:]
    me = member()
    for step, chunk in enumerate(chunks):
        grad_q[:, columns(me ^ step)] = chunk[...]
    present = rim_present(groups)
    spread = spreading(2)
    quarter = BLOCK // 4
    for b in range(nb):
        for part in range(2):
            total = grad_kv[part, b] + dot(spread, got_top[part, b * quarter : (b + 1) * quarter])
            if b == 0:
                total = total + jnp.where(present[0], got_low[part].astype(F32), 0.0)
            if b == nb - 1:
                total = total + jnp.where(present[1], got_high[part].astype(F32), 0.0)
            out[b, part] = total.astype(BF16)
    for step, chunk in enumerate(outs):
        chunk[...] = out[me ^ step]


def unpack_kernel(*refs):
    here, across, *refs = refs
    grad_kv, outs = refs[:GROUP], refs[GROUP:]
    outs[2][...] = (here[...] + across[...].astype(F32)).astype(BF16)
    me = member()
    for step in range(GROUP):
        at = columns(me ^ step)
        outs[0][:, at] = grad_kv[step][0]
        outs[1][:, at] = grad_kv[step][1]


def share():
    return lax.axis_index("mp")


def grad_kernel(*refs):
    pieces, out_weight, outs, (whole, heads) = refs[:N_MP], refs[N_MP], refs[N_MP + 1 : -2], refs[-2:]
    me = member()
    for step, piece in enumerate(pieces):
        whole[span(share() ^ step, piece.shape[0]), :] = piece[...]
    heads[...] = dot_nt(whole[...], out_weight[...]).astype(BF16)
    for step, out in enumerate(outs):
        out[...] = heads[:, columns(me ^ step)]


def project_kernel(*refs):
    chunks, out_weight, (kept, sent, attended, whole) = refs[:GROUP], refs[GROUP], refs[-4:]
    me = member()
    for step, chunk in enumerate(chunks):
        attended[:, columns(me ^ step)] = chunk[...]
    whole[...] = dot(attended[...], out_weight[...]).astype(BF16)
    rows = kept.shape[1]
    for far in range(2):
        kept[far] = whole[span(share() ^ (2 * far), rows), :]
        sent[far] = whole[span(share() ^ (2 * far + 1), rows), :]


def swapped(x, axis, step):
    return lax.ppermute(x, axis, [(i, i ^ step) for i in range(lax.axis_size(axis))])


def exchanged(chunks):
    got = {step: swapped(chunks[step], "seq", step) for step in (3, 1, 2)}
    return [chunks[0]] + [got[step] for step in range(1, GROUP)]


def crossed(arrays):
    count = lax.axis_size("seq")
    across = swapped(arrays[0], "seq", GROUP)
    if len(arrays) == 1:
        return [across]
    up = [(i, i + GROUP) for i in range(count - GROUP)]
    down = [(j, i) for i, j in up]
    return [across, lax.ppermute(arrays[1], "seq", up), lax.ppermute(arrays[2], "seq", down)]


def per_device(queries, keys, values, out_weight, out_grad):
    rows, width = queries.shape
    assert width == GROUP * HEAD_DIM and rows == BLOCK and lax.axis_size("mp") == N_MP
    count = lax.axis_size("seq")
    assert count % (2 * GROUP) == 0
    groups = count // GROUP
    nb = GROUP
    tokens = nb * rows
    half, quarter = rows // 2, rows // 4
    model = out_weight.shape[1]
    block = shape(2, rows, HEAD_DIM)
    sent = [shape(4, rows, HEAD_DIM)] if groups == 2 else [block] * 3
    score_flops = 2 * tokens * 5 * BLOCK * HEAD_DIM
    weight_flops = 2 * rows * out_weight.size

    chunk = shape(rows, HEAD_DIM)
    pairs = call(pack_kernel, [block] * GROUP, (keys, values))
    far = swapped(out_grad, "mp", 2)
    beside_1 = swapped(out_grad, "mp", 1)
    pairs = exchanged(pairs)
    near, level_1, far, *refs = call(
        functools.partial(gather_kernel, nb, groups),
        [shape(nb, 2, rows, HEAD_DIM), shape(2, tokens // 2, HEAD_DIM), shape(*far.shape)]
        + sent
        + [chunk] * GROUP,
        (queries, far, *pairs),
    )
    others = crossed(refs[:-GROUP])
    query_chunks = exchanged(refs[-GROUP:])
    pieces = [out_grad, beside_1, far, swapped(far, "mp", 1)]
    grad_chunks = call(
        grad_kernel,
        [chunk] * GROUP,
        (*pieces, out_weight),
        scratch=[pltpu.VMEM((rows, model), BF16), pltpu.VMEM((rows, width), BF16)],
        flops=weight_flops,
    )
    query, k_t, v_t, k1_t, v1_t, weights, stats = call(
        functools.partial(local_kernel, nb),
        [
            shape(3, nb, rows, HEAD_DIM),
            shape(HEAD_DIM, tokens),
            shape(HEAD_DIM, tokens),
            shape(HEAD_DIM, tokens // 2),
            shape(HEAD_DIM, tokens // 2),
            shape(nb, 4, BLOCK, BLOCK, dtype=F32),
            shape(nb, 8, BLOCK, dtype=F32),
        ],
        (near, level_1, *query_chunks, grad_chunks[0]),
        flops=score_flops,
    )
    grad_chunks = exchanged(grad_chunks)
    prob, *attended = call(
        functools.partial(forward_kernel, nb, groups),
        [shape(nb, 5, BLOCK, BLOCK)] + [chunk] * GROUP,
        (query, v_t, v1_t, weights, stats, *others, *grad_chunks),
        scratch=[pltpu.VMEM((nb, rows, HEAD_DIM), BF16)],
        flops=score_flops,
    )
    attended = exchanged(attended)
    grads, shift, *rim_grads = call(
        functools.partial(slope_kernel, nb, groups),
        [shape(nb, rows, HEAD_DIM), shape(nb, 5, BLOCK, BLOCK)] + sent,
        (query, near, level_1, prob, *others, *grad_chunks),
        scratch=[pltpu.VMEM((2, BLOCK, HEAD_DIM), F32), pltpu.VMEM((2, 2, BLOCK, HEAD_DIM), F32)],
        flops=score_flops,
    )
    other_grads = crossed(rim_grads)
    *grad_q, grad_kv = call(
        functools.partial(backward_kernel, nb, groups),
        [chunk] * GROUP + [shape(2, nb, rows, HEAD_DIM, dtype=F32)],
        (query, k_t, k1_t, prob, shift, grads, *others),
        scratch=[
            pltpu.VMEM((nb, rows, HEAD_DIM), BF16),
            pltpu.VMEM((2, tokens // 2, HEAD_DIM), F32),
        ],
        flops=1,
    )
    grad_q = exchanged(grad_q)
    local = rows // N_MP
    shares = shape(2, local, model)
    kept, given = call(
        project_kernel,
        [shares] * 2,
        (*attended, out_weight, grads),
        scratch=[pltpu.VMEM((rows, width), BF16), pltpu.VMEM((rows, model), BF16)],
        flops=weight_flops,
    )
    grad_q, *grad_kv = call(
        functools.partial(combine_kernel, nb, groups),
        [shape(rows, width)] + [block] * GROUP,
        (grad_kv, *other_grads, *grad_q),
        scratch=[pltpu.VMEM((nb, 2, rows, HEAD_DIM), BF16)],
        flops=20 * score_flops,
    )
    across, here = call(
        share_kernel,
        [shape(local, model), shape(local, model, dtype=F32)],
        (kept, swapped(given, "mp", 1), grad_kv[0]),
    )
    grad_kv = exchanged(grad_kv)
    across = swapped(across, "mp", 2)
    grad_k, grad_v, mixed = call(
        unpack_kernel,
        [shape(rows, width)] * 2 + [shape(local, model)],
        (here, across, *grad_kv),
    )
    return mixed, grad_q, grad_k, grad_v


def solution(mesh):
    return jax.shard_map(
        per_device,
        mesh=mesh,
        in_specs=(
            P("seq", "mp"),
            P("seq", "mp"),
            P("seq", "mp"),
            P("mp", None),
            P(("seq", "mp"), None),
        ),
        out_specs=(P(("seq", "mp"), None), P("seq", "mp"), P("seq", "mp"), P("seq", "mp")),
        check_vma=False,
    )
```

time: 111 us -> 69.5 us (0.63)
  waiting for transfers between devices: 32.4 us -> 19.7 us
  local copies, waits for them, and re-layouts: 15.7 us -> 5.39 us
  blocking collectives: 8.06 us -> 0 us
  starting transfers between devices: 35.7 us -> 30.3 us
  Pallas kernels: 16.9 us -> 13.1 us
    all_to_all x5 -> x0, starting transfers between devices: 22 us -> none  [regrouped(): return lax.all_to_all(x, 'seq', 0, 0, axis_index_groups=members)]
    ppermute x10 -> x25, starting transfers between devices: 13.7 us -> 30.3 us  [swapped(): lax.ppermute(x, axis, [(i, i ^ step) for i in range(lax.axis_size(axis))])]
    ppermute x10 -> x25, waiting for transfers between devices: 32.4 us -> 19.7 us  [swapped(): lax.ppermute(x, axis, [(i, i ^ step) for i in range(lax.axis_size(axis))])]
    unnamed x52 -> x12, local copies, waits for them, and re-layouts: 15.7 us -> 5.39 us
    all_to_all x1 -> x0, blocking collectives: 8.06 us -> none  [regrouped(): return lax.all_to_all(x, 'seq', 0, 0, axis_index_groups=members)]
    pallas_call x10 -> x11, Pallas kernels: 16.9 us -> 13.1 us  [call(): pl.pallas_call(kernel, out_shape=out_shape, in_specs=[pl.BlockSpec(memory...]
  transfers between devices with their start and end apart: 15 -> 25, of which waited for: 7 -> 10; matrix products, arithmetic and copies ran while one was open for 1% -> 0% of each run, Pallas kernels for 14% -> 11%
where the time goes in v4:
time: 69.5 us; the launch traced here: 69.2 us
  starting transfers between devices  30.3 us (44%)
  waiting for transfers between devices  19.7 us (28%)
  Pallas kernels  13.1 us (19%)
  local copies, waits for them, and re-layouts  5.39 us (8%)
  between operations  0.75 us (1%)
    ppermute x25, starting transfers between devices, swapped(): lax.ppermute(x, axis, [(i, i ^ step) for i in range(lax.axis_size(axis))])  30.3 us
    ppermute x25, waiting for transfers between devices, swapped(): lax.ppermute(x, axis, [(i, i ^ step) for i in range(lax.axis_size(axis))])  19.7 us
    pallas_call x11, Pallas kernels, call(): pl.pallas_call(kernel, out_shape=out_shape, in_specs=[pl.BlockSpec(memory...  13.1 us
    unnamed x12, local copies, waits for them, and re-layouts  5.39 us
  transfers between devices with their start and end apart: 25, of which 10 were waited for; matrix products, arithmetic and copies ran while one was open for 0% of the time, Pallas kernels for 11%

profile of v4, /device:TPU:0, one launch (start us, length us, event | category | flops | bytes accessed | tf_op | source)
XLA Modules:
  0.0 69.2 jit_solution(3512257324331969832)
XLA Ops:
  0.6 3.0 %collective-permute-start = (bf16[64,2048]{1,0:T(8,128)(2,1)}, bf16[64,2048]{1,0:T(8,128)(2,1)S(1)}, u32[]{:S(2)}, u32[]{:S(2)}) collective-permute-start(bf16[64,2048]{1,0:T(8,128)(2,1)} %refs_0_.1), channel_id=1, source_target_pairs={{0,2},{1,3},{2,0},{3,1},{4,6},{5,7},{6,4},{7,5},{8,10},{9,11},{10,... | collective-permute-start | bytes 786440 | tf_op jit(solution)/shard_map/ppermute | solution.py:362
  5.6 1.6 %collective-permute-start.1 = (bf16[2,256,128]{2,1,0:T(8,128)(2,1)S(1)}, bf16[2,256,128]{2,1,0:T(8,128)(2,1)S(1)}, u32[]{:S(2)}, u32[]{:S(2)}) collective-permute-start(bf16[2,256,128]{2,1,0:T(8,128)(2,1)S(1)} %get-tuple-element.53), channel_id=1, source_target_pairs={{0,4},{4,0},{8,12},{12,8},{16,20},{20,16},{24,28},{28,24},{1,5},{5... | collective-permute-start | bytes 393224 | tf_op jit(solution)/shard_map/ppermute | solution.py:362
  7.2 1.6 %collective-permute-start.2 = (bf16[2,256,128]{2,1,0:T(8,128)(2,1)S(1)}, bf16[2,256,128]{2,1,0:T(8,128)(2,1)S(1)}, u32[]{:S(2)}, u32[]{:S(2)}) collective-permute-start(bf16[2,256,128]{2,1,0:T(8,128)(2,1)S(1)} %get-tuple-element.54), channel_id=1, source_target_pairs={{0,8},{4,12},{8,0},{12,4},{16,24},{20,28},{24,16},{28,20},{1,9},{5... | collective-permute-start | bytes 393224 | tf_op jit(solution)/shard_map/ppermute | solution.py:362
  9.2 1.5 %collective-permute-done.1.refs_1_ = bf16[2,256,128]{2,1,0:T(8,128)(2,1)S(1)} collective-permute-done((bf16[2,256,128]{2,1,0:T(8,128)(2,1)S(1)}, bf16[2,256,128]{2,1,0:T(8,128)(2,1)S(1)}, u32[]{:S(2)}, u32[]{:S(2)}) %collective-permute-start.1) | collective-permute-done | bytes 131104 | tf_op jit(solution)/shard_map/ppermute | solution.py:362
  10.7 2.6 %collective-permute-done.2.refs_2_ = bf16[2,256,128]{2,1,0:T(8,128)(2,1)S(1)} collective-permute-done((bf16[2,256,128]{2,1,0:T(8,128)(2,1)S(1)}, bf16[2,256,128]{2,1,0:T(8,128)(2,1)S(1)}, u32[]{:S(2)}, u32[]{:S(2)}) %collective-permute-start.2) | collective-permute-done | bytes 131104 | tf_op jit(solution)/shard_map/ppermute | solution.py:362
  13.3 1.6 %collective-permute-done.3.refs_3_ = bf16[2,256,128]{2,1,0:T(8,128)(2,1)S(1)} collective-permute-done((bf16[2,256,128]{2,1,0:T(8,128)(2,1)S(1)}, bf16[2,256,128]{2,1,0:T(8,128)(2,1)S(1)}, u32[]{:S(2)}, u32[]{:S(2)}) %collective-permute-start.3) | collective-permute-done | bytes 131104 | tf_op jit(solution)/shard_map/ppermute | solution.py:362
  16.7 2.7 %collective-permute-start.9 = (bf16[4,256,128]{2,1,0:T(8,128)(2,1)S(1)}, bf16[4,256,128]{2,1,0:T(8,128)(2,1)S(1)}, u32[]{:S(2)}, u32[]{:S(2)}) collective-permute-start(bf16[4,256,128]{2,1,0:T(8,128)(2,1)S(1)} %get-tuple-element.69), channel_id=1, source_target_pairs={{0,16},{4,20},{8,24},{12,28},{16,0},{20,4},{24,8},{28,12},{1,17},{... | collective-permute-start | bytes 786440 | tf_op jit(solution)/shard_map/ppermute | solution.py:362
  20.6 1.6 %collective-permute-start.5 = (bf16[256,128]{1,0:T(8,128)(2,1)S(1)}, bf16[256,128]{1,0:T(8,128)(2,1)S(1)}, u32[]{:S(2)}, u32[]{:S(2)}) collective-permute-start(bf16[256,128]{1,0:T(8,128)(2,1)S(1)} %get-tuple-element.60), channel_id=1, source_target_pairs={{0,8},{4,12},{8,0},{12,4},{16,24},{20,28},{24,16},{28,20},{1,9},{5... | collective-permute-start | bytes 196616 | tf_op jit(solution)/shard_map/ppermute | solution.py:362
  22.9 1.6 %copy-done = bf16[512,2048]{1,0:T(8,128)(2,1)S(1)} copy-done((bf16[512,2048]{1,0:T(8,128)(2,1)S(1)}, bf16[512,2048]{1,0:T(8,128)(2,1)}, u32[]{:S(2)}) %copy-start) | copy-done | bytes 2097176
  27.6 1.6 %collective-permute-start.11 = (bf16[256,128]{1,0:T(8,128)(2,1)S(1)}, bf16[256,128]{1,0:T(8,128)(2,1)S(1)}, u32[]{:S(2)}, u32[]{:S(2)}) collective-permute-start(bf16[256,128]{1,0:T(8,128)(2,1)S(1)} %get-tuple-element.71), channel_id=1, source_target_pairs={{0,8},{4,12},{8,0},{12,4},{16,24},{20,28},{24,16},{28,20},{1,9},{5... | collective-permute-start | bytes 196616 | tf_op jit(solution)/shard_map/ppermute | solution.py:362
  29.1 1.5 %collective-permute-start.12 = (bf16[256,128]{1,0:T(8,128)(2,1)S(1)}, bf16[256,128]{1,0:T(8,128)(2,1)S(1)}, u32[]{:S(2)}, u32[]{:S(2)}) collective-permute-start(bf16[256,128]{1,0:T(8,128)(2,1)S(1)} %get-tuple-element.72), channel_id=1, source_target_pairs={{0,12},{4,8},{8,4},{12,0},{16,28},{20,24},{24,20},{28,16},{1,13},{... | collective-permute-start | bytes 196616 | tf_op jit(solution)/shard_map/ppermute | solution.py:362
  30.6 1.7 %shard_map.87 = (bf16[3,4,256,128]{3,2,1,0:T(8,128)(2,1)S(1)}, bf16[128,1024]{1,0:T(8,128)(2,1)S(1)}, bf16[128,1024]{1,0:T(8,128)(2,1)S(1)}, bf16[128,512]{1,0:T...) custom-call(bf16[4,2,256,128]{3,2,1,0:T(8,128)(2,1)S(1)} %get-tuple-element, ...), custom_call_target="tpu_custom_call" | custom-call | flops 335544320 | bytes 6914048 | tf_op jit(solution)/shard_map/pallas_call | solution.py:36
  33.5 2.0 %collective-permute-done.12.refs_9_.refs_8_ = bf16[256,128]{1,0:T(8,128)(2,1)S(1)} collective-permute-done((bf16[256,128]{1,0:T(8,128)(2,1)S(1)}, bf16[256,128]{1,0:T(8,128)(2,1)S(1)}, u32[]{:S(2)}, u32[]{:S(2)}) %collective-permute-start.12) | collective-permute-done | bytes 65568 | tf_op jit(solution)/shard_map/ppermute | solution.py:362
  35.4 1.6 %shard_map.88 = (bf16[4,5,256,256]{3,2,1,0:T(8,128)(2,1)S(1)}, bf16[256,128]{1,0:T(8,128)(2,1)S(1)}, bf16[256,128]{1,0:T(8,128)(2,1)S(1)}, bf16[256,128]{1,0:T(8,128)(2,1)S(1)}, bf16[256,128]{1,0:T(8,128)(2,1)S(1)}) custom-call(bf16[3,4,256,128]{3,2,1,0:T(8,128)(2,1)S(1)} %get-tuple-element.64.refs_0_, bf16[128,1024]{1,0:T(8,128)(2,1)S(1)} %get-tuple-element.65.refs_1_, ...), custom_call_target="tpu_custom_call" | custom-call | flops 335544320 | bytes 8814592 | tf_op jit(solution)/shard_map/pallas_call | solution.py:36
  37.1 2.9 %shard_map.89 = (bf16[4,256,128]{2,1,0:T(8,128)(2,1)S(1)}, bf16[4,5,256,256]{3,2,1,0:T(8,128)(2,1)S(1)}, bf16[4,256,128]{2,1,0:T(8,128)(2,1)S(1)}) custom-call(bf16[3,4,256,128]{3,2,1,0:T(8,128)(2,1)S(1)} %get-tuple-element.64.refs_0_, bf16[4,2,256,128]{3,2,1,0:T(8,128)(2,1)S(1)} %get-tuple-element.56.near.refs_1_, ...), custom_call_target="tpu_custom_call" | custom-call | flops 335544320 | bytes 7864320 | tf_op jit(solution)/shard_map/pallas_call | solution.py:36
  41.9 2.8 %collective-permute-start.14 = (bf16[256,128]{1,0:T(8,128)(2,1)S(1)}, bf16[256,128]{1,0:T(8,128)(2,1)S(1)}, u32[]{:S(2)}, u32[]{:S(2)}) collective-permute-start(bf16[256,128]{1,0:T(8,128)(2,1)S(1)} %get-tuple-element.75), channel_id=1, source_target_pairs={{0,8},{4,12},{8,0},{12,4},{16,24},{20,28},{24,16},{28,20},{1,9},{5... | collective-permute-start | bytes 196616 | tf_op jit(solution)/shard_map/ppermute | solution.py:362
  45.3 2.3 %shard_map.91 = (bf16[256,128]{1,0:T(8,128)(2,1)S(1)}, bf16[256,128]{1,0:T(8,128)(2,1)S(1)}, bf16[256,128]{1,0:T(8,128)(2,1)S(1)}, bf16[256,128]{1,0:T(8,128)(2,1)S(1)}, f32[2,4,256,128]{3,2,1,0:T(8,128)S(1)}) custom-call(bf16[3,4,256,128]{3,2,1,0:T(8,128)(2,1)S(1)} %get-tuple-element.64.refs_0_, bf16[128,1024]{1,0:T(8,128)(2,1)S(1)} %get-tuple-element.81.refs_1_, ...), custom_call_target="tpu_custom_call" | custom-call | flops 1 | bytes 8257536 | tf_op jit(solution)/shard_map/pallas_call | solution.py:36
  48.6 2.0 %collective-permute-start.19 = (bf16[256,128]{1,0:T(8,128)(2,1)S(1)}, bf16[256,128]{1,0:T(8,128)(2,1)S(1)}, u32[]{:S(2)}, u32[]{:S(2)}) collective-permute-start(bf16[256,128]{1,0:T(8,128)(2,1)S(1)} %get-tuple-element.88), channel_id=1, source_target_pairs={{0,8},{4,12},{8,0},{12,4},{16,24},{20,28},{24,16},{28,20},{1,9},{5... | collective-permute-start | bytes 196616 | tf_op jit(solution)/shard_map/ppermute | solution.py:362
  52.3 4.0 %collective-permute-done.19.refs_3_ = bf16[256,128]{1,0:T(8,128)(2,1)S(1)} collective-permute-done((bf16[256,128]{1,0:T(8,128)(2,1)S(1)}, bf16[256,128]{1,0:T(8,128)(2,1)S(1)}, u32[]{:S(2)}, u32[]{:S(2)}) %collective-permute-start.19) | collective-permute-done | bytes 65568 | tf_op jit(solution)/shard_map/ppermute | solution.py:362
  59.3 1.4 %collective-permute-start.22 = (bf16[2,256,128]{2,1,0:T(8,128)(2,1)S(1)}, bf16[2,256,128]{2,1,0:T(8,128)(2,1)S(1)}, u32[]{:S(2)}, u32[]{:S(2)}) collective-permute-start(bf16[2,256,128]{2,1,0:T(8,128)(2,1)S(1)} %get-tuple-element.93), channel_id=1, source_target_pairs={{0,4},{4,0},{8,12},{12,8},{16,20},{20,16},{24,28},{28,24},{1,5},{5... | collective-permute-start | bytes 393224 | tf_op jit(solution)/shard_map/ppermute | solution.py:362
  60.7 2.1 %collective-permute-start.24 = (bf16[2,256,128]{2,1,0:T(8,128)(2,1)S(1)}, bf16[2,256,128]{2,1,0:T(8,128)(2,1)S(1)}, u32[]{:S(2)}, u32[]{:S(2)}) collective-permute-start(bf16[2,256,128]{2,1,0:T(8,128)(2,1)S(1)} %get-tuple-element.95), channel_id=1, source_target_pairs={{0,12},{4,8},{8,4},{12,0},{16,28},{20,24},{24,20},{28,16},{1,13},{... | collective-permute-start | bytes 393224 | tf_op jit(solution)/shard_map/ppermute | solution.py:362
  62.7 2.1 %collective-permute-done.22.refs_3_ = bf16[2,256,128]{2,1,0:T(8,128)(2,1)S(1)} collective-permute-done((bf16[2,256,128]{2,1,0:T(8,128)(2,1)S(1)}, bf16[2,256,128]{2,1,0:T(8,128)(2,1)S(1)}, u32[]{:S(2)}, u32[]{:S(2)}) %collective-permute-start.22) | collective-permute-done | bytes 131104 | tf_op jit(solution)/shard_map/ppermute | solution.py:362
  64.8 2.0 %collective-permute-done.23.refs_4_ = bf16[2,256,128]{2,1,0:T(8,128)(2,1)S(1)} collective-permute-done((bf16[2,256,128]{2,1,0:T(8,128)(2,1)S(1)}, bf16[2,256,128]{2,1,0:T(8,128)(2,1)S(1)}, u32[]{:S(2)}, u32[]{:S(2)}) %collective-permute-start.23) | collective-permute-done | bytes 131104 | tf_op jit(solution)/shard_map/ppermute | solution.py:362
  66.8 1.4 %collective-permute-done.24.refs_5_ = bf16[2,256,128]{2,1,0:T(8,128)(2,1)S(1)} collective-permute-done((bf16[2,256,128]{2,1,0:T(8,128)(2,1)S(1)}, bf16[2,256,128]{2,1,0:T(8,128)(2,1)S(1)}, u32[]{:S(2)}, u32[]{:S(2)}) %collective-permute-start.24) | collective-permute-done | bytes 131104 | tf_op jit(solution)/shard_map/ppermute | solution.py:362
  (49 shorter events, 19.5 us)
Async XLA Ops:
  0.6 14.3 %collective-permute-start = (bf16[64,2048]{1,0:T(8,128)(2,1)}, bf16[64,2048]{1,0:T(8,128)(2,1)S(1)}, u32[]{:S(2)}, u32[]{:S(2)}) collective-permute-start(bf16[64,2048]{1,0:T(8,128)(2,1)} %refs_0_.1), channel_id=1, source_target_pairs={{0,2},{1,3},{2,0},{3,1},{4,6},{5,7},{6,4},{7,5},{8,10},{9,11},{10,... | collective-permute-start | bytes 786440 | tf_op jit(solution)/shard_map/ppermute | solution.py:362
  5.6 5.0 %collective-permute-start.1 = (bf16[2,256,128]{2,1,0:T(8,128)(2,1)S(1)}, bf16[2,256,128]{2,1,0:T(8,128)(2,1)S(1)}, u32[]{:S(2)}, u32[]{:S(2)}) collective-permute-start(bf16[2,256,128]{2,1,0:T(8,128)(2,1)S(1)} %get-tuple-element.53), channel_id=1, source_target_pairs={{0,4},{4,0},{8,12},{12,8},{16,20},{20,16},{24,28},{28,24},{1,5},{5... | collective-permute-start | bytes 393224 | tf_op jit(solution)/shard_map/ppermute | solution.py:362
  7.2 6.1 %collective-permute-start.2 = (bf16[2,256,128]{2,1,0:T(8,128)(2,1)S(1)}, bf16[2,256,128]{2,1,0:T(8,128)(2,1)S(1)}, u32[]{:S(2)}, u32[]{:S(2)}) collective-permute-start(bf16[2,256,128]{2,1,0:T(8,128)(2,1)S(1)} %get-tuple-element.54), channel_id=1, source_target_pairs={{0,8},{4,12},{8,0},{12,4},{16,24},{20,28},{24,16},{28,20},{1,9},{5... | collective-permute-start | bytes 393224 | tf_op jit(solution)/shard_map/ppermute | solution.py:362
  8.8 6.1 %collective-permute-start.3 = (bf16[2,256,128]{2,1,0:T(8,128)(2,1)S(1)}, bf16[2,256,128]{2,1,0:T(8,128)(2,1)S(1)}, u32[]{:S(2)}, u32[]{:S(2)}) collective-permute-start(bf16[2,256,128]{2,1,0:T(8,128)(2,1)S(1)} %get-tuple-element.55), channel_id=1, source_target_pairs={{0,12},{4,8},{8,4},{12,0},{16,28},{20,24},{24,20},{28,16},{1,13},{... | collective-permute-start | bytes 393224 | tf_op jit(solution)/shard_map/ppermute | solution.py:362
  9.2 13.0 %collective-permute-start.7 = (bf16[64,2048]{1,0:T(8,128)(2,1)}, bf16[64,2048]{1,0:T(8,128)(2,1)S(1)}, u32[]{:S(2)}, u32[]{:S(2)}) collective-permute-start(bf16[64,2048]{1,0:T(8,128)(2,1)} %refs_0_.1), channel_id=1, source_target_pairs={{0,1},{1,0},{2,3},{3,2},{4,5},{5,4},{6,7},{7,6},{8,9},{9,8},{10,11... | collective-permute-start | bytes 786440 | tf_op jit(solution)/shard_map/ppermute | solution.py:362
  16.6 6.2 %collective-permute-start.8 = (bf16[64,2048]{1,0:T(8,128)(2,1)S(1)}, bf16[64,2048]{1,0:T(8,128)(2,1)S(1)}, u32[]{:S(2)}, u32[]{:S(2)}) collective-permute-start(bf16[64,2048]{1,0:T(8,128)(2,1)S(1)} %get-tuple-element.62.refs_2_), channel_id=1, source_target_pairs={{0,1},{1,0},{2,3},{3,2},{4,5},{5,4},{6,7},{7,6},{8,9},{9,8},{10,11... | collective-permute-start | bytes 786440 | tf_op jit(solution)/shard_map/ppermute | solution.py:362
  16.7 15.6 %collective-permute-start.9 = (bf16[4,256,128]{2,1,0:T(8,128)(2,1)S(1)}, bf16[4,256,128]{2,1,0:T(8,128)(2,1)S(1)}, u32[]{:S(2)}, u32[]{:S(2)}) collective-permute-start(bf16[4,256,128]{2,1,0:T(8,128)(2,1)S(1)} %get-tuple-element.69), channel_id=1, source_target_pairs={{0,16},{4,20},{8,24},{12,28},{16,0},{20,4},{24,8},{28,12},{1,17},{... | collective-permute-start | bytes 786440 | tf_op jit(solution)/shard_map/ppermute | solution.py:362
  19.4 8.2 %collective-permute-start.4 = (bf16[256,128]{1,0:T(8,128)(2,1)S(1)}, bf16[256,128]{1,0:T(8,128)(2,1)S(1)}, u32[]{:S(2)}, u32[]{:S(2)}) collective-permute-start(bf16[256,128]{1,0:T(8,128)(2,1)S(1)} %get-tuple-element.59), channel_id=1, source_target_pairs={{0,4},{4,0},{8,12},{12,8},{16,20},{20,16},{24,28},{28,24},{1,5},{5... | collective-permute-start | bytes 196616 | tf_op jit(solution)/shard_map/ppermute | solution.py:362
  20.6 8.5 %collective-permute-start.5 = (bf16[256,128]{1,0:T(8,128)(2,1)S(1)}, bf16[256,128]{1,0:T(8,128)(2,1)S(1)}, u32[]{:S(2)}, u32[]{:S(2)}) collective-permute-start(bf16[256,128]{1,0:T(8,128)(2,1)S(1)} %get-tuple-element.60), channel_id=1, source_target_pairs={{0,8},{4,12},{8,0},{12,4},{16,24},{20,28},{24,16},{28,20},{1,9},{5... | collective-permute-start | bytes 196616 | tf_op jit(solution)/shard_map/ppermute | solution.py:362
  22.2 8.4 %collective-permute-start.6 = (bf16[256,128]{1,0:T(8,128)(2,1)S(1)}, bf16[256,128]{1,0:T(8,128)(2,1)S(1)}, u32[]{:S(2)}, u32[]{:S(2)}) collective-permute-start(bf16[256,128]{1,0:T(8,128)(2,1)S(1)} %get-tuple-element.61), channel_id=1, source_target_pairs={{0,12},{4,8},{8,4},{12,0},{16,28},{20,24},{24,20},{28,16},{1,13},{... | collective-permute-start | bytes 196616 | tf_op jit(solution)/shard_map/ppermute | solution.py:362
  26.3 6.0 %collective-permute-start.10 = (bf16[256,128]{1,0:T(8,128)(2,1)S(1)}, bf16[256,128]{1,0:T(8,128)(2,1)S(1)}, u32[]{:S(2)}, u32[]{:S(2)}) collective-permute-start(bf16[256,128]{1,0:T(8,128)(2,1)S(1)} %get-tuple-element.70), channel_id=1, source_target_pairs={{0,4},{4,0},{8,12},{12,8},{16,20},{20,16},{24,28},{28,24},{1,5},{5... | collective-permute-start | bytes 196616 | tf_op jit(solution)/shard_map/ppermute | solution.py:362
  27.6 5.9 %collective-permute-start.11 = (bf16[256,128]{1,0:T(8,128)(2,1)S(1)}, bf16[256,128]{1,0:T(8,128)(2,1)S(1)}, u32[]{:S(2)}, u32[]{:S(2)}) collective-permute-start(bf16[256,128]{1,0:T(8,128)(2,1)S(1)} %get-tuple-element.71), channel_id=1, source_target_pairs={{0,8},{4,12},{8,0},{12,4},{16,24},{20,28},{24,16},{28,20},{1,9},{5... | collective-permute-start | bytes 196616 | tf_op jit(solution)/shard_map/ppermute | solution.py:362
  29.1 6.3 %collective-permute-start.12 = (bf16[256,128]{1,0:T(8,128)(2,1)S(1)}, bf16[256,128]{1,0:T(8,128)(2,1)S(1)}, u32[]{:S(2)}, u32[]{:S(2)}) collective-permute-start(bf16[256,128]{1,0:T(8,128)(2,1)S(1)} %get-tuple-element.72), channel_id=1, source_target_pairs={{0,12},{4,8},{8,4},{12,0},{16,28},{20,24},{24,20},{28,16},{1,13},{... | collective-permute-start | bytes 196616 | tf_op jit(solution)/shard_map/ppermute | solution.py:362
  40.0 17.7 %collective-permute-start.17 = (bf16[4,256,128]{2,1,0:T(8,128)(2,1)S(1)}, bf16[4,256,128]{2,1,0:T(8,128)(2,1)S(1)}, u32[]{:S(2)}, u32[]{:S(2)}) collective-permute-start(bf16[4,256,128]{2,1,0:T(8,128)(2,1)S(1)} %get-tuple-element.85), channel_id=1, source_target_pairs={{0,16},{4,20},{8,24},{12,28},{16,0},{20,4},{24,8},{28,12},{1,17},{... | collective-permute-start | bytes 786440 | tf_op jit(solution)/shard_map/ppermute | solution.py:362
  40.7 7.8 %collective-permute-start.13 = (bf16[256,128]{1,0:T(8,128)(2,1)S(1)}, bf16[256,128]{1,0:T(8,128)(2,1)S(1)}, u32[]{:S(2)}, u32[]{:S(2)}) collective-permute-start(bf16[256,128]{1,0:T(8,128)(2,1)S(1)} %get-tuple-element.74), channel_id=1, source_target_pairs={{0,4},{4,0},{8,12},{12,8},{16,20},{20,16},{24,28},{28,24},{1,5},{5... | collective-permute-start | bytes 196616 | tf_op jit(solution)/shard_map/ppermute | solution.py:362
  41.9 8.7 %collective-permute-start.14 = (bf16[256,128]{1,0:T(8,128)(2,1)S(1)}, bf16[256,128]{1,0:T(8,128)(2,1)S(1)}, u32[]{:S(2)}, u32[]{:S(2)}) collective-permute-start(bf16[256,128]{1,0:T(8,128)(2,1)S(1)} %get-tuple-element.75), channel_id=1, source_target_pairs={{0,8},{4,12},{8,0},{12,4},{16,24},{20,28},{24,16},{28,20},{1,9},{5... | collective-permute-start | bytes 196616 | tf_op jit(solution)/shard_map/ppermute | solution.py:362
  44.7 6.7 %collective-permute-start.15 = (bf16[256,128]{1,0:T(8,128)(2,1)S(1)}, bf16[256,128]{1,0:T(8,128)(2,1)S(1)}, u32[]{:S(2)}, u32[]{:S(2)}) collective-permute-start(bf16[256,128]{1,0:T(8,128)(2,1)S(1)} %get-tuple-element.76), channel_id=1, source_target_pairs={{0,12},{4,8},{8,4},{12,0},{16,28},{20,24},{24,20},{28,16},{1,13},{... | collective-permute-start | bytes 196616 | tf_op jit(solution)/shard_map/ppermute | solution.py:362
  48.6 7.7 %collective-permute-start.19 = (bf16[256,128]{1,0:T(8,128)(2,1)S(1)}, bf16[256,128]{1,0:T(8,128)(2,1)S(1)}, u32[]{:S(2)}, u32[]{:S(2)}) collective-permute-start(bf16[256,128]{1,0:T(8,128)(2,1)S(1)} %get-tuple-element.88), channel_id=1, source_target_pairs={{0,8},{4,12},{8,0},{12,4},{16,24},{20,28},{24,16},{28,20},{1,9},{5... | collective-permute-start | bytes 196616 | tf_op jit(solution)/shard_map/ppermute | solution.py:362
  50.6 7.0 %collective-permute-start.20 = (bf16[256,128]{1,0:T(8,128)(2,1)S(1)}, bf16[256,128]{1,0:T(8,128)(2,1)S(1)}, u32[]{:S(2)}, u32[]{:S(2)}) collective-permute-start(bf16[256,128]{1,0:T(8,128)(2,1)S(1)} %get-tuple-element.89), channel_id=1, source_target_pairs={{0,12},{4,8},{8,4},{12,0},{16,28},{20,24},{24,20},{28,16},{1,13},{... | collective-permute-start | bytes 196616 | tf_op jit(solution)/shard_map/ppermute | solution.py:362
  52.2 6.4 %collective-permute-start.16 = (bf16[2,64,2048]{2,1,0:T(8,128)(2,1)S(1)}, bf16[2,64,2048]{2,1,0:T(8,128)(2,1)S(1)}, u32[]{:S(2)}, u32[]{:S(2)}) collective-permute-start(bf16[2,64,2048]{2,1,0:T(8,128)(2,1)S(1)} %get-tuple-element.80), channel_id=1, source_target_pairs={{0,1},{1,0},{2,3},{3,2},{4,5},{5,4},{6,7},{7,6},{8,9},{9,8},{10,11... | collective-permute-start | bytes 1572872 | tf_op jit(solution)/shard_map/ppermute | solution.py:362
  58.7 9.5 %collective-permute-start.21 = (bf16[64,2048]{1,0:T(8,128)(2,1)S(1)}, bf16[64,2048]{1,0:T(8,128)(2,1)S(1)}, u32[]{:S(2)}, u32[]{:S(2)}) collective-permute-start(bf16[64,2048]{1,0:T(8,128)(2,1)S(1)} %get-tuple-element.92), channel_id=1, source_target_pairs={{0,2},{1,3},{2,0},{3,1},{4,6},{5,7},{6,4},{7,5},{8,10},{9,11},{10,... | collective-permute-start | bytes 786440 | tf_op jit(solution)/shard_map/ppermute | solution.py:362
  59.3 5.6 %collective-permute-start.22 = (bf16[2,256,128]{2,1,0:T(8,128)(2,1)S(1)}, bf16[2,256,128]{2,1,0:T(8,128)(2,1)S(1)}, u32[]{:S(2)}, u32[]{:S(2)}) collective-permute-start(bf16[2,256,128]{2,1,0:T(8,128)(2,1)S(1)} %get-tuple-element.93), channel_id=1, source_target_pairs={{0,4},{4,0},{8,12},{12,8},{16,20},{20,16},{24,28},{28,24},{1,5},{5... | collective-permute-start | bytes 393224 | tf_op jit(solution)/shard_map/ppermute | solution.py:362
  60.6 6.2 %collective-permute-start.23 = (bf16[2,256,128]{2,1,0:T(8,128)(2,1)S(1)}, bf16[2,256,128]{2,1,0:T(8,128)(2,1)S(1)}, u32[]{:S(2)}, u32[]{:S(2)}) collective-permute-start(bf16[2,256,128]{2,1,0:T(8,128)(2,1)S(1)} %get-tuple-element.94), channel_id=1, source_target_pairs={{0,8},{4,12},{8,0},{12,4},{16,24},{20,28},{24,16},{28,20},{1,9},{5... | collective-permute-start | bytes 393224 | tf_op jit(solution)/shard_map/ppermute | solution.py:362
  60.7 7.5 %collective-permute-start.24 = (bf16[2,256,128]{2,1,0:T(8,128)(2,1)S(1)}, bf16[2,256,128]{2,1,0:T(8,128)(2,1)S(1)}, u32[]{:S(2)}, u32[]{:S(2)}) collective-permute-start(bf16[2,256,128]{2,1,0:T(8,128)(2,1)S(1)} %get-tuple-element.95), channel_id=1, source_target_pairs={{0,12},{4,8},{8,4},{12,0},{16,28},{20,24},{24,20},{28,16},{1,13},{... | collective-permute-start | bytes 393224 | tf_op jit(solution)/shard_map/ppermute | solution.py:362
  (7 other events, 16.2 us)

commit v5 on v4

--- a/solution.py
+++ b/solution.py
@@ -98,21 +98,31 @@
     return pl.ds(pl.multiple_of(index * HEAD_DIM, HEAD_DIM), HEAD_DIM)
 
 
-def pack_kernel(k, v, *outs):
-    me = member()
-    for step, out in enumerate(outs):
-        for part, source in enumerate((k, v)):
-            out[part] = source[:, columns(me ^ step)]
-
-
-def gather_kernel(nb, groups, q, far, *refs):
-    chunks, (near, level_1, far_out, *refs) = refs[:GROUP], refs[GROUP:]
+def pack_kernel(q, k, v, out_grad, *refs):
+    outs, (out_grad_out, sems) = refs[:GROUP], refs[GROUP:]
+    me = member()
+    copies = [pltpu.make_async_copy(out_grad, out_grad_out, sems.at[0])]
+    for step in (3, 1, 2, 0):
+        for part, source in enumerate((k, v, q)):
+            piece = source.at[:, columns(me ^ step)]
+            copies.append(pltpu.make_async_copy(piece, outs[step].at[part], sems.at[len(copies)]))
+    for copy in copies:
+        copy.start()
+    for copy in copies:
+        copy.wait()
+
+
+def copy_kernel(x, out):
+    out[...] = x[...]
+
+
+def gather_kernel(nb, groups, far, *refs):
+    chunks, (far_out, near, queries, level_1, *rims) = refs[:GROUP], refs[GROUP:]
     far_out[...] = far[...]
-    rims, queries = refs[:-GROUP], refs[-GROUP:]
     me = member()
     for step, chunk in enumerate(chunks):
-        near[me ^ step] = chunk[...]
-        queries[step][...] = q[:, columns(me ^ step)]
+        near[me ^ step] = chunk[:2]
+        queries[me ^ step] = chunk[2]
     pool = pooling()
     half = BLOCK // 2
     for part in range(2):
@@ -139,14 +149,11 @@
     return [side for side in range(3) if 0 <= b + side - 1 < nb]
 
 
-def local_kernel(nb, near, level_1, *refs):
-    chunks, _, (query, k_t, v_t, k1_t, v1_t, weights, stats) = refs[:GROUP], refs[GROUP], refs[GROUP + 1 :]
-    me = member()
-    for step, chunk in enumerate(chunks):
-        query[0, me ^ step] = chunk[...]
+def local_kernel(nb, near, queries, level_1, _, query, k_t, v_t, k1_t, v1_t, weights, stats):
     even_1, even_2 = averaging(1), averaging(2)
     for b in range(nb):
-        once = dot(even_1, query[0, b]).astype(BF16)
+        query[0, b] = queries[b]
+        once = dot(even_1, queries[b]).astype(BF16)
         query[1, b] = once
         query[2, b] = dot(even_2, once).astype(BF16)
         for part, transposed in enumerate((k_t, v_t)):
@@ -262,7 +269,7 @@
 def backward_kernel(nb, groups, *refs):
     (query, k_t, k1_t, prob, shift, grads), refs = refs[:6], refs[6:]
     (top_2, rim_low, rim_high), refs = from_others(groups, refs)
-    *outs, grad_kv, grad_q, sums_1 = refs
+    grad_q, grad_kv, sums_1 = refs
     k2_t = top_2[0].T
     even_1, even_2 = averaging(1), averaging(2)
     for b in range(nb):
@@ -277,9 +284,6 @@
             high, low = halves(dot(key_t, shift[b, part]))
             grad_t = grad_t + (dot(high, spread) + dot(low, spread))
         grad_q[b] = (SCALE * grad_t).T.astype(BF16)
-    me = member()
-    for step, out in enumerate(outs):
-        out[...] = grad_q[me ^ step]
     for c in range(nb // 2):
         users = [b for b in range(nb) if sibling(b) == c]
         sums_1[0, at_block(c)] = SCALE * sum(dot(shift[b, 3], query[1, b]) for b in users)
@@ -300,12 +304,8 @@
     here[...] = kept[0].astype(F32) + got[0].astype(F32)
 
 
-def combine_kernel(nb, groups, grad_kv, *refs):
-    (got_top, got_low, got_high), refs = from_others(groups, refs)
-    chunks, (grad_q, *outs, out) = refs[:GROUP], refs[GROUP:]
-    me = member()
-    for step, chunk in enumerate(chunks):
-        grad_q[:, columns(me ^ step)] = chunk[...]
+def combine_kernel(nb, groups, grad_q, grad_kv, *refs):
+    (got_top, got_low, got_high), (*outs, out) = from_others(groups, refs)
     present = rim_present(groups)
     spread = spreading(2)
     quarter = BLOCK // 4
@@ -317,19 +317,21 @@
             if b == nb - 1:
                 total = total + jnp.where(present[1], got_high[part].astype(F32), 0.0)
             out[b, part] = total.astype(BF16)
+    me = member()
     for step, chunk in enumerate(outs):
-        chunk[...] = out[me ^ step]
+        chunk[:2] = out[me ^ step]
+        chunk[2] = grad_q[me ^ step]
 
 
 def unpack_kernel(*refs):
     here, across, *refs = refs
-    grad_kv, outs = refs[:GROUP], refs[GROUP:]
-    outs[2][...] = (here[...] + across[...].astype(F32)).astype(BF16)
+    chunks, (*outs, mixed) = refs[:GROUP], refs[GROUP:]
+    mixed[...] = (here[...] + across[...].astype(F32)).astype(BF16)
     me = member()
     for step in range(GROUP):
         at = columns(me ^ step)
-        outs[0][:, at] = grad_kv[step][0]
-        outs[1][:, at] = grad_kv[step][1]
+        for part, out in enumerate(outs):
+            out[:, at] = chunks[step][part]
 
 
 def share():
@@ -393,24 +395,34 @@
     weight_flops = 2 * rows * out_weight.size
 
     chunk = shape(rows, HEAD_DIM)
-    pairs = call(pack_kernel, [block] * GROUP, (keys, values))
-    far = swapped(out_grad, "mp", 2)
-    beside_1 = swapped(out_grad, "mp", 1)
-    pairs = exchanged(pairs)
-    near, level_1, far, *refs = call(
+    triple = shape(3, rows, HEAD_DIM)
+    *chunks, own_grad = call(
+        pack_kernel,
+        [triple] * GROUP + [shape(*out_grad.shape)],
+        (queries, keys, values, out_grad),
+        scratch=[pltpu.SemaphoreType.DMA((1 + 3 * GROUP,))],
+        space=pltpu.HBM,
+        limit=56,
+    )
+    far = swapped(own_grad, "mp", 2)
+    chunks = exchanged(chunks)
+    chunks[:1] = call(copy_kernel, [triple], chunks[:1])
+    far, near, queries, level_1, *refs = call(
         functools.partial(gather_kernel, nb, groups),
-        [shape(nb, 2, rows, HEAD_DIM), shape(2, tokens // 2, HEAD_DIM), shape(*far.shape)]
-        + sent
-        + [chunk] * GROUP,
-        (queries, far, *pairs),
-    )
-    others = crossed(refs[:-GROUP])
-    query_chunks = exchanged(refs[-GROUP:])
-    pieces = [out_grad, beside_1, far, swapped(far, "mp", 1)]
+        [
+            shape(*out_grad.shape),
+            shape(nb, 2, rows, HEAD_DIM),
+            shape(nb, rows, HEAD_DIM),
+            shape(2, tokens // 2, HEAD_DIM),
+        ]
+        + sent,
+        (far, *chunks),
+    )
+    others = crossed(refs)
     grad_chunks = call(
         grad_kernel,
         [chunk] * GROUP,
-        (*pieces, out_weight),
+        (own_grad, swapped(own_grad, "mp", 1), far, swapped(far, "mp", 1), out_weight),
         scratch=[pltpu.VMEM((rows, model), BF16), pltpu.VMEM((rows, width), BF16)],
         flops=weight_flops,
     )
@@ -425,7 +437,7 @@
             shape(nb, 4, BLOCK, BLOCK, dtype=F32),
             shape(nb, 8, BLOCK, dtype=F32),
         ],
-        (near, level_1, *query_chunks, grad_chunks[0]),
+        (near, queries, level_1, grad_chunks[0]),
         flops=score_flops,
     )
     grad_chunks = exchanged(grad_chunks)
@@ -445,17 +457,13 @@
         flops=score_flops,
     )
     other_grads = crossed(rim_grads)
-    *grad_q, grad_kv = call(
+    grad_q, grad_kv = call(
         functools.partial(backward_kernel, nb, groups),
-        [chunk] * GROUP + [shape(2, nb, rows, HEAD_DIM, dtype=F32)],
+        [shape(nb, rows, HEAD_DIM), shape(2, nb, rows, HEAD_DIM, dtype=F32)],
         (query, k_t, k1_t, prob, shift, grads, *others),
-        scratch=[
-            pltpu.VMEM((nb, rows, HEAD_DIM), BF16),
-            pltpu.VMEM((2, tokens // 2, HEAD_DIM), F32),
-        ],
+        scratch=[pltpu.VMEM((2, tokens // 2, HEAD_DIM), F32)],
         flops=1,
     )
-    grad_q = exchanged(grad_q)
     local = rows // N_MP
     shares = shape(2, local, model)
     kept, given = call(
@@ -465,24 +473,24 @@
         scratch=[pltpu.VMEM((rows, width), BF16), pltpu.VMEM((rows, model), BF16)],
         flops=weight_flops,
     )
-    grad_q, *grad_kv = call(
+    chunks = call(
         functools.partial(combine_kernel, nb, groups),
-        [shape(rows, width)] + [block] * GROUP,
-        (grad_kv, *other_grads, *grad_q),
+        [triple] * GROUP,
+        (grad_q, grad_kv, *other_grads),
         scratch=[pltpu.VMEM((nb, 2, rows, HEAD_DIM), BF16)],
         flops=20 * score_flops,
     )
     across, here = call(
         share_kernel,
         [shape(local, model), shape(local, model, dtype=F32)],
-        (kept, swapped(given, "mp", 1), grad_kv[0]),
-    )
-    grad_kv = exchanged(grad_kv)
+        (kept, swapped(given, "mp", 1), chunks[0]),
+    )
+    chunks = exchanged(chunks)
     across = swapped(across, "mp", 2)
-    grad_k, grad_v, mixed = call(
+    grad_k, grad_v, grad_q, mixed = call(
         unpack_kernel,
-        [shape(rows, width)] * 2 + [shape(local, model)],
-        (here, across, *grad_kv),
+        [shape(rows, width)] * 3 + [shape(local, model)],
+        (here, across, *chunks),
     )
     return mixed, grad_q, grad_k, grad_v
 

time: 69.5 us -> 67.5 us (0.971)
  starting transfers between devices: 30.3 us -> 21.6 us
  waiting for transfers between devices: 19.7 us -> 28.2 us
  local copies, waits for them, and re-layouts: 5.39 us -> 1.88 us
  Pallas kernels: 13.1 us -> 14.9 us
    ppermute x25 -> x19, starting transfers between devices: 30.3 us -> 21.6 us  [swapped(): lax.ppermute(x, axis, [(i, i ^ step) for i in range(lax.axis_size(axis))])]
    ppermute x25 -> x19, waiting for transfers between devices: 19.7 us -> 28.2 us  [swapped(): lax.ppermute(x, axis, [(i, i ^ step) for i in range(lax.axis_size(axis))])]
    unnamed x12 -> x6, local copies, waits for them, and re-layouts: 5.39 us -> 1.88 us
    pallas_call x11 -> x12, Pallas kernels: 13.1 us -> 14.9 us  [call(): pl.pallas_call(kernel, out_shape=out_shape, in_specs=[pl.BlockSpec(memory...]
  transfers between devices with their start and end apart: 25 -> 19, of which waited for: 10 -> 11; matrix products, arithmetic and copies ran while one was open for 0% -> 0% of each run, Pallas kernels for 11% -> 10%
where the time goes in v5:
time: 67.5 us; the launch traced here: 67.3 us
  waiting for transfers between devices  28.2 us (42%)
  starting transfers between devices  21.6 us (32%)
  Pallas kernels  14.9 us (22%)
  local copies, waits for them, and re-layouts  1.88 us (3%)
  between operations  0.77 us (1%)
    ppermute x19, waiting for transfers between devices, swapped(): lax.ppermute(x, axis, [(i, i ^ step) for i in range(lax.axis_size(axis))])  28.2 us
    ppermute x19, starting transfers between devices, swapped(): lax.ppermute(x, axis, [(i, i ^ step) for i in range(lax.axis_size(axis))])  21.6 us
    pallas_call x12, Pallas kernels, call(): pl.pallas_call(kernel, out_shape=out_shape, in_specs=[pl.BlockSpec(memory...  14.9 us
    unnamed x6, local copies, waits for them, and re-layouts  1.88 us
  transfers between devices with their start and end apart: 19, of which 11 were waited for; matrix products, arithmetic and copies ran while one was open for 0% of the time, Pallas kernels for 10%

profile of v5, /device:TPU:0, one launch (start us, length us, event | category | flops | bytes accessed | tf_op | source)
XLA Modules:
  0.0 67.3 jit_solution(15593371859526844416)
XLA Ops:
  0.6 2.4 %shard_map.84 = (bf16[3,256,128]{2,1,0:T(8,128)(2,1)}, bf16[3,256,128]{2,1,0:T(8,128)(2,1)}, bf16[3,256,128]{2,1,0:T(8,128)(2,1)}, bf16[3,256,128]{2,1,0:T(8,128)(2,1)}, bf16[64,2048]{1,0:T(8,128)(2,1)}) custom-call(bf16[256,512]{1,0:T(8,128)(2,1)} %q.1, bf16[256,512]{1,0:T(8,128)(2,1)} %k.1, bf16[256,512]{1,0:T(8,128)(2,1)} %v.1, bf16[64,2048]{1,0:T(8,128)(2,1)} %out_grad.1), custom_call_target="tpu_custom_call" | custom-call | tf_op jit(solution)/shard_map/pallas_call | solution.py:36
  3.1 3.0 %collective-permute-start = (bf16[64,2048]{1,0:T(8,128)(2,1)}, bf16[64,2048]{1,0:T(8,128)(2,1)S(1)}, u32[]{:S(2)}, u32[]{:S(2)}) collective-permute-start(bf16[64,2048]{1,0:T(8,128)(2,1)} %get-tuple-element.47.refs_0_), channel_id=1, source_target_pairs={{0,2},{1,3},{2,0},{3,1},{4,6},{5,7},{6,4},{7,5},{8,10},{9,11},{10,... | collective-permute-start | bytes 786440 | tf_op jit(solution)/shard_map/ppermute | solution.py:364
  6.1 1.5 %collective-permute-start.1 = (bf16[3,256,128]{2,1,0:T(8,128)(2,1)}, bf16[3,256,128]{2,1,0:T(8,128)(2,1)S(1)}, u32[]{:S(2)}, u32[]{:S(2)}) collective-permute-start(bf16[3,256,128]{2,1,0:T(8,128)(2,1)} %get-tuple-element.49), channel_id=1, source_target_pairs={{0,4},{4,0},{8,12},{12,8},{16,20},{20,16},{24,28},{28,24},{1,5},{5... | collective-permute-start | bytes 589832 | tf_op jit(solution)/shard_map/ppermute | solution.py:364
  7.6 1.6 %collective-permute-start.2 = (bf16[3,256,128]{2,1,0:T(8,128)(2,1)}, bf16[3,256,128]{2,1,0:T(8,128)(2,1)S(1)}, u32[]{:S(2)}, u32[]{:S(2)}) collective-permute-start(bf16[3,256,128]{2,1,0:T(8,128)(2,1)} %get-tuple-element.50), channel_id=1, source_target_pairs={{0,8},{4,12},{8,0},{12,4},{16,24},{20,28},{24,16},{28,20},{1,9},{5... | collective-permute-start | bytes 589832 | tf_op jit(solution)/shard_map/ppermute | solution.py:364
  10.5 2.7 %collective-permute-done.1.refs_1_ = bf16[3,256,128]{2,1,0:T(8,128)(2,1)S(1)} collective-permute-done((bf16[3,256,128]{2,1,0:T(8,128)(2,1)}, bf16[3,256,128]{2,1,0:T(8,128)(2,1)S(1)}, u32[]{:S(2)}, u32[]{:S(2)}) %collective-permute-start.1) | collective-permute-done | bytes 196640 | tf_op jit(solution)/shard_map/ppermute | solution.py:364
  13.2 2.4 %collective-permute-done.2.refs_2_ = bf16[3,256,128]{2,1,0:T(8,128)(2,1)S(1)} collective-permute-done((bf16[3,256,128]{2,1,0:T(8,128)(2,1)}, bf16[3,256,128]{2,1,0:T(8,128)(2,1)S(1)}, u32[]{:S(2)}, u32[]{:S(2)}) %collective-permute-start.2) | collective-permute-done | bytes 196640 | tf_op jit(solution)/shard_map/ppermute | solution.py:364
  15.7 2.4 %collective-permute-done.3.refs_3_ = bf16[3,256,128]{2,1,0:T(8,128)(2,1)S(1)} collective-permute-done((bf16[3,256,128]{2,1,0:T(8,128)(2,1)}, bf16[3,256,128]{2,1,0:T(8,128)(2,1)S(1)}, u32[]{:S(2)}, u32[]{:S(2)}) %collective-permute-start.3) | collective-permute-done | bytes 196640 | tf_op jit(solution)/shard_map/ppermute | solution.py:364
  18.9 2.7 %collective-permute-start.6 = (bf16[4,256,128]{2,1,0:T(8,128)(2,1)S(1)}, bf16[4,256,128]{2,1,0:T(8,128)(2,1)S(1)}, u32[]{:S(2)}, u32[]{:S(2)}) collective-permute-start(bf16[4,256,128]{2,1,0:T(8,128)(2,1)S(1)} %get-tuple-element.62), channel_id=1, source_target_pairs={{0,16},{4,20},{8,24},{12,28},{16,0},{20,4},{24,8},{28,12},{1,17},{... | collective-permute-start | bytes 786440 | tf_op jit(solution)/shard_map/ppermute | solution.py:364
  23.3 1.6 %collective-permute-start.7 = (bf16[256,128]{1,0:T(8,128)(2,1)S(1)}, bf16[256,128]{1,0:T(8,128)(2,1)S(1)}, u32[]{:S(2)}, u32[]{:S(2)}) collective-permute-start(bf16[256,128]{1,0:T(8,128)(2,1)S(1)} %get-tuple-element.63), channel_id=1, source_target_pairs={{0,4},{4,0},{8,12},{12,8},{16,20},{20,16},{24,28},{28,24},{1,5},{5... | collective-permute-start | bytes 196616 | tf_op jit(solution)/shard_map/ppermute | solution.py:364
  24.9 1.6 %collective-permute-start.8 = (bf16[256,128]{1,0:T(8,128)(2,1)S(1)}, bf16[256,128]{1,0:T(8,128)(2,1)S(1)}, u32[]{:S(2)}, u32[]{:S(2)}) collective-permute-start(bf16[256,128]{1,0:T(8,128)(2,1)S(1)} %get-tuple-element.64), channel_id=1, source_target_pairs={{0,8},{4,12},{8,0},{12,4},{16,24},{20,28},{24,16},{28,20},{1,9},{5... | collective-permute-start | bytes 196616 | tf_op jit(solution)/shard_map/ppermute | solution.py:364
  26.9 1.7 %shard_map.88 = (bf16[3,4,256,128]{3,2,1,0:T(8,128)(2,1)S(1)}, bf16[128,1024]{1,0:T(8,128)(2,1)S(1)}, bf16[128,1024]{1,0:T(8,128)(2,1)S(1)}, bf16[128,512]{1,0:T...) custom-call(bf16[4,2,256,128]{3,2,1,0:T(8,128)(2,1)S(1)} %get-tuple-element, ...), custom_call_target="tpu_custom_call" | custom-call | flops 335544320 | bytes 6914048 | tf_op jit(solution)/shard_map/pallas_call | solution.py:36
  28.5 5.7 %collective-permute-done.6.refs_5_.refs_4_.refs_6_ = bf16[4,256,128]{2,1,0:T(8,128)(2,1)S(1)} collective-permute-done((bf16[4,256,128]{2,1,0:T(8,128)(2,1)S(1)}, bf16[4,256,128]{2,1,0:T(8,128)(2,1)S(1)}, u32[]{:S(2)}, u32[]{:S(2)}) %collective-permute-start.6) | collective-permute-done | bytes 262176 | tf_op jit(solution)/shard_map/ppermute | solution.py:364
  34.2 1.5 %collective-permute-done.9.refs_9_.refs_8_ = bf16[256,128]{1,0:T(8,128)(2,1)S(1)} collective-permute-done((bf16[256,128]{1,0:T(8,128)(2,1)S(1)}, bf16[256,128]{1,0:T(8,128)(2,1)S(1)}, u32[]{:S(2)}, u32[]{:S(2)}) %collective-permute-start.9) | collective-permute-done | bytes 65568 | tf_op jit(solution)/shard_map/ppermute | solution.py:364
  35.8 1.6 %shard_map.89 = (bf16[4,5,256,256]{3,2,1,0:T(8,128)(2,1)S(1)}, bf16[256,128]{1,0:T(8,128)(2,1)S(1)}, bf16[256,128]{1,0:T(8,128)(2,1)S(1)}, bf16[256,128]{1,0:T(8,128)(2,1)S(1)}, bf16[256,128]{1,0:T(8,128)(2,1)S(1)}) custom-call(bf16[3,4,256,128]{3,2,1,0:T(8,128)(2,1)S(1)} %get-tuple-element.57.refs_0_, bf16[128,1024]{1,0:T(8,128)(2,1)S(1)} %get-tuple-element.58.refs_1_, ...), custom_call_target="tpu_custom_call" | custom-call | flops 335544320 | bytes 8814592 | tf_op jit(solution)/shard_map/pallas_call | solution.py:36
  37.4 2.9 %shard_map.90 = (bf16[4,256,128]{2,1,0:T(8,128)(2,1)S(1)}, bf16[4,5,256,256]{3,2,1,0:T(8,128)(2,1)S(1)}, bf16[4,256,128]{2,1,0:T(8,128)(2,1)S(1)}) custom-call(bf16[3,4,256,128]{3,2,1,0:T(8,128)(2,1)S(1)} %get-tuple-element.57.refs_0_, bf16[4,2,256,128]{3,2,1,0:T(8,128)(2,1)S(1)} %get-tuple-element.52.near.refs_1_, ...), custom_call_target="tpu_custom_call" | custom-call | flops 335544320 | bytes 7864320 | tf_op jit(solution)/shard_map/pallas_call | solution.py:36
  41.2 3.6 %collective-permute-start.11 = (bf16[256,128]{1,0:T(8,128)(2,1)S(1)}, bf16[256,128]{1,0:T(8,128)(2,1)S(1)}, u32[]{:S(2)}, u32[]{:S(2)}) collective-permute-start(bf16[256,128]{1,0:T(8,128)(2,1)S(1)} %get-tuple-element.68), channel_id=1, source_target_pairs={{0,8},{4,12},{8,0},{12,4},{16,24},{20,28},{24,16},{28,20},{1,9},{5... | collective-permute-start | bytes 196616 | tf_op jit(solution)/shard_map/ppermute | solution.py:364
  44.8 2.3 %shard_map.92 = (bf16[4,256,128]{2,1,0:T(8,128)(2,1)S(1)}, f32[2,4,256,128]{3,2,1,0:T(8,128)S(1)}) custom-call(bf16[3,4,256,128]{3,2,1,0:T(8,128)(2,1)S(1)} %get-tuple-element.57.refs_0_, bf16[128,1024]{1,0:T(8,128)(2,1)S(1)} %get-tuple-element.74.refs_1_, bf16[128,512]{1,0:T(8,128)(2,1)S(1)} %get-tuple-element.75.refs_2_, ...), custom_call_target="tpu_custom_call" | custom-call | flops 1 | bytes 8257536 | tf_op jit(solution)/shard_map/pallas_call | solution.py:36
  47.5 3.1 %collective-permute-done.12.refs_3_ = bf16[256,128]{1,0:T(8,128)(2,1)S(1)} collective-permute-done((bf16[256,128]{1,0:T(8,128)(2,1)S(1)}, bf16[256,128]{1,0:T(8,128)(2,1)S(1)}, u32[]{:S(2)}, u32[]{:S(2)}) %collective-permute-start.12) | collective-permute-done | bytes 65568 | tf_op jit(solution)/shard_map/ppermute | solution.py:364
  51.5 1.6 %collective-permute-done.14.refs_0_ = bf16[4,256,128]{2,1,0:T(8,128)(2,1)S(1)} collective-permute-done((bf16[4,256,128]{2,1,0:T(8,128)(2,1)S(1)}, bf16[4,256,128]{2,1,0:T(8,128)(2,1)S(1)}, u32[]{:S(2)}, u32[]{:S(2)}) %collective-permute-start.14) | collective-permute-done | bytes 262176 | tf_op jit(solution)/shard_map/ppermute | solution.py:364
  54.3 2.2 %collective-permute-start.16 = (bf16[3,256,128]{2,1,0:T(8,128)(2,1)S(1)}, bf16[3,256,128]{2,1,0:T(8,128)(2,1)S(1)}, u32[]{:S(2)}, u32[]{:S(2)}) collective-permute-start(bf16[3,256,128]{2,1,0:T(8,128)(2,1)S(1)} %get-tuple-element.83), channel_id=1, source_target_pairs={{0,4},{4,0},{8,12},{12,8},{16,20},{20,16},{24,28},{28,24},{1,5},{5... | collective-permute-start | bytes 589832 | tf_op jit(solution)/shard_map/ppermute | solution.py:364
  56.4 1.5 %collective-permute-start.18 = (bf16[3,256,128]{2,1,0:T(8,128)(2,1)S(1)}, bf16[3,256,128]{2,1,0:T(8,128)(2,1)S(1)}, u32[]{:S(2)}, u32[]{:S(2)}) collective-permute-start(bf16[3,256,128]{2,1,0:T(8,128)(2,1)S(1)} %get-tuple-element.85), channel_id=1, source_target_pairs={{0,12},{4,8},{8,4},{12,0},{16,28},{20,24},{24,20},{28,16},{1,13},{... | collective-permute-start | bytes 589832 | tf_op jit(solution)/shard_map/ppermute | solution.py:364
  57.9 3.4 %collective-permute-done.16.refs_3_ = bf16[3,256,128]{2,1,0:T(8,128)(2,1)S(1)} collective-permute-done((bf16[3,256,128]{2,1,0:T(8,128)(2,1)S(1)}, bf16[3,256,128]{2,1,0:T(8,128)(2,1)S(1)}, u32[]{:S(2)}, u32[]{:S(2)}) %collective-permute-start.16) | collective-permute-done | bytes 196640 | tf_op jit(solution)/shard_map/ppermute | solution.py:364
  61.3 2.9 %collective-permute-done.17.refs_4_ = bf16[3,256,128]{2,1,0:T(8,128)(2,1)S(1)} collective-permute-done((bf16[3,256,128]{2,1,0:T(8,128)(2,1)S(1)}, bf16[3,256,128]{2,1,0:T(8,128)(2,1)S(1)}, u32[]{:S(2)}, u32[]{:S(2)}) %collective-permute-start.17) | collective-permute-done | bytes 196640 | tf_op jit(solution)/shard_map/ppermute | solution.py:364
  64.2 2.0 %collective-permute-done.18.refs_5_ = bf16[3,256,128]{2,1,0:T(8,128)(2,1)S(1)} collective-permute-done((bf16[3,256,128]{2,1,0:T(8,128)(2,1)S(1)}, bf16[3,256,128]{2,1,0:T(8,128)(2,1)S(1)}, u32[]{:S(2)}, u32[]{:S(2)}) %collective-permute-start.18) | collective-permute-done | bytes 196640 | tf_op jit(solution)/shard_map/ppermute | solution.py:364
  (32 shorter events, 8.8 us)
Async XLA Ops:
  0.6 20.9 %copy-start = (bf16[512,2048]{1,0:T(8,128)(2,1)S(1)}, bf16[512,2048]{1,0:T(8,128)(2,1)}, u32[]{:S(2)}) copy-start(bf16[512,2048]{1,0:T(8,128)(2,1)} %refs_4_.3) | copy-start | bytes 6291460
  3.1 15.0 %collective-permute-start = (bf16[64,2048]{1,0:T(8,128)(2,1)}, bf16[64,2048]{1,0:T(8,128)(2,1)S(1)}, u32[]{:S(2)}, u32[]{:S(2)}) collective-permute-start(bf16[64,2048]{1,0:T(8,128)(2,1)} %get-tuple-element.47.refs_0_), channel_id=1, source_target_pairs={{0,2},{1,3},{2,0},{3,1},{4,6},{5,7},{6,4},{7,5},{8,10},{9,11},{10,... | collective-permute-start | bytes 786440 | tf_op jit(solution)/shard_map/ppermute | solution.py:364
  6.1 7.1 %collective-permute-start.1 = (bf16[3,256,128]{2,1,0:T(8,128)(2,1)}, bf16[3,256,128]{2,1,0:T(8,128)(2,1)S(1)}, u32[]{:S(2)}, u32[]{:S(2)}) collective-permute-start(bf16[3,256,128]{2,1,0:T(8,128)(2,1)} %get-tuple-element.49), channel_id=1, source_target_pairs={{0,4},{4,0},{8,12},{12,8},{16,20},{20,16},{24,28},{28,24},{1,5},{5... | collective-permute-start | bytes 589832 | tf_op jit(solution)/shard_map/ppermute | solution.py:364
  7.6 8.1 %collective-permute-start.2 = (bf16[3,256,128]{2,1,0:T(8,128)(2,1)}, bf16[3,256,128]{2,1,0:T(8,128)(2,1)S(1)}, u32[]{:S(2)}, u32[]{:S(2)}) collective-permute-start(bf16[3,256,128]{2,1,0:T(8,128)(2,1)} %get-tuple-element.50), channel_id=1, source_target_pairs={{0,8},{4,12},{8,0},{12,4},{16,24},{20,28},{24,16},{28,20},{1,9},{5... | collective-permute-start | bytes 589832 | tf_op jit(solution)/shard_map/ppermute | solution.py:364
  9.2 8.9 %collective-permute-start.3 = (bf16[3,256,128]{2,1,0:T(8,128)(2,1)}, bf16[3,256,128]{2,1,0:T(8,128)(2,1)S(1)}, u32[]{:S(2)}, u32[]{:S(2)}) collective-permute-start(bf16[3,256,128]{2,1,0:T(8,128)(2,1)} %get-tuple-element.51), channel_id=1, source_target_pairs={{0,12},{4,8},{8,4},{12,0},{16,28},{20,24},{24,20},{28,16},{1,13},{... | collective-permute-start | bytes 589832 | tf_op jit(solution)/shard_map/ppermute | solution.py:364
  9.6 12.0 %collective-permute-start.4 = (bf16[64,2048]{1,0:T(8,128)(2,1)}, bf16[64,2048]{1,0:T(8,128)(2,1)S(1)}, u32[]{:S(2)}, u32[]{:S(2)}) collective-permute-start(bf16[64,2048]{1,0:T(8,128)(2,1)} %get-tuple-element.47.refs_0_), channel_id=1, source_target_pairs={{0,1},{1,0},{2,3},{3,2},{4,5},{5,4},{6,7},{7,6},{8,9},{9,8},{10,11... | collective-permute-start | bytes 786440 | tf_op jit(solution)/shard_map/ppermute | solution.py:364
  9.6 0.9 %copy-start.2 = (bf16[3,256,128]{2,1,0:T(8,128)(2,1)S(1)}, bf16[3,256,128]{2,1,0:T(8,128)(2,1)}, u32[]{:S(2)}) copy-start(bf16[3,256,128]{2,1,0:T(8,128)(2,1)} %get-tuple-element.48.x) | copy-start | bytes 589828
  18.8 2.7 %collective-permute-start.5 = (bf16[64,2048]{1,0:T(8,128)(2,1)S(1)}, bf16[64,2048]{1,0:T(8,128)(2,1)S(1)}, u32[]{:S(2)}, u32[]{:S(2)}) collective-permute-start(bf16[64,2048]{1,0:T(8,128)(2,1)S(1)} %get-tuple-element.55.refs_2_), channel_id=1, source_target_pairs={{0,1},{1,0},{2,3},{3,2},{4,5},{5,4},{6,7},{7,6},{8,9},{9,8},{10,11... | collective-permute-start | bytes 786440 | tf_op jit(solution)/shard_map/ppermute | solution.py:364
  18.9 15.3 %collective-permute-start.6 = (bf16[4,256,128]{2,1,0:T(8,128)(2,1)S(1)}, bf16[4,256,128]{2,1,0:T(8,128)(2,1)S(1)}, u32[]{:S(2)}, u32[]{:S(2)}) collective-permute-start(bf16[4,256,128]{2,1,0:T(8,128)(2,1)S(1)} %get-tuple-element.62), channel_id=1, source_target_pairs={{0,16},{4,20},{8,24},{12,28},{16,0},{20,4},{24,8},{28,12},{1,17},{... | collective-permute-start | bytes 786440 | tf_op jit(solution)/shard_map/ppermute | solution.py:364
  21.5 1.0 %copy-start.1 = (bf16[64,2048]{1,0:T(8,128)(2,1)S(1)}, bf16[64,2048]{1,0:T(8,128)(2,1)}, u32[]{:S(2)}) copy-start(bf16[64,2048]{1,0:T(8,128)(2,1)} %get-tuple-element.47.refs_0_) | copy-start | bytes 786436
  23.3 10.9 %collective-permute-start.7 = (bf16[256,128]{1,0:T(8,128)(2,1)S(1)}, bf16[256,128]{1,0:T(8,128)(2,1)S(1)}, u32[]{:S(2)}, u32[]{:S(2)}) collective-permute-start(bf16[256,128]{1,0:T(8,128)(2,1)S(1)} %get-tuple-element.63), channel_id=1, source_target_pairs={{0,4},{4,0},{8,12},{12,8},{16,20},{20,16},{24,28},{28,24},{1,5},{5... | collective-permute-start | bytes 196616 | tf_op jit(solution)/shard_map/ppermute | solution.py:364
  24.9 9.3 %collective-permute-start.8 = (bf16[256,128]{1,0:T(8,128)(2,1)S(1)}, bf16[256,128]{1,0:T(8,128)(2,1)S(1)}, u32[]{:S(2)}, u32[]{:S(2)}) collective-permute-start(bf16[256,128]{1,0:T(8,128)(2,1)S(1)} %get-tuple-element.64), channel_id=1, source_target_pairs={{0,8},{4,12},{8,0},{12,4},{16,24},{20,28},{24,16},{28,20},{1,9},{5... | collective-permute-start | bytes 196616 | tf_op jit(solution)/shard_map/ppermute | solution.py:364
  26.5 9.3 %collective-permute-start.9 = (bf16[256,128]{1,0:T(8,128)(2,1)S(1)}, bf16[256,128]{1,0:T(8,128)(2,1)S(1)}, u32[]{:S(2)}, u32[]{:S(2)}) collective-permute-start(bf16[256,128]{1,0:T(8,128)(2,1)S(1)} %get-tuple-element.65), channel_id=1, source_target_pairs={{0,12},{4,8},{8,4},{12,0},{16,28},{20,24},{24,20},{28,16},{1,13},{... | collective-permute-start | bytes 196616 | tf_op jit(solution)/shard_map/ppermute | solution.py:364
  40.3 12.9 %collective-permute-start.14 = (bf16[4,256,128]{2,1,0:T(8,128)(2,1)S(1)}, bf16[4,256,128]{2,1,0:T(8,128)(2,1)S(1)}, u32[]{:S(2)}, u32[]{:S(2)}) collective-permute-start(bf16[4,256,128]{2,1,0:T(8,128)(2,1)S(1)} %get-tuple-element.79), channel_id=1, source_target_pairs={{0,16},{4,20},{8,24},{12,28},{16,0},{20,4},{24,8},{28,12},{1,17},{... | collective-permute-start | bytes 786440 | tf_op jit(solution)/shard_map/ppermute | solution.py:364
  40.8 6.3 %collective-permute-start.10 = (bf16[256,128]{1,0:T(8,128)(2,1)S(1)}, bf16[256,128]{1,0:T(8,128)(2,1)S(1)}, u32[]{:S(2)}, u32[]{:S(2)}) collective-permute-start(bf16[256,128]{1,0:T(8,128)(2,1)S(1)} %get-tuple-element.67), channel_id=1, source_target_pairs={{0,4},{4,0},{8,12},{12,8},{16,20},{20,16},{24,28},{28,24},{1,5},{5... | collective-permute-start | bytes 196616 | tf_op jit(solution)/shard_map/ppermute | solution.py:364
  41.2 6.3 %collective-permute-start.11 = (bf16[256,128]{1,0:T(8,128)(2,1)S(1)}, bf16[256,128]{1,0:T(8,128)(2,1)S(1)}, u32[]{:S(2)}, u32[]{:S(2)}) collective-permute-start(bf16[256,128]{1,0:T(8,128)(2,1)S(1)} %get-tuple-element.68), channel_id=1, source_target_pairs={{0,8},{4,12},{8,0},{12,4},{16,24},{20,28},{24,16},{28,20},{1,9},{5... | collective-permute-start | bytes 196616 | tf_op jit(solution)/shard_map/ppermute | solution.py:364
  44.8 5.9 %collective-permute-start.12 = (bf16[256,128]{1,0:T(8,128)(2,1)S(1)}, bf16[256,128]{1,0:T(8,128)(2,1)S(1)}, u32[]{:S(2)}, u32[]{:S(2)}) collective-permute-start(bf16[256,128]{1,0:T(8,128)(2,1)S(1)} %get-tuple-element.69), channel_id=1, source_target_pairs={{0,12},{4,8},{8,4},{12,0},{16,28},{20,24},{24,20},{28,16},{1,13},{... | collective-permute-start | bytes 196616 | tf_op jit(solution)/shard_map/ppermute | solution.py:364
  51.4 2.0 %collective-permute-start.13 = (bf16[2,64,2048]{2,1,0:T(8,128)(2,1)S(1)}, bf16[2,64,2048]{2,1,0:T(8,128)(2,1)S(1)}, u32[]{:S(2)}, u32[]{:S(2)}) collective-permute-start(bf16[2,64,2048]{2,1,0:T(8,128)(2,1)S(1)} %get-tuple-element.73), channel_id=1, source_target_pairs={{0,1},{1,0},{2,3},{3,2},{4,5},{5,4},{6,7},{7,6},{8,9},{9,8},{10,11... | collective-permute-start | bytes 1572872 | tf_op jit(solution)/shard_map/ppermute | solution.py:364
  53.6 12.6 %collective-permute-start.15 = (bf16[64,2048]{1,0:T(8,128)(2,1)S(1)}, bf16[64,2048]{1,0:T(8,128)(2,1)S(1)}, u32[]{:S(2)}, u32[]{:S(2)}) collective-permute-start(bf16[64,2048]{1,0:T(8,128)(2,1)S(1)} %get-tuple-element.82), channel_id=1, source_target_pairs={{0,2},{1,3},{2,0},{3,1},{4,6},{5,7},{6,4},{7,5},{8,10},{9,11},{10,... | collective-permute-start | bytes 786440 | tf_op jit(solution)/shard_map/ppermute | solution.py:364
  54.3 7.1 %collective-permute-start.16 = (bf16[3,256,128]{2,1,0:T(8,128)(2,1)S(1)}, bf16[3,256,128]{2,1,0:T(8,128)(2,1)S(1)}, u32[]{:S(2)}, u32[]{:S(2)}) collective-permute-start(bf16[3,256,128]{2,1,0:T(8,128)(2,1)S(1)} %get-tuple-element.83), channel_id=1, source_target_pairs={{0,4},{4,0},{8,12},{12,8},{16,20},{20,16},{24,28},{28,24},{1,5},{5... | collective-permute-start | bytes 589832 | tf_op jit(solution)/shard_map/ppermute | solution.py:364
  56.4 7.8 %collective-permute-start.17 = (bf16[3,256,128]{2,1,0:T(8,128)(2,1)S(1)}, bf16[3,256,128]{2,1,0:T(8,128)(2,1)S(1)}, u32[]{:S(2)}, u32[]{:S(2)}) collective-permute-start(bf16[3,256,128]{2,1,0:T(8,128)(2,1)S(1)} %get-tuple-element.84), channel_id=1, source_target_pairs={{0,8},{4,12},{8,0},{12,4},{16,24},{20,28},{24,16},{28,20},{1,9},{5... | collective-permute-start | bytes 589832 | tf_op jit(solution)/shard_map/ppermute | solution.py:364
  56.4 9.8 %collective-permute-start.18 = (bf16[3,256,128]{2,1,0:T(8,128)(2,1)S(1)}, bf16[3,256,128]{2,1,0:T(8,128)(2,1)S(1)}, u32[]{:S(2)}, u32[]{:S(2)}) collective-permute-start(bf16[3,256,128]{2,1,0:T(8,128)(2,1)S(1)} %get-tuple-element.85), channel_id=1, source_target_pairs={{0,12},{4,8},{8,4},{12,0},{16,28},{20,24},{24,20},{28,16},{1,13},{... | collective-permute-start | bytes 589832 | tf_op jit(solution)/shard_map/ppermute | solution.py:364

commit v6 on v5

--- a/solution.py
+++ b/solution.py
@@ -31,12 +31,12 @@
 
 
 def call(kernel, out_shape, args, scratch=(), flops=0, limit=32, space=pltpu.VMEM):
-    whole = pl.BlockSpec(memory_space=pltpu.VMEM)
+    whole = pl.BlockSpec(memory_space=space)
     moved = sum(x.size * x.dtype.itemsize for x in (*args, *out_shape))
     return pl.pallas_call(
         kernel,
         out_shape=out_shape,
-        in_specs=[pl.BlockSpec(memory_space=space)] * len(args),
+        in_specs=[whole] * len(args),
         out_specs=[whole] * len(out_shape),
         scratch_shapes=scratch,
         compiler_params=pltpu.CompilerParams(vmem_limit_bytes=limit << 20),
@@ -112,11 +112,22 @@
         copy.wait()
 
 
-def copy_kernel(x, out):
-    out[...] = x[...]
-
-
-def gather_kernel(nb, groups, far, *refs):
+def pool_kernel(k, v, out):
+    pool = pooling()
+    half = BLOCK // 2
+    for part, source in enumerate((k, v)):
+        once = dot(pool, source[...]).astype(BF16)
+        twice = dot(pool[: half // 2, :half], once).astype(BF16)
+        for head in range(GROUP):
+            out[head, part] = twice[:, head * HEAD_DIM : (head + 1) * HEAD_DIM]
+
+
+def copy_kernel(x, y, x_out, y_out):
+    x_out[...] = x[...]
+    y_out[...] = y[...]
+
+
+def gather_kernel(nb, groups, far, _, *refs):
     chunks, (far_out, near, queries, level_1, *rims) = refs[:GROUP], refs[GROUP:]
     far_out[...] = far[...]
     me = member()
@@ -128,15 +139,18 @@
     for part in range(2):
         for b in range(nb):
             level_1[part, b * half : (b + 1) * half] = dot(pool, near[b, part]).astype(BF16)
-        for c in range(nb // 2):
-            block = dot(pool, level_1[part, at_block(c)]).astype(BF16)
-            rims[0][part, c * half : (c + 1) * half] = block
     if groups == 2:
         upper = lax.axis_index("seq") >= GROUP
-        rims[0][2:] = jnp.where(upper, near[0], near[nb - 1])
+        rims[0][...] = jnp.where(upper, near[0], near[nb - 1])
     else:
-        rims[1][...] = near[nb - 1]
-        rims[2][...] = near[0]
+        rims[0][...] = near[nb - 1]
+        rims[1][...] = near[0]
+
+
+def from_beside(groups, refs):
+    if groups == 2:
+        return (refs[0], refs[0]), refs[1:]
+    return refs[:2], refs[2:]
 
 
 def from_others(groups, refs):
@@ -185,9 +199,16 @@
 
 def forward_kernel(nb, groups, *refs):
     (query, v_t, v1_t, weights, stats), refs = refs[:5], refs[5:]
-    (top_2, rim_low, rim_high), refs = from_others(groups, refs)
-    prob, *outs, attended = refs[GROUP:]
+    (rim_low, rim_high), refs = from_beside(groups, refs)
+    chunks, (prob, grads, top_2, *outs, attended) = refs[:GROUP], refs[GROUP:]
     present = rim_present(groups)
+    me = member()
+    quarter = BLOCK // 4
+    for step, chunk in enumerate(chunks):
+        grads[me ^ step] = chunk[:BLOCK]
+        for part in range(2):
+            level = chunk[BLOCK + part * quarter : BLOCK + (part + 1) * quarter]
+            top_2[part, span(me ^ step, quarter), :] = level
     v2_t = top_2[1].T
     for b in range(nb):
         sides = rim_sides(b, nb)
@@ -219,18 +240,13 @@
             prob[b, side] = (weight * inverse).astype(BF16)
             context = context + dot((rim_high if side else rim_low)[1].T, prob[b, side])
         attended[b] = context.T.astype(BF16)
-    me = member()
     for step, out in enumerate(outs):
         out[...] = attended[me ^ step]
 
 
 def slope_kernel(nb, groups, *refs):
-    (query, near, level_1, prob), refs = refs[:4], refs[4:]
-    (top_2, rim_low, rim_high), refs = from_others(groups, refs)
-    chunks, (grads, shift, *rim_outs, sums, rim_sums) = refs[:GROUP], refs[GROUP:]
-    me = member()
-    for step, chunk in enumerate(chunks):
-        grads[me ^ step] = chunk[...]
+    (query, near, level_1, prob, grads, top_2), refs = refs[:6], refs[6:]
+    (rim_low, rim_high), (shift, *rim_outs, sums, rim_sums) = from_beside(groups, refs)
     for b in range(nb):
         grad = grads[b]
         slopes = []
@@ -267,8 +283,8 @@
 
 
 def backward_kernel(nb, groups, *refs):
-    (query, k_t, k1_t, prob, shift, grads), refs = refs[:6], refs[6:]
-    (top_2, rim_low, rim_high), refs = from_others(groups, refs)
+    (query, k_t, k1_t, prob, shift, grads, top_2), refs = refs[:7], refs[7:]
+    (rim_low, rim_high), refs = from_beside(groups, refs)
     grad_q, grad_kv, sums_1 = refs
     k2_t = top_2[0].T
     even_1, even_2 = averaging(1), averaging(2)
@@ -339,13 +355,17 @@
 
 
 def grad_kernel(*refs):
-    pieces, out_weight, outs, (whole, heads) = refs[:N_MP], refs[N_MP], refs[N_MP + 1 : -2], refs[-2:]
+    pieces, (out_weight, tops), refs = refs[:N_MP], refs[N_MP : N_MP + 2], refs[N_MP + 2 :]
+    *outs, whole, heads = refs
     me = member()
     for step, piece in enumerate(pieces):
         whole[span(share() ^ step, piece.shape[0]), :] = piece[...]
     heads[...] = dot_nt(whole[...], out_weight[...]).astype(BF16)
+    quarter = tops.shape[2]
     for step, out in enumerate(outs):
-        out[...] = heads[:, columns(me ^ step)]
+        out[:BLOCK] = heads[:, columns(me ^ step)]
+        for part in range(2):
+            out[BLOCK + part * quarter : BLOCK + (part + 1) * quarter] = tops[me ^ step, part]
 
 
 def project_kernel(*refs):
@@ -367,6 +387,15 @@
 def exchanged(chunks):
     got = {step: swapped(chunks[step], "seq", step) for step in (3, 1, 2)}
     return [chunks[0]] + [got[step] for step in range(1, GROUP)]
+
+
+def beside(arrays):
+    count = lax.axis_size("seq")
+    if len(arrays) == 1:
+        return [swapped(arrays[0], "seq", GROUP)]
+    up = [(i, i + GROUP) for i in range(count - GROUP)]
+    down = [(j, i) for i, j in up]
+    return [lax.ppermute(arrays[0], "seq", up), lax.ppermute(arrays[1], "seq", down)]
 
 
 def crossed(arrays):
@@ -391,6 +420,9 @@
     model = out_weight.shape[1]
     block = shape(2, rows, HEAD_DIM)
     sent = [shape(4, rows, HEAD_DIM)] if groups == 2 else [block] * 3
+    rims = [block] * (1 if groups == 2 else 2)
+    quarter = rows // 4
+    in_order = shape(nb, rows, HEAD_DIM)
     score_flops = 2 * tokens * 5 * BLOCK * HEAD_DIM
     weight_flops = 2 * rows * out_weight.size
 
@@ -406,7 +438,9 @@
     )
     far = swapped(own_grad, "mp", 2)
     chunks = exchanged(chunks)
-    chunks[:1] = call(copy_kernel, [triple], chunks[:1])
+    (tops,) = call(pool_kernel, [shape(GROUP, 2, quarter, HEAD_DIM)], (keys, values))
+    tops = swapped(tops, "seq", GROUP)
+    chunks[0], own_grad = call(copy_kernel, [triple, shape(*out_grad.shape)], (chunks[0], own_grad))
     far, near, queries, level_1, *refs = call(
         functools.partial(gather_kernel, nb, groups),
         [
@@ -415,14 +449,14 @@
             shape(nb, rows, HEAD_DIM),
             shape(2, tokens // 2, HEAD_DIM),
         ]
-        + sent,
-        (far, *chunks),
-    )
-    others = crossed(refs)
+        + rims,
+        (far, tops, *chunks),
+    )
+    rim_blocks = beside(refs)
     grad_chunks = call(
         grad_kernel,
-        [chunk] * GROUP,
-        (own_grad, swapped(own_grad, "mp", 1), far, swapped(far, "mp", 1), out_weight),
+        [shape(rows + 2 * quarter, HEAD_DIM)] * GROUP,
+        (own_grad, swapped(own_grad, "mp", 1), far, swapped(far, "mp", 1), out_weight, tops),
         scratch=[pltpu.VMEM((rows, model), BF16), pltpu.VMEM((rows, width), BF16)],
         flops=weight_flops,
     )
@@ -441,26 +475,26 @@
         flops=score_flops,
     )
     grad_chunks = exchanged(grad_chunks)
-    prob, *attended = call(
+    prob, grads, top_2, *attended = call(
         functools.partial(forward_kernel, nb, groups),
-        [shape(nb, 5, BLOCK, BLOCK)] + [chunk] * GROUP,
-        (query, v_t, v1_t, weights, stats, *others, *grad_chunks),
+        [shape(nb, 5, BLOCK, BLOCK), in_order, block] + [chunk] * GROUP,
+        (query, v_t, v1_t, weights, stats, *rim_blocks, *grad_chunks),
         scratch=[pltpu.VMEM((nb, rows, HEAD_DIM), BF16)],
         flops=score_flops,
     )
     attended = exchanged(attended)
-    grads, shift, *rim_grads = call(
+    shift, *rim_grads = call(
         functools.partial(slope_kernel, nb, groups),
-        [shape(nb, rows, HEAD_DIM), shape(nb, 5, BLOCK, BLOCK)] + sent,
-        (query, near, level_1, prob, *others, *grad_chunks),
+        [shape(nb, 5, BLOCK, BLOCK)] + sent,
+        (query, near, level_1, prob, grads, top_2, *rim_blocks),
         scratch=[pltpu.VMEM((2, BLOCK, HEAD_DIM), F32), pltpu.VMEM((2, 2, BLOCK, HEAD_DIM), F32)],
         flops=score_flops,
     )
     other_grads = crossed(rim_grads)
     grad_q, grad_kv = call(
         functools.partial(backward_kernel, nb, groups),
-        [shape(nb, rows, HEAD_DIM), shape(2, nb, rows, HEAD_DIM, dtype=F32)],
-        (query, k_t, k1_t, prob, shift, grads, *others),
+        [in_order, shape(2, nb, rows, HEAD_DIM, dtype=F32)],
+        (query, k_t, k1_t, prob, shift, grads, top_2, *rim_blocks),
         scratch=[pltpu.VMEM((2, tokens // 2, HEAD_DIM), F32)],
         flops=1,
     )
@@ -469,7 +503,7 @@
     kept, given = call(
         project_kernel,
         [shares] * 2,
-        (*attended, out_weight, grads),
+        (*attended, out_weight, shift),
         scratch=[pltpu.VMEM((rows, width), BF16), pltpu.VMEM((rows, model), BF16)],
         flops=weight_flops,
     )

time: 67.5 us -> 98 us (1.45)
  Pallas kernels: 14.9 us -> 45.6 us
  waiting for transfers between devices: 28.2 us -> 22.3 us
  starting transfers between devices: 21.6 us -> 25.4 us
  local copies, waits for them, and re-layouts: 1.88 us -> 3.78 us
    pallas_call x12 -> x13, Pallas kernels: 14.9 us -> 45.6 us  [call(): pl.pallas_call(kernel, out_shape=out_shape, in_specs=[whole] * len(args),...]
    ppermute x19 -> x20, waiting for transfers between devices: 28.2 us -> 22.3 us  [swapped(): lax.ppermute(x, axis, [(i, i ^ step) for i in range(lax.axis_size(axis))])]
    ppermute x19 -> x20, starting transfers between devices: 21.6 us -> 25.4 us  [swapped(): lax.ppermute(x, axis, [(i, i ^ step) for i in range(lax.axis_size(axis))])]
    unnamed x6 -> x10, local copies, waits for them, and re-layouts: 1.88 us -> 3.78 us
  transfers between devices with their start and end apart: 19 -> 20, of which waited for: 11 -> 11; matrix products, arithmetic and copies ran while one was open for 0% -> 0% of each run, Pallas kernels for 10% -> 7%
where the time goes in v6:
time: 98 us; the launch traced here: 97.8 us
  Pallas kernels  45.6 us (47%)
  starting transfers between devices  25.4 us (26%)
  waiting for transfers between devices  22.3 us (23%)
  local copies, waits for them, and re-layouts  3.78 us (4%)
    pallas_call x13, Pallas kernels, call(): pl.pallas_call(kernel, out_shape=out_shape, in_specs=[whole] * len(args),...  45.6 us
    ppermute x20, starting transfers between devices, swapped(): lax.ppermute(x, axis, [(i, i ^ step) for i in range(lax.axis_size(axis))])  25.4 us
    ppermute x20, waiting for transfers between devices, swapped(): lax.ppermute(x, axis, [(i, i ^ step) for i in range(lax.axis_size(axis))])  22.3 us
    unnamed x10, local copies, waits for them, and re-layouts  3.78 us
  transfers between devices with their start and end apart: 20, of which 11 were waited for; matrix products, arithmetic and copies ran while one was open for 0% of the time, Pallas kernels for 7%

profile of v6, /device:TPU:0, one launch (start us, length us, event | category | flops | bytes accessed | tf_op | source)
XLA Modules:
  0.0 97.8 jit_solution(12741207207841924005)
XLA Ops:
  0.6 33.0 %shard_map.84 = (bf16[3,256,128]{2,1,0:T(8,128)(2,1)}, bf16[3,256,128]{2,1,0:T(8,128)(2,1)}, bf16[3,256,128]{2,1,0:T(8,128)(2,1)}, bf16[3,256,128]{2,1,0:T(8,128)(2,1)}, bf16[64,2048]{1,0:T(8,128)(2,1)}) custom-call(bf16[256,512]{1,0:T(8,128)(2,1)} %q.1, bf16[256,512]{1,0:T(8,128)(2,1)} %k.3, bf16[256,512]{1,0:T(8,128)(2,1)} %v.3, bf16[64,2048]{1,0:T(8,128)(2,1)} %out_grad.1), custom_call_target="tpu_custom_call" | custom-call | tf_op jit(solution)/shard_map/pallas_call | solution.py:36
  33.6 3.0 %collective-permute-start = (bf16[64,2048]{1,0:T(8,128)(2,1)}, bf16[64,2048]{1,0:T(8,128)(2,1)S(1)}, u32[]{:S(2)}, u32[]{:S(2)}) collective-permute-start(bf16[64,2048]{1,0:T(8,128)(2,1)} %get-tuple-element.50.y), channel_id=1, source_target_pairs={{0,2},{1,3},{2,0},{3,1},{4,6},{5,7},{6,4},{7,5},{8,10},{9,11},{10,... | collective-permute-start | bytes 786440 | tf_op jit(solution)/shard_map/ppermute | solution.py:384
  36.6 1.5 %collective-permute-start.2 = (bf16[3,256,128]{2,1,0:T(8,128)(2,1)}, bf16[3,256,128]{2,1,0:T(8,128)(2,1)S(1)}, u32[]{:S(2)}, u32[]{:S(2)}) collective-permute-start(bf16[3,256,128]{2,1,0:T(8,128)(2,1)} %get-tuple-element.53), channel_id=1, source_target_pairs={{0,4},{4,0},{8,12},{12,8},{16,20},{20,16},{24,28},{28,24},{1,5},{5... | collective-permute-start | bytes 589832 | tf_op jit(solution)/shard_map/ppermute | solution.py:384
  38.2 1.6 %collective-permute-start.3 = (bf16[3,256,128]{2,1,0:T(8,128)(2,1)}, bf16[3,256,128]{2,1,0:T(8,128)(2,1)S(1)}, u32[]{:S(2)}, u32[]{:S(2)}) collective-permute-start(bf16[3,256,128]{2,1,0:T(8,128)(2,1)} %get-tuple-element.54), channel_id=1, source_target_pairs={{0,8},{4,12},{8,0},{12,4},{16,24},{20,28},{24,16},{28,20},{1,9},{5... | collective-permute-start | bytes 589832 | tf_op jit(solution)/shard_map/ppermute | solution.py:384
  42.5 2.7 %collective-permute-start.1 = (bf16[4,2,64,128]{3,2,1,0:T(8,128)(2,1)S(1)}, bf16[4,2,64,128]{3,2,1,0:T(8,128)(2,1)S(1)}, u32[]{:S(2)}, u32[]{:S(2)}) collective-permute-start(bf16[4,2,64,128]{3,2,1,0:T(8,128)(2,1)S(1)} %shard_map.85), channel_id=1, source_target_pairs={{0,16},{4,20},{8,24},{12,28},{16,0},{20,4},{24,8},{28,12},{1,17},{... | collective-permute-start | bytes 393224 | tf_op jit(solution)/shard_map/ppermute | solution.py:384
  47.1 3.4 %collective-permute-done.1._.refs_5_ = bf16[4,2,64,128]{3,2,1,0:T(8,128)(2,1)S(1)} collective-permute-done((bf16[4,2,64,128]{3,2,1,0:T(8,128)(2,1)S(1)}, bf16[4,2,64,128]{3,2,1,0:T(8,128)(2,1)S(1)}, u32[]{:S(2)}, u32[]{:S(2)}) %collective-permute-start.1) | collective-permute-done | bytes 131104 | tf_op jit(solution)/shard_map/ppermute | solution.py:384
  51.9 3.1 %collective-permute-start.7 = (bf16[2,256,128]{2,1,0:T(8,128)(2,1)S(1)}, bf16[2,256,128]{2,1,0:T(8,128)(2,1)S(1)}, u32[]{:S(2)}, u32[]{:S(2)}) collective-permute-start(bf16[2,256,128]{2,1,0:T(8,128)(2,1)S(1)} %get-tuple-element.67), channel_id=1, source_target_pairs={{0,16},{4,20},{8,24},{12,28},{16,0},{20,4},{24,8},{28,12},{1,17},{... | collective-permute-start | bytes 393224 | tf_op jit(solution)/shard_map/ppermute | solution.py:384
  56.5 2.1 %collective-permute-start.9 = (bf16[384,128]{1,0:T(8,128)(2,1)S(1)}, bf16[384,128]{1,0:T(8,128)(2,1)S(1)}, u32[]{:S(2)}, u32[]{:S(2)}) collective-permute-start(bf16[384,128]{1,0:T(8,128)(2,1)S(1)} %get-tuple-element.69), channel_id=1, source_target_pairs={{0,8},{4,12},{8,0},{12,4},{16,24},{20,28},{24,16},{28,20},{1,9},{5... | collective-permute-start | bytes 294920 | tf_op jit(solution)/shard_map/ppermute | solution.py:384
  59.3 1.7 %shard_map.89 = (bf16[3,4,256,128]{3,2,1,0:T(8,128)(2,1)S(1)}, bf16[128,1024]{1,0:T(8,128)(2,1)S(1)}, bf16[128,1024]{1,0:T(8,128)(2,1)S(1)}, bf16[128,512]{1,0:T...) custom-call(bf16[4,2,256,128]{3,2,1,0:T(8,128)(2,1)S(1)} %get-tuple-element, ...), custom_call_target="tpu_custom_call" | custom-call | flops 335544320 | bytes 6946816 | tf_op jit(solution)/shard_map/pallas_call | solution.py:36
  61.4 1.3 %collective-permute-done.9.refs_8_ = bf16[384,128]{1,0:T(8,128)(2,1)S(1)} collective-permute-done((bf16[384,128]{1,0:T(8,128)(2,1)S(1)}, bf16[384,128]{1,0:T(8,128)(2,1)S(1)}, u32[]{:S(2)}, u32[]{:S(2)}) %collective-permute-start.9) | collective-permute-done | bytes 98336 | tf_op jit(solution)/shard_map/ppermute | solution.py:384
  62.7 2.8 %collective-permute-done.10.refs_9_ = bf16[384,128]{1,0:T(8,128)(2,1)S(1)} collective-permute-done((bf16[384,128]{1,0:T(8,128)(2,1)S(1)}, bf16[384,128]{1,0:T(8,128)(2,1)S(1)}, u32[]{:S(2)}, u32[]{:S(2)}) %collective-permute-start.10) | collective-permute-done | bytes 98336 | tf_op jit(solution)/shard_map/ppermute | solution.py:384
  65.5 1.6 %shard_map.90 = (bf16[4,5,256,256]{3,2,1,0:T(8,128)(2,1)S(1)}, bf16[4,256,128]{2,1,0:T(8,128)(2,1)S(1)}, bf16[2,256,128]{2,1,0:T(8,128)(2,1)S(1)}, bf16[256,128]...) custom-call(bf16[3,4,256,128]{3,2,1,0:T(8,128)(2,1)S(1)} %get-tuple-, ...), custom_call_target="tpu_custom_call" | custom-call | flops 335544320 | bytes 9207808 | tf_op jit(solution)/shard_map/pallas_call | solution.py:36
  67.2 2.8 %shard_map.91 = (bf16[4,5,256,256]{3,2,1,0:T(8,128)(2,1)S(1)}, bf16[4,256,128]{2,1,0:T(8,128)(2,1)S(1)}) custom-call(bf16[3,4,256,128]{3,2,1,0:T(8,128)(2,1)S(1)} %get-tuple-element.62.refs_0_, bf16[4,2,256,128]{3,2,1,0:T(8,128)(2,1)S(1)} %get-tuple-element.56.near.refs_1_, bf16[2,512,128]{2,1,0:T(8,128)(2,1)S(1)} %get-tuple-element.58.level_1.refs_2_, ...), custom_call_target="tpu_custom_call" | custom-call | flops 335544320 | bytes 7602176 | tf_op jit(solution)/shard_map/pallas_call | solution.py:36
  70.0 1.2 %collective-permute-start.15 = (bf16[4,256,128]{2,1,0:T(8,128)(2,1)S(1)}, bf16[4,256,128]{2,1,0:T(8,128)(2,1)S(1)}, u32[]{:S(2)}, u32[]{:S(2)}) collective-permute-start(bf16[4,256,128]{2,1,0:T(8,128)(2,1)S(1)} %get-tuple-element.85), channel_id=1, source_target_pairs={{0,16},{4,20},{8,24},{12,28},{16,0},{20,4},{24,8},{28,12},{1,17},{... | collective-permute-start | bytes 786440 | tf_op jit(solution)/shard_map/ppermute | solution.py:384
  72.0 3.2 %collective-permute-start.12 = (bf16[256,128]{1,0:T(8,128)(2,1)S(1)}, bf16[256,128]{1,0:T(8,128)(2,1)S(1)}, u32[]{:S(2)}, u32[]{:S(2)}) collective-permute-start(bf16[256,128]{1,0:T(8,128)(2,1)S(1)} %get-tuple-element.73), channel_id=1, source_target_pairs={{0,8},{4,12},{8,0},{12,4},{16,24},{20,28},{24,16},{28,20},{1,9},{5... | collective-permute-start | bytes 196616 | tf_op jit(solution)/shard_map/ppermute | solution.py:384
  75.4 2.3 %shard_map.93 = (bf16[4,256,128]{2,1,0:T(8,128)(2,1)S(1)}, f32[2,4,256,128]{3,2,1,0:T(8,128)S(1)}) custom-call(bf16[3,4,256,128]{3,2,1,0:T(8,128)(2,1)S(1)} %get-tuple-element.62.refs_0_, bf16[128,1024]{1,0:T(8,128)(2,1)S(1)} %get-tuple-element.81.refs_1_, bf16[128,512]{1,0:T(8,128)(2,1)S(1)} %get-tuple-element.82.refs_2_, ...), custom_call_target="tpu_custom_call" | custom-call | flops 1 | bytes 8257536 | tf_op jit(solution)/shard_map/pallas_call | solution.py:36
  78.7 2.4 %collective-permute-done.13.refs_3_ = bf16[256,128]{1,0:T(8,128)(2,1)S(1)} collective-permute-done((bf16[256,128]{1,0:T(8,128)(2,1)S(1)}, bf16[256,128]{1,0:T(8,128)(2,1)S(1)}, u32[]{:S(2)}, u32[]{:S(2)}) %collective-permute-start.13) | collective-permute-done | bytes 65568 | tf_op jit(solution)/shard_map/ppermute | solution.py:384
  82.0 2.1 %collective-permute-done.15.refs_0_ = bf16[4,256,128]{2,1,0:T(8,128)(2,1)S(1)} collective-permute-done((bf16[4,256,128]{2,1,0:T(8,128)(2,1)S(1)}, bf16[4,256,128]{2,1,0:T(8,128)(2,1)S(1)}, u32[]{:S(2)}, u32[]{:S(2)}) %collective-permute-start.15) | collective-permute-done | bytes 262176 | tf_op jit(solution)/shard_map/ppermute | solution.py:384
  85.3 1.5 %collective-permute-start.18 = (bf16[3,256,128]{2,1,0:T(8,128)(2,1)S(1)}, bf16[3,256,128]{2,1,0:T(8,128)(2,1)S(1)}, u32[]{:S(2)}, u32[]{:S(2)}) collective-permute-start(bf16[3,256,128]{2,1,0:T(8,128)(2,1)S(1)} %get-tuple-element.90), channel_id=1, source_target_pairs={{0,8},{4,12},{8,0},{12,4},{16,24},{20,28},{24,16},{28,20},{1,9},{5... | collective-permute-start | bytes 589832 | tf_op jit(solution)/shard_map/ppermute | solution.py:384
  86.9 1.7 %collective-permute-start.19 = (bf16[3,256,128]{2,1,0:T(8,128)(2,1)S(1)}, bf16[3,256,128]{2,1,0:T(8,128)(2,1)S(1)}, u32[]{:S(2)}, u32[]{:S(2)}) collective-permute-start(bf16[3,256,128]{2,1,0:T(8,128)(2,1)S(1)} %get-tuple-element.91), channel_id=1, source_target_pairs={{0,12},{4,8},{8,4},{12,0},{16,28},{20,24},{24,20},{28,16},{1,13},{... | collective-permute-start | bytes 589832 | tf_op jit(solution)/shard_map/ppermute | solution.py:384
  88.6 3.4 %collective-permute-done.17.refs_3_ = bf16[3,256,128]{2,1,0:T(8,128)(2,1)S(1)} collective-permute-done((bf16[3,256,128]{2,1,0:T(8,128)(2,1)S(1)}, bf16[3,256,128]{2,1,0:T(8,128)(2,1)S(1)}, u32[]{:S(2)}, u32[]{:S(2)}) %collective-permute-start.17) | collective-permute-done | bytes 196640 | tf_op jit(solution)/shard_map/ppermute | solution.py:384
  92.1 1.1 %collective-permute-done.18.refs_4_ = bf16[3,256,128]{2,1,0:T(8,128)(2,1)S(1)} collective-permute-done((bf16[3,256,128]{2,1,0:T(8,128)(2,1)S(1)}, bf16[3,256,128]{2,1,0:T(8,128)(2,1)S(1)}, u32[]{:S(2)}, u32[]{:S(2)}) %collective-permute-start.18) | collective-permute-done | bytes 196640 | tf_op jit(solution)/shard_map/ppermute | solution.py:384
  93.2 3.5 %collective-permute-done.19.refs_5_ = bf16[3,256,128]{2,1,0:T(8,128)(2,1)S(1)} collective-permute-done((bf16[3,256,128]{2,1,0:T(8,128)(2,1)S(1)}, bf16[3,256,128]{2,1,0:T(8,128)(2,1)S(1)}, u32[]{:S(2)}, u32[]{:S(2)}) %collective-permute-start.19) | collective-permute-done | bytes 196640 | tf_op jit(solution)/shard_map/ppermute | solution.py:384
  96.7 1.1 %shard_map.96 = (bf16[256,512]{1,0:T(8,128)(2,1)}, bf16[256,512]{1,0:T(8,128)(2,1)}, bf16[256,512]{1,0:T(8,128)(2,1)}, bf16[64,2048]{1,0:T(8,128)(2,1)}) custom-call(f32[64,2048]{1,0:T(8,128)S(1)} %get-tuple-element.87.refs_0_, bf16[64,2048]{1,0:T(8,128)(2,1)S(1)} %collective-permute-done.16.refs_1_, bf16[3,256,128]{2,1,0:T(8,128)(2,1)S(1)} %get-tuple-element.86._.refs_2_, ...), custom_call_target="tpu_custom_call" | custom-call | tf_op jit(solution)/shard_map/pallas_call | solution.py:36
  (39 shorter events, 12.7 us)
Async XLA Ops:
  0.6 54.3 %copy-start = (bf16[512,2048]{1,0:T(8,128)(2,1)S(1)}, bf16[512,2048]{1,0:T(8,128)(2,1)}, u32[]{:S(2)}) copy-start(bf16[512,2048]{1,0:T(8,128)(2,1)} %refs_4_.3) | copy-start | bytes 6291460
  33.6 17.8 %collective-permute-start = (bf16[64,2048]{1,0:T(8,128)(2,1)}, bf16[64,2048]{1,0:T(8,128)(2,1)S(1)}, u32[]{:S(2)}, u32[]{:S(2)}) collective-permute-start(bf16[64,2048]{1,0:T(8,128)(2,1)} %get-tuple-element.50.y), channel_id=1, source_target_pairs={{0,2},{1,3},{2,0},{3,1},{4,6},{5,7},{6,4},{7,5},{8,10},{9,11},{10,... | collective-permute-start | bytes 786440 | tf_op jit(solution)/shard_map/ppermute | solution.py:384
  36.6 13.9 %collective-permute-start.2 = (bf16[3,256,128]{2,1,0:T(8,128)(2,1)}, bf16[3,256,128]{2,1,0:T(8,128)(2,1)S(1)}, u32[]{:S(2)}, u32[]{:S(2)}) collective-permute-start(bf16[3,256,128]{2,1,0:T(8,128)(2,1)} %get-tuple-element.53), channel_id=1, source_target_pairs={{0,4},{4,0},{8,12},{12,8},{16,20},{20,16},{24,28},{28,24},{1,5},{5... | collective-permute-start | bytes 589832 | tf_op jit(solution)/shard_map/ppermute | solution.py:384
  38.2 12.4 %collective-permute-start.3 = (bf16[3,256,128]{2,1,0:T(8,128)(2,1)}, bf16[3,256,128]{2,1,0:T(8,128)(2,1)S(1)}, u32[]{:S(2)}, u32[]{:S(2)}) collective-permute-start(bf16[3,256,128]{2,1,0:T(8,128)(2,1)} %get-tuple-element.54), channel_id=1, source_target_pairs={{0,8},{4,12},{8,0},{12,4},{16,24},{20,28},{24,16},{28,20},{1,9},{5... | collective-permute-start | bytes 589832 | tf_op jit(solution)/shard_map/ppermute | solution.py:384
  39.7 11.7 %collective-permute-start.4 = (bf16[3,256,128]{2,1,0:T(8,128)(2,1)}, bf16[3,256,128]{2,1,0:T(8,128)(2,1)S(1)}, u32[]{:S(2)}, u32[]{:S(2)}) collective-permute-start(bf16[3,256,128]{2,1,0:T(8,128)(2,1)} %get-tuple-element.55), channel_id=1, source_target_pairs={{0,12},{4,8},{8,4},{12,0},{16,28},{20,24},{24,20},{28,16},{1,13},{... | collective-permute-start | bytes 589832 | tf_op jit(solution)/shard_map/ppermute | solution.py:384
  40.1 0.9 copy-start.1
  41.1 0.9 copy-start.2
  42.5 8.0 %collective-permute-start.1 = (bf16[4,2,64,128]{3,2,1,0:T(8,128)(2,1)S(1)}, bf16[4,2,64,128]{3,2,1,0:T(8,128)(2,1)S(1)}, u32[]{:S(2)}, u32[]{:S(2)}) collective-permute-start(bf16[4,2,64,128]{3,2,1,0:T(8,128)(2,1)S(1)} %shard_map.85), channel_id=1, source_target_pairs={{0,16},{4,20},{8,24},{12,28},{16,0},{20,4},{24,8},{28,12},{1,17},{... | collective-permute-start | bytes 393224 | tf_op jit(solution)/shard_map/ppermute | solution.py:384
  45.2 0.9 copy-start.3
  50.6 4.4 %collective-permute-start.5 = (bf16[64,2048]{1,0:T(8,128)(2,1)S(1)}, bf16[64,2048]{1,0:T(8,128)(2,1)S(1)}, u32[]{:S(2)}, u32[]{:S(2)}) collective-permute-start(bf16[64,2048]{1,0:T(8,128)(2,1)S(1)} %get-tuple-element.59.refs_0_), channel_id=1, source_target_pairs={{0,1},{1,0},{2,3},{3,2},{4,5},{5,4},{6,7},{7,6},{8,9},{9,8},{10,11... | collective-permute-start | bytes 786440 | tf_op jit(solution)/shard_map/ppermute | solution.py:384
  51.8 3.1 %collective-permute-start.6 = (bf16[64,2048]{1,0:T(8,128)(2,1)S(1)}, bf16[64,2048]{1,0:T(8,128)(2,1)S(1)}, u32[]{:S(2)}, u32[]{:S(2)}) collective-permute-start(bf16[64,2048]{1,0:T(8,128)(2,1)S(1)} %get-tuple-element.60.refs_2_), channel_id=1, source_target_pairs={{0,1},{1,0},{2,3},{3,2},{4,5},{5,4},{6,7},{7,6},{8,9},{9,8},{10,11... | collective-permute-start | bytes 786440 | tf_op jit(solution)/shard_map/ppermute | solution.py:384
  51.9 9.5 %collective-permute-start.7 = (bf16[2,256,128]{2,1,0:T(8,128)(2,1)S(1)}, bf16[2,256,128]{2,1,0:T(8,128)(2,1)S(1)}, u32[]{:S(2)}, u32[]{:S(2)}) collective-permute-start(bf16[2,256,128]{2,1,0:T(8,128)(2,1)S(1)} %get-tuple-element.67), channel_id=1, source_target_pairs={{0,16},{4,20},{8,24},{12,28},{16,0},{20,4},{24,8},{28,12},{1,17},{... | collective-permute-start | bytes 393224 | tf_op jit(solution)/shard_map/ppermute | solution.py:384
  55.8 5.6 %collective-permute-start.8 = (bf16[384,128]{1,0:T(8,128)(2,1)S(1)}, bf16[384,128]{1,0:T(8,128)(2,1)S(1)}, u32[]{:S(2)}, u32[]{:S(2)}) collective-permute-start(bf16[384,128]{1,0:T(8,128)(2,1)S(1)} %get-tuple-element.68), channel_id=1, source_target_pairs={{0,4},{4,0},{8,12},{12,8},{16,20},{20,16},{24,28},{28,24},{1,5},{5... | collective-permute-start | bytes 294920 | tf_op jit(solution)/shard_map/ppermute | solution.py:384
  56.5 6.2 %collective-permute-start.9 = (bf16[384,128]{1,0:T(8,128)(2,1)S(1)}, bf16[384,128]{1,0:T(8,128)(2,1)S(1)}, u32[]{:S(2)}, u32[]{:S(2)}) collective-permute-start(bf16[384,128]{1,0:T(8,128)(2,1)S(1)} %get-tuple-element.69), channel_id=1, source_target_pairs={{0,8},{4,12},{8,0},{12,4},{16,24},{20,28},{24,16},{28,20},{1,9},{5... | collective-permute-start | bytes 294920 | tf_op jit(solution)/shard_map/ppermute | solution.py:384
  58.6 7.0 %collective-permute-start.10 = (bf16[384,128]{1,0:T(8,128)(2,1)S(1)}, bf16[384,128]{1,0:T(8,128)(2,1)S(1)}, u32[]{:S(2)}, u32[]{:S(2)}) collective-permute-start(bf16[384,128]{1,0:T(8,128)(2,1)S(1)} %get-tuple-element.70), channel_id=1, source_target_pairs={{0,12},{4,8},{8,4},{12,0},{16,28},{20,24},{24,20},{28,16},{1,13},{... | collective-permute-start | bytes 294920 | tf_op jit(solution)/shard_map/ppermute | solution.py:384
  70.0 14.0 %collective-permute-start.15 = (bf16[4,256,128]{2,1,0:T(8,128)(2,1)S(1)}, bf16[4,256,128]{2,1,0:T(8,128)(2,1)S(1)}, u32[]{:S(2)}, u32[]{:S(2)}) collective-permute-start(bf16[4,256,128]{2,1,0:T(8,128)(2,1)S(1)} %get-tuple-element.85), channel_id=1, source_target_pairs={{0,16},{4,20},{8,24},{12,28},{16,0},{20,4},{24,8},{28,12},{1,17},{... | collective-permute-start | bytes 786440 | tf_op jit(solution)/shard_map/ppermute | solution.py:384
  71.3 6.5 %collective-permute-start.11 = (bf16[256,128]{1,0:T(8,128)(2,1)S(1)}, bf16[256,128]{1,0:T(8,128)(2,1)S(1)}, u32[]{:S(2)}, u32[]{:S(2)}) collective-permute-start(bf16[256,128]{1,0:T(8,128)(2,1)S(1)} %get-tuple-element.72), channel_id=1, source_target_pairs={{0,4},{4,0},{8,12},{12,8},{16,20},{20,16},{24,28},{28,24},{1,5},{5... | collective-permute-start | bytes 196616 | tf_op jit(solution)/shard_map/ppermute | solution.py:384
  72.0 6.7 %collective-permute-start.12 = (bf16[256,128]{1,0:T(8,128)(2,1)S(1)}, bf16[256,128]{1,0:T(8,128)(2,1)S(1)}, u32[]{:S(2)}, u32[]{:S(2)}) collective-permute-start(bf16[256,128]{1,0:T(8,128)(2,1)S(1)} %get-tuple-element.73), channel_id=1, source_target_pairs={{0,8},{4,12},{8,0},{12,4},{16,24},{20,28},{24,16},{28,20},{1,9},{5... | collective-permute-start | bytes 196616 | tf_op jit(solution)/shard_map/ppermute | solution.py:384
  75.2 5.9 %collective-permute-start.13 = (bf16[256,128]{1,0:T(8,128)(2,1)S(1)}, bf16[256,128]{1,0:T(8,128)(2,1)S(1)}, u32[]{:S(2)}, u32[]{:S(2)}) collective-permute-start(bf16[256,128]{1,0:T(8,128)(2,1)S(1)} %get-tuple-element.74), channel_id=1, source_target_pairs={{0,12},{4,8},{8,4},{12,0},{16,28},{20,24},{24,20},{28,16},{1,13},{... | collective-permute-start | bytes 196616 | tf_op jit(solution)/shard_map/ppermute | solution.py:384
  81.9 2.5 %collective-permute-start.14 = (bf16[2,64,2048]{2,1,0:T(8,128)(2,1)S(1)}, bf16[2,64,2048]{2,1,0:T(8,128)(2,1)S(1)}, u32[]{:S(2)}, u32[]{:S(2)}) collective-permute-start(bf16[2,64,2048]{2,1,0:T(8,128)(2,1)S(1)} %get-tuple-element.80), channel_id=1, source_target_pairs={{0,1},{1,0},{2,3},{3,2},{4,5},{5,4},{6,7},{7,6},{8,9},{9,8},{10,11... | collective-permute-start | bytes 1572872 | tf_op jit(solution)/shard_map/ppermute | solution.py:384
  84.5 12.1 %collective-permute-start.16 = (bf16[64,2048]{1,0:T(8,128)(2,1)S(1)}, bf16[64,2048]{1,0:T(8,128)(2,1)S(1)}, u32[]{:S(2)}, u32[]{:S(2)}) collective-permute-start(bf16[64,2048]{1,0:T(8,128)(2,1)S(1)} %get-tuple-element.88), channel_id=1, source_target_pairs={{0,2},{1,3},{2,0},{3,1},{4,6},{5,7},{6,4},{7,5},{8,10},{9,11},{10,... | collective-permute-start | bytes 786440 | tf_op jit(solution)/shard_map/ppermute | solution.py:384
  85.1 6.9 %collective-permute-start.17 = (bf16[3,256,128]{2,1,0:T(8,128)(2,1)S(1)}, bf16[3,256,128]{2,1,0:T(8,128)(2,1)S(1)}, u32[]{:S(2)}, u32[]{:S(2)}) collective-permute-start(bf16[3,256,128]{2,1,0:T(8,128)(2,1)S(1)} %get-tuple-element.89), channel_id=1, source_target_pairs={{0,4},{4,0},{8,12},{12,8},{16,20},{20,16},{24,28},{28,24},{1,5},{5... | collective-permute-start | bytes 589832 | tf_op jit(solution)/shard_map/ppermute | solution.py:384
  85.3 7.8 %collective-permute-start.18 = (bf16[3,256,128]{2,1,0:T(8,128)(2,1)S(1)}, bf16[3,256,128]{2,1,0:T(8,128)(2,1)S(1)}, u32[]{:S(2)}, u32[]{:S(2)}) collective-permute-start(bf16[3,256,128]{2,1,0:T(8,128)(2,1)S(1)} %get-tuple-element.90), channel_id=1, source_target_pairs={{0,8},{4,12},{8,0},{12,4},{16,24},{20,28},{24,16},{28,20},{1,9},{5... | collective-permute-start | bytes 589832 | tf_op jit(solution)/shard_map/ppermute | solution.py:384
  86.9 9.8 %collective-permute-start.19 = (bf16[3,256,128]{2,1,0:T(8,128)(2,1)S(1)}, bf16[3,256,128]{2,1,0:T(8,128)(2,1)S(1)}, u32[]{:S(2)}, u32[]{:S(2)}) collective-permute-start(bf16[3,256,128]{2,1,0:T(8,128)(2,1)S(1)} %get-tuple-element.91), channel_id=1, source_target_pairs={{0,12},{4,8},{8,4},{12,0},{16,28},{20,24},{24,20},{28,16},{1,13},{... | collective-permute-start | bytes 589832 | tf_op jit(solution)/shard_map/ppermute | solution.py:384
  (1 other events, 0.9 us)

commit v7 on v6

--- a/solution.py
+++ b/solution.py
@@ -98,10 +98,10 @@
     return pl.ds(pl.multiple_of(index * HEAD_DIM, HEAD_DIM), HEAD_DIM)
 
 
-def pack_kernel(q, k, v, out_grad, *refs):
-    outs, (out_grad_out, sems) = refs[:GROUP], refs[GROUP:]
-    me = member()
-    copies = [pltpu.make_async_copy(out_grad, out_grad_out, sems.at[0])]
+def pack_kernel(q, k, v, *refs):
+    *outs, sems = refs
+    me = member()
+    copies = []
     for step in (3, 1, 2, 0):
         for part, source in enumerate((k, v, q)):
             piece = source.at[:, columns(me ^ step)]
@@ -122,9 +122,8 @@
             out[head, part] = twice[:, head * HEAD_DIM : (head + 1) * HEAD_DIM]
 
 
-def copy_kernel(x, y, x_out, y_out):
-    x_out[...] = x[...]
-    y_out[...] = y[...]
+def copy_kernel(x, _, out):
+    out[...] = x[...]
 
 
 def gather_kernel(nb, groups, far, _, *refs):
@@ -428,19 +427,19 @@
 
     chunk = shape(rows, HEAD_DIM)
     triple = shape(3, rows, HEAD_DIM)
-    *chunks, own_grad = call(
+    chunks = call(
         pack_kernel,
-        [triple] * GROUP + [shape(*out_grad.shape)],
-        (queries, keys, values, out_grad),
-        scratch=[pltpu.SemaphoreType.DMA((1 + 3 * GROUP,))],
+        [triple] * GROUP,
+        (queries, keys, values),
+        scratch=[pltpu.SemaphoreType.DMA((3 * GROUP,))],
         space=pltpu.HBM,
-        limit=56,
-    )
-    far = swapped(own_grad, "mp", 2)
+        limit=53,
+    )
+    far = swapped(out_grad, "mp", 2)
     chunks = exchanged(chunks)
     (tops,) = call(pool_kernel, [shape(GROUP, 2, quarter, HEAD_DIM)], (keys, values))
     tops = swapped(tops, "seq", GROUP)
-    chunks[0], own_grad = call(copy_kernel, [triple, shape(*out_grad.shape)], (chunks[0], own_grad))
+    (own_grad,) = call(copy_kernel, [shape(*out_grad.shape)], (out_grad, chunks[1]))
     far, near, queries, level_1, *refs = call(
         functools.partial(gather_kernel, nb, groups),
         [

time: 98 us -> 66.3 us (0.68)
  Pallas kernels: 45.6 us -> 13.9 us
    pallas_call x13, Pallas kernels: 45.6 us -> 13.9 us  [call(): pl.pallas_call(kernel, out_shape=out_shape, in_specs=[whole] * len(args),...]
    unnamed x10 -> x8, local copies, waits for them, and re-layouts: 3.78 us -> 2.85 us
  transfers between devices with their start and end apart: 20 -> 20, of which waited for: 11 -> 11; matrix products, arithmetic and copies ran while one was open for 0% -> 0% of each run, Pallas kernels for 7% -> 12%
where the time goes in v7:
time: 66.3 us; the launch traced here: 66.1 us
  starting transfers between devices  25.5 us (38%)
  waiting for transfers between devices  23.1 us (35%)
  Pallas kernels  13.9 us (21%)
  local copies, waits for them, and re-layouts  2.85 us (4%)
  between operations  0.77 us (1%)
    ppermute x20, starting transfers between devices, swapped(): lax.ppermute(x, axis, [(i, i ^ step) for i in range(lax.axis_size(axis))])  25.5 us
    ppermute x20, waiting for transfers between devices, swapped(): lax.ppermute(x, axis, [(i, i ^ step) for i in range(lax.axis_size(axis))])  23.1 us
    pallas_call x13, Pallas kernels, call(): pl.pallas_call(kernel, out_shape=out_shape, in_specs=[whole] * len(args),...  13.9 us
    unnamed x8, local copies, waits for them, and re-layouts  2.85 us
  transfers between devices with their start and end apart: 20, of which 11 were waited for; matrix products, arithmetic and copies ran while one was open for 0% of the time, Pallas kernels for 12%

profile of v7, /device:TPU:0, one launch (start us, length us, event | category | flops | bytes accessed | tf_op | source)
XLA Modules:
  0.0 66.1 jit_solution(8699124791838552796)
XLA Ops:
  0.6 3.0 %collective-permute-start = (bf16[64,2048]{1,0:T(8,128)(2,1)}, bf16[64,2048]{1,0:T(8,128)(2,1)S(1)}, u32[]{:S(2)}, u32[]{:S(2)}) collective-permute-start(bf16[64,2048]{1,0:T(8,128)(2,1)} %x.1), channel_id=1, source_target_pairs={{0,2},{1,3},{2,0},{3,1},{4,6},{5,7},{6,4},{7,5},{8,10},{9,11},{10,... | collective-permute-start | bytes 786440 | tf_op jit(solution)/shard_map/ppermute | solution.py:383
  3.6 1.3 %shard_map.85 = (bf16[3,256,128]{2,1,0:T(8,128)(2,1)S(1)}, bf16[3,256,128]{2,1,0:T(8,128)(2,1)S(1)}, bf16[3,256,128]{2,1,0:T(8,128)(2,1)S(1)}, bf16[3,256,128]{2,1,0:T(8,128)(2,1)S(1)}) custom-call(bf16[256,512]{1,0:T(8,128)(2,1)} %q.1, bf16[256,512]{1,0:T(8,128)(2,1)} %k.3, bf16[256,512]{1,0:T(8,128)(2,1)} %v.3), custom_call_target="tpu_custom_call" | custom-call | tf_op jit(solution)/shard_map/pallas_call | solution.py:36
  4.9 1.6 %collective-permute-start.2 = (bf16[3,256,128]{2,1,0:T(8,128)(2,1)S(1)}, bf16[3,256,128]{2,1,0:T(8,128)(2,1)S(1)}, u32[]{:S(2)}, u32[]{:S(2)}) collective-permute-start(bf16[3,256,128]{2,1,0:T(8,128)(2,1)S(1)} %get-tuple-element.48), channel_id=1, source_target_pairs={{0,4},{4,0},{8,12},{12,8},{16,20},{20,16},{24,28},{28,24},{1,5},{5... | collective-permute-start | bytes 589832 | tf_op jit(solution)/shard_map/ppermute | solution.py:383
  6.5 1.6 %collective-permute-start.3 = (bf16[3,256,128]{2,1,0:T(8,128)(2,1)S(1)}, bf16[3,256,128]{2,1,0:T(8,128)(2,1)S(1)}, u32[]{:S(2)}, u32[]{:S(2)}) collective-permute-start(bf16[3,256,128]{2,1,0:T(8,128)(2,1)S(1)} %get-tuple-element.49), channel_id=1, source_target_pairs={{0,8},{4,12},{8,0},{12,4},{16,24},{20,28},{24,16},{28,20},{1,9},{5... | collective-permute-start | bytes 589832 | tf_op jit(solution)/shard_map/ppermute | solution.py:383
  10.9 2.7 %collective-permute-start.1 = (bf16[4,2,64,128]{3,2,1,0:T(8,128)(2,1)S(1)}, bf16[4,2,64,128]{3,2,1,0:T(8,128)(2,1)S(1)}, u32[]{:S(2)}, u32[]{:S(2)}) collective-permute-start(bf16[4,2,64,128]{3,2,1,0:T(8,128)(2,1)S(1)} %shard_map.84), channel_id=1, source_target_pairs={{0,16},{4,20},{8,24},{12,28},{16,0},{20,4},{24,8},{28,12},{1,17},{... | collective-permute-start | bytes 393224 | tf_op jit(solution)/shard_map/ppermute | solution.py:383
  14.6 4.1 %collective-permute-done.1._.refs_5_ = bf16[4,2,64,128]{3,2,1,0:T(8,128)(2,1)S(1)} collective-permute-done((bf16[4,2,64,128]{3,2,1,0:T(8,128)(2,1)S(1)}, bf16[4,2,64,128]{3,2,1,0:T(8,128)(2,1)S(1)}, u32[]{:S(2)}, u32[]{:S(2)}) %collective-permute-start.1) | collective-permute-done | bytes 131104 | tf_op jit(solution)/shard_map/ppermute | solution.py:383
  20.0 2.6 %collective-permute-start.7 = (bf16[2,256,128]{2,1,0:T(8,128)(2,1)S(1)}, bf16[2,256,128]{2,1,0:T(8,128)(2,1)S(1)}, u32[]{:S(2)}, u32[]{:S(2)}) collective-permute-start(bf16[2,256,128]{2,1,0:T(8,128)(2,1)S(1)} %get-tuple-element.61), channel_id=1, source_target_pairs={{0,16},{4,20},{8,24},{12,28},{16,0},{20,4},{24,8},{28,12},{1,17},{... | collective-permute-start | bytes 393224 | tf_op jit(solution)/shard_map/ppermute | solution.py:383
  24.2 2.5 %collective-permute-start.9 = (bf16[384,128]{1,0:T(8,128)(2,1)S(1)}, bf16[384,128]{1,0:T(8,128)(2,1)S(1)}, u32[]{:S(2)}, u32[]{:S(2)}) collective-permute-start(bf16[384,128]{1,0:T(8,128)(2,1)S(1)} %get-tuple-element.63), channel_id=1, source_target_pairs={{0,8},{4,12},{8,0},{12,4},{16,24},{20,28},{24,16},{28,20},{1,9},{5... | collective-permute-start | bytes 294920 | tf_op jit(solution)/shard_map/ppermute | solution.py:383
  27.0 1.7 %shard_map.89 = (bf16[3,4,256,128]{3,2,1,0:T(8,128)(2,1)S(1)}, bf16[128,1024]{1,0:T(8,128)(2,1)S(1)}, bf16[128,1024]{1,0:T(8,128)(2,1)S(1)}, bf16[128,512]{1,0:T...) custom-call(bf16[4,2,256,128]{3,2,1,0:T(8,128)(2,1)S(1)} %get-tuple-element, ...), custom_call_target="tpu_custom_call" | custom-call | flops 335544320 | bytes 6946816 | tf_op jit(solution)/shard_map/pallas_call | solution.py:36
  29.8 1.2 %collective-permute-done.9.refs_8_ = bf16[384,128]{1,0:T(8,128)(2,1)S(1)} collective-permute-done((bf16[384,128]{1,0:T(8,128)(2,1)S(1)}, bf16[384,128]{1,0:T(8,128)(2,1)S(1)}, u32[]{:S(2)}, u32[]{:S(2)}) %collective-permute-start.9) | collective-permute-done | bytes 98336 | tf_op jit(solution)/shard_map/ppermute | solution.py:383
  30.9 2.4 %collective-permute-done.10.refs_9_ = bf16[384,128]{1,0:T(8,128)(2,1)S(1)} collective-permute-done((bf16[384,128]{1,0:T(8,128)(2,1)S(1)}, bf16[384,128]{1,0:T(8,128)(2,1)S(1)}, u32[]{:S(2)}, u32[]{:S(2)}) %collective-permute-start.10) | collective-permute-done | bytes 98336 | tf_op jit(solution)/shard_map/ppermute | solution.py:383
  33.4 1.6 %shard_map.90 = (bf16[4,5,256,256]{3,2,1,0:T(8,128)(2,1)S(1)}, bf16[4,256,128]{2,1,0:T(8,128)(2,1)S(1)}, bf16[2,256,128]{2,1,0:T(8,128)(2,1)S(1)}, bf16[256,128]...) custom-call(bf16[3,4,256,128]{3,2,1,0:T(8,128)(2,1)S(1)} %get-tuple-, ...), custom_call_target="tpu_custom_call" | custom-call | flops 335544320 | bytes 9207808 | tf_op jit(solution)/shard_map/pallas_call | solution.py:36
  35.0 2.8 %shard_map.91 = (bf16[4,5,256,256]{3,2,1,0:T(8,128)(2,1)S(1)}, bf16[4,256,128]{2,1,0:T(8,128)(2,1)S(1)}) custom-call(bf16[3,4,256,128]{3,2,1,0:T(8,128)(2,1)S(1)} %get-tuple-element.56.refs_0_, bf16[4,2,256,128]{3,2,1,0:T(8,128)(2,1)S(1)} %get-tuple-element.51.near.refs_1_, bf16[2,512,128]{2,1,0:T(8,128)(2,1)S(1)} %get-tuple-element.53.level_1.refs_2_, ...), custom_call_target="tpu_custom_call" | custom-call | flops 335544320 | bytes 7602176 | tf_op jit(solution)/shard_map/pallas_call | solution.py:36
  37.9 1.5 %collective-permute-start.15 = (bf16[4,256,128]{2,1,0:T(8,128)(2,1)S(1)}, bf16[4,256,128]{2,1,0:T(8,128)(2,1)S(1)}, u32[]{:S(2)}, u32[]{:S(2)}) collective-permute-start(bf16[4,256,128]{2,1,0:T(8,128)(2,1)S(1)} %get-tuple-element.79), channel_id=1, source_target_pairs={{0,16},{4,20},{8,24},{12,28},{16,0},{20,4},{24,8},{28,12},{1,17},{... | collective-permute-start | bytes 786440 | tf_op jit(solution)/shard_map/ppermute | solution.py:383
  40.1 3.2 %collective-permute-start.12 = (bf16[256,128]{1,0:T(8,128)(2,1)S(1)}, bf16[256,128]{1,0:T(8,128)(2,1)S(1)}, u32[]{:S(2)}, u32[]{:S(2)}) collective-permute-start(bf16[256,128]{1,0:T(8,128)(2,1)S(1)} %get-tuple-element.67), channel_id=1, source_target_pairs={{0,8},{4,12},{8,0},{12,4},{16,24},{20,28},{24,16},{28,20},{1,9},{5... | collective-permute-start | bytes 196616 | tf_op jit(solution)/shard_map/ppermute | solution.py:383
  43.5 2.3 %shard_map.93 = (bf16[4,256,128]{2,1,0:T(8,128)(2,1)S(1)}, f32[2,4,256,128]{3,2,1,0:T(8,128)S(1)}) custom-call(bf16[3,4,256,128]{3,2,1,0:T(8,128)(2,1)S(1)} %get-tuple-element.56.refs_0_, bf16[128,1024]{1,0:T(8,128)(2,1)S(1)} %get-tuple-element.75.refs_1_, bf16[128,512]{1,0:T(8,128)(2,1)S(1)} %get-tuple-element.76.refs_2_, ...), custom_call_target="tpu_custom_call" | custom-call | flops 1 | bytes 8257536 | tf_op jit(solution)/shard_map/pallas_call | solution.py:36
  45.9 1.1 %collective-permute-done.12.refs_2_ = bf16[256,128]{1,0:T(8,128)(2,1)S(1)} collective-permute-done((bf16[256,128]{1,0:T(8,128)(2,1)S(1)}, bf16[256,128]{1,0:T(8,128)(2,1)S(1)}, u32[]{:S(2)}, u32[]{:S(2)}) %collective-permute-start.12) | collective-permute-done | bytes 65568 | tf_op jit(solution)/shard_map/ppermute | solution.py:383
  46.9 2.3 %collective-permute-done.13.refs_3_ = bf16[256,128]{1,0:T(8,128)(2,1)S(1)} collective-permute-done((bf16[256,128]{1,0:T(8,128)(2,1)S(1)}, bf16[256,128]{1,0:T(8,128)(2,1)S(1)}, u32[]{:S(2)}, u32[]{:S(2)}) %collective-permute-start.13) | collective-permute-done | bytes 65568 | tf_op jit(solution)/shard_map/ppermute | solution.py:383
  50.1 2.1 %collective-permute-done.15.refs_0_ = bf16[4,256,128]{2,1,0:T(8,128)(2,1)S(1)} collective-permute-done((bf16[4,256,128]{2,1,0:T(8,128)(2,1)S(1)}, bf16[4,256,128]{2,1,0:T(8,128)(2,1)S(1)}, u32[]{:S(2)}, u32[]{:S(2)}) %collective-permute-start.15) | collective-permute-done | bytes 262176 | tf_op jit(solution)/shard_map/ppermute | solution.py:383
  53.6 1.6 %collective-permute-start.18 = (bf16[3,256,128]{2,1,0:T(8,128)(2,1)S(1)}, bf16[3,256,128]{2,1,0:T(8,128)(2,1)S(1)}, u32[]{:S(2)}, u32[]{:S(2)}) collective-permute-start(bf16[3,256,128]{2,1,0:T(8,128)(2,1)S(1)} %get-tuple-element.84), channel_id=1, source_target_pairs={{0,8},{4,12},{8,0},{12,4},{16,24},{20,28},{24,16},{28,20},{1,9},{5... | collective-permute-start | bytes 589832 | tf_op jit(solution)/shard_map/ppermute | solution.py:383
  55.2 1.7 %collective-permute-start.19 = (bf16[3,256,128]{2,1,0:T(8,128)(2,1)S(1)}, bf16[3,256,128]{2,1,0:T(8,128)(2,1)S(1)}, u32[]{:S(2)}, u32[]{:S(2)}) collective-permute-start(bf16[3,256,128]{2,1,0:T(8,128)(2,1)S(1)} %get-tuple-element.85), channel_id=1, source_target_pairs={{0,12},{4,8},{8,4},{12,0},{16,28},{20,24},{24,20},{28,16},{1,13},{... | collective-permute-start | bytes 589832 | tf_op jit(solution)/shard_map/ppermute | solution.py:383
  57.0 3.4 %collective-permute-done.17.refs_3_ = bf16[3,256,128]{2,1,0:T(8,128)(2,1)S(1)} collective-permute-done((bf16[3,256,128]{2,1,0:T(8,128)(2,1)S(1)}, bf16[3,256,128]{2,1,0:T(8,128)(2,1)S(1)}, u32[]{:S(2)}, u32[]{:S(2)}) %collective-permute-start.17) | collective-permute-done | bytes 196640 | tf_op jit(solution)/shard_map/ppermute | solution.py:383
  61.4 3.5 %collective-permute-done.19.refs_5_ = bf16[3,256,128]{2,1,0:T(8,128)(2,1)S(1)} collective-permute-done((bf16[3,256,128]{2,1,0:T(8,128)(2,1)S(1)}, bf16[3,256,128]{2,1,0:T(8,128)(2,1)S(1)}, u32[]{:S(2)}, u32[]{:S(2)}) %collective-permute-start.19) | collective-permute-done | bytes 196640 | tf_op jit(solution)/shard_map/ppermute | solution.py:383
  64.9 1.1 %shard_map.96 = (bf16[256,512]{1,0:T(8,128)(2,1)}, bf16[256,512]{1,0:T(8,128)(2,1)}, bf16[256,512]{1,0:T(8,128)(2,1)}, bf16[64,2048]{1,0:T(8,128)(2,1)}) custom-call(f32[64,2048]{1,0:T(8,128)S(1)} %get-tuple-element.81.refs_0_, bf16[64,2048]{1,0:T(8,128)(2,1)S(1)} %collective-permute-done.16.refs_1_, bf16[3,256,128]{2,1,0:T(8,128)(2,1)S(1)} %get-tuple-element.80._.refs_2_, ...), custom_call_target="tpu_custom_call" | custom-call | tf_op jit(solution)/shard_map/pallas_call | solution.py:36
  (37 shorter events, 12.2 us)
Async XLA Ops:
  0.6 22.0 %copy-start = (bf16[512,2048]{1,0:T(8,128)(2,1)S(1)}, bf16[512,2048]{1,0:T(8,128)(2,1)}, u32[]{:S(2)}) copy-start(bf16[512,2048]{1,0:T(8,128)(2,1)} %refs_4_.3) | copy-start | bytes 6291460
  0.6 18.9 %collective-permute-start = (bf16[64,2048]{1,0:T(8,128)(2,1)}, bf16[64,2048]{1,0:T(8,128)(2,1)S(1)}, u32[]{:S(2)}, u32[]{:S(2)}) collective-permute-start(bf16[64,2048]{1,0:T(8,128)(2,1)} %x.1), channel_id=1, source_target_pairs={{0,2},{1,3},{2,0},{3,1},{4,6},{5,7},{6,4},{7,5},{8,10},{9,11},{10,... | collective-permute-start | bytes 786440 | tf_op jit(solution)/shard_map/ppermute | solution.py:383
  4.9 8.6 %collective-permute-start.2 = (bf16[3,256,128]{2,1,0:T(8,128)(2,1)S(1)}, bf16[3,256,128]{2,1,0:T(8,128)(2,1)S(1)}, u32[]{:S(2)}, u32[]{:S(2)}) collective-permute-start(bf16[3,256,128]{2,1,0:T(8,128)(2,1)S(1)} %get-tuple-element.48), channel_id=1, source_target_pairs={{0,4},{4,0},{8,12},{12,8},{16,20},{20,16},{24,28},{28,24},{1,5},{5... | collective-permute-start | bytes 589832 | tf_op jit(solution)/shard_map/ppermute | solution.py:383
  6.5 12.2 %collective-permute-start.3 = (bf16[3,256,128]{2,1,0:T(8,128)(2,1)S(1)}, bf16[3,256,128]{2,1,0:T(8,128)(2,1)S(1)}, u32[]{:S(2)}, u32[]{:S(2)}) collective-permute-start(bf16[3,256,128]{2,1,0:T(8,128)(2,1)S(1)} %get-tuple-element.49), channel_id=1, source_target_pairs={{0,8},{4,12},{8,0},{12,4},{16,24},{20,28},{24,16},{28,20},{1,9},{5... | collective-permute-start | bytes 589832 | tf_op jit(solution)/shard_map/ppermute | solution.py:383
  8.1 11.5 %collective-permute-start.4 = (bf16[3,256,128]{2,1,0:T(8,128)(2,1)S(1)}, bf16[3,256,128]{2,1,0:T(8,128)(2,1)S(1)}, u32[]{:S(2)}, u32[]{:S(2)}) collective-permute-start(bf16[3,256,128]{2,1,0:T(8,128)(2,1)S(1)} %get-tuple-element.50), channel_id=1, source_target_pairs={{0,12},{4,8},{8,4},{12,0},{16,28},{20,24},{24,20},{28,16},{1,13},{... | collective-permute-start | bytes 589832 | tf_op jit(solution)/shard_map/ppermute | solution.py:383
  8.5 0.9 %copy-start.1 = (bf16[256,512]{1,0:T(8,128)(2,1)S(1)}, bf16[256,512]{1,0:T(8,128)(2,1)}, u32[]{:S(2)}) copy-start(bf16[256,512]{1,0:T(8,128)(2,1)} %k.3) | copy-start | bytes 786436
  9.4 0.9 %copy-start.2 = (bf16[256,512]{1,0:T(8,128)(2,1)S(1)}, bf16[256,512]{1,0:T(8,128)(2,1)}, u32[]{:S(2)}) copy-start(bf16[256,512]{1,0:T(8,128)(2,1)} %v.3) | copy-start | bytes 786436
  10.9 7.8 %collective-permute-start.1 = (bf16[4,2,64,128]{3,2,1,0:T(8,128)(2,1)S(1)}, bf16[4,2,64,128]{3,2,1,0:T(8,128)(2,1)S(1)}, u32[]{:S(2)}, u32[]{:S(2)}) collective-permute-start(bf16[4,2,64,128]{3,2,1,0:T(8,128)(2,1)S(1)} %shard_map.84), channel_id=1, source_target_pairs={{0,16},{4,20},{8,24},{12,28},{16,0},{20,4},{24,8},{28,12},{1,17},{... | collective-permute-start | bytes 393224 | tf_op jit(solution)/shard_map/ppermute | solution.py:383
  13.6 1.0 %copy-start.3 = (bf16[64,2048]{1,0:T(8,128)(2,1)S(1)}, bf16[64,2048]{1,0:T(8,128)(2,1)}, u32[]{:S(2)}) copy-start(bf16[64,2048]{1,0:T(8,128)(2,1)} %x.1) | copy-start | bytes 786436
  14.5 8.1 %collective-permute-start.5 = (bf16[64,2048]{1,0:T(8,128)(2,1)S(1)}, bf16[64,2048]{1,0:T(8,128)(2,1)S(1)}, u32[]{:S(2)}, u32[]{:S(2)}) collective-permute-start(bf16[64,2048]{1,0:T(8,128)(2,1)S(1)} %shard_map.87.refs_0_), channel_id=1, source_target_pairs={{0,1},{1,0},{2,3},{3,2},{4,5},{5,4},{6,7},{7,6},{8,9},{9,8},{10,11... | collective-permute-start | bytes 786440 | tf_op jit(solution)/shard_map/ppermute | solution.py:383
  19.9 2.7 %collective-permute-start.6 = (bf16[64,2048]{1,0:T(8,128)(2,1)S(1)}, bf16[64,2048]{1,0:T(8,128)(2,1)S(1)}, u32[]{:S(2)}, u32[]{:S(2)}) collective-permute-start(bf16[64,2048]{1,0:T(8,128)(2,1)S(1)} %get-tuple-element.54.refs_2_), channel_id=1, source_target_pairs={{0,1},{1,0},{2,3},{3,2},{4,5},{5,4},{6,7},{7,6},{8,9},{9,8},{10,11... | collective-permute-start | bytes 786440 | tf_op jit(solution)/shard_map/ppermute | solution.py:383
  20.0 9.7 %collective-permute-start.7 = (bf16[2,256,128]{2,1,0:T(8,128)(2,1)S(1)}, bf16[2,256,128]{2,1,0:T(8,128)(2,1)S(1)}, u32[]{:S(2)}, u32[]{:S(2)}) collective-permute-start(bf16[2,256,128]{2,1,0:T(8,128)(2,1)S(1)} %get-tuple-element.61), channel_id=1, source_target_pairs={{0,16},{4,20},{8,24},{12,28},{16,0},{20,4},{24,8},{28,12},{1,17},{... | collective-permute-start | bytes 393224 | tf_op jit(solution)/shard_map/ppermute | solution.py:383
  23.5 6.3 %collective-permute-start.8 = (bf16[384,128]{1,0:T(8,128)(2,1)S(1)}, bf16[384,128]{1,0:T(8,128)(2,1)S(1)}, u32[]{:S(2)}, u32[]{:S(2)}) collective-permute-start(bf16[384,128]{1,0:T(8,128)(2,1)S(1)} %get-tuple-element.62), channel_id=1, source_target_pairs={{0,4},{4,0},{8,12},{12,8},{16,20},{20,16},{24,28},{28,24},{1,5},{5... | collective-permute-start | bytes 294920 | tf_op jit(solution)/shard_map/ppermute | solution.py:383
  24.2 6.8 %collective-permute-start.9 = (bf16[384,128]{1,0:T(8,128)(2,1)S(1)}, bf16[384,128]{1,0:T(8,128)(2,1)S(1)}, u32[]{:S(2)}, u32[]{:S(2)}) collective-permute-start(bf16[384,128]{1,0:T(8,128)(2,1)S(1)} %get-tuple-element.63), channel_id=1, source_target_pairs={{0,8},{4,12},{8,0},{12,4},{16,24},{20,28},{24,16},{28,20},{1,9},{5... | collective-permute-start | bytes 294920 | tf_op jit(solution)/shard_map/ppermute | solution.py:383
  26.7 6.7 %collective-permute-start.10 = (bf16[384,128]{1,0:T(8,128)(2,1)S(1)}, bf16[384,128]{1,0:T(8,128)(2,1)S(1)}, u32[]{:S(2)}, u32[]{:S(2)}) collective-permute-start(bf16[384,128]{1,0:T(8,128)(2,1)S(1)} %get-tuple-element.64), channel_id=1, source_target_pairs={{0,12},{4,8},{8,4},{12,0},{16,28},{20,24},{24,20},{28,16},{1,13},{... | collective-permute-start | bytes 294920 | tf_op jit(solution)/shard_map/ppermute | solution.py:383
  37.9 14.4 %collective-permute-start.15 = (bf16[4,256,128]{2,1,0:T(8,128)(2,1)S(1)}, bf16[4,256,128]{2,1,0:T(8,128)(2,1)S(1)}, u32[]{:S(2)}, u32[]{:S(2)}) collective-permute-start(bf16[4,256,128]{2,1,0:T(8,128)(2,1)S(1)} %get-tuple-element.79), channel_id=1, source_target_pairs={{0,16},{4,20},{8,24},{12,28},{16,0},{20,4},{24,8},{28,12},{1,17},{... | collective-permute-start | bytes 786440 | tf_op jit(solution)/shard_map/ppermute | solution.py:383
  39.4 6.5 %collective-permute-start.11 = (bf16[256,128]{1,0:T(8,128)(2,1)S(1)}, bf16[256,128]{1,0:T(8,128)(2,1)S(1)}, u32[]{:S(2)}, u32[]{:S(2)}) collective-permute-start(bf16[256,128]{1,0:T(8,128)(2,1)S(1)} %get-tuple-element.66), channel_id=1, source_target_pairs={{0,4},{4,0},{8,12},{12,8},{16,20},{20,16},{24,28},{28,24},{1,5},{5... | collective-permute-start | bytes 196616 | tf_op jit(solution)/shard_map/ppermute | solution.py:383
  40.1 6.8 %collective-permute-start.12 = (bf16[256,128]{1,0:T(8,128)(2,1)S(1)}, bf16[256,128]{1,0:T(8,128)(2,1)S(1)}, u32[]{:S(2)}, u32[]{:S(2)}) collective-permute-start(bf16[256,128]{1,0:T(8,128)(2,1)S(1)} %get-tuple-element.67), channel_id=1, source_target_pairs={{0,8},{4,12},{8,0},{12,4},{16,24},{20,28},{24,16},{28,20},{1,9},{5... | collective-permute-start | bytes 196616 | tf_op jit(solution)/shard_map/ppermute | solution.py:383
  43.3 5.9 %collective-permute-start.13 = (bf16[256,128]{1,0:T(8,128)(2,1)S(1)}, bf16[256,128]{1,0:T(8,128)(2,1)S(1)}, u32[]{:S(2)}, u32[]{:S(2)}) collective-permute-start(bf16[256,128]{1,0:T(8,128)(2,1)S(1)} %get-tuple-element.68), channel_id=1, source_target_pairs={{0,12},{4,8},{8,4},{12,0},{16,28},{20,24},{24,20},{28,16},{1,13},{... | collective-permute-start | bytes 196616 | tf_op jit(solution)/shard_map/ppermute | solution.py:383
  50.0 2.6 %collective-permute-start.14 = (bf16[2,64,2048]{2,1,0:T(8,128)(2,1)S(1)}, bf16[2,64,2048]{2,1,0:T(8,128)(2,1)S(1)}, u32[]{:S(2)}, u32[]{:S(2)}) collective-permute-start(bf16[2,64,2048]{2,1,0:T(8,128)(2,1)S(1)} %get-tuple-element.74), channel_id=1, source_target_pairs={{0,1},{1,0},{2,3},{3,2},{4,5},{5,4},{6,7},{7,6},{8,9},{9,8},{10,11... | collective-permute-start | bytes 1572872 | tf_op jit(solution)/shard_map/ppermute | solution.py:383
  52.7 12.2 %collective-permute-start.16 = (bf16[64,2048]{1,0:T(8,128)(2,1)S(1)}, bf16[64,2048]{1,0:T(8,128)(2,1)S(1)}, u32[]{:S(2)}, u32[]{:S(2)}) collective-permute-start(bf16[64,2048]{1,0:T(8,128)(2,1)S(1)} %get-tuple-element.82), channel_id=1, source_target_pairs={{0,2},{1,3},{2,0},{3,1},{4,6},{5,7},{6,4},{7,5},{8,10},{9,11},{10,... | collective-permute-start | bytes 786440 | tf_op jit(solution)/shard_map/ppermute | solution.py:383
  53.5 6.9 %collective-permute-start.17 = (bf16[3,256,128]{2,1,0:T(8,128)(2,1)S(1)}, bf16[3,256,128]{2,1,0:T(8,128)(2,1)S(1)}, u32[]{:S(2)}, u32[]{:S(2)}) collective-permute-start(bf16[3,256,128]{2,1,0:T(8,128)(2,1)S(1)} %get-tuple-element.83), channel_id=1, source_target_pairs={{0,4},{4,0},{8,12},{12,8},{16,20},{20,16},{24,28},{28,24},{1,5},{5... | collective-permute-start | bytes 589832 | tf_op jit(solution)/shard_map/ppermute | solution.py:383
  53.6 7.8 %collective-permute-start.18 = (bf16[3,256,128]{2,1,0:T(8,128)(2,1)S(1)}, bf16[3,256,128]{2,1,0:T(8,128)(2,1)S(1)}, u32[]{:S(2)}, u32[]{:S(2)}) collective-permute-start(bf16[3,256,128]{2,1,0:T(8,128)(2,1)S(1)} %get-tuple-element.84), channel_id=1, source_target_pairs={{0,8},{4,12},{8,0},{12,4},{16,24},{20,28},{24,16},{28,20},{1,9},{5... | collective-permute-start | bytes 589832 | tf_op jit(solution)/shard_map/ppermute | solution.py:383
  55.2 9.7 %collective-permute-start.19 = (bf16[3,256,128]{2,1,0:T(8,128)(2,1)S(1)}, bf16[3,256,128]{2,1,0:T(8,128)(2,1)S(1)}, u32[]{:S(2)}, u32[]{:S(2)}) collective-permute-start(bf16[3,256,128]{2,1,0:T(8,128)(2,1)S(1)} %get-tuple-element.85), channel_id=1, source_target_pairs={{0,12},{4,8},{8,4},{12,0},{16,28},{20,24},{24,20},{28,16},{1,13},{... | collective-permute-start | bytes 589832 | tf_op jit(solution)/shard_map/ppermute | solution.py:383

commit v8 on v7

--- a/solution.py
+++ b/solution.py
@@ -199,7 +199,10 @@
 def forward_kernel(nb, groups, *refs):
     (query, v_t, v1_t, weights, stats), refs = refs[:5], refs[5:]
     (rim_low, rim_high), refs = from_beside(groups, refs)
-    chunks, (prob, grads, top_2, *outs, attended) = refs[:GROUP], refs[GROUP:]
+    chunks, refs = refs[:GROUP], refs[GROUP:]
+    (prob, grads, top_2, deltas, far_shift), refs = refs[:5], refs[5:]
+    outs, (*rim_outs, attended, sums, rim_sums) = refs[:GROUP], refs[GROUP:]
+    ones = jnp.ones((8, HEAD_DIM), BF16)
     present = rim_present(groups)
     me = member()
     quarter = BLOCK // 4
@@ -238,40 +241,25 @@
         for side, weight in zip(sides, fresh):
             prob[b, side] = (weight * inverse).astype(BF16)
             context = context + dot((rim_high if side else rim_low)[1].T, prob[b, side])
-        attended[b] = context.T.astype(BF16)
+        context = context.T
+        attended[b] = context.astype(BF16)
+        high, low = halves(grads[b].astype(F32) * context)
+        deltas[b] = dot_nt(ones, high) + dot_nt(ones, low)
     for step, out in enumerate(outs):
         out[...] = attended[me ^ step]
-
-
-def slope_kernel(nb, groups, *refs):
-    (query, near, level_1, prob, grads, top_2), refs = refs[:6], refs[6:]
-    (rim_low, rim_high), (shift, *rim_outs, sums, rim_sums) = from_beside(groups, refs)
     for b in range(nb):
-        grad = grads[b]
-        slopes = []
-        for side in range(3):
-            if side in near_sides(b, nb):
-                value = near[b + side - 1, 1]
-            else:
-                value = (rim_high if side else rim_low)[1]
-            slopes.append(dot_nt(value, grad))
-        slopes.append(dot_nt(level_1[1, at_block(sibling(b))], grad))
-        slopes.append(dot_nt(top_2[1], grad))
-        delta = 0.0
-        for part, slope in enumerate(slopes):
-            delta = delta + (prob[b, part].astype(F32) * slope).sum(0, keepdims=True)
-        for part, slope in enumerate(slopes):
-            shift[b, part] = (prob[b, part].astype(F32) * (slope - delta)).astype(BF16)
+        grad, delta = grads[b], deltas[b, :1]
+        shift = (prob[b, 4].astype(F32) * (dot_nt(top_2[1], grad) - delta)).astype(BF16)
+        far_shift[b, 0] = shift
+        key, value = SCALE * dot(shift, query[2, b]), dot(prob[b, 4], grad)
+        sums[0], sums[1] = (key, value) if b == 0 else (key + sums[0], value + sums[1])
         for side in rim_sides(b, nb):
-            rim_sums[side // 2, 0] = SCALE * dot(shift[b, side], query[0, b])
+            slope = dot_nt((rim_high if side else rim_low)[1], grad)
+            shift = (prob[b, side].astype(F32) * (slope - delta)).astype(BF16)
+            far_shift[b, 1] = shift
+            rim_sums[side // 2, 0] = SCALE * dot(shift, query[0, b])
             rim_sums[side // 2, 1] = dot(prob[b, side], grad)
-        key, value = SCALE * dot(shift[b, 4], query[2, b]), dot(prob[b, 4], grad)
-        if b:
-            key, value = key + sums[0], value + sums[1]
-        if b < nb - 1:
-            sums[0], sums[1] = key, value
-        else:
-            rim_outs[0][0], rim_outs[0][1] = key.astype(BF16), value.astype(BF16)
+    rim_outs[0][:2] = sums[...].astype(BF16)
     low, high = rim_sums[0], rim_sums[1]
     if groups == 2:
         upper = lax.axis_index("seq") >= GROUP
@@ -282,21 +270,28 @@
 
 
 def backward_kernel(nb, groups, *refs):
-    (query, k_t, k1_t, prob, shift, grads, top_2), refs = refs[:7], refs[7:]
+    (query, near, level_1, k_t, k1_t, prob, grads, top_2, deltas, far_shift), refs = refs[:10], refs[10:]
     (rim_low, rim_high), refs = from_beside(groups, refs)
-    grad_q, grad_kv, sums_1 = refs
+    grad_q, grad_kv, shift, sums_1 = refs
     k2_t = top_2[0].T
     even_1, even_2 = averaging(1), averaging(2)
     for b in range(nb):
+        grad, delta = grads[b], deltas[b, :1]
         grad_t = 0.0
         for side in range(3):
             if side in near_sides(b, nb):
-                key_t = k_t[:, at_block(b + side - 1)]
+                slope = dot_nt(near[b + side - 1, 1], grad)
+                part = (prob[b, side].astype(F32) * (slope - delta)).astype(BF16)
+                shift[b, side] = part
+                grad_t = grad_t + dot(k_t[:, at_block(b + side - 1)], part)
             else:
-                key_t = (rim_high if side else rim_low)[0].T
-            grad_t = grad_t + dot(key_t, shift[b, side])
-        for spread, key_t, part in ((even_1, k1_t[:, at_block(sibling(b))], 3), (even_2, k2_t, 4)):
-            high, low = halves(dot(key_t, shift[b, part]))
+                grad_t = grad_t + dot((rim_high if side else rim_low)[0].T, far_shift[b, 1])
+        slope = dot_nt(level_1[1, at_block(sibling(b))], grad)
+        part = (prob[b, 3].astype(F32) * (slope - delta)).astype(BF16)
+        shift[b, 3] = part
+        coarse = ((even_1, k1_t[:, at_block(sibling(b))], part), (even_2, k2_t, far_shift[b, 0]))
+        for spread, key_t, part in coarse:
+            high, low = halves(dot(key_t, part))
             grad_t = grad_t + (dot(high, spread) + dot(low, spread))
         grad_q[b] = (SCALE * grad_t).T.astype(BF16)
     for c in range(nb // 2):
@@ -474,27 +469,31 @@
         flops=score_flops,
     )
     grad_chunks = exchanged(grad_chunks)
-    prob, grads, top_2, *attended = call(
+    stat = shape(nb, 8, BLOCK, dtype=F32)
+    prob, grads, top_2, deltas, far_shift, *refs = call(
         functools.partial(forward_kernel, nb, groups),
-        [shape(nb, 5, BLOCK, BLOCK), in_order, block] + [chunk] * GROUP,
+        [shape(nb, 5, BLOCK, BLOCK), in_order, block, stat, shape(nb, 2, BLOCK, BLOCK)]
+        + [chunk] * GROUP
+        + sent,
         (query, v_t, v1_t, weights, stats, *rim_blocks, *grad_chunks),
-        scratch=[pltpu.VMEM((nb, rows, HEAD_DIM), BF16)],
+        scratch=[
+            pltpu.VMEM((nb, rows, HEAD_DIM), BF16),
+            pltpu.VMEM((2, BLOCK, HEAD_DIM), F32),
+            pltpu.VMEM((2, 2, BLOCK, HEAD_DIM), F32),
+        ],
         flops=score_flops,
     )
-    attended = exchanged(attended)
-    shift, *rim_grads = call(
-        functools.partial(slope_kernel, nb, groups),
-        [shape(nb, 5, BLOCK, BLOCK)] + sent,
-        (query, near, level_1, prob, grads, top_2, *rim_blocks),
-        scratch=[pltpu.VMEM((2, BLOCK, HEAD_DIM), F32), pltpu.VMEM((2, 2, BLOCK, HEAD_DIM), F32)],
-        flops=score_flops,
-    )
+    attended = exchanged(refs[:GROUP])
+    rim_grads = refs[GROUP:]
     other_grads = crossed(rim_grads)
     grad_q, grad_kv = call(
         functools.partial(backward_kernel, nb, groups),
         [in_order, shape(2, nb, rows, HEAD_DIM, dtype=F32)],
-        (query, k_t, k1_t, prob, shift, grads, top_2, *rim_blocks),
-        scratch=[pltpu.VMEM((2, tokens // 2, HEAD_DIM), F32)],
+        (query, near, level_1, k_t, k1_t, prob, grads, top_2, deltas, far_shift, *rim_blocks),
+        scratch=[
+            pltpu.VMEM((nb, 4, BLOCK, BLOCK), BF16),
+            pltpu.VMEM((2, tokens // 2, HEAD_DIM), F32),
+        ],
         flops=1,
     )
     local = rows // N_MP
@@ -502,7 +501,7 @@
     kept, given = call(
         project_kernel,
         [shares] * 2,
-        (*attended, out_weight, shift),
+        (*attended, out_weight, grad_q),
         scratch=[pltpu.VMEM((rows, width), BF16), pltpu.VMEM((rows, model), BF16)],
         flops=weight_flops,
     )

time: 66.3 us -> 66.5 us (level)
  Pallas kernels: 13.9 us -> 15.1 us
  waiting for transfers between devices: 23.1 us -> 22 us
    pallas_call x13 -> x12, Pallas kernels: 13.9 us -> 15.1 us  [call(): pl.pallas_call(kernel, out_shape=out_shape, in_specs=[whole] * len(args),...]
    ppermute x20, waiting for transfers between devices: 23.1 us -> 22 us  [swapped(): lax.ppermute(x, axis, [(i, i ^ step) for i in range(lax.axis_size(axis))])]
  transfers between devices with their start and end apart: 20 -> 20, of which waited for: 11 -> 10; matrix products, arithmetic and copies ran while one was open for 0% -> 0% of each run, Pallas kernels for 12% -> 14%
where the time goes in v8:
time: 66.5 us; the launch traced here: 66.2 us
  starting transfers between devices  25.5 us (38%)
  waiting for transfers between devices  22 us (33%)
  Pallas kernels  15.1 us (23%)
  local copies, waits for them, and re-layouts  2.85 us (4%)
  between operations  0.77 us (1%)
    ppermute x20, starting transfers between devices, swapped(): lax.ppermute(x, axis, [(i, i ^ step) for i in range(lax.axis_size(axis))])  25.5 us
    ppermute x20, waiting for transfers between devices, swapped(): lax.ppermute(x, axis, [(i, i ^ step) for i in range(lax.axis_size(axis))])  22 us
    pallas_call x12, Pallas kernels, call(): pl.pallas_call(kernel, out_shape=out_shape, in_specs=[whole] * len(args),...  15.1 us
    unnamed x8, local copies, waits for them, and re-layouts  2.85 us
  transfers between devices with their start and end apart: 20, of which 10 were waited for; matrix products, arithmetic and copies ran while one was open for 0% of the time, Pallas kernels for 14%

profile of v8, /device:TPU:0, one launch (start us, length us, event | category | flops | bytes accessed | tf_op | source)
XLA Modules:
  0.0 66.2 jit_solution(6259160613430612532)
XLA Ops:
  0.6 3.0 %collective-permute-start = (bf16[64,2048]{1,0:T(8,128)(2,1)}, bf16[64,2048]{1,0:T(8,128)(2,1)S(1)}, u32[]{:S(2)}, u32[]{:S(2)}) collective-permute-start(bf16[64,2048]{1,0:T(8,128)(2,1)} %x.1), channel_id=1, source_target_pairs={{0,2},{1,3},{2,0},{3,1},{4,6},{5,7},{6,4},{7,5},{8,10},{9,11},{10,... | collective-permute-start | bytes 786440 | tf_op jit(solution)/shard_map/ppermute | solution.py:378
  3.6 1.3 %shard_map.85 = (bf16[3,256,128]{2,1,0:T(8,128)(2,1)S(1)}, bf16[3,256,128]{2,1,0:T(8,128)(2,1)S(1)}, bf16[3,256,128]{2,1,0:T(8,128)(2,1)S(1)}, bf16[3,256,128]{2,1,0:T(8,128)(2,1)S(1)}) custom-call(bf16[256,512]{1,0:T(8,128)(2,1)} %q.1, bf16[256,512]{1,0:T(8,128)(2,1)} %k.3, bf16[256,512]{1,0:T(8,128)(2,1)} %v.3), custom_call_target="tpu_custom_call" | custom-call | tf_op jit(solution)/shard_map/pallas_call | solution.py:36
  4.9 1.6 %collective-permute-start.2 = (bf16[3,256,128]{2,1,0:T(8,128)(2,1)S(1)}, bf16[3,256,128]{2,1,0:T(8,128)(2,1)S(1)}, u32[]{:S(2)}, u32[]{:S(2)}) collective-permute-start(bf16[3,256,128]{2,1,0:T(8,128)(2,1)S(1)} %get-tuple-element.49), channel_id=1, source_target_pairs={{0,4},{4,0},{8,12},{12,8},{16,20},{20,16},{24,28},{28,24},{1,5},{5... | collective-permute-start | bytes 589832 | tf_op jit(solution)/shard_map/ppermute | solution.py:378
  6.5 1.6 %collective-permute-start.3 = (bf16[3,256,128]{2,1,0:T(8,128)(2,1)S(1)}, bf16[3,256,128]{2,1,0:T(8,128)(2,1)S(1)}, u32[]{:S(2)}, u32[]{:S(2)}) collective-permute-start(bf16[3,256,128]{2,1,0:T(8,128)(2,1)S(1)} %get-tuple-element.50), channel_id=1, source_target_pairs={{0,8},{4,12},{8,0},{12,4},{16,24},{20,28},{24,16},{28,20},{1,9},{5... | collective-permute-start | bytes 589832 | tf_op jit(solution)/shard_map/ppermute | solution.py:378
  10.9 2.7 %collective-permute-start.1 = (bf16[4,2,64,128]{3,2,1,0:T(8,128)(2,1)S(1)}, bf16[4,2,64,128]{3,2,1,0:T(8,128)(2,1)S(1)}, u32[]{:S(2)}, u32[]{:S(2)}) collective-permute-start(bf16[4,2,64,128]{3,2,1,0:T(8,128)(2,1)S(1)} %shard_map.84), channel_id=1, source_target_pairs={{0,16},{4,20},{8,24},{12,28},{16,0},{20,4},{24,8},{28,12},{1,17},{... | collective-permute-start | bytes 393224 | tf_op jit(solution)/shard_map/ppermute | solution.py:378
  14.6 4.1 %collective-permute-done.1._.refs_5_ = bf16[4,2,64,128]{3,2,1,0:T(8,128)(2,1)S(1)} collective-permute-done((bf16[4,2,64,128]{3,2,1,0:T(8,128)(2,1)S(1)}, bf16[4,2,64,128]{3,2,1,0:T(8,128)(2,1)S(1)}, u32[]{:S(2)}, u32[]{:S(2)}) %collective-permute-start.1) | collective-permute-done | bytes 131104 | tf_op jit(solution)/shard_map/ppermute | solution.py:378
  20.0 2.6 %collective-permute-start.7 = (bf16[2,256,128]{2,1,0:T(8,128)(2,1)S(1)}, bf16[2,256,128]{2,1,0:T(8,128)(2,1)S(1)}, u32[]{:S(2)}, u32[]{:S(2)}) collective-permute-start(bf16[2,256,128]{2,1,0:T(8,128)(2,1)S(1)} %get-tuple-element.62), channel_id=1, source_target_pairs={{0,16},{4,20},{8,24},{12,28},{16,0},{20,4},{24,8},{28,12},{1,17},{... | collective-permute-start | bytes 393224 | tf_op jit(solution)/shard_map/ppermute | solution.py:378
  24.2 2.5 %collective-permute-start.9 = (bf16[384,128]{1,0:T(8,128)(2,1)S(1)}, bf16[384,128]{1,0:T(8,128)(2,1)S(1)}, u32[]{:S(2)}, u32[]{:S(2)}) collective-permute-start(bf16[384,128]{1,0:T(8,128)(2,1)S(1)} %get-tuple-element.64), channel_id=1, source_target_pairs={{0,8},{4,12},{8,0},{12,4},{16,24},{20,28},{24,16},{28,20},{1,9},{5... | collective-permute-start | bytes 294920 | tf_op jit(solution)/shard_map/ppermute | solution.py:378
  27.0 1.7 %shard_map.89 = (bf16[3,4,256,128]{3,2,1,0:T(8,128)(2,1)S(1)}, bf16[128,1024]{1,0:T(8,128)(2,1)S(1)}, bf16[128,1024]{1,0:T(8,128)(2,1)S(1)}, bf16[128,512]{1,0:T...) custom-call(bf16[4,2,256,128]{3,2,1,0:T(8,128)(2,1)S(1)} %get-tuple-element, ...), custom_call_target="tpu_custom_call" | custom-call | flops 335544320 | bytes 6946816 | tf_op jit(solution)/shard_map/pallas_call | solution.py:36
  28.7 1.1 %collective-permute-done.7.refs_5_.refs_10_ = bf16[2,256,128]{2,1,0:T(8,128)(2,1)S(1)} collective-permute-done((bf16[2,256,128]{2,1,0:T(8,128)(2,1)S(1)}, bf16[2,256,128]{2,1,0:T(8,128)(2,1)S(1)}, u32[]{:S(2)}, u32[]{:S(2)}) %collective-permute-start.7) | collective-permute-done | bytes 131104 | tf_op jit(solution)/shard_map/ppermute | solution.py:378
  29.8 1.2 %collective-permute-done.9.refs_8_ = bf16[384,128]{1,0:T(8,128)(2,1)S(1)} collective-permute-done((bf16[384,128]{1,0:T(8,128)(2,1)S(1)}, bf16[384,128]{1,0:T(8,128)(2,1)S(1)}, u32[]{:S(2)}, u32[]{:S(2)}) %collective-permute-start.9) | collective-permute-done | bytes 98336 | tf_op jit(solution)/shard_map/ppermute | solution.py:378
  30.9 2.4 %collective-permute-done.10.refs_9_ = bf16[384,128]{1,0:T(8,128)(2,1)S(1)} collective-permute-done((bf16[384,128]{1,0:T(8,128)(2,1)S(1)}, bf16[384,128]{1,0:T(8,128)(2,1)S(1)}, u32[]{:S(2)}, u32[]{:S(2)}) %collective-permute-start.10) | collective-permute-done | bytes 98336 | tf_op jit(solution)/shard_map/ppermute | solution.py:378
  33.4 4.6 %shard_map.90 = (bf16[4,5,256,256]{3,2,1,0:T(8,128)(2,1)S(1)}, bf16[4,256,128]{2,1,0:T(8,128)(2,1)S(1)}, bf16[2,256,128]{2,1,0:T(8,128)(2,1)S(1)}, f32[4,8,256]{...) custom-call(bf16[3,4,256,128]{3,2,1,0:T(8,128)(2,1)S(1)} %get-tuple-, ...), custom_call_target="tpu_custom_call" | custom-call | flops 335544320 | bytes 10551296 | tf_op jit(solution)/shard_map/pallas_call | solution.py:36
  38.0 1.5 %collective-permute-start.15 = (bf16[4,256,128]{2,1,0:T(8,128)(2,1)S(1)}, bf16[4,256,128]{2,1,0:T(8,128)(2,1)S(1)}, u32[]{:S(2)}, u32[]{:S(2)}) collective-permute-start(bf16[4,256,128]{2,1,0:T(8,128)(2,1)S(1)} %get-tuple-element.81), channel_id=1, source_target_pairs={{0,16},{4,20},{8,24},{12,28},{16,0},{20,4},{24,8},{28,12},{1,17},{... | collective-permute-start | bytes 786440 | tf_op jit(solution)/shard_map/ppermute | solution.py:378
  40.2 3.2 %collective-permute-start.12 = (bf16[256,128]{1,0:T(8,128)(2,1)S(1)}, bf16[256,128]{1,0:T(8,128)(2,1)S(1)}, u32[]{:S(2)}, u32[]{:S(2)}) collective-permute-start(bf16[256,128]{1,0:T(8,128)(2,1)S(1)} %get-tuple-element.68), channel_id=1, source_target_pairs={{0,8},{4,12},{8,0},{12,4},{16,24},{20,28},{24,16},{28,20},{1,9},{5... | collective-permute-start | bytes 196616 | tf_op jit(solution)/shard_map/ppermute | solution.py:378
  43.6 3.5 %shard_map.91 = (bf16[4,256,128]{2,1,0:T(8,128)(2,1)S(1)}, f32[2,4,256,128]{3,2,1,0:T(8,128)S(1)}) custom-call(bf16[3,4,256,128]{3,2,1,0:T(8,128)(2,1)S(1)} %get-tuple-element.57.refs_0_, bf16[4,2,256,128]{3,2,1,0:T(8,128)(2,1)S(1)} %get-tuple-element.52.near.refs_1_, bf16[2,512,128]{2,1,0:T(8,128)(2,1)S(1)} %get-tuple-element.54.level_1.refs_2_, ...), custom_call_target="tpu_custom_call" | custom-call | flops 1 | bytes 7503872 | tf_op jit(solution)/shard_map/pallas_call | solution.py:36
  47.1 2.2 %collective-permute-done.13.refs_3_ = bf16[256,128]{1,0:T(8,128)(2,1)S(1)} collective-permute-done((bf16[256,128]{1,0:T(8,128)(2,1)S(1)}, bf16[256,128]{1,0:T(8,128)(2,1)S(1)}, u32[]{:S(2)}, u32[]{:S(2)}) %collective-permute-start.13) | collective-permute-done | bytes 65568 | tf_op jit(solution)/shard_map/ppermute | solution.py:378
  50.2 2.1 %collective-permute-done.15.refs_0_ = bf16[4,256,128]{2,1,0:T(8,128)(2,1)S(1)} collective-permute-done((bf16[4,256,128]{2,1,0:T(8,128)(2,1)S(1)}, bf16[4,256,128]{2,1,0:T(8,128)(2,1)S(1)}, u32[]{:S(2)}, u32[]{:S(2)}) %collective-permute-start.15) | collective-permute-done | bytes 262176 | tf_op jit(solution)/shard_map/ppermute | solution.py:378
  53.7 1.7 %collective-permute-start.18 = (bf16[3,256,128]{2,1,0:T(8,128)(2,1)S(1)}, bf16[3,256,128]{2,1,0:T(8,128)(2,1)S(1)}, u32[]{:S(2)}, u32[]{:S(2)}) collective-permute-start(bf16[3,256,128]{2,1,0:T(8,128)(2,1)S(1)} %get-tuple-element.86), channel_id=1, source_target_pairs={{0,8},{4,12},{8,0},{12,4},{16,24},{20,28},{24,16},{28,20},{1,9},{5... | collective-permute-start | bytes 589832 | tf_op jit(solution)/shard_map/ppermute | solution.py:378
  55.3 1.7 %collective-permute-start.19 = (bf16[3,256,128]{2,1,0:T(8,128)(2,1)S(1)}, bf16[3,256,128]{2,1,0:T(8,128)(2,1)S(1)}, u32[]{:S(2)}, u32[]{:S(2)}) collective-permute-start(bf16[3,256,128]{2,1,0:T(8,128)(2,1)S(1)} %get-tuple-element.87), channel_id=1, source_target_pairs={{0,12},{4,8},{8,4},{12,0},{16,28},{20,24},{24,20},{28,16},{1,13},{... | collective-permute-start | bytes 589832 | tf_op jit(solution)/shard_map/ppermute | solution.py:378
  57.1 3.4 %collective-permute-done.17.refs_3_ = bf16[3,256,128]{2,1,0:T(8,128)(2,1)S(1)} collective-permute-done((bf16[3,256,128]{2,1,0:T(8,128)(2,1)S(1)}, bf16[3,256,128]{2,1,0:T(8,128)(2,1)S(1)}, u32[]{:S(2)}, u32[]{:S(2)}) %collective-permute-start.17) | collective-permute-done | bytes 196640 | tf_op jit(solution)/shard_map/ppermute | solution.py:378
  60.5 1.0 %collective-permute-done.18.refs_4_ = bf16[3,256,128]{2,1,0:T(8,128)(2,1)S(1)} collective-permute-done((bf16[3,256,128]{2,1,0:T(8,128)(2,1)S(1)}, bf16[3,256,128]{2,1,0:T(8,128)(2,1)S(1)}, u32[]{:S(2)}, u32[]{:S(2)}) %collective-permute-start.18) | collective-permute-done | bytes 196640 | tf_op jit(solution)/shard_map/ppermute | solution.py:378
  61.5 3.5 %collective-permute-done.19.refs_5_ = bf16[3,256,128]{2,1,0:T(8,128)(2,1)S(1)} collective-permute-done((bf16[3,256,128]{2,1,0:T(8,128)(2,1)S(1)}, bf16[3,256,128]{2,1,0:T(8,128)(2,1)S(1)}, u32[]{:S(2)}, u32[]{:S(2)}) %collective-permute-start.19) | collective-permute-done | bytes 196640 | tf_op jit(solution)/shard_map/ppermute | solution.py:378
  65.0 1.1 %shard_map.95 = (bf16[256,512]{1,0:T(8,128)(2,1)}, bf16[256,512]{1,0:T(8,128)(2,1)}, bf16[256,512]{1,0:T(8,128)(2,1)}, bf16[64,2048]{1,0:T(8,128)(2,1)}) custom-call(f32[64,2048]{1,0:T(8,128)S(1)} %get-tuple-element.83.refs_0_, bf16[64,2048]{1,0:T(8,128)(2,1)S(1)} %collective-permute-done.16.refs_1_, bf16[3,256,128]{2,1,0:T(8,128)(2,1)S(1)} %get-tuple-element.82._.refs_2_, ...), custom_call_target="tpu_custom_call" | custom-call | tf_op jit(solution)/shard_map/pallas_call | solution.py:36
  (36 shorter events, 10.1 us)
Async XLA Ops:
  0.6 22.0 %copy-start = (bf16[512,2048]{1,0:T(8,128)(2,1)S(1)}, bf16[512,2048]{1,0:T(8,128)(2,1)}, u32[]{:S(2)}) copy-start(bf16[512,2048]{1,0:T(8,128)(2,1)} %refs_4_.3) | copy-start | bytes 6291460
  0.6 18.9 %collective-permute-start = (bf16[64,2048]{1,0:T(8,128)(2,1)}, bf16[64,2048]{1,0:T(8,128)(2,1)S(1)}, u32[]{:S(2)}, u32[]{:S(2)}) collective-permute-start(bf16[64,2048]{1,0:T(8,128)(2,1)} %x.1), channel_id=1, source_target_pairs={{0,2},{1,3},{2,0},{3,1},{4,6},{5,7},{6,4},{7,5},{8,10},{9,11},{10,... | collective-permute-start | bytes 786440 | tf_op jit(solution)/shard_map/ppermute | solution.py:378
  4.9 8.6 %collective-permute-start.2 = (bf16[3,256,128]{2,1,0:T(8,128)(2,1)S(1)}, bf16[3,256,128]{2,1,0:T(8,128)(2,1)S(1)}, u32[]{:S(2)}, u32[]{:S(2)}) collective-permute-start(bf16[3,256,128]{2,1,0:T(8,128)(2,1)S(1)} %get-tuple-element.49), channel_id=1, source_target_pairs={{0,4},{4,0},{8,12},{12,8},{16,20},{20,16},{24,28},{28,24},{1,5},{5... | collective-permute-start | bytes 589832 | tf_op jit(solution)/shard_map/ppermute | solution.py:378
  6.5 12.2 %collective-permute-start.3 = (bf16[3,256,128]{2,1,0:T(8,128)(2,1)S(1)}, bf16[3,256,128]{2,1,0:T(8,128)(2,1)S(1)}, u32[]{:S(2)}, u32[]{:S(2)}) collective-permute-start(bf16[3,256,128]{2,1,0:T(8,128)(2,1)S(1)} %get-tuple-element.50), channel_id=1, source_target_pairs={{0,8},{4,12},{8,0},{12,4},{16,24},{20,28},{24,16},{28,20},{1,9},{5... | collective-permute-start | bytes 589832 | tf_op jit(solution)/shard_map/ppermute | solution.py:378
  8.1 11.5 %collective-permute-start.4 = (bf16[3,256,128]{2,1,0:T(8,128)(2,1)S(1)}, bf16[3,256,128]{2,1,0:T(8,128)(2,1)S(1)}, u32[]{:S(2)}, u32[]{:S(2)}) collective-permute-start(bf16[3,256,128]{2,1,0:T(8,128)(2,1)S(1)} %get-tuple-element.51), channel_id=1, source_target_pairs={{0,12},{4,8},{8,4},{12,0},{16,28},{20,24},{24,20},{28,16},{1,13},{... | collective-permute-start | bytes 589832 | tf_op jit(solution)/shard_map/ppermute | solution.py:378
  8.5 0.9 %copy-start.1 = (bf16[256,512]{1,0:T(8,128)(2,1)S(1)}, bf16[256,512]{1,0:T(8,128)(2,1)}, u32[]{:S(2)}) copy-start(bf16[256,512]{1,0:T(8,128)(2,1)} %k.3) | copy-start | bytes 786436
  9.4 0.9 %copy-start.2 = (bf16[256,512]{1,0:T(8,128)(2,1)S(1)}, bf16[256,512]{1,0:T(8,128)(2,1)}, u32[]{:S(2)}) copy-start(bf16[256,512]{1,0:T(8,128)(2,1)} %v.3) | copy-start | bytes 786436
  10.9 7.8 %collective-permute-start.1 = (bf16[4,2,64,128]{3,2,1,0:T(8,128)(2,1)S(1)}, bf16[4,2,64,128]{3,2,1,0:T(8,128)(2,1)S(1)}, u32[]{:S(2)}, u32[]{:S(2)}) collective-permute-start(bf16[4,2,64,128]{3,2,1,0:T(8,128)(2,1)S(1)} %shard_map.84), channel_id=1, source_target_pairs={{0,16},{4,20},{8,24},{12,28},{16,0},{20,4},{24,8},{28,12},{1,17},{... | collective-permute-start | bytes 393224 | tf_op jit(solution)/shard_map/ppermute | solution.py:378
  13.6 1.0 %copy-start.3 = (bf16[64,2048]{1,0:T(8,128)(2,1)S(1)}, bf16[64,2048]{1,0:T(8,128)(2,1)}, u32[]{:S(2)}) copy-start(bf16[64,2048]{1,0:T(8,128)(2,1)} %x.1) | copy-start | bytes 786436
  14.5 8.1 %collective-permute-start.5 = (bf16[64,2048]{1,0:T(8,128)(2,1)S(1)}, bf16[64,2048]{1,0:T(8,128)(2,1)S(1)}, u32[]{:S(2)}, u32[]{:S(2)}) collective-permute-start(bf16[64,2048]{1,0:T(8,128)(2,1)S(1)} %shard_map.87.refs_0_), channel_id=1, source_target_pairs={{0,1},{1,0},{2,3},{3,2},{4,5},{5,4},{6,7},{7,6},{8,9},{9,8},{10,11... | collective-permute-start | bytes 786440 | tf_op jit(solution)/shard_map/ppermute | solution.py:378
  19.9 2.7 %collective-permute-start.6 = (bf16[64,2048]{1,0:T(8,128)(2,1)S(1)}, bf16[64,2048]{1,0:T(8,128)(2,1)S(1)}, u32[]{:S(2)}, u32[]{:S(2)}) collective-permute-start(bf16[64,2048]{1,0:T(8,128)(2,1)S(1)} %get-tuple-element.55.refs_2_), channel_id=1, source_target_pairs={{0,1},{1,0},{2,3},{3,2},{4,5},{5,4},{6,7},{7,6},{8,9},{9,8},{10,11... | collective-permute-start | bytes 786440 | tf_op jit(solution)/shard_map/ppermute | solution.py:378
  20.0 9.7 %collective-permute-start.7 = (bf16[2,256,128]{2,1,0:T(8,128)(2,1)S(1)}, bf16[2,256,128]{2,1,0:T(8,128)(2,1)S(1)}, u32[]{:S(2)}, u32[]{:S(2)}) collective-permute-start(bf16[2,256,128]{2,1,0:T(8,128)(2,1)S(1)} %get-tuple-element.62), channel_id=1, source_target_pairs={{0,16},{4,20},{8,24},{12,28},{16,0},{20,4},{24,8},{28,12},{1,17},{... | collective-permute-start | bytes 393224 | tf_op jit(solution)/shard_map/ppermute | solution.py:378
  23.5 6.3 %collective-permute-start.8 = (bf16[384,128]{1,0:T(8,128)(2,1)S(1)}, bf16[384,128]{1,0:T(8,128)(2,1)S(1)}, u32[]{:S(2)}, u32[]{:S(2)}) collective-permute-start(bf16[384,128]{1,0:T(8,128)(2,1)S(1)} %get-tuple-element.63), channel_id=1, source_target_pairs={{0,4},{4,0},{8,12},{12,8},{16,20},{20,16},{24,28},{28,24},{1,5},{5... | collective-permute-start | bytes 294920 | tf_op jit(solution)/shard_map/ppermute | solution.py:378
  24.2 6.8 %collective-permute-start.9 = (bf16[384,128]{1,0:T(8,128)(2,1)S(1)}, bf16[384,128]{1,0:T(8,128)(2,1)S(1)}, u32[]{:S(2)}, u32[]{:S(2)}) collective-permute-start(bf16[384,128]{1,0:T(8,128)(2,1)S(1)} %get-tuple-element.64), channel_id=1, source_target_pairs={{0,8},{4,12},{8,0},{12,4},{16,24},{20,28},{24,16},{28,20},{1,9},{5... | collective-permute-start | bytes 294920 | tf_op jit(solution)/shard_map/ppermute | solution.py:378
  26.7 6.7 %collective-permute-start.10 = (bf16[384,128]{1,0:T(8,128)(2,1)S(1)}, bf16[384,128]{1,0:T(8,128)(2,1)S(1)}, u32[]{:S(2)}, u32[]{:S(2)}) collective-permute-start(bf16[384,128]{1,0:T(8,128)(2,1)S(1)} %get-tuple-element.65), channel_id=1, source_target_pairs={{0,12},{4,8},{8,4},{12,0},{16,28},{20,24},{24,20},{28,16},{1,13},{... | collective-permute-start | bytes 294920 | tf_op jit(solution)/shard_map/ppermute | solution.py:378
  38.0 14.4 %collective-permute-start.15 = (bf16[4,256,128]{2,1,0:T(8,128)(2,1)S(1)}, bf16[4,256,128]{2,1,0:T(8,128)(2,1)S(1)}, u32[]{:S(2)}, u32[]{:S(2)}) collective-permute-start(bf16[4,256,128]{2,1,0:T(8,128)(2,1)S(1)} %get-tuple-element.81), channel_id=1, source_target_pairs={{0,16},{4,20},{8,24},{12,28},{16,0},{20,4},{24,8},{28,12},{1,17},{... | collective-permute-start | bytes 786440 | tf_op jit(solution)/shard_map/ppermute | solution.py:378
  39.5 7.6 %collective-permute-start.11 = (bf16[256,128]{1,0:T(8,128)(2,1)S(1)}, bf16[256,128]{1,0:T(8,128)(2,1)S(1)}, u32[]{:S(2)}, u32[]{:S(2)}) collective-permute-start(bf16[256,128]{1,0:T(8,128)(2,1)S(1)} %get-tuple-element.67), channel_id=1, source_target_pairs={{0,4},{4,0},{8,12},{12,8},{16,20},{20,16},{24,28},{28,24},{1,5},{5... | collective-permute-start | bytes 196616 | tf_op jit(solution)/shard_map/ppermute | solution.py:378
  40.2 6.9 %collective-permute-start.12 = (bf16[256,128]{1,0:T(8,128)(2,1)S(1)}, bf16[256,128]{1,0:T(8,128)(2,1)S(1)}, u32[]{:S(2)}, u32[]{:S(2)}) collective-permute-start(bf16[256,128]{1,0:T(8,128)(2,1)S(1)} %get-tuple-element.68), channel_id=1, source_target_pairs={{0,8},{4,12},{8,0},{12,4},{16,24},{20,28},{24,16},{28,20},{1,9},{5... | collective-permute-start | bytes 196616 | tf_op jit(solution)/shard_map/ppermute | solution.py:378
  43.5 5.9 %collective-permute-start.13 = (bf16[256,128]{1,0:T(8,128)(2,1)S(1)}, bf16[256,128]{1,0:T(8,128)(2,1)S(1)}, u32[]{:S(2)}, u32[]{:S(2)}) collective-permute-start(bf16[256,128]{1,0:T(8,128)(2,1)S(1)} %get-tuple-element.69), channel_id=1, source_target_pairs={{0,12},{4,8},{8,4},{12,0},{16,28},{20,24},{24,20},{28,16},{1,13},{... | collective-permute-start | bytes 196616 | tf_op jit(solution)/shard_map/ppermute | solution.py:378
  50.1 2.6 %collective-permute-start.14 = (bf16[2,64,2048]{2,1,0:T(8,128)(2,1)S(1)}, bf16[2,64,2048]{2,1,0:T(8,128)(2,1)S(1)}, u32[]{:S(2)}, u32[]{:S(2)}) collective-permute-start(bf16[2,64,2048]{2,1,0:T(8,128)(2,1)S(1)} %get-tuple-element.79), channel_id=1, source_target_pairs={{0,1},{1,0},{2,3},{3,2},{4,5},{5,4},{6,7},{7,6},{8,9},{9,8},{10,11... | collective-permute-start | bytes 1572872 | tf_op jit(solution)/shard_map/ppermute | solution.py:378
  52.8 12.2 %collective-permute-start.16 = (bf16[64,2048]{1,0:T(8,128)(2,1)S(1)}, bf16[64,2048]{1,0:T(8,128)(2,1)S(1)}, u32[]{:S(2)}, u32[]{:S(2)}) collective-permute-start(bf16[64,2048]{1,0:T(8,128)(2,1)S(1)} %get-tuple-element.84), channel_id=1, source_target_pairs={{0,2},{1,3},{2,0},{3,1},{4,6},{5,7},{6,4},{7,5},{8,10},{9,11},{10,... | collective-permute-start | bytes 786440 | tf_op jit(solution)/shard_map/ppermute | solution.py:378
  53.6 6.9 %collective-permute-start.17 = (bf16[3,256,128]{2,1,0:T(8,128)(2,1)S(1)}, bf16[3,256,128]{2,1,0:T(8,128)(2,1)S(1)}, u32[]{:S(2)}, u32[]{:S(2)}) collective-permute-start(bf16[3,256,128]{2,1,0:T(8,128)(2,1)S(1)} %get-tuple-element.85), channel_id=1, source_target_pairs={{0,4},{4,0},{8,12},{12,8},{16,20},{20,16},{24,28},{28,24},{1,5},{5... | collective-permute-start | bytes 589832 | tf_op jit(solution)/shard_map/ppermute | solution.py:378
  53.7 7.8 %collective-permute-start.18 = (bf16[3,256,128]{2,1,0:T(8,128)(2,1)S(1)}, bf16[3,256,128]{2,1,0:T(8,128)(2,1)S(1)}, u32[]{:S(2)}, u32[]{:S(2)}) collective-permute-start(bf16[3,256,128]{2,1,0:T(8,128)(2,1)S(1)} %get-tuple-element.86), channel_id=1, source_target_pairs={{0,8},{4,12},{8,0},{12,4},{16,24},{20,28},{24,16},{28,20},{1,9},{5... | collective-permute-start | bytes 589832 | tf_op jit(solution)/shard_map/ppermute | solution.py:378
  55.3 9.7 %collective-permute-start.19 = (bf16[3,256,128]{2,1,0:T(8,128)(2,1)S(1)}, bf16[3,256,128]{2,1,0:T(8,128)(2,1)S(1)}, u32[]{:S(2)}, u32[]{:S(2)}) collective-permute-start(bf16[3,256,128]{2,1,0:T(8,128)(2,1)S(1)} %get-tuple-element.87), channel_id=1, source_target_pairs={{0,12},{4,8},{8,4},{12,0},{16,28},{20,24},{24,20},{28,16},{1,13},{... | collective-permute-start | bytes 589832 | tf_op jit(solution)/shard_map/ppermute | solution.py:378

commit v9 on v8

--- a/solution.py
+++ b/solution.py
@@ -188,111 +188,114 @@
             weight = jnp.exp2(score - top)
             weights[b, side] = weight
             total = total + weight.sum(0, keepdims=True)
-        stats[b, :1] = top
-        stats[b, 1:2] = total
-
-
-def rim_sides(b, nb):
-    return [side for side in range(3) if not 0 <= b + side - 1 < nb]
+        stats[:1, at_block(b)] = top
+        stats[1:2, at_block(b)] = total
+
+
+def rims_of(nb, groups, low, high):
+    group = lax.axis_index("seq") // GROUP
+    if groups == 2:
+        return [(jnp.where(group > 0, 0, nb - 1), low, None)]
+    return [(0, low, group > 0), (nb - 1, high, group < groups - 1)]
 
 
 def forward_kernel(nb, groups, *refs):
     (query, v_t, v1_t, weights, stats), refs = refs[:5], refs[5:]
     (rim_low, rim_high), refs = from_beside(groups, refs)
     chunks, refs = refs[:GROUP], refs[GROUP:]
-    (prob, grads, top_2, deltas, far_shift), refs = refs[:5], refs[5:]
-    outs, (*rim_outs, attended, sums, rim_sums) = refs[:GROUP], refs[GROUP:]
-    ones = jnp.ones((8, HEAD_DIM), BF16)
-    present = rim_present(groups)
+    (prob, grads, top_2, deltas, far_shift, rim_shift), refs = refs[:6], refs[6:]
+    outs, (*rim_outs, attended, far_prob, rim_prob, row, context_t) = refs[:GROUP], refs[GROUP:]
+    rims = rims_of(nb, groups, rim_low, rim_high)
     me = member()
     quarter = BLOCK // 4
+    tokens = nb * BLOCK
     for step, chunk in enumerate(chunks):
         grads[me ^ step] = chunk[:BLOCK]
         for part in range(2):
             level = chunk[BLOCK + part * quarter : BLOCK + (part + 1) * quarter]
             top_2[part, span(me ^ step, quarter), :] = level
-    v2_t = top_2[1].T
+    coarse_query = query[2].reshape(tokens, HEAD_DIM)
+    coarse = dot_nt(top_2[0], coarse_query) * (SCALE * LOG2E)
+    row[:1] = jnp.maximum(stats[:1], coarse.max(0, keepdims=True))
+    scores = []
+    for b, block, present in rims:
+        score = dot_nt(block[0], query[0, b]) * (SCALE * LOG2E)
+        if present is not None:
+            score = jnp.where(present, score, -jnp.inf)
+        at = span(b, BLOCK)
+        row[:1, at] = jnp.maximum(row[:1, at], score.max(0, keepdims=True))
+        scores.append(score)
+    top = row[:1]
+    shrink = jnp.exp2(stats[:1] - top)
+    far = 4.0 * jnp.exp2(coarse - top)
+    row[1:2] = shrink * stats[1:2] + far.sum(0, keepdims=True)
+    fresh = []
+    for (b, _, _), score in zip(rims, scores):
+        at = span(b, BLOCK)
+        fresh.append(jnp.exp2(score - row[:1, at]))
+        row[1:2, at] += fresh[-1].sum(0, keepdims=True)
+    inverse = 1.0 / row[1:2]
+    row[2:3] = inverse
+    row[3:4] = shrink * inverse
+    far_prob[...] = (far * inverse).astype(BF16)
+    context_t[...] = dot(top_2[1].T, far_prob[...])
+    for i, (b, block, _) in enumerate(rims):
+        at = span(b, BLOCK)
+        rim_prob[i] = (fresh[i] * row[2:3, at]).astype(BF16)
+        context_t[:, at] += dot(block[1].T, rim_prob[i])
     for b in range(nb):
-        sides = rim_sides(b, nb)
-        scores = []
-        for side in sides:
-            score = dot_nt((rim_high if side else rim_low)[0], query[0, b]) * (SCALE * LOG2E)
-            scores.append(jnp.where(present[side // 2], score, -jnp.inf))
-        coarse = dot_nt(top_2[0], query[2, b]) * (SCALE * LOG2E)
-        old = stats[b, :1]
-        top = jnp.maximum(old, coarse.max(0, keepdims=True))
-        for score in scores:
-            top = jnp.maximum(top, score.max(0, keepdims=True))
-        shrink = jnp.exp2(old - top)
-        far = 4.0 * jnp.exp2(coarse - top)
-        total = shrink * stats[b, 1:2] + far.sum(0, keepdims=True)
-        fresh = []
-        for score in scores:
-            fresh.append(jnp.exp2(score - top))
-            total = total + fresh[-1].sum(0, keepdims=True)
-        inverse = 1.0 / total
-        shrink = shrink * inverse
-        prob[b, 4] = (far * inverse).astype(BF16)
+        shrink = row[3:4, at_block(b)]
         prob[b, 3] = (weights[b, 3] * shrink).astype(BF16)
-        context = dot(v2_t, prob[b, 4]) + dot(v1_t[:, at_block(sibling(b))], prob[b, 3])
+        context = context_t[:, at_block(b)] + dot(v1_t[:, at_block(sibling(b))], prob[b, 3])
         for side in near_sides(b, nb):
             prob[b, side] = (weights[b, side] * shrink).astype(BF16)
             context = context + dot(v_t[:, at_block(b + side - 1)], prob[b, side])
-        for side, weight in zip(sides, fresh):
-            prob[b, side] = (weight * inverse).astype(BF16)
-            context = context + dot((rim_high if side else rim_low)[1].T, prob[b, side])
-        context = context.T
-        attended[b] = context.astype(BF16)
-        high, low = halves(grads[b].astype(F32) * context)
-        deltas[b] = dot_nt(ones, high) + dot_nt(ones, low)
+        attended[b] = context.T.astype(BF16)
+        deltas[:1, at_block(b)] = (grads[b].T.astype(F32) * context).sum(0, keepdims=True)
+    grad = grads[...].reshape(tokens, HEAD_DIM)
+    slope = dot_nt(top_2[1], grad)
+    far_shift[...] = (far_prob[...].astype(F32) * (slope - deltas[:1])).astype(BF16)
+    rim_outs[0][0] = (SCALE * dot(far_shift[...], coarse_query)).astype(BF16)
+    rim_outs[0][1] = dot(far_prob[...], grad).astype(BF16)
+    pairs = []
+    for i, (b, block, _) in enumerate(rims):
+        slope = dot_nt(block[1], grads[b])
+        rim_shift[i] = (rim_prob[i].astype(F32) * (slope - deltas[:1, span(b, BLOCK)])).astype(BF16)
+        pairs.append((SCALE * dot(rim_shift[i], query[0, b]), dot(rim_prob[i], grads[b])))
+    for part in range(2):
+        if groups == 2:
+            rim_outs[0][2 + part] = pairs[0][part].astype(BF16)
+        else:
+            rim_outs[1][part] = pairs[1][part].astype(BF16)
+            rim_outs[2][part] = pairs[0][part].astype(BF16)
     for step, out in enumerate(outs):
         out[...] = attended[me ^ step]
+
+
+def backward_kernel(nb, groups, *refs):
+    (query, near, level_1, k_t, k1_t, prob, grads, top_2, deltas, far_shift, rim_shift), refs = refs[:11], refs[11:]
+    (rim_low, rim_high), refs = from_beside(groups, refs)
+    grad_q, grad_kv, shift, sums_1, query_t = refs
+    even_1, even_2 = averaging(1), averaging(2)
+    coarse = dot(top_2[0].T, far_shift[...])
     for b in range(nb):
-        grad, delta = grads[b], deltas[b, :1]
-        shift = (prob[b, 4].astype(F32) * (dot_nt(top_2[1], grad) - delta)).astype(BF16)
-        far_shift[b, 0] = shift
-        key, value = SCALE * dot(shift, query[2, b]), dot(prob[b, 4], grad)
-        sums[0], sums[1] = (key, value) if b == 0 else (key + sums[0], value + sums[1])
-        for side in rim_sides(b, nb):
-            slope = dot_nt((rim_high if side else rim_low)[1], grad)
-            shift = (prob[b, side].astype(F32) * (slope - delta)).astype(BF16)
-            far_shift[b, 1] = shift
-            rim_sums[side // 2, 0] = SCALE * dot(shift, query[0, b])
-            rim_sums[side // 2, 1] = dot(prob[b, side], grad)
-    rim_outs[0][:2] = sums[...].astype(BF16)
-    low, high = rim_sums[0], rim_sums[1]
-    if groups == 2:
-        upper = lax.axis_index("seq") >= GROUP
-        rim_outs[0][2:] = jnp.where(upper, low, high).astype(BF16)
-    else:
-        rim_outs[1][...] = high.astype(BF16)
-        rim_outs[2][...] = low.astype(BF16)
-
-
-def backward_kernel(nb, groups, *refs):
-    (query, near, level_1, k_t, k1_t, prob, grads, top_2, deltas, far_shift), refs = refs[:10], refs[10:]
-    (rim_low, rim_high), refs = from_beside(groups, refs)
-    grad_q, grad_kv, shift, sums_1 = refs
-    k2_t = top_2[0].T
-    even_1, even_2 = averaging(1), averaging(2)
+        high, low = halves(coarse[:, at_block(b)])
+        query_t[:, at_block(b)] = dot(high, even_2) + dot(low, even_2)
+    for i, (b, block, _) in enumerate(rims_of(nb, groups, rim_low, rim_high)):
+        query_t[:, span(b, BLOCK)] += dot(block[0].T, rim_shift[i])
     for b in range(nb):
-        grad, delta = grads[b], deltas[b, :1]
-        grad_t = 0.0
-        for side in range(3):
-            if side in near_sides(b, nb):
-                slope = dot_nt(near[b + side - 1, 1], grad)
-                part = (prob[b, side].astype(F32) * (slope - delta)).astype(BF16)
-                shift[b, side] = part
-                grad_t = grad_t + dot(k_t[:, at_block(b + side - 1)], part)
-            else:
-                grad_t = grad_t + dot((rim_high if side else rim_low)[0].T, far_shift[b, 1])
+        grad, delta = grads[b], deltas[:1, at_block(b)]
+        grad_t = query_t[:, at_block(b)]
+        for side in near_sides(b, nb):
+            slope = dot_nt(near[b + side - 1, 1], grad)
+            part = (prob[b, side].astype(F32) * (slope - delta)).astype(BF16)
+            shift[b, side] = part
+            grad_t = grad_t + dot(k_t[:, at_block(b + side - 1)], part)
         slope = dot_nt(level_1[1, at_block(sibling(b))], grad)
         part = (prob[b, 3].astype(F32) * (slope - delta)).astype(BF16)
         shift[b, 3] = part
-        coarse = ((even_1, k1_t[:, at_block(sibling(b))], part), (even_2, k2_t, far_shift[b, 0]))
-        for spread, key_t, part in coarse:
-            high, low = halves(dot(key_t, part))
-            grad_t = grad_t + (dot(high, spread) + dot(low, spread))
+        high, low = halves(dot(k1_t[:, at_block(sibling(b))], part))
+        grad_t = grad_t + (dot(high, even_1) + dot(low, even_1))
         grad_q[b] = (SCALE * grad_t).T.astype(BF16)
     for c in range(nb // 2):
         users = [b for b in range(nb) if sibling(b) == c]
@@ -463,23 +466,32 @@
             shape(HEAD_DIM, tokens // 2),
             shape(HEAD_DIM, tokens // 2),
             shape(nb, 4, BLOCK, BLOCK, dtype=F32),
-            shape(nb, 8, BLOCK, dtype=F32),
+            shape(8, tokens, dtype=F32),
         ],
         (near, queries, level_1, grad_chunks[0]),
         flops=score_flops,
     )
     grad_chunks = exchanged(grad_chunks)
-    stat = shape(nb, 8, BLOCK, dtype=F32)
-    prob, grads, top_2, deltas, far_shift, *refs = call(
+    rim_square = shape(len(rims), BLOCK, BLOCK)
+    prob, grads, top_2, deltas, far_shift, rim_shift, *refs = call(
         functools.partial(forward_kernel, nb, groups),
-        [shape(nb, 5, BLOCK, BLOCK), in_order, block, stat, shape(nb, 2, BLOCK, BLOCK)]
+        [
+            shape(nb, 4, BLOCK, BLOCK),
+            in_order,
+            block,
+            shape(8, tokens, dtype=F32),
+            shape(BLOCK, tokens),
+            rim_square,
+        ]
         + [chunk] * GROUP
         + sent,
         (query, v_t, v1_t, weights, stats, *rim_blocks, *grad_chunks),
         scratch=[
             pltpu.VMEM((nb, rows, HEAD_DIM), BF16),
-            pltpu.VMEM((2, BLOCK, HEAD_DIM), F32),
-            pltpu.VMEM((2, 2, BLOCK, HEAD_DIM), F32),
+            pltpu.VMEM((BLOCK, tokens), BF16),
+            pltpu.VMEM(rim_square.shape, BF16),
+            pltpu.VMEM((8, tokens), F32),
+            pltpu.VMEM((HEAD_DIM, tokens), F32),
         ],
         flops=score_flops,
     )
@@ -489,10 +501,11 @@
     grad_q, grad_kv = call(
         functools.partial(backward_kernel, nb, groups),
         [in_order, shape(2, nb, rows, HEAD_DIM, dtype=F32)],
-        (query, near, level_1, k_t, k1_t, prob, grads, top_2, deltas, far_shift, *rim_blocks),
+        (query, near, level_1, k_t, k1_t, prob, grads, top_2, deltas, far_shift, rim_shift, *rim_blocks),
         scratch=[
             pltpu.VMEM((nb, 4, BLOCK, BLOCK), BF16),
             pltpu.VMEM((2, tokens // 2, HEAD_DIM), F32),
+            pltpu.VMEM((HEAD_DIM, tokens), F32),
         ],
         flops=1,
     )

time: 66.5 us -> 63.9 us (0.961)
  Pallas kernels: 15.1 us -> 12.4 us
    pallas_call x12, Pallas kernels: 15.1 us -> 12.4 us  [call(): pl.pallas_call(kernel, out_shape=out_shape, in_specs=[whole] * len(args),...]
  transfers between devices with their start and end apart: 20 -> 20, of which waited for: 10 -> 11; matrix products, arithmetic and copies ran while one was open for 0% -> 0% of each run, Pallas kernels for 14% -> 14%
where the time goes in v9:
time: 63.9 us; the launch traced here: 63.6 us
  starting transfers between devices  25.5 us (40%)
  waiting for transfers between devices  22.1 us (35%)
  Pallas kernels  12.4 us (19%)
  local copies, waits for them, and re-layouts  2.85 us (4%)
  between operations  0.77 us (1%)
    ppermute x20, starting transfers between devices, swapped(): lax.ppermute(x, axis, [(i, i ^ step) for i in range(lax.axis_size(axis))])  25.5 us
    ppermute x20, waiting for transfers between devices, swapped(): lax.ppermute(x, axis, [(i, i ^ step) for i in range(lax.axis_size(axis))])  22.1 us
    pallas_call x12, Pallas kernels, call(): pl.pallas_call(kernel, out_shape=out_shape, in_specs=[whole] * len(args),...  12.4 us
    unnamed x8, local copies, waits for them, and re-layouts  2.85 us
  transfers between devices with their start and end apart: 20, of which 11 were waited for; matrix products, arithmetic and copies ran while one was open for 0% of the time, Pallas kernels for 14%

profile of v9, /device:TPU:0, one launch (start us, length us, event | category | flops | bytes accessed | tf_op | source)
XLA Modules:
  0.0 63.6 jit_solution(12215621483758649623)
XLA Ops:
  0.6 3.0 %collective-permute-start = (bf16[64,2048]{1,0:T(8,128)(2,1)}, bf16[64,2048]{1,0:T(8,128)(2,1)S(1)}, u32[]{:S(2)}, u32[]{:S(2)}) collective-permute-start(bf16[64,2048]{1,0:T(8,128)(2,1)} %x.1), channel_id=1, source_target_pairs={{0,2},{1,3},{2,0},{3,1},{4,6},{5,7},{6,4},{7,5},{8,10},{9,11},{10,... | collective-permute-start | bytes 786440 | tf_op jit(solution)/shard_map/ppermute | solution.py:381
  3.6 1.3 %shard_map.85 = (bf16[3,256,128]{2,1,0:T(8,128)(2,1)S(1)}, bf16[3,256,128]{2,1,0:T(8,128)(2,1)S(1)}, bf16[3,256,128]{2,1,0:T(8,128)(2,1)S(1)}, bf16[3,256,128]{2,1,0:T(8,128)(2,1)S(1)}) custom-call(bf16[256,512]{1,0:T(8,128)(2,1)} %q.1, bf16[256,512]{1,0:T(8,128)(2,1)} %k.3, bf16[256,512]{1,0:T(8,128)(2,1)} %v.3), custom_call_target="tpu_custom_call" | custom-call | tf_op jit(solution)/shard_map/pallas_call | solution.py:36
  4.9 1.6 %collective-permute-start.2 = (bf16[3,256,128]{2,1,0:T(8,128)(2,1)S(1)}, bf16[3,256,128]{2,1,0:T(8,128)(2,1)S(1)}, u32[]{:S(2)}, u32[]{:S(2)}) collective-permute-start(bf16[3,256,128]{2,1,0:T(8,128)(2,1)S(1)} %get-tuple-element.50), channel_id=1, source_target_pairs={{0,4},{4,0},{8,12},{12,8},{16,20},{20,16},{24,28},{28,24},{1,5},{5... | collective-permute-start | bytes 589832 | tf_op jit(solution)/shard_map/ppermute | solution.py:381
  6.5 1.6 %collective-permute-start.3 = (bf16[3,256,128]{2,1,0:T(8,128)(2,1)S(1)}, bf16[3,256,128]{2,1,0:T(8,128)(2,1)S(1)}, u32[]{:S(2)}, u32[]{:S(2)}) collective-permute-start(bf16[3,256,128]{2,1,0:T(8,128)(2,1)S(1)} %get-tuple-element.51), channel_id=1, source_target_pairs={{0,8},{4,12},{8,0},{12,4},{16,24},{20,28},{24,16},{28,20},{1,9},{5... | collective-permute-start | bytes 589832 | tf_op jit(solution)/shard_map/ppermute | solution.py:381
  10.9 2.7 %collective-permute-start.1 = (bf16[4,2,64,128]{3,2,1,0:T(8,128)(2,1)S(1)}, bf16[4,2,64,128]{3,2,1,0:T(8,128)(2,1)S(1)}, u32[]{:S(2)}, u32[]{:S(2)}) collective-permute-start(bf16[4,2,64,128]{3,2,1,0:T(8,128)(2,1)S(1)} %shard_map.84), channel_id=1, source_target_pairs={{0,16},{4,20},{8,24},{12,28},{16,0},{20,4},{24,8},{28,12},{1,17},{... | collective-permute-start | bytes 393224 | tf_op jit(solution)/shard_map/ppermute | solution.py:381
  14.6 4.1 %collective-permute-done.1._.refs_5_ = bf16[4,2,64,128]{3,2,1,0:T(8,128)(2,1)S(1)} collective-permute-done((bf16[4,2,64,128]{3,2,1,0:T(8,128)(2,1)S(1)}, bf16[4,2,64,128]{3,2,1,0:T(8,128)(2,1)S(1)}, u32[]{:S(2)}, u32[]{:S(2)}) %collective-permute-start.1) | collective-permute-done | bytes 131104 | tf_op jit(solution)/shard_map/ppermute | solution.py:381
  20.0 2.6 %collective-permute-start.7 = (bf16[2,256,128]{2,1,0:T(8,128)(2,1)S(1)}, bf16[2,256,128]{2,1,0:T(8,128)(2,1)S(1)}, u32[]{:S(2)}, u32[]{:S(2)}) collective-permute-start(bf16[2,256,128]{2,1,0:T(8,128)(2,1)S(1)} %get-tuple-element.63), channel_id=1, source_target_pairs={{0,16},{4,20},{8,24},{12,28},{16,0},{20,4},{24,8},{28,12},{1,17},{... | collective-permute-start | bytes 393224 | tf_op jit(solution)/shard_map/ppermute | solution.py:381
  24.2 2.5 %collective-permute-start.9 = (bf16[384,128]{1,0:T(8,128)(2,1)S(1)}, bf16[384,128]{1,0:T(8,128)(2,1)S(1)}, u32[]{:S(2)}, u32[]{:S(2)}) collective-permute-start(bf16[384,128]{1,0:T(8,128)(2,1)S(1)} %get-tuple-element.65), channel_id=1, source_target_pairs={{0,8},{4,12},{8,0},{12,4},{16,24},{20,28},{24,16},{28,20},{1,9},{5... | collective-permute-start | bytes 294920 | tf_op jit(solution)/shard_map/ppermute | solution.py:381
  27.0 1.7 %shard_map.89 = (bf16[3,4,256,128]{3,2,1,0:T(8,128)(2,1)S(1)}, bf16[128,1024]{1,0:T(8,128)(2,1)S(1)}, bf16[128,1024]{1,0:T(8,128)(2,1)S(1)}, bf16[128,512]{1,0:T...) custom-call(bf16[4,2,256,128]{3,2,1,0:T(8,128)(2,1)S(1)} %get-tuple-element.53, ...), custom_call_target="tpu_custom_call" | custom-call | flops 335544320 | bytes 6946816 | tf_op jit(solution)/shard_map/pallas_call | solution.py:36
  28.7 1.1 %collective-permute-done.7.refs_5_.refs_11_ = bf16[2,256,128]{2,1,0:T(8,128)(2,1)S(1)} collective-permute-done((bf16[2,256,128]{2,1,0:T(8,128)(2,1)S(1)}, bf16[2,256,128]{2,1,0:T(8,128)(2,1)S(1)}, u32[]{:S(2)}, u32[]{:S(2)}) %collective-permute-start.7) | collective-permute-done | bytes 131104 | tf_op jit(solution)/shard_map/ppermute | solution.py:381
  29.8 1.2 %collective-permute-done.9.refs_8_ = bf16[384,128]{1,0:T(8,128)(2,1)S(1)} collective-permute-done((bf16[384,128]{1,0:T(8,128)(2,1)S(1)}, bf16[384,128]{1,0:T(8,128)(2,1)S(1)}, u32[]{:S(2)}, u32[]{:S(2)}) %collective-permute-start.9) | collective-permute-done | bytes 98336 | tf_op jit(solution)/shard_map/ppermute | solution.py:381
  30.9 2.4 %collective-permute-done.10.refs_9_ = bf16[384,128]{1,0:T(8,128)(2,1)S(1)} collective-permute-done((bf16[384,128]{1,0:T(8,128)(2,1)S(1)}, bf16[384,128]{1,0:T(8,128)(2,1)S(1)}, u32[]{:S(2)}, u32[]{:S(2)}) %collective-permute-start.10) | collective-permute-done | bytes 98336 | tf_op jit(solution)/shard_map/ppermute | solution.py:381
  33.4 2.0 %shard_map.90 = (bf16[4,4,256,256]{3,2,1,0:T(8,128)(2,1)S(1)}, bf16[4,256,128]{2,1,0:T(8,128)(2,1)S(1)}, bf16[2,256,128]{2,1,0:T(8,128)(2,1)S(1)}, f32[8,1024]{1...) custom-call(bf16[3,4,256,128]{3,2,1,0:T(8,128)(2,1)S(1)} %get-tuple-, ...), custom_call_target="tpu_custom_call" | custom-call | flops 335544320 | bytes 9633792 | tf_op jit(solution)/shard_map/pallas_call | solution.py:36
  35.4 1.5 %collective-permute-start.15 = (bf16[4,256,128]{2,1,0:T(8,128)(2,1)S(1)}, bf16[4,256,128]{2,1,0:T(8,128)(2,1)S(1)}, u32[]{:S(2)}, u32[]{:S(2)}) collective-permute-start(bf16[4,256,128]{2,1,0:T(8,128)(2,1)S(1)} %get-tuple-element.83), channel_id=1, source_target_pairs={{0,16},{4,20},{8,24},{12,28},{16,0},{20,4},{24,8},{28,12},{1,17},{... | collective-permute-start | bytes 786440 | tf_op jit(solution)/shard_map/ppermute | solution.py:381
  37.7 3.2 %collective-permute-start.12 = (bf16[256,128]{1,0:T(8,128)(2,1)S(1)}, bf16[256,128]{1,0:T(8,128)(2,1)S(1)}, u32[]{:S(2)}, u32[]{:S(2)}) collective-permute-start(bf16[256,128]{1,0:T(8,128)(2,1)S(1)} %get-tuple-element.69), channel_id=1, source_target_pairs={{0,8},{4,12},{8,0},{12,4},{16,24},{20,28},{24,16},{28,20},{1,9},{5... | collective-permute-start | bytes 196616 | tf_op jit(solution)/shard_map/ppermute | solution.py:381
  41.0 3.4 %shard_map.91 = (bf16[4,256,128]{2,1,0:T(8,128)(2,1)S(1)}, f32[2,4,256,128]{3,2,1,0:T(8,128)S(1)}) custom-call(bf16[3,4,256,128]{3,2,1,0:T(8,128)(2,1)S(1)} %get-tuple-element.58.refs_0_, bf16[4,2,256,128]{3,2,1,0:T(8,128)(2,1)S(1)} %get-tuple-element.53.near.refs_1_, bf16[2,512,128]{2,1,0:T(8,128)(2,1)S(1)} %get-tuple-element.55.level_1.refs_2_, ...), custom_call_target="tpu_custom_call" | custom-call | flops 1 | bytes 6586368 | tf_op jit(solution)/shard_map/pallas_call | solution.py:36
  44.5 2.3 %collective-permute-done.13.refs_3_ = bf16[256,128]{1,0:T(8,128)(2,1)S(1)} collective-permute-done((bf16[256,128]{1,0:T(8,128)(2,1)S(1)}, bf16[256,128]{1,0:T(8,128)(2,1)S(1)}, u32[]{:S(2)}, u32[]{:S(2)}) %collective-permute-start.13) | collective-permute-done | bytes 65568 | tf_op jit(solution)/shard_map/ppermute | solution.py:381
  47.6 2.1 %collective-permute-done.15.refs_0_ = bf16[4,256,128]{2,1,0:T(8,128)(2,1)S(1)} collective-permute-done((bf16[4,256,128]{2,1,0:T(8,128)(2,1)S(1)}, bf16[4,256,128]{2,1,0:T(8,128)(2,1)S(1)}, u32[]{:S(2)}, u32[]{:S(2)}) %collective-permute-start.15) | collective-permute-done | bytes 262176 | tf_op jit(solution)/shard_map/ppermute | solution.py:381
  51.1 1.7 %collective-permute-start.18 = (bf16[3,256,128]{2,1,0:T(8,128)(2,1)S(1)}, bf16[3,256,128]{2,1,0:T(8,128)(2,1)S(1)}, u32[]{:S(2)}, u32[]{:S(2)}) collective-permute-start(bf16[3,256,128]{2,1,0:T(8,128)(2,1)S(1)} %get-tuple-element.88), channel_id=1, source_target_pairs={{0,8},{4,12},{8,0},{12,4},{16,24},{20,28},{24,16},{28,20},{1,9},{5... | collective-permute-start | bytes 589832 | tf_op jit(solution)/shard_map/ppermute | solution.py:381
  52.8 1.7 %collective-permute-start.19 = (bf16[3,256,128]{2,1,0:T(8,128)(2,1)S(1)}, bf16[3,256,128]{2,1,0:T(8,128)(2,1)S(1)}, u32[]{:S(2)}, u32[]{:S(2)}) collective-permute-start(bf16[3,256,128]{2,1,0:T(8,128)(2,1)S(1)} %get-tuple-element.89), channel_id=1, source_target_pairs={{0,12},{4,8},{8,4},{12,0},{16,28},{20,24},{24,20},{28,16},{1,13},{... | collective-permute-start | bytes 589832 | tf_op jit(solution)/shard_map/ppermute | solution.py:381
  54.5 3.4 %collective-permute-done.17.refs_3_ = bf16[3,256,128]{2,1,0:T(8,128)(2,1)S(1)} collective-permute-done((bf16[3,256,128]{2,1,0:T(8,128)(2,1)S(1)}, bf16[3,256,128]{2,1,0:T(8,128)(2,1)S(1)}, u32[]{:S(2)}, u32[]{:S(2)}) %collective-permute-start.17) | collective-permute-done | bytes 196640 | tf_op jit(solution)/shard_map/ppermute | solution.py:381
  57.9 1.0 %collective-permute-done.18.refs_4_ = bf16[3,256,128]{2,1,0:T(8,128)(2,1)S(1)} collective-permute-done((bf16[3,256,128]{2,1,0:T(8,128)(2,1)S(1)}, bf16[3,256,128]{2,1,0:T(8,128)(2,1)S(1)}, u32[]{:S(2)}, u32[]{:S(2)}) %collective-permute-start.18) | collective-permute-done | bytes 196640 | tf_op jit(solution)/shard_map/ppermute | solution.py:381
  59.0 3.5 %collective-permute-done.19.refs_5_ = bf16[3,256,128]{2,1,0:T(8,128)(2,1)S(1)} collective-permute-done((bf16[3,256,128]{2,1,0:T(8,128)(2,1)S(1)}, bf16[3,256,128]{2,1,0:T(8,128)(2,1)S(1)}, u32[]{:S(2)}, u32[]{:S(2)}) %collective-permute-start.19) | collective-permute-done | bytes 196640 | tf_op jit(solution)/shard_map/ppermute | solution.py:381
  62.5 1.1 %shard_map.95 = (bf16[256,512]{1,0:T(8,128)(2,1)}, bf16[256,512]{1,0:T(8,128)(2,1)}, bf16[256,512]{1,0:T(8,128)(2,1)}, bf16[64,2048]{1,0:T(8,128)(2,1)}) custom-call(f32[64,2048]{1,0:T(8,128)S(1)} %get-tuple-element.85.refs_0_, bf16[64,2048]{1,0:T(8,128)(2,1)S(1)} %collective-permute-done.16.refs_1_, bf16[3,256,128]{2,1,0:T(8,128)(2,1)S(1)} %get-tuple-element.84._.refs_2_, ...), custom_call_target="tpu_custom_call" | custom-call | tf_op jit(solution)/shard_map/pallas_call | solution.py:36
  (36 shorter events, 10.2 us)
Async XLA Ops:
  0.6 22.0 %copy-start = (bf16[512,2048]{1,0:T(8,128)(2,1)S(1)}, bf16[512,2048]{1,0:T(8,128)(2,1)}, u32[]{:S(2)}) copy-start(bf16[512,2048]{1,0:T(8,128)(2,1)} %refs_4_.3) | copy-start | bytes 6291460
  0.6 18.9 %collective-permute-start = (bf16[64,2048]{1,0:T(8,128)(2,1)}, bf16[64,2048]{1,0:T(8,128)(2,1)S(1)}, u32[]{:S(2)}, u32[]{:S(2)}) collective-permute-start(bf16[64,2048]{1,0:T(8,128)(2,1)} %x.1), channel_id=1, source_target_pairs={{0,2},{1,3},{2,0},{3,1},{4,6},{5,7},{6,4},{7,5},{8,10},{9,11},{10,... | collective-permute-start | bytes 786440 | tf_op jit(solution)/shard_map/ppermute | solution.py:381
  4.9 8.6 %collective-permute-start.2 = (bf16[3,256,128]{2,1,0:T(8,128)(2,1)S(1)}, bf16[3,256,128]{2,1,0:T(8,128)(2,1)S(1)}, u32[]{:S(2)}, u32[]{:S(2)}) collective-permute-start(bf16[3,256,128]{2,1,0:T(8,128)(2,1)S(1)} %get-tuple-element.50), channel_id=1, source_target_pairs={{0,4},{4,0},{8,12},{12,8},{16,20},{20,16},{24,28},{28,24},{1,5},{5... | collective-permute-start | bytes 589832 | tf_op jit(solution)/shard_map/ppermute | solution.py:381
  6.5 12.2 %collective-permute-start.3 = (bf16[3,256,128]{2,1,0:T(8,128)(2,1)S(1)}, bf16[3,256,128]{2,1,0:T(8,128)(2,1)S(1)}, u32[]{:S(2)}, u32[]{:S(2)}) collective-permute-start(bf16[3,256,128]{2,1,0:T(8,128)(2,1)S(1)} %get-tuple-element.51), channel_id=1, source_target_pairs={{0,8},{4,12},{8,0},{12,4},{16,24},{20,28},{24,16},{28,20},{1,9},{5... | collective-permute-start | bytes 589832 | tf_op jit(solution)/shard_map/ppermute | solution.py:381
  8.1 11.5 %collective-permute-start.4 = (bf16[3,256,128]{2,1,0:T(8,128)(2,1)S(1)}, bf16[3,256,128]{2,1,0:T(8,128)(2,1)S(1)}, u32[]{:S(2)}, u32[]{:S(2)}) collective-permute-start(bf16[3,256,128]{2,1,0:T(8,128)(2,1)S(1)} %get-tuple-element.52), channel_id=1, source_target_pairs={{0,12},{4,8},{8,4},{12,0},{16,28},{20,24},{24,20},{28,16},{1,13},{... | collective-permute-start | bytes 589832 | tf_op jit(solution)/shard_map/ppermute | solution.py:381
  8.5 0.9 %copy-start.1 = (bf16[256,512]{1,0:T(8,128)(2,1)S(1)}, bf16[256,512]{1,0:T(8,128)(2,1)}, u32[]{:S(2)}) copy-start(bf16[256,512]{1,0:T(8,128)(2,1)} %k.3) | copy-start | bytes 786436
  9.4 0.9 %copy-start.2 = (bf16[256,512]{1,0:T(8,128)(2,1)S(1)}, bf16[256,512]{1,0:T(8,128)(2,1)}, u32[]{:S(2)}) copy-start(bf16[256,512]{1,0:T(8,128)(2,1)} %v.3) | copy-start | bytes 786436
  10.9 7.8 %collective-permute-start.1 = (bf16[4,2,64,128]{3,2,1,0:T(8,128)(2,1)S(1)}, bf16[4,2,64,128]{3,2,1,0:T(8,128)(2,1)S(1)}, u32[]{:S(2)}, u32[]{:S(2)}) collective-permute-start(bf16[4,2,64,128]{3,2,1,0:T(8,128)(2,1)S(1)} %shard_map.84), channel_id=1, source_target_pairs={{0,16},{4,20},{8,24},{12,28},{16,0},{20,4},{24,8},{28,12},{1,17},{... | collective-permute-start | bytes 393224 | tf_op jit(solution)/shard_map/ppermute | solution.py:381
  13.6 1.0 %copy-start.3 = (bf16[64,2048]{1,0:T(8,128)(2,1)S(1)}, bf16[64,2048]{1,0:T(8,128)(2,1)}, u32[]{:S(2)}) copy-start(bf16[64,2048]{1,0:T(8,128)(2,1)} %x.1) | copy-start | bytes 786436
  14.5 8.1 %collective-permute-start.5 = (bf16[64,2048]{1,0:T(8,128)(2,1)S(1)}, bf16[64,2048]{1,0:T(8,128)(2,1)S(1)}, u32[]{:S(2)}, u32[]{:S(2)}) collective-permute-start(bf16[64,2048]{1,0:T(8,128)(2,1)S(1)} %shard_map.87.refs_0_), channel_id=1, source_target_pairs={{0,1},{1,0},{2,3},{3,2},{4,5},{5,4},{6,7},{7,6},{8,9},{9,8},{10,11... | collective-permute-start | bytes 786440 | tf_op jit(solution)/shard_map/ppermute | solution.py:381
  19.9 2.7 %collective-permute-start.6 = (bf16[64,2048]{1,0:T(8,128)(2,1)S(1)}, bf16[64,2048]{1,0:T(8,128)(2,1)S(1)}, u32[]{:S(2)}, u32[]{:S(2)}) collective-permute-start(bf16[64,2048]{1,0:T(8,128)(2,1)S(1)} %get-tuple-element.56.refs_2_), channel_id=1, source_target_pairs={{0,1},{1,0},{2,3},{3,2},{4,5},{5,4},{6,7},{7,6},{8,9},{9,8},{10,11... | collective-permute-start | bytes 786440 | tf_op jit(solution)/shard_map/ppermute | solution.py:381
  20.0 9.7 %collective-permute-start.7 = (bf16[2,256,128]{2,1,0:T(8,128)(2,1)S(1)}, bf16[2,256,128]{2,1,0:T(8,128)(2,1)S(1)}, u32[]{:S(2)}, u32[]{:S(2)}) collective-permute-start(bf16[2,256,128]{2,1,0:T(8,128)(2,1)S(1)} %get-tuple-element.63), channel_id=1, source_target_pairs={{0,16},{4,20},{8,24},{12,28},{16,0},{20,4},{24,8},{28,12},{1,17},{... | collective-permute-start | bytes 393224 | tf_op jit(solution)/shard_map/ppermute | solution.py:381
  23.5 6.3 %collective-permute-start.8 = (bf16[384,128]{1,0:T(8,128)(2,1)S(1)}, bf16[384,128]{1,0:T(8,128)(2,1)S(1)}, u32[]{:S(2)}, u32[]{:S(2)}) collective-permute-start(bf16[384,128]{1,0:T(8,128)(2,1)S(1)} %get-tuple-element.64), channel_id=1, source_target_pairs={{0,4},{4,0},{8,12},{12,8},{16,20},{20,16},{24,28},{28,24},{1,5},{5... | collective-permute-start | bytes 294920 | tf_op jit(solution)/shard_map/ppermute | solution.py:381
  24.2 6.8 %collective-permute-start.9 = (bf16[384,128]{1,0:T(8,128)(2,1)S(1)}, bf16[384,128]{1,0:T(8,128)(2,1)S(1)}, u32[]{:S(2)}, u32[]{:S(2)}) collective-permute-start(bf16[384,128]{1,0:T(8,128)(2,1)S(1)} %get-tuple-element.65), channel_id=1, source_target_pairs={{0,8},{4,12},{8,0},{12,4},{16,24},{20,28},{24,16},{28,20},{1,9},{5... | collective-permute-start | bytes 294920 | tf_op jit(solution)/shard_map/ppermute | solution.py:381
  26.7 6.7 %collective-permute-start.10 = (bf16[384,128]{1,0:T(8,128)(2,1)S(1)}, bf16[384,128]{1,0:T(8,128)(2,1)S(1)}, u32[]{:S(2)}, u32[]{:S(2)}) collective-permute-start(bf16[384,128]{1,0:T(8,128)(2,1)S(1)} %get-tuple-element.66), channel_id=1, source_target_pairs={{0,12},{4,8},{8,4},{12,0},{16,28},{20,24},{24,20},{28,16},{1,13},{... | collective-permute-start | bytes 294920 | tf_op jit(solution)/shard_map/ppermute | solution.py:381
  35.4 14.4 %collective-permute-start.15 = (bf16[4,256,128]{2,1,0:T(8,128)(2,1)S(1)}, bf16[4,256,128]{2,1,0:T(8,128)(2,1)S(1)}, u32[]{:S(2)}, u32[]{:S(2)}) collective-permute-start(bf16[4,256,128]{2,1,0:T(8,128)(2,1)S(1)} %get-tuple-element.83), channel_id=1, source_target_pairs={{0,16},{4,20},{8,24},{12,28},{16,0},{20,4},{24,8},{28,12},{1,17},{... | collective-permute-start | bytes 786440 | tf_op jit(solution)/shard_map/ppermute | solution.py:381
  36.9 7.5 %collective-permute-start.11 = (bf16[256,128]{1,0:T(8,128)(2,1)S(1)}, bf16[256,128]{1,0:T(8,128)(2,1)S(1)}, u32[]{:S(2)}, u32[]{:S(2)}) collective-permute-start(bf16[256,128]{1,0:T(8,128)(2,1)S(1)} %get-tuple-element.68), channel_id=1, source_target_pairs={{0,4},{4,0},{8,12},{12,8},{16,20},{20,16},{24,28},{28,24},{1,5},{5... | collective-permute-start | bytes 196616 | tf_op jit(solution)/shard_map/ppermute | solution.py:381
  37.7 6.8 %collective-permute-start.12 = (bf16[256,128]{1,0:T(8,128)(2,1)S(1)}, bf16[256,128]{1,0:T(8,128)(2,1)S(1)}, u32[]{:S(2)}, u32[]{:S(2)}) collective-permute-start(bf16[256,128]{1,0:T(8,128)(2,1)S(1)} %get-tuple-element.69), channel_id=1, source_target_pairs={{0,8},{4,12},{8,0},{12,4},{16,24},{20,28},{24,16},{28,20},{1,9},{5... | collective-permute-start | bytes 196616 | tf_op jit(solution)/shard_map/ppermute | solution.py:381
  40.9 5.9 %collective-permute-start.13 = (bf16[256,128]{1,0:T(8,128)(2,1)S(1)}, bf16[256,128]{1,0:T(8,128)(2,1)S(1)}, u32[]{:S(2)}, u32[]{:S(2)}) collective-permute-start(bf16[256,128]{1,0:T(8,128)(2,1)S(1)} %get-tuple-element.70), channel_id=1, source_target_pairs={{0,12},{4,8},{8,4},{12,0},{16,28},{20,24},{24,20},{28,16},{1,13},{... | collective-permute-start | bytes 196616 | tf_op jit(solution)/shard_map/ppermute | solution.py:381
  47.6 2.6 %collective-permute-start.14 = (bf16[2,64,2048]{2,1,0:T(8,128)(2,1)S(1)}, bf16[2,64,2048]{2,1,0:T(8,128)(2,1)S(1)}, u32[]{:S(2)}, u32[]{:S(2)}) collective-permute-start(bf16[2,64,2048]{2,1,0:T(8,128)(2,1)S(1)} %get-tuple-element.81), channel_id=1, source_target_pairs={{0,1},{1,0},{2,3},{3,2},{4,5},{5,4},{6,7},{7,6},{8,9},{9,8},{10,11... | collective-permute-start | bytes 1572872 | tf_op jit(solution)/shard_map/ppermute | solution.py:381
  50.3 12.2 %collective-permute-start.16 = (bf16[64,2048]{1,0:T(8,128)(2,1)S(1)}, bf16[64,2048]{1,0:T(8,128)(2,1)S(1)}, u32[]{:S(2)}, u32[]{:S(2)}) collective-permute-start(bf16[64,2048]{1,0:T(8,128)(2,1)S(1)} %get-tuple-element.86), channel_id=1, source_target_pairs={{0,2},{1,3},{2,0},{3,1},{4,6},{5,7},{6,4},{7,5},{8,10},{9,11},{10,... | collective-permute-start | bytes 786440 | tf_op jit(solution)/shard_map/ppermute | solution.py:381
  51.0 6.9 %collective-permute-start.17 = (bf16[3,256,128]{2,1,0:T(8,128)(2,1)S(1)}, bf16[3,256,128]{2,1,0:T(8,128)(2,1)S(1)}, u32[]{:S(2)}, u32[]{:S(2)}) collective-permute-start(bf16[3,256,128]{2,1,0:T(8,128)(2,1)S(1)} %get-tuple-element.87), channel_id=1, source_target_pairs={{0,4},{4,0},{8,12},{12,8},{16,20},{20,16},{24,28},{28,24},{1,5},{5... | collective-permute-start | bytes 589832 | tf_op jit(solution)/shard_map/ppermute | solution.py:381
  51.1 7.8 %collective-permute-start.18 = (bf16[3,256,128]{2,1,0:T(8,128)(2,1)S(1)}, bf16[3,256,128]{2,1,0:T(8,128)(2,1)S(1)}, u32[]{:S(2)}, u32[]{:S(2)}) collective-permute-start(bf16[3,256,128]{2,1,0:T(8,128)(2,1)S(1)} %get-tuple-element.88), channel_id=1, source_target_pairs={{0,8},{4,12},{8,0},{12,4},{16,24},{20,28},{24,16},{28,20},{1,9},{5... | collective-permute-start | bytes 589832 | tf_op jit(solution)/shard_map/ppermute | solution.py:381
  52.8 9.7 %collective-permute-start.19 = (bf16[3,256,128]{2,1,0:T(8,128)(2,1)S(1)}, bf16[3,256,128]{2,1,0:T(8,128)(2,1)S(1)}, u32[]{:S(2)}, u32[]{:S(2)}) collective-permute-start(bf16[3,256,128]{2,1,0:T(8,128)(2,1)S(1)} %get-tuple-element.89), channel_id=1, source_target_pairs={{0,12},{4,8},{8,4},{12,0},{16,28},{20,24},{24,20},{28,16},{1,13},{... | collective-permute-start | bytes 589832 | tf_op jit(solution)/shard_map/ppermute | solution.py:381

commit v10 on v9

--- a/solution.py
+++ b/solution.py
@@ -11,6 +11,7 @@
 BLOCK = 256
 LEVELS = 2
 GROUP = 4
+STEPS = (0, 3, 2, 1)
 N_MP = 4
 SCALE = HEAD_DIM**-0.5
 LOG2E = 1.4426950408889634
@@ -102,10 +103,10 @@
     *outs, sems = refs
     me = member()
     copies = []
-    for step in (3, 1, 2, 0):
+    for step, out in zip(STEPS, outs):
         for part, source in enumerate((k, v, q)):
             piece = source.at[:, columns(me ^ step)]
-            copies.append(pltpu.make_async_copy(piece, outs[step].at[part], sems.at[len(copies)]))
+            copies.append(pltpu.make_async_copy(piece, out.at[part], sems.at[len(copies)]))
     for copy in copies:
         copy.start()
     for copy in copies:
@@ -130,7 +131,7 @@
     chunks, (far_out, near, queries, level_1, *rims) = refs[:GROUP], refs[GROUP:]
     far_out[...] = far[...]
     me = member()
-    for step, chunk in enumerate(chunks):
+    for step, chunk in zip(STEPS, chunks):
         near[me ^ step] = chunk[:2]
         queries[me ^ step] = chunk[2]
     pool = pooling()
@@ -209,7 +210,7 @@
     me = member()
     quarter = BLOCK // 4
     tokens = nb * BLOCK
-    for step, chunk in enumerate(chunks):
+    for step, chunk in zip(STEPS, chunks):
         grads[me ^ step] = chunk[:BLOCK]
         for part in range(2):
             level = chunk[BLOCK + part * quarter : BLOCK + (part + 1) * quarter]
@@ -268,7 +269,7 @@
         else:
             rim_outs[1][part] = pairs[1][part].astype(BF16)
             rim_outs[2][part] = pairs[0][part].astype(BF16)
-    for step, out in enumerate(outs):
+    for step, out in zip(STEPS, outs):
         out[...] = attended[me ^ step]
 
 
@@ -312,12 +313,19 @@
             grad_kv[part, s] = total + (dot(spread, high) + dot(spread, low))
 
 
-def share_kernel(kept, got, _, across, here):
-    across[...] = (kept[1].astype(F32) + got[1].astype(F32)).astype(BF16)
-    here[...] = kept[0].astype(F32) + got[0].astype(F32)
-
-
-def combine_kernel(nb, groups, grad_q, grad_kv, *refs):
+def share_kernel(kept, *refs):
+    *got, across, here = refs
+    half = across.shape[0] // 2
+    for i, piece in enumerate(got):
+        far, at = i // 2, pl.ds(i % 2 * half, half)
+        total = kept[far, at, :].astype(F32) + piece[...].astype(F32)
+        if far:
+            across[at, :] = total.astype(BF16)
+        else:
+            here[at, :] = total
+
+
+def combine_kernel(nb, groups, grad_q, grad_kv, _, *refs):
     (got_top, got_low, got_high), (*outs, out) = from_others(groups, refs)
     present = rim_present(groups)
     spread = spreading(2)
@@ -331,7 +339,7 @@
                 total = total + jnp.where(present[1], got_high[part].astype(F32), 0.0)
             out[b, part] = total.astype(BF16)
     me = member()
-    for step, chunk in enumerate(outs):
+    for step, chunk in zip(STEPS, outs):
         chunk[:2] = out[me ^ step]
         chunk[2] = grad_q[me ^ step]
 
@@ -341,10 +349,10 @@
     chunks, (*outs, mixed) = refs[:GROUP], refs[GROUP:]
     mixed[...] = (here[...] + across[...].astype(F32)).astype(BF16)
     me = member()
-    for step in range(GROUP):
+    for step, chunk in zip(STEPS, chunks):
         at = columns(me ^ step)
         for part, out in enumerate(outs):
-            out[:, at] = chunks[step][part]
+            out[:, at] = chunk[part]
 
 
 def share():
@@ -359,22 +367,25 @@
         whole[span(share() ^ step, piece.shape[0]), :] = piece[...]
     heads[...] = dot_nt(whole[...], out_weight[...]).astype(BF16)
     quarter = tops.shape[2]
-    for step, out in enumerate(outs):
+    for step, out in zip(STEPS, outs):
         out[:BLOCK] = heads[:, columns(me ^ step)]
         for part in range(2):
             out[BLOCK + part * quarter : BLOCK + (part + 1) * quarter] = tops[me ^ step, part]
 
 
 def project_kernel(*refs):
-    chunks, out_weight, (kept, sent, attended, whole) = refs[:GROUP], refs[GROUP], refs[-4:]
-    me = member()
-    for step, chunk in enumerate(chunks):
+    chunks, out_weight, (kept, *sent, attended, whole) = refs[:GROUP], refs[GROUP], refs[GROUP + 2 :]
+    me = member()
+    for step, chunk in zip(STEPS, chunks):
         attended[:, columns(me ^ step)] = chunk[...]
     whole[...] = dot(attended[...], out_weight[...]).astype(BF16)
     rows = kept.shape[1]
     for far in range(2):
         kept[far] = whole[span(share() ^ (2 * far), rows), :]
-        sent[far] = whole[span(share() ^ (2 * far + 1), rows), :]
+        for part in range(2):
+            half = rows // 2
+            at = 2 * (share() ^ (2 * far + 1)) + part
+            sent[2 * far + part][...] = whole[span(at, half), :]
 
 
 def swapped(x, axis, step):
@@ -382,8 +393,7 @@
 
 
 def exchanged(chunks):
-    got = {step: swapped(chunks[step], "seq", step) for step in (3, 1, 2)}
-    return [chunks[0]] + [got[step] for step in range(1, GROUP)]
+    return [chunks[0]] + [swapped(chunk, "seq", step) for step, chunk in zip(STEPS[1:], chunks[1:])]
 
 
 def beside(arrays):
@@ -510,25 +520,24 @@
         flops=1,
     )
     local = rows // N_MP
-    shares = shape(2, local, model)
-    kept, given = call(
+    kept, *given = call(
         project_kernel,
-        [shares] * 2,
+        [shape(2, local, model)] + [shape(local // 2, model)] * 4,
         (*attended, out_weight, grad_q),
         scratch=[pltpu.VMEM((rows, width), BF16), pltpu.VMEM((rows, model), BF16)],
         flops=weight_flops,
     )
+    across, here = call(
+        share_kernel,
+        [shape(local, model), shape(local, model, dtype=F32)],
+        (kept, *(swapped(piece, "mp", 1) for piece in given)),
+    )
     chunks = call(
         functools.partial(combine_kernel, nb, groups),
         [triple] * GROUP,
-        (grad_q, grad_kv, *other_grads),
+        (grad_q, grad_kv, across, *other_grads),
         scratch=[pltpu.VMEM((nb, 2, rows, HEAD_DIM), BF16)],
         flops=20 * score_flops,
-    )
-    across, here = call(
-        share_kernel,
-        [shape(local, model), shape(local, model, dtype=F32)],
-        (kept, swapped(given, "mp", 1), chunks[0]),
     )
     chunks = exchanged(chunks)
     across = swapped(across, "mp", 2)

time: 63.9 us -> 62.1 us (0.972)
  waiting for transfers between devices: 22.1 us -> 17.6 us
  starting transfers between devices: 25.5 us -> 28.1 us
    ppermute x20 -> x23, waiting for transfers between devices: 22.1 us -> 17.6 us  [swapped(): lax.ppermute(x, axis, [(i, i ^ step) for i in range(lax.axis_size(axis))])]
    ppermute x20 -> x23, starting transfers between devices: 25.5 us -> 28.1 us  [swapped(): lax.ppermute(x, axis, [(i, i ^ step) for i in range(lax.axis_size(axis))])]
  transfers between devices with their start and end apart: 20 -> 23, of which waited for: 11 -> 15; matrix products, arithmetic and copies ran while one was open for 0% -> 0% of each run, Pallas kernels for 14% -> 15%
where the time goes in v10:
time: 62.1 us; the launch traced here: 61.8 us
  starting transfers between devices  28.1 us (45%)
  waiting for transfers between devices  17.6 us (28%)
  Pallas kernels  12.5 us (20%)
  local copies, waits for them, and re-layouts  2.85 us (5%)
  between operations  0.76 us (1%)
    ppermute x23, starting transfers between devices, swapped(): lax.ppermute(x, axis, [(i, i ^ step) for i in range(lax.axis_size(axis))])  28.1 us
    ppermute x23, waiting for transfers between devices, swapped(): lax.ppermute(x, axis, [(i, i ^ step) for i in range(lax.axis_size(axis))])  17.6 us
    pallas_call x12, Pallas kernels, call(): pl.pallas_call(kernel, out_shape=out_shape, in_specs=[whole] * len(args),...  12.5 us
    unnamed x8, local copies, waits for them, and re-layouts  2.85 us
  transfers between devices with their start and end apart: 23, of which 15 were waited for; matrix products, arithmetic and copies ran while one was open for 0% of the time, Pallas kernels for 15%

profile of v10, /device:TPU:0, one launch (start us, length us, event | category | flops | bytes accessed | tf_op | source)
XLA Modules:
  0.0 61.8 jit_solution(11271132169234917535)
XLA Ops:
  0.6 3.0 %collective-permute-start = (bf16[64,2048]{1,0:T(8,128)(2,1)}, bf16[64,2048]{1,0:T(8,128)(2,1)S(1)}, u32[]{:S(2)}, u32[]{:S(2)}) collective-permute-start(bf16[64,2048]{1,0:T(8,128)(2,1)} %x.1), channel_id=1, source_target_pairs={{0,2},{1,3},{2,0},{3,1},{4,6},{5,7},{6,4},{7,5},{8,10},{9,11},{10,... | collective-permute-start | bytes 786440 | tf_op jit(solution)/shard_map/ppermute | solution.py:392
  3.6 1.3 %shard_map.85 = (bf16[3,256,128]{2,1,0:T(8,128)(2,1)S(1)}, bf16[3,256,128]{2,1,0:T(8,128)(2,1)S(1)}, bf16[3,256,128]{2,1,0:T(8,128)(2,1)S(1)}, bf16[3,256,128]{2,1,0:T(8,128)(2,1)S(1)}) custom-call(bf16[256,512]{1,0:T(8,128)(2,1)} %q.1, bf16[256,512]{1,0:T(8,128)(2,1)} %k.3, bf16[256,512]{1,0:T(8,128)(2,1)} %v.3), custom_call_target="tpu_custom_call" | custom-call | tf_op jit(solution)/shard_map/pallas_call | solution.py:37
  4.9 2.6 %collective-permute-start.2 = (bf16[3,256,128]{2,1,0:T(8,128)(2,1)S(1)}, bf16[3,256,128]{2,1,0:T(8,128)(2,1)S(1)}, u32[]{:S(2)}, u32[]{:S(2)}) collective-permute-start(bf16[3,256,128]{2,1,0:T(8,128)(2,1)S(1)} %get-tuple-element.53), channel_id=1, source_target_pairs={{0,12},{4,8},{8,4},{12,0},{16,28},{20,24},{24,20},{28,16},{1,13},{... | collective-permute-start | bytes 589832 | tf_op jit(solution)/shard_map/ppermute | solution.py:392
  8.5 0.9 %copy-done.1 = bf16[256,512]{1,0:T(8,128)(2,1)S(1)} copy-done((bf16[256,512]{1,0:T(8,128)(2,1)S(1)}, bf16[256,512]{1,0:T(8,128)(2,1)}, u32[]{:S(2)}) %copy-start.1) | copy-done | bytes 262168
  9.4 0.9 %copy-done.2 = bf16[256,512]{1,0:T(8,128)(2,1)S(1)} copy-done((bf16[256,512]{1,0:T(8,128)(2,1)S(1)}, bf16[256,512]{1,0:T(8,128)(2,1)}, u32[]{:S(2)}) %copy-start.2) | copy-done | bytes 262168
  10.9 2.7 %collective-permute-start.1 = (bf16[4,2,64,128]{3,2,1,0:T(8,128)(2,1)S(1)}, bf16[4,2,64,128]{3,2,1,0:T(8,128)(2,1)S(1)}, u32[]{:S(2)}, u32[]{:S(2)}) collective-permute-start(bf16[4,2,64,128]{3,2,1,0:T(8,128)(2,1)S(1)} %shard_map.84), channel_id=1, source_target_pairs={{0,16},{4,20},{8,24},{12,28},{16,0},{20,4},{24,8},{28,12},{1,17},{... | collective-permute-start | bytes 393224 | tf_op jit(solution)/shard_map/ppermute | solution.py:392
  13.7 0.9 %copy-done.3 = bf16[64,2048]{1,0:T(8,128)(2,1)S(1)} copy-done((bf16[64,2048]{1,0:T(8,128)(2,1)S(1)}, bf16[64,2048]{1,0:T(8,128)(2,1)}, u32[]{:S(2)}) %copy-start.3) | copy-done | bytes 262168
  14.8 3.7 %collective-permute-done.1._.refs_5_ = bf16[4,2,64,128]{3,2,1,0:T(8,128)(2,1)S(1)} collective-permute-done((bf16[4,2,64,128]{3,2,1,0:T(8,128)(2,1)S(1)}, bf16[4,2,64,128]{3,2,1,0:T(8,128)(2,1)S(1)}, u32[]{:S(2)}, u32[]{:S(2)}) %collective-permute-start.1) | collective-permute-done | bytes 131104 | tf_op jit(solution)/shard_map/ppermute | solution.py:392
  18.5 0.9 %collective-permute-done.3.refs_2_ = bf16[3,256,128]{2,1,0:T(8,128)(2,1)S(1)} collective-permute-done((bf16[3,256,128]{2,1,0:T(8,128)(2,1)S(1)}, bf16[3,256,128]{2,1,0:T(8,128)(2,1)S(1)}, u32[]{:S(2)}, u32[]{:S(2)}) %collective-permute-start.3) | collective-permute-done | bytes 196640 | tf_op jit(solution)/shard_map/ppermute | solution.py:392
  19.8 2.6 %collective-permute-start.7 = (bf16[2,256,128]{2,1,0:T(8,128)(2,1)S(1)}, bf16[2,256,128]{2,1,0:T(8,128)(2,1)S(1)}, u32[]{:S(2)}, u32[]{:S(2)}) collective-permute-start(bf16[2,256,128]{2,1,0:T(8,128)(2,1)S(1)} %get-tuple-element.66), channel_id=1, source_target_pairs={{0,16},{4,20},{8,24},{12,28},{16,0},{20,4},{24,8},{28,12},{1,17},{... | collective-permute-start | bytes 393224 | tf_op jit(solution)/shard_map/ppermute | solution.py:392
  23.3 2.1 %collective-permute-start.8 = (bf16[384,128]{1,0:T(8,128)(2,1)S(1)}, bf16[384,128]{1,0:T(8,128)(2,1)S(1)}, u32[]{:S(2)}, u32[]{:S(2)}) collective-permute-start(bf16[384,128]{1,0:T(8,128)(2,1)S(1)} %get-tuple-element.67), channel_id=1, source_target_pairs={{0,12},{4,8},{8,4},{12,0},{16,28},{20,24},{24,20},{28,16},{1,13},{... | collective-permute-start | bytes 294920 | tf_op jit(solution)/shard_map/ppermute | solution.py:392
  25.4 1.5 %collective-permute-start.10 = (bf16[384,128]{1,0:T(8,128)(2,1)S(1)}, bf16[384,128]{1,0:T(8,128)(2,1)S(1)}, u32[]{:S(2)}, u32[]{:S(2)}) collective-permute-start(bf16[384,128]{1,0:T(8,128)(2,1)S(1)} %get-tuple-element.69), channel_id=1, source_target_pairs={{0,4},{4,0},{8,12},{12,8},{16,20},{20,16},{24,28},{28,24},{1,5},{5... | collective-permute-start | bytes 294920 | tf_op jit(solution)/shard_map/ppermute | solution.py:392
  26.9 1.7 %shard_map.89 = (bf16[3,4,256,128]{3,2,1,0:T(8,128)(2,1)S(1)}, bf16[128,1024]{1,0:T(8,128)(2,1)S(1)}, bf16[128,1024]{1,0:T(8,128)(2,1)S(1)}, bf16[128,512]{1,0:T...) custom-call(bf16[4,2,256,128]{3,2,1,0:T(8,128)(2,1)S(1)} %get-tuple-element.56, ...), custom_call_target="tpu_custom_call" | custom-call | flops 335544320 | bytes 6946816 | tf_op jit(solution)/shard_map/pallas_call | solution.py:37
  28.6 1.0 %collective-permute-done.7.refs_5_.refs_11_ = bf16[2,256,128]{2,1,0:T(8,128)(2,1)S(1)} collective-permute-done((bf16[2,256,128]{2,1,0:T(8,128)(2,1)S(1)}, bf16[2,256,128]{2,1,0:T(8,128)(2,1)S(1)}, u32[]{:S(2)}, u32[]{:S(2)}) %collective-permute-start.7) | collective-permute-done | bytes 131104 | tf_op jit(solution)/shard_map/ppermute | solution.py:392
  29.6 1.0 %collective-permute-done.8.refs_7_ = bf16[384,128]{1,0:T(8,128)(2,1)S(1)} collective-permute-done((bf16[384,128]{1,0:T(8,128)(2,1)S(1)}, bf16[384,128]{1,0:T(8,128)(2,1)S(1)}, u32[]{:S(2)}, u32[]{:S(2)}) %collective-permute-start.8) | collective-permute-done | bytes 98336 | tf_op jit(solution)/shard_map/ppermute | solution.py:392
  31.3 2.0 %shard_map.90 = (bf16[4,4,256,256]{3,2,1,0:T(8,128)(2,1)S(1)}, bf16[4,256,128]{2,1,0:T(8,128)(2,1)S(1)}, bf16[2,256,128]{2,1,0:T(8,128)(2,1)S(1)}, f32[8,1024]{1...) custom-call(bf16[3,4,256,128]{3,2,1,0:T(8,128)(2,1)S(1)} %get-tuple-, ...), custom_call_target="tpu_custom_call" | custom-call | flops 335544320 | bytes 9633792 | tf_op jit(solution)/shard_map/pallas_call | solution.py:37
  33.3 2.8 %collective-permute-start.19 = (bf16[4,256,128]{2,1,0:T(8,128)(2,1)S(1)}, bf16[4,256,128]{2,1,0:T(8,128)(2,1)S(1)}, u32[]{:S(2)}, u32[]{:S(2)}) collective-permute-start(bf16[4,256,128]{2,1,0:T(8,128)(2,1)S(1)} %get-tuple-element.91), channel_id=1, source_target_pairs={{0,16},{4,20},{8,24},{12,28},{16,0},{20,4},{24,8},{28,12},{1,17},{... | collective-permute-start | bytes 786440 | tf_op jit(solution)/shard_map/ppermute | solution.py:392
  36.2 3.0 %collective-permute-start.11 = (bf16[256,128]{1,0:T(8,128)(2,1)S(1)}, bf16[256,128]{1,0:T(8,128)(2,1)S(1)}, u32[]{:S(2)}, u32[]{:S(2)}) collective-permute-start(bf16[256,128]{1,0:T(8,128)(2,1)S(1)} %get-tuple-element.71), channel_id=1, source_target_pairs={{0,12},{4,8},{8,4},{12,0},{16,28},{20,24},{24,20},{28,16},{1,13},{... | collective-permute-start | bytes 196616 | tf_op jit(solution)/shard_map/ppermute | solution.py:392
  39.1 1.0 %collective-permute-start.13 = (bf16[256,128]{1,0:T(8,128)(2,1)S(1)}, bf16[256,128]{1,0:T(8,128)(2,1)S(1)}, u32[]{:S(2)}, u32[]{:S(2)}) collective-permute-start(bf16[256,128]{1,0:T(8,128)(2,1)S(1)} %get-tuple-element.73), channel_id=1, source_target_pairs={{0,4},{4,0},{8,12},{12,8},{16,20},{20,16},{24,28},{28,24},{1,5},{5... | collective-permute-start | bytes 196616 | tf_op jit(solution)/shard_map/ppermute | solution.py:392
  40.1 3.3 %shard_map.91 = (bf16[4,256,128]{2,1,0:T(8,128)(2,1)S(1)}, f32[2,4,256,128]{3,2,1,0:T(8,128)S(1)}) custom-call(bf16[3,4,256,128]{3,2,1,0:T(8,128)(2,1)S(1)} %get-tuple-element.61.refs_0_, bf16[4,2,256,128]{3,2,1,0:T(8,128)(2,1)S(1)} %get-tuple-element.56.near.refs_1_, bf16[2,512,128]{2,1,0:T(8,128)(2,1)S(1)} %get-tuple-element.58.level_1.refs_2_, ...), custom_call_target="tpu_custom_call" | custom-call | flops 1 | bytes 6586368 | tf_op jit(solution)/shard_map/pallas_call | solution.py:37
  48.2 3.1 %collective-permute-start.20 = (bf16[3,256,128]{2,1,0:T(8,128)(2,1)S(1)}, bf16[3,256,128]{2,1,0:T(8,128)(2,1)S(1)}, u32[]{:S(2)}, u32[]{:S(2)}) collective-permute-start(bf16[3,256,128]{2,1,0:T(8,128)(2,1)S(1)} %get-tuple-element.93), channel_id=1, source_target_pairs={{0,12},{4,8},{8,4},{12,0},{16,28},{20,24},{24,20},{28,16},{1,13},{... | collective-permute-start | bytes 589832 | tf_op jit(solution)/shard_map/ppermute | solution.py:392
  52.2 4.9 %collective-permute-done.20.refs_3_ = bf16[3,256,128]{2,1,0:T(8,128)(2,1)S(1)} collective-permute-done((bf16[3,256,128]{2,1,0:T(8,128)(2,1)S(1)}, bf16[3,256,128]{2,1,0:T(8,128)(2,1)S(1)}, u32[]{:S(2)}, u32[]{:S(2)}) %collective-permute-start.20) | collective-permute-done | bytes 196640 | tf_op jit(solution)/shard_map/ppermute | solution.py:392
  57.1 3.0 %collective-permute-done.21.refs_4_ = bf16[3,256,128]{2,1,0:T(8,128)(2,1)S(1)} collective-permute-done((bf16[3,256,128]{2,1,0:T(8,128)(2,1)S(1)}, bf16[3,256,128]{2,1,0:T(8,128)(2,1)S(1)}, u32[]{:S(2)}, u32[]{:S(2)}) %collective-permute-start.21) | collective-permute-done | bytes 196640 | tf_op jit(solution)/shard_map/ppermute | solution.py:392
  60.7 1.1 %shard_map.95 = (bf16[256,512]{1,0:T(8,128)(2,1)}, bf16[256,512]{1,0:T(8,128)(2,1)}, bf16[256,512]{1,0:T(8,128)(2,1)}, bf16[64,2048]{1,0:T(8,128)(2,1)}) custom-call(f32[64,2048]{1,0:T(8,128)S(1)} %get-tuple-element.88.refs_0_, bf16[64,2048]{1,0:T(8,128)(2,1)S(1)} %collective-permute-done.18.refs_1_, bf16[3,256,128]{2,1,0:T(8,128)(2,1)S(1)} %get-tuple-element.92.refs_2_, ...), custom_call_target="tpu_custom_call" | custom-call | tf_op jit(solution)/shard_map/pallas_call | solution.py:37
  (42 shorter events, 9.8 us)
Async XLA Ops:
  0.6 21.9 %copy-start = (bf16[512,2048]{1,0:T(8,128)(2,1)S(1)}, bf16[512,2048]{1,0:T(8,128)(2,1)}, u32[]{:S(2)}) copy-start(bf16[512,2048]{1,0:T(8,128)(2,1)} %refs_4_.3) | copy-start | bytes 6291460
  0.6 18.7 %collective-permute-start = (bf16[64,2048]{1,0:T(8,128)(2,1)}, bf16[64,2048]{1,0:T(8,128)(2,1)S(1)}, u32[]{:S(2)}, u32[]{:S(2)}) collective-permute-start(bf16[64,2048]{1,0:T(8,128)(2,1)} %x.1), channel_id=1, source_target_pairs={{0,2},{1,3},{2,0},{3,1},{4,6},{5,7},{6,4},{7,5},{8,10},{9,11},{10,... | collective-permute-start | bytes 786440 | tf_op jit(solution)/shard_map/ppermute | solution.py:392
  4.9 8.8 %collective-permute-start.2 = (bf16[3,256,128]{2,1,0:T(8,128)(2,1)S(1)}, bf16[3,256,128]{2,1,0:T(8,128)(2,1)S(1)}, u32[]{:S(2)}, u32[]{:S(2)}) collective-permute-start(bf16[3,256,128]{2,1,0:T(8,128)(2,1)S(1)} %get-tuple-element.53), channel_id=1, source_target_pairs={{0,12},{4,8},{8,4},{12,0},{16,28},{20,24},{24,20},{28,16},{1,13},{... | collective-permute-start | bytes 589832 | tf_op jit(solution)/shard_map/ppermute | solution.py:392
  7.5 11.8 %collective-permute-start.3 = (bf16[3,256,128]{2,1,0:T(8,128)(2,1)S(1)}, bf16[3,256,128]{2,1,0:T(8,128)(2,1)S(1)}, u32[]{:S(2)}, u32[]{:S(2)}) collective-permute-start(bf16[3,256,128]{2,1,0:T(8,128)(2,1)S(1)} %get-tuple-element.54), channel_id=1, source_target_pairs={{0,8},{4,12},{8,0},{12,4},{16,24},{20,28},{24,16},{28,20},{1,9},{5... | collective-permute-start | bytes 589832 | tf_op jit(solution)/shard_map/ppermute | solution.py:392
  8.0 11.4 %collective-permute-start.4 = (bf16[3,256,128]{2,1,0:T(8,128)(2,1)S(1)}, bf16[3,256,128]{2,1,0:T(8,128)(2,1)S(1)}, u32[]{:S(2)}, u32[]{:S(2)}) collective-permute-start(bf16[3,256,128]{2,1,0:T(8,128)(2,1)S(1)} %get-tuple-element.55), channel_id=1, source_target_pairs={{0,4},{4,0},{8,12},{12,8},{16,20},{20,16},{24,28},{28,24},{1,5},{5... | collective-permute-start | bytes 589832 | tf_op jit(solution)/shard_map/ppermute | solution.py:392
  10.9 7.6 %collective-permute-start.1 = (bf16[4,2,64,128]{3,2,1,0:T(8,128)(2,1)S(1)}, bf16[4,2,64,128]{3,2,1,0:T(8,128)(2,1)S(1)}, u32[]{:S(2)}, u32[]{:S(2)}) collective-permute-start(bf16[4,2,64,128]{3,2,1,0:T(8,128)(2,1)S(1)} %shard_map.84), channel_id=1, source_target_pairs={{0,16},{4,20},{8,24},{12,28},{16,0},{20,4},{24,8},{28,12},{1,17},{... | collective-permute-start | bytes 393224 | tf_op jit(solution)/shard_map/ppermute | solution.py:392
  14.7 7.8 %collective-permute-start.5 = (bf16[64,2048]{1,0:T(8,128)(2,1)S(1)}, bf16[64,2048]{1,0:T(8,128)(2,1)S(1)}, u32[]{:S(2)}, u32[]{:S(2)}) collective-permute-start(bf16[64,2048]{1,0:T(8,128)(2,1)S(1)} %shard_map.87.refs_0_), channel_id=1, source_target_pairs={{0,1},{1,0},{2,3},{3,2},{4,5},{5,4},{6,7},{7,6},{8,9},{9,8},{10,11... | collective-permute-start | bytes 786440 | tf_op jit(solution)/shard_map/ppermute | solution.py:392
  19.8 2.7 %collective-permute-start.6 = (bf16[64,2048]{1,0:T(8,128)(2,1)S(1)}, bf16[64,2048]{1,0:T(8,128)(2,1)S(1)}, u32[]{:S(2)}, u32[]{:S(2)}) collective-permute-start(bf16[64,2048]{1,0:T(8,128)(2,1)S(1)} %get-tuple-element.59.refs_2_), channel_id=1, source_target_pairs={{0,1},{1,0},{2,3},{3,2},{4,5},{5,4},{6,7},{7,6},{8,9},{9,8},{10,11... | collective-permute-start | bytes 786440 | tf_op jit(solution)/shard_map/ppermute | solution.py:392
  19.8 9.7 %collective-permute-start.7 = (bf16[2,256,128]{2,1,0:T(8,128)(2,1)S(1)}, bf16[2,256,128]{2,1,0:T(8,128)(2,1)S(1)}, u32[]{:S(2)}, u32[]{:S(2)}) collective-permute-start(bf16[2,256,128]{2,1,0:T(8,128)(2,1)S(1)} %get-tuple-element.66), channel_id=1, source_target_pairs={{0,16},{4,20},{8,24},{12,28},{16,0},{20,4},{24,8},{28,12},{1,17},{... | collective-permute-start | bytes 393224 | tf_op jit(solution)/shard_map/ppermute | solution.py:392
  23.3 7.3 %collective-permute-start.8 = (bf16[384,128]{1,0:T(8,128)(2,1)S(1)}, bf16[384,128]{1,0:T(8,128)(2,1)S(1)}, u32[]{:S(2)}, u32[]{:S(2)}) collective-permute-start(bf16[384,128]{1,0:T(8,128)(2,1)S(1)} %get-tuple-element.67), channel_id=1, source_target_pairs={{0,12},{4,8},{8,4},{12,0},{16,28},{20,24},{24,20},{28,16},{1,13},{... | collective-permute-start | bytes 294920 | tf_op jit(solution)/shard_map/ppermute | solution.py:392
  25.4 5.5 %collective-permute-start.9 = (bf16[384,128]{1,0:T(8,128)(2,1)S(1)}, bf16[384,128]{1,0:T(8,128)(2,1)S(1)}, u32[]{:S(2)}, u32[]{:S(2)}) collective-permute-start(bf16[384,128]{1,0:T(8,128)(2,1)S(1)} %get-tuple-element.68), channel_id=1, source_target_pairs={{0,8},{4,12},{8,0},{12,4},{16,24},{20,28},{24,16},{28,20},{1,9},{5... | collective-permute-start | bytes 294920 | tf_op jit(solution)/shard_map/ppermute | solution.py:392
  25.4 5.9 %collective-permute-start.10 = (bf16[384,128]{1,0:T(8,128)(2,1)S(1)}, bf16[384,128]{1,0:T(8,128)(2,1)S(1)}, u32[]{:S(2)}, u32[]{:S(2)}) collective-permute-start(bf16[384,128]{1,0:T(8,128)(2,1)S(1)} %get-tuple-element.69), channel_id=1, source_target_pairs={{0,4},{4,0},{8,12},{12,8},{16,20},{20,16},{24,28},{28,24},{1,5},{5... | collective-permute-start | bytes 294920 | tf_op jit(solution)/shard_map/ppermute | solution.py:392
  33.3 14.6 %collective-permute-start.19 = (bf16[4,256,128]{2,1,0:T(8,128)(2,1)S(1)}, bf16[4,256,128]{2,1,0:T(8,128)(2,1)S(1)}, u32[]{:S(2)}, u32[]{:S(2)}) collective-permute-start(bf16[4,256,128]{2,1,0:T(8,128)(2,1)S(1)} %get-tuple-element.91), channel_id=1, source_target_pairs={{0,16},{4,20},{8,24},{12,28},{16,0},{20,4},{24,8},{28,12},{1,17},{... | collective-permute-start | bytes 786440 | tf_op jit(solution)/shard_map/ppermute | solution.py:392
  36.2 7.3 %collective-permute-start.11 = (bf16[256,128]{1,0:T(8,128)(2,1)S(1)}, bf16[256,128]{1,0:T(8,128)(2,1)S(1)}, u32[]{:S(2)}, u32[]{:S(2)}) collective-permute-start(bf16[256,128]{1,0:T(8,128)(2,1)S(1)} %get-tuple-element.71), channel_id=1, source_target_pairs={{0,12},{4,8},{8,4},{12,0},{16,28},{20,24},{24,20},{28,16},{1,13},{... | collective-permute-start | bytes 196616 | tf_op jit(solution)/shard_map/ppermute | solution.py:392
  39.1 5.0 %collective-permute-start.12 = (bf16[256,128]{1,0:T(8,128)(2,1)S(1)}, bf16[256,128]{1,0:T(8,128)(2,1)S(1)}, u32[]{:S(2)}, u32[]{:S(2)}) collective-permute-start(bf16[256,128]{1,0:T(8,128)(2,1)S(1)} %get-tuple-element.72), channel_id=1, source_target_pairs={{0,8},{4,12},{8,0},{12,4},{16,24},{20,28},{24,16},{28,20},{1,9},{5... | collective-permute-start | bytes 196616 | tf_op jit(solution)/shard_map/ppermute | solution.py:392
  39.1 5.0 %collective-permute-start.13 = (bf16[256,128]{1,0:T(8,128)(2,1)S(1)}, bf16[256,128]{1,0:T(8,128)(2,1)S(1)}, u32[]{:S(2)}, u32[]{:S(2)}) collective-permute-start(bf16[256,128]{1,0:T(8,128)(2,1)S(1)} %get-tuple-element.73), channel_id=1, source_target_pairs={{0,4},{4,0},{8,12},{12,8},{16,20},{20,16},{24,28},{28,24},{1,5},{5... | collective-permute-start | bytes 196616 | tf_op jit(solution)/shard_map/ppermute | solution.py:392
  44.9 1.4 %collective-permute-start.14 = (bf16[32,2048]{1,0:T(8,128)(2,1)S(1)}, bf16[32,2048]{1,0:T(8,128)(2,1)S(1)}, u32[]{:S(2)}, u32[]{:S(2)}) collective-permute-start(bf16[32,2048]{1,0:T(8,128)(2,1)S(1)} %get-tuple-element.84), channel_id=1, source_target_pairs={{0,1},{1,0},{2,3},{3,2},{4,5},{5,4},{6,7},{7,6},{8,9},{9,8},{10,11... | collective-permute-start | bytes 393224 | tf_op jit(solution)/shard_map/ppermute | solution.py:392
  45.0 1.5 %collective-permute-start.15 = (bf16[32,2048]{1,0:T(8,128)(2,1)S(1)}, bf16[32,2048]{1,0:T(8,128)(2,1)S(1)}, u32[]{:S(2)}, u32[]{:S(2)}) collective-permute-start(bf16[32,2048]{1,0:T(8,128)(2,1)S(1)} %get-tuple-element.85), channel_id=1, source_target_pairs={{0,1},{1,0},{2,3},{3,2},{4,5},{5,4},{6,7},{7,6},{8,9},{9,8},{10,11... | collective-permute-start | bytes 393224 | tf_op jit(solution)/shard_map/ppermute | solution.py:392
  45.5 1.3 %collective-permute-start.16 = (bf16[32,2048]{1,0:T(8,128)(2,1)S(1)}, bf16[32,2048]{1,0:T(8,128)(2,1)S(1)}, u32[]{:S(2)}, u32[]{:S(2)}) collective-permute-start(bf16[32,2048]{1,0:T(8,128)(2,1)S(1)} %get-tuple-element.86), channel_id=1, source_target_pairs={{0,1},{1,0},{2,3},{3,2},{4,5},{5,4},{6,7},{7,6},{8,9},{9,8},{10,11... | collective-permute-start | bytes 393224 | tf_op jit(solution)/shard_map/ppermute | solution.py:392
  45.6 1.5 %collective-permute-start.17 = (bf16[32,2048]{1,0:T(8,128)(2,1)S(1)}, bf16[32,2048]{1,0:T(8,128)(2,1)S(1)}, u32[]{:S(2)}, u32[]{:S(2)}) collective-permute-start(bf16[32,2048]{1,0:T(8,128)(2,1)S(1)} %get-tuple-element.87), channel_id=1, source_target_pairs={{0,1},{1,0},{2,3},{3,2},{4,5},{5,4},{6,7},{7,6},{8,9},{9,8},{10,11... | collective-permute-start | bytes 393224 | tf_op jit(solution)/shard_map/ppermute | solution.py:392
  47.1 13.6 %collective-permute-start.18 = (bf16[64,2048]{1,0:T(8,128)(2,1)S(1)}, bf16[64,2048]{1,0:T(8,128)(2,1)S(1)}, u32[]{:S(2)}, u32[]{:S(2)}) collective-permute-start(bf16[64,2048]{1,0:T(8,128)(2,1)S(1)} %get-tuple-element.89._), channel_id=1, source_target_pairs={{0,2},{1,3},{2,0},{3,1},{4,6},{5,7},{6,4},{7,5},{8,10},{9,11},{10,... | collective-permute-start | bytes 786440 | tf_op jit(solution)/shard_map/ppermute | solution.py:392
  48.2 8.9 %collective-permute-start.20 = (bf16[3,256,128]{2,1,0:T(8,128)(2,1)S(1)}, bf16[3,256,128]{2,1,0:T(8,128)(2,1)S(1)}, u32[]{:S(2)}, u32[]{:S(2)}) collective-permute-start(bf16[3,256,128]{2,1,0:T(8,128)(2,1)S(1)} %get-tuple-element.93), channel_id=1, source_target_pairs={{0,12},{4,8},{8,4},{12,0},{16,28},{20,24},{24,20},{28,16},{1,13},{... | collective-permute-start | bytes 589832 | tf_op jit(solution)/shard_map/ppermute | solution.py:392
  51.4 8.8 %collective-permute-start.21 = (bf16[3,256,128]{2,1,0:T(8,128)(2,1)S(1)}, bf16[3,256,128]{2,1,0:T(8,128)(2,1)S(1)}, u32[]{:S(2)}, u32[]{:S(2)}) collective-permute-start(bf16[3,256,128]{2,1,0:T(8,128)(2,1)S(1)} %get-tuple-element.94), channel_id=1, source_target_pairs={{0,8},{4,12},{8,0},{12,4},{16,24},{20,28},{24,16},{28,20},{1,9},{5... | collective-permute-start | bytes 589832 | tf_op jit(solution)/shard_map/ppermute | solution.py:392
  51.4 9.3 %collective-permute-start.22 = (bf16[3,256,128]{2,1,0:T(8,128)(2,1)S(1)}, bf16[3,256,128]{2,1,0:T(8,128)(2,1)S(1)}, u32[]{:S(2)}, u32[]{:S(2)}) collective-permute-start(bf16[3,256,128]{2,1,0:T(8,128)(2,1)S(1)} %get-tuple-element.95), channel_id=1, source_target_pairs={{0,4},{4,0},{8,12},{12,8},{16,20},{20,16},{24,28},{28,24},{1,5},{5... | collective-permute-start | bytes 589832 | tf_op jit(solution)/shard_map/ppermute | solution.py:392
  (3 other events, 2.9 us)

commit v11 on v10

--- a/solution.py
+++ b/solution.py
@@ -31,14 +31,15 @@
     return jax.ShapeDtypeStruct(dims, dtype)
 
 
-def call(kernel, out_shape, args, scratch=(), flops=0, limit=32, space=pltpu.VMEM):
-    whole = pl.BlockSpec(memory_space=space)
+def call(kernel, out_shape, args, scratch=(), flops=0, limit=32, copied=0):
+    whole = pl.BlockSpec(memory_space=pltpu.VMEM)
+    kept = pl.BlockSpec(memory_space=pltpu.HBM)
     moved = sum(x.size * x.dtype.itemsize for x in (*args, *out_shape))
     return pl.pallas_call(
         kernel,
         out_shape=out_shape,
-        in_specs=[whole] * len(args),
-        out_specs=[whole] * len(out_shape),
+        in_specs=[kept if copied else whole] * len(args),
+        out_specs=[kept] * copied + [whole] * (len(out_shape) - copied),
         scratch_shapes=scratch,
         compiler_params=pltpu.CompilerParams(vmem_limit_bytes=limit << 20),
         cost_estimate=pl.CostEstimate(flops=flops, bytes_accessed=moved if flops else 0, transcendentals=0),
@@ -100,36 +101,34 @@
 
 
 def pack_kernel(q, k, v, *refs):
-    *outs, sems = refs
-    me = member()
-    copies = []
+    *outs, tops, held, sems = refs
+    me = member()
+    copies = [pltpu.make_async_copy(x, held.at[i], sems.at[i]) for i, x in enumerate((k, v))]
     for step, out in zip(STEPS, outs):
         for part, source in enumerate((k, v, q)):
             piece = source.at[:, columns(me ^ step)]
             copies.append(pltpu.make_async_copy(piece, out.at[part], sems.at[len(copies)]))
     for copy in copies:
         copy.start()
-    for copy in copies:
-        copy.wait()
-
-
-def pool_kernel(k, v, out):
     pool = pooling()
     half = BLOCK // 2
-    for part, source in enumerate((k, v)):
-        once = dot(pool, source[...]).astype(BF16)
+    for part in range(2):
+        copies[part].wait()
+        once = dot(pool, held[part]).astype(BF16)
         twice = dot(pool[: half // 2, :half], once).astype(BF16)
         for head in range(GROUP):
-            out[head, part] = twice[:, head * HEAD_DIM : (head + 1) * HEAD_DIM]
-
-
-def copy_kernel(x, _, out):
-    out[...] = x[...]
-
-
-def gather_kernel(nb, groups, far, _, *refs):
-    chunks, (far_out, near, queries, level_1, *rims) = refs[:GROUP], refs[GROUP:]
-    far_out[...] = far[...]
+            tops[head, part] = twice[:, head * HEAD_DIM : (head + 1) * HEAD_DIM]
+    for copy in copies[2:]:
+        copy.wait()
+
+
+def copy_kernel(x, y, _, x_out, y_out):
+    x_out[...] = x[...]
+    y_out[...] = y[...]
+
+
+def gather_kernel(nb, groups, *refs):
+    chunks, (near, queries, level_1, *rims) = refs[:GROUP], refs[GROUP:]
     me = member()
     for step, chunk in zip(STEPS, chunks):
         near[me ^ step] = chunk[:2]
@@ -435,29 +434,28 @@
 
     chunk = shape(rows, HEAD_DIM)
     triple = shape(3, rows, HEAD_DIM)
-    chunks = call(
+    *chunks, tops = call(
         pack_kernel,
-        [triple] * GROUP,
+        [triple] * GROUP + [shape(GROUP, 2, quarter, HEAD_DIM)],
         (queries, keys, values),
-        scratch=[pltpu.SemaphoreType.DMA((3 * GROUP,))],
-        space=pltpu.HBM,
+        scratch=[pltpu.VMEM((2, rows, width), BF16), pltpu.SemaphoreType.DMA((2 + 3 * GROUP,))],
+        copied=GROUP,
         limit=53,
     )
     far = swapped(out_grad, "mp", 2)
     chunks = exchanged(chunks)
-    (tops,) = call(pool_kernel, [shape(GROUP, 2, quarter, HEAD_DIM)], (keys, values))
     tops = swapped(tops, "seq", GROUP)
-    (own_grad,) = call(copy_kernel, [shape(*out_grad.shape)], (out_grad, chunks[1]))
-    far, near, queries, level_1, *refs = call(
+    own_grad, far = call(copy_kernel, [shape(*out_grad.shape)] * 2, (out_grad, far, chunks[1]))
+    near, queries, level_1, *refs = call(
         functools.partial(gather_kernel, nb, groups),
         [
-            shape(*out_grad.shape),
             shape(nb, 2, rows, HEAD_DIM),
             shape(nb, rows, HEAD_DIM),
             shape(2, tokens // 2, HEAD_DIM),
         ]
         + rims,
-        (far, tops, *chunks),
+        chunks,
+        flops=20 * score_flops,
     )
     rim_blocks = beside(refs)
     grad_chunks = call(

time: 62.1 us -> 60.5 us (0.974)
  waiting for transfers between devices: 17.6 us -> 19.6 us
  local copies, waits for them, and re-layouts: 2.85 us -> 0.95 us
  starting transfers between devices: 28.1 us -> 26.6 us
    ppermute x23, waiting for transfers between devices: 17.6 us -> 19.6 us  [swapped(): lax.ppermute(x, axis, [(i, i ^ step) for i in range(lax.axis_size(axis))])]
    unnamed x8 -> x4, local copies, waits for them, and re-layouts: 2.85 us -> 0.95 us
    ppermute x23, starting transfers between devices: 28.1 us -> 26.6 us  [swapped(): lax.ppermute(x, axis, [(i, i ^ step) for i in range(lax.axis_size(axis))])]
    pallas_call x12 -> x11, Pallas kernels: 12.5 us -> 12.4 us  [call(): pl.pallas_call(kernel, out_shape=out_shape, in_specs=[kept if copied else...]
  transfers between devices with their start and end apart: 23 -> 23, of which waited for: 15 -> 13; matrix products, arithmetic and copies ran while one was open for 0% -> 0% of each run, Pallas kernels for 15% -> 15%
where the time goes in v11:
time: 60.5 us; the launch traced here: 60.3 us
  starting transfers between devices  26.6 us (44%)
  waiting for transfers between devices  19.6 us (32%)
  Pallas kernels  12.4 us (20%)
  local copies, waits for them, and re-layouts  0.95 us (2%)
  between operations  0.74 us (1%)
    ppermute x23, starting transfers between devices, swapped(): lax.ppermute(x, axis, [(i, i ^ step) for i in range(lax.axis_size(axis))])  26.6 us
    ppermute x23, waiting for transfers between devices, swapped(): lax.ppermute(x, axis, [(i, i ^ step) for i in range(lax.axis_size(axis))])  19.6 us
    pallas_call x11, Pallas kernels, call(): pl.pallas_call(kernel, out_shape=out_shape, in_specs=[kept if copied else...  12.4 us
  transfers between devices with their start and end apart: 23, of which 13 were waited for; matrix products, arithmetic and copies ran while one was open for 0% of the time, Pallas kernels for 15%

profile of v11, /device:TPU:0, one launch (start us, length us, event | category | flops | bytes accessed | tf_op | source)
XLA Modules:
  0.0 60.3 jit_solution(14824748613075901173)
XLA Ops:
  0.6 3.0 %collective-permute-start.3 = (bf16[64,2048]{1,0:T(8,128)(2,1)}, bf16[64,2048]{1,0:T(8,128)(2,1)S(1)}, u32[]{:S(2)}, u32[]{:S(2)}) collective-permute-start(bf16[64,2048]{1,0:T(8,128)(2,1)} %x.1), channel_id=1, source_target_pairs={{0,2},{1,3},{2,0},{3,1},{4,6},{5,7},{6,4},{7,5},{8,10},{9,11},{10,... | collective-permute-start | bytes 786440 | tf_op jit(solution)/shard_map/ppermute | solution.py:391
  3.6 1.7 %shard_map.84 = (bf16[3,256,128]{2,1,0:T(8,128)(2,1)S(1)}, bf16[3,256,128]{2,1,0:T(8,128)(2,1)S(1)}, bf16[3,256,128]{2,1,0:T(8,128)(2,1)S(1)}, bf16[3,256,128]{2...) custom-call(bf16[256,512]{1,0:T(8,128)(2,1)} %q.1, bf16[256,512]{1,0:T(8,128)(2,1)} %k.1, bf16[256,512]{1,0:T(8,128)(2,1)} %v.1), custom_call_target="tpu_custom_call" | custom-call | tf_op jit(solution)/shard_map/pallas_call | solution.py:38
  5.4 2.6 %collective-permute-start = (bf16[3,256,128]{2,1,0:T(8,128)(2,1)S(1)}, bf16[3,256,128]{2,1,0:T(8,128)(2,1)S(1)}, u32[]{:S(2)}, u32[]{:S(2)}) collective-permute-start(bf16[3,256,128]{2,1,0:T(8,128)(2,1)S(1)} %get-tuple-element.55), channel_id=1, source_target_pairs={{0,12},{4,8},{8,4},{12,0},{16,28},{20,24},{24,20},{28,16},{1,13},{... | collective-permute-start | bytes 589832 | tf_op jit(solution)/shard_map/ppermute | solution.py:391
  8.9 2.6 %collective-permute-start.6 = (bf16[4,2,64,128]{3,2,1,0:T(8,128)(2,1)S(1)}, bf16[4,2,64,128]{3,2,1,0:T(8,128)(2,1)S(1)}, u32[]{:S(2)}, u32[]{:S(2)}) collective-permute-start(bf16[4,2,64,128]{3,2,1,0:T(8,128)(2,1)S(1)} %get-tuple-element.63), channel_id=1, source_target_pairs={{0,16},{4,20},{8,24},{12,28},{16,0},{20,4},{24,8},{28,12},{1,17},{... | collective-permute-start | bytes 393224 | tf_op jit(solution)/shard_map/ppermute | solution.py:391
  11.5 5.5 %collective-permute-done.refs_1_._ = bf16[3,256,128]{2,1,0:T(8,128)(2,1)S(1)} collective-permute-done((bf16[3,256,128]{2,1,0:T(8,128)(2,1)S(1)}, bf16[3,256,128]{2,1,0:T(8,128)(2,1)S(1)}, u32[]{:S(2)}, u32[]{:S(2)}) %collective-permute-start) | collective-permute-done | bytes 196640 | tf_op jit(solution)/shard_map/ppermute | solution.py:391
  17.0 0.9 %copy-done.1 = bf16[64,2048]{1,0:T(8,128)(2,1)S(1)} copy-done((bf16[64,2048]{1,0:T(8,128)(2,1)S(1)}, bf16[64,2048]{1,0:T(8,128)(2,1)}, u32[]{:S(2)}) %copy-start.1) | copy-done | bytes 262168
  18.6 1.3 %collective-permute-done.1.refs_2_ = bf16[3,256,128]{2,1,0:T(8,128)(2,1)S(1)} collective-permute-done((bf16[3,256,128]{2,1,0:T(8,128)(2,1)S(1)}, bf16[3,256,128]{2,1,0:T(8,128)(2,1)S(1)}, u32[]{:S(2)}, u32[]{:S(2)}) %collective-permute-start.1) | collective-permute-done | bytes 196640 | tf_op jit(solution)/shard_map/ppermute | solution.py:391
  20.2 1.8 %collective-permute-start.7 = (bf16[2,256,128]{2,1,0:T(8,128)(2,1)S(1)}, bf16[2,256,128]{2,1,0:T(8,128)(2,1)S(1)}, u32[]{:S(2)}, u32[]{:S(2)}) collective-permute-start(bf16[2,256,128]{2,1,0:T(8,128)(2,1)S(1)} %get-tuple-element.70), channel_id=1, source_target_pairs={{0,16},{4,20},{8,24},{12,28},{16,0},{20,4},{24,8},{28,12},{1,17},{... | collective-permute-start | bytes 393224 | tf_op jit(solution)/shard_map/ppermute | solution.py:391
  22.0 0.8 %shard_map.87 = (bf16[384,128]{1,0:T(8,128)(2,1)S(1)}, bf16[384,128]{1,0:T(8,128)(2,1)S(1)}, bf16[384,128]{1,0:T(8,128)(2,1)S(1)}, bf16[384,128]{1,0:T(8,128)(2,1)S(1)}) custom-call(bf16[64,2048]{1,0:T(8,128)(2,1)S(1)} %get-tuple-element.61.refs_0_, bf16[64,2048]{1,0:T(8,128)(2,1)S(1)} %collective-permute-done.4.refs_1_, ...), custom_call_target="tpu_custom_call" | custom-call | flops 536870912 | bytes 3670016 | tf_op jit(solution)/shard_map/pallas_call | solution.py:38
  22.8 2.5 %collective-permute-start.8 = (bf16[384,128]{1,0:T(8,128)(2,1)S(1)}, bf16[384,128]{1,0:T(8,128)(2,1)S(1)}, u32[]{:S(2)}, u32[]{:S(2)}) collective-permute-start(bf16[384,128]{1,0:T(8,128)(2,1)S(1)} %get-tuple-element.71), channel_id=1, source_target_pairs={{0,12},{4,8},{8,4},{12,0},{16,28},{20,24},{24,20},{28,16},{1,13},{... | collective-permute-start | bytes 294920 | tf_op jit(solution)/shard_map/ppermute | solution.py:391
  25.5 1.4 %collective-permute-start.10 = (bf16[384,128]{1,0:T(8,128)(2,1)S(1)}, bf16[384,128]{1,0:T(8,128)(2,1)S(1)}, u32[]{:S(2)}, u32[]{:S(2)}) collective-permute-start(bf16[384,128]{1,0:T(8,128)(2,1)S(1)} %get-tuple-element.73), channel_id=1, source_target_pairs={{0,4},{4,0},{8,12},{12,8},{16,20},{20,16},{24,28},{28,24},{1,5},{5... | collective-permute-start | bytes 294920 | tf_op jit(solution)/shard_map/ppermute | solution.py:391
  26.9 1.7 %shard_map.88 = (bf16[3,4,256,128]{3,2,1,0:T(8,128)(2,1)S(1)}, bf16[128,1024]{1,0:T(8,128)(2,1)S(1)}, bf16[128,1024]{1,0:T(8,128)(2,1)S(1)}, bf16[128,512]{1,0:T...) custom-call(bf16[4,2,256,128]{3,2,1,0:T(8,128)(2,1)S(1)} %get-tuple-element.58, ...), custom_call_target="tpu_custom_call" | custom-call | flops 335544320 | bytes 6946816 | tf_op jit(solution)/shard_map/pallas_call | solution.py:38
  28.5 2.4 %collective-permute-done.8.refs_7_ = bf16[384,128]{1,0:T(8,128)(2,1)S(1)} collective-permute-done((bf16[384,128]{1,0:T(8,128)(2,1)S(1)}, bf16[384,128]{1,0:T(8,128)(2,1)S(1)}, u32[]{:S(2)}, u32[]{:S(2)}) %collective-permute-start.8) | collective-permute-done | bytes 98336 | tf_op jit(solution)/shard_map/ppermute | solution.py:391
  30.9 2.0 %shard_map.89 = (bf16[4,4,256,256]{3,2,1,0:T(8,128)(2,1)S(1)}, bf16[4,256,128]{2,1,0:T(8,128)(2,1)S(1)}, bf16[2,256,128]{2,1,0:T(8,128)(2,1)S(1)}, f32[8,1024]{1...) custom-call(bf16[3,4,256,128]{3,2,1,0:T(8,128)(2,1)S(1)} %get-tuple-, ...), custom_call_target="tpu_custom_call" | custom-call | flops 335544320 | bytes 9633792 | tf_op jit(solution)/shard_map/pallas_call | solution.py:38
  32.9 1.9 %collective-permute-start.19 = (bf16[4,256,128]{2,1,0:T(8,128)(2,1)S(1)}, bf16[4,256,128]{2,1,0:T(8,128)(2,1)S(1)}, u32[]{:S(2)}, u32[]{:S(2)}) collective-permute-start(bf16[4,256,128]{2,1,0:T(8,128)(2,1)S(1)} %get-tuple-element.95), channel_id=1, source_target_pairs={{0,16},{4,20},{8,24},{12,28},{16,0},{20,4},{24,8},{28,12},{1,17},{... | collective-permute-start | bytes 786440 | tf_op jit(solution)/shard_map/ppermute | solution.py:391
  34.8 3.0 %collective-permute-start.11 = (bf16[256,128]{1,0:T(8,128)(2,1)S(1)}, bf16[256,128]{1,0:T(8,128)(2,1)S(1)}, u32[]{:S(2)}, u32[]{:S(2)}) collective-permute-start(bf16[256,128]{1,0:T(8,128)(2,1)S(1)} %get-tuple-element.75), channel_id=1, source_target_pairs={{0,12},{4,8},{8,4},{12,0},{16,28},{20,24},{24,20},{28,16},{1,13},{... | collective-permute-start | bytes 196616 | tf_op jit(solution)/shard_map/ppermute | solution.py:391
  37.8 1.0 %collective-permute-start.13 = (bf16[256,128]{1,0:T(8,128)(2,1)S(1)}, bf16[256,128]{1,0:T(8,128)(2,1)S(1)}, u32[]{:S(2)}, u32[]{:S(2)}) collective-permute-start(bf16[256,128]{1,0:T(8,128)(2,1)S(1)} %get-tuple-element.77), channel_id=1, source_target_pairs={{0,4},{4,0},{8,12},{12,8},{16,20},{20,16},{24,28},{28,24},{1,5},{5... | collective-permute-start | bytes 196616 | tf_op jit(solution)/shard_map/ppermute | solution.py:391
  38.7 3.4 %shard_map.90 = (bf16[4,256,128]{2,1,0:T(8,128)(2,1)S(1)}, f32[2,4,256,128]{3,2,1,0:T(8,128)S(1)}) custom-call(bf16[3,4,256,128]{3,2,1,0:T(8,128)(2,1)S(1)} %get-tuple-element.65.refs_0_, bf16[4,2,256,128]{3,2,1,0:T(8,128)(2,1)S(1)} %get-tuple-element.58.near.refs_1_, bf16[2,512,128]{2,1,0:T(8,128)(2,1)S(1)} %get-tuple-element.60.level_1.refs_2_, ...), custom_call_target="tpu_custom_call" | custom-call | flops 1 | bytes 6586368 | tf_op jit(solution)/shard_map/pallas_call | solution.py:38
  42.9 0.8 %shard_map.91 = (bf16[2,64,2048]{2,1,0:T(8,128)(2,1)S(1)}, bf16[32,2048]{1,0:T(8,128)(2,1)S(1)}, bf16[32,2048]{1,0:T(8,128)(2,1)S(1)}, bf16[32,2048]{1,0:T(8,128)(2,1)S(1)}, bf16[32,2048]{1,0:T(8,128)(2,1)S(1)}) custom-call(bf16[256,128]{1,0:T(8,128)(2,1)S(1)} %get-tuple-element.74.refs_0_, bf16[256,128]{1,0:T(8,128)(2,1)S(1)} %collective-permute-done.11.refs_1_, ...), custom_call_target="tpu_custom_call" | custom-call | flops 536870912 | bytes 3670016 | tf_op jit(solution)/shard_map/pallas_call | solution.py:38
  47.2 2.7 %collective-permute-start.20 = (bf16[3,256,128]{2,1,0:T(8,128)(2,1)S(1)}, bf16[3,256,128]{2,1,0:T(8,128)(2,1)S(1)}, u32[]{:S(2)}, u32[]{:S(2)}) collective-permute-start(bf16[3,256,128]{2,1,0:T(8,128)(2,1)S(1)} %get-tuple-element.97), channel_id=1, source_target_pairs={{0,12},{4,8},{8,4},{12,0},{16,28},{20,24},{24,20},{28,16},{1,13},{... | collective-permute-start | bytes 589832 | tf_op jit(solution)/shard_map/ppermute | solution.py:391
  50.1 0.8 %collective-permute-start.22 = (bf16[3,256,128]{2,1,0:T(8,128)(2,1)S(1)}, bf16[3,256,128]{2,1,0:T(8,128)(2,1)S(1)}, u32[]{:S(2)}, u32[]{:S(2)}) collective-permute-start(bf16[3,256,128]{2,1,0:T(8,128)(2,1)S(1)} %get-tuple-element.99), channel_id=1, source_target_pairs={{0,4},{4,0},{8,12},{12,8},{16,20},{20,16},{24,28},{28,24},{1,5},{5... | collective-permute-start | bytes 589832 | tf_op jit(solution)/shard_map/ppermute | solution.py:391
  50.9 5.1 %collective-permute-done.20.refs_3_ = bf16[3,256,128]{2,1,0:T(8,128)(2,1)S(1)} collective-permute-done((bf16[3,256,128]{2,1,0:T(8,128)(2,1)S(1)}, bf16[3,256,128]{2,1,0:T(8,128)(2,1)S(1)}, u32[]{:S(2)}, u32[]{:S(2)}) %collective-permute-start.20) | collective-permute-done | bytes 196640 | tf_op jit(solution)/shard_map/ppermute | solution.py:391
  56.0 2.7 %collective-permute-done.21.refs_4_ = bf16[3,256,128]{2,1,0:T(8,128)(2,1)S(1)} collective-permute-done((bf16[3,256,128]{2,1,0:T(8,128)(2,1)S(1)}, bf16[3,256,128]{2,1,0:T(8,128)(2,1)S(1)}, u32[]{:S(2)}, u32[]{:S(2)}) %collective-permute-start.21) | collective-permute-done | bytes 196640 | tf_op jit(solution)/shard_map/ppermute | solution.py:391
  59.2 1.1 %shard_map.94 = (bf16[256,512]{1,0:T(8,128)(2,1)}, bf16[256,512]{1,0:T(8,128)(2,1)}, bf16[256,512]{1,0:T(8,128)(2,1)}, bf16[64,2048]{1,0:T(8,128)(2,1)}) custom-call(f32[64,2048]{1,0:T(8,128)S(1)} %get-tuple-element.92.refs_0_, bf16[64,2048]{1,0:T(8,128)(2,1)S(1)} %collective-permute-done.18.refs_1_, bf16[3,256,128]{2,1,0:T(8,128)(2,1)S(1)} %get-tuple-element.96.refs_2_, ...), custom_call_target="tpu_custom_call" | custom-call | tf_op jit(solution)/shard_map/pallas_call | solution.py:38
  (37 shorter events, 7.1 us)
Async XLA Ops:
  0.6 16.4 %collective-permute-start.3 = (bf16[64,2048]{1,0:T(8,128)(2,1)}, bf16[64,2048]{1,0:T(8,128)(2,1)S(1)}, u32[]{:S(2)}, u32[]{:S(2)}) collective-permute-start(bf16[64,2048]{1,0:T(8,128)(2,1)} %x.1), channel_id=1, source_target_pairs={{0,2},{1,3},{2,0},{3,1},{4,6},{5,7},{6,4},{7,5},{8,10},{9,11},{10,... | collective-permute-start | bytes 786440 | tf_op jit(solution)/shard_map/ppermute | solution.py:391
  5.4 11.6 %collective-permute-start = (bf16[3,256,128]{2,1,0:T(8,128)(2,1)S(1)}, bf16[3,256,128]{2,1,0:T(8,128)(2,1)S(1)}, u32[]{:S(2)}, u32[]{:S(2)}) collective-permute-start(bf16[3,256,128]{2,1,0:T(8,128)(2,1)S(1)} %get-tuple-element.55), channel_id=1, source_target_pairs={{0,12},{4,8},{8,4},{12,0},{16,28},{20,24},{24,20},{28,16},{1,13},{... | collective-permute-start | bytes 589832 | tf_op jit(solution)/shard_map/ppermute | solution.py:391
  8.0 11.8 %collective-permute-start.1 = (bf16[3,256,128]{2,1,0:T(8,128)(2,1)S(1)}, bf16[3,256,128]{2,1,0:T(8,128)(2,1)S(1)}, u32[]{:S(2)}, u32[]{:S(2)}) collective-permute-start(bf16[3,256,128]{2,1,0:T(8,128)(2,1)S(1)} %get-tuple-element.56), channel_id=1, source_target_pairs={{0,8},{4,12},{8,0},{12,4},{16,24},{20,28},{24,16},{28,20},{1,9},{5... | collective-permute-start | bytes 589832 | tf_op jit(solution)/shard_map/ppermute | solution.py:391
  8.4 11.4 %collective-permute-start.2 = (bf16[3,256,128]{2,1,0:T(8,128)(2,1)S(1)}, bf16[3,256,128]{2,1,0:T(8,128)(2,1)S(1)}, u32[]{:S(2)}, u32[]{:S(2)}) collective-permute-start(bf16[3,256,128]{2,1,0:T(8,128)(2,1)S(1)} %get-tuple-element.57), channel_id=1, source_target_pairs={{0,4},{4,0},{8,12},{12,8},{16,20},{20,16},{24,28},{28,24},{1,5},{5... | collective-permute-start | bytes 589832 | tf_op jit(solution)/shard_map/ppermute | solution.py:391
  8.9 13.0 %collective-permute-start.6 = (bf16[4,2,64,128]{3,2,1,0:T(8,128)(2,1)S(1)}, bf16[4,2,64,128]{3,2,1,0:T(8,128)(2,1)S(1)}, u32[]{:S(2)}, u32[]{:S(2)}) collective-permute-start(bf16[4,2,64,128]{3,2,1,0:T(8,128)(2,1)S(1)} %get-tuple-element.63), channel_id=1, source_target_pairs={{0,16},{4,20},{8,24},{12,28},{16,0},{20,4},{24,8},{28,12},{1,17},{... | collective-permute-start | bytes 393224 | tf_op jit(solution)/shard_map/ppermute | solution.py:391
  18.0 4.0 %collective-permute-start.4 = (bf16[64,2048]{1,0:T(8,128)(2,1)S(1)}, bf16[64,2048]{1,0:T(8,128)(2,1)S(1)}, u32[]{:S(2)}, u32[]{:S(2)}) collective-permute-start(bf16[64,2048]{1,0:T(8,128)(2,1)S(1)} %get-tuple-element.61.refs_0_), channel_id=1, source_target_pairs={{0,1},{1,0},{2,3},{3,2},{4,5},{5,4},{6,7},{7,6},{8,9},{9,8},{10,11... | collective-permute-start | bytes 786440 | tf_op jit(solution)/shard_map/ppermute | solution.py:391
  18.1 3.9 %collective-permute-start.5 = (bf16[64,2048]{1,0:T(8,128)(2,1)S(1)}, bf16[64,2048]{1,0:T(8,128)(2,1)S(1)}, u32[]{:S(2)}, u32[]{:S(2)}) collective-permute-start(bf16[64,2048]{1,0:T(8,128)(2,1)S(1)} %get-tuple-element.62.refs_2_), channel_id=1, source_target_pairs={{0,1},{1,0},{2,3},{3,2},{4,5},{5,4},{6,7},{7,6},{8,9},{9,8},{10,11... | collective-permute-start | bytes 786440 | tf_op jit(solution)/shard_map/ppermute | solution.py:391
  19.8 2.1 %copy-start = (bf16[512,2048]{1,0:T(8,128)(2,1)S(1)}, bf16[512,2048]{1,0:T(8,128)(2,1)}, u32[]{:S(2)}) copy-start(bf16[512,2048]{1,0:T(8,128)(2,1)} %refs_4_.3) | copy-start | bytes 6291460
  20.2 8.3 %collective-permute-start.7 = (bf16[2,256,128]{2,1,0:T(8,128)(2,1)S(1)}, bf16[2,256,128]{2,1,0:T(8,128)(2,1)S(1)}, u32[]{:S(2)}, u32[]{:S(2)}) collective-permute-start(bf16[2,256,128]{2,1,0:T(8,128)(2,1)S(1)} %get-tuple-element.70), channel_id=1, source_target_pairs={{0,16},{4,20},{8,24},{12,28},{16,0},{20,4},{24,8},{28,12},{1,17},{... | collective-permute-start | bytes 393224 | tf_op jit(solution)/shard_map/ppermute | solution.py:391
  22.8 8.1 %collective-permute-start.8 = (bf16[384,128]{1,0:T(8,128)(2,1)S(1)}, bf16[384,128]{1,0:T(8,128)(2,1)S(1)}, u32[]{:S(2)}, u32[]{:S(2)}) collective-permute-start(bf16[384,128]{1,0:T(8,128)(2,1)S(1)} %get-tuple-element.71), channel_id=1, source_target_pairs={{0,12},{4,8},{8,4},{12,0},{16,28},{20,24},{24,20},{28,16},{1,13},{... | collective-permute-start | bytes 294920 | tf_op jit(solution)/shard_map/ppermute | solution.py:391
  25.3 5.6 %collective-permute-start.9 = (bf16[384,128]{1,0:T(8,128)(2,1)S(1)}, bf16[384,128]{1,0:T(8,128)(2,1)S(1)}, u32[]{:S(2)}, u32[]{:S(2)}) collective-permute-start(bf16[384,128]{1,0:T(8,128)(2,1)S(1)} %get-tuple-element.72), channel_id=1, source_target_pairs={{0,8},{4,12},{8,0},{12,4},{16,24},{20,28},{24,16},{28,20},{1,9},{5... | collective-permute-start | bytes 294920 | tf_op jit(solution)/shard_map/ppermute | solution.py:391
  25.5 5.4 %collective-permute-start.10 = (bf16[384,128]{1,0:T(8,128)(2,1)S(1)}, bf16[384,128]{1,0:T(8,128)(2,1)S(1)}, u32[]{:S(2)}, u32[]{:S(2)}) collective-permute-start(bf16[384,128]{1,0:T(8,128)(2,1)S(1)} %get-tuple-element.73), channel_id=1, source_target_pairs={{0,4},{4,0},{8,12},{12,8},{16,20},{20,16},{24,28},{28,24},{1,5},{5... | collective-permute-start | bytes 294920 | tf_op jit(solution)/shard_map/ppermute | solution.py:391
  32.9 14.0 %collective-permute-start.19 = (bf16[4,256,128]{2,1,0:T(8,128)(2,1)S(1)}, bf16[4,256,128]{2,1,0:T(8,128)(2,1)S(1)}, u32[]{:S(2)}, u32[]{:S(2)}) collective-permute-start(bf16[4,256,128]{2,1,0:T(8,128)(2,1)S(1)} %get-tuple-element.95), channel_id=1, source_target_pairs={{0,16},{4,20},{8,24},{12,28},{16,0},{20,4},{24,8},{28,12},{1,17},{... | collective-permute-start | bytes 786440 | tf_op jit(solution)/shard_map/ppermute | solution.py:391
  34.8 7.4 %collective-permute-start.11 = (bf16[256,128]{1,0:T(8,128)(2,1)S(1)}, bf16[256,128]{1,0:T(8,128)(2,1)S(1)}, u32[]{:S(2)}, u32[]{:S(2)}) collective-permute-start(bf16[256,128]{1,0:T(8,128)(2,1)S(1)} %get-tuple-element.75), channel_id=1, source_target_pairs={{0,12},{4,8},{8,4},{12,0},{16,28},{20,24},{24,20},{28,16},{1,13},{... | collective-permute-start | bytes 196616 | tf_op jit(solution)/shard_map/ppermute | solution.py:391
  37.8 5.1 %collective-permute-start.12 = (bf16[256,128]{1,0:T(8,128)(2,1)S(1)}, bf16[256,128]{1,0:T(8,128)(2,1)S(1)}, u32[]{:S(2)}, u32[]{:S(2)}) collective-permute-start(bf16[256,128]{1,0:T(8,128)(2,1)S(1)} %get-tuple-element.76), channel_id=1, source_target_pairs={{0,8},{4,12},{8,0},{12,4},{16,24},{20,28},{24,16},{28,20},{1,9},{5... | collective-permute-start | bytes 196616 | tf_op jit(solution)/shard_map/ppermute | solution.py:391
  37.8 5.1 %collective-permute-start.13 = (bf16[256,128]{1,0:T(8,128)(2,1)S(1)}, bf16[256,128]{1,0:T(8,128)(2,1)S(1)}, u32[]{:S(2)}, u32[]{:S(2)}) collective-permute-start(bf16[256,128]{1,0:T(8,128)(2,1)S(1)} %get-tuple-element.77), channel_id=1, source_target_pairs={{0,4},{4,0},{8,12},{12,8},{16,20},{20,16},{24,28},{28,24},{1,5},{5... | collective-permute-start | bytes 196616 | tf_op jit(solution)/shard_map/ppermute | solution.py:391
  43.7 1.4 %collective-permute-start.14 = (bf16[32,2048]{1,0:T(8,128)(2,1)S(1)}, bf16[32,2048]{1,0:T(8,128)(2,1)S(1)}, u32[]{:S(2)}, u32[]{:S(2)}) collective-permute-start(bf16[32,2048]{1,0:T(8,128)(2,1)S(1)} %get-tuple-element.88), channel_id=1, source_target_pairs={{0,1},{1,0},{2,3},{3,2},{4,5},{5,4},{6,7},{7,6},{8,9},{9,8},{10,11... | collective-permute-start | bytes 393224 | tf_op jit(solution)/shard_map/ppermute | solution.py:391
  43.8 1.5 %collective-permute-start.15 = (bf16[32,2048]{1,0:T(8,128)(2,1)S(1)}, bf16[32,2048]{1,0:T(8,128)(2,1)S(1)}, u32[]{:S(2)}, u32[]{:S(2)}) collective-permute-start(bf16[32,2048]{1,0:T(8,128)(2,1)S(1)} %get-tuple-element.89), channel_id=1, source_target_pairs={{0,1},{1,0},{2,3},{3,2},{4,5},{5,4},{6,7},{7,6},{8,9},{9,8},{10,11... | collective-permute-start | bytes 393224 | tf_op jit(solution)/shard_map/ppermute | solution.py:391
  44.3 1.3 %collective-permute-start.16 = (bf16[32,2048]{1,0:T(8,128)(2,1)S(1)}, bf16[32,2048]{1,0:T(8,128)(2,1)S(1)}, u32[]{:S(2)}, u32[]{:S(2)}) collective-permute-start(bf16[32,2048]{1,0:T(8,128)(2,1)S(1)} %get-tuple-element.90), channel_id=1, source_target_pairs={{0,1},{1,0},{2,3},{3,2},{4,5},{5,4},{6,7},{7,6},{8,9},{9,8},{10,11... | collective-permute-start | bytes 393224 | tf_op jit(solution)/shard_map/ppermute | solution.py:391
  44.4 1.5 %collective-permute-start.17 = (bf16[32,2048]{1,0:T(8,128)(2,1)S(1)}, bf16[32,2048]{1,0:T(8,128)(2,1)S(1)}, u32[]{:S(2)}, u32[]{:S(2)}) collective-permute-start(bf16[32,2048]{1,0:T(8,128)(2,1)S(1)} %get-tuple-element.91), channel_id=1, source_target_pairs={{0,1},{1,0},{2,3},{3,2},{4,5},{5,4},{6,7},{7,6},{8,9},{9,8},{10,11... | collective-permute-start | bytes 393224 | tf_op jit(solution)/shard_map/ppermute | solution.py:391
  45.9 13.3 %collective-permute-start.18 = (bf16[64,2048]{1,0:T(8,128)(2,1)S(1)}, bf16[64,2048]{1,0:T(8,128)(2,1)S(1)}, u32[]{:S(2)}, u32[]{:S(2)}) collective-permute-start(bf16[64,2048]{1,0:T(8,128)(2,1)S(1)} %get-tuple-element.93._), channel_id=1, source_target_pairs={{0,2},{1,3},{2,0},{3,1},{4,6},{5,7},{6,4},{7,5},{8,10},{9,11},{10,... | collective-permute-start | bytes 786440 | tf_op jit(solution)/shard_map/ppermute | solution.py:391
  47.2 8.8 %collective-permute-start.20 = (bf16[3,256,128]{2,1,0:T(8,128)(2,1)S(1)}, bf16[3,256,128]{2,1,0:T(8,128)(2,1)S(1)}, u32[]{:S(2)}, u32[]{:S(2)}) collective-permute-start(bf16[3,256,128]{2,1,0:T(8,128)(2,1)S(1)} %get-tuple-element.97), channel_id=1, source_target_pairs={{0,12},{4,8},{8,4},{12,0},{16,28},{20,24},{24,20},{28,16},{1,13},{... | collective-permute-start | bytes 589832 | tf_op jit(solution)/shard_map/ppermute | solution.py:391
  49.9 8.8 %collective-permute-start.21 = (bf16[3,256,128]{2,1,0:T(8,128)(2,1)S(1)}, bf16[3,256,128]{2,1,0:T(8,128)(2,1)S(1)}, u32[]{:S(2)}, u32[]{:S(2)}) collective-permute-start(bf16[3,256,128]{2,1,0:T(8,128)(2,1)S(1)} %get-tuple-element.98), channel_id=1, source_target_pairs={{0,8},{4,12},{8,0},{12,4},{16,24},{20,28},{24,16},{28,20},{1,9},{5... | collective-permute-start | bytes 589832 | tf_op jit(solution)/shard_map/ppermute | solution.py:391
  50.1 9.2 %collective-permute-start.22 = (bf16[3,256,128]{2,1,0:T(8,128)(2,1)S(1)}, bf16[3,256,128]{2,1,0:T(8,128)(2,1)S(1)}, u32[]{:S(2)}, u32[]{:S(2)}) collective-permute-start(bf16[3,256,128]{2,1,0:T(8,128)(2,1)S(1)} %get-tuple-element.99), channel_id=1, source_target_pairs={{0,4},{4,0},{8,12},{12,8},{16,20},{20,16},{24,28},{28,24},{1,5},{5... | collective-permute-start | bytes 589832 | tf_op jit(solution)/shard_map/ppermute | solution.py:391
  (1 other events, 1.0 us)

commit v12 on v11

--- a/solution.py
+++ b/solution.py
@@ -122,7 +122,7 @@
         copy.wait()
 
 
-def copy_kernel(x, y, _, x_out, y_out):
+def copy_kernel(x, y, x_out, y_out):
     x_out[...] = x[...]
     y_out[...] = y[...]
 
@@ -445,7 +445,7 @@
     far = swapped(out_grad, "mp", 2)
     chunks = exchanged(chunks)
     tops = swapped(tops, "seq", GROUP)
-    own_grad, far = call(copy_kernel, [shape(*out_grad.shape)] * 2, (out_grad, far, chunks[1]))
+    own_grad, far = call(copy_kernel, [shape(*out_grad.shape)] * 2, (out_grad, far))
     near, queries, level_1, *refs = call(
         functools.partial(gather_kernel, nb, groups),
         [

time: 60.5 us -> 59.9 us (0.990)
  starting transfers between devices: 26.6 us -> 25.4 us
    ppermute x23, starting transfers between devices: 26.6 us -> 25.4 us  [swapped(): lax.ppermute(x, axis, [(i, i ^ step) for i in range(lax.axis_size(axis))])]
where the time goes in v12:
time: 59.9 us; the launch traced here: 59.8 us
  starting transfers between devices  25.4 us (42%)
  waiting for transfers between devices  20.2 us (34%)
  Pallas kernels  12.4 us (21%)
  local copies, waits for them, and re-layouts  0.95 us (2%)
  between operations  0.75 us (1%)
    ppermute x23, starting transfers between devices, swapped(): lax.ppermute(x, axis, [(i, i ^ step) for i in range(lax.axis_size(axis))])  25.4 us
    ppermute x23, waiting for transfers between devices, swapped(): lax.ppermute(x, axis, [(i, i ^ step) for i in range(lax.axis_size(axis))])  20.2 us
    pallas_call x11, Pallas kernels, call(): pl.pallas_call(kernel, out_shape=out_shape, in_specs=[kept if copied else...  12.4 us
  transfers between devices with their start and end apart: 23, of which 13 were waited for; matrix products, arithmetic and copies ran while one was open for 0% of the time, Pallas kernels for 15%

profile of v12, /device:TPU:0, one launch (start us, length us, event | category | flops | bytes accessed | tf_op | source)
XLA Modules:
  0.0 59.8 jit_solution(3975531540385648587)
XLA Ops:
  0.6 3.0 %collective-permute-start.3 = (bf16[64,2048]{1,0:T(8,128)(2,1)}, bf16[64,2048]{1,0:T(8,128)(2,1)S(1)}, u32[]{:S(2)}, u32[]{:S(2)}) collective-permute-start(bf16[64,2048]{1,0:T(8,128)(2,1)} %x.1), channel_id=1, source_target_pairs={{0,2},{1,3},{2,0},{3,1},{4,6},{5,7},{6,4},{7,5},{8,10},{9,11},{10,... | collective-permute-start | bytes 786440 | tf_op jit(solution)/shard_map/ppermute | solution.py:391
  3.6 1.7 %shard_map.84 = (bf16[3,256,128]{2,1,0:T(8,128)(2,1)S(1)}, bf16[3,256,128]{2,1,0:T(8,128)(2,1)S(1)}, bf16[3,256,128]{2,1,0:T(8,128)(2,1)S(1)}, bf16[3,256,128]{2...) custom-call(bf16[256,512]{1,0:T(8,128)(2,1)} %q.1, bf16[256,512]{1,0:T(8,128)(2,1)} %k.1, bf16[256,512]{1,0:T(8,128)(2,1)} %v.1), custom_call_target="tpu_custom_call" | custom-call | tf_op jit(solution)/shard_map/pallas_call | solution.py:38
  5.4 2.6 %collective-permute-start = (bf16[3,256,128]{2,1,0:T(8,128)(2,1)S(1)}, bf16[3,256,128]{2,1,0:T(8,128)(2,1)S(1)}, u32[]{:S(2)}, u32[]{:S(2)}) collective-permute-start(bf16[3,256,128]{2,1,0:T(8,128)(2,1)S(1)} %get-tuple-element.55), channel_id=1, source_target_pairs={{0,12},{4,8},{8,4},{12,0},{16,28},{20,24},{24,20},{28,16},{1,13},{... | collective-permute-start | bytes 589832 | tf_op jit(solution)/shard_map/ppermute | solution.py:391
  8.9 2.6 %collective-permute-start.6 = (bf16[4,2,64,128]{3,2,1,0:T(8,128)(2,1)S(1)}, bf16[4,2,64,128]{3,2,1,0:T(8,128)(2,1)S(1)}, u32[]{:S(2)}, u32[]{:S(2)}) collective-permute-start(bf16[4,2,64,128]{3,2,1,0:T(8,128)(2,1)S(1)} %get-tuple-element.63), channel_id=1, source_target_pairs={{0,16},{4,20},{8,24},{12,28},{16,0},{20,4},{24,8},{28,12},{1,17},{... | collective-permute-start | bytes 393224 | tf_op jit(solution)/shard_map/ppermute | solution.py:391
  11.5 0.9 %copy-done.1 = bf16[64,2048]{1,0:T(8,128)(2,1)S(1)} copy-done((bf16[64,2048]{1,0:T(8,128)(2,1)S(1)}, bf16[64,2048]{1,0:T(8,128)(2,1)}, u32[]{:S(2)}) %copy-start.1) | copy-done | bytes 262168
  12.6 4.4 %collective-permute-done.refs_1_ = bf16[3,256,128]{2,1,0:T(8,128)(2,1)S(1)} collective-permute-done((bf16[3,256,128]{2,1,0:T(8,128)(2,1)S(1)}, bf16[3,256,128]{2,1,0:T(8,128)(2,1)S(1)}, u32[]{:S(2)}, u32[]{:S(2)}) %collective-permute-start) | collective-permute-done | bytes 196640 | tf_op jit(solution)/shard_map/ppermute | solution.py:391
  17.0 2.8 %collective-permute-done.1.refs_2_ = bf16[3,256,128]{2,1,0:T(8,128)(2,1)S(1)} collective-permute-done((bf16[3,256,128]{2,1,0:T(8,128)(2,1)S(1)}, bf16[3,256,128]{2,1,0:T(8,128)(2,1)S(1)}, u32[]{:S(2)}, u32[]{:S(2)}) %collective-permute-start.1) | collective-permute-done | bytes 196640 | tf_op jit(solution)/shard_map/ppermute | solution.py:391
  20.2 1.8 %collective-permute-start.7 = (bf16[2,256,128]{2,1,0:T(8,128)(2,1)S(1)}, bf16[2,256,128]{2,1,0:T(8,128)(2,1)S(1)}, u32[]{:S(2)}, u32[]{:S(2)}) collective-permute-start(bf16[2,256,128]{2,1,0:T(8,128)(2,1)S(1)} %get-tuple-element.70), channel_id=1, source_target_pairs={{0,16},{4,20},{8,24},{12,28},{16,0},{20,4},{24,8},{28,12},{1,17},{... | collective-permute-start | bytes 393224 | tf_op jit(solution)/shard_map/ppermute | solution.py:391
  22.0 0.8 %shard_map.87 = (bf16[384,128]{1,0:T(8,128)(2,1)S(1)}, bf16[384,128]{1,0:T(8,128)(2,1)S(1)}, bf16[384,128]{1,0:T(8,128)(2,1)S(1)}, bf16[384,128]{1,0:T(8,128)(2,1)S(1)}) custom-call(bf16[64,2048]{1,0:T(8,128)(2,1)S(1)} %get-tuple-element.61.refs_0_, bf16[64,2048]{1,0:T(8,128)(2,1)S(1)} %collective-permute-done.4.refs_1_, ...), custom_call_target="tpu_custom_call" | custom-call | flops 536870912 | bytes 3670016 | tf_op jit(solution)/shard_map/pallas_call | solution.py:38
  22.8 2.5 %collective-permute-start.8 = (bf16[384,128]{1,0:T(8,128)(2,1)S(1)}, bf16[384,128]{1,0:T(8,128)(2,1)S(1)}, u32[]{:S(2)}, u32[]{:S(2)}) collective-permute-start(bf16[384,128]{1,0:T(8,128)(2,1)S(1)} %get-tuple-element.71), channel_id=1, source_target_pairs={{0,12},{4,8},{8,4},{12,0},{16,28},{20,24},{24,20},{28,16},{1,13},{... | collective-permute-start | bytes 294920 | tf_op jit(solution)/shard_map/ppermute | solution.py:391
  25.5 1.4 %collective-permute-start.10 = (bf16[384,128]{1,0:T(8,128)(2,1)S(1)}, bf16[384,128]{1,0:T(8,128)(2,1)S(1)}, u32[]{:S(2)}, u32[]{:S(2)}) collective-permute-start(bf16[384,128]{1,0:T(8,128)(2,1)S(1)} %get-tuple-element.73), channel_id=1, source_target_pairs={{0,4},{4,0},{8,12},{12,8},{16,20},{20,16},{24,28},{28,24},{1,5},{5... | collective-permute-start | bytes 294920 | tf_op jit(solution)/shard_map/ppermute | solution.py:391
  26.9 1.7 %shard_map.88 = (bf16[3,4,256,128]{3,2,1,0:T(8,128)(2,1)S(1)}, bf16[128,1024]{1,0:T(8,128)(2,1)S(1)}, bf16[128,1024]{1,0:T(8,128)(2,1)S(1)}, bf16[128,512]{1,0:T...) custom-call(bf16[4,2,256,128]{3,2,1,0:T(8,128)(2,1)S(1)} %get-tuple-element.58, ...), custom_call_target="tpu_custom_call" | custom-call | flops 335544320 | bytes 6946816 | tf_op jit(solution)/shard_map/pallas_call | solution.py:38
  28.5 1.3 %collective-permute-done.8.refs_7_ = bf16[384,128]{1,0:T(8,128)(2,1)S(1)} collective-permute-done((bf16[384,128]{1,0:T(8,128)(2,1)S(1)}, bf16[384,128]{1,0:T(8,128)(2,1)S(1)}, u32[]{:S(2)}, u32[]{:S(2)}) %collective-permute-start.8) | collective-permute-done | bytes 98336 | tf_op jit(solution)/shard_map/ppermute | solution.py:391
  30.6 2.0 %shard_map.89 = (bf16[4,4,256,256]{3,2,1,0:T(8,128)(2,1)S(1)}, bf16[4,256,128]{2,1,0:T(8,128)(2,1)S(1)}, bf16[2,256,128]{2,1,0:T(8,128)(2,1)S(1)}, f32[8,1024]{1...) custom-call(bf16[3,4,256,128]{3,2,1,0:T(8,128)(2,1)S(1)} %get-tuple-, ...), custom_call_target="tpu_custom_call" | custom-call | flops 335544320 | bytes 9633792 | tf_op jit(solution)/shard_map/pallas_call | solution.py:38
  32.6 1.1 %collective-permute-start.19 = (bf16[4,256,128]{2,1,0:T(8,128)(2,1)S(1)}, bf16[4,256,128]{2,1,0:T(8,128)(2,1)S(1)}, u32[]{:S(2)}, u32[]{:S(2)}) collective-permute-start(bf16[4,256,128]{2,1,0:T(8,128)(2,1)S(1)} %get-tuple-element.95), channel_id=1, source_target_pairs={{0,16},{4,20},{8,24},{12,28},{16,0},{20,4},{24,8},{28,12},{1,17},{... | collective-permute-start | bytes 786440 | tf_op jit(solution)/shard_map/ppermute | solution.py:391
  33.7 3.5 %collective-permute-start.11 = (bf16[256,128]{1,0:T(8,128)(2,1)S(1)}, bf16[256,128]{1,0:T(8,128)(2,1)S(1)}, u32[]{:S(2)}, u32[]{:S(2)}) collective-permute-start(bf16[256,128]{1,0:T(8,128)(2,1)S(1)} %get-tuple-element.75), channel_id=1, source_target_pairs={{0,12},{4,8},{8,4},{12,0},{16,28},{20,24},{24,20},{28,16},{1,13},{... | collective-permute-start | bytes 196616 | tf_op jit(solution)/shard_map/ppermute | solution.py:391
  37.8 3.4 %shard_map.90 = (bf16[4,256,128]{2,1,0:T(8,128)(2,1)S(1)}, f32[2,4,256,128]{3,2,1,0:T(8,128)S(1)}) custom-call(bf16[3,4,256,128]{3,2,1,0:T(8,128)(2,1)S(1)} %get-tuple-element.65.refs_0_, bf16[4,2,256,128]{3,2,1,0:T(8,128)(2,1)S(1)} %get-tuple-element.58.near.refs_1_, bf16[2,512,128]{2,1,0:T(8,128)(2,1)S(1)} %get-tuple-element.60.level_1.refs_2_, ...), custom_call_target="tpu_custom_call" | custom-call | flops 1 | bytes 6586368 | tf_op jit(solution)/shard_map/pallas_call | solution.py:38
  41.5 0.8 %shard_map.91 = (bf16[2,64,2048]{2,1,0:T(8,128)(2,1)S(1)}, bf16[32,2048]{1,0:T(8,128)(2,1)S(1)}, bf16[32,2048]{1,0:T(8,128)(2,1)S(1)}, bf16[32,2048]{1,0:T(8,128)(2,1)S(1)}, bf16[32,2048]{1,0:T(8,128)(2,1)S(1)}) custom-call(bf16[256,128]{1,0:T(8,128)(2,1)S(1)} %get-tuple-element.74.refs_0_, bf16[256,128]{1,0:T(8,128)(2,1)S(1)} %collective-permute-done.11.refs_1_, ...), custom_call_target="tpu_custom_call" | custom-call | flops 536870912 | bytes 3670016 | tf_op jit(solution)/shard_map/pallas_call | solution.py:38
  45.2 1.0 %collective-permute-done.19.refs_0_ = bf16[4,256,128]{2,1,0:T(8,128)(2,1)S(1)} collective-permute-done((bf16[4,256,128]{2,1,0:T(8,128)(2,1)S(1)}, bf16[4,256,128]{2,1,0:T(8,128)(2,1)S(1)}, u32[]{:S(2)}, u32[]{:S(2)}) %collective-permute-start.19) | collective-permute-done | bytes 262176 | tf_op jit(solution)/shard_map/ppermute | solution.py:391
  46.5 2.8 %collective-permute-start.20 = (bf16[3,256,128]{2,1,0:T(8,128)(2,1)S(1)}, bf16[3,256,128]{2,1,0:T(8,128)(2,1)S(1)}, u32[]{:S(2)}, u32[]{:S(2)}) collective-permute-start(bf16[3,256,128]{2,1,0:T(8,128)(2,1)S(1)} %get-tuple-element.97), channel_id=1, source_target_pairs={{0,12},{4,8},{8,4},{12,0},{16,28},{20,24},{24,20},{28,16},{1,13},{... | collective-permute-start | bytes 589832 | tf_op jit(solution)/shard_map/ppermute | solution.py:391
  49.3 0.8 %collective-permute-start.22 = (bf16[3,256,128]{2,1,0:T(8,128)(2,1)S(1)}, bf16[3,256,128]{2,1,0:T(8,128)(2,1)S(1)}, u32[]{:S(2)}, u32[]{:S(2)}) collective-permute-start(bf16[3,256,128]{2,1,0:T(8,128)(2,1)S(1)} %get-tuple-element.99), channel_id=1, source_target_pairs={{0,4},{4,0},{8,12},{12,8},{16,20},{20,16},{24,28},{28,24},{1,5},{5... | collective-permute-start | bytes 589832 | tf_op jit(solution)/shard_map/ppermute | solution.py:391
  50.1 5.2 %collective-permute-done.20.refs_3_ = bf16[3,256,128]{2,1,0:T(8,128)(2,1)S(1)} collective-permute-done((bf16[3,256,128]{2,1,0:T(8,128)(2,1)S(1)}, bf16[3,256,128]{2,1,0:T(8,128)(2,1)S(1)}, u32[]{:S(2)}, u32[]{:S(2)}) %collective-permute-start.20) | collective-permute-done | bytes 196640 | tf_op jit(solution)/shard_map/ppermute | solution.py:391
  55.3 2.7 %collective-permute-done.21.refs_4_ = bf16[3,256,128]{2,1,0:T(8,128)(2,1)S(1)} collective-permute-done((bf16[3,256,128]{2,1,0:T(8,128)(2,1)S(1)}, bf16[3,256,128]{2,1,0:T(8,128)(2,1)S(1)}, u32[]{:S(2)}, u32[]{:S(2)}) %collective-permute-start.21) | collective-permute-done | bytes 196640 | tf_op jit(solution)/shard_map/ppermute | solution.py:391
  58.6 1.1 %shard_map.94 = (bf16[256,512]{1,0:T(8,128)(2,1)}, bf16[256,512]{1,0:T(8,128)(2,1)}, bf16[256,512]{1,0:T(8,128)(2,1)}, bf16[64,2048]{1,0:T(8,128)(2,1)}) custom-call(f32[64,2048]{1,0:T(8,128)S(1)} %get-tuple-element.92.refs_0_, bf16[64,2048]{1,0:T(8,128)(2,1)S(1)} %collective-permute-done.18.refs_1_, bf16[3,256,128]{2,1,0:T(8,128)(2,1)S(1)} %get-tuple-element.96.refs_2_, ...), custom_call_target="tpu_custom_call" | custom-call | tf_op jit(solution)/shard_map/pallas_call | solution.py:38
  (37 shorter events, 7.1 us)
Async XLA Ops:
  0.6 10.9 %collective-permute-start.3 = (bf16[64,2048]{1,0:T(8,128)(2,1)}, bf16[64,2048]{1,0:T(8,128)(2,1)S(1)}, u32[]{:S(2)}, u32[]{:S(2)}) collective-permute-start(bf16[64,2048]{1,0:T(8,128)(2,1)} %x.1), channel_id=1, source_target_pairs={{0,2},{1,3},{2,0},{3,1},{4,6},{5,7},{6,4},{7,5},{8,10},{9,11},{10,... | collective-permute-start | bytes 786440 | tf_op jit(solution)/shard_map/ppermute | solution.py:391
  5.4 11.6 %collective-permute-start = (bf16[3,256,128]{2,1,0:T(8,128)(2,1)S(1)}, bf16[3,256,128]{2,1,0:T(8,128)(2,1)S(1)}, u32[]{:S(2)}, u32[]{:S(2)}) collective-permute-start(bf16[3,256,128]{2,1,0:T(8,128)(2,1)S(1)} %get-tuple-element.55), channel_id=1, source_target_pairs={{0,12},{4,8},{8,4},{12,0},{16,28},{20,24},{24,20},{28,16},{1,13},{... | collective-permute-start | bytes 589832 | tf_op jit(solution)/shard_map/ppermute | solution.py:391
  8.0 11.8 %collective-permute-start.1 = (bf16[3,256,128]{2,1,0:T(8,128)(2,1)S(1)}, bf16[3,256,128]{2,1,0:T(8,128)(2,1)S(1)}, u32[]{:S(2)}, u32[]{:S(2)}) collective-permute-start(bf16[3,256,128]{2,1,0:T(8,128)(2,1)S(1)} %get-tuple-element.56), channel_id=1, source_target_pairs={{0,8},{4,12},{8,0},{12,4},{16,24},{20,28},{24,16},{28,20},{1,9},{5... | collective-permute-start | bytes 589832 | tf_op jit(solution)/shard_map/ppermute | solution.py:391
  8.4 11.4 %collective-permute-start.2 = (bf16[3,256,128]{2,1,0:T(8,128)(2,1)S(1)}, bf16[3,256,128]{2,1,0:T(8,128)(2,1)S(1)}, u32[]{:S(2)}, u32[]{:S(2)}) collective-permute-start(bf16[3,256,128]{2,1,0:T(8,128)(2,1)S(1)} %get-tuple-element.57), channel_id=1, source_target_pairs={{0,4},{4,0},{8,12},{12,8},{16,20},{20,16},{24,28},{28,24},{1,5},{5... | collective-permute-start | bytes 589832 | tf_op jit(solution)/shard_map/ppermute | solution.py:391
  8.9 13.0 %collective-permute-start.6 = (bf16[4,2,64,128]{3,2,1,0:T(8,128)(2,1)S(1)}, bf16[4,2,64,128]{3,2,1,0:T(8,128)(2,1)S(1)}, u32[]{:S(2)}, u32[]{:S(2)}) collective-permute-start(bf16[4,2,64,128]{3,2,1,0:T(8,128)(2,1)S(1)} %get-tuple-element.63), channel_id=1, source_target_pairs={{0,16},{4,20},{8,24},{12,28},{16,0},{20,4},{24,8},{28,12},{1,17},{... | collective-permute-start | bytes 393224 | tf_op jit(solution)/shard_map/ppermute | solution.py:391
  12.5 9.4 %collective-permute-start.4 = (bf16[64,2048]{1,0:T(8,128)(2,1)S(1)}, bf16[64,2048]{1,0:T(8,128)(2,1)S(1)}, u32[]{:S(2)}, u32[]{:S(2)}) collective-permute-start(bf16[64,2048]{1,0:T(8,128)(2,1)S(1)} %get-tuple-element.61.refs_0_), channel_id=1, source_target_pairs={{0,1},{1,0},{2,3},{3,2},{4,5},{5,4},{6,7},{7,6},{8,9},{9,8},{10,11... | collective-permute-start | bytes 786440 | tf_op jit(solution)/shard_map/ppermute | solution.py:391
  17.0 5.0 %collective-permute-start.5 = (bf16[64,2048]{1,0:T(8,128)(2,1)S(1)}, bf16[64,2048]{1,0:T(8,128)(2,1)S(1)}, u32[]{:S(2)}, u32[]{:S(2)}) collective-permute-start(bf16[64,2048]{1,0:T(8,128)(2,1)S(1)} %get-tuple-element.62.refs_2_), channel_id=1, source_target_pairs={{0,1},{1,0},{2,3},{3,2},{4,5},{5,4},{6,7},{7,6},{8,9},{9,8},{10,11... | collective-permute-start | bytes 786440 | tf_op jit(solution)/shard_map/ppermute | solution.py:391
  19.8 2.1 %copy-start = (bf16[512,2048]{1,0:T(8,128)(2,1)S(1)}, bf16[512,2048]{1,0:T(8,128)(2,1)}, u32[]{:S(2)}) copy-start(bf16[512,2048]{1,0:T(8,128)(2,1)} %refs_4_.3) | copy-start | bytes 6291460
  20.2 8.3 %collective-permute-start.7 = (bf16[2,256,128]{2,1,0:T(8,128)(2,1)S(1)}, bf16[2,256,128]{2,1,0:T(8,128)(2,1)S(1)}, u32[]{:S(2)}, u32[]{:S(2)}) collective-permute-start(bf16[2,256,128]{2,1,0:T(8,128)(2,1)S(1)} %get-tuple-element.70), channel_id=1, source_target_pairs={{0,16},{4,20},{8,24},{12,28},{16,0},{20,4},{24,8},{28,12},{1,17},{... | collective-permute-start | bytes 393224 | tf_op jit(solution)/shard_map/ppermute | solution.py:391
  22.8 7.0 %collective-permute-start.8 = (bf16[384,128]{1,0:T(8,128)(2,1)S(1)}, bf16[384,128]{1,0:T(8,128)(2,1)S(1)}, u32[]{:S(2)}, u32[]{:S(2)}) collective-permute-start(bf16[384,128]{1,0:T(8,128)(2,1)S(1)} %get-tuple-element.71), channel_id=1, source_target_pairs={{0,12},{4,8},{8,4},{12,0},{16,28},{20,24},{24,20},{28,16},{1,13},{... | collective-permute-start | bytes 294920 | tf_op jit(solution)/shard_map/ppermute | solution.py:391
  25.3 5.3 %collective-permute-start.9 = (bf16[384,128]{1,0:T(8,128)(2,1)S(1)}, bf16[384,128]{1,0:T(8,128)(2,1)S(1)}, u32[]{:S(2)}, u32[]{:S(2)}) collective-permute-start(bf16[384,128]{1,0:T(8,128)(2,1)S(1)} %get-tuple-element.72), channel_id=1, source_target_pairs={{0,8},{4,12},{8,0},{12,4},{16,24},{20,28},{24,16},{28,20},{1,9},{5... | collective-permute-start | bytes 294920 | tf_op jit(solution)/shard_map/ppermute | solution.py:391
  25.5 5.1 %collective-permute-start.10 = (bf16[384,128]{1,0:T(8,128)(2,1)S(1)}, bf16[384,128]{1,0:T(8,128)(2,1)S(1)}, u32[]{:S(2)}, u32[]{:S(2)}) collective-permute-start(bf16[384,128]{1,0:T(8,128)(2,1)S(1)} %get-tuple-element.73), channel_id=1, source_target_pairs={{0,4},{4,0},{8,12},{12,8},{16,20},{20,16},{24,28},{28,24},{1,5},{5... | collective-permute-start | bytes 294920 | tf_op jit(solution)/shard_map/ppermute | solution.py:391
  32.6 13.6 %collective-permute-start.19 = (bf16[4,256,128]{2,1,0:T(8,128)(2,1)S(1)}, bf16[4,256,128]{2,1,0:T(8,128)(2,1)S(1)}, u32[]{:S(2)}, u32[]{:S(2)}) collective-permute-start(bf16[4,256,128]{2,1,0:T(8,128)(2,1)S(1)} %get-tuple-element.95), channel_id=1, source_target_pairs={{0,16},{4,20},{8,24},{12,28},{16,0},{20,4},{24,8},{28,12},{1,17},{... | collective-permute-start | bytes 786440 | tf_op jit(solution)/shard_map/ppermute | solution.py:391
  33.7 7.5 %collective-permute-start.11 = (bf16[256,128]{1,0:T(8,128)(2,1)S(1)}, bf16[256,128]{1,0:T(8,128)(2,1)S(1)}, u32[]{:S(2)}, u32[]{:S(2)}) collective-permute-start(bf16[256,128]{1,0:T(8,128)(2,1)S(1)} %get-tuple-element.75), channel_id=1, source_target_pairs={{0,12},{4,8},{8,4},{12,0},{16,28},{20,24},{24,20},{28,16},{1,13},{... | collective-permute-start | bytes 196616 | tf_op jit(solution)/shard_map/ppermute | solution.py:391
  37.3 4.3 %collective-permute-start.12 = (bf16[256,128]{1,0:T(8,128)(2,1)S(1)}, bf16[256,128]{1,0:T(8,128)(2,1)S(1)}, u32[]{:S(2)}, u32[]{:S(2)}) collective-permute-start(bf16[256,128]{1,0:T(8,128)(2,1)S(1)} %get-tuple-element.76), channel_id=1, source_target_pairs={{0,8},{4,12},{8,0},{12,4},{16,24},{20,28},{24,16},{28,20},{1,9},{5... | collective-permute-start | bytes 196616 | tf_op jit(solution)/shard_map/ppermute | solution.py:391
  37.3 4.3 %collective-permute-start.13 = (bf16[256,128]{1,0:T(8,128)(2,1)S(1)}, bf16[256,128]{1,0:T(8,128)(2,1)S(1)}, u32[]{:S(2)}, u32[]{:S(2)}) collective-permute-start(bf16[256,128]{1,0:T(8,128)(2,1)S(1)} %get-tuple-element.77), channel_id=1, source_target_pairs={{0,4},{4,0},{8,12},{12,8},{16,20},{20,16},{24,28},{28,24},{1,5},{5... | collective-permute-start | bytes 196616 | tf_op jit(solution)/shard_map/ppermute | solution.py:391
  42.3 1.4 %collective-permute-start.14 = (bf16[32,2048]{1,0:T(8,128)(2,1)S(1)}, bf16[32,2048]{1,0:T(8,128)(2,1)S(1)}, u32[]{:S(2)}, u32[]{:S(2)}) collective-permute-start(bf16[32,2048]{1,0:T(8,128)(2,1)S(1)} %get-tuple-element.88), channel_id=1, source_target_pairs={{0,1},{1,0},{2,3},{3,2},{4,5},{5,4},{6,7},{7,6},{8,9},{9,8},{10,11... | collective-permute-start | bytes 393224 | tf_op jit(solution)/shard_map/ppermute | solution.py:391
  42.4 1.5 %collective-permute-start.15 = (bf16[32,2048]{1,0:T(8,128)(2,1)S(1)}, bf16[32,2048]{1,0:T(8,128)(2,1)S(1)}, u32[]{:S(2)}, u32[]{:S(2)}) collective-permute-start(bf16[32,2048]{1,0:T(8,128)(2,1)S(1)} %get-tuple-element.89), channel_id=1, source_target_pairs={{0,1},{1,0},{2,3},{3,2},{4,5},{5,4},{6,7},{7,6},{8,9},{9,8},{10,11... | collective-permute-start | bytes 393224 | tf_op jit(solution)/shard_map/ppermute | solution.py:391
  42.9 1.3 %collective-permute-start.16 = (bf16[32,2048]{1,0:T(8,128)(2,1)S(1)}, bf16[32,2048]{1,0:T(8,128)(2,1)S(1)}, u32[]{:S(2)}, u32[]{:S(2)}) collective-permute-start(bf16[32,2048]{1,0:T(8,128)(2,1)S(1)} %get-tuple-element.90), channel_id=1, source_target_pairs={{0,1},{1,0},{2,3},{3,2},{4,5},{5,4},{6,7},{7,6},{8,9},{9,8},{10,11... | collective-permute-start | bytes 393224 | tf_op jit(solution)/shard_map/ppermute | solution.py:391
  43.0 1.5 %collective-permute-start.17 = (bf16[32,2048]{1,0:T(8,128)(2,1)S(1)}, bf16[32,2048]{1,0:T(8,128)(2,1)S(1)}, u32[]{:S(2)}, u32[]{:S(2)}) collective-permute-start(bf16[32,2048]{1,0:T(8,128)(2,1)S(1)} %get-tuple-element.91), channel_id=1, source_target_pairs={{0,1},{1,0},{2,3},{3,2},{4,5},{5,4},{6,7},{7,6},{8,9},{9,8},{10,11... | collective-permute-start | bytes 393224 | tf_op jit(solution)/shard_map/ppermute | solution.py:391
  44.6 14.1 %collective-permute-start.18 = (bf16[64,2048]{1,0:T(8,128)(2,1)S(1)}, bf16[64,2048]{1,0:T(8,128)(2,1)S(1)}, u32[]{:S(2)}, u32[]{:S(2)}) collective-permute-start(bf16[64,2048]{1,0:T(8,128)(2,1)S(1)} %get-tuple-element.93._), channel_id=1, source_target_pairs={{0,2},{1,3},{2,0},{3,1},{4,6},{5,7},{6,4},{7,5},{8,10},{9,11},{10,... | collective-permute-start | bytes 786440 | tf_op jit(solution)/shard_map/ppermute | solution.py:391
  46.5 8.8 %collective-permute-start.20 = (bf16[3,256,128]{2,1,0:T(8,128)(2,1)S(1)}, bf16[3,256,128]{2,1,0:T(8,128)(2,1)S(1)}, u32[]{:S(2)}, u32[]{:S(2)}) collective-permute-start(bf16[3,256,128]{2,1,0:T(8,128)(2,1)S(1)} %get-tuple-element.97), channel_id=1, source_target_pairs={{0,12},{4,8},{8,4},{12,0},{16,28},{20,24},{24,20},{28,16},{1,13},{... | collective-permute-start | bytes 589832 | tf_op jit(solution)/shard_map/ppermute | solution.py:391
  49.3 8.6 %collective-permute-start.21 = (bf16[3,256,128]{2,1,0:T(8,128)(2,1)S(1)}, bf16[3,256,128]{2,1,0:T(8,128)(2,1)S(1)}, u32[]{:S(2)}, u32[]{:S(2)}) collective-permute-start(bf16[3,256,128]{2,1,0:T(8,128)(2,1)S(1)} %get-tuple-element.98), channel_id=1, source_target_pairs={{0,8},{4,12},{8,0},{12,4},{16,24},{20,28},{24,16},{28,20},{1,9},{5... | collective-permute-start | bytes 589832 | tf_op jit(solution)/shard_map/ppermute | solution.py:391
  49.3 9.3 %collective-permute-start.22 = (bf16[3,256,128]{2,1,0:T(8,128)(2,1)S(1)}, bf16[3,256,128]{2,1,0:T(8,128)(2,1)S(1)}, u32[]{:S(2)}, u32[]{:S(2)}) collective-permute-start(bf16[3,256,128]{2,1,0:T(8,128)(2,1)S(1)} %get-tuple-element.99), channel_id=1, source_target_pairs={{0,4},{4,0},{8,12},{12,8},{16,20},{20,16},{24,28},{28,24},{1,5},{5... | collective-permute-start | bytes 589832 | tf_op jit(solution)/shard_map/ppermute | solution.py:391
  (1 other events, 1.0 us)

commit v13 on v12

--- a/solution.py
+++ b/solution.py
@@ -101,30 +101,34 @@
 
 
 def pack_kernel(q, k, v, *refs):
-    *outs, tops, held, sems = refs
-    me = member()
-    copies = [pltpu.make_async_copy(x, held.at[i], sems.at[i]) for i, x in enumerate((k, v))]
+    *outs, sems = refs
+    me = member()
+    copies = []
     for step, out in zip(STEPS, outs):
         for part, source in enumerate((k, v, q)):
             piece = source.at[:, columns(me ^ step)]
             copies.append(pltpu.make_async_copy(piece, out.at[part], sems.at[len(copies)]))
     for copy in copies:
         copy.start()
+    for copy in copies:
+        copy.wait()
+
+
+def pool_kernel(*refs):
+    *chunks, out = refs
+    me = member()
     pool = pooling()
     half = BLOCK // 2
-    for part in range(2):
-        copies[part].wait()
-        once = dot(pool, held[part]).astype(BF16)
-        twice = dot(pool[: half // 2, :half], once).astype(BF16)
-        for head in range(GROUP):
-            tops[head, part] = twice[:, head * HEAD_DIM : (head + 1) * HEAD_DIM]
-    for copy in copies[2:]:
-        copy.wait()
-
-
-def copy_kernel(x, y, x_out, y_out):
-    x_out[...] = x[...]
-    y_out[...] = y[...]
+    for step, chunk in zip(STEPS, chunks):
+        for part in range(2):
+            once = dot(pool, chunk[part]).astype(BF16)
+            out[me ^ step, part] = dot(pool[: half // 2, :half], once).astype(BF16)
+
+
+def copy_kernel(*refs):
+    count = len(refs) // 2
+    for x, out in zip(refs[:count], refs[count:]):
+        out[...] = x[...]
 
 
 def gather_kernel(nb, groups, *refs):
@@ -434,18 +438,20 @@
 
     chunk = shape(rows, HEAD_DIM)
     triple = shape(3, rows, HEAD_DIM)
-    *chunks, tops = call(
+    chunks = call(
         pack_kernel,
-        [triple] * GROUP + [shape(GROUP, 2, quarter, HEAD_DIM)],
+        [triple] * GROUP,
         (queries, keys, values),
-        scratch=[pltpu.VMEM((2, rows, width), BF16), pltpu.SemaphoreType.DMA((2 + 3 * GROUP,))],
+        scratch=[pltpu.SemaphoreType.DMA((3 * GROUP,))],
         copied=GROUP,
         limit=53,
     )
     far = swapped(out_grad, "mp", 2)
+    (tops,) = call(pool_kernel, [shape(GROUP, 2, quarter, HEAD_DIM)], chunks)
     chunks = exchanged(chunks)
     tops = swapped(tops, "seq", GROUP)
-    own_grad, far = call(copy_kernel, [shape(*out_grad.shape)] * 2, (out_grad, far))
+    arrays = (out_grad, far, out_weight)
+    own_grad, far, out_weight = call(copy_kernel, [shape(*x.shape) for x in arrays], arrays)
     near, queries, level_1, *refs = call(
         functools.partial(gather_kernel, nb, groups),
         [

time: 59.9 us -> 59 us (0.985)
  waiting for transfers between devices: 20.2 us -> 16.3 us
  local copies, waits for them, and re-layouts: 0.95 us -> 2.54 us
  Pallas kernels: 12.4 us -> 13.5 us
    ppermute x23, waiting for transfers between devices: 20.2 us -> 16.3 us  [swapped(): lax.ppermute(x, axis, [(i, i ^ step) for i in range(lax.axis_size(axis))])]
    unnamed x4, local copies, waits for them, and re-layouts: 0.95 us -> 2.54 us
    pallas_call x11 -> x12, Pallas kernels: 12.4 us -> 13.5 us  [call(): pl.pallas_call(kernel, out_shape=out_shape, in_specs=[kept if copied else...]
  transfers between devices with their start and end apart: 23 -> 23, of which waited for: 13 -> 13; matrix products, arithmetic and copies ran while one was open for 0% -> 0% of each run, Pallas kernels for 15% -> 18%
where the time goes in v13:
time: 59 us; the launch traced here: 58.8 us
  starting transfers between devices  25.7 us (44%)
  waiting for transfers between devices  16.3 us (28%)
  Pallas kernels  13.5 us (23%)
  local copies, waits for them, and re-layouts  2.54 us (4%)
  between operations  0.75 us (1%)
    ppermute x23, starting transfers between devices, swapped(): lax.ppermute(x, axis, [(i, i ^ step) for i in range(lax.axis_size(axis))])  25.7 us
    ppermute x23, waiting for transfers between devices, swapped(): lax.ppermute(x, axis, [(i, i ^ step) for i in range(lax.axis_size(axis))])  16.3 us
    pallas_call x12, Pallas kernels, call(): pl.pallas_call(kernel, out_shape=out_shape, in_specs=[kept if copied else...  13.5 us
    unnamed x4, local copies, waits for them, and re-layouts  2.54 us
  transfers between devices with their start and end apart: 23, of which 13 were waited for; matrix products, arithmetic and copies ran while one was open for 0% of the time, Pallas kernels for 18%

profile of v13, /device:TPU:0, one launch (start us, length us, event | category | flops | bytes accessed | tf_op | source)
XLA Modules:
  0.0 58.8 jit_solution(13200674542143681152)
XLA Ops:
  0.6 3.0 %collective-permute-start.3 = (bf16[64,2048]{1,0:T(8,128)(2,1)}, bf16[64,2048]{1,0:T(8,128)(2,1)S(1)}, u32[]{:S(2)}, u32[]{:S(2)}) collective-permute-start(bf16[64,2048]{1,0:T(8,128)(2,1)} %refs_0_.1), channel_id=1, source_target_pairs={{0,2},{1,3},{2,0},{3,1},{4,6},{5,7},{6,4},{7,5},{8,10},{9,11},{10,... | collective-permute-start | bytes 786440 | tf_op jit(solution)/shard_map/ppermute | solution.py:395
  3.6 1.3 %shard_map.84 = (bf16[3,256,128]{2,1,0:T(8,128)(2,1)S(1)}, bf16[3,256,128]{2,1,0:T(8,128)(2,1)S(1)}, bf16[3,256,128]{2,1,0:T(8,128)(2,1)S(1)}, bf16[3,256,128]{2,1,0:T(8,128)(2,1)S(1)}) custom-call(bf16[256,512]{1,0:T(8,128)(2,1)} %q.1, bf16[256,512]{1,0:T(8,128)(2,1)} %k.1, bf16[256,512]{1,0:T(8,128)(2,1)} %v.1), custom_call_target="tpu_custom_call" | custom-call | tf_op jit(solution)/shard_map/pallas_call | solution.py:38
  4.9 2.6 %collective-permute-start = (bf16[3,256,128]{2,1,0:T(8,128)(2,1)S(1)}, bf16[3,256,128]{2,1,0:T(8,128)(2,1)S(1)}, u32[]{:S(2)}, u32[]{:S(2)}) collective-permute-start(bf16[3,256,128]{2,1,0:T(8,128)(2,1)S(1)} %get-tuple-element.55.refs_1_), channel_id=1, source_target_pairs={{0,12},{4,8},{8,4},{12,0},{16,28},{20,24},{24,20},{28,16},{1,13},{... | collective-permute-start | bytes 589832 | tf_op jit(solution)/shard_map/ppermute | solution.py:395
  8.5 1.4 %shard_map.87 = bf16[4,2,64,128]{3,2,1,0:T(8,128)(2,1)S(1)} custom-call(bf16[3,256,128]{2,1,0:T(8,128)(2,1)S(1)} %get-tuple-element.54.refs_0_, bf16[3,256,128]{2,1,0:T(8,128)(2,1)S(1)} %get-tuple-element.55.refs_1_, bf16[3,256,128]{2,1,0:T(8,128)(2,1)S(1)} %get-tuple-element.56.refs_2_, bf16[3,256,128]{2,1,0:T(8,128)(2,1)S(1)} %get-tuple-element.57.refs_3_), custom_call_target="tpu_custom_call" | custom-call | tf_op jit(solution)/shard_map/pallas_call | solution.py:38
  9.9 2.6 %collective-permute-start.6 = (bf16[4,2,64,128]{3,2,1,0:T(8,128)(2,1)S(1)}, bf16[4,2,64,128]{3,2,1,0:T(8,128)(2,1)S(1)}, u32[]{:S(2)}, u32[]{:S(2)}) collective-permute-start(bf16[4,2,64,128]{3,2,1,0:T(8,128)(2,1)S(1)} %shard_map.87), channel_id=1, source_target_pairs={{0,16},{4,20},{8,24},{12,28},{16,0},{20,4},{24,8},{28,12},{1,17},{... | collective-permute-start | bytes 393224 | tf_op jit(solution)/shard_map/ppermute | solution.py:395
  12.5 1.6 %copy-done = bf16[512,2048]{1,0:T(8,128)(2,1)S(1)} copy-done((bf16[512,2048]{1,0:T(8,128)(2,1)S(1)}, bf16[512,2048]{1,0:T(8,128)(2,1)}, u32[]{:S(2)}) %copy-start) | copy-done | bytes 2097176
  15.8 3.6 %collective-permute-done.1.refs_2_ = bf16[3,256,128]{2,1,0:T(8,128)(2,1)S(1)} collective-permute-done((bf16[3,256,128]{2,1,0:T(8,128)(2,1)S(1)}, bf16[3,256,128]{2,1,0:T(8,128)(2,1)S(1)}, u32[]{:S(2)}, u32[]{:S(2)}) %collective-permute-start.1) | collective-permute-done | bytes 196640 | tf_op jit(solution)/shard_map/ppermute | solution.py:395
  19.8 1.7 %collective-permute-start.7 = (bf16[2,256,128]{2,1,0:T(8,128)(2,1)S(1)}, bf16[2,256,128]{2,1,0:T(8,128)(2,1)S(1)}, u32[]{:S(2)}, u32[]{:S(2)}) collective-permute-start(bf16[2,256,128]{2,1,0:T(8,128)(2,1)S(1)} %get-tuple-element.70), channel_id=1, source_target_pairs={{0,16},{4,20},{8,24},{12,28},{16,0},{20,4},{24,8},{28,12},{1,17},{... | collective-permute-start | bytes 393224 | tf_op jit(solution)/shard_map/ppermute | solution.py:395
  22.4 2.3 %collective-permute-start.8 = (bf16[384,128]{1,0:T(8,128)(2,1)S(1)}, bf16[384,128]{1,0:T(8,128)(2,1)S(1)}, u32[]{:S(2)}, u32[]{:S(2)}) collective-permute-start(bf16[384,128]{1,0:T(8,128)(2,1)S(1)} %get-tuple-element.71), channel_id=1, source_target_pairs={{0,12},{4,8},{8,4},{12,0},{16,28},{20,24},{24,20},{28,16},{1,13},{... | collective-permute-start | bytes 294920 | tf_op jit(solution)/shard_map/ppermute | solution.py:395
  25.0 1.4 %collective-permute-start.10 = (bf16[384,128]{1,0:T(8,128)(2,1)S(1)}, bf16[384,128]{1,0:T(8,128)(2,1)S(1)}, u32[]{:S(2)}, u32[]{:S(2)}) collective-permute-start(bf16[384,128]{1,0:T(8,128)(2,1)S(1)} %get-tuple-element.73), channel_id=1, source_target_pairs={{0,4},{4,0},{8,12},{12,8},{16,20},{20,16},{24,28},{28,24},{1,5},{5... | collective-permute-start | bytes 294920 | tf_op jit(solution)/shard_map/ppermute | solution.py:395
  26.4 1.7 %shard_map.89 = (bf16[3,4,256,128]{3,2,1,0:T(8,128)(2,1)S(1)}, bf16[128,1024]{1,0:T(8,128)(2,1)S(1)}, bf16[128,1024]{1,0:T(8,128)(2,1)S(1)}, bf16[128,512]{1,0:T...) custom-call(bf16[4,2,256,128]{3,2,1,0:T(8,128)(2,1)S(1)} %get-tuple-element.58, ...), custom_call_target="tpu_custom_call" | custom-call | flops 335544320 | bytes 6946816 | tf_op jit(solution)/shard_map/pallas_call | solution.py:38
  28.0 1.3 %collective-permute-done.8.refs_7_ = bf16[384,128]{1,0:T(8,128)(2,1)S(1)} collective-permute-done((bf16[384,128]{1,0:T(8,128)(2,1)S(1)}, bf16[384,128]{1,0:T(8,128)(2,1)S(1)}, u32[]{:S(2)}, u32[]{:S(2)}) %collective-permute-start.8) | collective-permute-done | bytes 98336 | tf_op jit(solution)/shard_map/ppermute | solution.py:395
  30.1 2.0 %shard_map.90 = (bf16[4,4,256,256]{3,2,1,0:T(8,128)(2,1)S(1)}, bf16[4,256,128]{2,1,0:T(8,128)(2,1)S(1)}, bf16[2,256,128]{2,1,0:T(8,128)(2,1)S(1)}, f32[8,1024]{1...) custom-call(bf16[3,4,256,128]{3,2,1,0:T(8,128)(2,1)S(1)} %get-tuple-, ...), custom_call_target="tpu_custom_call" | custom-call | flops 335544320 | bytes 9633792 | tf_op jit(solution)/shard_map/pallas_call | solution.py:38
  32.1 1.0 %collective-permute-start.19 = (bf16[4,256,128]{2,1,0:T(8,128)(2,1)S(1)}, bf16[4,256,128]{2,1,0:T(8,128)(2,1)S(1)}, u32[]{:S(2)}, u32[]{:S(2)}) collective-permute-start(bf16[4,256,128]{2,1,0:T(8,128)(2,1)S(1)} %get-tuple-element.95), channel_id=1, source_target_pairs={{0,16},{4,20},{8,24},{12,28},{16,0},{20,4},{24,8},{28,12},{1,17},{... | collective-permute-start | bytes 786440 | tf_op jit(solution)/shard_map/ppermute | solution.py:395
  33.2 2.8 %collective-permute-start.11 = (bf16[256,128]{1,0:T(8,128)(2,1)S(1)}, bf16[256,128]{1,0:T(8,128)(2,1)S(1)}, u32[]{:S(2)}, u32[]{:S(2)}) collective-permute-start(bf16[256,128]{1,0:T(8,128)(2,1)S(1)} %get-tuple-element.75), channel_id=1, source_target_pairs={{0,12},{4,8},{8,4},{12,0},{16,28},{20,24},{24,20},{28,16},{1,13},{... | collective-permute-start | bytes 196616 | tf_op jit(solution)/shard_map/ppermute | solution.py:395
  36.0 1.2 %collective-permute-start.13 = (bf16[256,128]{1,0:T(8,128)(2,1)S(1)}, bf16[256,128]{1,0:T(8,128)(2,1)S(1)}, u32[]{:S(2)}, u32[]{:S(2)}) collective-permute-start(bf16[256,128]{1,0:T(8,128)(2,1)S(1)} %get-tuple-element.77), channel_id=1, source_target_pairs={{0,4},{4,0},{8,12},{12,8},{16,20},{20,16},{24,28},{28,24},{1,5},{5... | collective-permute-start | bytes 196616 | tf_op jit(solution)/shard_map/ppermute | solution.py:395
  37.1 3.3 %shard_map.91 = (bf16[4,256,128]{2,1,0:T(8,128)(2,1)S(1)}, f32[2,4,256,128]{3,2,1,0:T(8,128)S(1)}) custom-call(bf16[3,4,256,128]{3,2,1,0:T(8,128)(2,1)S(1)} %get-tuple-element.65.refs_0_, bf16[4,2,256,128]{3,2,1,0:T(8,128)(2,1)S(1)} %get-tuple-element.58.near.refs_1_, bf16[2,512,128]{2,1,0:T(8,128)(2,1)S(1)} %get-tuple-element.60.level_1.refs_2_, ...), custom_call_target="tpu_custom_call" | custom-call | flops 1 | bytes 6586368 | tf_op jit(solution)/shard_map/pallas_call | solution.py:38
  44.7 1.2 %collective-permute-done.19.refs_0_ = bf16[4,256,128]{2,1,0:T(8,128)(2,1)S(1)} collective-permute-done((bf16[4,256,128]{2,1,0:T(8,128)(2,1)S(1)}, bf16[4,256,128]{2,1,0:T(8,128)(2,1)S(1)}, u32[]{:S(2)}, u32[]{:S(2)}) %collective-permute-start.19) | collective-permute-done | bytes 262176 | tf_op jit(solution)/shard_map/ppermute | solution.py:395
  46.3 1.5 %collective-permute-start.20 = (bf16[3,256,128]{2,1,0:T(8,128)(2,1)S(1)}, bf16[3,256,128]{2,1,0:T(8,128)(2,1)S(1)}, u32[]{:S(2)}, u32[]{:S(2)}) collective-permute-start(bf16[3,256,128]{2,1,0:T(8,128)(2,1)S(1)} %get-tuple-element.97), channel_id=1, source_target_pairs={{0,12},{4,8},{8,4},{12,0},{16,28},{20,24},{24,20},{28,16},{1,13},{... | collective-permute-start | bytes 589832 | tf_op jit(solution)/shard_map/ppermute | solution.py:395
  48.4 1.4 %collective-permute-start.22 = (bf16[3,256,128]{2,1,0:T(8,128)(2,1)S(1)}, bf16[3,256,128]{2,1,0:T(8,128)(2,1)S(1)}, u32[]{:S(2)}, u32[]{:S(2)}) collective-permute-start(bf16[3,256,128]{2,1,0:T(8,128)(2,1)S(1)} %get-tuple-element.99), channel_id=1, source_target_pairs={{0,4},{4,0},{8,12},{12,8},{16,20},{20,16},{24,28},{28,24},{1,5},{5... | collective-permute-start | bytes 589832 | tf_op jit(solution)/shard_map/ppermute | solution.py:395
  49.8 2.9 %collective-permute-done.18.refs_1_ = bf16[64,2048]{1,0:T(8,128)(2,1)S(1)} collective-permute-done((bf16[64,2048]{1,0:T(8,128)(2,1)S(1)}, bf16[64,2048]{1,0:T(8,128)(2,1)S(1)}, u32[]{:S(2)}, u32[]{:S(2)}) %collective-permute-start.18) | collective-permute-done | bytes 262176 | tf_op jit(solution)/shard_map/ppermute | solution.py:395
  52.7 2.4 %collective-permute-done.20.refs_3_ = bf16[3,256,128]{2,1,0:T(8,128)(2,1)S(1)} collective-permute-done((bf16[3,256,128]{2,1,0:T(8,128)(2,1)S(1)}, bf16[3,256,128]{2,1,0:T(8,128)(2,1)S(1)}, u32[]{:S(2)}, u32[]{:S(2)}) %collective-permute-start.20) | collective-permute-done | bytes 196640 | tf_op jit(solution)/shard_map/ppermute | solution.py:395
  55.1 2.3 %collective-permute-done.21.refs_4_ = bf16[3,256,128]{2,1,0:T(8,128)(2,1)S(1)} collective-permute-done((bf16[3,256,128]{2,1,0:T(8,128)(2,1)S(1)}, bf16[3,256,128]{2,1,0:T(8,128)(2,1)S(1)}, u32[]{:S(2)}, u32[]{:S(2)}) %collective-permute-start.21) | collective-permute-done | bytes 196640 | tf_op jit(solution)/shard_map/ppermute | solution.py:395
  57.7 1.1 %shard_map.95 = (bf16[256,512]{1,0:T(8,128)(2,1)}, bf16[256,512]{1,0:T(8,128)(2,1)}, bf16[256,512]{1,0:T(8,128)(2,1)}, bf16[64,2048]{1,0:T(8,128)(2,1)}) custom-call(f32[64,2048]{1,0:T(8,128)S(1)} %get-tuple-element.92.refs_0_, bf16[64,2048]{1,0:T(8,128)(2,1)S(1)} %collective-permute-done.18.refs_1_, bf16[3,256,128]{2,1,0:T(8,128)(2,1)S(1)} %get-tuple-element.96.refs_2_, ...), custom_call_target="tpu_custom_call" | custom-call | tf_op jit(solution)/shard_map/pallas_call | solution.py:38
  (38 shorter events, 10.4 us)
Async XLA Ops:
  0.6 11.9 %collective-permute-start.3 = (bf16[64,2048]{1,0:T(8,128)(2,1)}, bf16[64,2048]{1,0:T(8,128)(2,1)S(1)}, u32[]{:S(2)}, u32[]{:S(2)}) collective-permute-start(bf16[64,2048]{1,0:T(8,128)(2,1)} %refs_0_.1), channel_id=1, source_target_pairs={{0,2},{1,3},{2,0},{3,1},{4,6},{5,7},{6,4},{7,5},{8,10},{9,11},{10,... | collective-permute-start | bytes 786440 | tf_op jit(solution)/shard_map/ppermute | solution.py:395
  4.9 10.4 %collective-permute-start = (bf16[3,256,128]{2,1,0:T(8,128)(2,1)S(1)}, bf16[3,256,128]{2,1,0:T(8,128)(2,1)S(1)}, u32[]{:S(2)}, u32[]{:S(2)}) collective-permute-start(bf16[3,256,128]{2,1,0:T(8,128)(2,1)S(1)} %get-tuple-element.55.refs_1_), channel_id=1, source_target_pairs={{0,12},{4,8},{8,4},{12,0},{16,28},{20,24},{24,20},{28,16},{1,13},{... | collective-permute-start | bytes 589832 | tf_op jit(solution)/shard_map/ppermute | solution.py:395
  7.5 11.8 %collective-permute-start.1 = (bf16[3,256,128]{2,1,0:T(8,128)(2,1)S(1)}, bf16[3,256,128]{2,1,0:T(8,128)(2,1)S(1)}, u32[]{:S(2)}, u32[]{:S(2)}) collective-permute-start(bf16[3,256,128]{2,1,0:T(8,128)(2,1)S(1)} %get-tuple-element.56.refs_2_), channel_id=1, source_target_pairs={{0,8},{4,12},{8,0},{12,4},{16,24},{20,28},{24,16},{28,20},{1,9},{5... | collective-permute-start | bytes 589832 | tf_op jit(solution)/shard_map/ppermute | solution.py:395
  8.0 11.4 %collective-permute-start.2 = (bf16[3,256,128]{2,1,0:T(8,128)(2,1)S(1)}, bf16[3,256,128]{2,1,0:T(8,128)(2,1)S(1)}, u32[]{:S(2)}, u32[]{:S(2)}) collective-permute-start(bf16[3,256,128]{2,1,0:T(8,128)(2,1)S(1)} %get-tuple-element.57.refs_3_), channel_id=1, source_target_pairs={{0,4},{4,0},{8,12},{12,8},{16,20},{20,16},{24,28},{28,24},{1,5},{5... | collective-permute-start | bytes 589832 | tf_op jit(solution)/shard_map/ppermute | solution.py:395
  9.9 11.6 %collective-permute-start.6 = (bf16[4,2,64,128]{3,2,1,0:T(8,128)(2,1)S(1)}, bf16[4,2,64,128]{3,2,1,0:T(8,128)(2,1)S(1)}, u32[]{:S(2)}, u32[]{:S(2)}) collective-permute-start(bf16[4,2,64,128]{3,2,1,0:T(8,128)(2,1)S(1)} %shard_map.87), channel_id=1, source_target_pairs={{0,16},{4,20},{8,24},{12,28},{16,0},{20,4},{24,8},{28,12},{1,17},{... | collective-permute-start | bytes 393224 | tf_op jit(solution)/shard_map/ppermute | solution.py:395
  12.5 1.6 %copy-start = (bf16[512,2048]{1,0:T(8,128)(2,1)S(1)}, bf16[512,2048]{1,0:T(8,128)(2,1)}, u32[]{:S(2)}) copy-start(bf16[512,2048]{1,0:T(8,128)(2,1)} %refs_2_.1) | copy-start | bytes 6291460
  15.2 6.3 %collective-permute-start.4 = (bf16[64,2048]{1,0:T(8,128)(2,1)S(1)}, bf16[64,2048]{1,0:T(8,128)(2,1)S(1)}, u32[]{:S(2)}, u32[]{:S(2)}) collective-permute-start(bf16[64,2048]{1,0:T(8,128)(2,1)S(1)} %get-tuple-element.61.refs_0_), channel_id=1, source_target_pairs={{0,1},{1,0},{2,3},{3,2},{4,5},{5,4},{6,7},{7,6},{8,9},{9,8},{10,11... | collective-permute-start | bytes 786440 | tf_op jit(solution)/shard_map/ppermute | solution.py:395
  15.3 6.2 %collective-permute-start.5 = (bf16[64,2048]{1,0:T(8,128)(2,1)S(1)}, bf16[64,2048]{1,0:T(8,128)(2,1)S(1)}, u32[]{:S(2)}, u32[]{:S(2)}) collective-permute-start(bf16[64,2048]{1,0:T(8,128)(2,1)S(1)} %get-tuple-element.62.refs_2_), channel_id=1, source_target_pairs={{0,1},{1,0},{2,3},{3,2},{4,5},{5,4},{6,7},{7,6},{8,9},{9,8},{10,11... | collective-permute-start | bytes 786440 | tf_op jit(solution)/shard_map/ppermute | solution.py:395
  19.8 8.3 %collective-permute-start.7 = (bf16[2,256,128]{2,1,0:T(8,128)(2,1)S(1)}, bf16[2,256,128]{2,1,0:T(8,128)(2,1)S(1)}, u32[]{:S(2)}, u32[]{:S(2)}) collective-permute-start(bf16[2,256,128]{2,1,0:T(8,128)(2,1)S(1)} %get-tuple-element.70), channel_id=1, source_target_pairs={{0,16},{4,20},{8,24},{12,28},{16,0},{20,4},{24,8},{28,12},{1,17},{... | collective-permute-start | bytes 393224 | tf_op jit(solution)/shard_map/ppermute | solution.py:395
  22.4 7.0 %collective-permute-start.8 = (bf16[384,128]{1,0:T(8,128)(2,1)S(1)}, bf16[384,128]{1,0:T(8,128)(2,1)S(1)}, u32[]{:S(2)}, u32[]{:S(2)}) collective-permute-start(bf16[384,128]{1,0:T(8,128)(2,1)S(1)} %get-tuple-element.71), channel_id=1, source_target_pairs={{0,12},{4,8},{8,4},{12,0},{16,28},{20,24},{24,20},{28,16},{1,13},{... | collective-permute-start | bytes 294920 | tf_op jit(solution)/shard_map/ppermute | solution.py:395
  24.7 5.4 %collective-permute-start.9 = (bf16[384,128]{1,0:T(8,128)(2,1)S(1)}, bf16[384,128]{1,0:T(8,128)(2,1)S(1)}, u32[]{:S(2)}, u32[]{:S(2)}) collective-permute-start(bf16[384,128]{1,0:T(8,128)(2,1)S(1)} %get-tuple-element.72), channel_id=1, source_target_pairs={{0,8},{4,12},{8,0},{12,4},{16,24},{20,28},{24,16},{28,20},{1,9},{5... | collective-permute-start | bytes 294920 | tf_op jit(solution)/shard_map/ppermute | solution.py:395
  25.0 5.1 %collective-permute-start.10 = (bf16[384,128]{1,0:T(8,128)(2,1)S(1)}, bf16[384,128]{1,0:T(8,128)(2,1)S(1)}, u32[]{:S(2)}, u32[]{:S(2)}) collective-permute-start(bf16[384,128]{1,0:T(8,128)(2,1)S(1)} %get-tuple-element.73), channel_id=1, source_target_pairs={{0,4},{4,0},{8,12},{12,8},{16,20},{20,16},{24,28},{28,24},{1,5},{5... | collective-permute-start | bytes 294920 | tf_op jit(solution)/shard_map/ppermute | solution.py:395
  32.1 13.8 %collective-permute-start.19 = (bf16[4,256,128]{2,1,0:T(8,128)(2,1)S(1)}, bf16[4,256,128]{2,1,0:T(8,128)(2,1)S(1)}, u32[]{:S(2)}, u32[]{:S(2)}) collective-permute-start(bf16[4,256,128]{2,1,0:T(8,128)(2,1)S(1)} %get-tuple-element.95), channel_id=1, source_target_pairs={{0,16},{4,20},{8,24},{12,28},{16,0},{20,4},{24,8},{28,12},{1,17},{... | collective-permute-start | bytes 786440 | tf_op jit(solution)/shard_map/ppermute | solution.py:395
  33.2 7.3 %collective-permute-start.11 = (bf16[256,128]{1,0:T(8,128)(2,1)S(1)}, bf16[256,128]{1,0:T(8,128)(2,1)S(1)}, u32[]{:S(2)}, u32[]{:S(2)}) collective-permute-start(bf16[256,128]{1,0:T(8,128)(2,1)S(1)} %get-tuple-element.75), channel_id=1, source_target_pairs={{0,12},{4,8},{8,4},{12,0},{16,28},{20,24},{24,20},{28,16},{1,13},{... | collective-permute-start | bytes 196616 | tf_op jit(solution)/shard_map/ppermute | solution.py:395
  35.9 5.1 %collective-permute-start.12 = (bf16[256,128]{1,0:T(8,128)(2,1)S(1)}, bf16[256,128]{1,0:T(8,128)(2,1)S(1)}, u32[]{:S(2)}, u32[]{:S(2)}) collective-permute-start(bf16[256,128]{1,0:T(8,128)(2,1)S(1)} %get-tuple-element.76), channel_id=1, source_target_pairs={{0,8},{4,12},{8,0},{12,4},{16,24},{20,28},{24,16},{28,20},{1,9},{5... | collective-permute-start | bytes 196616 | tf_op jit(solution)/shard_map/ppermute | solution.py:395
  36.0 5.1 %collective-permute-start.13 = (bf16[256,128]{1,0:T(8,128)(2,1)S(1)}, bf16[256,128]{1,0:T(8,128)(2,1)S(1)}, u32[]{:S(2)}, u32[]{:S(2)}) collective-permute-start(bf16[256,128]{1,0:T(8,128)(2,1)S(1)} %get-tuple-element.77), channel_id=1, source_target_pairs={{0,4},{4,0},{8,12},{12,8},{16,20},{20,16},{24,28},{28,24},{1,5},{5... | collective-permute-start | bytes 196616 | tf_op jit(solution)/shard_map/ppermute | solution.py:395
  41.9 1.4 %collective-permute-start.14 = (bf16[32,2048]{1,0:T(8,128)(2,1)S(1)}, bf16[32,2048]{1,0:T(8,128)(2,1)S(1)}, u32[]{:S(2)}, u32[]{:S(2)}) collective-permute-start(bf16[32,2048]{1,0:T(8,128)(2,1)S(1)} %get-tuple-element.88), channel_id=1, source_target_pairs={{0,1},{1,0},{2,3},{3,2},{4,5},{5,4},{6,7},{7,6},{8,9},{9,8},{10,11... | collective-permute-start | bytes 393224 | tf_op jit(solution)/shard_map/ppermute | solution.py:395
  41.9 1.5 %collective-permute-start.15 = (bf16[32,2048]{1,0:T(8,128)(2,1)S(1)}, bf16[32,2048]{1,0:T(8,128)(2,1)S(1)}, u32[]{:S(2)}, u32[]{:S(2)}) collective-permute-start(bf16[32,2048]{1,0:T(8,128)(2,1)S(1)} %get-tuple-element.89), channel_id=1, source_target_pairs={{0,1},{1,0},{2,3},{3,2},{4,5},{5,4},{6,7},{7,6},{8,9},{9,8},{10,11... | collective-permute-start | bytes 393224 | tf_op jit(solution)/shard_map/ppermute | solution.py:395
  42.4 1.3 %collective-permute-start.16 = (bf16[32,2048]{1,0:T(8,128)(2,1)S(1)}, bf16[32,2048]{1,0:T(8,128)(2,1)S(1)}, u32[]{:S(2)}, u32[]{:S(2)}) collective-permute-start(bf16[32,2048]{1,0:T(8,128)(2,1)S(1)} %get-tuple-element.90), channel_id=1, source_target_pairs={{0,1},{1,0},{2,3},{3,2},{4,5},{5,4},{6,7},{7,6},{8,9},{9,8},{10,11... | collective-permute-start | bytes 393224 | tf_op jit(solution)/shard_map/ppermute | solution.py:395
  42.5 1.5 %collective-permute-start.17 = (bf16[32,2048]{1,0:T(8,128)(2,1)S(1)}, bf16[32,2048]{1,0:T(8,128)(2,1)S(1)}, u32[]{:S(2)}, u32[]{:S(2)}) collective-permute-start(bf16[32,2048]{1,0:T(8,128)(2,1)S(1)} %get-tuple-element.91), channel_id=1, source_target_pairs={{0,1},{1,0},{2,3},{3,2},{4,5},{5,4},{6,7},{7,6},{8,9},{9,8},{10,11... | collective-permute-start | bytes 393224 | tf_op jit(solution)/shard_map/ppermute | solution.py:395
  44.1 8.6 %collective-permute-start.18 = (bf16[64,2048]{1,0:T(8,128)(2,1)S(1)}, bf16[64,2048]{1,0:T(8,128)(2,1)S(1)}, u32[]{:S(2)}, u32[]{:S(2)}) collective-permute-start(bf16[64,2048]{1,0:T(8,128)(2,1)S(1)} %get-tuple-element.93._), channel_id=1, source_target_pairs={{0,2},{1,3},{2,0},{3,1},{4,6},{5,7},{6,4},{7,5},{8,10},{9,11},{10,... | collective-permute-start | bytes 786440 | tf_op jit(solution)/shard_map/ppermute | solution.py:395
  46.3 8.8 %collective-permute-start.20 = (bf16[3,256,128]{2,1,0:T(8,128)(2,1)S(1)}, bf16[3,256,128]{2,1,0:T(8,128)(2,1)S(1)}, u32[]{:S(2)}, u32[]{:S(2)}) collective-permute-start(bf16[3,256,128]{2,1,0:T(8,128)(2,1)S(1)} %get-tuple-element.97), channel_id=1, source_target_pairs={{0,12},{4,8},{8,4},{12,0},{16,28},{20,24},{24,20},{28,16},{1,13},{... | collective-permute-start | bytes 589832 | tf_op jit(solution)/shard_map/ppermute | solution.py:395
  47.8 9.5 %collective-permute-start.21 = (bf16[3,256,128]{2,1,0:T(8,128)(2,1)S(1)}, bf16[3,256,128]{2,1,0:T(8,128)(2,1)S(1)}, u32[]{:S(2)}, u32[]{:S(2)}) collective-permute-start(bf16[3,256,128]{2,1,0:T(8,128)(2,1)S(1)} %get-tuple-element.98), channel_id=1, source_target_pairs={{0,8},{4,12},{8,0},{12,4},{16,24},{20,28},{24,16},{28,20},{1,9},{5... | collective-permute-start | bytes 589832 | tf_op jit(solution)/shard_map/ppermute | solution.py:395
  48.4 9.2 %collective-permute-start.22 = (bf16[3,256,128]{2,1,0:T(8,128)(2,1)S(1)}, bf16[3,256,128]{2,1,0:T(8,128)(2,1)S(1)}, u32[]{:S(2)}, u32[]{:S(2)}) collective-permute-start(bf16[3,256,128]{2,1,0:T(8,128)(2,1)S(1)} %get-tuple-element.99), channel_id=1, source_target_pairs={{0,4},{4,0},{8,12},{12,8},{16,20},{20,16},{24,28},{28,24},{1,5},{5... | collective-permute-start | bytes 589832 | tf_op jit(solution)/shard_map/ppermute | solution.py:395
  (1 other events, 0.9 us)

commit v14 on v13

--- a/solution.py
+++ b/solution.py
@@ -317,13 +317,13 @@
 
 
 def share_kernel(kept, *refs):
-    *got, across, here = refs
-    half = across.shape[0] // 2
+    *got, across_0, across_1, here = refs
+    half = across_0.shape[0]
     for i, piece in enumerate(got):
         far, at = i // 2, pl.ds(i % 2 * half, half)
         total = kept[far, at, :].astype(F32) + piece[...].astype(F32)
         if far:
-            across[at, :] = total.astype(BF16)
+            (across_0, across_1)[i % 2][...] = total.astype(BF16)
         else:
             here[at, :] = total
 
@@ -348,9 +348,12 @@
 
 
 def unpack_kernel(*refs):
-    here, across, *refs = refs
+    here, across_0, across_1, *refs = refs
     chunks, (*outs, mixed) = refs[:GROUP], refs[GROUP:]
-    mixed[...] = (here[...] + across[...].astype(F32)).astype(BF16)
+    half = across_0.shape[0]
+    for part, across in enumerate((across_0, across_1)):
+        at = pl.ds(part * half, half)
+        mixed[at, :] = (here[at, :] + across[...].astype(F32)).astype(BF16)
     me = member()
     for step, chunk in zip(STEPS, chunks):
         at = columns(me ^ step)
@@ -531,24 +534,24 @@
         scratch=[pltpu.VMEM((rows, width), BF16), pltpu.VMEM((rows, model), BF16)],
         flops=weight_flops,
     )
-    across, here = call(
+    *across, here = call(
         share_kernel,
-        [shape(local, model), shape(local, model, dtype=F32)],
+        [shape(local // 2, model)] * 2 + [shape(local, model, dtype=F32)],
         (kept, *(swapped(piece, "mp", 1) for piece in given)),
     )
     chunks = call(
         functools.partial(combine_kernel, nb, groups),
         [triple] * GROUP,
-        (grad_q, grad_kv, across, *other_grads),
+        (grad_q, grad_kv, here, *other_grads),
         scratch=[pltpu.VMEM((nb, 2, rows, HEAD_DIM), BF16)],
         flops=20 * score_flops,
     )
     chunks = exchanged(chunks)
-    across = swapped(across, "mp", 2)
+    across = [swapped(piece, "mp", 2) for piece in across]
     grad_k, grad_v, grad_q, mixed = call(
         unpack_kernel,
         [shape(rows, width)] * 3 + [shape(local, model)],
-        (here, across, *chunks),
+        (here, *across, *chunks),
     )
     return mixed, grad_q, grad_k, grad_v
 

time: 59 us -> 59 us (level)
  starting transfers between devices: 25.7 us -> 27.1 us
  waiting for transfers between devices: 16.3 us -> 14.9 us
    ppermute x23 -> x24, waiting for transfers between devices: 16.3 us -> 14.9 us  [swapped(): lax.ppermute(x, axis, [(i, i ^ step) for i in range(lax.axis_size(axis))])]
    ppermute x23 -> x24, starting transfers between devices: 25.7 us -> 27.1 us  [swapped(): lax.ppermute(x, axis, [(i, i ^ step) for i in range(lax.axis_size(axis))])]
  transfers between devices with their start and end apart: 23 -> 24, of which waited for: 13 -> 13; matrix products, arithmetic and copies ran while one was open for 0% -> 0% of each run, Pallas kernels for 18% -> 17%
where the time goes in v14:
time: 59 us; the launch traced here: 58.8 us
  starting transfers between devices  27.1 us (46%)
  waiting for transfers between devices  14.9 us (25%)
  Pallas kernels  13.5 us (23%)
  local copies, waits for them, and re-layouts  2.54 us (4%)
  between operations  0.75 us (1%)
    ppermute x24, starting transfers between devices, swapped(): lax.ppermute(x, axis, [(i, i ^ step) for i in range(lax.axis_size(axis))])  27.1 us
    ppermute x24, waiting for transfers between devices, swapped(): lax.ppermute(x, axis, [(i, i ^ step) for i in range(lax.axis_size(axis))])  14.9 us
    pallas_call x12, Pallas kernels, call(): pl.pallas_call(kernel, out_shape=out_shape, in_specs=[kept if copied else...  13.5 us
    unnamed x4, local copies, waits for them, and re-layouts  2.54 us
  transfers between devices with their start and end apart: 24, of which 13 were waited for; matrix products, arithmetic and copies ran while one was open for 0% of the time, Pallas kernels for 17%

profile of v14, /device:TPU:0, one launch (start us, length us, event | category | flops | bytes accessed | tf_op | source)
XLA Modules:
  0.0 58.8 jit_solution(1527327838051120319)
XLA Ops:
  0.6 3.0 %collective-permute-start.3 = (bf16[64,2048]{1,0:T(8,128)(2,1)}, bf16[64,2048]{1,0:T(8,128)(2,1)S(1)}, u32[]{:S(2)}, u32[]{:S(2)}) collective-permute-start(bf16[64,2048]{1,0:T(8,128)(2,1)} %refs_0_.1), channel_id=1, source_target_pairs={{0,2},{1,3},{2,0},{3,1},{4,6},{5,7},{6,4},{7,5},{8,10},{9,11},{10,... | collective-permute-start | bytes 786440 | tf_op jit(solution)/shard_map/ppermute | solution.py:398
  3.6 1.3 %shard_map.84 = (bf16[3,256,128]{2,1,0:T(8,128)(2,1)S(1)}, bf16[3,256,128]{2,1,0:T(8,128)(2,1)S(1)}, bf16[3,256,128]{2,1,0:T(8,128)(2,1)S(1)}, bf16[3,256,128]{2,1,0:T(8,128)(2,1)S(1)}) custom-call(bf16[256,512]{1,0:T(8,128)(2,1)} %q.1, bf16[256,512]{1,0:T(8,128)(2,1)} %k.1, bf16[256,512]{1,0:T(8,128)(2,1)} %v.1), custom_call_target="tpu_custom_call" | custom-call | tf_op jit(solution)/shard_map/pallas_call | solution.py:38
  4.9 2.6 %collective-permute-start = (bf16[3,256,128]{2,1,0:T(8,128)(2,1)S(1)}, bf16[3,256,128]{2,1,0:T(8,128)(2,1)S(1)}, u32[]{:S(2)}, u32[]{:S(2)}) collective-permute-start(bf16[3,256,128]{2,1,0:T(8,128)(2,1)S(1)} %get-tuple-element.56.refs_1_), channel_id=1, source_target_pairs={{0,12},{4,8},{8,4},{12,0},{16,28},{20,24},{24,20},{28,16},{1,13},{... | collective-permute-start | bytes 589832 | tf_op jit(solution)/shard_map/ppermute | solution.py:398
  8.5 1.4 %shard_map.87 = bf16[4,2,64,128]{3,2,1,0:T(8,128)(2,1)S(1)} custom-call(bf16[3,256,128]{2,1,0:T(8,128)(2,1)S(1)} %get-tuple-element.55.refs_0_, bf16[3,256,128]{2,1,0:T(8,128)(2,1)S(1)} %get-tuple-element.56.refs_1_, bf16[3,256,128]{2,1,0:T(8,128)(2,1)S(1)} %get-tuple-element.57.refs_2_, bf16[3,256,128]{2,1,0:T(8,128)(2,1)S(1)} %get-tuple-element.58.refs_3_), custom_call_target="tpu_custom_call" | custom-call | tf_op jit(solution)/shard_map/pallas_call | solution.py:38
  9.9 2.6 %collective-permute-start.6 = (bf16[4,2,64,128]{3,2,1,0:T(8,128)(2,1)S(1)}, bf16[4,2,64,128]{3,2,1,0:T(8,128)(2,1)S(1)}, u32[]{:S(2)}, u32[]{:S(2)}) collective-permute-start(bf16[4,2,64,128]{3,2,1,0:T(8,128)(2,1)S(1)} %shard_map.87), channel_id=1, source_target_pairs={{0,16},{4,20},{8,24},{12,28},{16,0},{20,4},{24,8},{28,12},{1,17},{... | collective-permute-start | bytes 393224 | tf_op jit(solution)/shard_map/ppermute | solution.py:398
  12.5 1.6 %copy-done = bf16[512,2048]{1,0:T(8,128)(2,1)S(1)} copy-done((bf16[512,2048]{1,0:T(8,128)(2,1)S(1)}, bf16[512,2048]{1,0:T(8,128)(2,1)}, u32[]{:S(2)}) %copy-start) | copy-done | bytes 2097176
  15.8 3.6 %collective-permute-done.1.refs_2_ = bf16[3,256,128]{2,1,0:T(8,128)(2,1)S(1)} collective-permute-done((bf16[3,256,128]{2,1,0:T(8,128)(2,1)S(1)}, bf16[3,256,128]{2,1,0:T(8,128)(2,1)S(1)}, u32[]{:S(2)}, u32[]{:S(2)}) %collective-permute-start.1) | collective-permute-done | bytes 196640 | tf_op jit(solution)/shard_map/ppermute | solution.py:398
  19.8 1.7 %collective-permute-start.7 = (bf16[2,256,128]{2,1,0:T(8,128)(2,1)S(1)}, bf16[2,256,128]{2,1,0:T(8,128)(2,1)S(1)}, u32[]{:S(2)}, u32[]{:S(2)}) collective-permute-start(bf16[2,256,128]{2,1,0:T(8,128)(2,1)S(1)} %get-tuple-element.71), channel_id=1, source_target_pairs={{0,16},{4,20},{8,24},{12,28},{16,0},{20,4},{24,8},{28,12},{1,17},{... | collective-permute-start | bytes 393224 | tf_op jit(solution)/shard_map/ppermute | solution.py:398
  22.4 2.3 %collective-permute-start.8 = (bf16[384,128]{1,0:T(8,128)(2,1)S(1)}, bf16[384,128]{1,0:T(8,128)(2,1)S(1)}, u32[]{:S(2)}, u32[]{:S(2)}) collective-permute-start(bf16[384,128]{1,0:T(8,128)(2,1)S(1)} %get-tuple-element.72), channel_id=1, source_target_pairs={{0,12},{4,8},{8,4},{12,0},{16,28},{20,24},{24,20},{28,16},{1,13},{... | collective-permute-start | bytes 294920 | tf_op jit(solution)/shard_map/ppermute | solution.py:398
  25.0 1.4 %collective-permute-start.10 = (bf16[384,128]{1,0:T(8,128)(2,1)S(1)}, bf16[384,128]{1,0:T(8,128)(2,1)S(1)}, u32[]{:S(2)}, u32[]{:S(2)}) collective-permute-start(bf16[384,128]{1,0:T(8,128)(2,1)S(1)} %get-tuple-element.74), channel_id=1, source_target_pairs={{0,4},{4,0},{8,12},{12,8},{16,20},{20,16},{24,28},{28,24},{1,5},{5... | collective-permute-start | bytes 294920 | tf_op jit(solution)/shard_map/ppermute | solution.py:398
  26.4 1.7 %shard_map.89 = (bf16[3,4,256,128]{3,2,1,0:T(8,128)(2,1)S(1)}, bf16[128,1024]{1,0:T(8,128)(2,1)S(1)}, bf16[128,1024]{1,0:T(8,128)(2,1)S(1)}, bf16[128,512]{1,0:T...) custom-call(bf16[4,2,256,128]{3,2,1,0:T(8,128)(2,1)S(1)} %get-tuple-element.59, ...), custom_call_target="tpu_custom_call" | custom-call | flops 335544320 | bytes 6946816 | tf_op jit(solution)/shard_map/pallas_call | solution.py:38
  28.0 1.3 %collective-permute-done.8.refs_7_ = bf16[384,128]{1,0:T(8,128)(2,1)S(1)} collective-permute-done((bf16[384,128]{1,0:T(8,128)(2,1)S(1)}, bf16[384,128]{1,0:T(8,128)(2,1)S(1)}, u32[]{:S(2)}, u32[]{:S(2)}) %collective-permute-start.8) | collective-permute-done | bytes 98336 | tf_op jit(solution)/shard_map/ppermute | solution.py:398
  30.1 2.0 %shard_map.90 = (bf16[4,4,256,256]{3,2,1,0:T(8,128)(2,1)S(1)}, bf16[4,256,128]{2,1,0:T(8,128)(2,1)S(1)}, bf16[2,256,128]{2,1,0:T(8,128)(2,1)S(1)}, f32[8,1024]{1...) custom-call(bf16[3,4,256,128]{3,2,1,0:T(8,128)(2,1)S(1)} %get-tuple-, ...), custom_call_target="tpu_custom_call" | custom-call | flops 335544320 | bytes 9633792 | tf_op jit(solution)/shard_map/pallas_call | solution.py:38
  32.1 1.0 %collective-permute-start.20 = (bf16[4,256,128]{2,1,0:T(8,128)(2,1)S(1)}, bf16[4,256,128]{2,1,0:T(8,128)(2,1)S(1)}, u32[]{:S(2)}, u32[]{:S(2)}) collective-permute-start(bf16[4,256,128]{2,1,0:T(8,128)(2,1)S(1)} %get-tuple-element.97), channel_id=1, source_target_pairs={{0,16},{4,20},{8,24},{12,28},{16,0},{20,4},{24,8},{28,12},{1,17},{... | collective-permute-start | bytes 786440 | tf_op jit(solution)/shard_map/ppermute | solution.py:398
  33.2 2.8 %collective-permute-start.11 = (bf16[256,128]{1,0:T(8,128)(2,1)S(1)}, bf16[256,128]{1,0:T(8,128)(2,1)S(1)}, u32[]{:S(2)}, u32[]{:S(2)}) collective-permute-start(bf16[256,128]{1,0:T(8,128)(2,1)S(1)} %get-tuple-element.76), channel_id=1, source_target_pairs={{0,12},{4,8},{8,4},{12,0},{16,28},{20,24},{24,20},{28,16},{1,13},{... | collective-permute-start | bytes 196616 | tf_op jit(solution)/shard_map/ppermute | solution.py:398
  36.0 1.2 %collective-permute-start.13 = (bf16[256,128]{1,0:T(8,128)(2,1)S(1)}, bf16[256,128]{1,0:T(8,128)(2,1)S(1)}, u32[]{:S(2)}, u32[]{:S(2)}) collective-permute-start(bf16[256,128]{1,0:T(8,128)(2,1)S(1)} %get-tuple-element.78), channel_id=1, source_target_pairs={{0,4},{4,0},{8,12},{12,8},{16,20},{20,16},{24,28},{28,24},{1,5},{5... | collective-permute-start | bytes 196616 | tf_op jit(solution)/shard_map/ppermute | solution.py:398
  37.1 3.3 %shard_map.91 = (bf16[4,256,128]{2,1,0:T(8,128)(2,1)S(1)}, f32[2,4,256,128]{3,2,1,0:T(8,128)S(1)}) custom-call(bf16[3,4,256,128]{3,2,1,0:T(8,128)(2,1)S(1)} %get-tuple-element.66.refs_0_, bf16[4,2,256,128]{3,2,1,0:T(8,128)(2,1)S(1)} %get-tuple-element.59.near.refs_1_, bf16[2,512,128]{2,1,0:T(8,128)(2,1)S(1)} %get-tuple-element.61.level_1.refs_2_, ...), custom_call_target="tpu_custom_call" | custom-call | flops 1 | bytes 6586368 | tf_op jit(solution)/shard_map/pallas_call | solution.py:38
  44.1 1.8 %collective-permute-done.20.refs_0_ = bf16[4,256,128]{2,1,0:T(8,128)(2,1)S(1)} collective-permute-done((bf16[4,256,128]{2,1,0:T(8,128)(2,1)S(1)}, bf16[4,256,128]{2,1,0:T(8,128)(2,1)S(1)}, u32[]{:S(2)}, u32[]{:S(2)}) %collective-permute-start.20) | collective-permute-done | bytes 262176 | tf_op jit(solution)/shard_map/ppermute | solution.py:398
  47.2 1.2 %collective-permute-start.22 = (bf16[3,256,128]{2,1,0:T(8,128)(2,1)S(1)}, bf16[3,256,128]{2,1,0:T(8,128)(2,1)S(1)}, u32[]{:S(2)}, u32[]{:S(2)}) collective-permute-start(bf16[3,256,128]{2,1,0:T(8,128)(2,1)S(1)} %get-tuple-element.100), channel_id=1, source_target_pairs={{0,8},{4,12},{8,0},{12,4},{16,24},{20,28},{24,16},{28,20},{1,9},{5... | collective-permute-start | bytes 589832 | tf_op jit(solution)/shard_map/ppermute | solution.py:398
  48.4 1.4 %collective-permute-start.23 = (bf16[3,256,128]{2,1,0:T(8,128)(2,1)S(1)}, bf16[3,256,128]{2,1,0:T(8,128)(2,1)S(1)}, u32[]{:S(2)}, u32[]{:S(2)}) collective-permute-start(bf16[3,256,128]{2,1,0:T(8,128)(2,1)S(1)} %get-tuple-element.101), channel_id=1, source_target_pairs={{0,4},{4,0},{8,12},{12,8},{16,20},{20,16},{24,28},{28,24},{1,5},{5... | collective-permute-start | bytes 589832 | tf_op jit(solution)/shard_map/ppermute | solution.py:398
  50.3 1.5 %collective-permute-start.19 = (bf16[32,2048]{1,0:T(8,128)(2,1)S(1)}, bf16[32,2048]{1,0:T(8,128)(2,1)S(1)}, u32[]{:S(2)}, u32[]{:S(2)}) collective-permute-start(bf16[32,2048]{1,0:T(8,128)(2,1)S(1)} %get-tuple-element.95), channel_id=1, source_target_pairs={{0,2},{1,3},{2,0},{3,1},{4,6},{5,7},{6,4},{7,5},{8,10},{9,11},{10,... | collective-permute-start | bytes 393224 | tf_op jit(solution)/shard_map/ppermute | solution.py:398
  51.8 3.4 %collective-permute-done.18.refs_1_ = bf16[32,2048]{1,0:T(8,128)(2,1)S(1)} collective-permute-done((bf16[32,2048]{1,0:T(8,128)(2,1)S(1)}, bf16[32,2048]{1,0:T(8,128)(2,1)S(1)}, u32[]{:S(2)}, u32[]{:S(2)}) %collective-permute-start.18) | collective-permute-done | bytes 131104 | tf_op jit(solution)/shard_map/ppermute | solution.py:398
  55.2 1.4 %collective-permute-done.19.refs_2_ = bf16[32,2048]{1,0:T(8,128)(2,1)S(1)} collective-permute-done((bf16[32,2048]{1,0:T(8,128)(2,1)S(1)}, bf16[32,2048]{1,0:T(8,128)(2,1)S(1)}, u32[]{:S(2)}, u32[]{:S(2)}) %collective-permute-start.19) | collective-permute-done | bytes 131104 | tf_op jit(solution)/shard_map/ppermute | solution.py:398
  57.7 1.1 %shard_map.95 = (bf16[256,512]{1,0:T(8,128)(2,1)}, bf16[256,512]{1,0:T(8,128)(2,1)}, bf16[256,512]{1,0:T(8,128)(2,1)}, bf16[64,2048]{1,0:T(8,128)(2,1)}) custom-call(f32[64,2048]{1,0:T(8,128)S(1)} %get-tuple-element.93._.refs_0_, bf16[32,2048]{1,0:T(8,128)(2,1)S(1)} %collective-permute-done.18.refs_1_, bf16[32,2048]{1,0:T(8,128)(2,1)S(1)} %collective-permute-done.19.refs_2_, ...), custom_call_target="tpu_custom_call" | custom-call | tf_op jit(solution)/shard_map/pallas_call | solution.py:38
  (40 shorter events, 11.3 us)
Async XLA Ops:
  0.6 11.9 %collective-permute-start.3 = (bf16[64,2048]{1,0:T(8,128)(2,1)}, bf16[64,2048]{1,0:T(8,128)(2,1)S(1)}, u32[]{:S(2)}, u32[]{:S(2)}) collective-permute-start(bf16[64,2048]{1,0:T(8,128)(2,1)} %refs_0_.1), channel_id=1, source_target_pairs={{0,2},{1,3},{2,0},{3,1},{4,6},{5,7},{6,4},{7,5},{8,10},{9,11},{10,... | collective-permute-start | bytes 786440 | tf_op jit(solution)/shard_map/ppermute | solution.py:398
  4.9 10.4 %collective-permute-start = (bf16[3,256,128]{2,1,0:T(8,128)(2,1)S(1)}, bf16[3,256,128]{2,1,0:T(8,128)(2,1)S(1)}, u32[]{:S(2)}, u32[]{:S(2)}) collective-permute-start(bf16[3,256,128]{2,1,0:T(8,128)(2,1)S(1)} %get-tuple-element.56.refs_1_), channel_id=1, source_target_pairs={{0,12},{4,8},{8,4},{12,0},{16,28},{20,24},{24,20},{28,16},{1,13},{... | collective-permute-start | bytes 589832 | tf_op jit(solution)/shard_map/ppermute | solution.py:398
  7.5 11.8 %collective-permute-start.1 = (bf16[3,256,128]{2,1,0:T(8,128)(2,1)S(1)}, bf16[3,256,128]{2,1,0:T(8,128)(2,1)S(1)}, u32[]{:S(2)}, u32[]{:S(2)}) collective-permute-start(bf16[3,256,128]{2,1,0:T(8,128)(2,1)S(1)} %get-tuple-element.57.refs_2_), channel_id=1, source_target_pairs={{0,8},{4,12},{8,0},{12,4},{16,24},{20,28},{24,16},{28,20},{1,9},{5... | collective-permute-start | bytes 589832 | tf_op jit(solution)/shard_map/ppermute | solution.py:398
  8.0 11.4 %collective-permute-start.2 = (bf16[3,256,128]{2,1,0:T(8,128)(2,1)S(1)}, bf16[3,256,128]{2,1,0:T(8,128)(2,1)S(1)}, u32[]{:S(2)}, u32[]{:S(2)}) collective-permute-start(bf16[3,256,128]{2,1,0:T(8,128)(2,1)S(1)} %get-tuple-element.58.refs_3_), channel_id=1, source_target_pairs={{0,4},{4,0},{8,12},{12,8},{16,20},{20,16},{24,28},{28,24},{1,5},{5... | collective-permute-start | bytes 589832 | tf_op jit(solution)/shard_map/ppermute | solution.py:398
  9.9 11.6 %collective-permute-start.6 = (bf16[4,2,64,128]{3,2,1,0:T(8,128)(2,1)S(1)}, bf16[4,2,64,128]{3,2,1,0:T(8,128)(2,1)S(1)}, u32[]{:S(2)}, u32[]{:S(2)}) collective-permute-start(bf16[4,2,64,128]{3,2,1,0:T(8,128)(2,1)S(1)} %shard_map.87), channel_id=1, source_target_pairs={{0,16},{4,20},{8,24},{12,28},{16,0},{20,4},{24,8},{28,12},{1,17},{... | collective-permute-start | bytes 393224 | tf_op jit(solution)/shard_map/ppermute | solution.py:398
  15.2 6.3 %collective-permute-start.4 = (bf16[64,2048]{1,0:T(8,128)(2,1)S(1)}, bf16[64,2048]{1,0:T(8,128)(2,1)S(1)}, u32[]{:S(2)}, u32[]{:S(2)}) collective-permute-start(bf16[64,2048]{1,0:T(8,128)(2,1)S(1)} %get-tuple-element.62.refs_0_), channel_id=1, source_target_pairs={{0,1},{1,0},{2,3},{3,2},{4,5},{5,4},{6,7},{7,6},{8,9},{9,8},{10,11... | collective-permute-start | bytes 786440 | tf_op jit(solution)/shard_map/ppermute | solution.py:398
  15.3 6.2 %collective-permute-start.5 = (bf16[64,2048]{1,0:T(8,128)(2,1)S(1)}, bf16[64,2048]{1,0:T(8,128)(2,1)S(1)}, u32[]{:S(2)}, u32[]{:S(2)}) collective-permute-start(bf16[64,2048]{1,0:T(8,128)(2,1)S(1)} %get-tuple-element.63.refs_2_), channel_id=1, source_target_pairs={{0,1},{1,0},{2,3},{3,2},{4,5},{5,4},{6,7},{7,6},{8,9},{9,8},{10,11... | collective-permute-start | bytes 786440 | tf_op jit(solution)/shard_map/ppermute | solution.py:398
  19.8 8.3 %collective-permute-start.7 = (bf16[2,256,128]{2,1,0:T(8,128)(2,1)S(1)}, bf16[2,256,128]{2,1,0:T(8,128)(2,1)S(1)}, u32[]{:S(2)}, u32[]{:S(2)}) collective-permute-start(bf16[2,256,128]{2,1,0:T(8,128)(2,1)S(1)} %get-tuple-element.71), channel_id=1, source_target_pairs={{0,16},{4,20},{8,24},{12,28},{16,0},{20,4},{24,8},{28,12},{1,17},{... | collective-permute-start | bytes 393224 | tf_op jit(solution)/shard_map/ppermute | solution.py:398
  22.4 7.0 %collective-permute-start.8 = (bf16[384,128]{1,0:T(8,128)(2,1)S(1)}, bf16[384,128]{1,0:T(8,128)(2,1)S(1)}, u32[]{:S(2)}, u32[]{:S(2)}) collective-permute-start(bf16[384,128]{1,0:T(8,128)(2,1)S(1)} %get-tuple-element.72), channel_id=1, source_target_pairs={{0,12},{4,8},{8,4},{12,0},{16,28},{20,24},{24,20},{28,16},{1,13},{... | collective-permute-start | bytes 294920 | tf_op jit(solution)/shard_map/ppermute | solution.py:398
  24.7 5.4 %collective-permute-start.9 = (bf16[384,128]{1,0:T(8,128)(2,1)S(1)}, bf16[384,128]{1,0:T(8,128)(2,1)S(1)}, u32[]{:S(2)}, u32[]{:S(2)}) collective-permute-start(bf16[384,128]{1,0:T(8,128)(2,1)S(1)} %get-tuple-element.73), channel_id=1, source_target_pairs={{0,8},{4,12},{8,0},{12,4},{16,24},{20,28},{24,16},{28,20},{1,9},{5... | collective-permute-start | bytes 294920 | tf_op jit(solution)/shard_map/ppermute | solution.py:398
  25.0 5.1 %collective-permute-start.10 = (bf16[384,128]{1,0:T(8,128)(2,1)S(1)}, bf16[384,128]{1,0:T(8,128)(2,1)S(1)}, u32[]{:S(2)}, u32[]{:S(2)}) collective-permute-start(bf16[384,128]{1,0:T(8,128)(2,1)S(1)} %get-tuple-element.74), channel_id=1, source_target_pairs={{0,4},{4,0},{8,12},{12,8},{16,20},{20,16},{24,28},{28,24},{1,5},{5... | collective-permute-start | bytes 294920 | tf_op jit(solution)/shard_map/ppermute | solution.py:398
  32.1 13.8 %collective-permute-start.20 = (bf16[4,256,128]{2,1,0:T(8,128)(2,1)S(1)}, bf16[4,256,128]{2,1,0:T(8,128)(2,1)S(1)}, u32[]{:S(2)}, u32[]{:S(2)}) collective-permute-start(bf16[4,256,128]{2,1,0:T(8,128)(2,1)S(1)} %get-tuple-element.97), channel_id=1, source_target_pairs={{0,16},{4,20},{8,24},{12,28},{16,0},{20,4},{24,8},{28,12},{1,17},{... | collective-permute-start | bytes 786440 | tf_op jit(solution)/shard_map/ppermute | solution.py:398
  33.2 7.3 %collective-permute-start.11 = (bf16[256,128]{1,0:T(8,128)(2,1)S(1)}, bf16[256,128]{1,0:T(8,128)(2,1)S(1)}, u32[]{:S(2)}, u32[]{:S(2)}) collective-permute-start(bf16[256,128]{1,0:T(8,128)(2,1)S(1)} %get-tuple-element.76), channel_id=1, source_target_pairs={{0,12},{4,8},{8,4},{12,0},{16,28},{20,24},{24,20},{28,16},{1,13},{... | collective-permute-start | bytes 196616 | tf_op jit(solution)/shard_map/ppermute | solution.py:398
  35.9 5.1 %collective-permute-start.12 = (bf16[256,128]{1,0:T(8,128)(2,1)S(1)}, bf16[256,128]{1,0:T(8,128)(2,1)S(1)}, u32[]{:S(2)}, u32[]{:S(2)}) collective-permute-start(bf16[256,128]{1,0:T(8,128)(2,1)S(1)} %get-tuple-element.77), channel_id=1, source_target_pairs={{0,8},{4,12},{8,0},{12,4},{16,24},{20,28},{24,16},{28,20},{1,9},{5... | collective-permute-start | bytes 196616 | tf_op jit(solution)/shard_map/ppermute | solution.py:398
  36.0 5.1 %collective-permute-start.13 = (bf16[256,128]{1,0:T(8,128)(2,1)S(1)}, bf16[256,128]{1,0:T(8,128)(2,1)S(1)}, u32[]{:S(2)}, u32[]{:S(2)}) collective-permute-start(bf16[256,128]{1,0:T(8,128)(2,1)S(1)} %get-tuple-element.78), channel_id=1, source_target_pairs={{0,4},{4,0},{8,12},{12,8},{16,20},{20,16},{24,28},{28,24},{1,5},{5... | collective-permute-start | bytes 196616 | tf_op jit(solution)/shard_map/ppermute | solution.py:398
  41.9 1.4 %collective-permute-start.14 = (bf16[32,2048]{1,0:T(8,128)(2,1)S(1)}, bf16[32,2048]{1,0:T(8,128)(2,1)S(1)}, u32[]{:S(2)}, u32[]{:S(2)}) collective-permute-start(bf16[32,2048]{1,0:T(8,128)(2,1)S(1)} %get-tuple-element.89), channel_id=1, source_target_pairs={{0,1},{1,0},{2,3},{3,2},{4,5},{5,4},{6,7},{7,6},{8,9},{9,8},{10,11... | collective-permute-start | bytes 393224 | tf_op jit(solution)/shard_map/ppermute | solution.py:398
  41.9 1.5 %collective-permute-start.15 = (bf16[32,2048]{1,0:T(8,128)(2,1)S(1)}, bf16[32,2048]{1,0:T(8,128)(2,1)S(1)}, u32[]{:S(2)}, u32[]{:S(2)}) collective-permute-start(bf16[32,2048]{1,0:T(8,128)(2,1)S(1)} %get-tuple-element.90), channel_id=1, source_target_pairs={{0,1},{1,0},{2,3},{3,2},{4,5},{5,4},{6,7},{7,6},{8,9},{9,8},{10,11... | collective-permute-start | bytes 393224 | tf_op jit(solution)/shard_map/ppermute | solution.py:398
  42.4 1.3 %collective-permute-start.16 = (bf16[32,2048]{1,0:T(8,128)(2,1)S(1)}, bf16[32,2048]{1,0:T(8,128)(2,1)S(1)}, u32[]{:S(2)}, u32[]{:S(2)}) collective-permute-start(bf16[32,2048]{1,0:T(8,128)(2,1)S(1)} %get-tuple-element.91), channel_id=1, source_target_pairs={{0,1},{1,0},{2,3},{3,2},{4,5},{5,4},{6,7},{7,6},{8,9},{9,8},{10,11... | collective-permute-start | bytes 393224 | tf_op jit(solution)/shard_map/ppermute | solution.py:398
  42.5 1.5 %collective-permute-start.17 = (bf16[32,2048]{1,0:T(8,128)(2,1)S(1)}, bf16[32,2048]{1,0:T(8,128)(2,1)S(1)}, u32[]{:S(2)}, u32[]{:S(2)}) collective-permute-start(bf16[32,2048]{1,0:T(8,128)(2,1)S(1)} %get-tuple-element.92), channel_id=1, source_target_pairs={{0,1},{1,0},{2,3},{3,2},{4,5},{5,4},{6,7},{7,6},{8,9},{9,8},{10,11... | collective-permute-start | bytes 393224 | tf_op jit(solution)/shard_map/ppermute | solution.py:398
  46.3 10.3 %collective-permute-start.21 = (bf16[3,256,128]{2,1,0:T(8,128)(2,1)S(1)}, bf16[3,256,128]{2,1,0:T(8,128)(2,1)S(1)}, u32[]{:S(2)}, u32[]{:S(2)}) collective-permute-start(bf16[3,256,128]{2,1,0:T(8,128)(2,1)S(1)} %get-tuple-element.99), channel_id=1, source_target_pairs={{0,12},{4,8},{8,4},{12,0},{16,28},{20,24},{24,20},{28,16},{1,13},{... | collective-permute-start | bytes 589832 | tf_op jit(solution)/shard_map/ppermute | solution.py:398
  47.2 10.1 %collective-permute-start.22 = (bf16[3,256,128]{2,1,0:T(8,128)(2,1)S(1)}, bf16[3,256,128]{2,1,0:T(8,128)(2,1)S(1)}, u32[]{:S(2)}, u32[]{:S(2)}) collective-permute-start(bf16[3,256,128]{2,1,0:T(8,128)(2,1)S(1)} %get-tuple-element.100), channel_id=1, source_target_pairs={{0,8},{4,12},{8,0},{12,4},{16,24},{20,28},{24,16},{28,20},{1,9},{5... | collective-permute-start | bytes 589832 | tf_op jit(solution)/shard_map/ppermute | solution.py:398
  48.4 9.2 %collective-permute-start.23 = (bf16[3,256,128]{2,1,0:T(8,128)(2,1)S(1)}, bf16[3,256,128]{2,1,0:T(8,128)(2,1)S(1)}, u32[]{:S(2)}, u32[]{:S(2)}) collective-permute-start(bf16[3,256,128]{2,1,0:T(8,128)(2,1)S(1)} %get-tuple-element.101), channel_id=1, source_target_pairs={{0,4},{4,0},{8,12},{12,8},{16,20},{20,16},{24,28},{28,24},{1,5},{5... | collective-permute-start | bytes 589832 | tf_op jit(solution)/shard_map/ppermute | solution.py:398
  49.8 5.4 %collective-permute-start.18 = (bf16[32,2048]{1,0:T(8,128)(2,1)S(1)}, bf16[32,2048]{1,0:T(8,128)(2,1)S(1)}, u32[]{:S(2)}, u32[]{:S(2)}) collective-permute-start(bf16[32,2048]{1,0:T(8,128)(2,1)S(1)} %get-tuple-element.94), channel_id=1, source_target_pairs={{0,2},{1,3},{2,0},{3,1},{4,6},{5,7},{6,4},{7,5},{8,10},{9,11},{10,... | collective-permute-start | bytes 393224 | tf_op jit(solution)/shard_map/ppermute | solution.py:398
  50.3 6.3 %collective-permute-start.19 = (bf16[32,2048]{1,0:T(8,128)(2,1)S(1)}, bf16[32,2048]{1,0:T(8,128)(2,1)S(1)}, u32[]{:S(2)}, u32[]{:S(2)}) collective-permute-start(bf16[32,2048]{1,0:T(8,128)(2,1)S(1)} %get-tuple-element.95), channel_id=1, source_target_pairs={{0,2},{1,3},{2,0},{3,1},{4,6},{5,7},{6,4},{7,5},{8,10},{9,11},{10,... | collective-permute-start | bytes 393224 | tf_op jit(solution)/shard_map/ppermute | solution.py:398
  (2 other events, 2.5 us)

commit v15 on v14

--- a/solution.py
+++ b/solution.py
@@ -9,6 +9,7 @@
 
 HEAD_DIM = 128
 BLOCK = 256
+REST = 3 * BLOCK // 4
 LEVELS = 2
 GROUP = 4
 STEPS = (0, 3, 2, 1)
@@ -51,7 +52,8 @@
 
 
 def span(index, size):
-    return pl.ds(pl.multiple_of(index * size, size), size)
+    start = index * size
+    return pl.ds(start if isinstance(start, int) else pl.multiple_of(start, size), size)
 
 
 def iota(dims, axis):
@@ -158,8 +160,12 @@
 
 def from_others(groups, refs):
     if groups == 2:
-        return (refs[0].at[:2], refs[0].at[2:], refs[0].at[2:]), refs[1:]
+        return (refs[0].at[: 2 * REST], refs[0].at[2 * REST :], refs[0].at[2 * REST :]), refs[1:]
     return refs[:3], refs[3:]
+
+
+def odd_group():
+    return lax.rem(lax.axis_index("seq") // GROUP, 2)
 
 
 def near_sides(b, nb):
@@ -208,7 +214,7 @@
     (rim_low, rim_high), refs = from_beside(groups, refs)
     chunks, refs = refs[:GROUP], refs[GROUP:]
     (prob, grads, top_2, deltas, far_shift, rim_shift), refs = refs[:6], refs[6:]
-    outs, (*rim_outs, attended, far_prob, rim_prob, row, context_t) = refs[:GROUP], refs[GROUP:]
+    outs, (*rim_outs, attended, far_prob, rim_prob, row, context_t, far_sums) = refs[:GROUP], refs[GROUP:]
     rims = rims_of(nb, groups, rim_low, rim_high)
     me = member()
     quarter = BLOCK // 4
@@ -259,19 +265,30 @@
     grad = grads[...].reshape(tokens, HEAD_DIM)
     slope = dot_nt(top_2[1], grad)
     far_shift[...] = (far_prob[...].astype(F32) * (slope - deltas[:1])).astype(BF16)
-    rim_outs[0][0] = (SCALE * dot(far_shift[...], coarse_query)).astype(BF16)
-    rim_outs[0][1] = dot(far_prob[...], grad).astype(BF16)
+    far_sums[0] = SCALE * dot(far_shift[...], coarse_query)
+    far_sums[1] = dot(far_prob[...], grad)
+    odd = odd_group()
+    spread = spreading(2)
+    folded = []
+    for part in range(2):
+        rest = far_sums[part, pl.ds(pl.multiple_of((1 - odd) * quarter, quarter), REST), :]
+        rim_outs[0][part * REST : (part + 1) * REST] = rest.astype(BF16)
+        high, low = halves(far_sums[part, pl.ds(pl.multiple_of(odd * REST, quarter), quarter), :])
+        folded.append(dot(spread, high) + dot(spread, low))
     pairs = []
     for i, (b, block, _) in enumerate(rims):
         slope = dot_nt(block[1], grads[b])
         rim_shift[i] = (rim_prob[i].astype(F32) * (slope - deltas[:1, span(b, BLOCK)])).astype(BF16)
         pairs.append((SCALE * dot(rim_shift[i], query[0, b]), dot(rim_prob[i], grads[b])))
     for part in range(2):
+        at = slice(part * BLOCK, (part + 1) * BLOCK)
         if groups == 2:
-            rim_outs[0][2 + part] = pairs[0][part].astype(BF16)
+            rim_outs[0][2 * REST + part * BLOCK : 2 * REST + (part + 1) * BLOCK] = (
+                pairs[0][part] + folded[part]
+            ).astype(BF16)
         else:
-            rim_outs[1][part] = pairs[1][part].astype(BF16)
-            rim_outs[2][part] = pairs[0][part].astype(BF16)
+            rim_outs[1][at] = (pairs[1][part] + jnp.where(odd == 0, folded[part], 0.0)).astype(BF16)
+            rim_outs[2][at] = (pairs[0][part] + jnp.where(odd == 1, folded[part], 0.0)).astype(BF16)
     for step, out in zip(STEPS, outs):
         out[...] = attended[me ^ step]
 
@@ -333,13 +350,20 @@
     present = rim_present(groups)
     spread = spreading(2)
     quarter = BLOCK // 4
+    odd = odd_group()
     for b in range(nb):
         for part in range(2):
-            total = grad_kv[part, b] + dot(spread, got_top[part, b * quarter : (b + 1) * quarter])
+            total = grad_kv[part, b]
+            place = 0 if b == 0 else 2 if b == nb - 1 else b - odd
+            level = dot(spread, got_top[span(part * (REST // quarter) + place, quarter), :])
+            rim = slice(part * BLOCK, (part + 1) * BLOCK)
             if b == 0:
-                total = total + jnp.where(present[0], got_low[part].astype(F32), 0.0)
+                level = jnp.where(odd == 0, level, 0.0)
+                total = total + jnp.where(present[0], got_low[rim].astype(F32), 0.0)
             if b == nb - 1:
-                total = total + jnp.where(present[1], got_high[part].astype(F32), 0.0)
+                level = jnp.where(odd == 1, level, 0.0)
+                total = total + jnp.where(present[1], got_high[rim].astype(F32), 0.0)
+            total = total + level
             out[b, part] = total.astype(BF16)
     me = member()
     for step, chunk in zip(STEPS, outs):
@@ -432,7 +456,9 @@
     half, quarter = rows // 2, rows // 4
     model = out_weight.shape[1]
     block = shape(2, rows, HEAD_DIM)
-    sent = [shape(4, rows, HEAD_DIM)] if groups == 2 else [block] * 3
+    sent = [shape(2 * REST + 2 * rows, HEAD_DIM)]
+    if groups > 2:
+        sent = [shape(2 * REST, HEAD_DIM)] + [shape(2 * rows, HEAD_DIM)] * 2
     rims = [block] * (1 if groups == 2 else 2)
     quarter = rows // 4
     in_order = shape(nb, rows, HEAD_DIM)
@@ -509,6 +535,7 @@
             pltpu.VMEM(rim_square.shape, BF16),
             pltpu.VMEM((8, tokens), F32),
             pltpu.VMEM((HEAD_DIM, tokens), F32),
+            pltpu.VMEM((2, BLOCK, HEAD_DIM), F32),
         ],
         flops=score_flops,
     )
@@ -524,7 +551,6 @@
             pltpu.VMEM((2, tokens // 2, HEAD_DIM), F32),
             pltpu.VMEM((HEAD_DIM, tokens), F32),
         ],
-        flops=1,
     )
     local = rows // N_MP
     kept, *given = call(
@@ -532,7 +558,6 @@
         [shape(2, local, model)] + [shape(local // 2, model)] * 4,
         (*attended, out_weight, grad_q),
         scratch=[pltpu.VMEM((rows, width), BF16), pltpu.VMEM((rows, model), BF16)],
-        flops=weight_flops,
     )
     *across, here = call(
         share_kernel,

time: 59 us -> 58.1 us (0.985)
  waiting for transfers between devices: 14.9 us -> 13.8 us
    ppermute x24, waiting for transfers between devices: 14.9 us -> 13.8 us  [swapped(): lax.ppermute(x, axis, [(i, i ^ step) for i in range(lax.axis_size(axis))])]
where the time goes in v15:
time: 58.1 us; the launch traced here: 57.9 us
  starting transfers between devices  27.1 us (47%)
  waiting for transfers between devices  13.8 us (24%)
  Pallas kernels  13.7 us (24%)
  local copies, waits for them, and re-layouts  2.54 us (4%)
  between operations  0.75 us (1%)
    ppermute x24, starting transfers between devices, swapped(): lax.ppermute(x, axis, [(i, i ^ step) for i in range(lax.axis_size(axis))])  27.1 us
    ppermute x24, waiting for transfers between devices, swapped(): lax.ppermute(x, axis, [(i, i ^ step) for i in range(lax.axis_size(axis))])  13.8 us
    pallas_call x12, Pallas kernels, call(): pl.pallas_call(kernel, out_shape=out_shape, in_specs=[kept if copied else...  13.7 us
    unnamed x4, local copies, waits for them, and re-layouts  2.54 us
  transfers between devices with their start and end apart: 24, of which 13 were waited for; matrix products, arithmetic and copies ran while one was open for 0% of the time, Pallas kernels for 17%

profile of v15, /device:TPU:0, one launch (start us, length us, event | category | flops | bytes accessed | tf_op | source)
XLA Modules:
  0.0 57.9 jit_solution(6604708013891795897)
XLA Ops:
  0.6 3.0 %collective-permute-start.3 = (bf16[64,2048]{1,0:T(8,128)(2,1)}, bf16[64,2048]{1,0:T(8,128)(2,1)S(1)}, u32[]{:S(2)}, u32[]{:S(2)}) collective-permute-start(bf16[64,2048]{1,0:T(8,128)(2,1)} %refs_0_.1), channel_id=1, source_target_pairs={{0,2},{1,3},{2,0},{3,1},{4,6},{5,7},{6,4},{7,5},{8,10},{9,11},{10,... | collective-permute-start | bytes 786440 | tf_op jit(solution)/shard_map/ppermute | solution.py:422
  3.6 1.3 %shard_map.84 = (bf16[3,256,128]{2,1,0:T(8,128)(2,1)S(1)}, bf16[3,256,128]{2,1,0:T(8,128)(2,1)S(1)}, bf16[3,256,128]{2,1,0:T(8,128)(2,1)S(1)}, bf16[3,256,128]{2,1,0:T(8,128)(2,1)S(1)}) custom-call(bf16[256,512]{1,0:T(8,128)(2,1)} %q.1, bf16[256,512]{1,0:T(8,128)(2,1)} %k.1, bf16[256,512]{1,0:T(8,128)(2,1)} %v.1), custom_call_target="tpu_custom_call" | custom-call | tf_op jit(solution)/shard_map/pallas_call | solution.py:39
  4.9 2.6 %collective-permute-start = (bf16[3,256,128]{2,1,0:T(8,128)(2,1)S(1)}, bf16[3,256,128]{2,1,0:T(8,128)(2,1)S(1)}, u32[]{:S(2)}, u32[]{:S(2)}) collective-permute-start(bf16[3,256,128]{2,1,0:T(8,128)(2,1)S(1)} %get-tuple-element.56.refs_1_), channel_id=1, source_target_pairs={{0,12},{4,8},{8,4},{12,0},{16,28},{20,24},{24,20},{28,16},{1,13},{... | collective-permute-start | bytes 589832 | tf_op jit(solution)/shard_map/ppermute | solution.py:422
  8.5 1.4 %shard_map.87 = bf16[4,2,64,128]{3,2,1,0:T(8,128)(2,1)S(1)} custom-call(bf16[3,256,128]{2,1,0:T(8,128)(2,1)S(1)} %get-tuple-element.55.refs_0_, bf16[3,256,128]{2,1,0:T(8,128)(2,1)S(1)} %get-tuple-element.56.refs_1_, bf16[3,256,128]{2,1,0:T(8,128)(2,1)S(1)} %get-tuple-element.57.refs_2_, bf16[3,256,128]{2,1,0:T(8,128)(2,1)S(1)} %get-tuple-element.58.refs_3_), custom_call_target="tpu_custom_call" | custom-call | tf_op jit(solution)/shard_map/pallas_call | solution.py:39
  9.9 2.6 %collective-permute-start.6 = (bf16[4,2,64,128]{3,2,1,0:T(8,128)(2,1)S(1)}, bf16[4,2,64,128]{3,2,1,0:T(8,128)(2,1)S(1)}, u32[]{:S(2)}, u32[]{:S(2)}) collective-permute-start(bf16[4,2,64,128]{3,2,1,0:T(8,128)(2,1)S(1)} %shard_map.87), channel_id=1, source_target_pairs={{0,16},{4,20},{8,24},{12,28},{16,0},{20,4},{24,8},{28,12},{1,17},{... | collective-permute-start | bytes 393224 | tf_op jit(solution)/shard_map/ppermute | solution.py:422
  12.5 1.6 %copy-done = bf16[512,2048]{1,0:T(8,128)(2,1)S(1)} copy-done((bf16[512,2048]{1,0:T(8,128)(2,1)S(1)}, bf16[512,2048]{1,0:T(8,128)(2,1)}, u32[]{:S(2)}) %copy-start) | copy-done | bytes 2097176
  14.1 0.9 %copy-done.1 = bf16[64,2048]{1,0:T(8,128)(2,1)S(1)} copy-done((bf16[64,2048]{1,0:T(8,128)(2,1)S(1)}, bf16[64,2048]{1,0:T(8,128)(2,1)}, u32[]{:S(2)}) %copy-start.1) | copy-done | bytes 262168
  15.8 3.6 %collective-permute-done.1.refs_2_ = bf16[3,256,128]{2,1,0:T(8,128)(2,1)S(1)} collective-permute-done((bf16[3,256,128]{2,1,0:T(8,128)(2,1)S(1)}, bf16[3,256,128]{2,1,0:T(8,128)(2,1)S(1)}, u32[]{:S(2)}, u32[]{:S(2)}) %collective-permute-start.1) | collective-permute-done | bytes 196640 | tf_op jit(solution)/shard_map/ppermute | solution.py:422
  19.8 1.7 %collective-permute-start.7 = (bf16[2,256,128]{2,1,0:T(8,128)(2,1)S(1)}, bf16[2,256,128]{2,1,0:T(8,128)(2,1)S(1)}, u32[]{:S(2)}, u32[]{:S(2)}) collective-permute-start(bf16[2,256,128]{2,1,0:T(8,128)(2,1)S(1)} %get-tuple-element.71), channel_id=1, source_target_pairs={{0,16},{4,20},{8,24},{12,28},{16,0},{20,4},{24,8},{28,12},{1,17},{... | collective-permute-start | bytes 393224 | tf_op jit(solution)/shard_map/ppermute | solution.py:422
  22.4 2.3 %collective-permute-start.8 = (bf16[384,128]{1,0:T(8,128)(2,1)S(1)}, bf16[384,128]{1,0:T(8,128)(2,1)S(1)}, u32[]{:S(2)}, u32[]{:S(2)}) collective-permute-start(bf16[384,128]{1,0:T(8,128)(2,1)S(1)} %get-tuple-element.72), channel_id=1, source_target_pairs={{0,12},{4,8},{8,4},{12,0},{16,28},{20,24},{24,20},{28,16},{1,13},{... | collective-permute-start | bytes 294920 | tf_op jit(solution)/shard_map/ppermute | solution.py:422
  25.0 1.4 %collective-permute-start.10 = (bf16[384,128]{1,0:T(8,128)(2,1)S(1)}, bf16[384,128]{1,0:T(8,128)(2,1)S(1)}, u32[]{:S(2)}, u32[]{:S(2)}) collective-permute-start(bf16[384,128]{1,0:T(8,128)(2,1)S(1)} %get-tuple-element.74), channel_id=1, source_target_pairs={{0,4},{4,0},{8,12},{12,8},{16,20},{20,16},{24,28},{28,24},{1,5},{5... | collective-permute-start | bytes 294920 | tf_op jit(solution)/shard_map/ppermute | solution.py:422
  26.4 1.7 %shard_map.89 = (bf16[3,4,256,128]{3,2,1,0:T(8,128)(2,1)S(1)}, bf16[128,1024]{1,0:T(8,128)(2,1)S(1)}, bf16[128,1024]{1,0:T(8,128)(2,1)S(1)}, bf16[128,512]{1,0:T...) custom-call(bf16[4,2,256,128]{3,2,1,0:T(8,128)(2,1)S(1)} %get-tuple-element.59, ...), custom_call_target="tpu_custom_call" | custom-call | flops 335544320 | bytes 6946816 | tf_op jit(solution)/shard_map/pallas_call | solution.py:39
  28.0 1.3 %collective-permute-done.8.refs_7_ = bf16[384,128]{1,0:T(8,128)(2,1)S(1)} collective-permute-done((bf16[384,128]{1,0:T(8,128)(2,1)S(1)}, bf16[384,128]{1,0:T(8,128)(2,1)S(1)}, u32[]{:S(2)}, u32[]{:S(2)}) %collective-permute-start.8) | collective-permute-done | bytes 98336 | tf_op jit(solution)/shard_map/ppermute | solution.py:422
  30.1 2.2 %shard_map.90 = (bf16[4,4,256,256]{3,2,1,0:T(8,128)(2,1)S(1)}, bf16[4,256,128]{2,1,0:T(8,128)(2,1)S(1)}, bf16[2,256,128]{2,1,0:T(8,128)(2,1)S(1)}, f32[8,1024]{1...) custom-call(bf16[3,4,256,128]{3,2,1,0:T(8,128)(2,1)S(1)} %get-tuple-, ...), custom_call_target="tpu_custom_call" | custom-call | flops 335544320 | bytes 9601024 | tf_op jit(solution)/shard_map/pallas_call | solution.py:39
  32.3 1.0 %collective-permute-start.20 = (bf16[896,128]{1,0:T(8,128)(2,1)S(1)}, bf16[896,128]{1,0:T(8,128)(2,1)S(1)}, u32[]{:S(2)}, u32[]{:S(2)}) collective-permute-start(bf16[896,128]{1,0:T(8,128)(2,1)S(1)} %get-tuple-element.97), channel_id=1, source_target_pairs={{0,16},{4,20},{8,24},{12,28},{16,0},{20,4},{24,8},{28,12},{1,17},{... | collective-permute-start | bytes 688136 | tf_op jit(solution)/shard_map/ppermute | solution.py:422
  33.3 2.8 %collective-permute-start.11 = (bf16[256,128]{1,0:T(8,128)(2,1)S(1)}, bf16[256,128]{1,0:T(8,128)(2,1)S(1)}, u32[]{:S(2)}, u32[]{:S(2)}) collective-permute-start(bf16[256,128]{1,0:T(8,128)(2,1)S(1)} %get-tuple-element.76), channel_id=1, source_target_pairs={{0,12},{4,8},{8,4},{12,0},{16,28},{20,24},{24,20},{28,16},{1,13},{... | collective-permute-start | bytes 196616 | tf_op jit(solution)/shard_map/ppermute | solution.py:422
  36.1 1.2 %collective-permute-start.13 = (bf16[256,128]{1,0:T(8,128)(2,1)S(1)}, bf16[256,128]{1,0:T(8,128)(2,1)S(1)}, u32[]{:S(2)}, u32[]{:S(2)}) collective-permute-start(bf16[256,128]{1,0:T(8,128)(2,1)S(1)} %get-tuple-element.78), channel_id=1, source_target_pairs={{0,4},{4,0},{8,12},{12,8},{16,20},{20,16},{24,28},{28,24},{1,5},{5... | collective-permute-start | bytes 196616 | tf_op jit(solution)/shard_map/ppermute | solution.py:422
  37.3 3.4 %shard_map.91 = (bf16[4,256,128]{2,1,0:T(8,128)(2,1)S(1)}, f32[2,4,256,128]{3,2,1,0:T(8,128)S(1)}) custom-call(bf16[3,4,256,128]{3,2,1,0:T(8,128)(2,1)S(1)} %get-tuple-element.66.refs_0_, bf16[4,2,256,128]{3,2,1,0:T(8,128)(2,1)S(1)} %get-tuple-element.59.near.refs_1_, bf16[2,512,128]{2,1,0:T(8,128)(2,1)S(1)} %get-tuple-element.61.level_1.refs_2_, ...), custom_call_target="tpu_custom_call" | custom-call | tf_op jit(solution)/shard_map/pallas_call | solution.py:39
  45.0 2.1 %collective-permute-start.21 = (bf16[3,256,128]{2,1,0:T(8,128)(2,1)S(1)}, bf16[3,256,128]{2,1,0:T(8,128)(2,1)S(1)}, u32[]{:S(2)}, u32[]{:S(2)}) collective-permute-start(bf16[3,256,128]{2,1,0:T(8,128)(2,1)S(1)} %get-tuple-element.99), channel_id=1, source_target_pairs={{0,12},{4,8},{8,4},{12,0},{16,28},{20,24},{24,20},{28,16},{1,13},{... | collective-permute-start | bytes 589832 | tf_op jit(solution)/shard_map/ppermute | solution.py:422
  47.2 1.4 %collective-permute-start.23 = (bf16[3,256,128]{2,1,0:T(8,128)(2,1)S(1)}, bf16[3,256,128]{2,1,0:T(8,128)(2,1)S(1)}, u32[]{:S(2)}, u32[]{:S(2)}) collective-permute-start(bf16[3,256,128]{2,1,0:T(8,128)(2,1)S(1)} %get-tuple-element.101), channel_id=1, source_target_pairs={{0,4},{4,0},{8,12},{12,8},{16,20},{20,16},{24,28},{28,24},{1,5},{5... | collective-permute-start | bytes 589832 | tf_op jit(solution)/shard_map/ppermute | solution.py:422
  49.1 1.5 %collective-permute-start.19 = (bf16[32,2048]{1,0:T(8,128)(2,1)S(1)}, bf16[32,2048]{1,0:T(8,128)(2,1)S(1)}, u32[]{:S(2)}, u32[]{:S(2)}) collective-permute-start(bf16[32,2048]{1,0:T(8,128)(2,1)S(1)} %get-tuple-element.95), channel_id=1, source_target_pairs={{0,2},{1,3},{2,0},{3,1},{4,6},{5,7},{6,4},{7,5},{8,10},{9,11},{10,... | collective-permute-start | bytes 393224 | tf_op jit(solution)/shard_map/ppermute | solution.py:422
  50.6 3.9 %collective-permute-done.18.refs_1_ = bf16[32,2048]{1,0:T(8,128)(2,1)S(1)} collective-permute-done((bf16[32,2048]{1,0:T(8,128)(2,1)S(1)}, bf16[32,2048]{1,0:T(8,128)(2,1)S(1)}, u32[]{:S(2)}, u32[]{:S(2)}) %collective-permute-start.18) | collective-permute-done | bytes 131104 | tf_op jit(solution)/shard_map/ppermute | solution.py:422
  54.5 1.4 %collective-permute-done.19.refs_2_ = bf16[32,2048]{1,0:T(8,128)(2,1)S(1)} collective-permute-done((bf16[32,2048]{1,0:T(8,128)(2,1)S(1)}, bf16[32,2048]{1,0:T(8,128)(2,1)S(1)}, u32[]{:S(2)}, u32[]{:S(2)}) %collective-permute-start.19) | collective-permute-done | bytes 131104 | tf_op jit(solution)/shard_map/ppermute | solution.py:422
  56.8 1.1 %shard_map.95 = (bf16[256,512]{1,0:T(8,128)(2,1)}, bf16[256,512]{1,0:T(8,128)(2,1)}, bf16[256,512]{1,0:T(8,128)(2,1)}, bf16[64,2048]{1,0:T(8,128)(2,1)}) custom-call(f32[64,2048]{1,0:T(8,128)S(1)} %get-tuple-element.93._.refs_0_, bf16[32,2048]{1,0:T(8,128)(2,1)S(1)} %collective-permute-done.18.refs_1_, bf16[32,2048]{1,0:T(8,128)(2,1)S(1)} %collective-permute-done.19.refs_2_, ...), custom_call_target="tpu_custom_call" | custom-call | tf_op jit(solution)/shard_map/pallas_call | solution.py:39
  (40 shorter events, 9.7 us)
Async XLA Ops:
  0.6 11.9 %collective-permute-start.3 = (bf16[64,2048]{1,0:T(8,128)(2,1)}, bf16[64,2048]{1,0:T(8,128)(2,1)S(1)}, u32[]{:S(2)}, u32[]{:S(2)}) collective-permute-start(bf16[64,2048]{1,0:T(8,128)(2,1)} %refs_0_.1), channel_id=1, source_target_pairs={{0,2},{1,3},{2,0},{3,1},{4,6},{5,7},{6,4},{7,5},{8,10},{9,11},{10,... | collective-permute-start | bytes 786440 | tf_op jit(solution)/shard_map/ppermute | solution.py:422
  4.9 10.4 %collective-permute-start = (bf16[3,256,128]{2,1,0:T(8,128)(2,1)S(1)}, bf16[3,256,128]{2,1,0:T(8,128)(2,1)S(1)}, u32[]{:S(2)}, u32[]{:S(2)}) collective-permute-start(bf16[3,256,128]{2,1,0:T(8,128)(2,1)S(1)} %get-tuple-element.56.refs_1_), channel_id=1, source_target_pairs={{0,12},{4,8},{8,4},{12,0},{16,28},{20,24},{24,20},{28,16},{1,13},{... | collective-permute-start | bytes 589832 | tf_op jit(solution)/shard_map/ppermute | solution.py:422
  7.5 11.8 %collective-permute-start.1 = (bf16[3,256,128]{2,1,0:T(8,128)(2,1)S(1)}, bf16[3,256,128]{2,1,0:T(8,128)(2,1)S(1)}, u32[]{:S(2)}, u32[]{:S(2)}) collective-permute-start(bf16[3,256,128]{2,1,0:T(8,128)(2,1)S(1)} %get-tuple-element.57.refs_2_), channel_id=1, source_target_pairs={{0,8},{4,12},{8,0},{12,4},{16,24},{20,28},{24,16},{28,20},{1,9},{5... | collective-permute-start | bytes 589832 | tf_op jit(solution)/shard_map/ppermute | solution.py:422
  8.0 11.4 %collective-permute-start.2 = (bf16[3,256,128]{2,1,0:T(8,128)(2,1)S(1)}, bf16[3,256,128]{2,1,0:T(8,128)(2,1)S(1)}, u32[]{:S(2)}, u32[]{:S(2)}) collective-permute-start(bf16[3,256,128]{2,1,0:T(8,128)(2,1)S(1)} %get-tuple-element.58.refs_3_), channel_id=1, source_target_pairs={{0,4},{4,0},{8,12},{12,8},{16,20},{20,16},{24,28},{28,24},{1,5},{5... | collective-permute-start | bytes 589832 | tf_op jit(solution)/shard_map/ppermute | solution.py:422
  9.9 11.6 %collective-permute-start.6 = (bf16[4,2,64,128]{3,2,1,0:T(8,128)(2,1)S(1)}, bf16[4,2,64,128]{3,2,1,0:T(8,128)(2,1)S(1)}, u32[]{:S(2)}, u32[]{:S(2)}) collective-permute-start(bf16[4,2,64,128]{3,2,1,0:T(8,128)(2,1)S(1)} %shard_map.87), channel_id=1, source_target_pairs={{0,16},{4,20},{8,24},{12,28},{16,0},{20,4},{24,8},{28,12},{1,17},{... | collective-permute-start | bytes 393224 | tf_op jit(solution)/shard_map/ppermute | solution.py:422
  15.2 6.3 %collective-permute-start.4 = (bf16[64,2048]{1,0:T(8,128)(2,1)S(1)}, bf16[64,2048]{1,0:T(8,128)(2,1)S(1)}, u32[]{:S(2)}, u32[]{:S(2)}) collective-permute-start(bf16[64,2048]{1,0:T(8,128)(2,1)S(1)} %get-tuple-element.62.refs_0_), channel_id=1, source_target_pairs={{0,1},{1,0},{2,3},{3,2},{4,5},{5,4},{6,7},{7,6},{8,9},{9,8},{10,11... | collective-permute-start | bytes 786440 | tf_op jit(solution)/shard_map/ppermute | solution.py:422
  15.3 6.2 %collective-permute-start.5 = (bf16[64,2048]{1,0:T(8,128)(2,1)S(1)}, bf16[64,2048]{1,0:T(8,128)(2,1)S(1)}, u32[]{:S(2)}, u32[]{:S(2)}) collective-permute-start(bf16[64,2048]{1,0:T(8,128)(2,1)S(1)} %get-tuple-element.63.refs_2_), channel_id=1, source_target_pairs={{0,1},{1,0},{2,3},{3,2},{4,5},{5,4},{6,7},{7,6},{8,9},{9,8},{10,11... | collective-permute-start | bytes 786440 | tf_op jit(solution)/shard_map/ppermute | solution.py:422
  19.8 8.3 %collective-permute-start.7 = (bf16[2,256,128]{2,1,0:T(8,128)(2,1)S(1)}, bf16[2,256,128]{2,1,0:T(8,128)(2,1)S(1)}, u32[]{:S(2)}, u32[]{:S(2)}) collective-permute-start(bf16[2,256,128]{2,1,0:T(8,128)(2,1)S(1)} %get-tuple-element.71), channel_id=1, source_target_pairs={{0,16},{4,20},{8,24},{12,28},{16,0},{20,4},{24,8},{28,12},{1,17},{... | collective-permute-start | bytes 393224 | tf_op jit(solution)/shard_map/ppermute | solution.py:422
  22.4 7.0 %collective-permute-start.8 = (bf16[384,128]{1,0:T(8,128)(2,1)S(1)}, bf16[384,128]{1,0:T(8,128)(2,1)S(1)}, u32[]{:S(2)}, u32[]{:S(2)}) collective-permute-start(bf16[384,128]{1,0:T(8,128)(2,1)S(1)} %get-tuple-element.72), channel_id=1, source_target_pairs={{0,12},{4,8},{8,4},{12,0},{16,28},{20,24},{24,20},{28,16},{1,13},{... | collective-permute-start | bytes 294920 | tf_op jit(solution)/shard_map/ppermute | solution.py:422
  24.7 5.4 %collective-permute-start.9 = (bf16[384,128]{1,0:T(8,128)(2,1)S(1)}, bf16[384,128]{1,0:T(8,128)(2,1)S(1)}, u32[]{:S(2)}, u32[]{:S(2)}) collective-permute-start(bf16[384,128]{1,0:T(8,128)(2,1)S(1)} %get-tuple-element.73), channel_id=1, source_target_pairs={{0,8},{4,12},{8,0},{12,4},{16,24},{20,28},{24,16},{28,20},{1,9},{5... | collective-permute-start | bytes 294920 | tf_op jit(solution)/shard_map/ppermute | solution.py:422
  25.0 5.1 %collective-permute-start.10 = (bf16[384,128]{1,0:T(8,128)(2,1)S(1)}, bf16[384,128]{1,0:T(8,128)(2,1)S(1)}, u32[]{:S(2)}, u32[]{:S(2)}) collective-permute-start(bf16[384,128]{1,0:T(8,128)(2,1)S(1)} %get-tuple-element.74), channel_id=1, source_target_pairs={{0,4},{4,0},{8,12},{12,8},{16,20},{20,16},{24,28},{28,24},{1,5},{5... | collective-permute-start | bytes 294920 | tf_op jit(solution)/shard_map/ppermute | solution.py:422
  32.3 12.4 %collective-permute-start.20 = (bf16[896,128]{1,0:T(8,128)(2,1)S(1)}, bf16[896,128]{1,0:T(8,128)(2,1)S(1)}, u32[]{:S(2)}, u32[]{:S(2)}) collective-permute-start(bf16[896,128]{1,0:T(8,128)(2,1)S(1)} %get-tuple-element.97), channel_id=1, source_target_pairs={{0,16},{4,20},{8,24},{12,28},{16,0},{20,4},{24,8},{28,12},{1,17},{... | collective-permute-start | bytes 688136 | tf_op jit(solution)/shard_map/ppermute | solution.py:422
  33.3 7.3 %collective-permute-start.11 = (bf16[256,128]{1,0:T(8,128)(2,1)S(1)}, bf16[256,128]{1,0:T(8,128)(2,1)S(1)}, u32[]{:S(2)}, u32[]{:S(2)}) collective-permute-start(bf16[256,128]{1,0:T(8,128)(2,1)S(1)} %get-tuple-element.76), channel_id=1, source_target_pairs={{0,12},{4,8},{8,4},{12,0},{16,28},{20,24},{24,20},{28,16},{1,13},{... | collective-permute-start | bytes 196616 | tf_op jit(solution)/shard_map/ppermute | solution.py:422
  36.1 4.9 %collective-permute-start.12 = (bf16[256,128]{1,0:T(8,128)(2,1)S(1)}, bf16[256,128]{1,0:T(8,128)(2,1)S(1)}, u32[]{:S(2)}, u32[]{:S(2)}) collective-permute-start(bf16[256,128]{1,0:T(8,128)(2,1)S(1)} %get-tuple-element.77), channel_id=1, source_target_pairs={{0,8},{4,12},{8,0},{12,4},{16,24},{20,28},{24,16},{28,20},{1,9},{5... | collective-permute-start | bytes 196616 | tf_op jit(solution)/shard_map/ppermute | solution.py:422
  36.1 4.9 %collective-permute-start.13 = (bf16[256,128]{1,0:T(8,128)(2,1)S(1)}, bf16[256,128]{1,0:T(8,128)(2,1)S(1)}, u32[]{:S(2)}, u32[]{:S(2)}) collective-permute-start(bf16[256,128]{1,0:T(8,128)(2,1)S(1)} %get-tuple-element.78), channel_id=1, source_target_pairs={{0,4},{4,0},{8,12},{12,8},{16,20},{20,16},{24,28},{28,24},{1,5},{5... | collective-permute-start | bytes 196616 | tf_op jit(solution)/shard_map/ppermute | solution.py:422
  41.8 1.4 %collective-permute-start.14 = (bf16[32,2048]{1,0:T(8,128)(2,1)S(1)}, bf16[32,2048]{1,0:T(8,128)(2,1)S(1)}, u32[]{:S(2)}, u32[]{:S(2)}) collective-permute-start(bf16[32,2048]{1,0:T(8,128)(2,1)S(1)} %get-tuple-element.89), channel_id=1, source_target_pairs={{0,1},{1,0},{2,3},{3,2},{4,5},{5,4},{6,7},{7,6},{8,9},{9,8},{10,11... | collective-permute-start | bytes 393224 | tf_op jit(solution)/shard_map/ppermute | solution.py:422
  41.9 1.5 %collective-permute-start.15 = (bf16[32,2048]{1,0:T(8,128)(2,1)S(1)}, bf16[32,2048]{1,0:T(8,128)(2,1)S(1)}, u32[]{:S(2)}, u32[]{:S(2)}) collective-permute-start(bf16[32,2048]{1,0:T(8,128)(2,1)S(1)} %get-tuple-element.90), channel_id=1, source_target_pairs={{0,1},{1,0},{2,3},{3,2},{4,5},{5,4},{6,7},{7,6},{8,9},{9,8},{10,11... | collective-permute-start | bytes 393224 | tf_op jit(solution)/shard_map/ppermute | solution.py:422
  42.4 1.3 %collective-permute-start.16 = (bf16[32,2048]{1,0:T(8,128)(2,1)S(1)}, bf16[32,2048]{1,0:T(8,128)(2,1)S(1)}, u32[]{:S(2)}, u32[]{:S(2)}) collective-permute-start(bf16[32,2048]{1,0:T(8,128)(2,1)S(1)} %get-tuple-element.91), channel_id=1, source_target_pairs={{0,1},{1,0},{2,3},{3,2},{4,5},{5,4},{6,7},{7,6},{8,9},{9,8},{10,11... | collective-permute-start | bytes 393224 | tf_op jit(solution)/shard_map/ppermute | solution.py:422
  42.4 1.5 %collective-permute-start.17 = (bf16[32,2048]{1,0:T(8,128)(2,1)S(1)}, bf16[32,2048]{1,0:T(8,128)(2,1)S(1)}, u32[]{:S(2)}, u32[]{:S(2)}) collective-permute-start(bf16[32,2048]{1,0:T(8,128)(2,1)S(1)} %get-tuple-element.92), channel_id=1, source_target_pairs={{0,1},{1,0},{2,3},{3,2},{4,5},{5,4},{6,7},{7,6},{8,9},{9,8},{10,11... | collective-permute-start | bytes 393224 | tf_op jit(solution)/shard_map/ppermute | solution.py:422
  45.0 10.9 %collective-permute-start.21 = (bf16[3,256,128]{2,1,0:T(8,128)(2,1)S(1)}, bf16[3,256,128]{2,1,0:T(8,128)(2,1)S(1)}, u32[]{:S(2)}, u32[]{:S(2)}) collective-permute-start(bf16[3,256,128]{2,1,0:T(8,128)(2,1)S(1)} %get-tuple-element.99), channel_id=1, source_target_pairs={{0,12},{4,8},{8,4},{12,0},{16,28},{20,24},{24,20},{28,16},{1,13},{... | collective-permute-start | bytes 589832 | tf_op jit(solution)/shard_map/ppermute | solution.py:422
  47.2 8.9 %collective-permute-start.22 = (bf16[3,256,128]{2,1,0:T(8,128)(2,1)S(1)}, bf16[3,256,128]{2,1,0:T(8,128)(2,1)S(1)}, u32[]{:S(2)}, u32[]{:S(2)}) collective-permute-start(bf16[3,256,128]{2,1,0:T(8,128)(2,1)S(1)} %get-tuple-element.100), channel_id=1, source_target_pairs={{0,8},{4,12},{8,0},{12,4},{16,24},{20,28},{24,16},{28,20},{1,9},{5... | collective-permute-start | bytes 589832 | tf_op jit(solution)/shard_map/ppermute | solution.py:422
  47.2 9.6 %collective-permute-start.23 = (bf16[3,256,128]{2,1,0:T(8,128)(2,1)S(1)}, bf16[3,256,128]{2,1,0:T(8,128)(2,1)S(1)}, u32[]{:S(2)}, u32[]{:S(2)}) collective-permute-start(bf16[3,256,128]{2,1,0:T(8,128)(2,1)S(1)} %get-tuple-element.101), channel_id=1, source_target_pairs={{0,4},{4,0},{8,12},{12,8},{16,20},{20,16},{24,28},{28,24},{1,5},{5... | collective-permute-start | bytes 589832 | tf_op jit(solution)/shard_map/ppermute | solution.py:422
  48.6 5.9 %collective-permute-start.18 = (bf16[32,2048]{1,0:T(8,128)(2,1)S(1)}, bf16[32,2048]{1,0:T(8,128)(2,1)S(1)}, u32[]{:S(2)}, u32[]{:S(2)}) collective-permute-start(bf16[32,2048]{1,0:T(8,128)(2,1)S(1)} %get-tuple-element.94), channel_id=1, source_target_pairs={{0,2},{1,3},{2,0},{3,1},{4,6},{5,7},{6,4},{7,5},{8,10},{9,11},{10,... | collective-permute-start | bytes 393224 | tf_op jit(solution)/shard_map/ppermute | solution.py:422
  49.1 6.8 %collective-permute-start.19 = (bf16[32,2048]{1,0:T(8,128)(2,1)S(1)}, bf16[32,2048]{1,0:T(8,128)(2,1)S(1)}, u32[]{:S(2)}, u32[]{:S(2)}) collective-permute-start(bf16[32,2048]{1,0:T(8,128)(2,1)S(1)} %get-tuple-element.95), channel_id=1, source_target_pairs={{0,2},{1,3},{2,0},{3,1},{4,6},{5,7},{6,4},{7,5},{8,10},{9,11},{10,... | collective-permute-start | bytes 393224 | tf_op jit(solution)/shard_map/ppermute | solution.py:422
  (2 other events, 2.5 us)

commit v16 on v15

--- a/solution.py
+++ b/solution.py
@@ -345,7 +345,7 @@
             here[at, :] = total
 
 
-def combine_kernel(nb, groups, grad_q, grad_kv, _, *refs):
+def combine_kernel(nb, groups, grad_q, grad_kv, *refs):
     (got_top, got_low, got_high), (*outs, out) = from_others(groups, refs)
     present = rim_present(groups)
     spread = spreading(2)
@@ -567,7 +567,7 @@
     chunks = call(
         functools.partial(combine_kernel, nb, groups),
         [triple] * GROUP,
-        (grad_q, grad_kv, here, *other_grads),
+        (grad_q, grad_kv, *other_grads),
         scratch=[pltpu.VMEM((nb, 2, rows, HEAD_DIM), BF16)],
         flops=20 * score_flops,
     )

time: 58.1 us -> 57.8 us (level)
  transfers between devices with their start and end apart: 24 -> 24, of which waited for: 13 -> 9; matrix products, arithmetic and copies ran while one was open for 0% -> 0% of each run, Pallas kernels for 17% -> 18%
where the time goes in v16:
time: 57.8 us; the launch traced here: 57.5 us
  starting transfers between devices  27.2 us (47%)
  Pallas kernels  13.7 us (24%)
  waiting for transfers between devices  13.4 us (23%)
  local copies, waits for them, and re-layouts  2.54 us (4%)
  between operations  0.75 us (1%)
    ppermute x24, starting transfers between devices, swapped(): lax.ppermute(x, axis, [(i, i ^ step) for i in range(lax.axis_size(axis))])  27.2 us
    pallas_call x12, Pallas kernels, call(): pl.pallas_call(kernel, out_shape=out_shape, in_specs=[kept if copied else...  13.7 us
    ppermute x24, waiting for transfers between devices, swapped(): lax.ppermute(x, axis, [(i, i ^ step) for i in range(lax.axis_size(axis))])  13.4 us
    unnamed x4, local copies, waits for them, and re-layouts  2.54 us
  transfers between devices with their start and end apart: 24, of which 9 were waited for; matrix products, arithmetic and copies ran while one was open for 0% of the time, Pallas kernels for 18%

profile of v16, /device:TPU:0, one launch (start us, length us, event | category | flops | bytes accessed | tf_op | source)
XLA Modules:
  0.0 57.5 jit_solution(1786564557325571779)
XLA Ops:
  0.6 3.0 %collective-permute-start.3 = (bf16[64,2048]{1,0:T(8,128)(2,1)}, bf16[64,2048]{1,0:T(8,128)(2,1)S(1)}, u32[]{:S(2)}, u32[]{:S(2)}) collective-permute-start(bf16[64,2048]{1,0:T(8,128)(2,1)} %refs_0_.1), channel_id=1, source_target_pairs={{0,2},{1,3},{2,0},{3,1},{4,6},{5,7},{6,4},{7,5},{8,10},{9,11},{10,... | collective-permute-start | bytes 786440 | tf_op jit(solution)/shard_map/ppermute | solution.py:422
  3.6 1.3 %shard_map.84 = (bf16[3,256,128]{2,1,0:T(8,128)(2,1)S(1)}, bf16[3,256,128]{2,1,0:T(8,128)(2,1)S(1)}, bf16[3,256,128]{2,1,0:T(8,128)(2,1)S(1)}, bf16[3,256,128]{2,1,0:T(8,128)(2,1)S(1)}) custom-call(bf16[256,512]{1,0:T(8,128)(2,1)} %q.1, bf16[256,512]{1,0:T(8,128)(2,1)} %k.1, bf16[256,512]{1,0:T(8,128)(2,1)} %v.1), custom_call_target="tpu_custom_call" | custom-call | tf_op jit(solution)/shard_map/pallas_call | solution.py:39
  4.9 2.6 %collective-permute-start = (bf16[3,256,128]{2,1,0:T(8,128)(2,1)S(1)}, bf16[3,256,128]{2,1,0:T(8,128)(2,1)S(1)}, u32[]{:S(2)}, u32[]{:S(2)}) collective-permute-start(bf16[3,256,128]{2,1,0:T(8,128)(2,1)S(1)} %get-tuple-element.56.refs_1_), channel_id=1, source_target_pairs={{0,12},{4,8},{8,4},{12,0},{16,28},{20,24},{24,20},{28,16},{1,13},{... | collective-permute-start | bytes 589832 | tf_op jit(solution)/shard_map/ppermute | solution.py:422
  8.5 1.4 %shard_map.87 = bf16[4,2,64,128]{3,2,1,0:T(8,128)(2,1)S(1)} custom-call(bf16[3,256,128]{2,1,0:T(8,128)(2,1)S(1)} %get-tuple-element.55.refs_0_, bf16[3,256,128]{2,1,0:T(8,128)(2,1)S(1)} %get-tuple-element.56.refs_1_, bf16[3,256,128]{2,1,0:T(8,128)(2,1)S(1)} %get-tuple-element.57.refs_2_, bf16[3,256,128]{2,1,0:T(8,128)(2,1)S(1)} %get-tuple-element.58.refs_3_), custom_call_target="tpu_custom_call" | custom-call | tf_op jit(solution)/shard_map/pallas_call | solution.py:39
  9.9 2.6 %collective-permute-start.6 = (bf16[4,2,64,128]{3,2,1,0:T(8,128)(2,1)S(1)}, bf16[4,2,64,128]{3,2,1,0:T(8,128)(2,1)S(1)}, u32[]{:S(2)}, u32[]{:S(2)}) collective-permute-start(bf16[4,2,64,128]{3,2,1,0:T(8,128)(2,1)S(1)} %shard_map.87), channel_id=1, source_target_pairs={{0,16},{4,20},{8,24},{12,28},{16,0},{20,4},{24,8},{28,12},{1,17},{... | collective-permute-start | bytes 393224 | tf_op jit(solution)/shard_map/ppermute | solution.py:422
  12.5 1.6 %copy-done = bf16[512,2048]{1,0:T(8,128)(2,1)S(1)} copy-done((bf16[512,2048]{1,0:T(8,128)(2,1)S(1)}, bf16[512,2048]{1,0:T(8,128)(2,1)}, u32[]{:S(2)}) %copy-start) | copy-done | bytes 2097176
  15.8 3.6 %collective-permute-done.1.refs_2_ = bf16[3,256,128]{2,1,0:T(8,128)(2,1)S(1)} collective-permute-done((bf16[3,256,128]{2,1,0:T(8,128)(2,1)S(1)}, bf16[3,256,128]{2,1,0:T(8,128)(2,1)S(1)}, u32[]{:S(2)}, u32[]{:S(2)}) %collective-permute-start.1) | collective-permute-done | bytes 196640 | tf_op jit(solution)/shard_map/ppermute | solution.py:422
  19.8 1.7 %collective-permute-start.7 = (bf16[2,256,128]{2,1,0:T(8,128)(2,1)S(1)}, bf16[2,256,128]{2,1,0:T(8,128)(2,1)S(1)}, u32[]{:S(2)}, u32[]{:S(2)}) collective-permute-start(bf16[2,256,128]{2,1,0:T(8,128)(2,1)S(1)} %get-tuple-element.71), channel_id=1, source_target_pairs={{0,16},{4,20},{8,24},{12,28},{16,0},{20,4},{24,8},{28,12},{1,17},{... | collective-permute-start | bytes 393224 | tf_op jit(solution)/shard_map/ppermute | solution.py:422
  22.4 2.3 %collective-permute-start.8 = (bf16[384,128]{1,0:T(8,128)(2,1)S(1)}, bf16[384,128]{1,0:T(8,128)(2,1)S(1)}, u32[]{:S(2)}, u32[]{:S(2)}) collective-permute-start(bf16[384,128]{1,0:T(8,128)(2,1)S(1)} %get-tuple-element.72), channel_id=1, source_target_pairs={{0,12},{4,8},{8,4},{12,0},{16,28},{20,24},{24,20},{28,16},{1,13},{... | collective-permute-start | bytes 294920 | tf_op jit(solution)/shard_map/ppermute | solution.py:422
  25.0 1.4 %collective-permute-start.10 = (bf16[384,128]{1,0:T(8,128)(2,1)S(1)}, bf16[384,128]{1,0:T(8,128)(2,1)S(1)}, u32[]{:S(2)}, u32[]{:S(2)}) collective-permute-start(bf16[384,128]{1,0:T(8,128)(2,1)S(1)} %get-tuple-element.74), channel_id=1, source_target_pairs={{0,4},{4,0},{8,12},{12,8},{16,20},{20,16},{24,28},{28,24},{1,5},{5... | collective-permute-start | bytes 294920 | tf_op jit(solution)/shard_map/ppermute | solution.py:422
  26.4 1.7 %shard_map.89 = (bf16[3,4,256,128]{3,2,1,0:T(8,128)(2,1)S(1)}, bf16[128,1024]{1,0:T(8,128)(2,1)S(1)}, bf16[128,1024]{1,0:T(8,128)(2,1)S(1)}, bf16[128,512]{1,0:T...) custom-call(bf16[4,2,256,128]{3,2,1,0:T(8,128)(2,1)S(1)} %get-tuple-element.59, ...), custom_call_target="tpu_custom_call" | custom-call | flops 335544320 | bytes 6946816 | tf_op jit(solution)/shard_map/pallas_call | solution.py:39
  28.0 1.3 %collective-permute-done.8.refs_7_ = bf16[384,128]{1,0:T(8,128)(2,1)S(1)} collective-permute-done((bf16[384,128]{1,0:T(8,128)(2,1)S(1)}, bf16[384,128]{1,0:T(8,128)(2,1)S(1)}, u32[]{:S(2)}, u32[]{:S(2)}) %collective-permute-start.8) | collective-permute-done | bytes 98336 | tf_op jit(solution)/shard_map/ppermute | solution.py:422
  30.1 2.2 %shard_map.90 = (bf16[4,4,256,256]{3,2,1,0:T(8,128)(2,1)S(1)}, bf16[4,256,128]{2,1,0:T(8,128)(2,1)S(1)}, bf16[2,256,128]{2,1,0:T(8,128)(2,1)S(1)}, f32[8,1024]{1...) custom-call(bf16[3,4,256,128]{3,2,1,0:T(8,128)(2,1)S(1)} %get-tuple-, ...), custom_call_target="tpu_custom_call" | custom-call | flops 335544320 | bytes 9601024 | tf_op jit(solution)/shard_map/pallas_call | solution.py:39
  32.3 1.0 %collective-permute-start.20 = (bf16[896,128]{1,0:T(8,128)(2,1)S(1)}, bf16[896,128]{1,0:T(8,128)(2,1)S(1)}, u32[]{:S(2)}, u32[]{:S(2)}) collective-permute-start(bf16[896,128]{1,0:T(8,128)(2,1)S(1)} %get-tuple-element.97), channel_id=1, source_target_pairs={{0,16},{4,20},{8,24},{12,28},{16,0},{20,4},{24,8},{28,12},{1,17},{... | collective-permute-start | bytes 688136 | tf_op jit(solution)/shard_map/ppermute | solution.py:422
  33.3 2.8 %collective-permute-start.11 = (bf16[256,128]{1,0:T(8,128)(2,1)S(1)}, bf16[256,128]{1,0:T(8,128)(2,1)S(1)}, u32[]{:S(2)}, u32[]{:S(2)}) collective-permute-start(bf16[256,128]{1,0:T(8,128)(2,1)S(1)} %get-tuple-element.76), channel_id=1, source_target_pairs={{0,12},{4,8},{8,4},{12,0},{16,28},{20,24},{24,20},{28,16},{1,13},{... | collective-permute-start | bytes 196616 | tf_op jit(solution)/shard_map/ppermute | solution.py:422
  36.1 1.2 %collective-permute-start.13 = (bf16[256,128]{1,0:T(8,128)(2,1)S(1)}, bf16[256,128]{1,0:T(8,128)(2,1)S(1)}, u32[]{:S(2)}, u32[]{:S(2)}) collective-permute-start(bf16[256,128]{1,0:T(8,128)(2,1)S(1)} %get-tuple-element.78), channel_id=1, source_target_pairs={{0,4},{4,0},{8,12},{12,8},{16,20},{20,16},{24,28},{28,24},{1,5},{5... | collective-permute-start | bytes 196616 | tf_op jit(solution)/shard_map/ppermute | solution.py:422
  37.3 3.4 %shard_map.91 = (bf16[4,256,128]{2,1,0:T(8,128)(2,1)S(1)}, f32[2,4,256,128]{3,2,1,0:T(8,128)S(1)}) custom-call(bf16[3,4,256,128]{3,2,1,0:T(8,128)(2,1)S(1)} %get-tuple-element.66.refs_0_, bf16[4,2,256,128]{3,2,1,0:T(8,128)(2,1)S(1)} %get-tuple-element.59.near.refs_1_, bf16[2,512,128]{2,1,0:T(8,128)(2,1)S(1)} %get-tuple-element.61.level_1.refs_2_, ...), custom_call_target="tpu_custom_call" | custom-call | tf_op jit(solution)/shard_map/pallas_call | solution.py:39
  42.9 1.8 %collective-permute-done.20.refs_0_ = bf16[896,128]{1,0:T(8,128)(2,1)S(1)} collective-permute-done((bf16[896,128]{1,0:T(8,128)(2,1)S(1)}, bf16[896,128]{1,0:T(8,128)(2,1)S(1)}, u32[]{:S(2)}, u32[]{:S(2)}) %collective-permute-start.20) | collective-permute-done | bytes 229408 | tf_op jit(solution)/shard_map/ppermute | solution.py:422
  46.0 1.1 %collective-permute-start.22 = (bf16[3,256,128]{2,1,0:T(8,128)(2,1)S(1)}, bf16[3,256,128]{2,1,0:T(8,128)(2,1)S(1)}, u32[]{:S(2)}, u32[]{:S(2)}) collective-permute-start(bf16[3,256,128]{2,1,0:T(8,128)(2,1)S(1)} %get-tuple-element.100), channel_id=1, source_target_pairs={{0,8},{4,12},{8,0},{12,4},{16,24},{20,28},{24,16},{28,20},{1,9},{5... | collective-permute-start | bytes 589832 | tf_op jit(solution)/shard_map/ppermute | solution.py:422
  47.2 1.4 %collective-permute-start.23 = (bf16[3,256,128]{2,1,0:T(8,128)(2,1)S(1)}, bf16[3,256,128]{2,1,0:T(8,128)(2,1)S(1)}, u32[]{:S(2)}, u32[]{:S(2)}) collective-permute-start(bf16[3,256,128]{2,1,0:T(8,128)(2,1)S(1)} %get-tuple-element.101), channel_id=1, source_target_pairs={{0,4},{4,0},{8,12},{12,8},{16,20},{20,16},{24,28},{28,24},{1,5},{5... | collective-permute-start | bytes 589832 | tf_op jit(solution)/shard_map/ppermute | solution.py:422
  49.3 1.5 %collective-permute-start.19 = (bf16[32,2048]{1,0:T(8,128)(2,1)S(1)}, bf16[32,2048]{1,0:T(8,128)(2,1)S(1)}, u32[]{:S(2)}, u32[]{:S(2)}) collective-permute-start(bf16[32,2048]{1,0:T(8,128)(2,1)S(1)} %get-tuple-element.95), channel_id=1, source_target_pairs={{0,2},{1,3},{2,0},{3,1},{4,6},{5,7},{6,4},{7,5},{8,10},{9,11},{10,... | collective-permute-start | bytes 393224 | tf_op jit(solution)/shard_map/ppermute | solution.py:422
  50.8 3.4 %collective-permute-done.18.refs_1_ = bf16[32,2048]{1,0:T(8,128)(2,1)S(1)} collective-permute-done((bf16[32,2048]{1,0:T(8,128)(2,1)S(1)}, bf16[32,2048]{1,0:T(8,128)(2,1)S(1)}, u32[]{:S(2)}, u32[]{:S(2)}) %collective-permute-start.18) | collective-permute-done | bytes 131104 | tf_op jit(solution)/shard_map/ppermute | solution.py:422
  54.1 1.4 %collective-permute-done.19.refs_2_ = bf16[32,2048]{1,0:T(8,128)(2,1)S(1)} collective-permute-done((bf16[32,2048]{1,0:T(8,128)(2,1)S(1)}, bf16[32,2048]{1,0:T(8,128)(2,1)S(1)}, u32[]{:S(2)}, u32[]{:S(2)}) %collective-permute-start.19) | collective-permute-done | bytes 131104 | tf_op jit(solution)/shard_map/ppermute | solution.py:422
  56.4 1.1 %shard_map.95 = (bf16[256,512]{1,0:T(8,128)(2,1)}, bf16[256,512]{1,0:T(8,128)(2,1)}, bf16[256,512]{1,0:T(8,128)(2,1)}, bf16[64,2048]{1,0:T(8,128)(2,1)}) custom-call(f32[64,2048]{1,0:T(8,128)S(1)} %get-tuple-element.93.refs_0_, bf16[32,2048]{1,0:T(8,128)(2,1)S(1)} %collective-permute-done.18.refs_1_, bf16[32,2048]{1,0:T(8,128)(2,1)S(1)} %collective-permute-done.19.refs_2_, ...), custom_call_target="tpu_custom_call" | custom-call | tf_op jit(solution)/shard_map/pallas_call | solution.py:39
  (40 shorter events, 10.0 us)
Async XLA Ops:
  0.6 11.9 %collective-permute-start.3 = (bf16[64,2048]{1,0:T(8,128)(2,1)}, bf16[64,2048]{1,0:T(8,128)(2,1)S(1)}, u32[]{:S(2)}, u32[]{:S(2)}) collective-permute-start(bf16[64,2048]{1,0:T(8,128)(2,1)} %refs_0_.1), channel_id=1, source_target_pairs={{0,2},{1,3},{2,0},{3,1},{4,6},{5,7},{6,4},{7,5},{8,10},{9,11},{10,... | collective-permute-start | bytes 786440 | tf_op jit(solution)/shard_map/ppermute | solution.py:422
  4.9 10.4 %collective-permute-start = (bf16[3,256,128]{2,1,0:T(8,128)(2,1)S(1)}, bf16[3,256,128]{2,1,0:T(8,128)(2,1)S(1)}, u32[]{:S(2)}, u32[]{:S(2)}) collective-permute-start(bf16[3,256,128]{2,1,0:T(8,128)(2,1)S(1)} %get-tuple-element.56.refs_1_), channel_id=1, source_target_pairs={{0,12},{4,8},{8,4},{12,0},{16,28},{20,24},{24,20},{28,16},{1,13},{... | collective-permute-start | bytes 589832 | tf_op jit(solution)/shard_map/ppermute | solution.py:422
  7.5 11.8 %collective-permute-start.1 = (bf16[3,256,128]{2,1,0:T(8,128)(2,1)S(1)}, bf16[3,256,128]{2,1,0:T(8,128)(2,1)S(1)}, u32[]{:S(2)}, u32[]{:S(2)}) collective-permute-start(bf16[3,256,128]{2,1,0:T(8,128)(2,1)S(1)} %get-tuple-element.57.refs_2_), channel_id=1, source_target_pairs={{0,8},{4,12},{8,0},{12,4},{16,24},{20,28},{24,16},{28,20},{1,9},{5... | collective-permute-start | bytes 589832 | tf_op jit(solution)/shard_map/ppermute | solution.py:422
  8.0 11.4 %collective-permute-start.2 = (bf16[3,256,128]{2,1,0:T(8,128)(2,1)S(1)}, bf16[3,256,128]{2,1,0:T(8,128)(2,1)S(1)}, u32[]{:S(2)}, u32[]{:S(2)}) collective-permute-start(bf16[3,256,128]{2,1,0:T(8,128)(2,1)S(1)} %get-tuple-element.58.refs_3_), channel_id=1, source_target_pairs={{0,4},{4,0},{8,12},{12,8},{16,20},{20,16},{24,28},{28,24},{1,5},{5... | collective-permute-start | bytes 589832 | tf_op jit(solution)/shard_map/ppermute | solution.py:422
  9.9 11.6 %collective-permute-start.6 = (bf16[4,2,64,128]{3,2,1,0:T(8,128)(2,1)S(1)}, bf16[4,2,64,128]{3,2,1,0:T(8,128)(2,1)S(1)}, u32[]{:S(2)}, u32[]{:S(2)}) collective-permute-start(bf16[4,2,64,128]{3,2,1,0:T(8,128)(2,1)S(1)} %shard_map.87), channel_id=1, source_target_pairs={{0,16},{4,20},{8,24},{12,28},{16,0},{20,4},{24,8},{28,12},{1,17},{... | collective-permute-start | bytes 393224 | tf_op jit(solution)/shard_map/ppermute | solution.py:422
  15.2 6.3 %collective-permute-start.4 = (bf16[64,2048]{1,0:T(8,128)(2,1)S(1)}, bf16[64,2048]{1,0:T(8,128)(2,1)S(1)}, u32[]{:S(2)}, u32[]{:S(2)}) collective-permute-start(bf16[64,2048]{1,0:T(8,128)(2,1)S(1)} %get-tuple-element.62.refs_0_), channel_id=1, source_target_pairs={{0,1},{1,0},{2,3},{3,2},{4,5},{5,4},{6,7},{7,6},{8,9},{9,8},{10,11... | collective-permute-start | bytes 786440 | tf_op jit(solution)/shard_map/ppermute | solution.py:422
  15.3 6.2 %collective-permute-start.5 = (bf16[64,2048]{1,0:T(8,128)(2,1)S(1)}, bf16[64,2048]{1,0:T(8,128)(2,1)S(1)}, u32[]{:S(2)}, u32[]{:S(2)}) collective-permute-start(bf16[64,2048]{1,0:T(8,128)(2,1)S(1)} %get-tuple-element.63.refs_2_), channel_id=1, source_target_pairs={{0,1},{1,0},{2,3},{3,2},{4,5},{5,4},{6,7},{7,6},{8,9},{9,8},{10,11... | collective-permute-start | bytes 786440 | tf_op jit(solution)/shard_map/ppermute | solution.py:422
  19.8 8.3 %collective-permute-start.7 = (bf16[2,256,128]{2,1,0:T(8,128)(2,1)S(1)}, bf16[2,256,128]{2,1,0:T(8,128)(2,1)S(1)}, u32[]{:S(2)}, u32[]{:S(2)}) collective-permute-start(bf16[2,256,128]{2,1,0:T(8,128)(2,1)S(1)} %get-tuple-element.71), channel_id=1, source_target_pairs={{0,16},{4,20},{8,24},{12,28},{16,0},{20,4},{24,8},{28,12},{1,17},{... | collective-permute-start | bytes 393224 | tf_op jit(solution)/shard_map/ppermute | solution.py:422
  22.4 7.0 %collective-permute-start.8 = (bf16[384,128]{1,0:T(8,128)(2,1)S(1)}, bf16[384,128]{1,0:T(8,128)(2,1)S(1)}, u32[]{:S(2)}, u32[]{:S(2)}) collective-permute-start(bf16[384,128]{1,0:T(8,128)(2,1)S(1)} %get-tuple-element.72), channel_id=1, source_target_pairs={{0,12},{4,8},{8,4},{12,0},{16,28},{20,24},{24,20},{28,16},{1,13},{... | collective-permute-start | bytes 294920 | tf_op jit(solution)/shard_map/ppermute | solution.py:422
  24.7 5.4 %collective-permute-start.9 = (bf16[384,128]{1,0:T(8,128)(2,1)S(1)}, bf16[384,128]{1,0:T(8,128)(2,1)S(1)}, u32[]{:S(2)}, u32[]{:S(2)}) collective-permute-start(bf16[384,128]{1,0:T(8,128)(2,1)S(1)} %get-tuple-element.73), channel_id=1, source_target_pairs={{0,8},{4,12},{8,0},{12,4},{16,24},{20,28},{24,16},{28,20},{1,9},{5... | collective-permute-start | bytes 294920 | tf_op jit(solution)/shard_map/ppermute | solution.py:422
  25.0 5.1 %collective-permute-start.10 = (bf16[384,128]{1,0:T(8,128)(2,1)S(1)}, bf16[384,128]{1,0:T(8,128)(2,1)S(1)}, u32[]{:S(2)}, u32[]{:S(2)}) collective-permute-start(bf16[384,128]{1,0:T(8,128)(2,1)S(1)} %get-tuple-element.74), channel_id=1, source_target_pairs={{0,4},{4,0},{8,12},{12,8},{16,20},{20,16},{24,28},{28,24},{1,5},{5... | collective-permute-start | bytes 294920 | tf_op jit(solution)/shard_map/ppermute | solution.py:422
  32.3 12.4 %collective-permute-start.20 = (bf16[896,128]{1,0:T(8,128)(2,1)S(1)}, bf16[896,128]{1,0:T(8,128)(2,1)S(1)}, u32[]{:S(2)}, u32[]{:S(2)}) collective-permute-start(bf16[896,128]{1,0:T(8,128)(2,1)S(1)} %get-tuple-element.97), channel_id=1, source_target_pairs={{0,16},{4,20},{8,24},{12,28},{16,0},{20,4},{24,8},{28,12},{1,17},{... | collective-permute-start | bytes 688136 | tf_op jit(solution)/shard_map/ppermute | solution.py:422
  33.3 7.3 %collective-permute-start.11 = (bf16[256,128]{1,0:T(8,128)(2,1)S(1)}, bf16[256,128]{1,0:T(8,128)(2,1)S(1)}, u32[]{:S(2)}, u32[]{:S(2)}) collective-permute-start(bf16[256,128]{1,0:T(8,128)(2,1)S(1)} %get-tuple-element.76), channel_id=1, source_target_pairs={{0,12},{4,8},{8,4},{12,0},{16,28},{20,24},{24,20},{28,16},{1,13},{... | collective-permute-start | bytes 196616 | tf_op jit(solution)/shard_map/ppermute | solution.py:422
  36.1 4.9 %collective-permute-start.12 = (bf16[256,128]{1,0:T(8,128)(2,1)S(1)}, bf16[256,128]{1,0:T(8,128)(2,1)S(1)}, u32[]{:S(2)}, u32[]{:S(2)}) collective-permute-start(bf16[256,128]{1,0:T(8,128)(2,1)S(1)} %get-tuple-element.77), channel_id=1, source_target_pairs={{0,8},{4,12},{8,0},{12,4},{16,24},{20,28},{24,16},{28,20},{1,9},{5... | collective-permute-start | bytes 196616 | tf_op jit(solution)/shard_map/ppermute | solution.py:422
  36.1 4.9 %collective-permute-start.13 = (bf16[256,128]{1,0:T(8,128)(2,1)S(1)}, bf16[256,128]{1,0:T(8,128)(2,1)S(1)}, u32[]{:S(2)}, u32[]{:S(2)}) collective-permute-start(bf16[256,128]{1,0:T(8,128)(2,1)S(1)} %get-tuple-element.78), channel_id=1, source_target_pairs={{0,4},{4,0},{8,12},{12,8},{16,20},{20,16},{24,28},{28,24},{1,5},{5... | collective-permute-start | bytes 196616 | tf_op jit(solution)/shard_map/ppermute | solution.py:422
  41.8 4.2 %collective-permute-start.14 = (bf16[32,2048]{1,0:T(8,128)(2,1)S(1)}, bf16[32,2048]{1,0:T(8,128)(2,1)S(1)}, u32[]{:S(2)}, u32[]{:S(2)}) collective-permute-start(bf16[32,2048]{1,0:T(8,128)(2,1)S(1)} %get-tuple-element.89), channel_id=1, source_target_pairs={{0,1},{1,0},{2,3},{3,2},{4,5},{5,4},{6,7},{7,6},{8,9},{9,8},{10,11... | collective-permute-start | bytes 393224 | tf_op jit(solution)/shard_map/ppermute | solution.py:422
  41.9 5.3 %collective-permute-start.15 = (bf16[32,2048]{1,0:T(8,128)(2,1)S(1)}, bf16[32,2048]{1,0:T(8,128)(2,1)S(1)}, u32[]{:S(2)}, u32[]{:S(2)}) collective-permute-start(bf16[32,2048]{1,0:T(8,128)(2,1)S(1)} %get-tuple-element.90), channel_id=1, source_target_pairs={{0,1},{1,0},{2,3},{3,2},{4,5},{5,4},{6,7},{7,6},{8,9},{9,8},{10,11... | collective-permute-start | bytes 393224 | tf_op jit(solution)/shard_map/ppermute | solution.py:422
  42.4 6.2 %collective-permute-start.16 = (bf16[32,2048]{1,0:T(8,128)(2,1)S(1)}, bf16[32,2048]{1,0:T(8,128)(2,1)S(1)}, u32[]{:S(2)}, u32[]{:S(2)}) collective-permute-start(bf16[32,2048]{1,0:T(8,128)(2,1)S(1)} %get-tuple-element.91), channel_id=1, source_target_pairs={{0,1},{1,0},{2,3},{3,2},{4,5},{5,4},{6,7},{7,6},{8,9},{9,8},{10,11... | collective-permute-start | bytes 393224 | tf_op jit(solution)/shard_map/ppermute | solution.py:422
  42.4 6.1 %collective-permute-start.17 = (bf16[32,2048]{1,0:T(8,128)(2,1)S(1)}, bf16[32,2048]{1,0:T(8,128)(2,1)S(1)}, u32[]{:S(2)}, u32[]{:S(2)}) collective-permute-start(bf16[32,2048]{1,0:T(8,128)(2,1)S(1)} %get-tuple-element.92), channel_id=1, source_target_pairs={{0,1},{1,0},{2,3},{3,2},{4,5},{5,4},{6,7},{7,6},{8,9},{9,8},{10,11... | collective-permute-start | bytes 393224 | tf_op jit(solution)/shard_map/ppermute | solution.py:422
  45.0 10.5 %collective-permute-start.21 = (bf16[3,256,128]{2,1,0:T(8,128)(2,1)S(1)}, bf16[3,256,128]{2,1,0:T(8,128)(2,1)S(1)}, u32[]{:S(2)}, u32[]{:S(2)}) collective-permute-start(bf16[3,256,128]{2,1,0:T(8,128)(2,1)S(1)} %get-tuple-element.99), channel_id=1, source_target_pairs={{0,12},{4,8},{8,4},{12,0},{16,28},{20,24},{24,20},{28,16},{1,13},{... | collective-permute-start | bytes 589832 | tf_op jit(solution)/shard_map/ppermute | solution.py:422
  46.0 10.0 %collective-permute-start.22 = (bf16[3,256,128]{2,1,0:T(8,128)(2,1)S(1)}, bf16[3,256,128]{2,1,0:T(8,128)(2,1)S(1)}, u32[]{:S(2)}, u32[]{:S(2)}) collective-permute-start(bf16[3,256,128]{2,1,0:T(8,128)(2,1)S(1)} %get-tuple-element.100), channel_id=1, source_target_pairs={{0,8},{4,12},{8,0},{12,4},{16,24},{20,28},{24,16},{28,20},{1,9},{5... | collective-permute-start | bytes 589832 | tf_op jit(solution)/shard_map/ppermute | solution.py:422
  47.2 9.2 %collective-permute-start.23 = (bf16[3,256,128]{2,1,0:T(8,128)(2,1)S(1)}, bf16[3,256,128]{2,1,0:T(8,128)(2,1)S(1)}, u32[]{:S(2)}, u32[]{:S(2)}) collective-permute-start(bf16[3,256,128]{2,1,0:T(8,128)(2,1)S(1)} %get-tuple-element.101), channel_id=1, source_target_pairs={{0,4},{4,0},{8,12},{12,8},{16,20},{20,16},{24,28},{28,24},{1,5},{5... | collective-permute-start | bytes 589832 | tf_op jit(solution)/shard_map/ppermute | solution.py:422
  48.7 5.4 %collective-permute-start.18 = (bf16[32,2048]{1,0:T(8,128)(2,1)S(1)}, bf16[32,2048]{1,0:T(8,128)(2,1)S(1)}, u32[]{:S(2)}, u32[]{:S(2)}) collective-permute-start(bf16[32,2048]{1,0:T(8,128)(2,1)S(1)} %get-tuple-element.94), channel_id=1, source_target_pairs={{0,2},{1,3},{2,0},{3,1},{4,6},{5,7},{6,4},{7,5},{8,10},{9,11},{10,... | collective-permute-start | bytes 393224 | tf_op jit(solution)/shard_map/ppermute | solution.py:422
  49.3 6.3 %collective-permute-start.19 = (bf16[32,2048]{1,0:T(8,128)(2,1)S(1)}, bf16[32,2048]{1,0:T(8,128)(2,1)S(1)}, u32[]{:S(2)}, u32[]{:S(2)}) collective-permute-start(bf16[32,2048]{1,0:T(8,128)(2,1)S(1)} %get-tuple-element.95), channel_id=1, source_target_pairs={{0,2},{1,3},{2,0},{3,1},{4,6},{5,7},{6,4},{7,5},{8,10},{9,11},{10,... | collective-permute-start | bytes 393224 | tf_op jit(solution)/shard_map/ppermute | solution.py:422
  (2 other events, 2.5 us)

commit v17 on v16

--- a/solution.py
+++ b/solution.py
@@ -133,8 +133,8 @@
         out[...] = x[...]
 
 
-def gather_kernel(nb, groups, *refs):
-    chunks, (near, queries, level_1, *rims) = refs[:GROUP], refs[GROUP:]
+def gather_kernel(nb, *refs):
+    chunks, (near, queries, level_1) = refs[:GROUP], refs[GROUP:]
     me = member()
     for step, chunk in zip(STEPS, chunks):
         near[me ^ step] = chunk[:2]
@@ -144,12 +144,20 @@
     for part in range(2):
         for b in range(nb):
             level_1[part, b * half : (b + 1) * half] = dot(pool, near[b, part]).astype(BF16)
+
+
+def rim_kernel(groups, *refs):
+    chunks, outs = refs[:GROUP], refs[GROUP:]
+    me = member()
+    members = [GROUP - 1, 0]
     if groups == 2:
-        upper = lax.axis_index("seq") >= GROUP
-        rims[0][...] = jnp.where(upper, near[0], near[nb - 1])
-    else:
-        rims[0][...] = near[nb - 1]
-        rims[1][...] = near[0]
+        members = [jnp.where(lax.axis_index("seq") >= GROUP, 0, GROUP - 1)]
+    for wanted, out in zip(members, outs):
+        for step, chunk in zip(STEPS, chunks):
+
+            @pl.when(me ^ step == wanted)
+            def _():
+                out[...] = chunk[:2]
 
 
 def from_beside(groups, refs):
@@ -166,6 +174,12 @@
 
 def odd_group():
     return lax.rem(lax.axis_index("seq") // GROUP, 2)
+
+
+def near_window(b, nb):
+    sides = near_sides(b, nb)
+    low, high = sides[0], sides[-1] + 1
+    return slice(low, high), slice((b + low - 1) * BLOCK, (b + high - 1) * BLOCK)
 
 
 def near_sides(b, nb):
@@ -257,9 +271,10 @@
         shrink = row[3:4, at_block(b)]
         prob[b, 3] = (weights[b, 3] * shrink).astype(BF16)
         context = context_t[:, at_block(b)] + dot(v1_t[:, at_block(sibling(b))], prob[b, 3])
-        for side in near_sides(b, nb):
-            prob[b, side] = (weights[b, side] * shrink).astype(BF16)
-            context = context + dot(v_t[:, at_block(b + side - 1)], prob[b, side])
+        sides, keys = near_window(b, nb)
+        parts = (weights[b, sides] * shrink).astype(BF16)
+        prob[b, sides] = parts
+        context = context + dot(v_t[:, keys], parts.reshape(-1, BLOCK))
         attended[b] = context.T.astype(BF16)
         deltas[:1, at_block(b)] = (grads[b].T.astype(F32) * context).sum(0, keepdims=True)
     grad = grads[...].reshape(tokens, HEAD_DIM)
@@ -306,12 +321,12 @@
         query_t[:, span(b, BLOCK)] += dot(block[0].T, rim_shift[i])
     for b in range(nb):
         grad, delta = grads[b], deltas[:1, at_block(b)]
-        grad_t = query_t[:, at_block(b)]
-        for side in near_sides(b, nb):
-            slope = dot_nt(near[b + side - 1, 1], grad)
-            part = (prob[b, side].astype(F32) * (slope - delta)).astype(BF16)
-            shift[b, side] = part
-            grad_t = grad_t + dot(k_t[:, at_block(b + side - 1)], part)
+        sides, keys = near_window(b, nb)
+        blocks = slice(keys.start // BLOCK, keys.stop // BLOCK)
+        slope = dot_nt(near[blocks, 1].reshape(-1, HEAD_DIM), grad)
+        parts = (prob[b, sides].reshape(-1, BLOCK).astype(F32) * (slope - delta)).astype(BF16)
+        shift[b, sides] = parts.reshape(-1, BLOCK, BLOCK)
+        grad_t = query_t[:, at_block(b)] + dot(k_t[:, keys], parts)
         slope = dot_nt(level_1[1, at_block(sibling(b))], grad)
         part = (prob[b, 3].astype(F32) * (slope - delta)).astype(BF16)
         shift[b, 3] = part
@@ -481,18 +496,16 @@
     tops = swapped(tops, "seq", GROUP)
     arrays = (out_grad, far, out_weight)
     own_grad, far, out_weight = call(copy_kernel, [shape(*x.shape) for x in arrays], arrays)
-    near, queries, level_1, *refs = call(
-        functools.partial(gather_kernel, nb, groups),
+    rim_blocks = beside(call(functools.partial(rim_kernel, groups), rims, chunks, flops=20 * score_flops))
+    near, queries, level_1 = call(
+        functools.partial(gather_kernel, nb),
         [
             shape(nb, 2, rows, HEAD_DIM),
             shape(nb, rows, HEAD_DIM),
             shape(2, tokens // 2, HEAD_DIM),
-        ]
-        + rims,
+        ],
         chunks,
-        flops=20 * score_flops,
-    )
-    rim_blocks = beside(refs)
+    )
     grad_chunks = call(
         grad_kernel,
         [shape(rows + 2 * quarter, HEAD_DIM)] * GROUP,

time: 57.8 us -> 57.1 us (0.988)
  waiting for transfers between devices: 13.4 us -> 12 us
  Pallas kernels: 13.7 us -> 14.3 us
    ppermute x24, waiting for transfers between devices: 13.4 us -> 12 us  [swapped(): lax.ppermute(x, axis, [(i, i ^ step) for i in range(lax.axis_size(axis))])]
    pallas_call x12 -> x13, Pallas kernels: 13.7 us -> 14.3 us  [call(): pl.pallas_call(kernel, out_shape=out_shape, in_specs=[kept if copied else...]
  transfers between devices with their start and end apart: 24 -> 24, of which waited for: 9 -> 7; matrix products, arithmetic and copies ran while one was open for 0% -> 0% of each run, Pallas kernels for 18% -> 19%
where the time goes in v17:
time: 57.1 us; the launch traced here: 56.8 us
  starting transfers between devices  27.2 us (48%)
  Pallas kernels  14.3 us (25%)
  waiting for transfers between devices  12 us (21%)
  local copies, waits for them, and re-layouts  2.54 us (4%)
  between operations  0.78 us (1%)
    ppermute x24, starting transfers between devices, swapped(): lax.ppermute(x, axis, [(i, i ^ step) for i in range(lax.axis_size(axis))])  27.2 us
    pallas_call x13, Pallas kernels, call(): pl.pallas_call(kernel, out_shape=out_shape, in_specs=[kept if copied else...  14.3 us
    ppermute x24, waiting for transfers between devices, swapped(): lax.ppermute(x, axis, [(i, i ^ step) for i in range(lax.axis_size(axis))])  12 us
    unnamed x4, local copies, waits for them, and re-layouts  2.54 us
  transfers between devices with their start and end apart: 24, of which 7 were waited for; matrix products, arithmetic and copies ran while one was open for 0% of the time, Pallas kernels for 19%

profile of v17, /device:TPU:0, one launch (start us, length us, event | category | flops | bytes accessed | tf_op | source)
XLA Modules:
  0.0 56.8 jit_solution(1603457069712260752)
XLA Ops:
  0.6 3.0 %collective-permute-start.3 = (bf16[64,2048]{1,0:T(8,128)(2,1)}, bf16[64,2048]{1,0:T(8,128)(2,1)S(1)}, u32[]{:S(2)}, u32[]{:S(2)}) collective-permute-start(bf16[64,2048]{1,0:T(8,128)(2,1)} %refs_0_.1), channel_id=1, source_target_pairs={{0,2},{1,3},{2,0},{3,1},{4,6},{5,7},{6,4},{7,5},{8,10},{9,11},{10,... | collective-permute-start | bytes 786440 | tf_op jit(solution)/shard_map/ppermute | solution.py:437
  3.6 1.3 %shard_map.84 = (bf16[3,256,128]{2,1,0:T(8,128)(2,1)S(1)}, bf16[3,256,128]{2,1,0:T(8,128)(2,1)S(1)}, bf16[3,256,128]{2,1,0:T(8,128)(2,1)S(1)}, bf16[3,256,128]{2,1,0:T(8,128)(2,1)S(1)}) custom-call(bf16[256,512]{1,0:T(8,128)(2,1)} %q.1, bf16[256,512]{1,0:T(8,128)(2,1)} %k.1, bf16[256,512]{1,0:T(8,128)(2,1)} %v.1), custom_call_target="tpu_custom_call" | custom-call | tf_op jit(solution)/shard_map/pallas_call | solution.py:39
  4.9 2.6 %collective-permute-start = (bf16[3,256,128]{2,1,0:T(8,128)(2,1)S(1)}, bf16[3,256,128]{2,1,0:T(8,128)(2,1)S(1)}, u32[]{:S(2)}, u32[]{:S(2)}) collective-permute-start(bf16[3,256,128]{2,1,0:T(8,128)(2,1)S(1)} %get-tuple-element.55.refs_1_), channel_id=1, source_target_pairs={{0,12},{4,8},{8,4},{12,0},{16,28},{20,24},{24,20},{28,16},{1,13},{... | collective-permute-start | bytes 589832 | tf_op jit(solution)/shard_map/ppermute | solution.py:437
  8.5 1.4 %shard_map.87 = bf16[4,2,64,128]{3,2,1,0:T(8,128)(2,1)S(1)} custom-call(bf16[3,256,128]{2,1,0:T(8,128)(2,1)S(1)} %get-tuple-element.54.refs_0_, bf16[3,256,128]{2,1,0:T(8,128)(2,1)S(1)} %get-tuple-element.55.refs_1_, bf16[3,256,128]{2,1,0:T(8,128)(2,1)S(1)} %get-tuple-element.56.refs_2_, bf16[3,256,128]{2,1,0:T(8,128)(2,1)S(1)} %get-tuple-element.57.refs_3_), custom_call_target="tpu_custom_call" | custom-call | tf_op jit(solution)/shard_map/pallas_call | solution.py:39
  9.9 2.6 %collective-permute-start.6 = (bf16[4,2,64,128]{3,2,1,0:T(8,128)(2,1)S(1)}, bf16[4,2,64,128]{3,2,1,0:T(8,128)(2,1)S(1)}, u32[]{:S(2)}, u32[]{:S(2)}) collective-permute-start(bf16[4,2,64,128]{3,2,1,0:T(8,128)(2,1)S(1)} %shard_map.87), channel_id=1, source_target_pairs={{0,16},{4,20},{8,24},{12,28},{16,0},{20,4},{24,8},{28,12},{1,17},{... | collective-permute-start | bytes 393224 | tf_op jit(solution)/shard_map/ppermute | solution.py:437
  12.5 1.6 %copy-done = bf16[512,2048]{1,0:T(8,128)(2,1)S(1)} copy-done((bf16[512,2048]{1,0:T(8,128)(2,1)S(1)}, bf16[512,2048]{1,0:T(8,128)(2,1)}, u32[]{:S(2)}) %copy-start) | copy-done | bytes 2097176
  15.8 3.6 %collective-permute-done.1.refs_2_ = bf16[3,256,128]{2,1,0:T(8,128)(2,1)S(1)} collective-permute-done((bf16[3,256,128]{2,1,0:T(8,128)(2,1)S(1)}, bf16[3,256,128]{2,1,0:T(8,128)(2,1)S(1)}, u32[]{:S(2)}, u32[]{:S(2)}) %collective-permute-start.1) | collective-permute-done | bytes 196640 | tf_op jit(solution)/shard_map/ppermute | solution.py:437
  19.4 1.8 %collective-permute-start.7 = (bf16[2,256,128]{2,1,0:T(8,128)(2,1)S(1)}, bf16[2,256,128]{2,1,0:T(8,128)(2,1)S(1)}, u32[]{:S(2)}, u32[]{:S(2)}) collective-permute-start(bf16[2,256,128]{2,1,0:T(8,128)(2,1)S(1)} %shard_map.90), channel_id=1, source_target_pairs={{0,16},{4,20},{8,24},{12,28},{16,0},{20,4},{24,8},{28,12},{1,17},{... | collective-permute-start | bytes 393224 | tf_op jit(solution)/shard_map/ppermute | solution.py:437
  22.0 2.3 %collective-permute-start.8 = (bf16[384,128]{1,0:T(8,128)(2,1)S(1)}, bf16[384,128]{1,0:T(8,128)(2,1)S(1)}, u32[]{:S(2)}, u32[]{:S(2)}) collective-permute-start(bf16[384,128]{1,0:T(8,128)(2,1)S(1)} %get-tuple-element.70), channel_id=1, source_target_pairs={{0,12},{4,8},{8,4},{12,0},{16,28},{20,24},{24,20},{28,16},{1,13},{... | collective-permute-start | bytes 294920 | tf_op jit(solution)/shard_map/ppermute | solution.py:437
  24.6 1.4 %collective-permute-start.10 = (bf16[384,128]{1,0:T(8,128)(2,1)S(1)}, bf16[384,128]{1,0:T(8,128)(2,1)S(1)}, u32[]{:S(2)}, u32[]{:S(2)}) collective-permute-start(bf16[384,128]{1,0:T(8,128)(2,1)S(1)} %get-tuple-element.72), channel_id=1, source_target_pairs={{0,4},{4,0},{8,12},{12,8},{16,20},{20,16},{24,28},{28,24},{1,5},{5... | collective-permute-start | bytes 294920 | tf_op jit(solution)/shard_map/ppermute | solution.py:437
  26.4 1.7 %shard_map.89 = (bf16[3,4,256,128]{3,2,1,0:T(8,128)(2,1)S(1)}, bf16[128,1024]{1,0:T(8,128)(2,1)S(1)}, bf16[128,1024]{1,0:T(8,128)(2,1)S(1)}, bf16[128,512]{1,0:T...) custom-call(bf16[4,2,256,128]{3,2,1,0:T(8,128)(2,1)S(1)} %get-tuple-element.58, ...), custom_call_target="tpu_custom_call" | custom-call | flops 335544320 | bytes 6946816 | tf_op jit(solution)/shard_map/pallas_call | solution.py:39
  29.7 2.2 %shard_map.91 = (bf16[4,4,256,256]{3,2,1,0:T(8,128)(2,1)S(1)}, bf16[4,256,128]{2,1,0:T(8,128)(2,1)S(1)}, bf16[2,256,128]{2,1,0:T(8,128)(2,1)S(1)}, f32[8,1024]{1...) custom-call(bf16[3,4,256,128]{3,2,1,0:T(8,128)(2,1)S(1)} %get-tuple-, ...), custom_call_target="tpu_custom_call" | custom-call | flops 335544320 | bytes 9601024 | tf_op jit(solution)/shard_map/pallas_call | solution.py:39
  31.9 1.0 %collective-permute-start.20 = (bf16[896,128]{1,0:T(8,128)(2,1)S(1)}, bf16[896,128]{1,0:T(8,128)(2,1)S(1)}, u32[]{:S(2)}, u32[]{:S(2)}) collective-permute-start(bf16[896,128]{1,0:T(8,128)(2,1)S(1)} %get-tuple-element.95), channel_id=1, source_target_pairs={{0,16},{4,20},{8,24},{12,28},{16,0},{20,4},{24,8},{28,12},{1,17},{... | collective-permute-start | bytes 688136 | tf_op jit(solution)/shard_map/ppermute | solution.py:437
  33.0 2.8 %collective-permute-start.11 = (bf16[256,128]{1,0:T(8,128)(2,1)S(1)}, bf16[256,128]{1,0:T(8,128)(2,1)S(1)}, u32[]{:S(2)}, u32[]{:S(2)}) collective-permute-start(bf16[256,128]{1,0:T(8,128)(2,1)S(1)} %get-tuple-element.74), channel_id=1, source_target_pairs={{0,12},{4,8},{8,4},{12,0},{16,28},{20,24},{24,20},{28,16},{1,13},{... | collective-permute-start | bytes 196616 | tf_op jit(solution)/shard_map/ppermute | solution.py:437
  35.7 1.2 %collective-permute-start.13 = (bf16[256,128]{1,0:T(8,128)(2,1)S(1)}, bf16[256,128]{1,0:T(8,128)(2,1)S(1)}, u32[]{:S(2)}, u32[]{:S(2)}) collective-permute-start(bf16[256,128]{1,0:T(8,128)(2,1)S(1)} %get-tuple-element.76), channel_id=1, source_target_pairs={{0,4},{4,0},{8,12},{12,8},{16,20},{20,16},{24,28},{28,24},{1,5},{5... | collective-permute-start | bytes 196616 | tf_op jit(solution)/shard_map/ppermute | solution.py:437
  36.9 4.0 %shard_map.92 = (bf16[4,256,128]{2,1,0:T(8,128)(2,1)S(1)}, f32[2,4,256,128]{3,2,1,0:T(8,128)S(1)}) custom-call(bf16[3,4,256,128]{3,2,1,0:T(8,128)(2,1)S(1)} %get-tuple-element.65.refs_0_, bf16[4,2,256,128]{3,2,1,0:T(8,128)(2,1)S(1)} %get-tuple-element.58.near.refs_1_, bf16[2,512,128]{2,1,0:T(8,128)(2,1)S(1)} %get-tuple-element.60.level_1.refs_2_, ...), custom_call_target="tpu_custom_call" | custom-call | tf_op jit(solution)/shard_map/pallas_call | solution.py:39
  42.9 1.3 %collective-permute-done.20.refs_0_ = bf16[896,128]{1,0:T(8,128)(2,1)S(1)} collective-permute-done((bf16[896,128]{1,0:T(8,128)(2,1)S(1)}, bf16[896,128]{1,0:T(8,128)(2,1)S(1)}, u32[]{:S(2)}, u32[]{:S(2)}) %collective-permute-start.20) | collective-permute-done | bytes 229408 | tf_op jit(solution)/shard_map/ppermute | solution.py:437
  44.5 1.2 %collective-permute-start.21 = (bf16[3,256,128]{2,1,0:T(8,128)(2,1)S(1)}, bf16[3,256,128]{2,1,0:T(8,128)(2,1)S(1)}, u32[]{:S(2)}, u32[]{:S(2)}) collective-permute-start(bf16[3,256,128]{2,1,0:T(8,128)(2,1)S(1)} %get-tuple-element.97), channel_id=1, source_target_pairs={{0,12},{4,8},{8,4},{12,0},{16,28},{20,24},{24,20},{28,16},{1,13},{... | collective-permute-start | bytes 589832 | tf_op jit(solution)/shard_map/ppermute | solution.py:437
  45.7 1.1 %collective-permute-start.22 = (bf16[3,256,128]{2,1,0:T(8,128)(2,1)S(1)}, bf16[3,256,128]{2,1,0:T(8,128)(2,1)S(1)}, u32[]{:S(2)}, u32[]{:S(2)}) collective-permute-start(bf16[3,256,128]{2,1,0:T(8,128)(2,1)S(1)} %get-tuple-element.98), channel_id=1, source_target_pairs={{0,8},{4,12},{8,0},{12,4},{16,24},{20,28},{24,16},{28,20},{1,9},{5... | collective-permute-start | bytes 589832 | tf_op jit(solution)/shard_map/ppermute | solution.py:437
  46.8 1.2 %collective-permute-start.23 = (bf16[3,256,128]{2,1,0:T(8,128)(2,1)S(1)}, bf16[3,256,128]{2,1,0:T(8,128)(2,1)S(1)}, u32[]{:S(2)}, u32[]{:S(2)}) collective-permute-start(bf16[3,256,128]{2,1,0:T(8,128)(2,1)S(1)} %get-tuple-element.99), channel_id=1, source_target_pairs={{0,4},{4,0},{8,12},{12,8},{16,20},{20,16},{24,28},{28,24},{1,5},{5... | collective-permute-start | bytes 589832 | tf_op jit(solution)/shard_map/ppermute | solution.py:437
  48.8 1.5 %collective-permute-start.19 = (bf16[32,2048]{1,0:T(8,128)(2,1)S(1)}, bf16[32,2048]{1,0:T(8,128)(2,1)S(1)}, u32[]{:S(2)}, u32[]{:S(2)}) collective-permute-start(bf16[32,2048]{1,0:T(8,128)(2,1)S(1)} %get-tuple-element.93), channel_id=1, source_target_pairs={{0,2},{1,3},{2,0},{3,1},{4,6},{5,7},{6,4},{7,5},{8,10},{9,11},{10,... | collective-permute-start | bytes 393224 | tf_op jit(solution)/shard_map/ppermute | solution.py:437
  50.2 3.1 %collective-permute-done.18.refs_1_ = bf16[32,2048]{1,0:T(8,128)(2,1)S(1)} collective-permute-done((bf16[32,2048]{1,0:T(8,128)(2,1)S(1)}, bf16[32,2048]{1,0:T(8,128)(2,1)S(1)}, u32[]{:S(2)}, u32[]{:S(2)}) %collective-permute-start.18) | collective-permute-done | bytes 131104 | tf_op jit(solution)/shard_map/ppermute | solution.py:437
  53.4 1.4 %collective-permute-done.19.refs_2_ = bf16[32,2048]{1,0:T(8,128)(2,1)S(1)} collective-permute-done((bf16[32,2048]{1,0:T(8,128)(2,1)S(1)}, bf16[32,2048]{1,0:T(8,128)(2,1)S(1)}, u32[]{:S(2)}, u32[]{:S(2)}) %collective-permute-start.19) | collective-permute-done | bytes 131104 | tf_op jit(solution)/shard_map/ppermute | solution.py:437
  55.7 1.1 %shard_map.96 = (bf16[256,512]{1,0:T(8,128)(2,1)}, bf16[256,512]{1,0:T(8,128)(2,1)}, bf16[256,512]{1,0:T(8,128)(2,1)}, bf16[64,2048]{1,0:T(8,128)(2,1)}) custom-call(f32[64,2048]{1,0:T(8,128)S(1)} %get-tuple-element.91.refs_0_, bf16[32,2048]{1,0:T(8,128)(2,1)S(1)} %collective-permute-done.18.refs_1_, bf16[32,2048]{1,0:T(8,128)(2,1)S(1)} %collective-permute-done.19.refs_2_, ...), custom_call_target="tpu_custom_call" | custom-call | tf_op jit(solution)/shard_map/pallas_call | solution.py:39
  (41 shorter events, 9.8 us)
Async XLA Ops:
  0.6 11.9 %collective-permute-start.3 = (bf16[64,2048]{1,0:T(8,128)(2,1)}, bf16[64,2048]{1,0:T(8,128)(2,1)S(1)}, u32[]{:S(2)}, u32[]{:S(2)}) collective-permute-start(bf16[64,2048]{1,0:T(8,128)(2,1)} %refs_0_.1), channel_id=1, source_target_pairs={{0,2},{1,3},{2,0},{3,1},{4,6},{5,7},{6,4},{7,5},{8,10},{9,11},{10,... | collective-permute-start | bytes 786440 | tf_op jit(solution)/shard_map/ppermute | solution.py:437
  4.9 10.4 %collective-permute-start = (bf16[3,256,128]{2,1,0:T(8,128)(2,1)S(1)}, bf16[3,256,128]{2,1,0:T(8,128)(2,1)S(1)}, u32[]{:S(2)}, u32[]{:S(2)}) collective-permute-start(bf16[3,256,128]{2,1,0:T(8,128)(2,1)S(1)} %get-tuple-element.55.refs_1_), channel_id=1, source_target_pairs={{0,12},{4,8},{8,4},{12,0},{16,28},{20,24},{24,20},{28,16},{1,13},{... | collective-permute-start | bytes 589832 | tf_op jit(solution)/shard_map/ppermute | solution.py:437
  7.5 11.8 %collective-permute-start.1 = (bf16[3,256,128]{2,1,0:T(8,128)(2,1)S(1)}, bf16[3,256,128]{2,1,0:T(8,128)(2,1)S(1)}, u32[]{:S(2)}, u32[]{:S(2)}) collective-permute-start(bf16[3,256,128]{2,1,0:T(8,128)(2,1)S(1)} %get-tuple-element.56.refs_2_), channel_id=1, source_target_pairs={{0,8},{4,12},{8,0},{12,4},{16,24},{20,28},{24,16},{28,20},{1,9},{5... | collective-permute-start | bytes 589832 | tf_op jit(solution)/shard_map/ppermute | solution.py:437
  8.0 11.4 %collective-permute-start.2 = (bf16[3,256,128]{2,1,0:T(8,128)(2,1)S(1)}, bf16[3,256,128]{2,1,0:T(8,128)(2,1)S(1)}, u32[]{:S(2)}, u32[]{:S(2)}) collective-permute-start(bf16[3,256,128]{2,1,0:T(8,128)(2,1)S(1)} %get-tuple-element.57.refs_3_), channel_id=1, source_target_pairs={{0,4},{4,0},{8,12},{12,8},{16,20},{20,16},{24,28},{28,24},{1,5},{5... | collective-permute-start | bytes 589832 | tf_op jit(solution)/shard_map/ppermute | solution.py:437
  9.9 11.2 %collective-permute-start.6 = (bf16[4,2,64,128]{3,2,1,0:T(8,128)(2,1)S(1)}, bf16[4,2,64,128]{3,2,1,0:T(8,128)(2,1)S(1)}, u32[]{:S(2)}, u32[]{:S(2)}) collective-permute-start(bf16[4,2,64,128]{3,2,1,0:T(8,128)(2,1)S(1)} %shard_map.87), channel_id=1, source_target_pairs={{0,16},{4,20},{8,24},{12,28},{16,0},{20,4},{24,8},{28,12},{1,17},{... | collective-permute-start | bytes 393224 | tf_op jit(solution)/shard_map/ppermute | solution.py:437
  15.2 5.9 %collective-permute-start.4 = (bf16[64,2048]{1,0:T(8,128)(2,1)S(1)}, bf16[64,2048]{1,0:T(8,128)(2,1)S(1)}, u32[]{:S(2)}, u32[]{:S(2)}) collective-permute-start(bf16[64,2048]{1,0:T(8,128)(2,1)S(1)} %get-tuple-element.61.refs_0_), channel_id=1, source_target_pairs={{0,1},{1,0},{2,3},{3,2},{4,5},{5,4},{6,7},{7,6},{8,9},{9,8},{10,11... | collective-permute-start | bytes 786440 | tf_op jit(solution)/shard_map/ppermute | solution.py:437
  15.3 5.8 %collective-permute-start.5 = (bf16[64,2048]{1,0:T(8,128)(2,1)S(1)}, bf16[64,2048]{1,0:T(8,128)(2,1)S(1)}, u32[]{:S(2)}, u32[]{:S(2)}) collective-permute-start(bf16[64,2048]{1,0:T(8,128)(2,1)S(1)} %get-tuple-element.62.refs_2_), channel_id=1, source_target_pairs={{0,1},{1,0},{2,3},{3,2},{4,5},{5,4},{6,7},{7,6},{8,9},{9,8},{10,11... | collective-permute-start | bytes 786440 | tf_op jit(solution)/shard_map/ppermute | solution.py:437
  19.4 8.6 %collective-permute-start.7 = (bf16[2,256,128]{2,1,0:T(8,128)(2,1)S(1)}, bf16[2,256,128]{2,1,0:T(8,128)(2,1)S(1)}, u32[]{:S(2)}, u32[]{:S(2)}) collective-permute-start(bf16[2,256,128]{2,1,0:T(8,128)(2,1)S(1)} %shard_map.90), channel_id=1, source_target_pairs={{0,16},{4,20},{8,24},{12,28},{16,0},{20,4},{24,8},{28,12},{1,17},{... | collective-permute-start | bytes 393224 | tf_op jit(solution)/shard_map/ppermute | solution.py:437
  22.0 7.0 %collective-permute-start.8 = (bf16[384,128]{1,0:T(8,128)(2,1)S(1)}, bf16[384,128]{1,0:T(8,128)(2,1)S(1)}, u32[]{:S(2)}, u32[]{:S(2)}) collective-permute-start(bf16[384,128]{1,0:T(8,128)(2,1)S(1)} %get-tuple-element.70), channel_id=1, source_target_pairs={{0,12},{4,8},{8,4},{12,0},{16,28},{20,24},{24,20},{28,16},{1,13},{... | collective-permute-start | bytes 294920 | tf_op jit(solution)/shard_map/ppermute | solution.py:437
  24.3 5.4 %collective-permute-start.9 = (bf16[384,128]{1,0:T(8,128)(2,1)S(1)}, bf16[384,128]{1,0:T(8,128)(2,1)S(1)}, u32[]{:S(2)}, u32[]{:S(2)}) collective-permute-start(bf16[384,128]{1,0:T(8,128)(2,1)S(1)} %get-tuple-element.71), channel_id=1, source_target_pairs={{0,8},{4,12},{8,0},{12,4},{16,24},{20,28},{24,16},{28,20},{1,9},{5... | collective-permute-start | bytes 294920 | tf_op jit(solution)/shard_map/ppermute | solution.py:437
  24.6 5.1 %collective-permute-start.10 = (bf16[384,128]{1,0:T(8,128)(2,1)S(1)}, bf16[384,128]{1,0:T(8,128)(2,1)S(1)}, u32[]{:S(2)}, u32[]{:S(2)}) collective-permute-start(bf16[384,128]{1,0:T(8,128)(2,1)S(1)} %get-tuple-element.72), channel_id=1, source_target_pairs={{0,4},{4,0},{8,12},{12,8},{16,20},{20,16},{24,28},{28,24},{1,5},{5... | collective-permute-start | bytes 294920 | tf_op jit(solution)/shard_map/ppermute | solution.py:437
  31.9 12.2 %collective-permute-start.20 = (bf16[896,128]{1,0:T(8,128)(2,1)S(1)}, bf16[896,128]{1,0:T(8,128)(2,1)S(1)}, u32[]{:S(2)}, u32[]{:S(2)}) collective-permute-start(bf16[896,128]{1,0:T(8,128)(2,1)S(1)} %get-tuple-element.95), channel_id=1, source_target_pairs={{0,16},{4,20},{8,24},{12,28},{16,0},{20,4},{24,8},{28,12},{1,17},{... | collective-permute-start | bytes 688136 | tf_op jit(solution)/shard_map/ppermute | solution.py:437
  33.0 8.0 %collective-permute-start.11 = (bf16[256,128]{1,0:T(8,128)(2,1)S(1)}, bf16[256,128]{1,0:T(8,128)(2,1)S(1)}, u32[]{:S(2)}, u32[]{:S(2)}) collective-permute-start(bf16[256,128]{1,0:T(8,128)(2,1)S(1)} %get-tuple-element.74), channel_id=1, source_target_pairs={{0,12},{4,8},{8,4},{12,0},{16,28},{20,24},{24,20},{28,16},{1,13},{... | collective-permute-start | bytes 196616 | tf_op jit(solution)/shard_map/ppermute | solution.py:437
  35.7 5.2 %collective-permute-start.12 = (bf16[256,128]{1,0:T(8,128)(2,1)S(1)}, bf16[256,128]{1,0:T(8,128)(2,1)S(1)}, u32[]{:S(2)}, u32[]{:S(2)}) collective-permute-start(bf16[256,128]{1,0:T(8,128)(2,1)S(1)} %get-tuple-element.75), channel_id=1, source_target_pairs={{0,8},{4,12},{8,0},{12,4},{16,24},{20,28},{24,16},{28,20},{1,9},{5... | collective-permute-start | bytes 196616 | tf_op jit(solution)/shard_map/ppermute | solution.py:437
  35.7 5.2 %collective-permute-start.13 = (bf16[256,128]{1,0:T(8,128)(2,1)S(1)}, bf16[256,128]{1,0:T(8,128)(2,1)S(1)}, u32[]{:S(2)}, u32[]{:S(2)}) collective-permute-start(bf16[256,128]{1,0:T(8,128)(2,1)S(1)} %get-tuple-element.76), channel_id=1, source_target_pairs={{0,4},{4,0},{8,12},{12,8},{16,20},{20,16},{24,28},{28,24},{1,5},{5... | collective-permute-start | bytes 196616 | tf_op jit(solution)/shard_map/ppermute | solution.py:437
  41.8 3.9 %collective-permute-start.14 = (bf16[32,2048]{1,0:T(8,128)(2,1)S(1)}, bf16[32,2048]{1,0:T(8,128)(2,1)S(1)}, u32[]{:S(2)}, u32[]{:S(2)}) collective-permute-start(bf16[32,2048]{1,0:T(8,128)(2,1)S(1)} %get-tuple-element.87), channel_id=1, source_target_pairs={{0,1},{1,0},{2,3},{3,2},{4,5},{5,4},{6,7},{7,6},{8,9},{9,8},{10,11... | collective-permute-start | bytes 393224 | tf_op jit(solution)/shard_map/ppermute | solution.py:437
  41.9 4.9 %collective-permute-start.15 = (bf16[32,2048]{1,0:T(8,128)(2,1)S(1)}, bf16[32,2048]{1,0:T(8,128)(2,1)S(1)}, u32[]{:S(2)}, u32[]{:S(2)}) collective-permute-start(bf16[32,2048]{1,0:T(8,128)(2,1)S(1)} %get-tuple-element.88), channel_id=1, source_target_pairs={{0,1},{1,0},{2,3},{3,2},{4,5},{5,4},{6,7},{7,6},{8,9},{9,8},{10,11... | collective-permute-start | bytes 393224 | tf_op jit(solution)/shard_map/ppermute | solution.py:437
  42.4 5.7 %collective-permute-start.16 = (bf16[32,2048]{1,0:T(8,128)(2,1)S(1)}, bf16[32,2048]{1,0:T(8,128)(2,1)S(1)}, u32[]{:S(2)}, u32[]{:S(2)}) collective-permute-start(bf16[32,2048]{1,0:T(8,128)(2,1)S(1)} %get-tuple-element.89), channel_id=1, source_target_pairs={{0,1},{1,0},{2,3},{3,2},{4,5},{5,4},{6,7},{7,6},{8,9},{9,8},{10,11... | collective-permute-start | bytes 393224 | tf_op jit(solution)/shard_map/ppermute | solution.py:437
  42.4 5.6 %collective-permute-start.17 = (bf16[32,2048]{1,0:T(8,128)(2,1)S(1)}, bf16[32,2048]{1,0:T(8,128)(2,1)S(1)}, u32[]{:S(2)}, u32[]{:S(2)}) collective-permute-start(bf16[32,2048]{1,0:T(8,128)(2,1)S(1)} %get-tuple-element.90), channel_id=1, source_target_pairs={{0,1},{1,0},{2,3},{3,2},{4,5},{5,4},{6,7},{7,6},{8,9},{9,8},{10,11... | collective-permute-start | bytes 393224 | tf_op jit(solution)/shard_map/ppermute | solution.py:437
  44.5 10.3 %collective-permute-start.21 = (bf16[3,256,128]{2,1,0:T(8,128)(2,1)S(1)}, bf16[3,256,128]{2,1,0:T(8,128)(2,1)S(1)}, u32[]{:S(2)}, u32[]{:S(2)}) collective-permute-start(bf16[3,256,128]{2,1,0:T(8,128)(2,1)S(1)} %get-tuple-element.97), channel_id=1, source_target_pairs={{0,12},{4,8},{8,4},{12,0},{16,28},{20,24},{24,20},{28,16},{1,13},{... | collective-permute-start | bytes 589832 | tf_op jit(solution)/shard_map/ppermute | solution.py:437
  45.7 10.0 %collective-permute-start.22 = (bf16[3,256,128]{2,1,0:T(8,128)(2,1)S(1)}, bf16[3,256,128]{2,1,0:T(8,128)(2,1)S(1)}, u32[]{:S(2)}, u32[]{:S(2)}) collective-permute-start(bf16[3,256,128]{2,1,0:T(8,128)(2,1)S(1)} %get-tuple-element.98), channel_id=1, source_target_pairs={{0,8},{4,12},{8,0},{12,4},{16,24},{20,28},{24,16},{28,20},{1,9},{5... | collective-permute-start | bytes 589832 | tf_op jit(solution)/shard_map/ppermute | solution.py:437
  46.8 8.9 %collective-permute-start.23 = (bf16[3,256,128]{2,1,0:T(8,128)(2,1)S(1)}, bf16[3,256,128]{2,1,0:T(8,128)(2,1)S(1)}, u32[]{:S(2)}, u32[]{:S(2)}) collective-permute-start(bf16[3,256,128]{2,1,0:T(8,128)(2,1)S(1)} %get-tuple-element.99), channel_id=1, source_target_pairs={{0,4},{4,0},{8,12},{12,8},{16,20},{20,16},{24,28},{28,24},{1,5},{5... | collective-permute-start | bytes 589832 | tf_op jit(solution)/shard_map/ppermute | solution.py:437
  48.2 5.2 %collective-permute-start.18 = (bf16[32,2048]{1,0:T(8,128)(2,1)S(1)}, bf16[32,2048]{1,0:T(8,128)(2,1)S(1)}, u32[]{:S(2)}, u32[]{:S(2)}) collective-permute-start(bf16[32,2048]{1,0:T(8,128)(2,1)S(1)} %get-tuple-element.92), channel_id=1, source_target_pairs={{0,2},{1,3},{2,0},{3,1},{4,6},{5,7},{6,4},{7,5},{8,10},{9,11},{10,... | collective-permute-start | bytes 393224 | tf_op jit(solution)/shard_map/ppermute | solution.py:437
  48.8 6.0 %collective-permute-start.19 = (bf16[32,2048]{1,0:T(8,128)(2,1)S(1)}, bf16[32,2048]{1,0:T(8,128)(2,1)S(1)}, u32[]{:S(2)}, u32[]{:S(2)}) collective-permute-start(bf16[32,2048]{1,0:T(8,128)(2,1)S(1)} %get-tuple-element.93), channel_id=1, source_target_pairs={{0,2},{1,3},{2,0},{3,1},{4,6},{5,7},{6,4},{7,5},{8,10},{9,11},{10,... | collective-permute-start | bytes 393224 | tf_op jit(solution)/shard_map/ppermute | solution.py:437
  (2 other events, 2.5 us)

commit v18 on v17

--- a/solution.py
+++ b/solution.py
@@ -321,12 +321,12 @@
         query_t[:, span(b, BLOCK)] += dot(block[0].T, rim_shift[i])
     for b in range(nb):
         grad, delta = grads[b], deltas[:1, at_block(b)]
-        sides, keys = near_window(b, nb)
-        blocks = slice(keys.start // BLOCK, keys.stop // BLOCK)
-        slope = dot_nt(near[blocks, 1].reshape(-1, HEAD_DIM), grad)
-        parts = (prob[b, sides].reshape(-1, BLOCK).astype(F32) * (slope - delta)).astype(BF16)
-        shift[b, sides] = parts.reshape(-1, BLOCK, BLOCK)
-        grad_t = query_t[:, at_block(b)] + dot(k_t[:, keys], parts)
+        grad_t = query_t[:, at_block(b)]
+        for side in near_sides(b, nb):
+            slope = dot_nt(near[b + side - 1, 1], grad)
+            part = (prob[b, side].astype(F32) * (slope - delta)).astype(BF16)
+            shift[b, side] = part
+            grad_t = grad_t + dot(k_t[:, at_block(b + side - 1)], part)
         slope = dot_nt(level_1[1, at_block(sibling(b))], grad)
         part = (prob[b, 3].astype(F32) * (slope - delta)).astype(BF16)
         shift[b, 3] = part

time: 57.1 us -> 57.1 us (level)
  waiting for transfers between devices: 12 us -> 12.7 us
  Pallas kernels: 14.3 us -> 13.7 us
    ppermute x24, waiting for transfers between devices: 12 us -> 12.7 us  [swapped(): lax.ppermute(x, axis, [(i, i ^ step) for i in range(lax.axis_size(axis))])]
    pallas_call x13, Pallas kernels: 14.3 us -> 13.7 us  [call(): pl.pallas_call(kernel, out_shape=out_shape, in_specs=[kept if copied else...]
  transfers between devices with their start and end apart: 24 -> 24, of which waited for: 7 -> 8; matrix products, arithmetic and copies ran while one was open for 0% -> 0% of each run, Pallas kernels for 19% -> 18%
where the time goes in v18:
time: 57.1 us; the launch traced here: 56.8 us
  starting transfers between devices  27.2 us (48%)
  Pallas kernels  13.7 us (24%)
  waiting for transfers between devices  12.7 us (22%)
  local copies, waits for them, and re-layouts  2.54 us (4%)
  between operations  0.76 us (1%)
    ppermute x24, starting transfers between devices, swapped(): lax.ppermute(x, axis, [(i, i ^ step) for i in range(lax.axis_size(axis))])  27.2 us
    pallas_call x13, Pallas kernels, call(): pl.pallas_call(kernel, out_shape=out_shape, in_specs=[kept if copied else...  13.7 us
    ppermute x24, waiting for transfers between devices, swapped(): lax.ppermute(x, axis, [(i, i ^ step) for i in range(lax.axis_size(axis))])  12.7 us
    unnamed x4, local copies, waits for them, and re-layouts  2.54 us
  transfers between devices with their start and end apart: 24, of which 8 were waited for; matrix products, arithmetic and copies ran while one was open for 0% of the time, Pallas kernels for 18%

profile of v18, /device:TPU:0, one launch (start us, length us, event | category | flops | bytes accessed | tf_op | source)
XLA Modules:
  0.0 56.8 jit_solution(15412666596460327841)
XLA Ops:
  0.6 3.0 %collective-permute-start.3 = (bf16[64,2048]{1,0:T(8,128)(2,1)}, bf16[64,2048]{1,0:T(8,128)(2,1)S(1)}, u32[]{:S(2)}, u32[]{:S(2)}) collective-permute-start(bf16[64,2048]{1,0:T(8,128)(2,1)} %refs_0_.1), channel_id=1, source_target_pairs={{0,2},{1,3},{2,0},{3,1},{4,6},{5,7},{6,4},{7,5},{8,10},{9,11},{10,... | collective-permute-start | bytes 786440 | tf_op jit(solution)/shard_map/ppermute | solution.py:437
  3.6 1.3 %shard_map.84 = (bf16[3,256,128]{2,1,0:T(8,128)(2,1)S(1)}, bf16[3,256,128]{2,1,0:T(8,128)(2,1)S(1)}, bf16[3,256,128]{2,1,0:T(8,128)(2,1)S(1)}, bf16[3,256,128]{2,1,0:T(8,128)(2,1)S(1)}) custom-call(bf16[256,512]{1,0:T(8,128)(2,1)} %q.1, bf16[256,512]{1,0:T(8,128)(2,1)} %k.1, bf16[256,512]{1,0:T(8,128)(2,1)} %v.1), custom_call_target="tpu_custom_call" | custom-call | tf_op jit(solution)/shard_map/pallas_call | solution.py:39
  4.9 2.6 %collective-permute-start = (bf16[3,256,128]{2,1,0:T(8,128)(2,1)S(1)}, bf16[3,256,128]{2,1,0:T(8,128)(2,1)S(1)}, u32[]{:S(2)}, u32[]{:S(2)}) collective-permute-start(bf16[3,256,128]{2,1,0:T(8,128)(2,1)S(1)} %get-tuple-element.55.refs_1_), channel_id=1, source_target_pairs={{0,12},{4,8},{8,4},{12,0},{16,28},{20,24},{24,20},{28,16},{1,13},{... | collective-permute-start | bytes 589832 | tf_op jit(solution)/shard_map/ppermute | solution.py:437
  8.5 1.4 %shard_map.87 = bf16[4,2,64,128]{3,2,1,0:T(8,128)(2,1)S(1)} custom-call(bf16[3,256,128]{2,1,0:T(8,128)(2,1)S(1)} %get-tuple-element.54.refs_0_, bf16[3,256,128]{2,1,0:T(8,128)(2,1)S(1)} %get-tuple-element.55.refs_1_, bf16[3,256,128]{2,1,0:T(8,128)(2,1)S(1)} %get-tuple-element.56.refs_2_, bf16[3,256,128]{2,1,0:T(8,128)(2,1)S(1)} %get-tuple-element.57.refs_3_), custom_call_target="tpu_custom_call" | custom-call | tf_op jit(solution)/shard_map/pallas_call | solution.py:39
  9.9 2.6 %collective-permute-start.6 = (bf16[4,2,64,128]{3,2,1,0:T(8,128)(2,1)S(1)}, bf16[4,2,64,128]{3,2,1,0:T(8,128)(2,1)S(1)}, u32[]{:S(2)}, u32[]{:S(2)}) collective-permute-start(bf16[4,2,64,128]{3,2,1,0:T(8,128)(2,1)S(1)} %shard_map.87), channel_id=1, source_target_pairs={{0,16},{4,20},{8,24},{12,28},{16,0},{20,4},{24,8},{28,12},{1,17},{... | collective-permute-start | bytes 393224 | tf_op jit(solution)/shard_map/ppermute | solution.py:437
  12.5 1.6 %copy-done = bf16[512,2048]{1,0:T(8,128)(2,1)S(1)} copy-done((bf16[512,2048]{1,0:T(8,128)(2,1)S(1)}, bf16[512,2048]{1,0:T(8,128)(2,1)}, u32[]{:S(2)}) %copy-start) | copy-done | bytes 2097176
  15.8 3.6 %collective-permute-done.1.refs_2_ = bf16[3,256,128]{2,1,0:T(8,128)(2,1)S(1)} collective-permute-done((bf16[3,256,128]{2,1,0:T(8,128)(2,1)S(1)}, bf16[3,256,128]{2,1,0:T(8,128)(2,1)S(1)}, u32[]{:S(2)}, u32[]{:S(2)}) %collective-permute-start.1) | collective-permute-done | bytes 196640 | tf_op jit(solution)/shard_map/ppermute | solution.py:437
  19.4 1.8 %collective-permute-start.7 = (bf16[2,256,128]{2,1,0:T(8,128)(2,1)S(1)}, bf16[2,256,128]{2,1,0:T(8,128)(2,1)S(1)}, u32[]{:S(2)}, u32[]{:S(2)}) collective-permute-start(bf16[2,256,128]{2,1,0:T(8,128)(2,1)S(1)} %shard_map.90), channel_id=1, source_target_pairs={{0,16},{4,20},{8,24},{12,28},{16,0},{20,4},{24,8},{28,12},{1,17},{... | collective-permute-start | bytes 393224 | tf_op jit(solution)/shard_map/ppermute | solution.py:437
  22.0 2.3 %collective-permute-start.8 = (bf16[384,128]{1,0:T(8,128)(2,1)S(1)}, bf16[384,128]{1,0:T(8,128)(2,1)S(1)}, u32[]{:S(2)}, u32[]{:S(2)}) collective-permute-start(bf16[384,128]{1,0:T(8,128)(2,1)S(1)} %get-tuple-element.70), channel_id=1, source_target_pairs={{0,12},{4,8},{8,4},{12,0},{16,28},{20,24},{24,20},{28,16},{1,13},{... | collective-permute-start | bytes 294920 | tf_op jit(solution)/shard_map/ppermute | solution.py:437
  24.6 1.4 %collective-permute-start.10 = (bf16[384,128]{1,0:T(8,128)(2,1)S(1)}, bf16[384,128]{1,0:T(8,128)(2,1)S(1)}, u32[]{:S(2)}, u32[]{:S(2)}) collective-permute-start(bf16[384,128]{1,0:T(8,128)(2,1)S(1)} %get-tuple-element.72), channel_id=1, source_target_pairs={{0,4},{4,0},{8,12},{12,8},{16,20},{20,16},{24,28},{28,24},{1,5},{5... | collective-permute-start | bytes 294920 | tf_op jit(solution)/shard_map/ppermute | solution.py:437
  26.4 1.7 %shard_map.89 = (bf16[3,4,256,128]{3,2,1,0:T(8,128)(2,1)S(1)}, bf16[128,1024]{1,0:T(8,128)(2,1)S(1)}, bf16[128,1024]{1,0:T(8,128)(2,1)S(1)}, bf16[128,512]{1,0:T...) custom-call(bf16[4,2,256,128]{3,2,1,0:T(8,128)(2,1)S(1)} %get-tuple-element.58, ...), custom_call_target="tpu_custom_call" | custom-call | flops 335544320 | bytes 6946816 | tf_op jit(solution)/shard_map/pallas_call | solution.py:39
  29.7 2.2 %shard_map.91 = (bf16[4,4,256,256]{3,2,1,0:T(8,128)(2,1)S(1)}, bf16[4,256,128]{2,1,0:T(8,128)(2,1)S(1)}, bf16[2,256,128]{2,1,0:T(8,128)(2,1)S(1)}, f32[8,1024]{1...) custom-call(bf16[3,4,256,128]{3,2,1,0:T(8,128)(2,1)S(1)} %get-tuple-, ...), custom_call_target="tpu_custom_call" | custom-call | flops 335544320 | bytes 9601024 | tf_op jit(solution)/shard_map/pallas_call | solution.py:39
  31.9 1.0 %collective-permute-start.20 = (bf16[896,128]{1,0:T(8,128)(2,1)S(1)}, bf16[896,128]{1,0:T(8,128)(2,1)S(1)}, u32[]{:S(2)}, u32[]{:S(2)}) collective-permute-start(bf16[896,128]{1,0:T(8,128)(2,1)S(1)} %get-tuple-element.95), channel_id=1, source_target_pairs={{0,16},{4,20},{8,24},{12,28},{16,0},{20,4},{24,8},{28,12},{1,17},{... | collective-permute-start | bytes 688136 | tf_op jit(solution)/shard_map/ppermute | solution.py:437
  33.0 2.8 %collective-permute-start.11 = (bf16[256,128]{1,0:T(8,128)(2,1)S(1)}, bf16[256,128]{1,0:T(8,128)(2,1)S(1)}, u32[]{:S(2)}, u32[]{:S(2)}) collective-permute-start(bf16[256,128]{1,0:T(8,128)(2,1)S(1)} %get-tuple-element.74), channel_id=1, source_target_pairs={{0,12},{4,8},{8,4},{12,0},{16,28},{20,24},{24,20},{28,16},{1,13},{... | collective-permute-start | bytes 196616 | tf_op jit(solution)/shard_map/ppermute | solution.py:437
  35.7 1.2 %collective-permute-start.13 = (bf16[256,128]{1,0:T(8,128)(2,1)S(1)}, bf16[256,128]{1,0:T(8,128)(2,1)S(1)}, u32[]{:S(2)}, u32[]{:S(2)}) collective-permute-start(bf16[256,128]{1,0:T(8,128)(2,1)S(1)} %get-tuple-element.76), channel_id=1, source_target_pairs={{0,4},{4,0},{8,12},{12,8},{16,20},{20,16},{24,28},{28,24},{1,5},{5... | collective-permute-start | bytes 196616 | tf_op jit(solution)/shard_map/ppermute | solution.py:437
  36.9 3.3 %shard_map.92 = (bf16[4,256,128]{2,1,0:T(8,128)(2,1)S(1)}, f32[2,4,256,128]{3,2,1,0:T(8,128)S(1)}) custom-call(bf16[3,4,256,128]{3,2,1,0:T(8,128)(2,1)S(1)} %get-tuple-element.65.refs_0_, bf16[4,2,256,128]{3,2,1,0:T(8,128)(2,1)S(1)} %get-tuple-element.58.near.refs_1_, bf16[2,512,128]{2,1,0:T(8,128)(2,1)S(1)} %get-tuple-element.60.level_1.refs_2_, ...), custom_call_target="tpu_custom_call" | custom-call | tf_op jit(solution)/shard_map/pallas_call | solution.py:39
  42.6 1.6 %collective-permute-done.20.refs_0_ = bf16[896,128]{1,0:T(8,128)(2,1)S(1)} collective-permute-done((bf16[896,128]{1,0:T(8,128)(2,1)S(1)}, bf16[896,128]{1,0:T(8,128)(2,1)S(1)}, u32[]{:S(2)}, u32[]{:S(2)}) %collective-permute-start.20) | collective-permute-done | bytes 229408 | tf_op jit(solution)/shard_map/ppermute | solution.py:437
  44.5 1.2 %collective-permute-start.21 = (bf16[3,256,128]{2,1,0:T(8,128)(2,1)S(1)}, bf16[3,256,128]{2,1,0:T(8,128)(2,1)S(1)}, u32[]{:S(2)}, u32[]{:S(2)}) collective-permute-start(bf16[3,256,128]{2,1,0:T(8,128)(2,1)S(1)} %get-tuple-element.97), channel_id=1, source_target_pairs={{0,12},{4,8},{8,4},{12,0},{16,28},{20,24},{24,20},{28,16},{1,13},{... | collective-permute-start | bytes 589832 | tf_op jit(solution)/shard_map/ppermute | solution.py:437
  45.7 1.1 %collective-permute-start.22 = (bf16[3,256,128]{2,1,0:T(8,128)(2,1)S(1)}, bf16[3,256,128]{2,1,0:T(8,128)(2,1)S(1)}, u32[]{:S(2)}, u32[]{:S(2)}) collective-permute-start(bf16[3,256,128]{2,1,0:T(8,128)(2,1)S(1)} %get-tuple-element.98), channel_id=1, source_target_pairs={{0,8},{4,12},{8,0},{12,4},{16,24},{20,28},{24,16},{28,20},{1,9},{5... | collective-permute-start | bytes 589832 | tf_op jit(solution)/shard_map/ppermute | solution.py:437
  46.8 1.2 %collective-permute-start.23 = (bf16[3,256,128]{2,1,0:T(8,128)(2,1)S(1)}, bf16[3,256,128]{2,1,0:T(8,128)(2,1)S(1)}, u32[]{:S(2)}, u32[]{:S(2)}) collective-permute-start(bf16[3,256,128]{2,1,0:T(8,128)(2,1)S(1)} %get-tuple-element.99), channel_id=1, source_target_pairs={{0,4},{4,0},{8,12},{12,8},{16,20},{20,16},{24,28},{28,24},{1,5},{5... | collective-permute-start | bytes 589832 | tf_op jit(solution)/shard_map/ppermute | solution.py:437
  48.8 1.5 %collective-permute-start.19 = (bf16[32,2048]{1,0:T(8,128)(2,1)S(1)}, bf16[32,2048]{1,0:T(8,128)(2,1)S(1)}, u32[]{:S(2)}, u32[]{:S(2)}) collective-permute-start(bf16[32,2048]{1,0:T(8,128)(2,1)S(1)} %get-tuple-element.93), channel_id=1, source_target_pairs={{0,2},{1,3},{2,0},{3,1},{4,6},{5,7},{6,4},{7,5},{8,10},{9,11},{10,... | collective-permute-start | bytes 393224 | tf_op jit(solution)/shard_map/ppermute | solution.py:437
  50.2 3.1 %collective-permute-done.18.refs_1_ = bf16[32,2048]{1,0:T(8,128)(2,1)S(1)} collective-permute-done((bf16[32,2048]{1,0:T(8,128)(2,1)S(1)}, bf16[32,2048]{1,0:T(8,128)(2,1)S(1)}, u32[]{:S(2)}, u32[]{:S(2)}) %collective-permute-start.18) | collective-permute-done | bytes 131104 | tf_op jit(solution)/shard_map/ppermute | solution.py:437
  53.3 1.4 %collective-permute-done.19.refs_2_ = bf16[32,2048]{1,0:T(8,128)(2,1)S(1)} collective-permute-done((bf16[32,2048]{1,0:T(8,128)(2,1)S(1)}, bf16[32,2048]{1,0:T(8,128)(2,1)S(1)}, u32[]{:S(2)}, u32[]{:S(2)}) %collective-permute-start.19) | collective-permute-done | bytes 131104 | tf_op jit(solution)/shard_map/ppermute | solution.py:437
  55.7 1.1 %shard_map.96 = (bf16[256,512]{1,0:T(8,128)(2,1)}, bf16[256,512]{1,0:T(8,128)(2,1)}, bf16[256,512]{1,0:T(8,128)(2,1)}, bf16[64,2048]{1,0:T(8,128)(2,1)}) custom-call(f32[64,2048]{1,0:T(8,128)S(1)} %get-tuple-element.91.refs_0_, bf16[32,2048]{1,0:T(8,128)(2,1)S(1)} %collective-permute-done.18.refs_1_, bf16[32,2048]{1,0:T(8,128)(2,1)S(1)} %collective-permute-done.19.refs_2_, ...), custom_call_target="tpu_custom_call" | custom-call | tf_op jit(solution)/shard_map/pallas_call | solution.py:39
  (41 shorter events, 10.2 us)
Async XLA Ops:
  0.6 11.9 %collective-permute-start.3 = (bf16[64,2048]{1,0:T(8,128)(2,1)}, bf16[64,2048]{1,0:T(8,128)(2,1)S(1)}, u32[]{:S(2)}, u32[]{:S(2)}) collective-permute-start(bf16[64,2048]{1,0:T(8,128)(2,1)} %refs_0_.1), channel_id=1, source_target_pairs={{0,2},{1,3},{2,0},{3,1},{4,6},{5,7},{6,4},{7,5},{8,10},{9,11},{10,... | collective-permute-start | bytes 786440 | tf_op jit(solution)/shard_map/ppermute | solution.py:437
  4.9 10.4 %collective-permute-start = (bf16[3,256,128]{2,1,0:T(8,128)(2,1)S(1)}, bf16[3,256,128]{2,1,0:T(8,128)(2,1)S(1)}, u32[]{:S(2)}, u32[]{:S(2)}) collective-permute-start(bf16[3,256,128]{2,1,0:T(8,128)(2,1)S(1)} %get-tuple-element.55.refs_1_), channel_id=1, source_target_pairs={{0,12},{4,8},{8,4},{12,0},{16,28},{20,24},{24,20},{28,16},{1,13},{... | collective-permute-start | bytes 589832 | tf_op jit(solution)/shard_map/ppermute | solution.py:437
  7.5 11.8 %collective-permute-start.1 = (bf16[3,256,128]{2,1,0:T(8,128)(2,1)S(1)}, bf16[3,256,128]{2,1,0:T(8,128)(2,1)S(1)}, u32[]{:S(2)}, u32[]{:S(2)}) collective-permute-start(bf16[3,256,128]{2,1,0:T(8,128)(2,1)S(1)} %get-tuple-element.56.refs_2_), channel_id=1, source_target_pairs={{0,8},{4,12},{8,0},{12,4},{16,24},{20,28},{24,16},{28,20},{1,9},{5... | collective-permute-start | bytes 589832 | tf_op jit(solution)/shard_map/ppermute | solution.py:437
  8.0 11.4 %collective-permute-start.2 = (bf16[3,256,128]{2,1,0:T(8,128)(2,1)S(1)}, bf16[3,256,128]{2,1,0:T(8,128)(2,1)S(1)}, u32[]{:S(2)}, u32[]{:S(2)}) collective-permute-start(bf16[3,256,128]{2,1,0:T(8,128)(2,1)S(1)} %get-tuple-element.57.refs_3_), channel_id=1, source_target_pairs={{0,4},{4,0},{8,12},{12,8},{16,20},{20,16},{24,28},{28,24},{1,5},{5... | collective-permute-start | bytes 589832 | tf_op jit(solution)/shard_map/ppermute | solution.py:437
  9.9 11.2 %collective-permute-start.6 = (bf16[4,2,64,128]{3,2,1,0:T(8,128)(2,1)S(1)}, bf16[4,2,64,128]{3,2,1,0:T(8,128)(2,1)S(1)}, u32[]{:S(2)}, u32[]{:S(2)}) collective-permute-start(bf16[4,2,64,128]{3,2,1,0:T(8,128)(2,1)S(1)} %shard_map.87), channel_id=1, source_target_pairs={{0,16},{4,20},{8,24},{12,28},{16,0},{20,4},{24,8},{28,12},{1,17},{... | collective-permute-start | bytes 393224 | tf_op jit(solution)/shard_map/ppermute | solution.py:437
  15.2 5.9 %collective-permute-start.4 = (bf16[64,2048]{1,0:T(8,128)(2,1)S(1)}, bf16[64,2048]{1,0:T(8,128)(2,1)S(1)}, u32[]{:S(2)}, u32[]{:S(2)}) collective-permute-start(bf16[64,2048]{1,0:T(8,128)(2,1)S(1)} %get-tuple-element.61.refs_0_), channel_id=1, source_target_pairs={{0,1},{1,0},{2,3},{3,2},{4,5},{5,4},{6,7},{7,6},{8,9},{9,8},{10,11... | collective-permute-start | bytes 786440 | tf_op jit(solution)/shard_map/ppermute | solution.py:437
  15.3 5.8 %collective-permute-start.5 = (bf16[64,2048]{1,0:T(8,128)(2,1)S(1)}, bf16[64,2048]{1,0:T(8,128)(2,1)S(1)}, u32[]{:S(2)}, u32[]{:S(2)}) collective-permute-start(bf16[64,2048]{1,0:T(8,128)(2,1)S(1)} %get-tuple-element.62.refs_2_), channel_id=1, source_target_pairs={{0,1},{1,0},{2,3},{3,2},{4,5},{5,4},{6,7},{7,6},{8,9},{9,8},{10,11... | collective-permute-start | bytes 786440 | tf_op jit(solution)/shard_map/ppermute | solution.py:437
  19.4 8.6 %collective-permute-start.7 = (bf16[2,256,128]{2,1,0:T(8,128)(2,1)S(1)}, bf16[2,256,128]{2,1,0:T(8,128)(2,1)S(1)}, u32[]{:S(2)}, u32[]{:S(2)}) collective-permute-start(bf16[2,256,128]{2,1,0:T(8,128)(2,1)S(1)} %shard_map.90), channel_id=1, source_target_pairs={{0,16},{4,20},{8,24},{12,28},{16,0},{20,4},{24,8},{28,12},{1,17},{... | collective-permute-start | bytes 393224 | tf_op jit(solution)/shard_map/ppermute | solution.py:437
  22.0 7.0 %collective-permute-start.8 = (bf16[384,128]{1,0:T(8,128)(2,1)S(1)}, bf16[384,128]{1,0:T(8,128)(2,1)S(1)}, u32[]{:S(2)}, u32[]{:S(2)}) collective-permute-start(bf16[384,128]{1,0:T(8,128)(2,1)S(1)} %get-tuple-element.70), channel_id=1, source_target_pairs={{0,12},{4,8},{8,4},{12,0},{16,28},{20,24},{24,20},{28,16},{1,13},{... | collective-permute-start | bytes 294920 | tf_op jit(solution)/shard_map/ppermute | solution.py:437
  24.3 5.4 %collective-permute-start.9 = (bf16[384,128]{1,0:T(8,128)(2,1)S(1)}, bf16[384,128]{1,0:T(8,128)(2,1)S(1)}, u32[]{:S(2)}, u32[]{:S(2)}) collective-permute-start(bf16[384,128]{1,0:T(8,128)(2,1)S(1)} %get-tuple-element.71), channel_id=1, source_target_pairs={{0,8},{4,12},{8,0},{12,4},{16,24},{20,28},{24,16},{28,20},{1,9},{5... | collective-permute-start | bytes 294920 | tf_op jit(solution)/shard_map/ppermute | solution.py:437
  24.6 5.1 %collective-permute-start.10 = (bf16[384,128]{1,0:T(8,128)(2,1)S(1)}, bf16[384,128]{1,0:T(8,128)(2,1)S(1)}, u32[]{:S(2)}, u32[]{:S(2)}) collective-permute-start(bf16[384,128]{1,0:T(8,128)(2,1)S(1)} %get-tuple-element.72), channel_id=1, source_target_pairs={{0,4},{4,0},{8,12},{12,8},{16,20},{20,16},{24,28},{28,24},{1,5},{5... | collective-permute-start | bytes 294920 | tf_op jit(solution)/shard_map/ppermute | solution.py:437
  31.9 12.2 %collective-permute-start.20 = (bf16[896,128]{1,0:T(8,128)(2,1)S(1)}, bf16[896,128]{1,0:T(8,128)(2,1)S(1)}, u32[]{:S(2)}, u32[]{:S(2)}) collective-permute-start(bf16[896,128]{1,0:T(8,128)(2,1)S(1)} %get-tuple-element.95), channel_id=1, source_target_pairs={{0,16},{4,20},{8,24},{12,28},{16,0},{20,4},{24,8},{28,12},{1,17},{... | collective-permute-start | bytes 688136 | tf_op jit(solution)/shard_map/ppermute | solution.py:437
  33.0 7.3 %collective-permute-start.11 = (bf16[256,128]{1,0:T(8,128)(2,1)S(1)}, bf16[256,128]{1,0:T(8,128)(2,1)S(1)}, u32[]{:S(2)}, u32[]{:S(2)}) collective-permute-start(bf16[256,128]{1,0:T(8,128)(2,1)S(1)} %get-tuple-element.74), channel_id=1, source_target_pairs={{0,12},{4,8},{8,4},{12,0},{16,28},{20,24},{24,20},{28,16},{1,13},{... | collective-permute-start | bytes 196616 | tf_op jit(solution)/shard_map/ppermute | solution.py:437
  35.7 4.9 %collective-permute-start.12 = (bf16[256,128]{1,0:T(8,128)(2,1)S(1)}, bf16[256,128]{1,0:T(8,128)(2,1)S(1)}, u32[]{:S(2)}, u32[]{:S(2)}) collective-permute-start(bf16[256,128]{1,0:T(8,128)(2,1)S(1)} %get-tuple-element.75), channel_id=1, source_target_pairs={{0,8},{4,12},{8,0},{12,4},{16,24},{20,28},{24,16},{28,20},{1,9},{5... | collective-permute-start | bytes 196616 | tf_op jit(solution)/shard_map/ppermute | solution.py:437
  35.7 4.9 %collective-permute-start.13 = (bf16[256,128]{1,0:T(8,128)(2,1)S(1)}, bf16[256,128]{1,0:T(8,128)(2,1)S(1)}, u32[]{:S(2)}, u32[]{:S(2)}) collective-permute-start(bf16[256,128]{1,0:T(8,128)(2,1)S(1)} %get-tuple-element.76), channel_id=1, source_target_pairs={{0,4},{4,0},{8,12},{12,8},{16,20},{20,16},{24,28},{28,24},{1,5},{5... | collective-permute-start | bytes 196616 | tf_op jit(solution)/shard_map/ppermute | solution.py:437
  41.5 4.2 %collective-permute-start.14 = (bf16[32,2048]{1,0:T(8,128)(2,1)S(1)}, bf16[32,2048]{1,0:T(8,128)(2,1)S(1)}, u32[]{:S(2)}, u32[]{:S(2)}) collective-permute-start(bf16[32,2048]{1,0:T(8,128)(2,1)S(1)} %get-tuple-element.87), channel_id=1, source_target_pairs={{0,1},{1,0},{2,3},{3,2},{4,5},{5,4},{6,7},{7,6},{8,9},{9,8},{10,11... | collective-permute-start | bytes 393224 | tf_op jit(solution)/shard_map/ppermute | solution.py:437
  41.6 5.2 %collective-permute-start.15 = (bf16[32,2048]{1,0:T(8,128)(2,1)S(1)}, bf16[32,2048]{1,0:T(8,128)(2,1)S(1)}, u32[]{:S(2)}, u32[]{:S(2)}) collective-permute-start(bf16[32,2048]{1,0:T(8,128)(2,1)S(1)} %get-tuple-element.88), channel_id=1, source_target_pairs={{0,1},{1,0},{2,3},{3,2},{4,5},{5,4},{6,7},{7,6},{8,9},{9,8},{10,11... | collective-permute-start | bytes 393224 | tf_op jit(solution)/shard_map/ppermute | solution.py:437
  42.1 6.0 %collective-permute-start.16 = (bf16[32,2048]{1,0:T(8,128)(2,1)S(1)}, bf16[32,2048]{1,0:T(8,128)(2,1)S(1)}, u32[]{:S(2)}, u32[]{:S(2)}) collective-permute-start(bf16[32,2048]{1,0:T(8,128)(2,1)S(1)} %get-tuple-element.89), channel_id=1, source_target_pairs={{0,1},{1,0},{2,3},{3,2},{4,5},{5,4},{6,7},{7,6},{8,9},{9,8},{10,11... | collective-permute-start | bytes 393224 | tf_op jit(solution)/shard_map/ppermute | solution.py:437
  42.1 5.9 %collective-permute-start.17 = (bf16[32,2048]{1,0:T(8,128)(2,1)S(1)}, bf16[32,2048]{1,0:T(8,128)(2,1)S(1)}, u32[]{:S(2)}, u32[]{:S(2)}) collective-permute-start(bf16[32,2048]{1,0:T(8,128)(2,1)S(1)} %get-tuple-element.90), channel_id=1, source_target_pairs={{0,1},{1,0},{2,3},{3,2},{4,5},{5,4},{6,7},{7,6},{8,9},{9,8},{10,11... | collective-permute-start | bytes 393224 | tf_op jit(solution)/shard_map/ppermute | solution.py:437
  44.5 10.3 %collective-permute-start.21 = (bf16[3,256,128]{2,1,0:T(8,128)(2,1)S(1)}, bf16[3,256,128]{2,1,0:T(8,128)(2,1)S(1)}, u32[]{:S(2)}, u32[]{:S(2)}) collective-permute-start(bf16[3,256,128]{2,1,0:T(8,128)(2,1)S(1)} %get-tuple-element.97), channel_id=1, source_target_pairs={{0,12},{4,8},{8,4},{12,0},{16,28},{20,24},{24,20},{28,16},{1,13},{... | collective-permute-start | bytes 589832 | tf_op jit(solution)/shard_map/ppermute | solution.py:437
  45.7 10.0 %collective-permute-start.22 = (bf16[3,256,128]{2,1,0:T(8,128)(2,1)S(1)}, bf16[3,256,128]{2,1,0:T(8,128)(2,1)S(1)}, u32[]{:S(2)}, u32[]{:S(2)}) collective-permute-start(bf16[3,256,128]{2,1,0:T(8,128)(2,1)S(1)} %get-tuple-element.98), channel_id=1, source_target_pairs={{0,8},{4,12},{8,0},{12,4},{16,24},{20,28},{24,16},{28,20},{1,9},{5... | collective-permute-start | bytes 589832 | tf_op jit(solution)/shard_map/ppermute | solution.py:437
  46.8 8.9 %collective-permute-start.23 = (bf16[3,256,128]{2,1,0:T(8,128)(2,1)S(1)}, bf16[3,256,128]{2,1,0:T(8,128)(2,1)S(1)}, u32[]{:S(2)}, u32[]{:S(2)}) collective-permute-start(bf16[3,256,128]{2,1,0:T(8,128)(2,1)S(1)} %get-tuple-element.99), channel_id=1, source_target_pairs={{0,4},{4,0},{8,12},{12,8},{16,20},{20,16},{24,28},{28,24},{1,5},{5... | collective-permute-start | bytes 589832 | tf_op jit(solution)/shard_map/ppermute | solution.py:437
  48.2 5.2 %collective-permute-start.18 = (bf16[32,2048]{1,0:T(8,128)(2,1)S(1)}, bf16[32,2048]{1,0:T(8,128)(2,1)S(1)}, u32[]{:S(2)}, u32[]{:S(2)}) collective-permute-start(bf16[32,2048]{1,0:T(8,128)(2,1)S(1)} %get-tuple-element.92), channel_id=1, source_target_pairs={{0,2},{1,3},{2,0},{3,1},{4,6},{5,7},{6,4},{7,5},{8,10},{9,11},{10,... | collective-permute-start | bytes 393224 | tf_op jit(solution)/shard_map/ppermute | solution.py:437
  48.8 6.0 %collective-permute-start.19 = (bf16[32,2048]{1,0:T(8,128)(2,1)S(1)}, bf16[32,2048]{1,0:T(8,128)(2,1)S(1)}, u32[]{:S(2)}, u32[]{:S(2)}) collective-permute-start(bf16[32,2048]{1,0:T(8,128)(2,1)S(1)} %get-tuple-element.93), channel_id=1, source_target_pairs={{0,2},{1,3},{2,0},{3,1},{4,6},{5,7},{6,4},{7,5},{8,10},{9,11},{10,... | collective-permute-start | bytes 393224 | tf_op jit(solution)/shard_map/ppermute | solution.py:437
  (2 other events, 2.5 us)

commit v19 on v18

--- a/solution.py
+++ b/solution.py
@@ -127,10 +127,12 @@
             out[me ^ step, part] = dot(pool[: half // 2, :half], once).astype(BF16)
 
 
-def copy_kernel(*refs):
-    count = len(refs) // 2
-    for x, out in zip(refs[:count], refs[count:]):
-        out[...] = x[...]
+def copy_kernel(out_grad, weight, low, high, out_grad_out, weight_out, far):
+    out_grad_out[...] = out_grad[...]
+    weight_out[...] = weight[...]
+    half = low.shape[0]
+    far[:half] = low[...]
+    far[half:] = high[...]
 
 
 def gather_kernel(nb, *refs):
@@ -490,12 +492,15 @@
         copied=GROUP,
         limit=53,
     )
-    far = swapped(out_grad, "mp", 2)
+    half = out_grad.shape[0] // 2
+    far = [swapped(piece, "mp", 2) for piece in (out_grad[:half], out_grad[half:])]
     (tops,) = call(pool_kernel, [shape(GROUP, 2, quarter, HEAD_DIM)], chunks)
     chunks = exchanged(chunks)
     tops = swapped(tops, "seq", GROUP)
-    arrays = (out_grad, far, out_weight)
-    own_grad, far, out_weight = call(copy_kernel, [shape(*x.shape) for x in arrays], arrays)
+    arrays = (out_grad, out_weight, *far)
+    own_grad, out_weight, far = call(
+        copy_kernel, [shape(*x.shape) for x in (out_grad, out_weight, out_grad)], arrays
+    )
     rim_blocks = beside(call(functools.partial(rim_kernel, groups), rims, chunks, flops=20 * score_flops))
     near, queries, level_1 = call(
         functools.partial(gather_kernel, nb),

time: 57.1 us -> 60.6 us (1.061)
  starting transfers between devices: 27.2 us -> 30.3 us
  waiting for transfers between devices: 12.7 us -> 13.5 us
    ppermute x24 -> x25, starting transfers between devices: 27.2 us -> 30.3 us  [swapped(): lax.ppermute(x, axis, [(i, i ^ step) for i in range(lax.axis_size(axis))])]
    unnamed x4, local copies, waits for them, and re-layouts: 2.54 us -> 0.96 us
    slice x0 -> x1, local copies, waits for them, and re-layouts: none -> 0.98 us  [per_device(): out_grad[half:]]
    ppermute x24 -> x25, waiting for transfers between devices: 12.7 us -> 13.5 us  [swapped(): lax.ppermute(x, axis, [(i, i ^ step) for i in range(lax.axis_size(axis))])]
  transfers between devices with their start and end apart: 24 -> 25, of which waited for: 8 -> 8; matrix products, arithmetic and copies ran while one was open for 0% -> 2% of each run, Pallas kernels for 18% -> 15%
where the time goes in v19:
time: 60.6 us; the launch traced here: 60.4 us
  starting transfers between devices  30.3 us (50%)
  Pallas kernels  13.8 us (23%)
  waiting for transfers between devices  13.5 us (22%)
  local copies, waits for them, and re-layouts  1.94 us (3%)
  between operations  0.77 us (1%)
    ppermute x25, starting transfers between devices, swapped(): lax.ppermute(x, axis, [(i, i ^ step) for i in range(lax.axis_size(axis))])  30.3 us
    pallas_call x13, Pallas kernels, call(): pl.pallas_call(kernel, out_shape=out_shape, in_specs=[kept if copied else...  13.8 us
    ppermute x25, waiting for transfers between devices, swapped(): lax.ppermute(x, axis, [(i, i ^ step) for i in range(lax.axis_size(axis))])  13.5 us
  transfers between devices with their start and end apart: 25, of which 8 were waited for; matrix products, arithmetic and copies ran while one was open for 2% of the time, Pallas kernels for 15%

profile of v19, /device:TPU:0, one launch (start us, length us, event | category | flops | bytes accessed | tf_op | source)
XLA Modules:
  0.0 60.4 jit_solution(7050658221120195181)
XLA Ops:
  0.6 1.4 %shard_map.84 = (bf16[3,256,128]{2,1,0:T(8,128)(2,1)S(1)}, bf16[3,256,128]{2,1,0:T(8,128)(2,1)S(1)}, bf16[3,256,128]{2,1,0:T(8,128)(2,1)S(1)}, bf16[3,256,128]{2,1,0:T(8,128)(2,1)S(1)}) custom-call(bf16[256,512]{1,0:T(8,128)(2,1)} %q.1, bf16[256,512]{1,0:T(8,128)(2,1)} %k.1, bf16[256,512]{1,0:T(8,128)(2,1)} %v.1), custom_call_target="tpu_custom_call" | custom-call | tf_op jit(solution)/shard_map/pallas_call | solution.py:39
  2.1 4.0 %collective-permute-start = (bf16[3,256,128]{2,1,0:T(8,128)(2,1)S(1)}, bf16[3,256,128]{2,1,0:T(8,128)(2,1)S(1)}, u32[]{:S(2)}, u32[]{:S(2)}) collective-permute-start(bf16[3,256,128]{2,1,0:T(8,128)(2,1)S(1)} %get-tuple-element.55.refs_1_), channel_id=1, source_target_pairs={{0,12},{4,8},{8,4},{12,0},{16,28},{20,24},{24,20},{28,16},{1,13},{... | collective-permute-start | bytes 589832 | tf_op jit(solution)/shard_map/ppermute | solution.py:439
  6.8 1.0 %fusion = (bf16[32,2048]{1,0:T(8,128)(2,1)S(1)}, bf16[32,2048]{1,0:T(8,128)(2,1)S(1)}) fusion(bf16[64,2048]{1,0:T(8,128)(2,1)} %out_grad.1), kind=kLoop, calls=%fused_computation | loop fusion | bytes 524288 | tf_op jit(solution)/shard_map/slice | solution.py:496
  7.8 1.9 %collective-permute-start.4 = (bf16[32,2048]{1,0:T(8,128)(2,1)S(1)}, bf16[32,2048]{1,0:T(8,128)(2,1)S(1)}, u32[]{:S(2)}, u32[]{:S(2)}) collective-permute-start(bf16[32,2048]{1,0:T(8,128)(2,1)S(1)} %get-tuple-element.104), channel_id=1, source_target_pairs={{0,2},{1,3},{2,0},{3,1},{4,6},{5,7},{6,4},{7,5},{8,10},{9,11},{10,... | collective-permute-start | bytes 393224 | tf_op jit(solution)/shard_map/ppermute | solution.py:439
  9.9 1.4 %shard_map.87 = bf16[4,2,64,128]{3,2,1,0:T(8,128)(2,1)S(1)} custom-call(bf16[3,256,128]{2,1,0:T(8,128)(2,1)S(1)} %get-tuple-element.54.refs_0_, bf16[3,256,128]{2,1,0:T(8,128)(2,1)S(1)} %get-tuple-element.55.refs_1_, bf16[3,256,128]{2,1,0:T(8,128)(2,1)S(1)} %get-tuple-element.56.refs_2_, bf16[3,256,128]{2,1,0:T(8,128)(2,1)S(1)} %get-tuple-element.57.refs_3_), custom_call_target="tpu_custom_call" | custom-call | tf_op jit(solution)/shard_map/pallas_call | solution.py:39
  11.3 2.6 %collective-permute-done.4.high = bf16[32,2048]{1,0:T(8,128)(2,1)S(1)} collective-permute-done((bf16[32,2048]{1,0:T(8,128)(2,1)S(1)}, bf16[32,2048]{1,0:T(8,128)(2,1)S(1)}, u32[]{:S(2)}, u32[]{:S(2)}) %collective-permute-start.4) | collective-permute-done | bytes 131104 | tf_op jit(solution)/shard_map/ppermute | solution.py:439
  13.9 2.6 %collective-permute-start.7 = (bf16[4,2,64,128]{3,2,1,0:T(8,128)(2,1)S(1)}, bf16[4,2,64,128]{3,2,1,0:T(8,128)(2,1)S(1)}, u32[]{:S(2)}, u32[]{:S(2)}) collective-permute-start(bf16[4,2,64,128]{3,2,1,0:T(8,128)(2,1)S(1)} %shard_map.87), channel_id=1, source_target_pairs={{0,16},{4,20},{8,24},{12,28},{16,0},{20,4},{24,8},{28,12},{1,17},{... | collective-permute-start | bytes 393224 | tf_op jit(solution)/shard_map/ppermute | solution.py:439
  16.5 0.9 %copy-done.1 = bf16[64,2048]{1,0:T(8,128)(2,1)S(1)} copy-done((bf16[64,2048]{1,0:T(8,128)(2,1)S(1)}, bf16[64,2048]{1,0:T(8,128)(2,1)}, u32[]{:S(2)}) %copy-start.1) | copy-done | bytes 262168
  18.3 1.5 %collective-permute-start.8 = (bf16[2,256,128]{2,1,0:T(8,128)(2,1)S(1)}, bf16[2,256,128]{2,1,0:T(8,128)(2,1)S(1)}, u32[]{:S(2)}, u32[]{:S(2)}) collective-permute-start(bf16[2,256,128]{2,1,0:T(8,128)(2,1)S(1)} %shard_map.90), channel_id=1, source_target_pairs={{0,16},{4,20},{8,24},{12,28},{16,0},{20,4},{24,8},{28,12},{1,17},{... | collective-permute-start | bytes 393224 | tf_op jit(solution)/shard_map/ppermute | solution.py:439
  19.7 1.8 %collective-permute-done.7.refs_5_ = bf16[4,2,64,128]{3,2,1,0:T(8,128)(2,1)S(1)} collective-permute-done((bf16[4,2,64,128]{3,2,1,0:T(8,128)(2,1)S(1)}, bf16[4,2,64,128]{3,2,1,0:T(8,128)(2,1)S(1)}, u32[]{:S(2)}, u32[]{:S(2)}) %collective-permute-start.7) | collective-permute-done | bytes 131104 | tf_op jit(solution)/shard_map/ppermute | solution.py:439
  22.4 4.3 %collective-permute-start.9 = (bf16[384,128]{1,0:T(8,128)(2,1)S(1)}, bf16[384,128]{1,0:T(8,128)(2,1)S(1)}, u32[]{:S(2)}, u32[]{:S(2)}) collective-permute-start(bf16[384,128]{1,0:T(8,128)(2,1)S(1)} %get-tuple-element.70), channel_id=1, source_target_pairs={{0,12},{4,8},{8,4},{12,0},{16,28},{20,24},{24,20},{28,16},{1,13},{... | collective-permute-start | bytes 294920 | tf_op jit(solution)/shard_map/ppermute | solution.py:439
  27.8 1.7 %shard_map.89 = (bf16[3,4,256,128]{3,2,1,0:T(8,128)(2,1)S(1)}, bf16[128,1024]{1,0:T(8,128)(2,1)S(1)}, bf16[128,1024]{1,0:T(8,128)(2,1)S(1)}, bf16[128,512]{1,0:T...) custom-call(bf16[4,2,256,128]{3,2,1,0:T(8,128)(2,1)S(1)} %get-tuple-element.58, ...), custom_call_target="tpu_custom_call" | custom-call | flops 335544320 | bytes 6946816 | tf_op jit(solution)/shard_map/pallas_call | solution.py:39
  29.5 1.8 %collective-permute-done.10.refs_8_ = bf16[384,128]{1,0:T(8,128)(2,1)S(1)} collective-permute-done((bf16[384,128]{1,0:T(8,128)(2,1)S(1)}, bf16[384,128]{1,0:T(8,128)(2,1)S(1)}, u32[]{:S(2)}, u32[]{:S(2)}) %collective-permute-start.10) | collective-permute-done | bytes 98336 | tf_op jit(solution)/shard_map/ppermute | solution.py:439
  31.4 2.2 %shard_map.91 = (bf16[4,4,256,256]{3,2,1,0:T(8,128)(2,1)S(1)}, bf16[4,256,128]{2,1,0:T(8,128)(2,1)S(1)}, bf16[2,256,128]{2,1,0:T(8,128)(2,1)S(1)}, f32[8,1024]{1...) custom-call(bf16[3,4,256,128]{3,2,1,0:T(8,128)(2,1)S(1)} %get-tuple-, ...), custom_call_target="tpu_custom_call" | custom-call | flops 335544320 | bytes 9601024 | tf_op jit(solution)/shard_map/pallas_call | solution.py:39
  33.6 3.7 %collective-permute-start.21 = (bf16[896,128]{1,0:T(8,128)(2,1)S(1)}, bf16[896,128]{1,0:T(8,128)(2,1)S(1)}, u32[]{:S(2)}, u32[]{:S(2)}) collective-permute-start(bf16[896,128]{1,0:T(8,128)(2,1)S(1)} %get-tuple-element.95), channel_id=1, source_target_pairs={{0,16},{4,20},{8,24},{12,28},{16,0},{20,4},{24,8},{28,12},{1,17},{... | collective-permute-start | bytes 688136 | tf_op jit(solution)/shard_map/ppermute | solution.py:439
  37.3 2.0 %collective-permute-start.12 = (bf16[256,128]{1,0:T(8,128)(2,1)S(1)}, bf16[256,128]{1,0:T(8,128)(2,1)S(1)}, u32[]{:S(2)}, u32[]{:S(2)}) collective-permute-start(bf16[256,128]{1,0:T(8,128)(2,1)S(1)} %get-tuple-element.74), channel_id=1, source_target_pairs={{0,12},{4,8},{8,4},{12,0},{16,28},{20,24},{24,20},{28,16},{1,13},{... | collective-permute-start | bytes 196616 | tf_op jit(solution)/shard_map/ppermute | solution.py:439
  39.4 1.4 %collective-permute-start.14 = (bf16[256,128]{1,0:T(8,128)(2,1)S(1)}, bf16[256,128]{1,0:T(8,128)(2,1)S(1)}, u32[]{:S(2)}, u32[]{:S(2)}) collective-permute-start(bf16[256,128]{1,0:T(8,128)(2,1)S(1)} %get-tuple-element.76), channel_id=1, source_target_pairs={{0,4},{4,0},{8,12},{12,8},{16,20},{20,16},{24,28},{28,24},{1,5},{5... | collective-permute-start | bytes 196616 | tf_op jit(solution)/shard_map/ppermute | solution.py:439
  40.8 3.4 %shard_map.92 = (bf16[4,256,128]{2,1,0:T(8,128)(2,1)S(1)}, f32[2,4,256,128]{3,2,1,0:T(8,128)S(1)}) custom-call(bf16[3,4,256,128]{3,2,1,0:T(8,128)(2,1)S(1)} %get-tuple-element.65.refs_0_, bf16[4,2,256,128]{3,2,1,0:T(8,128)(2,1)S(1)} %get-tuple-element.58.near.refs_1_, bf16[2,512,128]{2,1,0:T(8,128)(2,1)S(1)} %get-tuple-element.60.level_1.refs_2_, ...), custom_call_target="tpu_custom_call" | custom-call | tf_op jit(solution)/shard_map/pallas_call | solution.py:39
  47.2 1.6 %collective-permute-start.22 = (bf16[3,256,128]{2,1,0:T(8,128)(2,1)S(1)}, bf16[3,256,128]{2,1,0:T(8,128)(2,1)S(1)}, u32[]{:S(2)}, u32[]{:S(2)}) collective-permute-start(bf16[3,256,128]{2,1,0:T(8,128)(2,1)S(1)} %get-tuple-element.97), channel_id=1, source_target_pairs={{0,12},{4,8},{8,4},{12,0},{16,28},{20,24},{24,20},{28,16},{1,13},{... | collective-permute-start | bytes 589832 | tf_op jit(solution)/shard_map/ppermute | solution.py:439
  48.8 1.9 %collective-permute-start.24 = (bf16[3,256,128]{2,1,0:T(8,128)(2,1)S(1)}, bf16[3,256,128]{2,1,0:T(8,128)(2,1)S(1)}, u32[]{:S(2)}, u32[]{:S(2)}) collective-permute-start(bf16[3,256,128]{2,1,0:T(8,128)(2,1)S(1)} %get-tuple-element.99), channel_id=1, source_target_pairs={{0,4},{4,0},{8,12},{12,8},{16,20},{20,16},{24,28},{28,24},{1,5},{5... | collective-permute-start | bytes 589832 | tf_op jit(solution)/shard_map/ppermute | solution.py:439
  50.9 1.5 %collective-permute-start.19 = (bf16[32,2048]{1,0:T(8,128)(2,1)S(1)}, bf16[32,2048]{1,0:T(8,128)(2,1)S(1)}, u32[]{:S(2)}, u32[]{:S(2)}) collective-permute-start(bf16[32,2048]{1,0:T(8,128)(2,1)S(1)} %get-tuple-element.92), channel_id=1, source_target_pairs={{0,2},{1,3},{2,0},{3,1},{4,6},{5,7},{6,4},{7,5},{8,10},{9,11},{10,... | collective-permute-start | bytes 393224 | tf_op jit(solution)/shard_map/ppermute | solution.py:439
  53.0 4.0 %collective-permute-done.19.refs_1_ = bf16[32,2048]{1,0:T(8,128)(2,1)S(1)} collective-permute-done((bf16[32,2048]{1,0:T(8,128)(2,1)S(1)}, bf16[32,2048]{1,0:T(8,128)(2,1)S(1)}, u32[]{:S(2)}, u32[]{:S(2)}) %collective-permute-start.19) | collective-permute-done | bytes 131104 | tf_op jit(solution)/shard_map/ppermute | solution.py:439
  57.0 1.4 %collective-permute-done.20.refs_2_ = bf16[32,2048]{1,0:T(8,128)(2,1)S(1)} collective-permute-done((bf16[32,2048]{1,0:T(8,128)(2,1)S(1)}, bf16[32,2048]{1,0:T(8,128)(2,1)S(1)}, u32[]{:S(2)}, u32[]{:S(2)}) %collective-permute-start.20) | collective-permute-done | bytes 131104 | tf_op jit(solution)/shard_map/ppermute | solution.py:439
  59.2 1.1 %shard_map.96 = (bf16[256,512]{1,0:T(8,128)(2,1)}, bf16[256,512]{1,0:T(8,128)(2,1)}, bf16[256,512]{1,0:T(8,128)(2,1)}, bf16[64,2048]{1,0:T(8,128)(2,1)}) custom-call(f32[64,2048]{1,0:T(8,128)S(1)} %get-tuple-element.91.refs_0_, bf16[32,2048]{1,0:T(8,128)(2,1)S(1)} %collective-permute-done.19.refs_1_, bf16[32,2048]{1,0:T(8,128)(2,1)S(1)} %collective-permute-done.20.refs_2_, ...), custom_call_target="tpu_custom_call" | custom-call | tf_op jit(solution)/shard_map/pallas_call | solution.py:39
  (44 shorter events, 8.4 us)
Async XLA Ops:
  2.1 15.7 %collective-permute-start = (bf16[3,256,128]{2,1,0:T(8,128)(2,1)S(1)}, bf16[3,256,128]{2,1,0:T(8,128)(2,1)S(1)}, u32[]{:S(2)}, u32[]{:S(2)}) collective-permute-start(bf16[3,256,128]{2,1,0:T(8,128)(2,1)S(1)} %get-tuple-element.55.refs_1_), channel_id=1, source_target_pairs={{0,12},{4,8},{8,4},{12,0},{16,28},{20,24},{24,20},{28,16},{1,13},{... | collective-permute-start | bytes 589832 | tf_op jit(solution)/shard_map/ppermute | solution.py:439
  6.1 12.1 %collective-permute-start.1 = (bf16[3,256,128]{2,1,0:T(8,128)(2,1)S(1)}, bf16[3,256,128]{2,1,0:T(8,128)(2,1)S(1)}, u32[]{:S(2)}, u32[]{:S(2)}) collective-permute-start(bf16[3,256,128]{2,1,0:T(8,128)(2,1)S(1)} %get-tuple-element.56.refs_2_), channel_id=1, source_target_pairs={{0,8},{4,12},{8,0},{12,4},{16,24},{20,28},{24,16},{28,20},{1,9},{5... | collective-permute-start | bytes 589832 | tf_op jit(solution)/shard_map/ppermute | solution.py:439
  6.6 11.7 %collective-permute-start.2 = (bf16[3,256,128]{2,1,0:T(8,128)(2,1)S(1)}, bf16[3,256,128]{2,1,0:T(8,128)(2,1)S(1)}, u32[]{:S(2)}, u32[]{:S(2)}) collective-permute-start(bf16[3,256,128]{2,1,0:T(8,128)(2,1)S(1)} %get-tuple-element.57.refs_3_), channel_id=1, source_target_pairs={{0,4},{4,0},{8,12},{12,8},{16,20},{20,16},{24,28},{28,24},{1,5},{5... | collective-permute-start | bytes 589832 | tf_op jit(solution)/shard_map/ppermute | solution.py:439
  7.8 6.1 %collective-permute-start.4 = (bf16[32,2048]{1,0:T(8,128)(2,1)S(1)}, bf16[32,2048]{1,0:T(8,128)(2,1)S(1)}, u32[]{:S(2)}, u32[]{:S(2)}) collective-permute-start(bf16[32,2048]{1,0:T(8,128)(2,1)S(1)} %get-tuple-element.104), channel_id=1, source_target_pairs={{0,2},{1,3},{2,0},{3,1},{4,6},{5,7},{6,4},{7,5},{8,10},{9,11},{10,... | collective-permute-start | bytes 393224 | tf_op jit(solution)/shard_map/ppermute | solution.py:439
  9.6 6.9 %collective-permute-start.3 = (bf16[32,2048]{1,0:T(8,128)(2,1)S(1)}, bf16[32,2048]{1,0:T(8,128)(2,1)S(1)}, u32[]{:S(2)}, u32[]{:S(2)}) collective-permute-start(bf16[32,2048]{1,0:T(8,128)(2,1)S(1)} %get-tuple-element.105), channel_id=1, source_target_pairs={{0,2},{1,3},{2,0},{3,1},{4,6},{5,7},{6,4},{7,5},{8,10},{9,11},{10,... | collective-permute-start | bytes 393224 | tf_op jit(solution)/shard_map/ppermute | solution.py:439
  13.9 7.7 %collective-permute-start.7 = (bf16[4,2,64,128]{3,2,1,0:T(8,128)(2,1)S(1)}, bf16[4,2,64,128]{3,2,1,0:T(8,128)(2,1)S(1)}, u32[]{:S(2)}, u32[]{:S(2)}) collective-permute-start(bf16[4,2,64,128]{3,2,1,0:T(8,128)(2,1)S(1)} %shard_map.87), channel_id=1, source_target_pairs={{0,16},{4,20},{8,24},{12,28},{16,0},{20,4},{24,8},{28,12},{1,17},{... | collective-permute-start | bytes 393224 | tf_op jit(solution)/shard_map/ppermute | solution.py:439
  17.7 3.9 %collective-permute-start.5 = (bf16[64,2048]{1,0:T(8,128)(2,1)S(1)}, bf16[64,2048]{1,0:T(8,128)(2,1)S(1)}, u32[]{:S(2)}, u32[]{:S(2)}) collective-permute-start(bf16[64,2048]{1,0:T(8,128)(2,1)S(1)} %get-tuple-element.61.refs_0_), channel_id=1, source_target_pairs={{0,1},{1,0},{2,3},{3,2},{4,5},{5,4},{6,7},{7,6},{8,9},{9,8},{10,11... | collective-permute-start | bytes 786440 | tf_op jit(solution)/shard_map/ppermute | solution.py:439
  17.8 3.8 %collective-permute-start.6 = (bf16[64,2048]{1,0:T(8,128)(2,1)S(1)}, bf16[64,2048]{1,0:T(8,128)(2,1)S(1)}, u32[]{:S(2)}, u32[]{:S(2)}) collective-permute-start(bf16[64,2048]{1,0:T(8,128)(2,1)S(1)} %get-tuple-element.62.refs_2_), channel_id=1, source_target_pairs={{0,1},{1,0},{2,3},{3,2},{4,5},{5,4},{6,7},{7,6},{8,9},{9,8},{10,11... | collective-permute-start | bytes 786440 | tf_op jit(solution)/shard_map/ppermute | solution.py:439
  18.3 11.1 %collective-permute-start.8 = (bf16[2,256,128]{2,1,0:T(8,128)(2,1)S(1)}, bf16[2,256,128]{2,1,0:T(8,128)(2,1)S(1)}, u32[]{:S(2)}, u32[]{:S(2)}) collective-permute-start(bf16[2,256,128]{2,1,0:T(8,128)(2,1)S(1)} %shard_map.90), channel_id=1, source_target_pairs={{0,16},{4,20},{8,24},{12,28},{16,0},{20,4},{24,8},{28,12},{1,17},{... | collective-permute-start | bytes 393224 | tf_op jit(solution)/shard_map/ppermute | solution.py:439
  22.4 7.1 %collective-permute-start.9 = (bf16[384,128]{1,0:T(8,128)(2,1)S(1)}, bf16[384,128]{1,0:T(8,128)(2,1)S(1)}, u32[]{:S(2)}, u32[]{:S(2)}) collective-permute-start(bf16[384,128]{1,0:T(8,128)(2,1)S(1)} %get-tuple-element.70), channel_id=1, source_target_pairs={{0,12},{4,8},{8,4},{12,0},{16,28},{20,24},{24,20},{28,16},{1,13},{... | collective-permute-start | bytes 294920 | tf_op jit(solution)/shard_map/ppermute | solution.py:439
  26.8 4.6 %collective-permute-start.10 = (bf16[384,128]{1,0:T(8,128)(2,1)S(1)}, bf16[384,128]{1,0:T(8,128)(2,1)S(1)}, u32[]{:S(2)}, u32[]{:S(2)}) collective-permute-start(bf16[384,128]{1,0:T(8,128)(2,1)S(1)} %get-tuple-element.71), channel_id=1, source_target_pairs={{0,8},{4,12},{8,0},{12,4},{16,24},{20,28},{24,16},{28,20},{1,9},{5... | collective-permute-start | bytes 294920 | tf_op jit(solution)/shard_map/ppermute | solution.py:439
  26.8 4.6 %collective-permute-start.11 = (bf16[384,128]{1,0:T(8,128)(2,1)S(1)}, bf16[384,128]{1,0:T(8,128)(2,1)S(1)}, u32[]{:S(2)}, u32[]{:S(2)}) collective-permute-start(bf16[384,128]{1,0:T(8,128)(2,1)S(1)} %get-tuple-element.72), channel_id=1, source_target_pairs={{0,4},{4,0},{8,12},{12,8},{16,20},{20,16},{24,28},{28,24},{1,5},{5... | collective-permute-start | bytes 294920 | tf_op jit(solution)/shard_map/ppermute | solution.py:439
  33.6 13.3 %collective-permute-start.21 = (bf16[896,128]{1,0:T(8,128)(2,1)S(1)}, bf16[896,128]{1,0:T(8,128)(2,1)S(1)}, u32[]{:S(2)}, u32[]{:S(2)}) collective-permute-start(bf16[896,128]{1,0:T(8,128)(2,1)S(1)} %get-tuple-element.95), channel_id=1, source_target_pairs={{0,16},{4,20},{8,24},{12,28},{16,0},{20,4},{24,8},{28,12},{1,17},{... | collective-permute-start | bytes 688136 | tf_op jit(solution)/shard_map/ppermute | solution.py:439
  37.3 6.8 %collective-permute-start.12 = (bf16[256,128]{1,0:T(8,128)(2,1)S(1)}, bf16[256,128]{1,0:T(8,128)(2,1)S(1)}, u32[]{:S(2)}, u32[]{:S(2)}) collective-permute-start(bf16[256,128]{1,0:T(8,128)(2,1)S(1)} %get-tuple-element.74), channel_id=1, source_target_pairs={{0,12},{4,8},{8,4},{12,0},{16,28},{20,24},{24,20},{28,16},{1,13},{... | collective-permute-start | bytes 196616 | tf_op jit(solution)/shard_map/ppermute | solution.py:439
  39.2 5.7 %collective-permute-start.13 = (bf16[256,128]{1,0:T(8,128)(2,1)S(1)}, bf16[256,128]{1,0:T(8,128)(2,1)S(1)}, u32[]{:S(2)}, u32[]{:S(2)}) collective-permute-start(bf16[256,128]{1,0:T(8,128)(2,1)S(1)} %get-tuple-element.75), channel_id=1, source_target_pairs={{0,8},{4,12},{8,0},{12,4},{16,24},{20,28},{24,16},{28,20},{1,9},{5... | collective-permute-start | bytes 196616 | tf_op jit(solution)/shard_map/ppermute | solution.py:439
  39.4 5.6 %collective-permute-start.14 = (bf16[256,128]{1,0:T(8,128)(2,1)S(1)}, bf16[256,128]{1,0:T(8,128)(2,1)S(1)}, u32[]{:S(2)}, u32[]{:S(2)}) collective-permute-start(bf16[256,128]{1,0:T(8,128)(2,1)S(1)} %get-tuple-element.76), channel_id=1, source_target_pairs={{0,4},{4,0},{8,12},{12,8},{16,20},{20,16},{24,28},{28,24},{1,5},{5... | collective-permute-start | bytes 196616 | tf_op jit(solution)/shard_map/ppermute | solution.py:439
  45.8 3.0 %collective-permute-start.15 = (bf16[32,2048]{1,0:T(8,128)(2,1)S(1)}, bf16[32,2048]{1,0:T(8,128)(2,1)S(1)}, u32[]{:S(2)}, u32[]{:S(2)}) collective-permute-start(bf16[32,2048]{1,0:T(8,128)(2,1)S(1)} %get-tuple-element.87), channel_id=1, source_target_pairs={{0,1},{1,0},{2,3},{3,2},{4,5},{5,4},{6,7},{7,6},{8,9},{9,8},{10,11... | collective-permute-start | bytes 393224 | tf_op jit(solution)/shard_map/ppermute | solution.py:439
  46.3 4.4 %collective-permute-start.17 = (bf16[32,2048]{1,0:T(8,128)(2,1)S(1)}, bf16[32,2048]{1,0:T(8,128)(2,1)S(1)}, u32[]{:S(2)}, u32[]{:S(2)}) collective-permute-start(bf16[32,2048]{1,0:T(8,128)(2,1)S(1)} %get-tuple-element.89), channel_id=1, source_target_pairs={{0,1},{1,0},{2,3},{3,2},{4,5},{5,4},{6,7},{7,6},{8,9},{9,8},{10,11... | collective-permute-start | bytes 393224 | tf_op jit(solution)/shard_map/ppermute | solution.py:439
  46.4 4.3 %collective-permute-start.18 = (bf16[32,2048]{1,0:T(8,128)(2,1)S(1)}, bf16[32,2048]{1,0:T(8,128)(2,1)S(1)}, u32[]{:S(2)}, u32[]{:S(2)}) collective-permute-start(bf16[32,2048]{1,0:T(8,128)(2,1)S(1)} %get-tuple-element.90), channel_id=1, source_target_pairs={{0,1},{1,0},{2,3},{3,2},{4,5},{5,4},{6,7},{7,6},{8,9},{9,8},{10,11... | collective-permute-start | bytes 393224 | tf_op jit(solution)/shard_map/ppermute | solution.py:439
  47.2 11.2 %collective-permute-start.22 = (bf16[3,256,128]{2,1,0:T(8,128)(2,1)S(1)}, bf16[3,256,128]{2,1,0:T(8,128)(2,1)S(1)}, u32[]{:S(2)}, u32[]{:S(2)}) collective-permute-start(bf16[3,256,128]{2,1,0:T(8,128)(2,1)S(1)} %get-tuple-element.97), channel_id=1, source_target_pairs={{0,12},{4,8},{8,4},{12,0},{16,28},{20,24},{24,20},{28,16},{1,13},{... | collective-permute-start | bytes 589832 | tf_op jit(solution)/shard_map/ppermute | solution.py:439
  48.8 9.6 %collective-permute-start.23 = (bf16[3,256,128]{2,1,0:T(8,128)(2,1)S(1)}, bf16[3,256,128]{2,1,0:T(8,128)(2,1)S(1)}, u32[]{:S(2)}, u32[]{:S(2)}) collective-permute-start(bf16[3,256,128]{2,1,0:T(8,128)(2,1)S(1)} %get-tuple-element.98), channel_id=1, source_target_pairs={{0,8},{4,12},{8,0},{12,4},{16,24},{20,28},{24,16},{28,20},{1,9},{5... | collective-permute-start | bytes 589832 | tf_op jit(solution)/shard_map/ppermute | solution.py:439
  48.8 10.4 %collective-permute-start.24 = (bf16[3,256,128]{2,1,0:T(8,128)(2,1)S(1)}, bf16[3,256,128]{2,1,0:T(8,128)(2,1)S(1)}, u32[]{:S(2)}, u32[]{:S(2)}) collective-permute-start(bf16[3,256,128]{2,1,0:T(8,128)(2,1)S(1)} %get-tuple-element.99), channel_id=1, source_target_pairs={{0,4},{4,0},{8,12},{12,8},{16,20},{20,16},{24,28},{28,24},{1,5},{5... | collective-permute-start | bytes 589832 | tf_op jit(solution)/shard_map/ppermute | solution.py:439
  50.9 6.1 %collective-permute-start.19 = (bf16[32,2048]{1,0:T(8,128)(2,1)S(1)}, bf16[32,2048]{1,0:T(8,128)(2,1)S(1)}, u32[]{:S(2)}, u32[]{:S(2)}) collective-permute-start(bf16[32,2048]{1,0:T(8,128)(2,1)S(1)} %get-tuple-element.92), channel_id=1, source_target_pairs={{0,2},{1,3},{2,0},{3,1},{4,6},{5,7},{6,4},{7,5},{8,10},{9,11},{10,... | collective-permute-start | bytes 393224 | tf_op jit(solution)/shard_map/ppermute | solution.py:439
  52.4 6.0 %collective-permute-start.20 = (bf16[32,2048]{1,0:T(8,128)(2,1)S(1)}, bf16[32,2048]{1,0:T(8,128)(2,1)S(1)}, u32[]{:S(2)}, u32[]{:S(2)}) collective-permute-start(bf16[32,2048]{1,0:T(8,128)(2,1)S(1)} %get-tuple-element.93), channel_id=1, source_target_pairs={{0,2},{1,3},{2,0},{3,1},{4,6},{5,7},{6,4},{7,5},{8,10},{9,11},{10,... | collective-permute-start | bytes 393224 | tf_op jit(solution)/shard_map/ppermute | solution.py:439
  (3 other events, 19.9 us)

commit v20 on v19

--- a/solution.py
+++ b/solution.py
@@ -116,17 +116,6 @@
         copy.wait()
 
 
-def pool_kernel(*refs):
-    *chunks, out = refs
-    me = member()
-    pool = pooling()
-    half = BLOCK // 2
-    for step, chunk in zip(STEPS, chunks):
-        for part in range(2):
-            once = dot(pool, chunk[part]).astype(BF16)
-            out[me ^ step, part] = dot(pool[: half // 2, :half], once).astype(BF16)
-
-
 def copy_kernel(out_grad, weight, low, high, out_grad_out, weight_out, far):
     out_grad_out[...] = out_grad[...]
     weight_out[...] = weight[...]
@@ -148,24 +137,38 @@
             level_1[part, b * half : (b + 1) * half] = dot(pool, near[b, part]).astype(BF16)
 
 
-def rim_kernel(groups, *refs):
-    chunks, outs = refs[:GROUP], refs[GROUP:]
-    me = member()
-    members = [GROUP - 1, 0]
-    if groups == 2:
-        members = [jnp.where(lax.axis_index("seq") >= GROUP, 0, GROUP - 1)]
-    for wanted, out in zip(members, outs):
+def pooled_twice(rows):
+    pool = pooling()
+    half = BLOCK // 2
+    once = dot(pool, rows).astype(BF16)
+    return dot(pool[: half // 2, :half], once).astype(BF16)
+
+
+def cross_kernel(groups, *refs):
+    chunks, (top, *outs, levels) = refs[:GROUP], refs[GROUP:]
+    me = member()
+    quarter = BLOCK // 4
+    side_by_side = [chunk[part] for chunk in chunks for part in range(2)]
+    pooled = pooled_twice(jnp.concatenate(side_by_side, axis=1))
+    for i, step in enumerate(STEPS):
+        for part in range(2):
+            at = (2 * i + part) * HEAD_DIM
+            levels[part, span(me ^ step, quarter), :] = pooled[:, at : at + HEAD_DIM]
+    odd = odd_group()
+    for part in range(2):
+        rest = levels[part, pl.ds(pl.multiple_of(odd * quarter, quarter), REST), :]
+        top[part * REST : (part + 1) * REST] = rest
+    members = [(GROUP - 1, outs[0], 0), (0, outs[1], 0)] if groups > 2 else [
+        (jnp.where(odd == 1, 0, GROUP - 1), top, 2 * REST)
+    ]
+    for wanted, out, start in members:
         for step, chunk in zip(STEPS, chunks):
 
             @pl.when(me ^ step == wanted)
             def _():
-                out[...] = chunk[:2]
-
-
-def from_beside(groups, refs):
-    if groups == 2:
-        return (refs[0], refs[0]), refs[1:]
-    return refs[:2], refs[2:]
+                for part in range(2):
+                    at = start + part * BLOCK
+                    out[at : at + BLOCK] = chunk[part]
 
 
 def from_others(groups, refs):
@@ -227,7 +230,7 @@
 
 def forward_kernel(nb, groups, *refs):
     (query, v_t, v1_t, weights, stats), refs = refs[:5], refs[5:]
-    (rim_low, rim_high), refs = from_beside(groups, refs)
+    (got_top, rim_low, rim_high), refs = from_others(groups, refs)
     chunks, refs = refs[:GROUP], refs[GROUP:]
     (prob, grads, top_2, deltas, far_shift, rim_shift), refs = refs[:6], refs[6:]
     outs, (*rim_outs, attended, far_prob, rim_prob, row, context_t, far_sums) = refs[:GROUP], refs[GROUP:]
@@ -236,16 +239,20 @@
     quarter = BLOCK // 4
     tokens = nb * BLOCK
     for step, chunk in zip(STEPS, chunks):
-        grads[me ^ step] = chunk[:BLOCK]
-        for part in range(2):
-            level = chunk[BLOCK + part * quarter : BLOCK + (part + 1) * quarter]
-            top_2[part, span(me ^ step, quarter), :] = level
+        grads[me ^ step] = chunk[...]
+    odd = odd_group()
+    for part in range(2):
+        at = slice(part * BLOCK, (part + 1) * BLOCK)
+        beside_me = jnp.where(odd == 1, rim_low[at], rim_high[at]) if groups > 2 else rim_low[at]
+        rest = pl.ds(pl.multiple_of((1 - odd) * quarter, quarter), REST)
+        top_2[part, rest, :] = got_top[part * REST : (part + 1) * REST]
+        top_2[part, pl.ds(pl.multiple_of(odd * REST, quarter), quarter), :] = pooled_twice(beside_me)
     coarse_query = query[2].reshape(tokens, HEAD_DIM)
     coarse = dot_nt(top_2[0], coarse_query) * (SCALE * LOG2E)
     row[:1] = jnp.maximum(stats[:1], coarse.max(0, keepdims=True))
     scores = []
     for b, block, present in rims:
-        score = dot_nt(block[0], query[0, b]) * (SCALE * LOG2E)
+        score = dot_nt(block[:BLOCK], query[0, b]) * (SCALE * LOG2E)
         if present is not None:
             score = jnp.where(present, score, -jnp.inf)
         at = span(b, BLOCK)
@@ -268,7 +275,7 @@
     for i, (b, block, _) in enumerate(rims):
         at = span(b, BLOCK)
         rim_prob[i] = (fresh[i] * row[2:3, at]).astype(BF16)
-        context_t[:, at] += dot(block[1].T, rim_prob[i])
+        context_t[:, at] += dot(block[BLOCK:].T, rim_prob[i])
     for b in range(nb):
         shrink = row[3:4, at_block(b)]
         prob[b, 3] = (weights[b, 3] * shrink).astype(BF16)
@@ -284,7 +291,6 @@
     far_shift[...] = (far_prob[...].astype(F32) * (slope - deltas[:1])).astype(BF16)
     far_sums[0] = SCALE * dot(far_shift[...], coarse_query)
     far_sums[1] = dot(far_prob[...], grad)
-    odd = odd_group()
     spread = spreading(2)
     folded = []
     for part in range(2):
@@ -294,7 +300,7 @@
         folded.append(dot(spread, high) + dot(spread, low))
     pairs = []
     for i, (b, block, _) in enumerate(rims):
-        slope = dot_nt(block[1], grads[b])
+        slope = dot_nt(block[BLOCK:], grads[b])
         rim_shift[i] = (rim_prob[i].astype(F32) * (slope - deltas[:1, span(b, BLOCK)])).astype(BF16)
         pairs.append((SCALE * dot(rim_shift[i], query[0, b]), dot(rim_prob[i], grads[b])))
     for part in range(2):
@@ -312,7 +318,7 @@
 
 def backward_kernel(nb, groups, *refs):
     (query, near, level_1, k_t, k1_t, prob, grads, top_2, deltas, far_shift, rim_shift), refs = refs[:11], refs[11:]
-    (rim_low, rim_high), refs = from_beside(groups, refs)
+    (_, rim_low, rim_high), refs = from_others(groups, refs)
     grad_q, grad_kv, shift, sums_1, query_t = refs
     even_1, even_2 = averaging(1), averaging(2)
     coarse = dot(top_2[0].T, far_shift[...])
@@ -320,7 +326,7 @@
         high, low = halves(coarse[:, at_block(b)])
         query_t[:, at_block(b)] = dot(high, even_2) + dot(low, even_2)
     for i, (b, block, _) in enumerate(rims_of(nb, groups, rim_low, rim_high)):
-        query_t[:, span(b, BLOCK)] += dot(block[0].T, rim_shift[i])
+        query_t[:, span(b, BLOCK)] += dot(block[:BLOCK].T, rim_shift[i])
     for b in range(nb):
         grad, delta = grads[b], deltas[:1, at_block(b)]
         grad_t = query_t[:, at_block(b)]
@@ -407,17 +413,14 @@
 
 
 def grad_kernel(*refs):
-    pieces, (out_weight, tops), refs = refs[:N_MP], refs[N_MP : N_MP + 2], refs[N_MP + 2 :]
+    pieces, out_weight, refs = refs[:N_MP], refs[N_MP], refs[N_MP + 1 :]
     *outs, whole, heads = refs
     me = member()
     for step, piece in enumerate(pieces):
         whole[span(share() ^ step, piece.shape[0]), :] = piece[...]
     heads[...] = dot_nt(whole[...], out_weight[...]).astype(BF16)
-    quarter = tops.shape[2]
     for step, out in zip(STEPS, outs):
-        out[:BLOCK] = heads[:, columns(me ^ step)]
-        for part in range(2):
-            out[BLOCK + part * quarter : BLOCK + (part + 1) * quarter] = tops[me ^ step, part]
+        out[...] = heads[:, columns(me ^ step)]
 
 
 def project_kernel(*refs):
@@ -441,15 +444,6 @@
 
 def exchanged(chunks):
     return [chunks[0]] + [swapped(chunk, "seq", step) for step, chunk in zip(STEPS[1:], chunks[1:])]
-
-
-def beside(arrays):
-    count = lax.axis_size("seq")
-    if len(arrays) == 1:
-        return [swapped(arrays[0], "seq", GROUP)]
-    up = [(i, i + GROUP) for i in range(count - GROUP)]
-    down = [(j, i) for i, j in up]
-    return [lax.ppermute(arrays[0], "seq", up), lax.ppermute(arrays[1], "seq", down)]
 
 
 def crossed(arrays):
@@ -494,14 +488,19 @@
     )
     half = out_grad.shape[0] // 2
     far = [swapped(piece, "mp", 2) for piece in (out_grad[:half], out_grad[half:])]
-    (tops,) = call(pool_kernel, [shape(GROUP, 2, quarter, HEAD_DIM)], chunks)
     chunks = exchanged(chunks)
-    tops = swapped(tops, "seq", GROUP)
     arrays = (out_grad, out_weight, *far)
     own_grad, out_weight, far = call(
         copy_kernel, [shape(*x.shape) for x in (out_grad, out_weight, out_grad)], arrays
     )
-    rim_blocks = beside(call(functools.partial(rim_kernel, groups), rims, chunks, flops=20 * score_flops))
+    refs = call(
+        functools.partial(cross_kernel, groups),
+        sent,
+        chunks,
+        scratch=[pltpu.VMEM((2, rows, HEAD_DIM), BF16)],
+        flops=20 * score_flops,
+    )
+    rim_blocks = crossed(refs)
     near, queries, level_1 = call(
         functools.partial(gather_kernel, nb),
         [
@@ -513,8 +512,8 @@
     )
     grad_chunks = call(
         grad_kernel,
-        [shape(rows + 2 * quarter, HEAD_DIM)] * GROUP,
-        (own_grad, swapped(own_grad, "mp", 1), far, swapped(far, "mp", 1), out_weight, tops),
+        [chunk] * GROUP,
+        (own_grad, swapped(own_grad, "mp", 1), far, swapped(far, "mp", 1), out_weight),
         scratch=[pltpu.VMEM((rows, model), BF16), pltpu.VMEM((rows, width), BF16)],
         flops=weight_flops,
     )

time: 60.6 us -> 60.8 us (level)
  starting transfers between devices: 30.3 us -> 25.5 us
  waiting for transfers between devices: 13.5 us -> 17.4 us
  local copies, waits for them, and re-layouts: 1.94 us -> 3.53 us
  Pallas kernels: 13.8 us -> 13.1 us
    ppermute x25 -> x24, starting transfers between devices: 30.3 us -> 25.5 us  [swapped(): lax.ppermute(x, axis, [(i, i ^ step) for i in range(lax.axis_size(axis))])]
    ppermute x25 -> x24, waiting for transfers between devices: 13.5 us -> 17.4 us  [swapped(): lax.ppermute(x, axis, [(i, i ^ step) for i in range(lax.axis_size(axis))])]
    unnamed x4, local copies, waits for them, and re-layouts: 0.96 us -> 2.54 us
    pallas_call x13 -> x12, Pallas kernels: 13.8 us -> 13.1 us  [call(): pl.pallas_call(kernel, out_shape=out_shape, in_specs=[kept if copied else...]
  transfers between devices with their start and end apart: 25 -> 24, of which waited for: 8 -> 10; matrix products, arithmetic and copies ran while one was open for 2% -> 2% of each run, Pallas kernels for 15% -> 13%
where the time goes in v20:
time: 60.8 us; the launch traced here: 60.2 us
  starting transfers between devices  25.5 us (42%)
  waiting for transfers between devices  17.4 us (29%)
  Pallas kernels  13.1 us (22%)
  local copies, waits for them, and re-layouts  3.53 us (6%)
  between operations  0.76 us (1%)
    ppermute x24, starting transfers between devices, swapped(): lax.ppermute(x, axis, [(i, i ^ step) for i in range(lax.axis_size(axis))])  25.5 us
    ppermute x24, waiting for transfers between devices, swapped(): lax.ppermute(x, axis, [(i, i ^ step) for i in range(lax.axis_size(axis))])  17.4 us
    pallas_call x12, Pallas kernels, call(): pl.pallas_call(kernel, out_shape=out_shape, in_specs=[kept if copied else...  13.1 us
    unnamed x4, local copies, waits for them, and re-layouts  2.54 us
  transfers between devices with their start and end apart: 24, of which 10 were waited for; matrix products, arithmetic and copies ran while one was open for 2% of the time, Pallas kernels for 13%

profile of v20, /device:TPU:0, one launch (start us, length us, event | category | flops | bytes accessed | tf_op | source)
XLA Modules:
  0.0 60.2 jit_solution(3553358587626861909)
XLA Ops:
  0.6 1.3 %shard_map.84 = (bf16[3,256,128]{2,1,0:T(8,128)(2,1)S(1)}, bf16[3,256,128]{2,1,0:T(8,128)(2,1)S(1)}, bf16[3,256,128]{2,1,0:T(8,128)(2,1)S(1)}, bf16[3,256,128]{2,1,0:T(8,128)(2,1)S(1)}) custom-call(bf16[256,512]{1,0:T(8,128)(2,1)} %q.1, bf16[256,512]{1,0:T(8,128)(2,1)} %k.1, bf16[256,512]{1,0:T(8,128)(2,1)} %v.1), custom_call_target="tpu_custom_call" | custom-call | tf_op jit(solution)/shard_map/pallas_call | solution.py:39
  1.9 4.0 %collective-permute-start = (bf16[3,256,128]{2,1,0:T(8,128)(2,1)S(1)}, bf16[3,256,128]{2,1,0:T(8,128)(2,1)S(1)}, u32[]{:S(2)}, u32[]{:S(2)}) collective-permute-start(bf16[3,256,128]{2,1,0:T(8,128)(2,1)S(1)} %get-tuple-element.55), channel_id=1, source_target_pairs={{0,12},{4,8},{8,4},{12,0},{16,28},{20,24},{24,20},{28,16},{1,13},{... | collective-permute-start | bytes 589832 | tf_op jit(solution)/shard_map/ppermute | solution.py:442
  6.6 1.0 %fusion = (bf16[32,2048]{1,0:T(8,128)(2,1)S(1)}, bf16[32,2048]{1,0:T(8,128)(2,1)S(1)}) fusion(bf16[64,2048]{1,0:T(8,128)(2,1)} %out_grad.1), kind=kLoop, calls=%fused_computation | loop fusion | bytes 524288 | tf_op jit(solution)/shard_map/slice | solution.py:490
  7.6 1.9 %collective-permute-start.4 = (bf16[32,2048]{1,0:T(8,128)(2,1)S(1)}, bf16[32,2048]{1,0:T(8,128)(2,1)S(1)}, u32[]{:S(2)}, u32[]{:S(2)}) collective-permute-start(bf16[32,2048]{1,0:T(8,128)(2,1)S(1)} %get-tuple-element.104), channel_id=1, source_target_pairs={{0,2},{1,3},{2,0},{3,1},{4,6},{5,7},{6,4},{7,5},{8,10},{9,11},{10,... | collective-permute-start | bytes 393224 | tf_op jit(solution)/shard_map/ppermute | solution.py:442
  9.7 4.1 %collective-permute-done.4.high = bf16[32,2048]{1,0:T(8,128)(2,1)S(1)} collective-permute-done((bf16[32,2048]{1,0:T(8,128)(2,1)S(1)}, bf16[32,2048]{1,0:T(8,128)(2,1)S(1)}, u32[]{:S(2)}, u32[]{:S(2)}) %collective-permute-start.4) | collective-permute-done | bytes 131104 | tf_op jit(solution)/shard_map/ppermute | solution.py:442
  13.8 1.4 %collective-permute-done.3.low = bf16[32,2048]{1,0:T(8,128)(2,1)S(1)} collective-permute-done((bf16[32,2048]{1,0:T(8,128)(2,1)S(1)}, bf16[32,2048]{1,0:T(8,128)(2,1)S(1)}, u32[]{:S(2)}, u32[]{:S(2)}) %collective-permute-start.3) | collective-permute-done | bytes 131104 | tf_op jit(solution)/shard_map/ppermute | solution.py:442
  15.2 1.6 %copy-done = bf16[512,2048]{1,0:T(8,128)(2,1)S(1)} copy-done((bf16[512,2048]{1,0:T(8,128)(2,1)S(1)}, bf16[512,2048]{1,0:T(8,128)(2,1)}, u32[]{:S(2)}) %copy-start) | copy-done | bytes 2097176
  16.8 0.9 %copy-done.1 = bf16[64,2048]{1,0:T(8,128)(2,1)S(1)} copy-done((bf16[64,2048]{1,0:T(8,128)(2,1)S(1)}, bf16[64,2048]{1,0:T(8,128)(2,1)}, u32[]{:S(2)}) %copy-start.1) | copy-done | bytes 262168
  18.9 2.7 %collective-permute-start.7 = (bf16[896,128]{1,0:T(8,128)(2,1)S(1)}, bf16[896,128]{1,0:T(8,128)(2,1)S(1)}, u32[]{:S(2)}, u32[]{:S(2)}) collective-permute-start(bf16[896,128]{1,0:T(8,128)(2,1)S(1)} %shard_map.89), channel_id=1, source_target_pairs={{0,16},{4,20},{8,24},{12,28},{16,0},{20,4},{24,8},{28,12},{1,17},{... | collective-permute-start | bytes 688136 | tf_op jit(solution)/shard_map/ppermute | solution.py:442
  21.6 0.8 %shard_map.87 = (bf16[256,128]{1,0:T(8,128)(2,1)S(1)}, bf16[256,128]{1,0:T(8,128)(2,1)S(1)}, bf16[256,128]{1,0:T(8,128)(2,1)S(1)}, bf16[256,128]{1,0:T(8,128)(2,1)S(1)}) custom-call(bf16[64,2048]{1,0:T(8,128)(2,1)S(1)} %get-tuple-element.61.refs_0_, bf16[64,2048]{1,0:T(8,128)(2,1)S(1)} %collective-permute-done.5.refs_1_, ...), custom_call_target="tpu_custom_call" | custom-call | flops 536870912 | bytes 3407872 | tf_op jit(solution)/shard_map/pallas_call | solution.py:39
  22.4 2.6 %collective-permute-start.8 = (bf16[256,128]{1,0:T(8,128)(2,1)S(1)}, bf16[256,128]{1,0:T(8,128)(2,1)S(1)}, u32[]{:S(2)}, u32[]{:S(2)}) collective-permute-start(bf16[256,128]{1,0:T(8,128)(2,1)S(1)} %get-tuple-element.70), channel_id=1, source_target_pairs={{0,12},{4,8},{8,4},{12,0},{16,28},{20,24},{24,20},{28,16},{1,13},{... | collective-permute-start | bytes 196616 | tf_op jit(solution)/shard_map/ppermute | solution.py:442
  26.3 1.7 %shard_map.88 = (bf16[3,4,256,128]{3,2,1,0:T(8,128)(2,1)S(1)}, bf16[128,1024]{1,0:T(8,128)(2,1)S(1)}, bf16[128,1024]{1,0:T(8,128)(2,1)S(1)}, bf16[128,512]{1,0:T...) custom-call(bf16[4,2,256,128]{3,2,1,0:T(8,128)(2,1)S(1)} %get-tuple-element.58, ...), custom_call_target="tpu_custom_call" | custom-call | flops 335544320 | bytes 6914048 | tf_op jit(solution)/shard_map/pallas_call | solution.py:39
  28.0 4.5 %collective-permute-done.7.refs_5_.refs_11_ = bf16[896,128]{1,0:T(8,128)(2,1)S(1)} collective-permute-done((bf16[896,128]{1,0:T(8,128)(2,1)S(1)}, bf16[896,128]{1,0:T(8,128)(2,1)S(1)}, u32[]{:S(2)}, u32[]{:S(2)}) %collective-permute-start.7) | collective-permute-done | bytes 229408 | tf_op jit(solution)/shard_map/ppermute | solution.py:442
  32.9 2.6 %shard_map.90 = (bf16[4,4,256,256]{3,2,1,0:T(8,128)(2,1)S(1)}, bf16[4,256,128]{2,1,0:T(8,128)(2,1)S(1)}, bf16[2,256,128]{2,1,0:T(8,128)(2,1)S(1)}, f32[8,1024]{1...) custom-call(bf16[3,4,256,128]{3,2,1,0:T(8,128)(2,1)S(1)} %get-tuple-, ...), custom_call_target="tpu_custom_call" | custom-call | flops 335544320 | bytes 9568256 | tf_op jit(solution)/shard_map/pallas_call | solution.py:39
  35.6 4.5 %collective-permute-start.11 = (bf16[256,128]{1,0:T(8,128)(2,1)S(1)}, bf16[256,128]{1,0:T(8,128)(2,1)S(1)}, u32[]{:S(2)}, u32[]{:S(2)}) collective-permute-start(bf16[256,128]{1,0:T(8,128)(2,1)S(1)} %get-tuple-element.74), channel_id=1, source_target_pairs={{0,12},{4,8},{8,4},{12,0},{16,28},{20,24},{24,20},{28,16},{1,13},{... | collective-permute-start | bytes 196616 | tf_op jit(solution)/shard_map/ppermute | solution.py:442
  40.7 3.3 %shard_map.91 = (bf16[4,256,128]{2,1,0:T(8,128)(2,1)S(1)}, f32[2,4,256,128]{3,2,1,0:T(8,128)S(1)}) custom-call(bf16[3,4,256,128]{3,2,1,0:T(8,128)(2,1)S(1)} %get-tuple-element.65.refs_0_, bf16[4,2,256,128]{3,2,1,0:T(8,128)(2,1)S(1)} %get-tuple-element.58.near.refs_1_, bf16[2,512,128]{2,1,0:T(8,128)(2,1)S(1)} %get-tuple-element.60.level_1.refs_2_, ...), custom_call_target="tpu_custom_call" | custom-call | tf_op jit(solution)/shard_map/pallas_call | solution.py:39
  44.8 0.8 %shard_map.92 = (bf16[2,64,2048]{2,1,0:T(8,128)(2,1)S(1)}, bf16[32,2048]{1,0:T(8,128)(2,1)S(1)}, bf16[32,2048]{1,0:T(8,128)(2,1)S(1)}, bf16[32,2048]{1,0:T(8,128)(2,1)S(1)}, bf16[32,2048]{1,0:T(8,128)(2,1)S(1)}) custom-call(bf16[256,128]{1,0:T(8,128)(2,1)S(1)} %get-tuple-element.73.refs_0_, bf16[256,128]{1,0:T(8,128)(2,1)S(1)} %collective-permute-done.11.refs_1_, ...), custom_call_target="tpu_custom_call" | custom-call | tf_op jit(solution)/shard_map/pallas_call | solution.py:39
  46.7 1.0 %collective-permute-done.20.refs_0_ = bf16[896,128]{1,0:T(8,128)(2,1)S(1)} collective-permute-done((bf16[896,128]{1,0:T(8,128)(2,1)S(1)}, bf16[896,128]{1,0:T(8,128)(2,1)S(1)}, u32[]{:S(2)}, u32[]{:S(2)}) %collective-permute-start.20) | collective-permute-done | bytes 229408 | tf_op jit(solution)/shard_map/ppermute | solution.py:442
  48.0 1.3 %collective-permute-start.21 = (bf16[3,256,128]{2,1,0:T(8,128)(2,1)S(1)}, bf16[3,256,128]{2,1,0:T(8,128)(2,1)S(1)}, u32[]{:S(2)}, u32[]{:S(2)}) collective-permute-start(bf16[3,256,128]{2,1,0:T(8,128)(2,1)S(1)} %get-tuple-element.97), channel_id=1, source_target_pairs={{0,12},{4,8},{8,4},{12,0},{16,28},{20,24},{24,20},{28,16},{1,13},{... | collective-permute-start | bytes 589832 | tf_op jit(solution)/shard_map/ppermute | solution.py:442
  49.3 1.8 %collective-permute-start.22 = (bf16[3,256,128]{2,1,0:T(8,128)(2,1)S(1)}, bf16[3,256,128]{2,1,0:T(8,128)(2,1)S(1)}, u32[]{:S(2)}, u32[]{:S(2)}) collective-permute-start(bf16[3,256,128]{2,1,0:T(8,128)(2,1)S(1)} %get-tuple-element.98), channel_id=1, source_target_pairs={{0,8},{4,12},{8,0},{12,4},{16,24},{20,28},{24,16},{28,20},{1,9},{5... | collective-permute-start | bytes 589832 | tf_op jit(solution)/shard_map/ppermute | solution.py:442
  51.7 1.6 %collective-permute-start.18 = (bf16[32,2048]{1,0:T(8,128)(2,1)S(1)}, bf16[32,2048]{1,0:T(8,128)(2,1)S(1)}, u32[]{:S(2)}, u32[]{:S(2)}) collective-permute-start(bf16[32,2048]{1,0:T(8,128)(2,1)S(1)} %get-tuple-element.92), channel_id=1, source_target_pairs={{0,2},{1,3},{2,0},{3,1},{4,6},{5,7},{6,4},{7,5},{8,10},{9,11},{10,... | collective-permute-start | bytes 393224 | tf_op jit(solution)/shard_map/ppermute | solution.py:442
  53.8 3.1 %collective-permute-done.18.refs_1_ = bf16[32,2048]{1,0:T(8,128)(2,1)S(1)} collective-permute-done((bf16[32,2048]{1,0:T(8,128)(2,1)S(1)}, bf16[32,2048]{1,0:T(8,128)(2,1)S(1)}, u32[]{:S(2)}, u32[]{:S(2)}) %collective-permute-start.18) | collective-permute-done | bytes 131104 | tf_op jit(solution)/shard_map/ppermute | solution.py:442
  56.8 1.4 %collective-permute-done.19.refs_2_ = bf16[32,2048]{1,0:T(8,128)(2,1)S(1)} collective-permute-done((bf16[32,2048]{1,0:T(8,128)(2,1)S(1)}, bf16[32,2048]{1,0:T(8,128)(2,1)S(1)}, u32[]{:S(2)}, u32[]{:S(2)}) %collective-permute-start.19) | collective-permute-done | bytes 131104 | tf_op jit(solution)/shard_map/ppermute | solution.py:442
  59.1 1.1 %shard_map.95 = (bf16[256,512]{1,0:T(8,128)(2,1)}, bf16[256,512]{1,0:T(8,128)(2,1)}, bf16[256,512]{1,0:T(8,128)(2,1)}, bf16[64,2048]{1,0:T(8,128)(2,1)}) custom-call(f32[64,2048]{1,0:T(8,128)S(1)} %get-tuple-element.91.refs_0_, bf16[32,2048]{1,0:T(8,128)(2,1)S(1)} %collective-permute-done.18.refs_1_, bf16[32,2048]{1,0:T(8,128)(2,1)S(1)} %collective-permute-done.19.refs_2_, ...), custom_call_target="tpu_custom_call" | custom-call | tf_op jit(solution)/shard_map/pallas_call | solution.py:39
  (41 shorter events, 8.6 us)
Async XLA Ops:
  1.9 16.5 %collective-permute-start = (bf16[3,256,128]{2,1,0:T(8,128)(2,1)S(1)}, bf16[3,256,128]{2,1,0:T(8,128)(2,1)S(1)}, u32[]{:S(2)}, u32[]{:S(2)}) collective-permute-start(bf16[3,256,128]{2,1,0:T(8,128)(2,1)S(1)} %get-tuple-element.55), channel_id=1, source_target_pairs={{0,12},{4,8},{8,4},{12,0},{16,28},{20,24},{24,20},{28,16},{1,13},{... | collective-permute-start | bytes 589832 | tf_op jit(solution)/shard_map/ppermute | solution.py:442
  6.0 12.5 %collective-permute-start.1 = (bf16[3,256,128]{2,1,0:T(8,128)(2,1)S(1)}, bf16[3,256,128]{2,1,0:T(8,128)(2,1)S(1)}, u32[]{:S(2)}, u32[]{:S(2)}) collective-permute-start(bf16[3,256,128]{2,1,0:T(8,128)(2,1)S(1)} %get-tuple-element.56), channel_id=1, source_target_pairs={{0,8},{4,12},{8,0},{12,4},{16,24},{20,28},{24,16},{28,20},{1,9},{5... | collective-permute-start | bytes 589832 | tf_op jit(solution)/shard_map/ppermute | solution.py:442
  6.4 12.0 %collective-permute-start.2 = (bf16[3,256,128]{2,1,0:T(8,128)(2,1)S(1)}, bf16[3,256,128]{2,1,0:T(8,128)(2,1)S(1)}, u32[]{:S(2)}, u32[]{:S(2)}) collective-permute-start(bf16[3,256,128]{2,1,0:T(8,128)(2,1)S(1)} %get-tuple-element.57), channel_id=1, source_target_pairs={{0,4},{4,0},{8,12},{12,8},{16,20},{20,16},{24,28},{28,24},{1,5},{5... | collective-permute-start | bytes 589832 | tf_op jit(solution)/shard_map/ppermute | solution.py:442
  7.6 6.1 %collective-permute-start.4 = (bf16[32,2048]{1,0:T(8,128)(2,1)S(1)}, bf16[32,2048]{1,0:T(8,128)(2,1)S(1)}, u32[]{:S(2)}, u32[]{:S(2)}) collective-permute-start(bf16[32,2048]{1,0:T(8,128)(2,1)S(1)} %get-tuple-element.104), channel_id=1, source_target_pairs={{0,2},{1,3},{2,0},{3,1},{4,6},{5,7},{6,4},{7,5},{8,10},{9,11},{10,... | collective-permute-start | bytes 393224 | tf_op jit(solution)/shard_map/ppermute | solution.py:442
  9.5 5.7 %collective-permute-start.3 = (bf16[32,2048]{1,0:T(8,128)(2,1)S(1)}, bf16[32,2048]{1,0:T(8,128)(2,1)S(1)}, u32[]{:S(2)}, u32[]{:S(2)}) collective-permute-start(bf16[32,2048]{1,0:T(8,128)(2,1)S(1)} %get-tuple-element.105), channel_id=1, source_target_pairs={{0,2},{1,3},{2,0},{3,1},{4,6},{5,7},{6,4},{7,5},{8,10},{9,11},{10,... | collective-permute-start | bytes 393224 | tf_op jit(solution)/shard_map/ppermute | solution.py:442
  17.9 3.7 %collective-permute-start.5 = (bf16[64,2048]{1,0:T(8,128)(2,1)S(1)}, bf16[64,2048]{1,0:T(8,128)(2,1)S(1)}, u32[]{:S(2)}, u32[]{:S(2)}) collective-permute-start(bf16[64,2048]{1,0:T(8,128)(2,1)S(1)} %get-tuple-element.61.refs_0_), channel_id=1, source_target_pairs={{0,1},{1,0},{2,3},{3,2},{4,5},{5,4},{6,7},{7,6},{8,9},{9,8},{10,11... | collective-permute-start | bytes 786440 | tf_op jit(solution)/shard_map/ppermute | solution.py:442
  18.0 3.6 %collective-permute-start.6 = (bf16[64,2048]{1,0:T(8,128)(2,1)S(1)}, bf16[64,2048]{1,0:T(8,128)(2,1)S(1)}, u32[]{:S(2)}, u32[]{:S(2)}) collective-permute-start(bf16[64,2048]{1,0:T(8,128)(2,1)S(1)} %get-tuple-element.62.refs_2_), channel_id=1, source_target_pairs={{0,1},{1,0},{2,3},{3,2},{4,5},{5,4},{6,7},{7,6},{8,9},{9,8},{10,11... | collective-permute-start | bytes 786440 | tf_op jit(solution)/shard_map/ppermute | solution.py:442
  18.9 13.6 %collective-permute-start.7 = (bf16[896,128]{1,0:T(8,128)(2,1)S(1)}, bf16[896,128]{1,0:T(8,128)(2,1)S(1)}, u32[]{:S(2)}, u32[]{:S(2)}) collective-permute-start(bf16[896,128]{1,0:T(8,128)(2,1)S(1)} %shard_map.89), channel_id=1, source_target_pairs={{0,16},{4,20},{8,24},{12,28},{16,0},{20,4},{24,8},{28,12},{1,17},{... | collective-permute-start | bytes 688136 | tf_op jit(solution)/shard_map/ppermute | solution.py:442
  22.4 10.0 %collective-permute-start.8 = (bf16[256,128]{1,0:T(8,128)(2,1)S(1)}, bf16[256,128]{1,0:T(8,128)(2,1)S(1)}, u32[]{:S(2)}, u32[]{:S(2)}) collective-permute-start(bf16[256,128]{1,0:T(8,128)(2,1)S(1)} %get-tuple-element.70), channel_id=1, source_target_pairs={{0,12},{4,8},{8,4},{12,0},{16,28},{20,24},{24,20},{28,16},{1,13},{... | collective-permute-start | bytes 196616 | tf_op jit(solution)/shard_map/ppermute | solution.py:442
  25.0 7.9 %collective-permute-start.9 = (bf16[256,128]{1,0:T(8,128)(2,1)S(1)}, bf16[256,128]{1,0:T(8,128)(2,1)S(1)}, u32[]{:S(2)}, u32[]{:S(2)}) collective-permute-start(bf16[256,128]{1,0:T(8,128)(2,1)S(1)} %get-tuple-element.71), channel_id=1, source_target_pairs={{0,8},{4,12},{8,0},{12,4},{16,24},{20,28},{24,16},{28,20},{1,9},{5... | collective-permute-start | bytes 196616 | tf_op jit(solution)/shard_map/ppermute | solution.py:442
  25.5 7.4 %collective-permute-start.10 = (bf16[256,128]{1,0:T(8,128)(2,1)S(1)}, bf16[256,128]{1,0:T(8,128)(2,1)S(1)}, u32[]{:S(2)}, u32[]{:S(2)}) collective-permute-start(bf16[256,128]{1,0:T(8,128)(2,1)S(1)} %get-tuple-element.72), channel_id=1, source_target_pairs={{0,4},{4,0},{8,12},{12,8},{16,20},{20,16},{24,28},{28,24},{1,5},{5... | collective-permute-start | bytes 196616 | tf_op jit(solution)/shard_map/ppermute | solution.py:442
  35.5 12.2 %collective-permute-start.20 = (bf16[896,128]{1,0:T(8,128)(2,1)S(1)}, bf16[896,128]{1,0:T(8,128)(2,1)S(1)}, u32[]{:S(2)}, u32[]{:S(2)}) collective-permute-start(bf16[896,128]{1,0:T(8,128)(2,1)S(1)} %get-tuple-element.95), channel_id=1, source_target_pairs={{0,16},{4,20},{8,24},{12,28},{16,0},{20,4},{24,8},{28,12},{1,17},{... | collective-permute-start | bytes 688136 | tf_op jit(solution)/shard_map/ppermute | solution.py:442
  35.6 8.4 %collective-permute-start.11 = (bf16[256,128]{1,0:T(8,128)(2,1)S(1)}, bf16[256,128]{1,0:T(8,128)(2,1)S(1)}, u32[]{:S(2)}, u32[]{:S(2)}) collective-permute-start(bf16[256,128]{1,0:T(8,128)(2,1)S(1)} %get-tuple-element.74), channel_id=1, source_target_pairs={{0,12},{4,8},{8,4},{12,0},{16,28},{20,24},{24,20},{28,16},{1,13},{... | collective-permute-start | bytes 196616 | tf_op jit(solution)/shard_map/ppermute | solution.py:442
  40.1 4.7 %collective-permute-start.12 = (bf16[256,128]{1,0:T(8,128)(2,1)S(1)}, bf16[256,128]{1,0:T(8,128)(2,1)S(1)}, u32[]{:S(2)}, u32[]{:S(2)}) collective-permute-start(bf16[256,128]{1,0:T(8,128)(2,1)S(1)} %get-tuple-element.75), channel_id=1, source_target_pairs={{0,8},{4,12},{8,0},{12,4},{16,24},{20,28},{24,16},{28,20},{1,9},{5... | collective-permute-start | bytes 196616 | tf_op jit(solution)/shard_map/ppermute | solution.py:442
  40.1 4.7 %collective-permute-start.13 = (bf16[256,128]{1,0:T(8,128)(2,1)S(1)}, bf16[256,128]{1,0:T(8,128)(2,1)S(1)}, u32[]{:S(2)}, u32[]{:S(2)}) collective-permute-start(bf16[256,128]{1,0:T(8,128)(2,1)S(1)} %get-tuple-element.76), channel_id=1, source_target_pairs={{0,4},{4,0},{8,12},{12,8},{16,20},{20,16},{24,28},{28,24},{1,5},{5... | collective-permute-start | bytes 196616 | tf_op jit(solution)/shard_map/ppermute | solution.py:442
  45.6 3.7 %collective-permute-start.14 = (bf16[32,2048]{1,0:T(8,128)(2,1)S(1)}, bf16[32,2048]{1,0:T(8,128)(2,1)S(1)}, u32[]{:S(2)}, u32[]{:S(2)}) collective-permute-start(bf16[32,2048]{1,0:T(8,128)(2,1)S(1)} %get-tuple-element.87), channel_id=1, source_target_pairs={{0,1},{1,0},{2,3},{3,2},{4,5},{5,4},{6,7},{7,6},{8,9},{9,8},{10,11... | collective-permute-start | bytes 393224 | tf_op jit(solution)/shard_map/ppermute | solution.py:442
  45.7 5.4 %collective-permute-start.15 = (bf16[32,2048]{1,0:T(8,128)(2,1)S(1)}, bf16[32,2048]{1,0:T(8,128)(2,1)S(1)}, u32[]{:S(2)}, u32[]{:S(2)}) collective-permute-start(bf16[32,2048]{1,0:T(8,128)(2,1)S(1)} %get-tuple-element.88), channel_id=1, source_target_pairs={{0,1},{1,0},{2,3},{3,2},{4,5},{5,4},{6,7},{7,6},{8,9},{9,8},{10,11... | collective-permute-start | bytes 393224 | tf_op jit(solution)/shard_map/ppermute | solution.py:442
  46.2 5.4 %collective-permute-start.16 = (bf16[32,2048]{1,0:T(8,128)(2,1)S(1)}, bf16[32,2048]{1,0:T(8,128)(2,1)S(1)}, u32[]{:S(2)}, u32[]{:S(2)}) collective-permute-start(bf16[32,2048]{1,0:T(8,128)(2,1)S(1)} %get-tuple-element.89), channel_id=1, source_target_pairs={{0,1},{1,0},{2,3},{3,2},{4,5},{5,4},{6,7},{7,6},{8,9},{9,8},{10,11... | collective-permute-start | bytes 393224 | tf_op jit(solution)/shard_map/ppermute | solution.py:442
  46.3 5.3 %collective-permute-start.17 = (bf16[32,2048]{1,0:T(8,128)(2,1)S(1)}, bf16[32,2048]{1,0:T(8,128)(2,1)S(1)}, u32[]{:S(2)}, u32[]{:S(2)}) collective-permute-start(bf16[32,2048]{1,0:T(8,128)(2,1)S(1)} %get-tuple-element.90), channel_id=1, source_target_pairs={{0,1},{1,0},{2,3},{3,2},{4,5},{5,4},{6,7},{7,6},{8,9},{9,8},{10,11... | collective-permute-start | bytes 393224 | tf_op jit(solution)/shard_map/ppermute | solution.py:442
  48.0 10.2 %collective-permute-start.21 = (bf16[3,256,128]{2,1,0:T(8,128)(2,1)S(1)}, bf16[3,256,128]{2,1,0:T(8,128)(2,1)S(1)}, u32[]{:S(2)}, u32[]{:S(2)}) collective-permute-start(bf16[3,256,128]{2,1,0:T(8,128)(2,1)S(1)} %get-tuple-element.97), channel_id=1, source_target_pairs={{0,12},{4,8},{8,4},{12,0},{16,28},{20,24},{24,20},{28,16},{1,13},{... | collective-permute-start | bytes 589832 | tf_op jit(solution)/shard_map/ppermute | solution.py:442
  49.3 9.1 %collective-permute-start.22 = (bf16[3,256,128]{2,1,0:T(8,128)(2,1)S(1)}, bf16[3,256,128]{2,1,0:T(8,128)(2,1)S(1)}, u32[]{:S(2)}, u32[]{:S(2)}) collective-permute-start(bf16[3,256,128]{2,1,0:T(8,128)(2,1)S(1)} %get-tuple-element.98), channel_id=1, source_target_pairs={{0,8},{4,12},{8,0},{12,4},{16,24},{20,28},{24,16},{28,20},{1,9},{5... | collective-permute-start | bytes 589832 | tf_op jit(solution)/shard_map/ppermute | solution.py:442
  51.0 8.1 %collective-permute-start.23 = (bf16[3,256,128]{2,1,0:T(8,128)(2,1)S(1)}, bf16[3,256,128]{2,1,0:T(8,128)(2,1)S(1)}, u32[]{:S(2)}, u32[]{:S(2)}) collective-permute-start(bf16[3,256,128]{2,1,0:T(8,128)(2,1)S(1)} %get-tuple-element.99), channel_id=1, source_target_pairs={{0,4},{4,0},{8,12},{12,8},{16,20},{20,16},{24,28},{28,24},{1,5},{5... | collective-permute-start | bytes 589832 | tf_op jit(solution)/shard_map/ppermute | solution.py:442
  51.7 5.1 %collective-permute-start.18 = (bf16[32,2048]{1,0:T(8,128)(2,1)S(1)}, bf16[32,2048]{1,0:T(8,128)(2,1)S(1)}, u32[]{:S(2)}, u32[]{:S(2)}) collective-permute-start(bf16[32,2048]{1,0:T(8,128)(2,1)S(1)} %get-tuple-element.92), channel_id=1, source_target_pairs={{0,2},{1,3},{2,0},{3,1},{4,6},{5,7},{6,4},{7,5},{8,10},{9,11},{10,... | collective-permute-start | bytes 393224 | tf_op jit(solution)/shard_map/ppermute | solution.py:442
  53.3 5.0 %collective-permute-start.19 = (bf16[32,2048]{1,0:T(8,128)(2,1)S(1)}, bf16[32,2048]{1,0:T(8,128)(2,1)S(1)}, u32[]{:S(2)}, u32[]{:S(2)}) collective-permute-start(bf16[32,2048]{1,0:T(8,128)(2,1)S(1)} %get-tuple-element.93), channel_id=1, source_target_pairs={{0,2},{1,3},{2,0},{3,1},{4,6},{5,7},{6,4},{7,5},{8,10},{9,11},{10,... | collective-permute-start | bytes 393224 | tf_op jit(solution)/shard_map/ppermute | solution.py:442
  (2 other events, 2.5 us)

commit v21 on v20

--- a/solution.py
+++ b/solution.py
@@ -116,12 +116,12 @@
         copy.wait()
 
 
-def copy_kernel(out_grad, weight, low, high, out_grad_out, weight_out, far):
-    out_grad_out[...] = out_grad[...]
-    weight_out[...] = weight[...]
+def copy_kernel(out_grad, low, high, _, *outs):
     half = low.shape[0]
-    far[:half] = low[...]
-    far[half:] = high[...]
+    outs[0][...] = out_grad[:half]
+    outs[1][...] = out_grad[half:]
+    outs[2][...] = low[...]
+    outs[3][...] = high[...]
 
 
 def gather_kernel(nb, *refs):
@@ -413,11 +413,11 @@
 
 
 def grad_kernel(*refs):
-    pieces, out_weight, refs = refs[:N_MP], refs[N_MP], refs[N_MP + 1 :]
+    pieces, out_weight, refs = refs[: 2 * N_MP], refs[2 * N_MP], refs[2 * N_MP + 1 :]
     *outs, whole, heads = refs
     me = member()
-    for step, piece in enumerate(pieces):
-        whole[span(share() ^ step, piece.shape[0]), :] = piece[...]
+    for i, piece in enumerate(pieces):
+        whole[span(2 * (share() ^ (i // 2)) + i % 2, piece.shape[0]), :] = piece[...]
     heads[...] = dot_nt(whole[...], out_weight[...]).astype(BF16)
     for step, out in zip(STEPS, outs):
         out[...] = heads[:, columns(me ^ step)]
@@ -489,10 +489,6 @@
     half = out_grad.shape[0] // 2
     far = [swapped(piece, "mp", 2) for piece in (out_grad[:half], out_grad[half:])]
     chunks = exchanged(chunks)
-    arrays = (out_grad, out_weight, *far)
-    own_grad, out_weight, far = call(
-        copy_kernel, [shape(*x.shape) for x in (out_grad, out_weight, out_grad)], arrays
-    )
     refs = call(
         functools.partial(cross_kernel, groups),
         sent,
@@ -501,6 +497,9 @@
         flops=20 * score_flops,
     )
     rim_blocks = crossed(refs)
+    pieces = call(copy_kernel, [shape(half, model)] * N_MP, (out_grad, *far, refs[0]))
+    beside_us = [swapped(piece, "mp", 1) for piece in pieces]
+    pieces = [*pieces[:2], *beside_us[:2], *pieces[2:], *beside_us[2:]]
     near, queries, level_1 = call(
         functools.partial(gather_kernel, nb),
         [
@@ -513,9 +512,8 @@
     grad_chunks = call(
         grad_kernel,
         [chunk] * GROUP,
-        (own_grad, swapped(own_grad, "mp", 1), far, swapped(far, "mp", 1), out_weight),
+        (*pieces, out_weight),
         scratch=[pltpu.VMEM((rows, model), BF16), pltpu.VMEM((rows, width), BF16)],
-        flops=weight_flops,
     )
     query, k_t, v_t, k1_t, v1_t, weights, stats = call(
         functools.partial(local_kernel, nb),
@@ -529,7 +527,6 @@
             shape(8, tokens, dtype=F32),
         ],
         (near, queries, level_1, grad_chunks[0]),
-        flops=score_flops,
     )
     grad_chunks = exchanged(grad_chunks)
     rim_square = shape(len(rims), BLOCK, BLOCK)

time: 60.8 us -> 60.9 us (level)
  waiting for transfers between devices: 17.4 us -> 20.6 us
  local copies, waits for them, and re-layouts: 3.53 us -> 0.99 us
    ppermute x24 -> x26, waiting for transfers between devices: 17.4 us -> 20.6 us  [swapped(): lax.ppermute(x, axis, [(i, i ^ step) for i in range(lax.axis_size(axis))])]
    unnamed x4, local copies, waits for them, and re-layouts: 2.54 us -> 0.01 us
    ppermute x24 -> x26, starting transfers between devices: 25.5 us -> 25.4 us  [swapped(): lax.ppermute(x, axis, [(i, i ^ step) for i in range(lax.axis_size(axis))])]
  transfers between devices with their start and end apart: 24 -> 26, of which waited for: 10 -> 13; matrix products, arithmetic and copies ran while one was open for 2% -> 2% of each run, Pallas kernels for 13% -> 13%
where the time goes in v21:
time: 60.9 us; the launch traced here: 60.7 us
  starting transfers between devices  25.4 us (42%)
  waiting for transfers between devices  20.6 us (34%)
  Pallas kernels  12.9 us (21%)
  local copies, waits for them, and re-layouts  0.99 us (2%)
  between operations  0.76 us (1%)
    ppermute x26, starting transfers between devices, swapped(): lax.ppermute(x, axis, [(i, i ^ step) for i in range(lax.axis_size(axis))])  25.4 us
    ppermute x26, waiting for transfers between devices, swapped(): lax.ppermute(x, axis, [(i, i ^ step) for i in range(lax.axis_size(axis))])  20.6 us
    pallas_call x12, Pallas kernels, call(): pl.pallas_call(kernel, out_shape=out_shape, in_specs=[kept if copied else...  12.9 us
  transfers between devices with their start and end apart: 26, of which 13 were waited for; matrix products, arithmetic and copies ran while one was open for 2% of the time, Pallas kernels for 13%

profile of v21, /device:TPU:0, one launch (start us, length us, event | category | flops | bytes accessed | tf_op | source)
XLA Modules:
  0.0 60.7 jit_solution(12911946235871668649)
XLA Ops:
  0.6 1.3 %shard_map.84 = (bf16[3,256,128]{2,1,0:T(8,128)(2,1)S(1)}, bf16[3,256,128]{2,1,0:T(8,128)(2,1)S(1)}, bf16[3,256,128]{2,1,0:T(8,128)(2,1)S(1)}, bf16[3,256,128]{2,1,0:T(8,128)(2,1)S(1)}) custom-call(bf16[256,512]{1,0:T(8,128)(2,1)} %q.1, bf16[256,512]{1,0:T(8,128)(2,1)} %k.1, bf16[256,512]{1,0:T(8,128)(2,1)} %v.1), custom_call_target="tpu_custom_call" | custom-call | tf_op jit(solution)/shard_map/pallas_call | solution.py:39
  1.9 4.0 %collective-permute-start = (bf16[3,256,128]{2,1,0:T(8,128)(2,1)S(1)}, bf16[3,256,128]{2,1,0:T(8,128)(2,1)S(1)}, u32[]{:S(2)}, u32[]{:S(2)}) collective-permute-start(bf16[3,256,128]{2,1,0:T(8,128)(2,1)S(1)} %get-tuple-element.56), channel_id=1, source_target_pairs={{0,12},{4,8},{8,4},{12,0},{16,28},{20,24},{24,20},{28,16},{1,13},{... | collective-permute-start | bytes 589832 | tf_op jit(solution)/shard_map/ppermute | solution.py:442
  6.6 1.0 %fusion = (bf16[32,2048]{1,0:T(8,128)(2,1)S(1)}, bf16[32,2048]{1,0:T(8,128)(2,1)S(1)}) fusion(bf16[64,2048]{1,0:T(8,128)(2,1)} %out_grad.1), kind=kLoop, calls=%fused_computation | loop fusion | bytes 524288 | tf_op jit(solution)/shard_map/slice | solution.py:490
  7.6 1.9 %collective-permute-start.4 = (bf16[32,2048]{1,0:T(8,128)(2,1)S(1)}, bf16[32,2048]{1,0:T(8,128)(2,1)S(1)}, u32[]{:S(2)}, u32[]{:S(2)}) collective-permute-start(bf16[32,2048]{1,0:T(8,128)(2,1)S(1)} %get-tuple-element.106), channel_id=1, source_target_pairs={{0,2},{1,3},{2,0},{3,1},{4,6},{5,7},{6,4},{7,5},{8,10},{9,11},{10,... | collective-permute-start | bytes 393224 | tf_op jit(solution)/shard_map/ppermute | solution.py:442
  9.7 2.0 %collective-permute-done.refs_1_ = bf16[3,256,128]{2,1,0:T(8,128)(2,1)S(1)} collective-permute-done((bf16[3,256,128]{2,1,0:T(8,128)(2,1)S(1)}, bf16[3,256,128]{2,1,0:T(8,128)(2,1)S(1)}, u32[]{:S(2)}, u32[]{:S(2)}) %collective-permute-start) | collective-permute-done | bytes 196640 | tf_op jit(solution)/shard_map/ppermute | solution.py:442
  11.7 3.6 %collective-permute-done.1.refs_2_ = bf16[3,256,128]{2,1,0:T(8,128)(2,1)S(1)} collective-permute-done((bf16[3,256,128]{2,1,0:T(8,128)(2,1)S(1)}, bf16[3,256,128]{2,1,0:T(8,128)(2,1)S(1)}, u32[]{:S(2)}, u32[]{:S(2)}) %collective-permute-start.1) | collective-permute-done | bytes 196640 | tf_op jit(solution)/shard_map/ppermute | solution.py:442
  15.7 2.6 %collective-permute-start.9 = (bf16[896,128]{1,0:T(8,128)(2,1)S(1)}, bf16[896,128]{1,0:T(8,128)(2,1)S(1)}, u32[]{:S(2)}, u32[]{:S(2)}) collective-permute-start(bf16[896,128]{1,0:T(8,128)(2,1)S(1)} %shard_map.86._), channel_id=1, source_target_pairs={{0,16},{4,20},{8,24},{12,28},{16,0},{20,4},{24,8},{28,12},{1,17},{... | collective-permute-start | bytes 688136 | tf_op jit(solution)/shard_map/ppermute | solution.py:442
  20.5 0.8 %shard_map.88 = (bf16[256,128]{1,0:T(8,128)(2,1)S(1)}, bf16[256,128]{1,0:T(8,128)(2,1)S(1)}, bf16[256,128]{1,0:T(8,128)(2,1)S(1)}, bf16[256,128]{1,0:T(8,128)(2,1)S(1)}) custom-call(bf16[32,2048]{1,0:T(8,128)(2,1)S(1)} %get-tuple-element.62.refs_0_, bf16[32,2048]{1,0:T(8,128)(2,1)S(1)} %get-tuple-element.63.refs_1_, ...), custom_call_target="tpu_custom_call" | custom-call | tf_op jit(solution)/shard_map/pallas_call | solution.py:39
  21.4 2.5 %collective-permute-start.10 = (bf16[256,128]{1,0:T(8,128)(2,1)S(1)}, bf16[256,128]{1,0:T(8,128)(2,1)S(1)}, u32[]{:S(2)}, u32[]{:S(2)}) collective-permute-start(bf16[256,128]{1,0:T(8,128)(2,1)S(1)} %get-tuple-element.72), channel_id=1, source_target_pairs={{0,12},{4,8},{8,4},{12,0},{16,28},{20,24},{24,20},{28,16},{1,13},{... | collective-permute-start | bytes 196616 | tf_op jit(solution)/shard_map/ppermute | solution.py:442
  25.3 1.7 %shard_map.89 = (bf16[3,4,256,128]{3,2,1,0:T(8,128)(2,1)S(1)}, bf16[128,1024]{1,0:T(8,128)(2,1)S(1)}, bf16[128,1024]{1,0:T(8,128)(2,1)S(1)}, bf16[128,512]{1,0:T...) custom-call(bf16[4,2,256,128]{3,2,1,0:T(8,128)(2,1)S(1)} %get-tuple-element.59, ...), custom_call_target="tpu_custom_call" | custom-call | tf_op jit(solution)/shard_map/pallas_call | solution.py:39
  27.0 3.8 %collective-permute-done.10.refs_7_ = bf16[256,128]{1,0:T(8,128)(2,1)S(1)} collective-permute-done((bf16[256,128]{1,0:T(8,128)(2,1)S(1)}, bf16[256,128]{1,0:T(8,128)(2,1)S(1)}, u32[]{:S(2)}, u32[]{:S(2)}) %collective-permute-start.10) | collective-permute-done | bytes 65568 | tf_op jit(solution)/shard_map/ppermute | solution.py:442
  30.8 1.0 %collective-permute-done.11.refs_8_ = bf16[256,128]{1,0:T(8,128)(2,1)S(1)} collective-permute-done((bf16[256,128]{1,0:T(8,128)(2,1)S(1)}, bf16[256,128]{1,0:T(8,128)(2,1)S(1)}, u32[]{:S(2)}, u32[]{:S(2)}) %collective-permute-start.11) | collective-permute-done | bytes 65568 | tf_op jit(solution)/shard_map/ppermute | solution.py:442
  31.8 2.6 %shard_map.90 = (bf16[4,4,256,256]{3,2,1,0:T(8,128)(2,1)S(1)}, bf16[4,256,128]{2,1,0:T(8,128)(2,1)S(1)}, bf16[2,256,128]{2,1,0:T(8,128)(2,1)S(1)}, f32[8,1024]{1...) custom-call(bf16[3,4,256,128]{3,2,1,0:T(8,128)(2,1)S(1)} %get-tuple-, ...), custom_call_target="tpu_custom_call" | custom-call | flops 335544320 | bytes 9568256 | tf_op jit(solution)/shard_map/pallas_call | solution.py:39
  35.1 2.6 %collective-permute-start.13 = (bf16[256,128]{1,0:T(8,128)(2,1)S(1)}, bf16[256,128]{1,0:T(8,128)(2,1)S(1)}, u32[]{:S(2)}, u32[]{:S(2)}) collective-permute-start(bf16[256,128]{1,0:T(8,128)(2,1)S(1)} %get-tuple-element.76), channel_id=1, source_target_pairs={{0,12},{4,8},{8,4},{12,0},{16,28},{20,24},{24,20},{28,16},{1,13},{... | collective-permute-start | bytes 196616 | tf_op jit(solution)/shard_map/ppermute | solution.py:442
  37.7 1.4 %collective-permute-start.15 = (bf16[256,128]{1,0:T(8,128)(2,1)S(1)}, bf16[256,128]{1,0:T(8,128)(2,1)S(1)}, u32[]{:S(2)}, u32[]{:S(2)}) collective-permute-start(bf16[256,128]{1,0:T(8,128)(2,1)S(1)} %get-tuple-element.78), channel_id=1, source_target_pairs={{0,4},{4,0},{8,12},{12,8},{16,20},{20,16},{24,28},{28,24},{1,5},{5... | collective-permute-start | bytes 196616 | tf_op jit(solution)/shard_map/ppermute | solution.py:442
  39.0 3.3 %shard_map.91 = (bf16[4,256,128]{2,1,0:T(8,128)(2,1)S(1)}, f32[2,4,256,128]{3,2,1,0:T(8,128)S(1)}) custom-call(bf16[3,4,256,128]{3,2,1,0:T(8,128)(2,1)S(1)} %get-tuple-element.67.refs_0_, bf16[4,2,256,128]{3,2,1,0:T(8,128)(2,1)S(1)} %get-tuple-element.59.near.refs_1_, bf16[2,512,128]{2,1,0:T(8,128)(2,1)S(1)} %get-tuple-element.61.level_1.refs_2_, ...), custom_call_target="tpu_custom_call" | custom-call | tf_op jit(solution)/shard_map/pallas_call | solution.py:39
  44.6 2.6 %collective-permute-done.22.refs_0_ = bf16[896,128]{1,0:T(8,128)(2,1)S(1)} collective-permute-done((bf16[896,128]{1,0:T(8,128)(2,1)S(1)}, bf16[896,128]{1,0:T(8,128)(2,1)S(1)}, u32[]{:S(2)}, u32[]{:S(2)}) %collective-permute-start.22) | collective-permute-done | bytes 229408 | tf_op jit(solution)/shard_map/ppermute | solution.py:442
  47.8 1.9 %collective-permute-start.24 = (bf16[3,256,128]{2,1,0:T(8,128)(2,1)S(1)}, bf16[3,256,128]{2,1,0:T(8,128)(2,1)S(1)}, u32[]{:S(2)}, u32[]{:S(2)}) collective-permute-start(bf16[3,256,128]{2,1,0:T(8,128)(2,1)S(1)} %get-tuple-element.100), channel_id=1, source_target_pairs={{0,8},{4,12},{8,0},{12,4},{16,24},{20,28},{24,16},{28,20},{1,9},{5... | collective-permute-start | bytes 589832 | tf_op jit(solution)/shard_map/ppermute | solution.py:442
  49.7 1.4 %collective-permute-start.25 = (bf16[3,256,128]{2,1,0:T(8,128)(2,1)S(1)}, bf16[3,256,128]{2,1,0:T(8,128)(2,1)S(1)}, u32[]{:S(2)}, u32[]{:S(2)}) collective-permute-start(bf16[3,256,128]{2,1,0:T(8,128)(2,1)S(1)} %get-tuple-element.101), channel_id=1, source_target_pairs={{0,4},{4,0},{8,12},{12,8},{16,20},{20,16},{24,28},{28,24},{1,5},{5... | collective-permute-start | bytes 589832 | tf_op jit(solution)/shard_map/ppermute | solution.py:442
  51.2 1.6 %collective-permute-start.20 = (bf16[32,2048]{1,0:T(8,128)(2,1)S(1)}, bf16[32,2048]{1,0:T(8,128)(2,1)S(1)}, u32[]{:S(2)}, u32[]{:S(2)}) collective-permute-start(bf16[32,2048]{1,0:T(8,128)(2,1)S(1)} %get-tuple-element.94), channel_id=1, source_target_pairs={{0,2},{1,3},{2,0},{3,1},{4,6},{5,7},{6,4},{7,5},{8,10},{9,11},{10,... | collective-permute-start | bytes 393224 | tf_op jit(solution)/shard_map/ppermute | solution.py:442
  53.3 4.0 %collective-permute-done.20.refs_1_ = bf16[32,2048]{1,0:T(8,128)(2,1)S(1)} collective-permute-done((bf16[32,2048]{1,0:T(8,128)(2,1)S(1)}, bf16[32,2048]{1,0:T(8,128)(2,1)S(1)}, u32[]{:S(2)}, u32[]{:S(2)}) %collective-permute-start.20) | collective-permute-done | bytes 131104 | tf_op jit(solution)/shard_map/ppermute | solution.py:442
  57.3 1.4 %collective-permute-done.21.refs_2_ = bf16[32,2048]{1,0:T(8,128)(2,1)S(1)} collective-permute-done((bf16[32,2048]{1,0:T(8,128)(2,1)S(1)}, bf16[32,2048]{1,0:T(8,128)(2,1)S(1)}, u32[]{:S(2)}, u32[]{:S(2)}) %collective-permute-start.21) | collective-permute-done | bytes 131104 | tf_op jit(solution)/shard_map/ppermute | solution.py:442
  58.7 0.8 %collective-permute-done.25.refs_6_ = bf16[3,256,128]{2,1,0:T(8,128)(2,1)S(1)} collective-permute-done((bf16[3,256,128]{2,1,0:T(8,128)(2,1)S(1)}, bf16[3,256,128]{2,1,0:T(8,128)(2,1)S(1)}, u32[]{:S(2)}, u32[]{:S(2)}) %collective-permute-start.25) | collective-permute-done | bytes 196640 | tf_op jit(solution)/shard_map/ppermute | solution.py:442
  59.6 1.1 %shard_map.95 = (bf16[256,512]{1,0:T(8,128)(2,1)}, bf16[256,512]{1,0:T(8,128)(2,1)}, bf16[256,512]{1,0:T(8,128)(2,1)}, bf16[64,2048]{1,0:T(8,128)(2,1)}) custom-call(f32[64,2048]{1,0:T(8,128)S(1)} %get-tuple-element.93.refs_0_, bf16[32,2048]{1,0:T(8,128)(2,1)S(1)} %collective-permute-done.20.refs_1_, bf16[32,2048]{1,0:T(8,128)(2,1)S(1)} %collective-permute-done.21.refs_2_, ...), custom_call_target="tpu_custom_call" | custom-call | tf_op jit(solution)/shard_map/pallas_call | solution.py:39
  (45 shorter events, 9.0 us)
Async XLA Ops:
  1.9 9.8 %collective-permute-start = (bf16[3,256,128]{2,1,0:T(8,128)(2,1)S(1)}, bf16[3,256,128]{2,1,0:T(8,128)(2,1)S(1)}, u32[]{:S(2)}, u32[]{:S(2)}) collective-permute-start(bf16[3,256,128]{2,1,0:T(8,128)(2,1)S(1)} %get-tuple-element.56), channel_id=1, source_target_pairs={{0,12},{4,8},{8,4},{12,0},{16,28},{20,24},{24,20},{28,16},{1,13},{... | collective-permute-start | bytes 589832 | tf_op jit(solution)/shard_map/ppermute | solution.py:442
  6.0 9.3 %collective-permute-start.1 = (bf16[3,256,128]{2,1,0:T(8,128)(2,1)S(1)}, bf16[3,256,128]{2,1,0:T(8,128)(2,1)S(1)}, u32[]{:S(2)}, u32[]{:S(2)}) collective-permute-start(bf16[3,256,128]{2,1,0:T(8,128)(2,1)S(1)} %get-tuple-element.57), channel_id=1, source_target_pairs={{0,8},{4,12},{8,0},{12,4},{16,24},{20,28},{24,16},{28,20},{1,9},{5... | collective-permute-start | bytes 589832 | tf_op jit(solution)/shard_map/ppermute | solution.py:442
  6.4 8.9 %collective-permute-start.2 = (bf16[3,256,128]{2,1,0:T(8,128)(2,1)S(1)}, bf16[3,256,128]{2,1,0:T(8,128)(2,1)S(1)}, u32[]{:S(2)}, u32[]{:S(2)}) collective-permute-start(bf16[3,256,128]{2,1,0:T(8,128)(2,1)S(1)} %get-tuple-element.58), channel_id=1, source_target_pairs={{0,4},{4,0},{8,12},{12,8},{16,20},{20,16},{24,28},{28,24},{1,5},{5... | collective-permute-start | bytes 589832 | tf_op jit(solution)/shard_map/ppermute | solution.py:442
  7.6 10.8 %collective-permute-start.4 = (bf16[32,2048]{1,0:T(8,128)(2,1)S(1)}, bf16[32,2048]{1,0:T(8,128)(2,1)S(1)}, u32[]{:S(2)}, u32[]{:S(2)}) collective-permute-start(bf16[32,2048]{1,0:T(8,128)(2,1)S(1)} %get-tuple-element.106), channel_id=1, source_target_pairs={{0,2},{1,3},{2,0},{3,1},{4,6},{5,7},{6,4},{7,5},{8,10},{9,11},{10,... | collective-permute-start | bytes 393224 | tf_op jit(solution)/shard_map/ppermute | solution.py:442
  9.5 8.9 %collective-permute-start.3 = (bf16[32,2048]{1,0:T(8,128)(2,1)S(1)}, bf16[32,2048]{1,0:T(8,128)(2,1)S(1)}, u32[]{:S(2)}, u32[]{:S(2)}) collective-permute-start(bf16[32,2048]{1,0:T(8,128)(2,1)S(1)} %get-tuple-element.107), channel_id=1, source_target_pairs={{0,2},{1,3},{2,0},{3,1},{4,6},{5,7},{6,4},{7,5},{8,10},{9,11},{10,... | collective-permute-start | bytes 393224 | tf_op jit(solution)/shard_map/ppermute | solution.py:442
  15.7 16.1 %collective-permute-start.9 = (bf16[896,128]{1,0:T(8,128)(2,1)S(1)}, bf16[896,128]{1,0:T(8,128)(2,1)S(1)}, u32[]{:S(2)}, u32[]{:S(2)}) collective-permute-start(bf16[896,128]{1,0:T(8,128)(2,1)S(1)} %shard_map.86._), channel_id=1, source_target_pairs={{0,16},{4,20},{8,24},{12,28},{16,0},{20,4},{24,8},{28,12},{1,17},{... | collective-permute-start | bytes 688136 | tf_op jit(solution)/shard_map/ppermute | solution.py:442
  18.5 1.5 %collective-permute-start.6 = (bf16[32,2048]{1,0:T(8,128)(2,1)S(1)}, bf16[32,2048]{1,0:T(8,128)(2,1)S(1)}, u32[]{:S(2)}, u32[]{:S(2)}) collective-permute-start(bf16[32,2048]{1,0:T(8,128)(2,1)S(1)} %get-tuple-element.63.refs_1_), channel_id=1, source_target_pairs={{0,1},{1,0},{2,3},{3,2},{4,5},{5,4},{6,7},{7,6},{8,9},{9,8},{10,11... | collective-permute-start | bytes 393224 | tf_op jit(solution)/shard_map/ppermute | solution.py:442
  19.1 1.5 %collective-permute-start.8 = (bf16[32,2048]{1,0:T(8,128)(2,1)S(1)}, bf16[32,2048]{1,0:T(8,128)(2,1)S(1)}, u32[]{:S(2)}, u32[]{:S(2)}) collective-permute-start(bf16[32,2048]{1,0:T(8,128)(2,1)S(1)} %get-tuple-element.65.refs_5_), channel_id=1, source_target_pairs={{0,1},{1,0},{2,3},{3,2},{4,5},{5,4},{6,7},{7,6},{8,9},{9,8},{10,11... | collective-permute-start | bytes 393224 | tf_op jit(solution)/shard_map/ppermute | solution.py:442
  21.4 9.4 %collective-permute-start.10 = (bf16[256,128]{1,0:T(8,128)(2,1)S(1)}, bf16[256,128]{1,0:T(8,128)(2,1)S(1)}, u32[]{:S(2)}, u32[]{:S(2)}) collective-permute-start(bf16[256,128]{1,0:T(8,128)(2,1)S(1)} %get-tuple-element.72), channel_id=1, source_target_pairs={{0,12},{4,8},{8,4},{12,0},{16,28},{20,24},{24,20},{28,16},{1,13},{... | collective-permute-start | bytes 196616 | tf_op jit(solution)/shard_map/ppermute | solution.py:442
  23.9 7.9 %collective-permute-start.11 = (bf16[256,128]{1,0:T(8,128)(2,1)S(1)}, bf16[256,128]{1,0:T(8,128)(2,1)S(1)}, u32[]{:S(2)}, u32[]{:S(2)}) collective-permute-start(bf16[256,128]{1,0:T(8,128)(2,1)S(1)} %get-tuple-element.73), channel_id=1, source_target_pairs={{0,8},{4,12},{8,0},{12,4},{16,24},{20,28},{24,16},{28,20},{1,9},{5... | collective-permute-start | bytes 196616 | tf_op jit(solution)/shard_map/ppermute | solution.py:442
  24.3 7.4 %collective-permute-start.12 = (bf16[256,128]{1,0:T(8,128)(2,1)S(1)}, bf16[256,128]{1,0:T(8,128)(2,1)S(1)}, u32[]{:S(2)}, u32[]{:S(2)}) collective-permute-start(bf16[256,128]{1,0:T(8,128)(2,1)S(1)} %get-tuple-element.74), channel_id=1, source_target_pairs={{0,4},{4,0},{8,12},{12,8},{16,20},{20,16},{24,28},{28,24},{1,5},{5... | collective-permute-start | bytes 196616 | tf_op jit(solution)/shard_map/ppermute | solution.py:442
  34.4 12.8 %collective-permute-start.22 = (bf16[896,128]{1,0:T(8,128)(2,1)S(1)}, bf16[896,128]{1,0:T(8,128)(2,1)S(1)}, u32[]{:S(2)}, u32[]{:S(2)}) collective-permute-start(bf16[896,128]{1,0:T(8,128)(2,1)S(1)} %get-tuple-element.97), channel_id=1, source_target_pairs={{0,16},{4,20},{8,24},{12,28},{16,0},{20,4},{24,8},{28,12},{1,17},{... | collective-permute-start | bytes 688136 | tf_op jit(solution)/shard_map/ppermute | solution.py:442
  35.1 7.3 %collective-permute-start.13 = (bf16[256,128]{1,0:T(8,128)(2,1)S(1)}, bf16[256,128]{1,0:T(8,128)(2,1)S(1)}, u32[]{:S(2)}, u32[]{:S(2)}) collective-permute-start(bf16[256,128]{1,0:T(8,128)(2,1)S(1)} %get-tuple-element.76), channel_id=1, source_target_pairs={{0,12},{4,8},{8,4},{12,0},{16,28},{20,24},{24,20},{28,16},{1,13},{... | collective-permute-start | bytes 196616 | tf_op jit(solution)/shard_map/ppermute | solution.py:442
  37.7 5.0 %collective-permute-start.14 = (bf16[256,128]{1,0:T(8,128)(2,1)S(1)}, bf16[256,128]{1,0:T(8,128)(2,1)S(1)}, u32[]{:S(2)}, u32[]{:S(2)}) collective-permute-start(bf16[256,128]{1,0:T(8,128)(2,1)S(1)} %get-tuple-element.77), channel_id=1, source_target_pairs={{0,8},{4,12},{8,0},{12,4},{16,24},{20,28},{24,16},{28,20},{1,9},{5... | collective-permute-start | bytes 196616 | tf_op jit(solution)/shard_map/ppermute | solution.py:442
  37.7 5.0 %collective-permute-start.15 = (bf16[256,128]{1,0:T(8,128)(2,1)S(1)}, bf16[256,128]{1,0:T(8,128)(2,1)S(1)}, u32[]{:S(2)}, u32[]{:S(2)}) collective-permute-start(bf16[256,128]{1,0:T(8,128)(2,1)S(1)} %get-tuple-element.78), channel_id=1, source_target_pairs={{0,4},{4,0},{8,12},{12,8},{16,20},{20,16},{24,28},{28,24},{1,5},{5... | collective-permute-start | bytes 196616 | tf_op jit(solution)/shard_map/ppermute | solution.py:442
  43.5 4.3 %collective-permute-start.16 = (bf16[32,2048]{1,0:T(8,128)(2,1)S(1)}, bf16[32,2048]{1,0:T(8,128)(2,1)S(1)}, u32[]{:S(2)}, u32[]{:S(2)}) collective-permute-start(bf16[32,2048]{1,0:T(8,128)(2,1)S(1)} %get-tuple-element.89), channel_id=1, source_target_pairs={{0,1},{1,0},{2,3},{3,2},{4,5},{5,4},{6,7},{7,6},{8,9},{9,8},{10,11... | collective-permute-start | bytes 393224 | tf_op jit(solution)/shard_map/ppermute | solution.py:442
  43.6 6.1 %collective-permute-start.17 = (bf16[32,2048]{1,0:T(8,128)(2,1)S(1)}, bf16[32,2048]{1,0:T(8,128)(2,1)S(1)}, u32[]{:S(2)}, u32[]{:S(2)}) collective-permute-start(bf16[32,2048]{1,0:T(8,128)(2,1)S(1)} %get-tuple-element.90), channel_id=1, source_target_pairs={{0,1},{1,0},{2,3},{3,2},{4,5},{5,4},{6,7},{7,6},{8,9},{9,8},{10,11... | collective-permute-start | bytes 393224 | tf_op jit(solution)/shard_map/ppermute | solution.py:442
  44.1 7.0 %collective-permute-start.18 = (bf16[32,2048]{1,0:T(8,128)(2,1)S(1)}, bf16[32,2048]{1,0:T(8,128)(2,1)S(1)}, u32[]{:S(2)}, u32[]{:S(2)}) collective-permute-start(bf16[32,2048]{1,0:T(8,128)(2,1)S(1)} %get-tuple-element.91), channel_id=1, source_target_pairs={{0,1},{1,0},{2,3},{3,2},{4,5},{5,4},{6,7},{7,6},{8,9},{9,8},{10,11... | collective-permute-start | bytes 393224 | tf_op jit(solution)/shard_map/ppermute | solution.py:442
  44.2 6.9 %collective-permute-start.19 = (bf16[32,2048]{1,0:T(8,128)(2,1)S(1)}, bf16[32,2048]{1,0:T(8,128)(2,1)S(1)}, u32[]{:S(2)}, u32[]{:S(2)}) collective-permute-start(bf16[32,2048]{1,0:T(8,128)(2,1)S(1)} %get-tuple-element.92), channel_id=1, source_target_pairs={{0,1},{1,0},{2,3},{3,2},{4,5},{5,4},{6,7},{7,6},{8,9},{9,8},{10,11... | collective-permute-start | bytes 393224 | tf_op jit(solution)/shard_map/ppermute | solution.py:442
  47.5 11.2 %collective-permute-start.23 = (bf16[3,256,128]{2,1,0:T(8,128)(2,1)S(1)}, bf16[3,256,128]{2,1,0:T(8,128)(2,1)S(1)}, u32[]{:S(2)}, u32[]{:S(2)}) collective-permute-start(bf16[3,256,128]{2,1,0:T(8,128)(2,1)S(1)} %get-tuple-element.99), channel_id=1, source_target_pairs={{0,12},{4,8},{8,4},{12,0},{16,28},{20,24},{24,20},{28,16},{1,13},{... | collective-permute-start | bytes 589832 | tf_op jit(solution)/shard_map/ppermute | solution.py:442
  47.8 10.9 %collective-permute-start.24 = (bf16[3,256,128]{2,1,0:T(8,128)(2,1)S(1)}, bf16[3,256,128]{2,1,0:T(8,128)(2,1)S(1)}, u32[]{:S(2)}, u32[]{:S(2)}) collective-permute-start(bf16[3,256,128]{2,1,0:T(8,128)(2,1)S(1)} %get-tuple-element.100), channel_id=1, source_target_pairs={{0,8},{4,12},{8,0},{12,4},{16,24},{20,28},{24,16},{28,20},{1,9},{5... | collective-permute-start | bytes 589832 | tf_op jit(solution)/shard_map/ppermute | solution.py:442
  49.7 9.9 %collective-permute-start.25 = (bf16[3,256,128]{2,1,0:T(8,128)(2,1)S(1)}, bf16[3,256,128]{2,1,0:T(8,128)(2,1)S(1)}, u32[]{:S(2)}, u32[]{:S(2)}) collective-permute-start(bf16[3,256,128]{2,1,0:T(8,128)(2,1)S(1)} %get-tuple-element.101), channel_id=1, source_target_pairs={{0,4},{4,0},{8,12},{12,8},{16,20},{20,16},{24,28},{28,24},{1,5},{5... | collective-permute-start | bytes 589832 | tf_op jit(solution)/shard_map/ppermute | solution.py:442
  51.2 6.1 %collective-permute-start.20 = (bf16[32,2048]{1,0:T(8,128)(2,1)S(1)}, bf16[32,2048]{1,0:T(8,128)(2,1)S(1)}, u32[]{:S(2)}, u32[]{:S(2)}) collective-permute-start(bf16[32,2048]{1,0:T(8,128)(2,1)S(1)} %get-tuple-element.94), channel_id=1, source_target_pairs={{0,2},{1,3},{2,0},{3,1},{4,6},{5,7},{6,4},{7,5},{8,10},{9,11},{10,... | collective-permute-start | bytes 393224 | tf_op jit(solution)/shard_map/ppermute | solution.py:442
  52.8 5.9 %collective-permute-start.21 = (bf16[32,2048]{1,0:T(8,128)(2,1)S(1)}, bf16[32,2048]{1,0:T(8,128)(2,1)S(1)}, u32[]{:S(2)}, u32[]{:S(2)}) collective-permute-start(bf16[32,2048]{1,0:T(8,128)(2,1)S(1)} %get-tuple-element.95), channel_id=1, source_target_pairs={{0,2},{1,3},{2,0},{3,1},{4,6},{5,7},{6,4},{7,5},{8,10},{9,11},{10,... | collective-permute-start | bytes 393224 | tf_op jit(solution)/shard_map/ppermute | solution.py:442
  (4 other events, 11.1 us)
